TPU v7x, 32 devices: a whole 2x2x4 slice. The times are simulated.
32 devices in a mesh: mol: 2 (over x), orb: 8 (over z, y), aux: 2 (over core).
Axes of the slice: x: 2, y: 2, z: 4, core: 2. Of those that a mesh axis runs over, the one named last changes fastest.
Arguments:
- blocks: bfloat16 [256, 512, 256], P(('mol', 'orb'), 'aux'), parts along dimension 0, may hold values from -1.5 to 1.5
- vir_energy: float32 [256, 256], P(('mol', 'orb')), parts along dimension 0, may hold values from 0.5 to 3
- occ_energy: float32 [256], P(('mol', 'orb')), parts along dimension 0, may hold values from -1.5 to -0.3
- domain_size: int32 [256], P(('mol', 'orb')), parts along dimension 0, may hold values from 128 to 256, as said below
- partner_owner: int32 [1024, 1], P(('mol', 'orb')), parts along dimension 0, may hold values from 0 to 7; in each aligned block of 64 rows (0 to 63, 64 to 127, ...) at most 8 rows name the same one
- partner_slot: int32 [1024], P(('mol', 'orb')), parts along dimension 0, may hold values from 0 to 15
Outputs:
- pair_energy: float32 [1024], P(('mol', 'orb')), parts along dimension 0
- density: float32 [256, 256, 256], P(('mol', 'orb'), 'aux'), parts along dimension 0
There are 2 independent parts, one for each index of `mol`. A program takes and returns all parts, laid end to end along the dimension named above; each array names one. Nothing has to cross between parts.
Inputs may be any that keep to these rules, and one draw needn't show every extreme that they name: `partner_owner`: among the 64 pairs of one device no owner is named more than 8 times, a bound that some block reaches. `domain_size`: some orbital's domain is full.
All inputs are finite; a program needn't handle non-finite values.
Results may differ from a plain program's by a relative error of at most 0.0019.
Values may be sent and summed in bfloat16 or wider, within the bound.
No kernel may reach another device: no remote copies, remote signals or barrier semaphores. Data moves between devices by JAX's collectives and lax.ppermute only.
A program may use at most 128 MiB of HBM per device.

v0:
```python
import jax
import jax.numpy as jnp
from jax import lax
from jax.sharding import PartitionSpec as P


def slot_ranks(owner):
    count = owner.shape[0]
    order = jnp.arange(count, dtype=jnp.int32)
    same = (owner[:, None] == owner[None, :]) & (order[None, :] < order[:, None])
    return jnp.sum(same.astype(jnp.int32), axis=1)


def on_device(blocks, vir_energy, occ_energy, domain_size, partner_owner, partner_slot):
    occ_dev, half_aux, nvd = blocks.shape
    pair_dev = partner_slot.shape[0]
    per_orb = pair_dev // occ_dev
    peers = lax.axis_size("orb")
    cap = max(2, (pair_dev + peers - 1) // peers)
    owner = partner_owner[:, 0]
    ranks = slot_ranks(owner)
    target = owner * cap + ranks
    wanted = (target[:, None] == jnp.arange(peers * cap, dtype=jnp.int32)[None, :]).astype(
        jnp.int32
    )
    requests = jnp.sum(wanted * partner_slot[:, None], axis=0).reshape(peers, cap)
    incoming = lax.all_to_all(requests, "orb", split_axis=0, concat_axis=0, tiled=True)
    flat_in = incoming.reshape(-1)
    send_blocks = jnp.take(blocks, flat_in, axis=0).reshape(peers, cap, half_aux, nvd)
    send_vir = jnp.take(vir_energy, flat_in, axis=0).reshape(peers, cap, nvd)
    send_occ = jnp.take(occ_energy, flat_in).reshape(peers, cap)
    send_size = jnp.take(domain_size, flat_in).astype(jnp.float32).reshape(peers, cap)
    got_blocks = lax.all_to_all(send_blocks, "orb", split_axis=0, concat_axis=0, tiled=True)
    got_vir, got_occ, got_size = (
        lax.all_to_all(send_vir, "orb", split_axis=0, concat_axis=0, tiled=True),
        lax.all_to_all(send_occ, "orb", split_axis=0, concat_axis=0, tiled=True),
        lax.all_to_all(send_size, "orb", split_axis=0, concat_axis=0, tiled=True),
    )
    partner = jnp.take(got_blocks.reshape(peers * cap, half_aux, nvd), target, axis=0).reshape(
        occ_dev, per_orb, half_aux, nvd
    )
    partner_vir = jnp.take(got_vir.reshape(peers * cap, nvd), target, axis=0).reshape(
        occ_dev, per_orb, nvd
    )
    partner_occ = jnp.take(got_occ.reshape(-1), target).reshape(occ_dev, per_orb)
    partner_size = jnp.take(got_size.reshape(-1), target).reshape(occ_dev, per_orb)
    half = nvd // lax.axis_size("aux")
    integrals = lax.psum_scatter(
        jnp.einsum("oqa,opqb->aopb", blocks, partner, preferred_element_type=jnp.float32),
        "aux",
        scatter_dimension=0,
        tiled=True,
    )
    row_start = lax.axis_index("aux") * half
    rows = row_start + jnp.arange(half, dtype=jnp.int32)
    cols = jnp.arange(nvd, dtype=jnp.int32).astype(jnp.float32)
    mask = (rows[:, None, None, None] < domain_size[None, :, None, None]) & (
        cols[None, None, None, :] < partner_size[None, :, :, None]
    )
    integrals = jnp.where(mask, integrals, jnp.zeros_like(integrals))
    vir_rows = lax.dynamic_slice_in_dim(vir_energy, row_start, half, 1)
    gap = (
        vir_rows.T[:, :, None, None]
        + partner_vir[None, :, :, :]
        - occ_energy[None, :, None, None]
        - partner_occ[None, :, :, None]
    )
    amp_rows = (-integrals / gap).astype(jnp.bfloat16)
    partial_energy = jnp.sum(integrals * amp_rows.astype(jnp.float32), axis=(0, 3))
    energy = lax.psum(partial_energy, "aux").reshape(pair_dev) / nvd
    density = jnp.einsum(
        "aopb,copb->oac",
        amp_rows,
        lax.all_gather(amp_rows, "aux", axis=0, tiled=True),
        preferred_element_type=jnp.float32,
    )
    return (energy, density)


def solution(mesh):
    in_specs = (
        P(("mol", "orb"), "aux", None),
        P(("mol", "orb"), None),
        P(("mol", "orb")),
        P(("mol", "orb")),
        P(("mol", "orb"), None),
        P(("mol", "orb")),
    )
    out_specs = (P(("mol", "orb")), P(("mol", "orb"), "aux", None))
    return jax.shard_map(
        on_device, mesh=mesh, in_specs=in_specs, out_specs=out_specs, check_vma=False
    )
```

profile of v0, /device:TPU:0, one launch (start us, length us, event | category | flops | bytes accessed | tf_op | source)
XLA Modules:
  0.0 330.7 jit_solution(10678069272241972537)
XLA Ops:
  7.2 1.0 convert_reduce_fusion
  8.2 0.7 fusion.7
  8.9 0.7 select_reduce_fusion
  9.6 0.1 all_to_all.20
  9.7 13.5 %all_to_all.31 = s32[8,1,8]{2,1,0:T(1,128)S(1)} all-to-all(s32[8,1,8]{2,1,0:T(1,128)S(1)} %bitcast.48), channel_id=1, replica_groups=mesh['mol'=2,'orb'=8,'aux'=2] {'orb'}, dimensions={0} | all-to-all | bytes 512 | tf_op jit(solution)/shard_map/all_to_all | solution.py:27
  23.2 0.5 broadcast.161
  23.7 0.7 reduce.13
  24.4 0.1 reshape.165
  24.5 5.5 %gather_fusion.1 = bf16[64,256,256]{2,1,0:T(8,128)(2,1)} fusion(bf16[16,256,256]{2,1,0:T(8,128)(2,1)S(1)} %copy-done, s32[1024]{0:T(1024)S(1)} %pad_clamp_fusion.2), kind=kCustom, calls=%fused_computation.3 | custom fusion | bytes 16777472 | tf_op jit(solution)/shard_map/jit(_take)/gather | solution.py:29
  30.0 7.5 %broadcast_select_fusion = bf16[8,8,256,256]{3,2,1,0:T(8,128)(2,1)} fusion(bf16[8,8,256,256]{3,2,1,0:T(8,128)(2,1)} %bitcast.44, pred[8,8]{1,0:T(8,128)(4,1)S(1)} %compare_and_fusion), kind=kLoop, calls=%fused_computation.12 | loop fusion | flops 4194304 | bytes 16777280 | tf_op jit(solution)/shard_map/jit(_take)/select_n | solution.py:29
  37.5 5.1 %all-to-all-start.2 = ((bf16[8,8,256,256]{3,2,1,0:T(8,128)(2,1)}), bf16[8,8,256,256]{3,2,1,0:T(8,128)(2,1)}, u32[]{:S(2)}, u32[]{:S(2)}) async-start(bf16[8,8,256,256]{3,2,1,0:T(8,128)(2,1)} %broadcast_select_fusion), calls=%async_computation.2 | async-start | bytes 16777216 | tf_op jit(solution)/shard_map/all_to_all | solution.py:33
  42.7 0.1 broadcast_in_dim.74
  42.8 181.7 %all-to-all-done.2 = bf16[8,8,256,256]{3,2,1,0:T(8,128)(2,1)} async-done(((bf16[8,8,256,256]{3,2,1,0:T(8,128)(2,1)}), bf16[8,8,256,256]{3,2,1,0:T(8,128)(2,1)}, u32[]{:S(2)}, u32[]{:S(2)}) %all-to-all-start.2) | async-done | bytes 8388640 | tf_op jit(solution)/shard_map/all_to_all | solution.py:33
  224.5 8.9 %gather_fusion.2 = bf16[64,256,256]{2,1,0:T(8,128)(2,1)} fusion(bf16[64,256,256]{2,1,0:T(8,128)(2,1)} %bitcast.11, s32[1024]{0:T(1024)S(1)} %pad_clamp_fusion), kind=kCustom, calls=%fused_computation.4 | custom fusion | bytes 16777472 | tf_op jit(solution)/shard_map/jit(_take)/gather | solution.py:39
  233.4 12.3 %copy.27 = bf16[16,4,256,256]{2,3,1,0:T(8,128)(2,1)} copy(bf16[16,4,256,256]{3,2,1,0:T(8,128)(2,1)} %bitcast.43) | data formatting | bytes 16777216 | tf_op jit(solution)/shard_map/jit(_take)/gather | solution.py:39
  245.7 11.5 %convolution_bitcast_fusion = f32[256,16,4,256]{0,3,2,1:T(8,128)} fusion(bf16[16,4,256,256]{2,3,1,0:T(8,128)(2,1)} %copy.27, pred[16,4]{1,0:T(8,128)(4,1)S(1)} %broadcast_in_dim.74, bf16[16,256,256]{2,1,0:T(8,128)(2,1)S(1)} %copy-done), kind=kOutput, calls=%fused_computation.8 | convolution fusion | flops 2151677952 | bytes 27263040 | tf_op jit(solution)/shard_map/oqa,opqb->aopb/dot_general | solution.py:49
  257.3 0.6 copy-done.4
  258.0 0.8 gather_fusion
  258.8 0.1 gather.40
  258.9 0.8 gather_fusion.5
  259.6 0.1 gather.50
  259.7 0.6 select_convert_fusion
  260.3 0.6 broadcast_select_fusion.2
  260.9 3.6 %all-to-all-start.4 = ((f32[8,1,8]{2,1,0:T(1,128)}), f32[8,1,8]{2,1,0:T(1,128)S(1)}, u32[]{:S(2)}, u32[]{:S(2)}) async-start(f32[8,1,8]{2,1,0:T(1,128)} %bitcast.20), calls=%async_computation.5 | async-start | bytes 8192 | tf_op jit(solution)/shard_map/all_to_all | solution.py:36
  264.5 0.7 gather_fusion.3
  265.2 5.7 %all-to-all-done.4 = f32[8,1,8]{2,1,0:T(1,128)S(1)} async-done(((f32[8,1,8]{2,1,0:T(1,128)}), f32[8,1,8]{2,1,0:T(1,128)S(1)}, u32[]{:S(2)}, u32[]{:S(2)}) %all-to-all-start.4) | async-done | bytes 288 | tf_op jit(solution)/shard_map/all_to_all | solution.py:36
  270.9 3.3 all-to-all-start.1
  274.2 0.7 bitcast_select_fusion
  274.9 0.5 broadcast.162
  275.4 0.7 reduce.14
  276.1 0.1 reshape.170
  276.2 4.4 %all-to-all-done.1 = f32[8,1,8]{2,1,0:T(1,128)S(1)} async-done(((f32[8,1,8]{2,1,0:T(1,128)}), f32[8,1,8]{2,1,0:T(1,128)S(1)}, u32[]{:S(2)}, u32[]{:S(2)}) %all-to-all-start.1) | async-done | bytes 288 | tf_op jit(solution)/shard_map/all_to_all | solution.py:37
  280.6 3.4 %all-to-all-start.3 = ((f32[8,8,256]{2,1,0:T(8,128)}), f32[8,8,256]{2,1,0:T(8,128)S(1)}, u32[]{:S(2)}, u32[]{:S(2)}) async-start(f32[8,8,256]{2,1,0:T(8,128)} %bitcast_select_fusion), calls=%async_computation.4 | async-start | bytes 131072 | tf_op jit(solution)/shard_map/all_to_all | solution.py:35
  284.0 0.7 reduce.15
  284.7 0.1 reshape.166
  284.8 0.8 gather_fusion.7
  285.5 0.8 gather_fusion.6
  286.3 0.1 lt.128
  286.4 0.1 sub.20
  286.5 0.1 broadcast_compare_fusion
  286.6 4.2 %all-to-all-done.3 = f32[8,8,256]{2,1,0:T(8,128)S(1)} async-done(((f32[8,8,256]{2,1,0:T(8,128)}), f32[8,8,256]{2,1,0:T(8,128)S(1)}, u32[]{:S(2)}, u32[]{:S(2)}) %all-to-all-start.3) | async-done | bytes 65568 | tf_op jit(solution)/shard_map/all_to_all | solution.py:35
  290.8 0.7 gather_fusion.4
  291.5 0.1 broadcast_select_fusion.1
  291.6 8.7 %multiply_reduce_fusion = (f32[16,4]{1,0:T(8,128)S(1)}, bf16[128,16,4,256]{0,3,2,1:T(8,128)(2,1)}) fusion(f32[128,16,4,256]{0,3,2,1:T(8,128)} %reduce-scatter.2.cloned.1.call-done, pred[16,4,256]{2,1,0:T(4,128)(4,1)S(1)} %broadcast_compare_fusion, pred[128,16]{0,1:T(8,128)(4,1)S(1)} %broadcast_compare_fusion.1, f32[16,4]{1,0:T(8,128)S(1)} %sub.20, ...), kind=kLoop, calls=%fused_computation.9 | loop fusion | flops 23068608 | bytes 12675648 | tf_op jit(solution)/shard_map/reduce_sum | solution.py:69
  300.3 2.5 psum.7
  302.9 0.6 div.14
  303.5 12.8 %all-gather.2.cloned.1.call-done = bf16[256,16,4,256]{0,3,2,1:T(8,128)(2,1)} async-done(((bf16[128,16,4,256]{0,3,2,1:T(8,128)(2,1)}), bf16[256,16,4,256]{0,3,2,1:T(8,128)(2,1)}) %all-gather.2.cloned.1.call-update) | async-done | bytes 8388624 | tf_op jit(solution)/shard_map/all_gather | solution.py:74
  316.3 7.5 %convolution_bitcast_fusion.1 = f32[16,128,256]{2,1,0:T(8,128)} fusion(bf16[128,16,4,256]{0,3,2,1:T(8,128)(2,1)} %get-tuple-element.4, bf16[256,16,4,256]{0,3,2,1:T(8,128)(2,1)} %all-gather.2.cloned.1.call-done), kind=kOutput, calls=%fused_computation.17 | convolution fusion | flops 1073741824 | bytes 14680064 | tf_op jit(solution)/shard_map/aopb,copb->oac/dot_general | solution.py:71
  (30 shorter events, 0.3 us)
Async XLA Ops:
  7.2 17.4 %copy-start = (bf16[16,256,256]{2,1,0:T(8,128)(2,1)S(1)}, bf16[16,256,256]{2,1,0:T(8,128)(2,1)}, u32[]{:S(2)}) copy-start(bf16[16,256,256]{2,1,0:T(8,128)(2,1)} %param.8) | copy-start | bytes 6291460
  37.5 5.2 %copy-start.5 = (s32[64,1]{0,1:T(1,128)S(1)}, s32[64,1]{0,1:T(1,128)}, u32[]{:S(2)}) copy-start(s32[64,1]{0,1:T(1,128)} %param.12) | copy-start | bytes 772
  37.5 187.0 %all-to-all-start.2 = ((bf16[8,8,256,256]{3,2,1,0:T(8,128)(2,1)}), bf16[8,8,256,256]{3,2,1,0:T(8,128)(2,1)}, u32[]{:S(2)}, u32[]{:S(2)}) async-start(bf16[8,8,256,256]{3,2,1,0:T(8,128)(2,1)} %broadcast_select_fusion), calls=%async_computation.2 | async-start | bytes 16777216 | tf_op jit(solution)/shard_map/all_to_all | solution.py:33
  42.6 249.0 %reduce-scatter.2.cloned.1.call-start = ((), (), s32[]{:S(2)}) async-start(), calls=%async_computation.6 | async-start | bytes 25165824 | tf_op jit(solution)/shard_map/reduce_scatter | solution.py:48
  257.2 0.7 copy-start.4
  257.2 0.7 copy-start.2
  257.2 1.7 copy-start.3
  260.9 10.0 %all-to-all-start.4 = ((f32[8,1,8]{2,1,0:T(1,128)}), f32[8,1,8]{2,1,0:T(1,128)S(1)}, u32[]{:S(2)}, u32[]{:S(2)}) async-start(f32[8,1,8]{2,1,0:T(1,128)} %bitcast.20), calls=%async_computation.5 | async-start | bytes 8192 | tf_op jit(solution)/shard_map/all_to_all | solution.py:36
  270.9 9.7 %all-to-all-start.1 = ((f32[8,1,8]{2,1,0:T(1,128)}), f32[8,1,8]{2,1,0:T(1,128)S(1)}, u32[]{:S(2)}, u32[]{:S(2)}) async-start(f32[8,1,8]{2,1,0:T(1,128)} %bitcast.8), calls=%async_computation.1 | async-start | bytes 8192 | tf_op jit(solution)/shard_map/all_to_all | solution.py:37
  280.6 10.2 %all-to-all-start.3 = ((f32[8,8,256]{2,1,0:T(8,128)}), f32[8,8,256]{2,1,0:T(8,128)S(1)}, u32[]{:S(2)}, u32[]{:S(2)}) async-start(f32[8,8,256]{2,1,0:T(8,128)} %bitcast_select_fusion), calls=%async_computation.4 | async-start | bytes 131072 | tf_op jit(solution)/shard_map/all_to_all | solution.py:35
  284.0 32.3 %all-gather.2.cloned.1.call-start = ((), (), s32[]{:S(2)}) async-start(), calls=%async_computation.7 | async-start | bytes 12582912 | tf_op jit(solution)/shard_map/all_gather | solution.py:74
  302.9 21.0 %copy-start.1 = (bf16[16,256,256]{2,1,0:T(8,128)(2,1)S(1)}, bf16[16,256,256]{2,1,0:T(8,128)(2,1)}, u32[]{:S(2)}) copy-start(bf16[16,256,256]{2,1,0:T(8,128)(2,1)} %param.8) | copy-start | bytes 6291460
Sparse Core Ops, SparseCore 0:
  257.3 25.3 reduce-scatter.1
  300.5 15.7 all-gather.1
where the time goes:
time: 332 us; the launch traced here: 331 us
  waiting for transfers between devices  209 us (63%)
  local copies, waits for them, and re-layouts  34.2 us (10%)
  other arithmetic  22.8 us (7%)
  matrix products  19 us (6%)
  blocking collectives  16 us (5%)
  starting transfers between devices  15.4 us (5%)
  between operations  14.2 us (4%)
    all_to_all x1, waiting for transfers between devices, on_device(): lax.all_to_all(send_blocks, 'orb', split_axis=0, concat_axis=0, tiled=True)  182 us
    gather x2, local copies, waits for them, and re-layouts, on_device(): jnp.take(got_blocks.reshape(peers * cap, half_aux, nvd), target, axis=0)  21.2 us
    all_to_all x1, blocking collectives, on_device(): lax.all_to_all(requests, 'orb', split_axis=0, concat_axis=0, tiled=True)  13.5 us
    all_gather x1, waiting for transfers between devices, on_device(): lax.all_gather(amp_rows, 'aux', axis=0, tiled=True)  12.8 us
    dot_general x1, matrix products, on_device(): jnp.einsum('oqa,opqb->aopb', blocks, partner, preferred_element_type=jnp....  11.5 us
    reduce_sum x1, other arithmetic, on_device(): jnp.sum(integrals * amp_rows.astype(jnp.float32), axis=(0, 3))  8.71 us
    dot_general x1, matrix products, on_device(): jnp.einsum('aopb,copb->oac', amp_rows, lax.all_gather(amp_rows, 'aux', ax...  7.55 us
    select_n x1, other arithmetic, on_device(): jnp.take(blocks, flat_in, axis=0).reshape(peers, cap, half_aux, nvd)  7.46 us
  transfers between devices with their start and end apart: 6, of which 5 were waited for; matrix products, arithmetic and copies ran while one was open for 3% of the time, Pallas kernels for 0%

commit v1 on v0

--- a/solution.py
+++ b/solution.py
@@ -1,7 +1,15 @@
 import jax
 import jax.numpy as jnp
 from jax import lax
+from jax.experimental import pallas as pl
+from jax.experimental.pallas import tpu as pltpu
 from jax.sharding import PartitionSpec as P
+
+f32, bf16, i32 = jnp.float32, jnp.bfloat16, jnp.int32
+ANY = pl.BlockSpec(memory_space=pl.ANY)
+SMEM = pl.BlockSpec(memory_space=pltpu.SMEM)
+VMEM = pl.BlockSpec(memory_space=pltpu.VMEM)
+LIMIT = 48 * 1024 * 1024
 
 
 def slot_ranks(owner):
@@ -11,7 +19,7 @@
     return jnp.sum(same.astype(jnp.int32), axis=1)
 
 
-def on_device(blocks, vir_energy, occ_energy, domain_size, partner_owner, partner_slot):
+def by_requests(blocks, vir_energy, occ_energy, domain_size, partner_owner, partner_slot):
     occ_dev, half_aux, nvd = blocks.shape
     pair_dev = partner_slot.shape[0]
     per_orb = pair_dev // occ_dev
@@ -77,6 +85,233 @@
     return (energy, density)
 
 
+def fits_line(mesh):
+    return mesh.shape["orb"] == 8 and mesh.shape["aux"] == 2
+
+
+def table_of(bases, fields):
+    return jnp.concatenate([bases] + fields).astype(i32)
+
+
+def pack_kernel(call, cap, count, tbl, x, out, sems):
+    base = tbl[call]
+    copies = []
+    for r in range(cap):
+        slot = tbl[8 + base + r]
+        copies.append(pltpu.make_async_copy(x.at[slot], out.at[r], sems.at[r]))
+        copies[-1].start()
+    for copy in copies:
+        copy.wait()
+
+
+def pack(tbl, call, x, cap):
+    return pl.pallas_call(
+        lambda *refs: pack_kernel(call, cap, 64, *refs),
+        out_shape=jax.ShapeDtypeStruct((cap,) + x.shape[1:], x.dtype),
+        in_specs=[SMEM, ANY],
+        out_specs=ANY,
+        scratch_shapes=[pltpu.SemaphoreType.DMA((cap,))],
+        compiler_params=pltpu.CompilerParams(vmem_limit_bytes=LIMIT),
+        cost_estimate=pl.CostEstimate(
+            flops=0, bytes_accessed=2 * cap * x.shape[1] * x.shape[2] * 2, transcendentals=0
+        ),
+        name="pack",
+    )(tbl, x)
+
+
+def amplitudes_kernel(
+    call, by_slot, per_orb, tbl, rows, vcol, a0, a1, j0, j1, tin, tout, energy,
+    sv, s0, s1, b0, b1, st, sem, sem_out,
+):
+    cap = sv.shape[0]
+    n = rows.shape[0]
+    base = tbl[call]
+    loads = []
+    for r in range(cap):
+        p = tbl[8 + base + r]
+        i = lax.div(p, per_orb)
+        slot = tbl[8 + n + base + r] if by_slot else r
+        pairs = (
+            (vcol.at[i], sv.at[r]),
+            (a0.at[i], s0.at[r]),
+            (a1.at[i], s1.at[r]),
+            (j0.at[slot], b0.at[r]),
+            (j1.at[slot], b1.at[r]),
+        )
+        group = []
+        for k, (source, target) in enumerate(pairs):
+            copy = pltpu.make_async_copy(source, target, sem.at[r, k])
+            copy.start()
+            group.append(copy)
+        loads.append(group)
+    nvd, half = sv.shape[1], sv.shape[2]
+    live_a = lax.broadcasted_iota(i32, (nvd, half), 0)
+    live_b = lax.broadcasted_iota(i32, (nvd, half), 1)
+    row8 = rows[pl.ds(pl.multiple_of(base, cap), cap), :]
+    stores = []
+    for r in range(cap):
+        p = tbl[8 + base + r]
+        size_i = tbl[8 + 2 * n + base + r]
+        size_j = tbl[8 + 3 * n + base + r]
+        for copy in loads[r]:
+            copy.wait()
+        k = jnp.dot(s0[r], b0[r], preferred_element_type=f32)
+        k += jnp.dot(s1[r], b1[r], preferred_element_type=f32)
+        k = jnp.where((live_a < size_i) & (live_b < size_j), k, 0.0)
+        gap = sv[r] + row8[r : r + 1, :]
+        t = (-k / gap).astype(bf16)
+        st[r] = t
+        copy = pltpu.make_async_copy(st.at[r], tout.at[p], sem_out.at[r])
+        copy.start()
+        stores.append(copy)
+        energy[r] = jnp.sum((k * t.astype(f32)).reshape(nvd // 8, 8, half), axis=0)
+    for copy in stores:
+        copy.wait()
+
+
+def amplitudes(call, by_slot, per_orb, tbl, rows, vcol, a0, a1, j0, j1, t_all, cap):
+    nvd, half = vcol.shape[1:]
+    qa = j0.shape[1]
+    return pl.pallas_call(
+        lambda *refs: amplitudes_kernel(call, by_slot, per_orb, *refs),
+        out_shape=(
+            jax.ShapeDtypeStruct(t_all.shape, t_all.dtype),
+            jax.ShapeDtypeStruct((cap, 8, half), f32),
+        ),
+        in_specs=[SMEM, VMEM, ANY, ANY, ANY, ANY, ANY, ANY],
+        out_specs=(ANY, VMEM),
+        scratch_shapes=[
+            pltpu.VMEM((cap, nvd, half), f32),
+            pltpu.VMEM((cap, nvd, qa), bf16),
+            pltpu.VMEM((cap, nvd, qa), bf16),
+            pltpu.VMEM((cap, qa, half), bf16),
+            pltpu.VMEM((cap, qa, half), bf16),
+            pltpu.VMEM((cap, nvd, half), bf16),
+            pltpu.SemaphoreType.DMA((cap, 5)),
+            pltpu.SemaphoreType.DMA((cap,)),
+        ],
+        input_output_aliases={7: 0},
+        compiler_params=pltpu.CompilerParams(vmem_limit_bytes=LIMIT),
+        cost_estimate=pl.CostEstimate(
+            flops=cap * 4 * nvd * qa * half,
+            bytes_accessed=cap * (nvd * half * 6 + 4 * nvd * qa + 4 * qa * half),
+            transcendentals=0,
+        ),
+        name="amplitudes",
+    )(tbl, rows, vcol, a0, a1, j0, j1, t_all)
+
+
+def density_kernel(start, t, d):
+    half = d.shape[1]
+    first = pl.multiple_of(start[0], half)
+    left = jnp.concatenate([t[k, pl.ds(first, half), :] for k in range(t.shape[0])], axis=1)
+    right = jnp.concatenate([t[k] for k in range(t.shape[0])], axis=1)
+    d[0] = lax.dot_general(left, right, (((1,), (1,)), ((), ())), preferred_element_type=f32)
+
+
+def density_rows(t_all, start, per_orb, half):
+    npair, nvd, width = t_all.shape
+    occ = npair // per_orb
+    return pl.pallas_call(
+        density_kernel,
+        out_shape=jax.ShapeDtypeStruct((occ, half, nvd), f32),
+        grid_spec=pltpu.PrefetchScalarGridSpec(
+            num_scalar_prefetch=1,
+            grid=(occ,),
+            in_specs=[pl.BlockSpec((per_orb, nvd, width), lambda i, s: (i, 0, 0))],
+            out_specs=pl.BlockSpec((1, half, nvd), lambda i, s: (i, 0, 0)),
+        ),
+        compiler_params=pltpu.CompilerParams(vmem_limit_bytes=LIMIT),
+        cost_estimate=pl.CostEstimate(
+            flops=2 * npair * half * nvd * width,
+            bytes_accessed=npair * nvd * width * 2 + occ * half * nvd * 4,
+            transcendentals=0,
+        ),
+        name="density_rows",
+    )(start.reshape(1), t_all)
+
+
+def line_plan(blocks, vir_energy, occ_energy, domain_size, partner_owner, partner_slot):
+    occ, qa, nvd = blocks.shape
+    pair_dev = partner_slot.shape[0]
+    per_orb = pair_dev // occ
+    peers = 8
+    cap = pair_dev // peers
+    half = nvd // 2
+    me, core = lax.axis_index("orb"), lax.axis_index("aux")
+    z, y = me // 2, me % 2
+    middle = (z == 1) | (z == 2)
+    swap_core = [(0, 1), (1, 0)]
+    swap_y = [(o, o ^ 1) for o in range(peers)]
+    swap_half = [(o, o ^ 2) for o in range(peers)]
+    cross = [(2, 4), (3, 5), (4, 2), (5, 3)]
+    outward = [(2, 0), (3, 1), (4, 6), (5, 7)]
+
+    other = lax.ppermute(blocks, "aux", swap_core)
+    col0 = core * half
+    own = [lax.dynamic_slice_in_dim(x, col0, half, 2) for x in (blocks, other)]
+
+    owner = partner_owner[:, 0]
+    target = owner * cap + slot_ranks(owner)
+    hit = target[None, :] == jnp.arange(pair_dev, dtype=i32)[:, None]
+    pairs = jnp.arange(pair_dev, dtype=i32)
+    order = jnp.sum(jnp.where(hit, pairs[None, :], 0), axis=1)
+    slots = jnp.sum(jnp.where(hit, partner_slot[None, :], 0), axis=1)
+    small = jnp.concatenate(
+        [
+            vir_energy,
+            occ_energy[:, None],
+            domain_size.astype(f32)[:, None],
+            jnp.zeros((occ, 126), f32),
+        ],
+        axis=1,
+    )
+    every = lax.all_gather(small, "orb", axis=0, tiled=True)
+    theirs = jnp.take(every, (pairs // cap) * occ + slots, axis=0)
+    mine = jnp.take(small, order // per_orb, axis=0)
+    rows = lax.dynamic_slice_in_dim(theirs, col0, half, 1) - (
+        theirs[:, nvd : nvd + 1] + mine[:, nvd : nvd + 1]
+    )
+    size_i = mine[:, nvd + 1].astype(i32)
+    size_j = theirs[:, nvd + 1].astype(i32) - col0
+    lower = z < 2
+    column = jnp.stack([z, z ^ 1, jnp.where(lower, 2, 1), jnp.where(lower, 3, 0)])
+    bases = jnp.concatenate([column * 2 + y, column * 2 + (1 - y)]) * cap
+    tbl = table_of(bases, [order, slots, size_i, size_j])
+    wanted = table_of(bases, [lax.ppermute(slots, "orb", swap_y)])
+    vcol = jnp.broadcast_to(vir_energy[:, :, None], (occ, nvd, half))
+    left = [jnp.swapaxes(x, 1, 2) for x in (blocks, other)]
+
+    near = [lax.ppermute(x, "orb", swap_half) for x in own]
+    mid = [lax.ppermute(x, "orb", cross) for x in own]
+    mid_out = [lax.ppermute(x, "orb", outward) for x in mid]
+    far = [lax.ppermute(x, "orb", cross) for x in near]
+    far_out = [lax.ppermute(x, "orb", outward) for x in far]
+    third = [jnp.where(middle, a, b) for a, b in zip(mid, mid_out)]
+    fourth = [jnp.where(middle, a, b) for a, b in zip(far, far_out)]
+    sources = [own, near, third, fourth]
+    beside = [
+        [lax.ppermute(pack(wanted, k, x, cap), "orb", swap_y) for x in source]
+        for k, source in enumerate(sources)
+    ]
+
+    t_all = jnp.zeros((pair_dev, nvd, half), bf16)
+    energies = [None] * 8
+    for k in (0, 1, 4, 2, 5, 3, 6, 7):
+        j0, j1 = sources[k] if k < 4 else beside[k - 4]
+        t_all, energies[k] = amplitudes(
+            k, k < 4, per_orb, tbl, rows, vcol, left[0], left[1], j0, j1, t_all, cap
+        )
+    away = lax.ppermute(density_rows(t_all, (1 - core) * half, per_orb, half), "aux", swap_core)
+    density = density_rows(t_all, core * half, per_orb, half) + away
+
+    sums = jnp.sum(jnp.stack(energies), axis=(2, 3)).reshape(pair_dev)
+    place = (bases[:, None] + jnp.arange(cap, dtype=i32)[None, :]).reshape(pair_dev)
+    spot = target[:, None] == place[None, :]
+    energy = lax.psum(jnp.sum(jnp.where(spot, sums[None, :], 0.0), axis=1), "aux") / nvd
+    return (energy, density)
+
+
 def solution(mesh):
     in_specs = (
         P(("mol", "orb"), "aux", None),
@@ -88,5 +323,5 @@
     )
     out_specs = (P(("mol", "orb")), P(("mol", "orb"), "aux", None))
     return jax.shard_map(
-        on_device, mesh=mesh, in_specs=in_specs, out_specs=out_specs, check_vma=False
-    )
+        line_plan if fits_line(mesh) else by_requests, mesh=mesh, in_specs=in_specs, out_specs=out_specs, check_vma=False
+    )

time: 332 us -> 286 us (0.86)
  waiting for transfers between devices: 209 us -> 53.4 us
  Pallas kernels: 0 us -> 80.6 us
  blocking collectives: 16 us -> 72.6 us
  matrix products: 19 us -> 0 us
  between operations: 14.2 us -> 1.33 us
  starting transfers between devices: 15.4 us -> 26.6 us
  other arithmetic: 22.8 us -> 14.8 us
    all_to_all x4 -> x0, waiting for transfers between devices: 196 us -> none  [the longest x1 182 us: on_device(): lax.all_to_all(send_blocks, 'orb', split_axis=0, concat_axis=0, tiled=True)]
    pallas_call x0 -> x18, Pallas kernels: none -> 80.6 us  [the longest x8 50 us: amplitudes(): pl.pallas_call(lambda *refs: amplitudes_kernel(call, by_slot, per_orb, *r...]
    all_gather x0 -> x1, blocking collectives: none -> 69 us  [line_plan(): every = lax.all_gather(small, 'orb', axis=0, tiled=True)]
    ppermute x0 -> x21, waiting for transfers between devices: none -> 53.4 us  [the longest x2 33.1 us: line_plan(): near = [lax.ppermute(x, 'orb', swap_half) for x in own]]
    gather x12 -> x2, local copies, waits for them, and re-layouts: 31.3 us -> 1.32 us  [the longest x1 0.66 us: line_plan(): mine = jnp.take(small, order // per_orb, axis=0)]
    ppermute x0 -> x21, starting transfers between devices: none -> 26.6 us  [the longest x8 6.22 us: line_plan(): lax.ppermute(pack(wanted, k, x, cap), 'orb', swap_y)]
    dot_general x2 -> x0, matrix products: 19 us -> none  [the longest x1 11.5 us: on_device(): jnp.einsum('oqa,opqb->aopb', blocks, partner, preferred_element_type=jnp....]
    all_to_all x4 -> x0, starting transfers between devices: 15.3 us -> none  [the longest x1 5.09 us: on_device(): lax.all_to_all(send_blocks, 'orb', split_axis=0, concat_axis=0, tiled=True)]
  transfers between devices with their start and end apart: 6 -> 21, of which waited for: 5 -> 4; matrix products, arithmetic and copies ran while one was open for 3% -> 12% of each run, Pallas kernels for 0% -> 23%
where the time goes in v1:
time: 286 us; the launch traced here: 284 us
  Pallas kernels  80.6 us (28%)
  blocking collectives  72.6 us (25%)
  waiting for transfers between devices  53.4 us (19%)
  local copies, waits for them, and re-layouts  35.1 us (12%)
  starting transfers between devices  26.6 us (9%)
  other arithmetic  14.8 us (5%)
    all_gather x1, blocking collectives, line_plan(): every = lax.all_gather(small, 'orb', axis=0, tiled=True)  69 us
    pallas_call x8, Pallas kernels, amplitudes(): pl.pallas_call(lambda *refs: amplitudes_kernel(call, by_slot, per_orb, *r...  50 us
    ppermute x2, waiting for transfers between devices, line_plan(): near = [lax.ppermute(x, 'orb', swap_half) for x in own]  33.1 us
    pallas_call x2, Pallas kernels, density_rows(): pl.pallas_call(density_kernel, out_shape=jax.ShapeDtypeStruct((occ, half,...  19.7 us
    ppermute x2, waiting for transfers between devices, line_plan(): mid_out = [lax.ppermute(x, 'orb', outward) for x in mid]  14.1 us
    unnamed x58, local copies, waits for them, and re-layouts  12.6 us
    pallas_call x8, Pallas kernels, pack(): pl.pallas_call(lambda *refs: pack_kernel(call, cap, 64, *refs), out_shape...  11 us
    ppermute x8, starting transfers between devices, line_plan(): lax.ppermute(pack(wanted, k, x, cap), 'orb', swap_y)  6.22 us
  transfers between devices with their start and end apart: 21, of which 4 were waited for; matrix products, arithmetic and copies ran while one was open for 12% of the time, Pallas kernels for 23%

profile of v1, /device:TPU:0, one launch (start us, length us, event | category | flops | bytes accessed | tf_op | source)
XLA Modules:
  0.0 284.5 jit_solution(14833151206867725934)
XLA Ops:
  0.6 2.9 %copy.60 = bf16[16,256,256]{1,2,0:T(8,128)(2,1)S(1)} copy(bf16[16,256,256]{2,1,0:T(8,128)(2,1)} %param.6) | data formatting | bytes 4194304 | tf_op args[0]
  4.1 2.7 collective-permute-start.1
  6.8 1.6 collective-permute-start.3
  8.8 1.6 collective-permute-start.7
  10.5 2.3 constant_dynamic-slice_fusion
  12.9 3.4 %collective-permute-start.2 = (bf16[16,256,128]{1,2,0:T(8,128)(2,1)}, bf16[16,256,128]{1,2,0:T(8,128)(2,1)}, u32[]{:S(2)}, u32[]{:S(2)}) collective-permute-start(bf16[16,256,128]{1,2,0:T(8,128)(2,1)} %constant_dynamic-slice_fusion), channel_id=1, source_target_pairs={{0,4},{2,6},{4,0},{6,2},{8,12},{10,14},{12,8},{14,10},{1,5},{3,7},... | collective-permute-start | bytes 3145736 | tf_op jit(solution)/shard_map/ppermute | solution.py:285
  16.7 14.3 %collective-permute-done.1 = bf16[16,256,128]{1,2,0:T(8,128)(2,1)} collective-permute-done((bf16[16,256,128]{1,2,0:T(8,128)(2,1)S(1)}, bf16[16,256,128]{1,2,0:T(8,128)(2,1)}, u32[]{:S(2)}, u32[]{:S(2)}) %collective-permute-start.1) | collective-permute-done | bytes 1048608 | tf_op jit(solution)/shard_map/ppermute | solution.py:285
  31.0 1.7 collective-permute-start.10
  32.7 1.6 collective-permute-start.5
  34.3 18.9 %collective-permute-done.2 = bf16[16,256,128]{1,2,0:T(8,128)(2,1)} collective-permute-done((bf16[16,256,128]{1,2,0:T(8,128)(2,1)}, bf16[16,256,128]{1,2,0:T(8,128)(2,1)}, u32[]{:S(2)}, u32[]{:S(2)}) %collective-permute-start.2) | collective-permute-done | bytes 1048608 | tf_op jit(solution)/shard_map/ppermute | solution.py:285
  53.2 1.7 collective-permute-start.12
  56.3 69.0 %all_gather.3 = f32[128,384]{1,0:T(8,128)S(1)} all-gather(f32[16,384]{1,0:T(8,128)S(1)} %maximum_maximum_fusion), channel_id=1, replica_groups=mesh['mol'=2,'orb'=8,'aux'=2] {'orb'}, dimensions={0}, use_global_device_ids=true | all-gather | bytes 221184 | tf_op jit(solution)/shard_map/all_gather | solution.py:269
  129.4 1.5 collective-permute-start.13
  131.9 1.5 pack.8
  133.4 1.6 copy.65.refs_5_.refs_1_
  135.1 1.3 pack.10
  137.2 1.6 copy.64.refs_6_.refs_1_
  138.8 1.3 pack.9
  141.0 2.0 collective-permute-start.14
  143.0 2.3 broadcast_select_fusion.3
  145.3 1.6 copy.69.refs_5_.refs_1_
  146.9 1.3 pack.12
  149.1 2.3 copy.66.refs_6_.refs_1_
  152.6 1.3 pack.11
  154.8 2.3 broadcast_select_fusion.1
  157.1 2.3 copy.73.refs_5_.refs_1_
  162.7 14.1 %collective-permute-done.6 = bf16[16,256,128]{1,2,0:T(8,128)(2,1)} collective-permute-done((bf16[16,256,128]{1,2,0:T(8,128)(2,1)}, bf16[16,256,128]{1,2,0:T(8,128)(2,1)}, u32[]{:S(2)}, u32[]{:S(2)}) %collective-permute-start.6) | collective-permute-done | bytes 1048608 | tf_op jit(solution)/shard_map/ppermute | solution.py:287
  176.8 2.3 broadcast_select_fusion.2
  179.2 2.3 copy.70.refs_6_.refs_1_
  184.8 6.1 %collective-permute-done.13 = bf16[16,256,128]{1,2,0:T(8,128)(2,1)} collective-permute-done((bf16[16,256,128]{1,2,0:T(8,128)(2,1)}, bf16[16,256,128]{1,2,0:T(8,128)(2,1)}, u32[]{:S(2)}, u32[]{:S(2)}) %collective-permute-start.13) | collective-permute-done | bytes 1048608 | tf_op jit(solution)/shard_map/ppermute | solution.py:289
  190.9 2.3 broadcast_select_fusion
  193.2 2.3 copy.74.refs_6_.refs_1_
  196.7 1.5 pack.15
  198.2 2.1 collective-permute-start.18
  200.4 1.9 collective-permute-start.19
  203.5 3.1 %broadcast_in_dim.84.refs_7_ = bf16[64,256,128]{2,1,0:T(8,128)(2,1)} broadcast(bf16[]{:T(256)} %constant.106.clone.1), dimensions={} | broadcast | bytes 4194306 | tf_op jit(solution)/shard_map/broadcast_in_dim | solution.py:298
  206.5 6.2 %amplitudes.8 = (bf16[64,256,128]{2,1,0:T(8,128)(2,1)}, f32[8,8,128]{2,1,0:T(8,128)S(1)}) custom-call(s32[264]{0:T(512)S(1)} %concatenate.22.refs_0_, f32[64,128]{1,0:T(8,128)S(1)} %dynamic-slice_subtract_fusion.refs_1_, f32[16,256,128]{2,1,0:T(8,128)S(1)} %broadcast_in_dim.83.refs_2_, ...), custom_call_target="tpu_custom_call", output_to_operand_aliasing={{0}: (7, {})} | custom-call | flops 268435456 | bytes 4718592 | tf_op jit(solution)/shard_map/amplitudes/pallas_call | solution.py:175
  212.8 6.2 %amplitudes.9 = (bf16[64,256,128]{2,1,0:T(8,128)(2,1)}, f32[8,8,128]{2,1,0:T(8,128)S(1)}) custom-call(s32[264]{0:T(512)S(1)} %concatenate.22.refs_0_, f32[64,128]{1,0:T(8,128)S(1)} %dynamic-slice_subtract_fusion.refs_1_, f32[16,256,128]{2,1,0:T(8,128)S(1)} %broadcast_in_dim.83.refs_2_, ...), custom_call_target="tpu_custom_call", output_to_operand_aliasing={{0}: (7, {})} | custom-call | flops 268435456 | bytes 4718592 | tf_op jit(solution)/shard_map/amplitudes/pallas_call | solution.py:175
  219.0 6.2 %amplitudes.10 = (bf16[64,256,128]{2,1,0:T(8,128)(2,1)}, f32[8,8,128]{2,1,0:T(8,128)S(1)}) custom-call(s32[264]{0:T(512)S(1)} %concatenate.22.refs_0_, f32[64,128]{1,0:T(8,128)S(1)} %dynamic-slice_subtract_fusion.refs_1_, f32[16,256,128]{2,1,0:T(8,128)S(1)} %broadcast_in_dim.83.refs_2_, ...), custom_call_target="tpu_custom_call", output_to_operand_aliasing={{0}: (7, {})} | custom-call | flops 268435456 | bytes 4718592 | tf_op jit(solution)/shard_map/amplitudes/pallas_call | solution.py:175
  225.3 6.2 %amplitudes.11 = (bf16[64,256,128]{2,1,0:T(8,128)(2,1)}, f32[8,8,128]{2,1,0:T(8,128)S(1)}) custom-call(s32[264]{0:T(512)S(1)} %concatenate.22.refs_0_, f32[64,128]{1,0:T(8,128)S(1)} %dynamic-slice_subtract_fusion.refs_1_, f32[16,256,128]{2,1,0:T(8,128)S(1)} %broadcast_in_dim.83.refs_2_, ...), custom_call_target="tpu_custom_call", output_to_operand_aliasing={{0}: (7, {})} | custom-call | flops 268435456 | bytes 4718592 | tf_op jit(solution)/shard_map/amplitudes/pallas_call | solution.py:175
  231.6 6.2 %amplitudes.12 = (bf16[64,256,128]{2,1,0:T(8,128)(2,1)}, f32[8,8,128]{2,1,0:T(8,128)S(1)}) custom-call(s32[264]{0:T(512)S(1)} %concatenate.22.refs_0_, f32[64,128]{1,0:T(8,128)S(1)} %dynamic-slice_subtract_fusion.refs_1_, f32[16,256,128]{2,1,0:T(8,128)S(1)} %broadcast_in_dim.83.refs_2_, ...), custom_call_target="tpu_custom_call", output_to_operand_aliasing={{0}: (7, {})} | custom-call | flops 268435456 | bytes 4718592 | tf_op jit(solution)/shard_map/amplitudes/pallas_call | solution.py:175
  237.8 6.4 %amplitudes.13 = (bf16[64,256,128]{2,1,0:T(8,128)(2,1)}, f32[8,8,128]{2,1,0:T(8,128)S(1)}) custom-call(s32[264]{0:T(512)S(1)} %concatenate.22.refs_0_, f32[64,128]{1,0:T(8,128)S(1)} %dynamic-slice_subtract_fusion.refs_1_, f32[16,256,128]{2,1,0:T(8,128)S(1)} %broadcast_in_dim.83.refs_2_, ...), custom_call_target="tpu_custom_call", output_to_operand_aliasing={{0}: (7, {})} | custom-call | flops 268435456 | bytes 4718592 | tf_op jit(solution)/shard_map/amplitudes/pallas_call | solution.py:175
  244.3 6.2 %amplitudes.14 = (bf16[64,256,128]{2,1,0:T(8,128)(2,1)}, f32[8,8,128]{2,1,0:T(8,128)S(1)}) custom-call(s32[264]{0:T(512)S(1)} %concatenate.22.refs_0_, f32[64,128]{1,0:T(8,128)S(1)} %dynamic-slice_subtract_fusion.refs_1_, f32[16,256,128]{2,1,0:T(8,128)S(1)} %broadcast_in_dim.83.refs_2_, ...), custom_call_target="tpu_custom_call", output_to_operand_aliasing={{0}: (7, {})} | custom-call | flops 268435456 | bytes 4718592 | tf_op jit(solution)/shard_map/amplitudes/pallas_call | solution.py:175
  250.6 6.2 %amplitudes.15 = (bf16[64,256,128]{2,1,0:T(8,128)(2,1)}, f32[8,8,128]{2,1,0:T(8,128)S(1)}) custom-call(s32[264]{0:T(512)S(1)} %concatenate.22.refs_0_, f32[64,128]{1,0:T(8,128)S(1)} %dynamic-slice_subtract_fusion.refs_1_, f32[16,256,128]{2,1,0:T(8,128)S(1)} %broadcast_in_dim.83.refs_2_, ...), custom_call_target="tpu_custom_call", output_to_operand_aliasing={{0}: (7, {})} | custom-call | flops 268435456 | bytes 4718592 | tf_op jit(solution)/shard_map/amplitudes/pallas_call | solution.py:175
  256.8 9.8 %density_rows.3 = f32[16,128,256]{2,1,0:T(8,128)S(1)} custom-call(s32[1]{0:T(128)} %bitcast.24.start, bf16[64,256,128]{2,1,0:T(8,128)(2,1)} %get-tuple-element.33.t), custom_call_target="tpu_custom_call" | custom-call | flops 536870912 | bytes 6291456 | tf_op jit(solution)/shard_map/density_rows/pallas_call | solution.py:215
  267.3 3.6 %psum.7 = f32[64]{0:T(128)S(1)} all-reduce(f32[64]{0:T(128)S(1)} %select_reduce_fusion), channel_id=1, replica_groups=mesh['mol'=2,'orb'=8,'aux'=2] {'aux'}, use_global_device_ids=true, to_apply=%region_5.6 | all-reduce | flops 64 | bytes 512 | tf_op jit(solution)/shard_map/psum | solution.py:311
  270.9 9.8 %density_rows.2 = f32[16,128,256]{2,1,0:T(8,128)S(1)} custom-call(s32[1]{0:T(128)} %bitcast.23.start, bf16[64,256,128]{2,1,0:T(8,128)(2,1)} %get-tuple-element.33.t), custom_call_target="tpu_custom_call" | custom-call | flops 536870912 | bytes 6291456 | tf_op jit(solution)/shard_map/density_rows/pallas_call | solution.py:215
  281.2 3.2 %add.166 = f32[16,128,256]{2,1,0:T(8,128)} add(f32[16,128,256]{2,1,0:T(8,128)S(1)} %density_rows.2, f32[16,128,256]{2,1,0:T(8,128)} %collective-permute-done.20) | non-fusion elementwise | flops 524288 | bytes 6291456 | tf_op jit(solution)/shard_map/add | solution.py:306
  (124 shorter events, 22.6 us)
Async XLA Ops:
  3.5 9.4 %copy-start = (bf16[16,256,256]{1,2,0:T(8,128)(2,1)}, bf16[16,256,256]{1,2,0:T(8,128)(2,1)S(1)}, u32[]{:S(2)}) copy-start(bf16[16,256,256]{1,2,0:T(8,128)(2,1)S(1)} %copy.60) | copy-start | bytes 6291460
  3.5 5.0 %copy-start.24 = (s32[64,1]{0,1:T(1,128)S(1)}, s32[64,1]{0,1:T(1,128)}, u32[]{:S(2)}) copy-start(s32[64,1]{0,1:T(1,128)} %param.10) | copy-start | bytes 772
  3.5 5.2 %copy-start.22 = (s32[64]{0:T(128)S(1)}, s32[64]{0:T(128)}, u32[]{:S(2)}) copy-start(s32[64]{0:T(128)} %param.11) | copy-start | bytes 772
  3.5 7.0 %collective-permute-start = (bf16[16,256,256]{1,2,0:T(8,128)(2,1)S(1)}, bf16[16,256,256]{1,2,0:T(8,128)(2,1)}, u32[]{:S(2)}, u32[]{:S(2)}) collective-permute-start(bf16[16,256,256]{1,2,0:T(8,128)(2,1)S(1)} %copy.60), channel_id=1, source_target_pairs={{0,1},{1,0},{2,3},{3,2},{4,5},{5,4},{6,7},{7,6},{8,9},{9,8},{10,11... | collective-permute-start | bytes 6291464 | tf_op jit(solution)/shard_map/ppermute | solution.py:250
  4.0 12.3 %copy-start.23 = (s32[16]{0:T(128)S(1)}, s32[16]{0:T(128)}, u32[]{:S(2)}) copy-start(s32[16]{0:T(128)} %param.9) | copy-start | bytes 196
  4.0 12.4 %copy-start.21 = (f32[16]{0:T(128)S(1)}, f32[16]{0:T(128)}, u32[]{:S(2)}) copy-start(f32[16]{0:T(128)} %param.8) | copy-start | bytes 196
  4.1 12.6 %copy-start.20 = (f32[16,256]{1,0:T(8,128)S(1)}, f32[16,256]{1,0:T(8,128)}, u32[]{:S(2)}) copy-start(f32[16,256]{1,0:T(8,128)} %param.7) | copy-start | bytes 49156
  4.1 26.8 %collective-permute-start.1 = (bf16[16,256,128]{1,2,0:T(8,128)(2,1)S(1)}, bf16[16,256,128]{1,2,0:T(8,128)(2,1)}, u32[]{:S(2)}, u32[]{:S(2)}) collective-permute-start(bf16[16,256,128]{1,2,0:T(8,128)(2,1)S(1)} %constant_dynamic-slice_fusion.1), channel_id=1, source_target_pairs={{0,4},{2,6},{4,0},{6,2},{8,12},{10,14},{12,8},{14,10},{1,5},{3,7},... | collective-permute-start | bytes 3145736 | tf_op jit(solution)/shard_map/ppermute | solution.py:285
  6.8 48.1 %collective-permute-start.3 = (bf16[16,256,128]{1,2,0:T(8,128)(2,1)S(1)}, bf16[16,256,128]{1,2,0:T(8,128)(2,1)}, u32[]{:S(2)}, u32[]{:S(2)}) collective-permute-start(bf16[16,256,128]{1,2,0:T(8,128)(2,1)S(1)} %constant_dynamic-slice_fusion.1), channel_id=1, source_target_pairs={{4,8},{6,10},{8,4},{10,6},{5,9},{7,11},{9,5},{11,7},{20,24},{22,26... | collective-permute-start | bytes 3145736 | tf_op jit(solution)/shard_map/ppermute | solution.py:286
  8.8 123.0 %collective-permute-start.7 = (s32[64]{0:T(128)S(1)}, s32[64]{0:T(128)S(1)}, u32[]{:S(2)}, u32[]{:S(2)}) collective-permute-start(s32[64]{0:T(128)S(1)} %get-tuple-element.34), channel_id=1, source_target_pairs={{0,2},{2,0},{4,6},{6,4},{8,10},{10,8},{12,14},{14,12},{1,3},{3,1},... | collective-permute-start | bytes 776 | tf_op jit(solution)/shard_map/ppermute | solution.py:281
  12.9 40.3 %collective-permute-start.2 = (bf16[16,256,128]{1,2,0:T(8,128)(2,1)}, bf16[16,256,128]{1,2,0:T(8,128)(2,1)}, u32[]{:S(2)}, u32[]{:S(2)}) collective-permute-start(bf16[16,256,128]{1,2,0:T(8,128)(2,1)} %constant_dynamic-slice_fusion), channel_id=1, source_target_pairs={{0,4},{2,6},{4,0},{6,2},{8,12},{10,14},{12,8},{14,10},{1,5},{3,7},... | collective-permute-start | bytes 3145736 | tf_op jit(solution)/shard_map/ppermute | solution.py:285
  31.0 95.1 %collective-permute-start.10 = (bf16[16,256,128]{1,2,0:T(8,128)(2,1)}, bf16[16,256,128]{1,2,0:T(8,128)(2,1)}, u32[]{:S(2)}, u32[]{:S(2)}) collective-permute-start(bf16[16,256,128]{1,2,0:T(8,128)(2,1)} %collective-permute-done.1), channel_id=1, source_target_pairs={{4,8},{6,10},{8,4},{10,6},{5,9},{7,11},{9,5},{11,7},{20,24},{22,26... | collective-permute-start | bytes 3145736 | tf_op jit(solution)/shard_map/ppermute | solution.py:288
  32.7 95.4 %collective-permute-start.5 = (bf16[16,256,128]{1,2,0:T(8,128)(2,1)}, bf16[16,256,128]{1,2,0:T(8,128)(2,1)}, u32[]{:S(2)}, u32[]{:S(2)}) collective-permute-start(bf16[16,256,128]{1,2,0:T(8,128)(2,1)} %constant_dynamic-slice_fusion), channel_id=1, source_target_pairs={{4,8},{6,10},{8,4},{10,6},{5,9},{7,11},{9,5},{11,7},{20,24},{22,26... | collective-permute-start | bytes 3145736 | tf_op jit(solution)/shard_map/ppermute | solution.py:286
  53.2 76.2 %collective-permute-start.12 = (bf16[16,256,128]{1,2,0:T(8,128)(2,1)}, bf16[16,256,128]{1,2,0:T(8,128)(2,1)}, u32[]{:S(2)}, u32[]{:S(2)}) collective-permute-start(bf16[16,256,128]{1,2,0:T(8,128)(2,1)} %collective-permute-done.2), channel_id=1, source_target_pairs={{4,8},{6,10},{8,4},{10,6},{5,9},{7,11},{9,5},{11,7},{20,24},{22,26... | collective-permute-start | bytes 3145736 | tf_op jit(solution)/shard_map/ppermute | solution.py:288
  55.0 86.0 %collective-permute-start.4 = (bf16[16,256,128]{1,2,0:T(8,128)(2,1)}, bf16[16,256,128]{1,2,0:T(8,128)(2,1)}, u32[]{:S(2)}, u32[]{:S(2)}) collective-permute-start(bf16[16,256,128]{1,2,0:T(8,128)(2,1)} %collective-permute-done.3), channel_id=1, source_target_pairs={{4,0},{6,2},{8,12},{10,14},{5,1},{7,3},{9,13},{11,15},{20,16},{22,... | collective-permute-start | bytes 3145736 | tf_op jit(solution)/shard_map/ppermute | solution.py:287
  126.0 28.7 %collective-permute-start.11 = (bf16[16,256,128]{1,2,0:T(8,128)(2,1)}, bf16[16,256,128]{1,2,0:T(8,128)(2,1)}, u32[]{:S(2)}, u32[]{:S(2)}) collective-permute-start(bf16[16,256,128]{1,2,0:T(8,128)(2,1)} %collective-permute-done.10), channel_id=1, source_target_pairs={{4,0},{6,2},{8,12},{10,14},{5,1},{7,3},{9,13},{11,15},{20,16},{22,... | collective-permute-start | bytes 3145736 | tf_op jit(solution)/shard_map/ppermute | solution.py:289
  128.1 48.7 %collective-permute-start.6 = (bf16[16,256,128]{1,2,0:T(8,128)(2,1)}, bf16[16,256,128]{1,2,0:T(8,128)(2,1)}, u32[]{:S(2)}, u32[]{:S(2)}) collective-permute-start(bf16[16,256,128]{1,2,0:T(8,128)(2,1)} %collective-permute-done.5), channel_id=1, source_target_pairs={{4,0},{6,2},{8,12},{10,14},{5,1},{7,3},{9,13},{11,15},{20,16},{22,... | collective-permute-start | bytes 3145736 | tf_op jit(solution)/shard_map/ppermute | solution.py:287
  129.4 61.5 %collective-permute-start.13 = (bf16[16,256,128]{1,2,0:T(8,128)(2,1)}, bf16[16,256,128]{1,2,0:T(8,128)(2,1)}, u32[]{:S(2)}, u32[]{:S(2)}) collective-permute-start(bf16[16,256,128]{1,2,0:T(8,128)(2,1)} %collective-permute-done.12), channel_id=1, source_target_pairs={{4,0},{6,2},{8,12},{10,14},{5,1},{7,3},{9,13},{11,15},{20,16},{22,... | collective-permute-start | bytes 3145736 | tf_op jit(solution)/shard_map/ppermute | solution.py:289
  133.3 64.8 %collective-permute-start.8 = (bf16[8,256,128]{2,1,0:T(8,128)(2,1)}, bf16[8,256,128]{2,1,0:T(8,128)(2,1)}, u32[]{:S(2)}, u32[]{:S(2)}) collective-permute-start(bf16[8,256,128]{2,1,0:T(8,128)(2,1)} %pack.8), channel_id=1, source_target_pairs={{0,2},{2,0},{4,6},{6,4},{8,10},{10,8},{12,14},{14,12},{1,3},{3,1},... | collective-permute-start | bytes 1572872 | tf_op jit(solution)/shard_map/ppermute | solution.py:294
  136.4 0.8 copy-start.19
  138.8 4.2 %copy-start.6 = (bf16[16,256,128]{2,1,0:T(8,128)(2,1)}, bf16[16,256,128]{2,1,0:T(8,128)(2,1)S(1)}, u32[]{:S(2)}) copy-start(bf16[16,256,128]{2,1,0:T(8,128)(2,1)S(1)} %copy.64.refs_6_.refs_1_) | copy-start | bytes 3145732
  140.2 0.8 copy-start.18
  141.0 59.3 %collective-permute-start.14 = (bf16[8,256,128]{2,1,0:T(8,128)(2,1)}, bf16[8,256,128]{2,1,0:T(8,128)(2,1)}, u32[]{:S(2)}, u32[]{:S(2)}) collective-permute-start(bf16[8,256,128]{2,1,0:T(8,128)(2,1)} %copy-done.19), channel_id=1, source_target_pairs={{0,2},{2,0},{4,6},{6,4},{8,10},{10,8},{12,14},{14,12},{1,3},{3,1},... | collective-permute-start | bytes 1572872 | tf_op jit(solution)/shard_map/ppermute | solution.py:294
  148.3 0.8 copy-start.14
  151.4 1.2 copy-start.8
  153.9 0.8 copy-start.16
  154.7 45.6 %collective-permute-start.9 = (bf16[8,256,128]{2,1,0:T(8,128)(2,1)}, bf16[8,256,128]{2,1,0:T(8,128)(2,1)}, u32[]{:S(2)}, u32[]{:S(2)}) collective-permute-start(bf16[8,256,128]{2,1,0:T(8,128)(2,1)} %copy-done.18), channel_id=1, source_target_pairs={{0,2},{2,0},{4,6},{6,4},{8,10},{10,8},{12,14},{14,12},{1,3},{3,1},... | collective-permute-start | bytes 1572872 | tf_op jit(solution)/shard_map/ppermute | solution.py:294
  159.3 1.2 copy-start.4
  161.9 0.8 copy-start.15
  176.8 67.5 %collective-permute-start.16 = (bf16[8,256,128]{2,1,0:T(8,128)(2,1)}, bf16[8,256,128]{2,1,0:T(8,128)(2,1)}, u32[]{:S(2)}, u32[]{:S(2)}) collective-permute-start(bf16[8,256,128]{2,1,0:T(8,128)(2,1)} %copy-done.14), channel_id=1, source_target_pairs={{0,2},{2,0},{4,6},{6,4},{8,10},{10,8},{12,14},{14,12},{1,3},{3,1},... | collective-permute-start | bytes 1572872 | tf_op jit(solution)/shard_map/ppermute | solution.py:294
  181.4 1.2 copy-start.12
  184.0 0.8 copy-start.17
  190.9 40.6 %collective-permute-start.15 = (bf16[8,256,128]{2,1,0:T(8,128)(2,1)}, bf16[8,256,128]{2,1,0:T(8,128)(2,1)}, u32[]{:S(2)}, u32[]{:S(2)}) collective-permute-start(bf16[8,256,128]{2,1,0:T(8,128)(2,1)} %copy-done.16), channel_id=1, source_target_pairs={{0,2},{2,0},{4,6},{6,4},{8,10},{10,8},{12,14},{14,12},{1,3},{3,1},... | collective-permute-start | bytes 1572872 | tf_op jit(solution)/shard_map/ppermute | solution.py:294
  195.5 1.2 copy-start.10
  198.2 52.3 %collective-permute-start.18 = (bf16[8,256,128]{2,1,0:T(8,128)(2,1)}, bf16[8,256,128]{2,1,0:T(8,128)(2,1)}, u32[]{:S(2)}, u32[]{:S(2)}) collective-permute-start(bf16[8,256,128]{2,1,0:T(8,128)(2,1)} %copy-done.15), channel_id=1, source_target_pairs={{0,2},{2,0},{4,6},{6,4},{8,10},{10,8},{12,14},{14,12},{1,3},{3,1},... | collective-permute-start | bytes 1572872 | tf_op jit(solution)/shard_map/ppermute | solution.py:294
  200.3 44.0 %collective-permute-start.17 = (bf16[8,256,128]{2,1,0:T(8,128)(2,1)}, bf16[8,256,128]{2,1,0:T(8,128)(2,1)}, u32[]{:S(2)}, u32[]{:S(2)}) collective-permute-start(bf16[8,256,128]{2,1,0:T(8,128)(2,1)} %copy-done.17), channel_id=1, source_target_pairs={{0,2},{2,0},{4,6},{6,4},{8,10},{10,8},{12,14},{14,12},{1,3},{3,1},... | collective-permute-start | bytes 1572872 | tf_op jit(solution)/shard_map/ppermute | solution.py:294
  200.4 50.2 %collective-permute-start.19 = (bf16[8,256,128]{2,1,0:T(8,128)(2,1)}, bf16[8,256,128]{2,1,0:T(8,128)(2,1)}, u32[]{:S(2)}, u32[]{:S(2)}) collective-permute-start(bf16[8,256,128]{2,1,0:T(8,128)(2,1)} %pack.15), channel_id=1, source_target_pairs={{0,2},{2,0},{4,6},{6,4},{8,10},{10,8},{12,14},{14,12},{1,3},{3,1},... | collective-permute-start | bytes 1572872 | tf_op jit(solution)/shard_map/ppermute | solution.py:294
  203.5 3.1 %copy-start.7 = (bf16[16,256,128]{2,1,0:T(8,128)(2,1)S(1)}, bf16[16,256,128]{2,1,0:T(8,128)(2,1)}, u32[]{:S(2)}) copy-start(bf16[16,256,128]{2,1,0:T(8,128)(2,1)} %copy-done.6) | copy-start | bytes 3145732
  206.5 6.2 %copy-start.9 = (bf16[16,256,128]{2,1,0:T(8,128)(2,1)S(1)}, bf16[16,256,128]{2,1,0:T(8,128)(2,1)}, u32[]{:S(2)}) copy-start(bf16[16,256,128]{2,1,0:T(8,128)(2,1)} %copy.66.refs_6_.refs_1_) | copy-start | bytes 3145732
  212.8 6.2 %copy-start.1 = (bf16[16,256,256]{1,2,0:T(8,128)(2,1)S(1)}, bf16[16,256,256]{1,2,0:T(8,128)(2,1)}, u32[]{:S(2)}) copy-start(bf16[16,256,256]{1,2,0:T(8,128)(2,1)} %copy-done) | copy-start | bytes 6291460
  219.0 6.2 %copy-start.13 = (bf16[16,256,128]{2,1,0:T(8,128)(2,1)S(1)}, bf16[16,256,128]{2,1,0:T(8,128)(2,1)}, u32[]{:S(2)}) copy-start(bf16[16,256,128]{2,1,0:T(8,128)(2,1)} %copy.70.refs_6_.refs_1_) | copy-start | bytes 3145732
  225.3 6.3 %copy-start.2 = (bf16[16,256,256]{1,2,0:T(8,128)(2,1)S(1)}, bf16[16,256,256]{1,2,0:T(8,128)(2,1)}, u32[]{:S(2)}) copy-start(bf16[16,256,256]{1,2,0:T(8,128)(2,1)} %copy-done) | copy-start | bytes 6291460
  231.5 6.3 %copy-start.5 = (bf16[16,256,128]{2,1,0:T(8,128)(2,1)S(1)}, bf16[16,256,128]{2,1,0:T(8,128)(2,1)}, u32[]{:S(2)}) copy-start(bf16[16,256,128]{2,1,0:T(8,128)(2,1)} %copy.73.refs_5_.refs_1_) | copy-start | bytes 3145732
  231.6 6.3 %copy-start.11 = (bf16[16,256,128]{2,1,0:T(8,128)(2,1)S(1)}, bf16[16,256,128]{2,1,0:T(8,128)(2,1)}, u32[]{:S(2)}) copy-start(bf16[16,256,128]{2,1,0:T(8,128)(2,1)} %copy.74.refs_6_.refs_1_) | copy-start | bytes 3145732
  237.8 6.5 %copy-start.3 = (bf16[16,256,256]{1,2,0:T(8,128)(2,1)S(1)}, bf16[16,256,256]{1,2,0:T(8,128)(2,1)}, u32[]{:S(2)}) copy-start(bf16[16,256,256]{1,2,0:T(8,128)(2,1)} %copy-done) | copy-start | bytes 6291460
  266.6 14.6 %collective-permute-start.20 = (f32[16,128,256]{2,1,0:T(8,128)S(1)}, f32[16,128,256]{2,1,0:T(8,128)}, u32[]{:S(2)}, u32[]{:S(2)}) collective-permute-start(f32[16,128,256]{2,1,0:T(8,128)S(1)} %density_rows.3), channel_id=1, source_target_pairs={{0,1},{1,0},{2,3},{3,2},{4,5},{5,4},{6,7},{7,6},{8,9},{9,8},{10,11... | collective-permute-start | bytes 6291464 | tf_op jit(solution)/shard_map/ppermute | solution.py:305

commit v2 on v1

--- a/solution.py
+++ b/solution.py
@@ -6,7 +6,7 @@
 from jax.sharding import PartitionSpec as P
 
 f32, bf16, i32 = jnp.float32, jnp.bfloat16, jnp.int32
-ANY = pl.BlockSpec(memory_space=pl.ANY)
+HBM = pl.BlockSpec(memory_space=pltpu.HBM)
 SMEM = pl.BlockSpec(memory_space=pltpu.SMEM)
 VMEM = pl.BlockSpec(memory_space=pltpu.VMEM)
 LIMIT = 48 * 1024 * 1024
@@ -90,47 +90,80 @@
 
 
 def table_of(bases, fields):
-    return jnp.concatenate([bases] + fields).astype(i32)
-
-
-def pack_kernel(call, cap, count, tbl, x, out, sems):
+    return jnp.concatenate([bases] + [x.astype(i32) for x in fields])
+
+
+def pack_kernel(call, cap, tbl, *refs):
+    sources, out, sems = refs[:-2], refs[-2], refs[-1]
     base = tbl[call]
-    copies = []
-    for r in range(cap):
-        slot = tbl[8 + base + r]
-        copies.append(pltpu.make_async_copy(x.at[slot], out.at[r], sems.at[r]))
-        copies[-1].start()
-    for copy in copies:
-        copy.wait()
-
-
-def pack(tbl, call, x, cap):
+
+    def move(x):
+        copies = []
+        for r in range(cap):
+            slot = tbl[9 + base + r]
+            copies.append(pltpu.make_async_copy(x.at[slot], out.at[r], sems.at[r]))
+            copies[-1].start()
+        for copy in copies:
+            copy.wait()
+
+    by_place(tbl, sources, move)
+
+
+def by_place(tbl, sources, act):
+    if len(sources) == 1:
+        act(*sources)
+    else:
+        pl.when(tbl[8] == 1)(lambda: act(sources[0]))
+        pl.when(tbl[8] == 0)(lambda: act(sources[1]))
+
+
+def pack(tbl, call, sources, cap):
+    x = sources[0]
     return pl.pallas_call(
-        lambda *refs: pack_kernel(call, cap, 64, *refs),
+        lambda *refs: pack_kernel(call, cap, *refs),
         out_shape=jax.ShapeDtypeStruct((cap,) + x.shape[1:], x.dtype),
-        in_specs=[SMEM, ANY],
-        out_specs=ANY,
+        in_specs=[SMEM] + [HBM] * len(sources),
+        out_specs=HBM,
         scratch_shapes=[pltpu.SemaphoreType.DMA((cap,))],
         compiler_params=pltpu.CompilerParams(vmem_limit_bytes=LIMIT),
         cost_estimate=pl.CostEstimate(
             flops=0, bytes_accessed=2 * cap * x.shape[1] * x.shape[2] * 2, transcendentals=0
         ),
         name="pack",
-    )(tbl, x)
-
-
-def amplitudes_kernel(
-    call, by_slot, per_orb, tbl, rows, vcol, a0, a1, j0, j1, tin, tout, energy,
-    sv, s0, s1, b0, b1, st, sem, sem_out,
-):
+    )(tbl, *sources)
+
+
+def turn_kernel(x, out):
+    for r in range(x.shape[0]):
+        out[r] = x[r].T
+
+
+def turn(x):
+    count, rows, cols = x.shape
+    step = 4 if count % 4 == 0 else 1
+    return pl.pallas_call(
+        turn_kernel,
+        out_shape=jax.ShapeDtypeStruct((count, cols, rows), x.dtype),
+        grid=(count // step,),
+        in_specs=[pl.BlockSpec((step, rows, cols), lambda i: (i, 0, 0))],
+        out_specs=pl.BlockSpec((step, cols, rows), lambda i: (i, 0, 0)),
+        compiler_params=pltpu.CompilerParams(vmem_limit_bytes=LIMIT),
+        cost_estimate=pl.CostEstimate(
+            flops=0, bytes_accessed=2 * count * rows * cols * 2, transcendentals=0
+        ),
+        name="turn",
+    )(x)
+
+
+def amplitudes_kernel(call, by_slot, per_orb, places, tbl, rows, vcol, a0, a1, *refs):
+    js, (tin, tout, energy, sv, s0, s1, b0, b1, st, sem, sem_out) = refs[:-11], refs[-11:]
     cap = sv.shape[0]
     n = rows.shape[0]
     base = tbl[call]
-    loads = []
-    for r in range(cap):
-        p = tbl[8 + base + r]
-        i = lax.div(p, per_orb)
-        slot = tbl[8 + n + base + r] if by_slot else r
+
+    def loads_of(r, j0, j1):
+        i = lax.div(tbl[9 + base + r], per_orb)
+        slot = tbl[9 + n + base + r] if by_slot else r
         pairs = (
             (vcol.at[i], sv.at[r]),
             (a0.at[i], s0.at[r]),
@@ -138,48 +171,52 @@
             (j0.at[slot], b0.at[r]),
             (j1.at[slot], b1.at[r]),
         )
-        group = []
-        for k, (source, target) in enumerate(pairs):
-            copy = pltpu.make_async_copy(source, target, sem.at[r, k])
+        return [pltpu.make_async_copy(x, to, sem.at[r, k]) for k, (x, to) in enumerate(pairs)]
+
+    def load(j):
+        copies = [copy for r in range(cap) for copy in loads_of(r, *j)]
+        for copy in copies:
             copy.start()
-            group.append(copy)
-        loads.append(group)
+        for copy in copies:
+            copy.wait()
+
+    by_place(tbl, [js[2 * k : 2 * k + 2] for k in range(places)], load)
     nvd, half = sv.shape[1], sv.shape[2]
     live_a = lax.broadcasted_iota(i32, (nvd, half), 0)
     live_b = lax.broadcasted_iota(i32, (nvd, half), 1)
     row8 = rows[pl.ds(pl.multiple_of(base, cap), cap), :]
-    stores = []
     for r in range(cap):
-        p = tbl[8 + base + r]
-        size_i = tbl[8 + 2 * n + base + r]
-        size_j = tbl[8 + 3 * n + base + r]
-        for copy in loads[r]:
-            copy.wait()
+        size_i = tbl[9 + 2 * n + base + r]
+        size_j = tbl[9 + 3 * n + base + r]
         k = jnp.dot(s0[r], b0[r], preferred_element_type=f32)
         k += jnp.dot(s1[r], b1[r], preferred_element_type=f32)
         k = jnp.where((live_a < size_i) & (live_b < size_j), k, 0.0)
         gap = sv[r] + row8[r : r + 1, :]
         t = (-k / gap).astype(bf16)
         st[r] = t
-        copy = pltpu.make_async_copy(st.at[r], tout.at[p], sem_out.at[r])
+        energy[r] = jnp.sum((k * t.astype(f32)).reshape(nvd // 8, 8, half), axis=0)
+    stores = [
+        pltpu.make_async_copy(st.at[r], tout.at[tbl[9 + base + r]], sem_out.at[r])
+        for r in range(cap)
+    ]
+    for copy in stores:
         copy.start()
-        stores.append(copy)
-        energy[r] = jnp.sum((k * t.astype(f32)).reshape(nvd // 8, 8, half), axis=0)
     for copy in stores:
         copy.wait()
 
 
-def amplitudes(call, by_slot, per_orb, tbl, rows, vcol, a0, a1, j0, j1, t_all, cap):
+def amplitudes(call, by_slot, per_orb, tbl, rows, vcol, left, sources, t_all, cap):
     nvd, half = vcol.shape[1:]
-    qa = j0.shape[1]
+    qa = left[0].shape[2]
+    blocks = [x for pair in sources for x in pair]
     return pl.pallas_call(
-        lambda *refs: amplitudes_kernel(call, by_slot, per_orb, *refs),
+        lambda *refs: amplitudes_kernel(call, by_slot, per_orb, len(sources), *refs),
         out_shape=(
             jax.ShapeDtypeStruct(t_all.shape, t_all.dtype),
             jax.ShapeDtypeStruct((cap, 8, half), f32),
         ),
-        in_specs=[SMEM, VMEM, ANY, ANY, ANY, ANY, ANY, ANY],
-        out_specs=(ANY, VMEM),
+        in_specs=[SMEM, VMEM, HBM, HBM, HBM] + [HBM] * len(blocks) + [HBM],
+        out_specs=(HBM, VMEM),
         scratch_shapes=[
             pltpu.VMEM((cap, nvd, half), f32),
             pltpu.VMEM((cap, nvd, qa), bf16),
@@ -190,7 +227,7 @@
             pltpu.SemaphoreType.DMA((cap, 5)),
             pltpu.SemaphoreType.DMA((cap,)),
         ],
-        input_output_aliases={7: 0},
+        input_output_aliases={5 + len(blocks): 0},
         compiler_params=pltpu.CompilerParams(vmem_limit_bytes=LIMIT),
         cost_estimate=pl.CostEstimate(
             flops=cap * 4 * nvd * qa * half,
@@ -198,28 +235,32 @@
             transcendentals=0,
         ),
         name="amplitudes",
-    )(tbl, rows, vcol, a0, a1, j0, j1, t_all)
+    )(tbl, rows, vcol, *left, *blocks, t_all)
 
 
 def density_kernel(start, t, d):
-    half = d.shape[1]
+    count, half = d.shape[:2]
+    per_orb = t.shape[0] // count
     first = pl.multiple_of(start[0], half)
-    left = jnp.concatenate([t[k, pl.ds(first, half), :] for k in range(t.shape[0])], axis=1)
-    right = jnp.concatenate([t[k] for k in range(t.shape[0])], axis=1)
-    d[0] = lax.dot_general(left, right, (((1,), (1,)), ((), ())), preferred_element_type=f32)
+    for o in range(count):
+        own = range(o * per_orb, (o + 1) * per_orb)
+        left = jnp.concatenate([t[k, pl.ds(first, half), :] for k in own], axis=1)
+        right = jnp.concatenate([t[k] for k in own], axis=1)
+        d[o] = lax.dot_general(left, right, (((1,), (1,)), ((), ())), preferred_element_type=f32)
 
 
 def density_rows(t_all, start, per_orb, half):
     npair, nvd, width = t_all.shape
     occ = npair // per_orb
+    step = 4 if occ % 4 == 0 else 1
     return pl.pallas_call(
         density_kernel,
         out_shape=jax.ShapeDtypeStruct((occ, half, nvd), f32),
         grid_spec=pltpu.PrefetchScalarGridSpec(
             num_scalar_prefetch=1,
-            grid=(occ,),
-            in_specs=[pl.BlockSpec((per_orb, nvd, width), lambda i, s: (i, 0, 0))],
-            out_specs=pl.BlockSpec((1, half, nvd), lambda i, s: (i, 0, 0)),
+            grid=(occ // step,),
+            in_specs=[pl.BlockSpec((step * per_orb, nvd, width), lambda i, s: (i, 0, 0))],
+            out_specs=pl.BlockSpec((step, half, nvd), lambda i, s: (i, 0, 0)),
         ),
         compiler_params=pltpu.CompilerParams(vmem_limit_bytes=LIMIT),
         cost_estimate=pl.CostEstimate(
@@ -266,8 +307,11 @@
         ],
         axis=1,
     )
-    every = lax.all_gather(small, "orb", axis=0, tiled=True)
-    theirs = jnp.take(every, (pairs // cap) * occ + slots, axis=0)
+    every = small[None]
+    for bit in (1, 2, 4):
+        got = lax.ppermute(every, "orb", [(o, o ^ bit) for o in range(peers)])
+        every = jnp.concatenate([every, got])
+    theirs = jnp.take(every.reshape(peers * occ, -1), ((pairs // cap) ^ me) * occ + slots, axis=0)
     mine = jnp.take(small, order // per_orb, axis=0)
     rows = lax.dynamic_slice_in_dim(theirs, col0, half, 1) - (
         theirs[:, nvd : nvd + 1] + mine[:, nvd : nvd + 1]
@@ -277,30 +321,28 @@
     lower = z < 2
     column = jnp.stack([z, z ^ 1, jnp.where(lower, 2, 1), jnp.where(lower, 3, 0)])
     bases = jnp.concatenate([column * 2 + y, column * 2 + (1 - y)]) * cap
-    tbl = table_of(bases, [order, slots, size_i, size_j])
-    wanted = table_of(bases, [lax.ppermute(slots, "orb", swap_y)])
+    tbl = table_of(bases, [middle[None], order, slots, size_i, size_j])
+    wanted = table_of(bases, [middle[None], lax.ppermute(slots, "orb", swap_y)])
     vcol = jnp.broadcast_to(vir_energy[:, :, None], (occ, nvd, half))
-    left = [jnp.swapaxes(x, 1, 2) for x in (blocks, other)]
+    left = [turn(x) for x in (blocks, other)]
 
     near = [lax.ppermute(x, "orb", swap_half) for x in own]
     mid = [lax.ppermute(x, "orb", cross) for x in own]
     mid_out = [lax.ppermute(x, "orb", outward) for x in mid]
     far = [lax.ppermute(x, "orb", cross) for x in near]
     far_out = [lax.ppermute(x, "orb", outward) for x in far]
-    third = [jnp.where(middle, a, b) for a, b in zip(mid, mid_out)]
-    fourth = [jnp.where(middle, a, b) for a, b in zip(far, far_out)]
-    sources = [own, near, third, fourth]
+    sources = [[own], [near], [mid, mid_out], [far, far_out]]
     beside = [
-        [lax.ppermute(pack(wanted, k, x, cap), "orb", swap_y) for x in source]
+        [lax.ppermute(pack(wanted, k, x, cap), "orb", swap_y) for x in zip(*source)]
         for k, source in enumerate(sources)
     ]
 
     t_all = jnp.zeros((pair_dev, nvd, half), bf16)
     energies = [None] * 8
     for k in (0, 1, 4, 2, 5, 3, 6, 7):
-        j0, j1 = sources[k] if k < 4 else beside[k - 4]
+        source = sources[k] if k < 4 else [beside[k - 4]]
         t_all, energies[k] = amplitudes(
-            k, k < 4, per_orb, tbl, rows, vcol, left[0], left[1], j0, j1, t_all, cap
+            k, k < 4, per_orb, tbl, rows, vcol, left, source, t_all, cap
         )
     away = lax.ppermute(density_rows(t_all, (1 - core) * half, per_orb, half), "aux", swap_core)
     density = density_rows(t_all, core * half, per_orb, half) + away
@@ -308,7 +350,8 @@
     sums = jnp.sum(jnp.stack(energies), axis=(2, 3)).reshape(pair_dev)
     place = (bases[:, None] + jnp.arange(cap, dtype=i32)[None, :]).reshape(pair_dev)
     spot = target[:, None] == place[None, :]
-    energy = lax.psum(jnp.sum(jnp.where(spot, sums[None, :], 0.0), axis=1), "aux") / nvd
+    energy = jnp.sum(jnp.where(spot, sums[None, :], 0.0), axis=1)
+    energy = (energy + lax.ppermute(energy, "aux", swap_core)) / nvd
     return (energy, density)
 
 

time: 286 us -> 342 us (1.20)
  Pallas kernels: 80.6 us -> 166 us
  blocking collectives: 72.6 us -> 0 us
  starting transfers between devices: 26.6 us -> 76.5 us
  waiting for transfers between devices: 53.4 us -> 76.2 us
  local copies, waits for them, and re-layouts: 35.1 us -> 12.9 us
  other arithmetic: 14.8 us -> 7.82 us
    pallas_call x16 -> x18, Pallas kernels: 61 us -> 158 us  [the longest x8 109 us: pack(): pl.pallas_call(lambda *refs: pack_kernel(call, cap, *refs), out_shape=jax...]
    all_gather x1 -> x0, blocking collectives: 69 us -> none  [line_plan(): every = lax.all_gather(small, 'orb', axis=0, tiled=True)]
    ppermute x1 -> x5, starting transfers between devices: 1.58 us -> 49.6 us  [the longest x3 47.5 us: line_plan(): got = lax.ppermute(every, 'orb', [(o, o ^ bit) for o in range(peers)])]
    ppermute x1 -> x5, waiting for transfers between devices: 0.01 us -> 41.9 us  [the longest x3 39.9 us: line_plan(): got = lax.ppermute(every, 'orb', [(o, o ^ bit) for o in range(peers)])]
    ppermute x2, waiting for transfers between devices: 14.1 us -> 0.01 us  [line_plan(): mid_out = [lax.ppermute(x, 'orb', outward) for x in mid]]
    pallas_call x2, Pallas kernels: 19.7 us -> 7.98 us  [density_rows(): pl.pallas_call(density_kernel, out_shape=jax.ShapeDtypeStruct((occ, half,...]
    select_n x6 -> x2, other arithmetic: 9.38 us -> 0.73 us  [line_plan(): jnp.take(every.reshape(peers * occ, -1), (pairs // cap ^ me) * occ + slot...]
    select_n x4 -> x0, local copies, waits for them, and re-layouts: 8.45 us -> none  [the longest x2 4.55 us: line_plan(): fourth = [jnp.where(middle, a, b) for a, b in zip(far, far_out)]]
  transfers between devices with their start and end apart: 21 -> 25, of which waited for: 4 -> 4; matrix products, arithmetic and copies ran while one was open for 12% -> 4% of each run, Pallas kernels for 23% -> 46%
where the time goes in v2:
time: 342 us; the launch traced here: 341 us
  Pallas kernels  166 us (49%)
  starting transfers between devices  76.5 us (22%)
  waiting for transfers between devices  76.2 us (22%)
  local copies, waits for them, and re-layouts  12.9 us (4%)
  other arithmetic  7.82 us (2%)
    pallas_call x8, Pallas kernels, pack(): pl.pallas_call(lambda *refs: pack_kernel(call, cap, *refs), out_shape=jax...  109 us
    ppermute x3, starting transfers between devices, line_plan(): got = lax.ppermute(every, 'orb', [(o, o ^ bit) for o in range(peers)])  47.5 us
    pallas_call x8, Pallas kernels, amplitudes(): pl.pallas_call(lambda *refs: amplitudes_kernel(call, by_slot, per_orb, le...  45.9 us
    ppermute x3, waiting for transfers between devices, line_plan(): got = lax.ppermute(every, 'orb', [(o, o ^ bit) for o in range(peers)])  39.9 us
    ppermute x2, waiting for transfers between devices, line_plan(): near = [lax.ppermute(x, 'orb', swap_half) for x in own]  34.3 us
    ppermute x8, starting transfers between devices, line_plan(): lax.ppermute(pack(wanted, k, x, cap), 'orb', swap_y)  8.37 us
    pallas_call x2, Pallas kernels, density_rows(): pl.pallas_call(density_kernel, out_shape=jax.ShapeDtypeStruct((occ, half,...  7.98 us
    ppermute x2, starting transfers between devices, line_plan(): near = [lax.ppermute(x, 'orb', swap_half) for x in own]  7.06 us
  transfers between devices with their start and end apart: 25, of which 4 were waited for; matrix products, arithmetic and copies ran while one was open for 4% of the time, Pallas kernels for 46%

profile of v2, /device:TPU:0, one launch (start us, length us, event | category | flops | bytes accessed | tf_op | source)
XLA Modules:
  0.0 340.8 jit_solution(1273801051679775872)
XLA Ops:
  1.2 1.3 constant_dynamic-slice_fusion.1.refs_5_.refs_1_
  2.5 2.7 collective-permute-start.4
  6.2 1.5 collective-permute-start
  8.0 1.3 constant_dynamic-slice_fusion.refs_6_.refs_1_
  9.3 4.4 %collective-permute-start.5 = (bf16[16,256,128]{2,1,0:T(8,128)(2,1)S(1)}, bf16[16,256,128]{2,1,0:T(8,128)(2,1)}, u32[]{:S(2)}, u32[]{:S(2)}) collective-permute-start(bf16[16,256,128]{2,1,0:T(8,128)(2,1)S(1)} %constant_dynamic-slice_fusion.refs_6_.refs_1_), channel_id=1, source_target_pairs={{0,4},{2,6},{4,0},{6,2},{8,12},{10,14},{12,8},{14,10},{1,5},{3,7},... | collective-permute-start | bytes 3145736 | tf_op jit(solution)/shard_map/ppermute | solution.py:329
  13.8 15.5 %collective-permute-done.4.refs_5_.refs_1_ = bf16[16,256,128]{2,1,0:T(8,128)(2,1)} collective-permute-done((bf16[16,256,128]{2,1,0:T(8,128)(2,1)S(1)}, bf16[16,256,128]{2,1,0:T(8,128)(2,1)}, u32[]{:S(2)}, u32[]{:S(2)}) %collective-permute-start.4) | collective-permute-done | bytes 1048608 | tf_op jit(solution)/shard_map/ppermute | solution.py:329
  29.3 1.7 collective-permute-start.13
  31.1 1.7 collective-permute-start.7
  32.8 18.8 %collective-permute-done.5.refs_6_.refs_1_ = bf16[16,256,128]{2,1,0:T(8,128)(2,1)} collective-permute-done((bf16[16,256,128]{2,1,0:T(8,128)(2,1)S(1)}, bf16[16,256,128]{2,1,0:T(8,128)(2,1)}, u32[]{:S(2)}, u32[]{:S(2)}) %collective-permute-start.5) | collective-permute-done | bytes 1048608 | tf_op jit(solution)/shard_map/ppermute | solution.py:329
  51.6 1.7 collective-permute-start.14
  53.9 1.3 collective-permute-start.8
  55.2 1.3 collective-permute-start.15
  57.4 1.3 collective-permute-start.9
  58.7 1.3 collective-permute-start.16
  60.7 45.1 %collective-permute-start.1 = (f32[2,16,384]{2,1,0:T(8,128)S(1)}, f32[2,16,384]{2,1,0:T(8,128)S(1)}, u32[]{:S(2)}, u32[]{:S(2)}) collective-permute-start(f32[2,16,384]{2,1,0:T(8,128)S(1)} %pad_maximum_fusion.2), channel_id=1, source_target_pairs={{0,4},{2,6},{4,0},{6,2},{8,12},{10,14},{12,8},{14,10},{1,5},{3,7},... | collective-permute-start | bytes 147464 | tf_op jit(solution)/shard_map/ppermute | solution.py:312
  105.7 1.6 copy-done.8
  107.3 0.8 turn.2.refs_3_
  108.1 1.3 copy-done
  110.1 39.8 %collective-permute-done.1 = f32[2,16,384]{2,1,0:T(8,128)S(1)} collective-permute-done((f32[2,16,384]{2,1,0:T(8,128)S(1)}, f32[2,16,384]{2,1,0:T(8,128)S(1)}, u32[]{:S(2)}, u32[]{:S(2)}) %collective-permute-start.1) | collective-permute-done | bytes 49184 | tf_op jit(solution)/shard_map/ppermute | solution.py:312
  149.9 1.5 collective-permute-start.10
  151.4 2.0 collective-permute-done.10
  153.4 0.9 collective-permute-start.2
  154.4 1.4 pack.8
  155.9 17.6 %pack.10 = bf16[8,256,128]{2,1,0:T(8,128)(2,1)} custom-call(s32[73]{0:T(128)S(1)} %pad_add_fusion.refs_0_, bf16[16,256,128]{2,1,0:T(8,128)(2,1)} %collective-permute-done.4.refs_5_.refs_1_), custom_call_target="tpu_custom_call" | custom-call | bytes 1048576 | tf_op jit(solution)/shard_map/pack/pallas_call | solution.py:122
  173.5 1.4 pack.9
  174.9 1.6 collective-permute-start.11
  177.0 1.5 collective-permute-start.12
  180.5 17.6 %pack.12 = bf16[8,256,128]{2,1,0:T(8,128)(2,1)} custom-call(s32[73]{0:T(128)S(1)} %pad_add_fusion.refs_0_, bf16[16,256,128]{2,1,0:T(8,128)(2,1)S(1)} %collective-permute-done.6.refs_5_.refs_1_, bf16[16,256,128]{2,1,0:T(8,128)(2,1)} %collective-permute-done.8.refs_7_.refs_2_), custom_call_target="tpu_custom_call" | custom-call | bytes 1048576 | tf_op jit(solution)/shard_map/pack/pallas_call | solution.py:122
  198.2 17.6 %pack.11 = bf16[8,256,128]{2,1,0:T(8,128)(2,1)} custom-call(s32[73]{0:T(128)S(1)} %pad_add_fusion.refs_0_, bf16[16,256,128]{2,1,0:T(8,128)(2,1)} %collective-permute-done.5.refs_6_.refs_1_), custom_call_target="tpu_custom_call" | custom-call | bytes 1048576 | tf_op jit(solution)/shard_map/pack/pallas_call | solution.py:122
  215.8 17.7 %pack.14 = bf16[8,256,128]{2,1,0:T(8,128)(2,1)} custom-call(s32[73]{0:T(128)S(1)} %pad_add_fusion.refs_0_, bf16[16,256,128]{2,1,0:T(8,128)(2,1)} %collective-permute-done.13.refs_5_.refs_1_, bf16[16,256,128]{2,1,0:T(8,128)(2,1)} %collective-permute-done.15.refs_7_.refs_2_), custom_call_target="tpu_custom_call" | custom-call | bytes 1048576 | tf_op jit(solution)/shard_map/pack/pallas_call | solution.py:122
  234.0 17.7 %pack.13 = bf16[8,256,128]{2,1,0:T(8,128)(2,1)} custom-call(s32[73]{0:T(128)S(1)} %pad_add_fusion.refs_0_, bf16[16,256,128]{2,1,0:T(8,128)(2,1)} %collective-permute-done.7.refs_6_.refs_1_, bf16[16,256,128]{2,1,0:T(8,128)(2,1)} %collective-permute-done.9.refs_8_.refs_2_), custom_call_target="tpu_custom_call" | custom-call | bytes 1048576 | tf_op jit(solution)/shard_map/pack/pallas_call | solution.py:122
  251.7 1.6 collective-permute-start.18
  253.3 17.7 %pack.15 = bf16[8,256,128]{2,1,0:T(8,128)(2,1)} custom-call(s32[73]{0:T(128)S(1)} %pad_add_fusion.refs_0_, bf16[16,256,128]{2,1,0:T(8,128)(2,1)} %collective-permute-done.14.refs_6_.refs_1_, bf16[16,256,128]{2,1,0:T(8,128)(2,1)} %collective-permute-done.16.refs_8_.refs_2_), custom_call_target="tpu_custom_call" | custom-call | bytes 1048576 | tf_op jit(solution)/shard_map/pack/pallas_call | solution.py:122
  271.5 1.5 collective-permute-start.20
  274.0 2.7 turn.3.refs_4_
  276.8 1.4 copy-done.4
  278.8 3.0 broadcast_in_dim.90.refs_7_
  281.7 6.1 %amplitudes.8 = (bf16[64,256,128]{2,1,0:T(8,128)(2,1)}, f32[8,8,128]{2,1,0:T(8,128)S(1)}) custom-call(s32[265]{0:T(512)S(1)} %concatenate.36.refs_0_, f32[64,128]{1,0:T(8,128)S(1)} %dynamic-slice_subtract_fusion.refs_1_, f32[16,256,128]{2,1,0:T(8,128)S(1)} %broadcast_in_dim.89.refs_2_, ...), custom_call_target="tpu_custom_call", output_to_operand_aliasing={{0}: (7, {})} | custom-call | flops 268435456 | bytes 4718592 | tf_op jit(solution)/shard_map/amplitudes/pallas_call | solution.py:212
  287.8 5.0 %amplitudes.9 = (bf16[64,256,128]{2,1,0:T(8,128)(2,1)}, f32[8,8,128]{2,1,0:T(8,128)S(1)}) custom-call(s32[265]{0:T(512)S(1)} %concatenate.36.refs_0_, f32[64,128]{1,0:T(8,128)S(1)} %dynamic-slice_subtract_fusion.refs_1_, f32[16,256,128]{2,1,0:T(8,128)S(1)} %broadcast_in_dim.89.refs_2_, ...), custom_call_target="tpu_custom_call", output_to_operand_aliasing={{0}: (7, {})} | custom-call | flops 268435456 | bytes 4718592 | tf_op jit(solution)/shard_map/amplitudes/pallas_call | solution.py:212
  292.8 6.2 %amplitudes.10 = (bf16[64,256,128]{2,1,0:T(8,128)(2,1)}, f32[8,8,128]{2,1,0:T(8,128)S(1)}) custom-call(s32[265]{0:T(512)S(1)} %concatenate.36.refs_0_, f32[64,128]{1,0:T(8,128)S(1)} %dynamic-slice_subtract_fusion.refs_1_, f32[16,256,128]{2,1,0:T(8,128)S(1)} %broadcast_in_dim.89.refs_2_, ...), custom_call_target="tpu_custom_call", output_to_operand_aliasing={{0}: (7, {})} | custom-call | flops 268435456 | bytes 4718592 | tf_op jit(solution)/shard_map/amplitudes/pallas_call | solution.py:212
  299.1 5.1 %amplitudes.11 = (bf16[64,256,128]{2,1,0:T(8,128)(2,1)}, f32[8,8,128]{2,1,0:T(8,128)S(1)}) custom-call(s32[265]{0:T(512)S(1)} %concatenate.36.refs_0_, f32[64,128]{1,0:T(8,128)S(1)} %dynamic-slice_subtract_fusion.refs_1_, f32[16,256,128]{2,1,0:T(8,128)} %copy-done.5, bf16[16,256,256]{2,1,0:T(8,128)(2,1)} %copy-done, ...), custom_call_target="tpu_custom_call", output_to_operand_aliasing={{0}: (9, {})} | custom-call | flops 268435456 | bytes 4718592 | tf_op jit(solution)/shard_map/amplitudes/pallas_call | solution.py:212
  304.2 6.2 %amplitudes.12 = (bf16[64,256,128]{2,1,0:T(8,128)(2,1)}, f32[8,8,128]{2,1,0:T(8,128)S(1)}) custom-call(s32[265]{0:T(512)S(1)} %concatenate.36.refs_0_, f32[64,128]{1,0:T(8,128)S(1)} %dynamic-slice_subtract_fusion.refs_1_, f32[16,256,128]{2,1,0:T(8,128)S(1)} %copy-done.6, bf16[16,256,256]{2,1,0:T(8,128)(2,1)S(1)} %copy-done.2, ...), custom_call_target="tpu_custom_call", output_to_operand_aliasing={{0}: (7, {})} | custom-call | flops 268435456 | bytes 4718592 | tf_op jit(solution)/shard_map/amplitudes/pallas_call | solution.py:212
  310.4 5.0 %amplitudes.13 = (bf16[64,256,128]{2,1,0:T(8,128)(2,1)}, f32[8,8,128]{2,1,0:T(8,128)S(1)}) custom-call(s32[265]{0:T(512)S(1)} %concatenate.36.refs_0_, f32[64,128]{1,0:T(8,128)S(1)} %dynamic-slice_subtract_fusion.refs_1_, f32[16,256,128]{2,1,0:T(8,128)} %copy-done.5, bf16[16,256,256]{2,1,0:T(8,128)(2,1)} %copy-done, ...), custom_call_target="tpu_custom_call", output_to_operand_aliasing={{0}: (9, {})} | custom-call | flops 268435456 | bytes 4718592 | tf_op jit(solution)/shard_map/amplitudes/pallas_call | solution.py:212
  315.5 6.2 %amplitudes.14 = (bf16[64,256,128]{2,1,0:T(8,128)(2,1)}, f32[8,8,128]{2,1,0:T(8,128)S(1)}) custom-call(s32[265]{0:T(512)S(1)} %concatenate.36.refs_0_, f32[64,128]{1,0:T(8,128)S(1)} %dynamic-slice_subtract_fusion.refs_1_, f32[16,256,128]{2,1,0:T(8,128)S(1)} %copy-done.7, bf16[16,256,256]{2,1,0:T(8,128)(2,1)S(1)} %copy-done.3, ...), custom_call_target="tpu_custom_call", output_to_operand_aliasing={{0}: (7, {})} | custom-call | flops 268435456 | bytes 4718592 | tf_op jit(solution)/shard_map/amplitudes/pallas_call | solution.py:212
  321.7 6.2 %amplitudes.15 = (bf16[64,256,128]{2,1,0:T(8,128)(2,1)}, f32[8,8,128]{2,1,0:T(8,128)S(1)}) custom-call(s32[265]{0:T(512)S(1)} %concatenate.36.refs_0_, f32[64,128]{1,0:T(8,128)S(1)} %dynamic-slice_subtract_fusion.refs_1_, f32[16,256,128]{2,1,0:T(8,128)S(1)} %copy-done.7, bf16[16,256,256]{2,1,0:T(8,128)(2,1)S(1)} %copy-done.3, ...), custom_call_target="tpu_custom_call", output_to_operand_aliasing={{0}: (7, {})} | custom-call | flops 268435456 | bytes 4718592 | tf_op jit(solution)/shard_map/amplitudes/pallas_call | solution.py:212
  327.9 4.0 %density_rows.3 = f32[16,128,256]{2,1,0:T(8,128)S(1)} custom-call(s32[1]{0:T(128)} %bitcast.25.start, bf16[64,256,128]{2,1,0:T(8,128)(2,1)} %get-tuple-element.33.t), custom_call_target="tpu_custom_call" | custom-call | flops 536870912 | bytes 6291456 | tf_op jit(solution)/shard_map/density_rows/pallas_call | solution.py:256
  333.1 4.0 %density_rows.2 = f32[16,128,256]{2,1,0:T(8,128)S(1)} custom-call(s32[1]{0:T(128)} %bitcast.24.start, bf16[64,256,128]{2,1,0:T(8,128)(2,1)} %get-tuple-element.33.t), custom_call_target="tpu_custom_call" | custom-call | flops 536870912 | bytes 6291456 | tf_op jit(solution)/shard_map/density_rows/pallas_call | solution.py:256
  337.6 3.2 add.168
  (113 shorter events, 11.8 us)
Async XLA Ops:
  0.6 5.3 %copy-start.18 = (s32[16]{0:T(128)S(1)}, s32[16]{0:T(128)}, u32[]{:S(2)}) copy-start(s32[16]{0:T(128)} %param.9) | copy-start | bytes 196
  0.6 5.4 %copy-start.15 = (f32[16]{0:T(128)S(1)}, f32[16]{0:T(128)}, u32[]{:S(2)}) copy-start(f32[16]{0:T(128)} %param.8) | copy-start | bytes 196
  0.7 5.5 %copy-start.9 = (f32[16,256]{1,0:T(8,128)S(1)}, f32[16,256]{1,0:T(8,128)}, u32[]{:S(2)}) copy-start(f32[16,256]{1,0:T(8,128)} %param.7) | copy-start | bytes 49156
  0.7 7.1 %copy-start.19 = (s32[64,1]{0,1:T(1,128)S(1)}, s32[64,1]{0,1:T(1,128)}, u32[]{:S(2)}) copy-start(s32[64,1]{0,1:T(1,128)} %param.10) | copy-start | bytes 772
  0.7 7.3 %collective-permute-start.3 = (bf16[16,256,256]{2,1,0:T(8,128)(2,1)}, bf16[16,256,256]{2,1,0:T(8,128)(2,1)}, u32[]{:S(2)}, u32[]{:S(2)}) collective-permute-start(bf16[16,256,256]{2,1,0:T(8,128)(2,1)} %x.1), channel_id=1, source_target_pairs={{0,1},{1,0},{2,3},{3,2},{4,5},{5,4},{6,7},{7,6},{8,9},{9,8},{10,11... | collective-permute-start | bytes 6291464 | tf_op jit(solution)/shard_map/ppermute | solution.py:291
  1.2 12.5 %copy-start.16 = (s32[64]{0:T(128)S(1)}, s32[64]{0:T(128)}, u32[]{:S(2)}) copy-start(s32[64]{0:T(128)} %param.11) | copy-start | bytes 772
  2.5 26.8 %collective-permute-start.4 = (bf16[16,256,128]{2,1,0:T(8,128)(2,1)S(1)}, bf16[16,256,128]{2,1,0:T(8,128)(2,1)}, u32[]{:S(2)}, u32[]{:S(2)}) collective-permute-start(bf16[16,256,128]{2,1,0:T(8,128)(2,1)S(1)} %constant_dynamic-slice_fusion.1.refs_5_.refs_1_), channel_id=1, source_target_pairs={{0,4},{2,6},{4,0},{6,2},{8,12},{10,14},{12,8},{14,10},{1,5},{3,7},... | collective-permute-start | bytes 3145736 | tf_op jit(solution)/shard_map/ppermute | solution.py:329
  5.2 48.7 %collective-permute-start.6 = (bf16[16,256,128]{2,1,0:T(8,128)(2,1)S(1)}, bf16[16,256,128]{2,1,0:T(8,128)(2,1)S(1)}, u32[]{:S(2)}, u32[]{:S(2)}) collective-permute-start(bf16[16,256,128]{2,1,0:T(8,128)(2,1)S(1)} %constant_dynamic-slice_fusion.1.refs_5_.refs_1_), channel_id=1, source_target_pairs={{4,8},{6,10},{8,4},{10,6},{5,9},{7,11},{9,5},{11,7},{20,24},{22,26... | collective-permute-start | bytes 3145736 | tf_op jit(solution)/shard_map/ppermute | solution.py:330
  6.2 54.4 %collective-permute-start = (f32[1,16,384]{2,1,0:T(8,128)S(1)}, f32[1,16,384]{2,1,0:T(8,128)S(1)}, u32[]{:S(2)}, u32[]{:S(2)}) collective-permute-start(f32[1,16,384]{2,1,0:T(8,128)S(1)} %fusion.14), channel_id=1, source_target_pairs={{0,2},{2,0},{4,6},{6,4},{8,10},{10,8},{12,14},{14,12},{1,3},{3,1},... | collective-permute-start | bytes 73736 | tf_op jit(solution)/shard_map/ppermute | solution.py:312
  9.3 42.3 %collective-permute-start.5 = (bf16[16,256,128]{2,1,0:T(8,128)(2,1)S(1)}, bf16[16,256,128]{2,1,0:T(8,128)(2,1)}, u32[]{:S(2)}, u32[]{:S(2)}) collective-permute-start(bf16[16,256,128]{2,1,0:T(8,128)(2,1)S(1)} %constant_dynamic-slice_fusion.refs_6_.refs_1_), channel_id=1, source_target_pairs={{0,4},{2,6},{4,0},{6,2},{8,12},{10,14},{12,8},{14,10},{1,5},{3,7},... | collective-permute-start | bytes 3145736 | tf_op jit(solution)/shard_map/ppermute | solution.py:329
  29.3 25.9 %collective-permute-start.13 = (bf16[16,256,128]{2,1,0:T(8,128)(2,1)}, bf16[16,256,128]{2,1,0:T(8,128)(2,1)}, u32[]{:S(2)}, u32[]{:S(2)}) collective-permute-start(bf16[16,256,128]{2,1,0:T(8,128)(2,1)} %collective-permute-done.4.refs_5_.refs_1_), channel_id=1, source_target_pairs={{4,8},{6,10},{8,4},{10,6},{5,9},{7,11},{9,5},{11,7},{20,24},{22,26... | collective-permute-start | bytes 3145736 | tf_op jit(solution)/shard_map/ppermute | solution.py:332
  31.1 26.3 %collective-permute-start.7 = (bf16[16,256,128]{2,1,0:T(8,128)(2,1)S(1)}, bf16[16,256,128]{2,1,0:T(8,128)(2,1)}, u32[]{:S(2)}, u32[]{:S(2)}) collective-permute-start(bf16[16,256,128]{2,1,0:T(8,128)(2,1)S(1)} %constant_dynamic-slice_fusion.refs_6_.refs_1_), channel_id=1, source_target_pairs={{4,8},{6,10},{8,4},{10,6},{5,9},{7,11},{9,5},{11,7},{20,24},{22,26... | collective-permute-start | bytes 3145736 | tf_op jit(solution)/shard_map/ppermute | solution.py:330
  51.6 7.1 %collective-permute-start.14 = (bf16[16,256,128]{2,1,0:T(8,128)(2,1)}, bf16[16,256,128]{2,1,0:T(8,128)(2,1)}, u32[]{:S(2)}, u32[]{:S(2)}) collective-permute-start(bf16[16,256,128]{2,1,0:T(8,128)(2,1)} %collective-permute-done.5.refs_6_.refs_1_), channel_id=1, source_target_pairs={{4,8},{6,10},{8,4},{10,6},{5,9},{7,11},{9,5},{11,7},{20,24},{22,26... | collective-permute-start | bytes 3145736 | tf_op jit(solution)/shard_map/ppermute | solution.py:332
  53.9 122.6 %collective-permute-start.8 = (bf16[16,256,128]{2,1,0:T(8,128)(2,1)S(1)}, bf16[16,256,128]{2,1,0:T(8,128)(2,1)}, u32[]{:S(2)}, u32[]{:S(2)}) collective-permute-start(bf16[16,256,128]{2,1,0:T(8,128)(2,1)S(1)} %collective-permute-done.6.refs_5_.refs_1_), channel_id=1, source_target_pairs={{4,0},{6,2},{8,12},{10,14},{5,1},{7,3},{9,13},{11,15},{20,16},{22,... | collective-permute-start | bytes 3145736 | tf_op jit(solution)/shard_map/ppermute | solution.py:331
  55.2 121.9 %collective-permute-start.15 = (bf16[16,256,128]{2,1,0:T(8,128)(2,1)}, bf16[16,256,128]{2,1,0:T(8,128)(2,1)}, u32[]{:S(2)}, u32[]{:S(2)}) collective-permute-start(bf16[16,256,128]{2,1,0:T(8,128)(2,1)} %collective-permute-done.13.refs_5_.refs_1_), channel_id=1, source_target_pairs={{4,0},{6,2},{8,12},{10,14},{5,1},{7,3},{9,13},{11,15},{20,16},{22,... | collective-permute-start | bytes 3145736 | tf_op jit(solution)/shard_map/ppermute | solution.py:333
  56.5 97.8 %copy-start.11 = (s32[8]{0:T(128)}, s32[8]{0:T(128)S(1)}, u32[]{:S(2)}) copy-start(s32[8]{0:T(128)S(1)} %add_multiply_fusion.1) | copy-start | bytes 100
  57.4 176.1 %collective-permute-start.9 = (bf16[16,256,128]{2,1,0:T(8,128)(2,1)}, bf16[16,256,128]{2,1,0:T(8,128)(2,1)}, u32[]{:S(2)}, u32[]{:S(2)}) collective-permute-start(bf16[16,256,128]{2,1,0:T(8,128)(2,1)} %collective-permute-done.7.refs_6_.refs_1_), channel_id=1, source_target_pairs={{4,0},{6,2},{8,12},{10,14},{5,1},{7,3},{9,13},{11,15},{20,16},{22,... | collective-permute-start | bytes 3145736 | tf_op jit(solution)/shard_map/ppermute | solution.py:331
  58.7 193.0 %collective-permute-start.16 = (bf16[16,256,128]{2,1,0:T(8,128)(2,1)}, bf16[16,256,128]{2,1,0:T(8,128)(2,1)}, u32[]{:S(2)}, u32[]{:S(2)}) collective-permute-start(bf16[16,256,128]{2,1,0:T(8,128)(2,1)} %collective-permute-done.14.refs_6_.refs_1_), channel_id=1, source_target_pairs={{4,0},{6,2},{8,12},{10,14},{5,1},{7,3},{9,13},{11,15},{20,16},{22,... | collective-permute-start | bytes 3145736 | tf_op jit(solution)/shard_map/ppermute | solution.py:333
  60.7 89.2 %collective-permute-start.1 = (f32[2,16,384]{2,1,0:T(8,128)S(1)}, f32[2,16,384]{2,1,0:T(8,128)S(1)}, u32[]{:S(2)}, u32[]{:S(2)}) collective-permute-start(f32[2,16,384]{2,1,0:T(8,128)S(1)} %pad_maximum_fusion.2), channel_id=1, source_target_pairs={{0,4},{2,6},{4,0},{6,2},{8,12},{10,14},{12,8},{14,10},{1,5},{3,7},... | collective-permute-start | bytes 147464 | tf_op jit(solution)/shard_map/ppermute | solution.py:312
  105.7 1.6 copy-start.8
  108.1 1.3 copy-start
  149.9 3.5 %collective-permute-start.10 = (s32[64]{0:T(128)S(1)}, s32[64]{0:T(128)S(1)}, u32[]{:S(2)}, u32[]{:S(2)}) collective-permute-start(s32[64]{0:T(128)S(1)} %get-tuple-element.34), channel_id=1, source_target_pairs={{0,2},{2,0},{4,6},{6,4},{8,10},{10,8},{12,14},{14,12},{1,3},{3,1},... | collective-permute-start | bytes 776 | tf_op jit(solution)/shard_map/ppermute | solution.py:325
  153.4 21.5 %collective-permute-start.2 = (f32[4,16,384]{2,1,0:T(8,128)S(1)}, f32[4,16,384]{2,1,0:T(8,128)S(1)}, u32[]{:S(2)}, u32[]{:S(2)}) collective-permute-start(f32[4,16,384]{2,1,0:T(8,128)S(1)} %pad_maximum_fusion.1), channel_id=1, source_target_pairs={{0,8},{2,10},{4,12},{6,14},{8,0},{10,2},{12,4},{14,6},{1,9},{3,11}... | collective-permute-start | bytes 294920 | tf_op jit(solution)/shard_map/ppermute | solution.py:312
  174.9 96.0 %collective-permute-start.11 = (bf16[8,256,128]{2,1,0:T(8,128)(2,1)}, bf16[8,256,128]{2,1,0:T(8,128)(2,1)}, u32[]{:S(2)}, u32[]{:S(2)}) collective-permute-start(bf16[8,256,128]{2,1,0:T(8,128)(2,1)} %pack.8), channel_id=1, source_target_pairs={{0,2},{2,0},{4,6},{6,4},{8,10},{10,8},{12,14},{14,12},{1,3},{3,1},... | collective-permute-start | bytes 1572872 | tf_op jit(solution)/shard_map/ppermute | solution.py:336
  176.5 95.0 %collective-permute-start.17 = (bf16[8,256,128]{2,1,0:T(8,128)(2,1)}, bf16[8,256,128]{2,1,0:T(8,128)(2,1)}, u32[]{:S(2)}, u32[]{:S(2)}) collective-permute-start(bf16[8,256,128]{2,1,0:T(8,128)(2,1)} %pack.10), channel_id=1, source_target_pairs={{0,2},{2,0},{4,6},{6,4},{8,10},{10,8},{12,14},{14,12},{1,3},{3,1},... | collective-permute-start | bytes 1572872 | tf_op jit(solution)/shard_map/ppermute | solution.py:336
  177.0 96.0 %collective-permute-start.12 = (bf16[8,256,128]{2,1,0:T(8,128)(2,1)}, bf16[8,256,128]{2,1,0:T(8,128)(2,1)}, u32[]{:S(2)}, u32[]{:S(2)}) collective-permute-start(bf16[8,256,128]{2,1,0:T(8,128)(2,1)} %pack.9), channel_id=1, source_target_pairs={{0,2},{2,0},{4,6},{6,4},{8,10},{10,8},{12,14},{14,12},{1,3},{3,1},... | collective-permute-start | bytes 1572872 | tf_op jit(solution)/shard_map/ppermute | solution.py:336
  233.4 40.3 %copy-start.12 = (s32[8]{0:T(128)S(1)}, s32[8]{0:T(128)}, u32[]{:S(2)}) copy-start(s32[8]{0:T(128)} %copy-done.11) | copy-start | bytes 100
  233.4 40.3 %copy-start.13 = (s32[64]{0:T(128)S(1)}, s32[64]{0:T(128)}, u32[]{:S(2)}) copy-start(s32[64]{0:T(128)} %fusion.3) | copy-start | bytes 772
  233.5 82.0 %collective-permute-start.19 = (bf16[8,256,128]{2,1,0:T(8,128)(2,1)}, bf16[8,256,128]{2,1,0:T(8,128)(2,1)}, u32[]{:S(2)}, u32[]{:S(2)}) collective-permute-start(bf16[8,256,128]{2,1,0:T(8,128)(2,1)} %pack.12), channel_id=1, source_target_pairs={{0,2},{2,0},{4,6},{6,4},{8,10},{10,8},{12,14},{14,12},{1,3},{3,1},... | collective-permute-start | bytes 1572872 | tf_op jit(solution)/shard_map/ppermute | solution.py:336
  251.7 52.5 %collective-permute-start.18 = (bf16[8,256,128]{2,1,0:T(8,128)(2,1)}, bf16[8,256,128]{2,1,0:T(8,128)(2,1)}, u32[]{:S(2)}, u32[]{:S(2)}) collective-permute-start(bf16[8,256,128]{2,1,0:T(8,128)(2,1)} %pack.11), channel_id=1, source_target_pairs={{0,2},{2,0},{4,6},{6,4},{8,10},{10,8},{12,14},{14,12},{1,3},{3,1},... | collective-permute-start | bytes 1572872 | tf_op jit(solution)/shard_map/ppermute | solution.py:336
  271.0 50.7 %collective-permute-start.21 = (bf16[8,256,128]{2,1,0:T(8,128)(2,1)}, bf16[8,256,128]{2,1,0:T(8,128)(2,1)}, u32[]{:S(2)}, u32[]{:S(2)}) collective-permute-start(bf16[8,256,128]{2,1,0:T(8,128)(2,1)} %pack.14), channel_id=1, source_target_pairs={{0,2},{2,0},{4,6},{6,4},{8,10},{10,8},{12,14},{14,12},{1,3},{3,1},... | collective-permute-start | bytes 1572872 | tf_op jit(solution)/shard_map/ppermute | solution.py:336
  271.5 43.9 %collective-permute-start.20 = (bf16[8,256,128]{2,1,0:T(8,128)(2,1)}, bf16[8,256,128]{2,1,0:T(8,128)(2,1)}, u32[]{:S(2)}, u32[]{:S(2)}) collective-permute-start(bf16[8,256,128]{2,1,0:T(8,128)(2,1)} %pack.13), channel_id=1, source_target_pairs={{0,2},{2,0},{4,6},{6,4},{8,10},{10,8},{12,14},{14,12},{1,3},{3,1},... | collective-permute-start | bytes 1572872 | tf_op jit(solution)/shard_map/ppermute | solution.py:336
  273.1 48.6 %collective-permute-start.22 = (bf16[8,256,128]{2,1,0:T(8,128)(2,1)}, bf16[8,256,128]{2,1,0:T(8,128)(2,1)}, u32[]{:S(2)}, u32[]{:S(2)}) collective-permute-start(bf16[8,256,128]{2,1,0:T(8,128)(2,1)} %pack.15), channel_id=1, source_target_pairs={{0,2},{2,0},{4,6},{6,4},{8,10},{10,8},{12,14},{14,12},{1,3},{3,1},... | collective-permute-start | bytes 1572872 | tf_op jit(solution)/shard_map/ppermute | solution.py:336
  274.0 4.1 %copy-start.10 = (f32[16,256]{1,0:T(8,128)S(1)}, f32[16,256]{1,0:T(8,128)}, u32[]{:S(2)}) copy-start(f32[16,256]{1,0:T(8,128)} %param.7) | copy-start | bytes 49156
  276.8 1.4 copy-start.4
  278.8 14.1 %copy-start.5 = (f32[16,256,128]{2,1,0:T(8,128)}, f32[16,256,128]{2,1,0:T(8,128)S(1)}, u32[]{:S(2)}) copy-start(f32[16,256,128]{2,1,0:T(8,128)S(1)} %broadcast_in_dim.89.refs_2_) | copy-start | bytes 6291460
  287.8 5.0 %copy-start.1 = (bf16[16,256,256]{2,1,0:T(8,128)(2,1)S(1)}, bf16[16,256,256]{2,1,0:T(8,128)(2,1)}, u32[]{:S(2)}) copy-start(bf16[16,256,256]{2,1,0:T(8,128)(2,1)} %copy-done) | copy-start | bytes 6291460
  299.1 5.1 %copy-start.2 = (bf16[16,256,256]{2,1,0:T(8,128)(2,1)S(1)}, bf16[16,256,256]{2,1,0:T(8,128)(2,1)}, u32[]{:S(2)}) copy-start(bf16[16,256,256]{2,1,0:T(8,128)(2,1)} %copy-done) | copy-start | bytes 6291460
  299.1 5.1 %copy-start.6 = (f32[16,256,128]{2,1,0:T(8,128)S(1)}, f32[16,256,128]{2,1,0:T(8,128)}, u32[]{:S(2)}) copy-start(f32[16,256,128]{2,1,0:T(8,128)} %copy-done.5) | copy-start | bytes 6291460
  310.4 5.1 %copy-start.3 = (bf16[16,256,256]{2,1,0:T(8,128)(2,1)S(1)}, bf16[16,256,256]{2,1,0:T(8,128)(2,1)}, u32[]{:S(2)}) copy-start(bf16[16,256,256]{2,1,0:T(8,128)(2,1)} %copy-done) | copy-start | bytes 6291460
  310.4 5.1 %copy-start.7 = (f32[16,256,128]{2,1,0:T(8,128)S(1)}, f32[16,256,128]{2,1,0:T(8,128)}, u32[]{:S(2)}) copy-start(f32[16,256,128]{2,1,0:T(8,128)} %copy-done.5) | copy-start | bytes 6291460
  327.9 4.5 %copy-start.14 = (s32[64]{0:T(128)S(1)}, s32[64]{0:T(128)}, u32[]{:S(2)}) copy-start(s32[64]{0:T(128)} %add.152) | copy-start | bytes 772
  327.9 4.5 %copy-start.17 = (s32[64]{0:T(128)S(1)}, s32[64]{0:T(128)}, u32[]{:S(2)}) copy-start(s32[64]{0:T(128)} %fusion.13) | copy-start | bytes 772
  331.9 5.7 %collective-permute-start.24 = (f32[16,128,256]{2,1,0:T(8,128)S(1)}, f32[16,128,256]{2,1,0:T(8,128)}, u32[]{:S(2)}, u32[]{:S(2)}) collective-permute-start(f32[16,128,256]{2,1,0:T(8,128)S(1)} %density_rows.3), channel_id=1, source_target_pairs={{0,1},{1,0},{2,3},{3,2},{4,5},{5,4},{6,7},{7,6},{8,9},{9,8},{10,11... | collective-permute-start | bytes 6291464 | tf_op jit(solution)/shard_map/ppermute | solution.py:347
  332.5 4.5 %collective-permute-start.23 = (f32[64]{0:T(128)S(1)}, f32[64]{0:T(128)S(1)}, u32[]{:S(2)}, u32[]{:S(2)}) collective-permute-start(f32[64]{0:T(128)S(1)} %select_reduce_fusion), channel_id=1, source_target_pairs={{0,1},{1,0},{2,3},{3,2},{4,5},{5,4},{6,7},{7,6},{8,9},{9,8},{10,11... | collective-permute-start | bytes 776 | tf_op jit(solution)/shard_map/ppermute | solution.py:354

commit v3 on v2

--- a/solution.py
+++ b/solution.py
@@ -89,48 +89,39 @@
     return mesh.shape["orb"] == 8 and mesh.shape["aux"] == 2
 
 
-def table_of(bases, fields):
-    return jnp.concatenate([bases] + [x.astype(i32) for x in fields])
-
-
-def pack_kernel(call, cap, tbl, *refs):
-    sources, out, sems = refs[:-2], refs[-2], refs[-1]
+HEAD = 10
+
+
+def table_of(fields):
+    return jnp.concatenate([x.astype(i32) for x in fields])
+
+
+def pack_kernel(call, after, tbl, x, *refs):
+    out, sems = refs[after:]
+    cap = out.shape[0]
     base = tbl[call]
-
-    def move(x):
-        copies = []
-        for r in range(cap):
-            slot = tbl[9 + base + r]
-            copies.append(pltpu.make_async_copy(x.at[slot], out.at[r], sems.at[r]))
-            copies[-1].start()
-        for copy in copies:
-            copy.wait()
-
-    by_place(tbl, sources, move)
-
-
-def by_place(tbl, sources, act):
-    if len(sources) == 1:
-        act(*sources)
-    else:
-        pl.when(tbl[8] == 1)(lambda: act(sources[0]))
-        pl.when(tbl[8] == 0)(lambda: act(sources[1]))
-
-
-def pack(tbl, call, sources, cap):
-    x = sources[0]
+    copies = []
+    for r in range(cap):
+        slot = tbl[HEAD + base + r]
+        copies.append(pltpu.make_async_copy(x.at[slot], out.at[r], sems.at[r]))
+        copies[-1].start()
+    for copy in copies:
+        copy.wait()
+
+
+def pack(tbl, call, x, cap, after=()):
     return pl.pallas_call(
-        lambda *refs: pack_kernel(call, cap, *refs),
+        lambda *refs: pack_kernel(call, len(after), *refs),
         out_shape=jax.ShapeDtypeStruct((cap,) + x.shape[1:], x.dtype),
-        in_specs=[SMEM] + [HBM] * len(sources),
-        out_specs=HBM,
+        in_specs=[SMEM, HBM] + [HBM] * len(after),
+        out_specs=VMEM,
         scratch_shapes=[pltpu.SemaphoreType.DMA((cap,))],
         compiler_params=pltpu.CompilerParams(vmem_limit_bytes=LIMIT),
         cost_estimate=pl.CostEstimate(
             flops=0, bytes_accessed=2 * cap * x.shape[1] * x.shape[2] * 2, transcendentals=0
         ),
         name="pack",
-    )(tbl, *sources)
+    )(tbl, x, *after)
 
 
 def turn_kernel(x, out):
@@ -155,68 +146,133 @@
     )(x)
 
 
-def amplitudes_kernel(call, by_slot, per_orb, places, tbl, rows, vcol, a0, a1, *refs):
-    js, (tin, tout, energy, sv, s0, s1, b0, b1, st, sem, sem_out) = refs[:-11], refs[-11:]
+def amplitudes_kernel(mode, call, per_orb, after, tbl, rows, vcol, *refs):
+    outs, (energy, sv, s0, s1, b0, b1, st, sem, sem_out) = refs[:-9], refs[-9:]
+    if mode == "client":
+        left, js, tout = outs[:4], outs[4:6], outs[-1]
+    else:
+        left, js, ready, tout = outs[:2], outs[2:], outs[-3 - after], outs[-1]
     cap = sv.shape[0]
     n = rows.shape[0]
+    nvd, half = sv.shape[1], sv.shape[2]
     base = tbl[call]
-
-    def loads_of(r, j0, j1):
-        i = lax.div(tbl[9 + base + r], per_orb)
-        slot = tbl[9 + n + base + r] if by_slot else r
-        pairs = (
-            (vcol.at[i], sv.at[r]),
-            (a0.at[i], s0.at[r]),
-            (a1.at[i], s1.at[r]),
-            (j0.at[slot], b0.at[r]),
-            (j1.at[slot], b1.at[r]),
-        )
-        return [pltpu.make_async_copy(x, to, sem.at[r, k]) for k, (x, to) in enumerate(pairs)]
-
-    def load(j):
-        copies = [copy for r in range(cap) for copy in loads_of(r, *j)]
+    middle = tbl[8] == 1
+
+    def place(r):
+        return tbl[HEAD + base + r]
+
+    def load(j0, j1):
+        copies = []
+        for r in range(cap):
+            i = lax.div(place(r), per_orb)
+            slot = r if mode == "asked" else tbl[HEAD + n + base + r]
+            todo = [(vcol.at[i], sv.at[r]), (j0.at[slot], b0.at[r]), (j1.at[slot], b1.at[r])]
+            if mode == "client":
+                here = pl.ds(pl.multiple_of(tbl[9], half), half)
+                there = pl.ds(pl.multiple_of(half - tbl[9], half), half)
+                todo += [
+                    (left[0].at[i], s0.at[r, here, :]),
+                    (left[1].at[i], s1.at[r, here, :]),
+                    (left[2].at[i], s1.at[r, there, :]),
+                    (left[3].at[i], s0.at[r, there, :]),
+                ]
+            else:
+                todo += [(left[0].at[i], s0.at[r]), (left[1].at[i], s1.at[r])]
+            copies += [
+                pltpu.make_async_copy(x, to, sem.at[r, k]) for k, (x, to) in enumerate(todo)
+            ]
         for copy in copies:
             copy.start()
         for copy in copies:
             copy.wait()
 
-    by_place(tbl, [js[2 * k : 2 * k + 2] for k in range(places)], load)
-    nvd, half = sv.shape[1], sv.shape[2]
-    live_a = lax.broadcasted_iota(i32, (nvd, half), 0)
-    live_b = lax.broadcasted_iota(i32, (nvd, half), 1)
-    row8 = rows[pl.ds(pl.multiple_of(base, cap), cap), :]
-    for r in range(cap):
-        size_i = tbl[9 + 2 * n + base + r]
-        size_j = tbl[9 + 3 * n + base + r]
-        k = jnp.dot(s0[r], b0[r], preferred_element_type=f32)
-        k += jnp.dot(s1[r], b1[r], preferred_element_type=f32)
-        k = jnp.where((live_a < size_i) & (live_b < size_j), k, 0.0)
-        gap = sv[r] + row8[r : r + 1, :]
-        t = (-k / gap).astype(bf16)
-        st[r] = t
-        energy[r] = jnp.sum((k * t.astype(f32)).reshape(nvd // 8, 8, half), axis=0)
-    stores = [
-        pltpu.make_async_copy(st.at[r], tout.at[tbl[9 + base + r]], sem_out.at[r])
-        for r in range(cap)
-    ]
-    for copy in stores:
-        copy.start()
-    for copy in stores:
-        copy.wait()
-
-
-def amplitudes(call, by_slot, per_orb, tbl, rows, vcol, left, sources, t_all, cap):
+    def make():
+        live_a = lax.broadcasted_iota(i32, (nvd, half), 0)
+        live_b = lax.broadcasted_iota(i32, (nvd, half), 1)
+        row8 = rows[pl.ds(pl.multiple_of(base, cap), cap), :]
+        for r in range(cap):
+            size_i = tbl[HEAD + 2 * n + base + r]
+            size_j = tbl[HEAD + 3 * n + base + r]
+            k = jnp.dot(s0[r], b0[r], preferred_element_type=f32)
+            k += jnp.dot(s1[r], b1[r], preferred_element_type=f32)
+            k = jnp.where((live_a < size_i) & (live_b < size_j), k, 0.0)
+            gap = sv[r] + row8[r : r + 1, :]
+            t = (-k / gap).astype(bf16)
+            st[r] = t
+            energy[r] = jnp.sum((k * t.astype(f32)).reshape(nvd // 8, 8, half), axis=0)
+
+    def store():
+        stores = [
+            pltpu.make_async_copy(st.at[r], tout.at[place(r)], sem_out.at[r]) for r in range(cap)
+        ]
+        for copy in stores:
+            copy.start()
+        for copy in stores:
+            copy.wait()
+
+    if mode == "slots":
+        load(js[0], js[1])
+        make()
+        store()
+    elif mode == "asked":
+        if len(js) - 2 - after >= 4:
+            pl.when(middle)(lambda: load(js[0], js[1]))
+            pl.when(jnp.logical_not(middle))(lambda: load(js[2], js[3]))
+        else:
+            load(js[0], js[1])
+        make()
+        store()
+    elif mode == "served":
+
+        @pl.when(middle)
+        def _():
+            load(js[0], js[1])
+            make()
+
+        @pl.when(jnp.logical_not(middle))
+        def _():
+            energy[...] = jnp.zeros_like(energy)
+            copies = [
+                pltpu.make_async_copy(ready.at[r], st.at[r], sem.at[r, 0]) for r in range(cap)
+            ]
+            for copy in copies:
+                copy.start()
+            for copy in copies:
+                copy.wait()
+
+        store()
+    else:
+
+        @pl.when(middle)
+        def _():
+            load(js[0], js[1])
+            make()
+            tout[...] = st[...]
+
+        @pl.when(jnp.logical_not(middle))
+        def _():
+            energy[...] = jnp.zeros_like(energy)
+            tout[...] = jnp.zeros_like(tout)
+
+
+def amplitudes(mode, call, per_orb, tables, left, sources, t_all, cap, after=()):
+    tbl, rows, vcol = tables
     nvd, half = vcol.shape[1:]
     qa = left[0].shape[2]
-    blocks = [x for pair in sources for x in pair]
+    operands = (tbl, rows, vcol, *left, *sources, *after)
+    client = mode == "client"
+    aliases = {} if client else {len(operands): 0}
+    if not client:
+        operands += (t_all,)
+    t_shape = (cap, nvd, half) if client else t_all.shape
     return pl.pallas_call(
-        lambda *refs: amplitudes_kernel(call, by_slot, per_orb, len(sources), *refs),
+        lambda *refs: amplitudes_kernel(mode, call, per_orb, len(after), *refs),
         out_shape=(
-            jax.ShapeDtypeStruct(t_all.shape, t_all.dtype),
+            jax.ShapeDtypeStruct(t_shape, bf16),
             jax.ShapeDtypeStruct((cap, 8, half), f32),
         ),
-        in_specs=[SMEM, VMEM, HBM, HBM, HBM] + [HBM] * len(blocks) + [HBM],
-        out_specs=(HBM, VMEM),
+        in_specs=[SMEM, VMEM] + [HBM] * (len(operands) - 2),
+        out_specs=(VMEM if client else HBM, VMEM),
         scratch_shapes=[
             pltpu.VMEM((cap, nvd, half), f32),
             pltpu.VMEM((cap, nvd, qa), bf16),
@@ -224,10 +280,10 @@
             pltpu.VMEM((cap, qa, half), bf16),
             pltpu.VMEM((cap, qa, half), bf16),
             pltpu.VMEM((cap, nvd, half), bf16),
-            pltpu.SemaphoreType.DMA((cap, 5)),
+            pltpu.SemaphoreType.DMA((cap, 7)),
             pltpu.SemaphoreType.DMA((cap,)),
         ],
-        input_output_aliases={5 + len(blocks): 0},
+        input_output_aliases=aliases,
         compiler_params=pltpu.CompilerParams(vmem_limit_bytes=LIMIT),
         cost_estimate=pl.CostEstimate(
             flops=cap * 4 * nvd * qa * half,
@@ -235,7 +291,7 @@
             transcendentals=0,
         ),
         name="amplitudes",
-    )(tbl, rows, vcol, *left, *blocks, t_all)
+    )(*operands)
 
 
 def density_kernel(start, t, d):
@@ -279,79 +335,144 @@
     peers = 8
     cap = pair_dev // peers
     half = nvd // 2
+    wide = nvd + 128
     me, core = lax.axis_index("orb"), lax.axis_index("aux")
     z, y = me // 2, me % 2
+    lower = z < 2
     middle = (z == 1) | (z == 2)
-    swap_core = [(0, 1), (1, 0)]
-    swap_y = [(o, o ^ 1) for o in range(peers)]
-    swap_half = [(o, o ^ 2) for o in range(peers)]
+    col0 = core * half
+
+    def pp(x, perm):
+        return lax.ppermute(x, "orb", perm)
+
+    def swap_core(x):
+        return lax.ppermute(x, "aux", [(0, 1), (1, 0)])
+
+    def flip(bit):
+        return [(o, o ^ bit) for o in range(peers)]
+
     cross = [(2, 4), (3, 5), (4, 2), (5, 3)]
     outward = [(2, 0), (3, 1), (4, 6), (5, 7)]
-
-    other = lax.ppermute(blocks, "aux", swap_core)
-    col0 = core * half
+    y_middle = [(2, 3), (3, 2), (4, 5), (5, 4)]
+    y_end = [(0, 1), (1, 0), (6, 7), (7, 6)]
+
+    other = swap_core(blocks)
     own = [lax.dynamic_slice_in_dim(x, col0, half, 2) for x in (blocks, other)]
 
     owner = partner_owner[:, 0]
     target = owner * cap + slot_ranks(owner)
-    hit = target[None, :] == jnp.arange(pair_dev, dtype=i32)[:, None]
     pairs = jnp.arange(pair_dev, dtype=i32)
+    hit = target[None, :] == pairs[:, None]
     order = jnp.sum(jnp.where(hit, pairs[None, :], 0), axis=1)
     slots = jnp.sum(jnp.where(hit, partner_slot[None, :], 0), axis=1)
+    lists = jnp.concatenate([order, slots]).astype(f32)
     small = jnp.concatenate(
         [
-            vir_energy,
-            occ_energy[:, None],
-            domain_size.astype(f32)[:, None],
-            jnp.zeros((occ, 126), f32),
-        ],
-        axis=1,
-    )
-    every = small[None]
-    for bit in (1, 2, 4):
-        got = lax.ppermute(every, "orb", [(o, o ^ bit) for o in range(peers)])
-        every = jnp.concatenate([every, got])
-    theirs = jnp.take(every.reshape(peers * occ, -1), ((pairs // cap) ^ me) * occ + slots, axis=0)
-    mine = jnp.take(small, order // per_orb, axis=0)
-    rows = lax.dynamic_slice_in_dim(theirs, col0, half, 1) - (
-        theirs[:, nvd : nvd + 1] + mine[:, nvd : nvd + 1]
-    )
-    size_i = mine[:, nvd + 1].astype(i32)
-    size_j = theirs[:, nvd + 1].astype(i32) - col0
-    lower = z < 2
+            jnp.concatenate(
+                [
+                    vir_energy,
+                    occ_energy[:, None],
+                    domain_size.astype(f32)[:, None],
+                    jnp.zeros((occ, wide - nvd - 2), f32),
+                ],
+                axis=1,
+            ),
+            jnp.pad(lists[None], ((0, 7), (0, wide - lists.shape[0]))),
+        ]
+    )
+    both = jnp.stack([small, pp(small, flip(1))])
+    every = jnp.concatenate([both] + [pp(both, flip(bit)) for bit in (2, 4, 6)])
+    orbitals = every[:, :occ].reshape(peers * occ, wide)
+
     column = jnp.stack([z, z ^ 1, jnp.where(lower, 2, 1), jnp.where(lower, 3, 0)])
     bases = jnp.concatenate([column * 2 + y, column * 2 + (1 - y)]) * cap
-    tbl = table_of(bases, [middle[None], order, slots, size_i, size_j])
-    wanted = table_of(bases, [middle[None], lax.ppermute(slots, "orb", swap_y)])
-    vcol = jnp.broadcast_to(vir_energy[:, :, None], (occ, nvd, half))
+    head = [bases, middle[None], col0[None]]
+
+    def lists_of(x):
+        found = every[x, occ, : 2 * pair_dev].astype(i32)
+        return found[:pair_dev], found[pair_dev:]
+
+    def tables_of(x):
+        order, slots = lists_of(x)
+        theirs = jnp.take(orbitals, ((pairs // cap) ^ me) * occ + slots, axis=0)
+        mine = jnp.take(every[x, :occ], order // per_orb, axis=0)
+        rows = lax.dynamic_slice_in_dim(theirs, col0, half, 1) - (
+            theirs[:, nvd : nvd + 1] + mine[:, nvd : nvd + 1]
+        )
+        size_i, size_j = mine[:, nvd + 1], theirs[:, nvd + 1].astype(i32) - col0
+        vcol = jnp.broadcast_to(every[x, :occ, :nvd, None], (occ, nvd, half))
+        return table_of(head + [order, slots, size_i, size_j]), rows, vcol
+
+    tables = tables_of(0)
+    beside_list = table_of(head + [lists_of(1)[1]])
+    relay_list = table_of(head + [lists_of(3)[1]])
+    own, tables, beside_list, relay_list = lax.optimization_barrier(
+        (own, tables, beside_list, relay_list)
+    )
+    near = [pp(x, flip(2)) for x in own]
+    mid = [pp(x, cross) for x in own]
+    beside = [[pp(pack(beside_list, 0, x, cap), flip(1)) for x in own]]
     left = [turn(x) for x in (blocks, other)]
-
-    near = [lax.ppermute(x, "orb", swap_half) for x in own]
-    mid = [lax.ppermute(x, "orb", cross) for x in own]
-    mid_out = [lax.ppermute(x, "orb", outward) for x in mid]
-    far = [lax.ppermute(x, "orb", cross) for x in near]
-    far_out = [lax.ppermute(x, "orb", outward) for x in far]
-    sources = [[own], [near], [mid, mid_out], [far, far_out]]
-    beside = [
-        [lax.ppermute(pack(wanted, k, x, cap), "orb", swap_y) for x in zip(*source)]
-        for k, source in enumerate(sources)
-    ]
-
+    energies = [None] * 8
     t_all = jnp.zeros((pair_dev, nvd, half), bf16)
-    energies = [None] * 8
-    for k in (0, 1, 4, 2, 5, 3, 6, 7):
-        source = sources[k] if k < 4 else [beside[k - 4]]
+
+    def own_pairs(k, mode, sources, t_all, after=()):
         t_all, energies[k] = amplitudes(
-            k, k < 4, per_orb, tbl, rows, vcol, left, source, t_all, cap
+            mode, k, per_orb, tables, left, sources, t_all, cap, after
         )
-    away = lax.ppermute(density_rows(t_all, (1 - core) * half, per_orb, half), "aux", swap_core)
+        return t_all
+
+    t_all = own_pairs(0, "slots", own, t_all)
+    far = [pp(x, cross) for x in near]
+    token = energies[0]
+    beside_near, third_y, third_relay, across = [], [], [], []
+    for q in range(2):
+        x = pack(beside_list, 1, near[q], cap, (token,))
+        beside_near.append(pp(x, flip(1)))
+        across.append(swap_core(near[q]))
+        x = pack(relay_list, 2, mid[q], cap, (x,))
+        third_relay.append(pp(x, outward))
+        token = pack(beside_list, 2, mid[q], cap, (x,))
+        third_y.append(pp(token, y_middle))
+    t_all = own_pairs(4, "asked", beside[0], t_all, (token,))
+    t_all = own_pairs(1, "slots", near, t_all)
+    client_left = [turn(x) for x in near + across]
+    client = tables_of(2)
+    gone_2, client_energy_2 = amplitudes(
+        "client", 2, per_orb, client, client_left, mid, None, cap, (energies[1],)
+    )
+    ready_2 = pp(gone_2, outward)
+    third_end = [pp(x, y_end) for x in third_relay]
+    t_all = own_pairs(5, "asked", beside_near, t_all, (client_energy_2, *third_relay))
+    fourth_y, fourth_relay = [], []
+    token = energies[5]
+    for q in range(2):
+        x = pack(relay_list, 3, far[q], cap, (token,))
+        fourth_relay.append(pp(x, outward))
+        token = pack(beside_list, 3, far[q], cap, (x,))
+        fourth_y.append(pp(token, y_middle))
+    gone_3, client_energy_3 = amplitudes(
+        "client", 3, per_orb, client, client_left, far, None, cap, (token,)
+    )
+    ready_3 = pp(gone_3, outward)
+    fourth_end = [pp(x, y_end) for x in fourth_relay]
+    t_all = own_pairs(
+        2, "served", mid + [ready_2], t_all, (client_energy_3, fourth_relay[0])
+    )
+    t_all = own_pairs(6, "asked", third_y + third_end, t_all)
+    t_all = own_pairs(3, "served", far + [ready_3], t_all, (fourth_relay[1],))
+    t_all = own_pairs(7, "asked", fourth_y + fourth_end, t_all)
+
+    away = swap_core(density_rows(t_all, (1 - core) * half, per_orb, half))
     density = density_rows(t_all, core * half, per_orb, half) + away
 
-    sums = jnp.sum(jnp.stack(energies), axis=(2, 3)).reshape(pair_dev)
+    sums = jnp.sum(jnp.stack(energies), axis=(2, 3))
+    served = pp(jnp.sum(jnp.stack([client_energy_2, client_energy_3]), axis=(2, 3)), outward)
+    sums = jnp.concatenate([sums[:2], sums[2:4] + served, sums[4:]]).reshape(pair_dev)
     place = (bases[:, None] + jnp.arange(cap, dtype=i32)[None, :]).reshape(pair_dev)
     spot = target[:, None] == place[None, :]
     energy = jnp.sum(jnp.where(spot, sums[None, :], 0.0), axis=1)
-    energy = (energy + lax.ppermute(energy, "aux", swap_core)) / nvd
+    energy = (energy + swap_core(energy)) / nvd
     return (energy, density)
 
 

time: 342 us -> 239 us (0.70)
  Pallas kernels: 166 us -> 86.5 us
  starting transfers between devices: 76.5 us -> 44.6 us
  local copies, waits for them, and re-layouts: 12.9 us -> 29.2 us
  waiting for transfers between devices: 76.2 us -> 60.5 us
  other arithmetic: 7.82 us -> 14.3 us
    pallas_call x16 -> x22, Pallas kernels: 155 us -> 69.3 us  [the longest x10 46.5 us: amplitudes(): pl.pallas_call(lambda *refs: amplitudes_kernel(mode, call, per_orb, len(a...]
    ppermute x25 -> x34, starting transfers between devices: 76.5 us -> 44.6 us  [the longest x29 43.5 us: pp(): return lax.ppermute(x, 'orb', perm)]
    ppermute x25 -> x34, waiting for transfers between devices: 76.2 us -> 60.5 us  [the longest x29 60.5 us: pp(): return lax.ppermute(x, 'orb', perm)]
    unnamed x47 -> x64, local copies, waits for them, and re-layouts: 4.38 us -> 13.8 us
    pallas_call x2 -> x6, Pallas kernels: 3.52 us -> 9.18 us  [turn(): pl.pallas_call(turn_kernel, out_shape=jax.ShapeDtypeStruct((count, cols,...]
  transfers between devices with their start and end apart: 25 -> 34, of which waited for: 4 -> 9; matrix products, arithmetic and copies ran while one was open for 4% -> 11% of each run, Pallas kernels for 46% -> 32%
where the time goes in v3:
time: 239 us; the launch traced here: 237 us
  Pallas kernels  86.5 us (36%)
  waiting for transfers between devices  60.5 us (25%)
  starting transfers between devices  44.6 us (19%)
  local copies, waits for them, and re-layouts  29.2 us (12%)
  other arithmetic  14.3 us (6%)
    ppermute x29, waiting for transfers between devices, pp(): return lax.ppermute(x, 'orb', perm)  60.5 us
    pallas_call x10, Pallas kernels, amplitudes(): pl.pallas_call(lambda *refs: amplitudes_kernel(mode, call, per_orb, len(a...  46.5 us
    ppermute x29, starting transfers between devices, pp(): return lax.ppermute(x, 'orb', perm)  43.5 us
    pallas_call x12, Pallas kernels, pack(): pl.pallas_call(lambda *refs: pack_kernel(call, len(after), *refs), out_sh...  22.9 us
    unnamed x64, local copies, waits for them, and re-layouts  13.8 us
    pallas_call x6, Pallas kernels, turn(): pl.pallas_call(turn_kernel, out_shape=jax.ShapeDtypeStruct((count, cols,...  9.18 us
    pallas_call x2, Pallas kernels, density_rows(): pl.pallas_call(density_kernel, out_shape=jax.ShapeDtypeStruct((occ, half,...  7.99 us
  transfers between devices with their start and end apart: 34, of which 9 were waited for; matrix products, arithmetic and copies ran while one was open for 11% of the time, Pallas kernels for 32%

profile of v3, /device:TPU:0, one launch (start us, length us, event | category | flops | bytes accessed | tf_op | source)
XLA Modules:
  0.0 236.8 jit_solution(12383814826634382238)
XLA Ops:
  5.3 3.0 %collective-permute-start.1 = (f32[24,384]{1,0:T(8,128)S(1)}, f32[24,384]{1,0:T(8,128)S(1)}, u32[]{:S(2)}, u32[]{:S(2)}) collective-permute-start(f32[24,384]{1,0:T(8,128)S(1)} %get-tuple-element.75), channel_id=1, source_target_pairs={{0,2},{2,0},{4,6},{6,4},{8,10},{10,8},{12,14},{14,12},{1,3},{3,1},... | collective-permute-start | bytes 110600 | tf_op jit(solution)/shard_map/ppermute | solution.py:346
  9.2 2.3 constant_dynamic-slice_fusion.1.refs_5_.refs_1_
  11.6 1.6 collective-permute-start.2
  13.3 2.6 %collective-permute-start.3 = (f32[2,24,384]{2,1,0:T(8,128)S(1)}, f32[2,24,384]{2,1,0:T(8,128)S(1)}, u32[]{:S(2)}, u32[]{:S(2)}) collective-permute-start(f32[2,24,384]{2,1,0:T(8,128)S(1)} %pad_maximum_fusion), channel_id=1, source_target_pairs={{0,8},{2,10},{4,12},{6,14},{8,0},{10,2},{12,4},{14,6},{1,9},{3,11}... | collective-permute-start | bytes 221192 | tf_op jit(solution)/shard_map/ppermute | solution.py:346
  16.4 5.8 %collective-permute-done.3 = f32[2,24,384]{2,1,0:T(8,128)S(1)} collective-permute-done((f32[2,24,384]{2,1,0:T(8,128)S(1)}, f32[2,24,384]{2,1,0:T(8,128)S(1)}, u32[]{:S(2)}, u32[]{:S(2)}) %collective-permute-start.3) | collective-permute-done | bytes 73760 | tf_op jit(solution)/shard_map/ppermute | solution.py:346
  26.8 1.7 collective-permute-start.5
  29.2 3.4 %collective-permute-start.6 = (bf16[16,256,128]{2,1,0:T(8,128)(2,1)S(1)}, bf16[16,256,128]{2,1,0:T(8,128)(2,1)S(1)}, u32[]{:S(2)}, u32[]{:S(2)}) collective-permute-start(bf16[16,256,128]{2,1,0:T(8,128)(2,1)S(1)} %constant_dynamic-slice_fusion.refs_6_.refs_1_), channel_id=1, source_target_pairs={{0,4},{2,6},{4,0},{6,2},{8,12},{10,14},{12,8},{14,10},{1,5},{3,7},... | collective-permute-start | bytes 3145736 | tf_op jit(solution)/shard_map/ppermute | solution.py:346
  33.3 1.7 pack.12
  35.7 2.1 pack.13
  37.8 15.4 %collective-permute-done.5.refs_1_.refs_5_.x = bf16[16,256,128]{2,1,0:T(8,128)(2,1)} collective-permute-done((bf16[16,256,128]{2,1,0:T(8,128)(2,1)}, bf16[16,256,128]{2,1,0:T(8,128)(2,1)}, u32[]{:S(2)}, u32[]{:S(2)}) %collective-permute-start.5) | collective-permute-done | bytes 1048608 | tf_op jit(solution)/shard_map/ppermute | solution.py:346
  58.0 3.0 %broadcast_in_dim.96.refs_7_ = bf16[64,256,128]{2,1,0:T(8,128)(2,1)} broadcast(bf16[]{:T(256)} %constant.107.clone.1), dimensions={} | broadcast | bytes 4194306 | tf_op jit(solution)/shard_map/broadcast_in_dim | solution.py:417
  61.0 5.7 %amplitudes.10 = (bf16[64,256,128]{2,1,0:T(8,128)(2,1)}, f32[8,8,128]{2,1,0:T(8,128)S(1)}) custom-call(s32[266]{0:T(512)S(1)} %concatenate.58.refs_0_, f32[64,128]{1,0:T(8,128)S(1)} %dynamic-slice_subtract_fusion.1.refs_1_, f32[16,256,128]{2,1,0:T(8,128)S(1)} %broadcast_in_dim.95.refs_2_, ...), custom_call_target="tpu_custom_call", output_to_operand_aliasing={{0}: (7, {})} | custom-call | flops 268435456 | bytes 4718592 | tf_op jit(solution)/shard_map/amplitudes/pallas_call | solution.py:268
  66.7 1.7 pack.14.refs_2_
  68.4 2.1 pack.15.refs_2_
  73.2 2.4 collective-permute-done.6.refs_1_.refs_6_.x
  75.6 2.1 pack.17.refs_2_
  77.8 2.1 pack.18.refs_2_
  87.4 9.3 %collective-permute-done.19.refs_9_ = bf16[8,256,128]{2,1,0:T(8,128)(2,1)} collective-permute-done((bf16[8,256,128]{2,1,0:T(8,128)(2,1)}, bf16[8,256,128]{2,1,0:T(8,128)(2,1)}, u32[]{:S(2)}, u32[]{:S(2)}) %collective-permute-start.19) | collective-permute-done | bytes 524320 | tf_op jit(solution)/shard_map/ppermute | solution.py:346
  97.2 1.6 collective-permute-start.14
  98.8 1.6 collective-permute-start.15
  106.5 2.2 collective-permute-done.16.refs_5_
  110.2 2.2 collective-permute-start.26
  113.1 2.5 %turn.8.refs_3_ = bf16[16,128,256]{2,1,0:T(8,128)(2,1)S(1)} custom-call(bf16[16,256,128]{2,1,0:T(8,128)(2,1)} %collective-permute-done.5.refs_1_.refs_5_.x), custom_call_target="tpu_custom_call" | custom-call | bytes 2097152 | tf_op jit(solution)/shard_map/turn/pallas_call | solution.py:135
  116.1 7.0 %amplitudes.11 = (bf16[64,256,128]{2,1,0:T(8,128)(2,1)}, f32[8,8,128]{2,1,0:T(8,128)S(1)}) custom-call(s32[266]{0:T(512)S(1)} %concatenate.58.refs_0_, f32[64,128]{1,0:T(8,128)S(1)} %dynamic-slice_subtract_fusion.1.refs_1_, f32[16,256,128]{2,1,0:T(8,128)S(1)} %broadcast_in_dim.95.refs_2_, ...), custom_call_target="tpu_custom_call", output_to_operand_aliasing={{0}: (8, {})} | custom-call | flops 268435456 | bytes 4718592 | tf_op jit(solution)/shard_map/amplitudes/pallas_call | solution.py:268
  123.1 5.7 %amplitudes.12 = (bf16[64,256,128]{2,1,0:T(8,128)(2,1)}, f32[8,8,128]{2,1,0:T(8,128)S(1)}) custom-call(s32[266]{0:T(512)S(1)} %concatenate.58.refs_0_, f32[64,128]{1,0:T(8,128)S(1)} %dynamic-slice_subtract_fusion.1.refs_1_, f32[16,256,128]{2,1,0:T(8,128)S(1)} %broadcast_in_dim.95.refs_2_, ...), custom_call_target="tpu_custom_call", output_to_operand_aliasing={{0}: (7, {})} | custom-call | flops 268435456 | bytes 4718592 | tf_op jit(solution)/shard_map/amplitudes/pallas_call | solution.py:268
  128.9 2.3 turn.10.refs_5_
  131.2 2.3 turn.11.refs_6_
  133.5 2.0 broadcast_in_dim.98.refs_2_
  135.5 2.2 amplitudes.13
  137.8 5.1 %amplitudes.14 = (bf16[64,256,128]{2,1,0:T(8,128)(2,1)}, f32[8,8,128]{2,1,0:T(8,128)S(1)}) custom-call(s32[266]{0:T(512)S(1)} %concatenate.58.refs_0_, f32[64,128]{1,0:T(8,128)S(1)} %dynamic-slice_subtract_fusion.1.refs_1_, f32[16,256,128]{2,1,0:T(8,128)S(1)} %broadcast_in_dim.95.refs_2_, ...), custom_call_target="tpu_custom_call", output_to_operand_aliasing={{0}: (10, {})} | custom-call | flops 268435456 | bytes 4718592 | tf_op jit(solution)/shard_map/amplitudes/pallas_call | solution.py:268
  142.9 3.7 %collective-permute-start.25 = (bf16[8,256,128]{2,1,0:T(8,128)(2,1)}, bf16[8,256,128]{2,1,0:T(8,128)(2,1)}, u32[]{:S(2)}, u32[]{:S(2)}) collective-permute-start(bf16[8,256,128]{2,1,0:T(8,128)(2,1)} %collective-permute-done.18.refs_8_), channel_id=1, source_target_pairs={{0,2},{2,0},{12,14},{14,12},{1,3},{3,1},{13,15},{15,13},{16,18},{1... | collective-permute-start | bytes 1572872 | tf_op jit(solution)/shard_map/ppermute | solution.py:346
  146.6 2.5 %pack.20.refs_2_ = bf16[8,256,128]{2,1,0:T(8,128)(2,1)} custom-call(s32[74]{0:T(128)S(1)} %get-tuple-element.38.refs_0_, bf16[16,256,128]{2,1,0:T(8,128)(2,1)} %collective-permute-done.14.refs_1_.refs_7_.refs_5_, f32[8,8,128]{2,1,0:T(8,128)S(1)} %get-tuple-element.45.refs_2_), custom_call_target="tpu_custom_call" | custom-call | bytes 1048576 | tf_op jit(solution)/shard_map/pack/pallas_call | solution.py:113
  149.1 1.7 pack.21.refs_2_
  152.2 2.5 %pack.22.refs_2_ = bf16[8,256,128]{2,1,0:T(8,128)(2,1)} custom-call(s32[74]{0:T(128)S(1)} %get-tuple-element.38.refs_0_, bf16[16,256,128]{2,1,0:T(8,128)(2,1)} %collective-permute-done.15.refs_1_.refs_8_.refs_6_, bf16[8,256,128]{2,1,0:T(8,128)(2,1)S(1)} %pack.21.refs_2_), custom_call_target="tpu_custom_call" | custom-call | bytes 1048576 | tf_op jit(solution)/shard_map/pack/pallas_call | solution.py:113
  157.3 1.7 pack.23.refs_9_
  159.0 2.0 amplitudes.15
  164.0 6.8 %collective-permute-done.20.refs_9_ = bf16[8,256,128]{2,1,0:T(8,128)(2,1)} collective-permute-done((bf16[8,256,128]{2,1,0:T(8,128)(2,1)}, bf16[8,256,128]{2,1,0:T(8,128)(2,1)}, u32[]{:S(2)}, u32[]{:S(2)}) %collective-permute-start.20) | collective-permute-done | bytes 524320 | tf_op jit(solution)/shard_map/ppermute | solution.py:346
  171.5 10.5 %collective-permute-done.22.refs_8_ = bf16[8,256,128]{2,1,0:T(8,128)(2,1)} collective-permute-done((bf16[8,256,128]{2,1,0:T(8,128)(2,1)}, bf16[8,256,128]{2,1,0:T(8,128)(2,1)}, u32[]{:S(2)}, u32[]{:S(2)}) %collective-permute-start.22) | collective-permute-done | bytes 524320 | tf_op jit(solution)/shard_map/ppermute | solution.py:346
  182.0 3.4 %collective-permute-start.30 = (bf16[8,256,128]{2,1,0:T(8,128)(2,1)}, bf16[8,256,128]{2,1,0:T(8,128)(2,1)S(1)}, u32[]{:S(2)}, u32[]{:S(2)}) collective-permute-start(bf16[8,256,128]{2,1,0:T(8,128)(2,1)} %collective-permute-done.22.refs_8_), channel_id=1, source_target_pairs={{0,2},{2,0},{12,14},{14,12},{1,3},{3,1},{13,15},{15,13},{16,18},{1... | collective-permute-start | bytes 1572872 | tf_op jit(solution)/shard_map/ppermute | solution.py:346
  185.5 7.8 %collective-permute-done.13.refs_7_ = bf16[8,256,128]{2,1,0:T(8,128)(2,1)} collective-permute-done((bf16[8,256,128]{2,1,0:T(8,128)(2,1)}, bf16[8,256,128]{2,1,0:T(8,128)(2,1)}, u32[]{:S(2)}, u32[]{:S(2)}) %collective-permute-start.13) | collective-permute-done | bytes 524320 | tf_op jit(solution)/shard_map/ppermute | solution.py:346
  193.3 3.4 %collective-permute-start.29 = (bf16[8,256,128]{2,1,0:T(8,128)(2,1)}, bf16[8,256,128]{2,1,0:T(8,128)(2,1)S(1)}, u32[]{:S(2)}, u32[]{:S(2)}) collective-permute-start(bf16[8,256,128]{2,1,0:T(8,128)(2,1)} %collective-permute-done.20.refs_9_), channel_id=1, source_target_pairs={{0,2},{2,0},{12,14},{14,12},{1,3},{3,1},{13,15},{15,13},{16,18},{1... | collective-permute-start | bytes 1572872 | tf_op jit(solution)/shard_map/ppermute | solution.py:346
  198.5 3.0 %amplitudes.16 = (bf16[64,256,128]{2,1,0:T(8,128)(2,1)}, f32[8,8,128]{2,1,0:T(8,128)S(1)}) custom-call(s32[266]{0:T(512)S(1)} %concatenate.58.refs_0_, f32[64,128]{1,0:T(8,128)S(1)} %dynamic-slice_subtract_fusion.1.refs_1_, f32[16,256,128]{2,1,0:T(8,128)S(1)} %broadcast_in_dim.95.refs_2_, ...), custom_call_target="tpu_custom_call", output_to_operand_aliasing={{0}: (10, {})} | custom-call | flops 268435456 | bytes 4718592 | tf_op jit(solution)/shard_map/amplitudes/pallas_call | solution.py:268
  201.6 5.9 %amplitudes.17 = (bf16[64,256,128]{2,1,0:T(8,128)(2,1)}, f32[8,8,128]{2,1,0:T(8,128)S(1)}) custom-call(s32[266]{0:T(512)S(1)} %concatenate.58.refs_0_, f32[64,128]{1,0:T(8,128)S(1)} %dynamic-slice_subtract_fusion.1.refs_1_, f32[16,256,128]{2,1,0:T(8,128)S(1)} %broadcast_in_dim.95.refs_2_, ...), custom_call_target="tpu_custom_call", output_to_operand_aliasing={{0}: (9, {})} | custom-call | flops 268435456 | bytes 4718592 | tf_op jit(solution)/shard_map/amplitudes/pallas_call | solution.py:268
  207.5 3.0 %amplitudes.18 = (bf16[64,256,128]{2,1,0:T(8,128)(2,1)}, f32[8,8,128]{2,1,0:T(8,128)S(1)}) custom-call(s32[266]{0:T(512)S(1)} %concatenate.58.refs_0_, f32[64,128]{1,0:T(8,128)S(1)} %dynamic-slice_subtract_fusion.1.refs_1_, f32[16,256,128]{2,1,0:T(8,128)S(1)} %broadcast_in_dim.95.refs_2_, ...), custom_call_target="tpu_custom_call", output_to_operand_aliasing={{0}: (9, {})} | custom-call | flops 268435456 | bytes 4718592 | tf_op jit(solution)/shard_map/amplitudes/pallas_call | solution.py:268
  210.6 6.7 %amplitudes.19 = (bf16[64,256,128]{2,1,0:T(8,128)(2,1)}, f32[8,8,128]{2,1,0:T(8,128)S(1)}) custom-call(s32[266]{0:T(512)S(1)} %concatenate.58.refs_0_, f32[64,128]{1,0:T(8,128)S(1)} %dynamic-slice_subtract_fusion.1.refs_1_, f32[16,256,128]{2,1,0:T(8,128)S(1)} %broadcast_in_dim.95.refs_2_, ...), custom_call_target="tpu_custom_call", output_to_operand_aliasing={{0}: (9, {})} | custom-call | flops 268435456 | bytes 4718592 | tf_op jit(solution)/shard_map/amplitudes/pallas_call | solution.py:268
  217.3 4.0 %density_rows.3 = f32[16,128,256]{2,1,0:T(8,128)S(1)} custom-call(s32[1]{0:T(128)} %bitcast.38.start, bf16[64,256,128]{2,1,0:T(8,128)(2,1)} %get-tuple-element.57.t), custom_call_target="tpu_custom_call" | custom-call | flops 536870912 | bytes 6291456 | tf_op jit(solution)/shard_map/density_rows/pallas_call | solution.py:312
  229.0 4.0 %density_rows.2 = f32[16,128,256]{2,1,0:T(8,128)S(1)} custom-call(s32[1]{0:T(128)} %bitcast.8.start, bf16[64,256,128]{2,1,0:T(8,128)(2,1)} %get-tuple-element.57.t), custom_call_target="tpu_custom_call" | custom-call | flops 536870912 | bytes 6291456 | tf_op jit(solution)/shard_map/density_rows/pallas_call | solution.py:312
  233.6 3.2 %add.116 = f32[16,128,256]{2,1,0:T(8,128)} add(f32[16,128,256]{2,1,0:T(8,128)S(1)} %density_rows.2, f32[16,128,256]{2,1,0:T(8,128)} %collective-permute-done.33) | non-fusion elementwise | flops 524288 | bytes 6291456 | tf_op jit(solution)/shard_map/add | solution.py:467
  (182 shorter events, 54.3 us)
Async XLA Ops:
  5.3 6.3 %collective-permute-start.1 = (f32[24,384]{1,0:T(8,128)S(1)}, f32[24,384]{1,0:T(8,128)S(1)}, u32[]{:S(2)}, u32[]{:S(2)}) collective-permute-start(f32[24,384]{1,0:T(8,128)S(1)} %get-tuple-element.75), channel_id=1, source_target_pairs={{0,2},{2,0},{4,6},{6,4},{8,10},{10,8},{12,14},{14,12},{1,3},{3,1},... | collective-permute-start | bytes 110600 | tf_op jit(solution)/shard_map/ppermute | solution.py:346
  8.3 16.5 %collective-permute-start = (bf16[16,256,256]{2,1,0:T(8,128)(2,1)}, bf16[16,256,256]{2,1,0:T(8,128)(2,1)S(1)}, u32[]{:S(2)}, u32[]{:S(2)}) collective-permute-start(bf16[16,256,256]{2,1,0:T(8,128)(2,1)} %x.3), channel_id=1, source_target_pairs={{0,1},{1,0},{2,3},{3,2},{4,5},{5,4},{6,7},{7,6},{8,9},{9,8},{10,11... | collective-permute-start | bytes 6291464 | tf_op jit(solution)/shard_map/ppermute | solution.py:349
  11.6 4.7 %collective-permute-start.2 = (f32[2,24,384]{2,1,0:T(8,128)S(1)}, f32[2,24,384]{2,1,0:T(8,128)S(1)}, u32[]{:S(2)}, u32[]{:S(2)}) collective-permute-start(f32[2,24,384]{2,1,0:T(8,128)S(1)} %pad_maximum_fusion), channel_id=1, source_target_pairs={{0,4},{2,6},{4,0},{6,2},{8,12},{10,14},{12,8},{14,10},{1,5},{3,7},... | collective-permute-start | bytes 221192 | tf_op jit(solution)/shard_map/ppermute | solution.py:346
  13.3 8.9 %collective-permute-start.3 = (f32[2,24,384]{2,1,0:T(8,128)S(1)}, f32[2,24,384]{2,1,0:T(8,128)S(1)}, u32[]{:S(2)}, u32[]{:S(2)}) collective-permute-start(f32[2,24,384]{2,1,0:T(8,128)S(1)} %pad_maximum_fusion), channel_id=1, source_target_pairs={{0,8},{2,10},{4,12},{6,14},{8,0},{10,2},{12,4},{14,6},{1,9},{3,11}... | collective-permute-start | bytes 221192 | tf_op jit(solution)/shard_map/ppermute | solution.py:346
  15.9 6.4 %collective-permute-start.4 = (f32[2,24,384]{2,1,0:T(8,128)S(1)}, f32[2,24,384]{2,1,0:T(8,128)S(1)}, u32[]{:S(2)}, u32[]{:S(2)}) collective-permute-start(f32[2,24,384]{2,1,0:T(8,128)S(1)} %pad_maximum_fusion), channel_id=1, source_target_pairs={{0,12},{2,14},{4,8},{6,10},{8,4},{10,6},{12,0},{14,2},{1,13},{3,15... | collective-permute-start | bytes 221192 | tf_op jit(solution)/shard_map/ppermute | solution.py:346
  16.4 6.0 %copy-start.25 = (f32[2,24,384]{2,1,0:T(8,128)}, f32[2,24,384]{2,1,0:T(8,128)S(1)}, u32[]{:S(2)}) copy-start(f32[2,24,384]{2,1,0:T(8,128)S(1)} %collective-permute-done.2) | copy-start | bytes 221188
  26.7 27.0 %copy-start.8 = (bf16[16,256,256]{2,1,0:T(8,128)(2,1)S(1)}, bf16[16,256,256]{2,1,0:T(8,128)(2,1)}, u32[]{:S(2)}) copy-start(bf16[16,256,256]{2,1,0:T(8,128)(2,1)} %x.3) | copy-start | bytes 6291460
  26.8 26.5 %collective-permute-start.5 = (bf16[16,256,128]{2,1,0:T(8,128)(2,1)}, bf16[16,256,128]{2,1,0:T(8,128)(2,1)}, u32[]{:S(2)}, u32[]{:S(2)}) collective-permute-start(bf16[16,256,128]{2,1,0:T(8,128)(2,1)} %constant_dynamic-slice_fusion.1.refs_5_.refs_1_), channel_id=1, source_target_pairs={{0,4},{2,6},{4,0},{6,2},{8,12},{10,14},{12,8},{14,10},{1,5},{3,7},... | collective-permute-start | bytes 3145736 | tf_op jit(solution)/shard_map/ppermute | solution.py:346
  28.5 40.0 %collective-permute-start.10 = (bf16[16,256,128]{2,1,0:T(8,128)(2,1)}, bf16[16,256,128]{2,1,0:T(8,128)(2,1)S(1)}, u32[]{:S(2)}, u32[]{:S(2)}) collective-permute-start(bf16[16,256,128]{2,1,0:T(8,128)(2,1)} %constant_dynamic-slice_fusion.1.refs_5_.refs_1_), channel_id=1, source_target_pairs={{4,8},{6,10},{8,4},{10,6},{5,9},{7,11},{9,5},{11,7},{20,24},{22,26... | collective-permute-start | bytes 3145736 | tf_op jit(solution)/shard_map/ppermute | solution.py:346
  29.2 46.4 %collective-permute-start.6 = (bf16[16,256,128]{2,1,0:T(8,128)(2,1)S(1)}, bf16[16,256,128]{2,1,0:T(8,128)(2,1)S(1)}, u32[]{:S(2)}, u32[]{:S(2)}) collective-permute-start(bf16[16,256,128]{2,1,0:T(8,128)(2,1)S(1)} %constant_dynamic-slice_fusion.refs_6_.refs_1_), channel_id=1, source_target_pairs={{0,4},{2,6},{4,0},{6,2},{8,12},{10,14},{12,8},{14,10},{1,5},{3,7},... | collective-permute-start | bytes 3145736 | tf_op jit(solution)/shard_map/ppermute | solution.py:346
  32.6 45.2 %collective-permute-start.9 = (bf16[16,256,128]{2,1,0:T(8,128)(2,1)S(1)}, bf16[16,256,128]{2,1,0:T(8,128)(2,1)S(1)}, u32[]{:S(2)}, u32[]{:S(2)}) collective-permute-start(bf16[16,256,128]{2,1,0:T(8,128)(2,1)S(1)} %constant_dynamic-slice_fusion.refs_6_.refs_1_), channel_id=1, source_target_pairs={{4,8},{6,10},{8,4},{10,6},{5,9},{7,11},{9,5},{11,7},{20,24},{22,26... | collective-permute-start | bytes 3145736 | tf_op jit(solution)/shard_map/ppermute | solution.py:346
  35.0 47.2 %collective-permute-start.7 = (bf16[8,256,128]{2,1,0:T(8,128)(2,1)S(1)}, bf16[8,256,128]{2,1,0:T(8,128)(2,1)S(1)}, u32[]{:S(2)}, u32[]{:S(2)}) collective-permute-start(bf16[8,256,128]{2,1,0:T(8,128)(2,1)S(1)} %pack.12), channel_id=1, source_target_pairs={{0,2},{2,0},{4,6},{6,4},{8,10},{10,8},{12,14},{14,12},{1,3},{3,1},... | collective-permute-start | bytes 1572872 | tf_op jit(solution)/shard_map/ppermute | solution.py:346
  37.8 18.0 %copy-start.10 = (bf16[16,256,256]{2,1,0:T(8,128)(2,1)S(1)}, bf16[16,256,256]{2,1,0:T(8,128)(2,1)}, u32[]{:S(2)}) copy-start(bf16[16,256,256]{2,1,0:T(8,128)(2,1)} %copy-done.9) | copy-start | bytes 6291460
  53.2 31.9 %collective-permute-start.8 = (bf16[8,256,128]{2,1,0:T(8,128)(2,1)}, bf16[8,256,128]{2,1,0:T(8,128)(2,1)}, u32[]{:S(2)}, u32[]{:S(2)}) collective-permute-start(bf16[8,256,128]{2,1,0:T(8,128)(2,1)} %pack.13), channel_id=1, source_target_pairs={{0,2},{2,0},{4,6},{6,4},{8,10},{10,8},{12,14},{14,12},{1,3},{3,1},... | collective-permute-start | bytes 1572872 | tf_op jit(solution)/shard_map/ppermute | solution.py:346
  68.4 4.8 %copy-start.15 = (bf16[8,256,128]{2,1,0:T(8,128)(2,1)}, bf16[8,256,128]{2,1,0:T(8,128)(2,1)S(1)}, u32[]{:S(2)}) copy-start(bf16[8,256,128]{2,1,0:T(8,128)(2,1)S(1)} %pack.14.refs_2_) | copy-start | bytes 1572868
  70.6 28.3 %collective-permute-start.18 = (bf16[8,256,128]{2,1,0:T(8,128)(2,1)}, bf16[8,256,128]{2,1,0:T(8,128)(2,1)}, u32[]{:S(2)}, u32[]{:S(2)}) collective-permute-start(bf16[8,256,128]{2,1,0:T(8,128)(2,1)} %pack.15.refs_2_), channel_id=1, source_target_pairs={{4,0},{6,2},{8,12},{10,14},{5,1},{7,3},{9,13},{11,15},{20,16},{22,... | collective-permute-start | bytes 1572872 | tf_op jit(solution)/shard_map/ppermute | solution.py:346
  73.2 4.5 %copy-start.11 = (bf16[8,256,128]{2,1,0:T(8,128)(2,1)}, bf16[8,256,128]{2,1,0:T(8,128)(2,1)S(1)}, u32[]{:S(2)}) copy-start(bf16[8,256,128]{2,1,0:T(8,128)(2,1)S(1)} %pack.16.refs_2_) | copy-start | bytes 1572868
  75.6 4.4 %copy-start.6 = (bf16[16,256,128]{2,1,0:T(8,128)(2,1)}, bf16[16,256,128]{2,1,0:T(8,128)(2,1)S(1)}, u32[]{:S(2)}) copy-start(bf16[16,256,128]{2,1,0:T(8,128)(2,1)S(1)} %collective-permute-done.6.refs_1_.refs_6_.x) | copy-start | bytes 3145732
  77.7 19.5 %collective-permute-start.17 = (bf16[8,256,128]{2,1,0:T(8,128)(2,1)}, bf16[8,256,128]{2,1,0:T(8,128)(2,1)}, u32[]{:S(2)}, u32[]{:S(2)}) collective-permute-start(bf16[8,256,128]{2,1,0:T(8,128)(2,1)} %pack.17.refs_2_), channel_id=1, source_target_pairs={{0,2},{2,0},{4,6},{6,4},{8,10},{10,8},{12,14},{14,12},{1,3},{3,1},... | collective-permute-start | bytes 1572872 | tf_op jit(solution)/shard_map/ppermute | solution.py:346
  80.9 15.7 %collective-permute-start.19 = (bf16[8,256,128]{2,1,0:T(8,128)(2,1)}, bf16[8,256,128]{2,1,0:T(8,128)(2,1)}, u32[]{:S(2)}, u32[]{:S(2)}) collective-permute-start(bf16[8,256,128]{2,1,0:T(8,128)(2,1)} %pack.18.refs_2_), channel_id=1, source_target_pairs={{4,0},{6,2},{8,12},{10,14},{5,1},{7,3},{9,13},{11,15},{20,16},{22,... | collective-permute-start | bytes 1572872 | tf_op jit(solution)/shard_map/ppermute | solution.py:346
  83.1 26.3 %collective-permute-start.11 = (bf16[16,256,128]{2,1,0:T(8,128)(2,1)}, bf16[16,256,128]{2,1,0:T(8,128)(2,1)}, u32[]{:S(2)}, u32[]{:S(2)}) collective-permute-start(bf16[16,256,128]{2,1,0:T(8,128)(2,1)} %collective-permute-done.5.refs_1_.refs_5_.x), channel_id=1, source_target_pairs={{0,1},{1,0},{2,3},{3,2},{4,5},{5,4},{6,7},{7,6},{8,9},{9,8},{10,11... | collective-permute-start | bytes 3145736 | tf_op jit(solution)/shard_map/ppermute | solution.py:349
  85.1 25.1 %collective-permute-start.12 = (bf16[16,256,128]{2,1,0:T(8,128)(2,1)}, bf16[16,256,128]{2,1,0:T(8,128)(2,1)}, u32[]{:S(2)}, u32[]{:S(2)}) collective-permute-start(bf16[16,256,128]{2,1,0:T(8,128)(2,1)} %copy-done.6), channel_id=1, source_target_pairs={{0,1},{1,0},{2,3},{3,2},{4,5},{5,4},{6,7},{7,6},{8,9},{9,8},{10,11... | collective-permute-start | bytes 3145736 | tf_op jit(solution)/shard_map/ppermute | solution.py:349
  96.7 12.0 %collective-permute-start.16 = (bf16[8,256,128]{2,1,0:T(8,128)(2,1)}, bf16[8,256,128]{2,1,0:T(8,128)(2,1)}, u32[]{:S(2)}, u32[]{:S(2)}) collective-permute-start(bf16[8,256,128]{2,1,0:T(8,128)(2,1)} %copy-done.15), channel_id=1, source_target_pairs={{0,2},{2,0},{4,6},{6,4},{8,10},{10,8},{12,14},{14,12},{1,3},{3,1},... | collective-permute-start | bytes 1572872 | tf_op jit(solution)/shard_map/ppermute | solution.py:346
  97.2 45.7 %collective-permute-start.14 = (bf16[16,256,128]{2,1,0:T(8,128)(2,1)}, bf16[16,256,128]{2,1,0:T(8,128)(2,1)}, u32[]{:S(2)}, u32[]{:S(2)}) collective-permute-start(bf16[16,256,128]{2,1,0:T(8,128)(2,1)} %collective-permute-done.5.refs_1_.refs_5_.x), channel_id=1, source_target_pairs={{4,8},{6,10},{8,4},{10,6},{5,9},{7,11},{9,5},{11,7},{20,24},{22,26... | collective-permute-start | bytes 3145736 | tf_op jit(solution)/shard_map/ppermute | solution.py:346
  98.8 52.0 %collective-permute-start.15 = (bf16[16,256,128]{2,1,0:T(8,128)(2,1)}, bf16[16,256,128]{2,1,0:T(8,128)(2,1)}, u32[]{:S(2)}, u32[]{:S(2)}) collective-permute-start(bf16[16,256,128]{2,1,0:T(8,128)(2,1)} %copy-done.6), channel_id=1, source_target_pairs={{4,8},{6,10},{8,4},{10,6},{5,9},{7,11},{9,5},{11,7},{20,24},{22,26... | collective-permute-start | bytes 3145736 | tf_op jit(solution)/shard_map/ppermute | solution.py:346
  105.1 3.6 %copy-start.12 = (bf16[8,256,128]{2,1,0:T(8,128)(2,1)S(1)}, bf16[8,256,128]{2,1,0:T(8,128)(2,1)}, u32[]{:S(2)}) copy-start(bf16[8,256,128]{2,1,0:T(8,128)(2,1)} %copy-done.11) | copy-start | bytes 1572868
  105.1 10.5 %copy-start.7 = (bf16[16,256,128]{2,1,0:T(8,128)(2,1)S(1)}, bf16[16,256,128]{2,1,0:T(8,128)(2,1)}, u32[]{:S(2)}) copy-start(bf16[16,256,128]{2,1,0:T(8,128)(2,1)} %copy-done.6) | copy-start | bytes 3145732
  108.7 47.3 %collective-permute-start.23 = (bf16[8,256,128]{2,1,0:T(8,128)(2,1)S(1)}, bf16[8,256,128]{2,1,0:T(8,128)(2,1)S(1)}, u32[]{:S(2)}, u32[]{:S(2)}) collective-permute-start(bf16[8,256,128]{2,1,0:T(8,128)(2,1)S(1)} %copy-done.12), channel_id=1, source_target_pairs={{4,6},{6,4},{8,10},{10,8},{5,7},{7,5},{9,11},{11,9},{20,22},{22,20... | collective-permute-start | bytes 1572872 | tf_op jit(solution)/shard_map/ppermute | solution.py:346
  109.4 45.2 %collective-permute-start.24 = (bf16[8,256,128]{2,1,0:T(8,128)(2,1)S(1)}, bf16[8,256,128]{2,1,0:T(8,128)(2,1)S(1)}, u32[]{:S(2)}, u32[]{:S(2)}) collective-permute-start(bf16[8,256,128]{2,1,0:T(8,128)(2,1)S(1)} %pack.19.refs_7_), channel_id=1, source_target_pairs={{4,6},{6,4},{8,10},{10,8},{5,7},{7,5},{9,11},{11,9},{20,22},{22,20... | collective-permute-start | bytes 1572872 | tf_op jit(solution)/shard_map/ppermute | solution.py:346
  110.2 50.9 %collective-permute-start.26 = (bf16[8,256,128]{2,1,0:T(8,128)(2,1)}, bf16[8,256,128]{2,1,0:T(8,128)(2,1)S(1)}, u32[]{:S(2)}, u32[]{:S(2)}) collective-permute-start(bf16[8,256,128]{2,1,0:T(8,128)(2,1)} %collective-permute-done.19.refs_9_), channel_id=1, source_target_pairs={{0,2},{2,0},{12,14},{14,12},{1,3},{3,1},{13,15},{15,13},{16,18},{1... | collective-permute-start | bytes 1572872 | tf_op jit(solution)/shard_map/ppermute | solution.py:346
  142.9 20.4 %collective-permute-start.25 = (bf16[8,256,128]{2,1,0:T(8,128)(2,1)}, bf16[8,256,128]{2,1,0:T(8,128)(2,1)}, u32[]{:S(2)}, u32[]{:S(2)}) collective-permute-start(bf16[8,256,128]{2,1,0:T(8,128)(2,1)} %collective-permute-done.18.refs_8_), channel_id=1, source_target_pairs={{0,2},{2,0},{12,14},{14,12},{1,3},{3,1},{13,15},{15,13},{16,18},{1... | collective-permute-start | bytes 1572872 | tf_op jit(solution)/shard_map/ppermute | solution.py:346
  150.8 5.1 %copy-start.13 = (bf16[8,256,128]{2,1,0:T(8,128)(2,1)}, bf16[8,256,128]{2,1,0:T(8,128)(2,1)S(1)}, u32[]{:S(2)}) copy-start(bf16[8,256,128]{2,1,0:T(8,128)(2,1)S(1)} %pack.21.refs_2_) | copy-start | bytes 1572868
  150.9 19.9 %collective-permute-start.20 = (bf16[8,256,128]{2,1,0:T(8,128)(2,1)}, bf16[8,256,128]{2,1,0:T(8,128)(2,1)}, u32[]{:S(2)}, u32[]{:S(2)}) collective-permute-start(bf16[8,256,128]{2,1,0:T(8,128)(2,1)} %pack.20.refs_2_), channel_id=1, source_target_pairs={{4,0},{6,2},{8,12},{10,14},{5,1},{7,3},{9,13},{11,15},{20,16},{22,... | collective-permute-start | bytes 1572872 | tf_op jit(solution)/shard_map/ppermute | solution.py:346
  154.6 6.4 %copy-start.20 = (bf16[8,256,128]{2,1,0:T(8,128)(2,1)}, bf16[8,256,128]{2,1,0:T(8,128)(2,1)S(1)}, u32[]{:S(2)}) copy-start(bf16[8,256,128]{2,1,0:T(8,128)(2,1)S(1)} %collective-permute-done.24.refs_6_) | copy-start | bytes 1572868
  154.7 27.4 %collective-permute-start.22 = (bf16[8,256,128]{2,1,0:T(8,128)(2,1)}, bf16[8,256,128]{2,1,0:T(8,128)(2,1)}, u32[]{:S(2)}, u32[]{:S(2)}) collective-permute-start(bf16[8,256,128]{2,1,0:T(8,128)(2,1)} %pack.22.refs_2_), channel_id=1, source_target_pairs={{4,0},{6,2},{8,12},{10,14},{5,1},{7,3},{9,13},{11,15},{20,16},{22,... | collective-permute-start | bytes 1572872 | tf_op jit(solution)/shard_map/ppermute | solution.py:346
  156.0 5.1 %copy-start.18 = (bf16[8,256,128]{2,1,0:T(8,128)(2,1)}, bf16[8,256,128]{2,1,0:T(8,128)(2,1)S(1)}, u32[]{:S(2)}) copy-start(bf16[8,256,128]{2,1,0:T(8,128)(2,1)S(1)} %collective-permute-done.23.refs_5_) | copy-start | bytes 1572868
  156.0 37.3 %collective-permute-start.13 = (bf16[8,256,128]{2,1,0:T(8,128)(2,1)}, bf16[8,256,128]{2,1,0:T(8,128)(2,1)}, u32[]{:S(2)}, u32[]{:S(2)}) collective-permute-start(bf16[8,256,128]{2,1,0:T(8,128)(2,1)} %get-tuple-element.42), channel_id=1, source_target_pairs={{4,0},{6,2},{8,12},{10,14},{5,1},{7,3},{9,13},{11,15},{20,16},{22,... | collective-permute-start | bytes 1572872 | tf_op jit(solution)/shard_map/ppermute | solution.py:346
  159.0 37.7 %copy-start.26 = (s32[64,1]{0,1:T(1,128)S(1)}, s32[64,1]{0,1:T(1,128)}, u32[]{:S(2)}) copy-start(s32[64,1]{0,1:T(1,128)} %param.14) | copy-start | bytes 772
  161.9 45.6 %collective-permute-start.21 = (bf16[8,256,128]{2,1,0:T(8,128)(2,1)}, bf16[8,256,128]{2,1,0:T(8,128)(2,1)}, u32[]{:S(2)}, u32[]{:S(2)}) collective-permute-start(bf16[8,256,128]{2,1,0:T(8,128)(2,1)} %get-tuple-element.49), channel_id=1, source_target_pairs={{4,0},{6,2},{8,12},{10,14},{5,1},{7,3},{9,13},{11,15},{20,16},{22,... | collective-permute-start | bytes 1572872 | tf_op jit(solution)/shard_map/ppermute | solution.py:346
  163.3 47.2 %collective-permute-start.28 = (bf16[8,256,128]{2,1,0:T(8,128)(2,1)}, bf16[8,256,128]{2,1,0:T(8,128)(2,1)S(1)}, u32[]{:S(2)}, u32[]{:S(2)}) collective-permute-start(bf16[8,256,128]{2,1,0:T(8,128)(2,1)} %copy-done.14), channel_id=1, source_target_pairs={{4,6},{6,4},{8,10},{10,8},{5,7},{7,5},{9,11},{11,9},{20,22},{22,20... | collective-permute-start | bytes 1572872 | tf_op jit(solution)/shard_map/ppermute | solution.py:346
  170.8 39.7 %collective-permute-start.27 = (bf16[8,256,128]{2,1,0:T(8,128)(2,1)}, bf16[8,256,128]{2,1,0:T(8,128)(2,1)S(1)}, u32[]{:S(2)}, u32[]{:S(2)}) collective-permute-start(bf16[8,256,128]{2,1,0:T(8,128)(2,1)} %copy-done.13), channel_id=1, source_target_pairs={{4,6},{6,4},{8,10},{10,8},{5,7},{7,5},{9,11},{11,9},{20,22},{22,20... | collective-permute-start | bytes 1572872 | tf_op jit(solution)/shard_map/ppermute | solution.py:346
  182.0 28.5 %collective-permute-start.30 = (bf16[8,256,128]{2,1,0:T(8,128)(2,1)}, bf16[8,256,128]{2,1,0:T(8,128)(2,1)S(1)}, u32[]{:S(2)}, u32[]{:S(2)}) collective-permute-start(bf16[8,256,128]{2,1,0:T(8,128)(2,1)} %collective-permute-done.22.refs_8_), channel_id=1, source_target_pairs={{0,2},{2,0},{12,14},{14,12},{1,3},{3,1},{13,15},{15,13},{16,18},{1... | collective-permute-start | bytes 1572872 | tf_op jit(solution)/shard_map/ppermute | solution.py:346
  193.3 17.3 %collective-permute-start.29 = (bf16[8,256,128]{2,1,0:T(8,128)(2,1)}, bf16[8,256,128]{2,1,0:T(8,128)(2,1)S(1)}, u32[]{:S(2)}, u32[]{:S(2)}) collective-permute-start(bf16[8,256,128]{2,1,0:T(8,128)(2,1)} %collective-permute-done.20.refs_9_), channel_id=1, source_target_pairs={{0,2},{2,0},{12,14},{14,12},{1,3},{3,1},{13,15},{15,13},{16,18},{1... | collective-permute-start | bytes 1572872 | tf_op jit(solution)/shard_map/ppermute | solution.py:346
  198.5 3.0 %copy-start.21 = (bf16[8,256,128]{2,1,0:T(8,128)(2,1)S(1)}, bf16[8,256,128]{2,1,0:T(8,128)(2,1)}, u32[]{:S(2)}) copy-start(bf16[8,256,128]{2,1,0:T(8,128)(2,1)} %copy-done.20) | copy-start | bytes 1572868
  198.5 3.0 %copy-start.23 = (bf16[8,256,128]{2,1,0:T(8,128)(2,1)S(1)}, bf16[8,256,128]{2,1,0:T(8,128)(2,1)}, u32[]{:S(2)}) copy-start(bf16[8,256,128]{2,1,0:T(8,128)(2,1)} %copy-done.22) | copy-start | bytes 1572868
  221.3 12.3 %collective-permute-start.33 = (f32[16,128,256]{2,1,0:T(8,128)S(1)}, f32[16,128,256]{2,1,0:T(8,128)}, u32[]{:S(2)}, u32[]{:S(2)}) collective-permute-start(f32[16,128,256]{2,1,0:T(8,128)S(1)} %density_rows.3), channel_id=1, source_target_pairs={{0,1},{1,0},{2,3},{3,2},{4,5},{5,4},{6,7},{7,6},{8,9},{9,8},{10,11... | collective-permute-start | bytes 6291464 | tf_op jit(solution)/shard_map/ppermute | solution.py:349
  222.1 6.1 %collective-permute-start.31 = (f32[2,8]{1,0:T(2,128)S(1)}, f32[2,8]{1,0:T(2,128)S(1)}, u32[]{:S(2)}, u32[]{:S(2)}) collective-permute-start(f32[2,8]{1,0:T(2,128)S(1)} %maximum_reduce_fusion), channel_id=1, source_target_pairs={{4,0},{6,2},{8,12},{10,14},{5,1},{7,3},{9,13},{11,15},{20,16},{22,... | collective-permute-start | bytes 200 | tf_op jit(solution)/shard_map/ppermute | solution.py:346
  228.5 4.6 %collective-permute-start.32 = (f32[64]{0:T(128)S(1)}, f32[64]{0:T(128)S(1)}, u32[]{:S(2)}, u32[]{:S(2)}) collective-permute-start(f32[64]{0:T(128)S(1)} %select_reduce_fusion), channel_id=1, source_target_pairs={{0,1},{1,0},{2,3},{3,2},{4,5},{5,4},{6,7},{7,6},{8,9},{9,8},{10,11... | collective-permute-start | bytes 776 | tf_op jit(solution)/shard_map/ppermute | solution.py:349
  (13 other events, 20.9 us)

commit v4 on v0

--- a/solution.py
+++ b/solution.py
@@ -1,7 +1,15 @@
 import jax
 import jax.numpy as jnp
 from jax import lax
+from jax.experimental import pallas as pl
+from jax.experimental.pallas import tpu as pltpu
 from jax.sharding import PartitionSpec as P
+
+f32, bf16, i32 = jnp.float32, jnp.bfloat16, jnp.int32
+HBM = pl.BlockSpec(memory_space=pltpu.HBM)
+SMEM = pl.BlockSpec(memory_space=pltpu.SMEM)
+VMEM = pl.BlockSpec(memory_space=pltpu.VMEM)
+LIMIT = 48 * 1024 * 1024
 
 
 def slot_ranks(owner):
@@ -11,7 +19,7 @@
     return jnp.sum(same.astype(jnp.int32), axis=1)
 
 
-def on_device(blocks, vir_energy, occ_energy, domain_size, partner_owner, partner_slot):
+def by_requests(blocks, vir_energy, occ_energy, domain_size, partner_owner, partner_slot):
     occ_dev, half_aux, nvd = blocks.shape
     pair_dev = partner_slot.shape[0]
     per_orb = pair_dev // occ_dev
@@ -77,6 +85,413 @@
     return (energy, density)
 
 
+def fits_line(mesh):
+    return mesh.shape["orb"] == 8 and mesh.shape["aux"] == 2
+
+
+HEAD = 10
+
+
+def table_of(fields):
+    return jnp.concatenate([x.astype(i32) for x in fields])
+
+
+TINY = pl.CostEstimate(flops=1, bytes_accessed=1, transcendentals=0)
+PARAMS = pltpu.CompilerParams(vmem_limit_bytes=LIMIT)
+
+
+def pack_kernel(call, only_middle, relayed, after, tbl, *refs):
+    out, sems = refs[-2:]
+    halves, cap = out.shape[:2]
+    base = tbl[call]
+    middle = tbl[8] == 1
+
+    def run(copies):
+        for copy in copies:
+            copy.start()
+        for copy in copies:
+            copy.wait()
+
+    def gather():
+        run(
+            [
+                pltpu.make_async_copy(
+                    refs[q].at[tbl[HEAD + base + r]], out.at[q, r], sems.at[q, r]
+                )
+                for q in range(halves)
+                for r in range(cap)
+            ]
+        )
+
+    if not only_middle and not relayed:
+        gather()
+    else:
+        pl.when(middle)(gather)
+    if relayed:
+        came = refs[halves]
+
+        @pl.when(jnp.logical_not(middle))
+        def _():
+            run(
+                [pltpu.make_async_copy(came.at[q], out.at[q], sems.at[q, 0]) for q in range(halves)]
+            )
+
+
+def pack(tbl, call, sources, cap, only_middle=False, relayed=None, after=()):
+    halves = len(sources)
+    shape = (halves, cap) + sources[0].shape[1:]
+    operands = (*sources, *(() if relayed is None else (relayed,)), *after)
+    return pl.pallas_call(
+        lambda *refs: pack_kernel(call, only_middle, relayed is not None, len(after), *refs),
+        out_shape=jax.ShapeDtypeStruct(shape, bf16),
+        in_specs=[SMEM] + [HBM] * len(operands),
+        out_specs=VMEM,
+        scratch_shapes=[pltpu.SemaphoreType.DMA((halves, cap))],
+        compiler_params=PARAMS,
+        cost_estimate=TINY,
+        name="pack",
+    )(tbl, *operands)
+
+
+def turn_kernel(*refs):
+    half = len(refs) // 2
+    for x, out in zip(refs[:half], refs[half:]):
+        for r in range(x.shape[0]):
+            out[r] = x[r].T
+
+
+def turn(arrays):
+    count, rows, cols = arrays[0].shape
+    step = 4 if count % 4 == 0 else 1
+    n = len(arrays)
+    return pl.pallas_call(
+        turn_kernel,
+        out_shape=[jax.ShapeDtypeStruct((count, cols, rows), bf16)] * n,
+        grid=(count // step,),
+        in_specs=[pl.BlockSpec((step, rows, cols), lambda i: (i, 0, 0))] * n,
+        out_specs=[pl.BlockSpec((step, cols, rows), lambda i: (i, 0, 0))] * n,
+        compiler_params=PARAMS,
+        cost_estimate=TINY,
+        name="turn",
+    )(*arrays)
+
+
+def amplitudes_kernel(mode, call, per_orb, first, tbl, rows, vcol, *refs):
+    sv, s0, s1, b0, b1, st, se, sem, sem_out = refs[-9:]
+    client = mode == "client"
+    if client:
+        tout = refs[-10]
+        left, js = refs[:4], refs[4:6]
+    else:
+        tout, eout = refs[-11:-9]
+        left, js = refs[:2], refs[2:5]
+    if mode == "asked":
+        js = (js[0].at[0], js[0].at[1])
+    if mode == "asked_two":
+        js = (js[0].at[0], js[1].at[0])
+    cap = sv.shape[0]
+    n = rows.shape[0]
+    nvd, half = sv.shape[1], sv.shape[2]
+    base = tbl[call]
+    middle = tbl[8] == 1
+
+    def place(r):
+        return tbl[HEAD + base + r]
+
+    def run(copies):
+        for copy in copies:
+            copy.start()
+        for copy in copies:
+            copy.wait()
+
+    def load():
+        copies = []
+        for r in range(cap):
+            i = lax.div(place(r), per_orb)
+            slot = r if mode.startswith("asked") else tbl[HEAD + n + base + r]
+            todo = [
+                (vcol.at[i], sv.at[r]),
+                (js[0].at[slot], b0.at[r]),
+                (js[1].at[slot], b1.at[r]),
+            ]
+            if client:
+                here = pl.ds(pl.multiple_of(tbl[9], half), half)
+                there = pl.ds(pl.multiple_of(half - tbl[9], half), half)
+                todo += [
+                    (left[0].at[i], s0.at[r, here, :]),
+                    (left[1].at[i], s1.at[r, here, :]),
+                    (left[2].at[i], s1.at[r, there, :]),
+                    (left[3].at[i], s0.at[r, there, :]),
+                ]
+            else:
+                todo += [(left[0].at[i], s0.at[r]), (left[1].at[i], s1.at[r])]
+            copies += [
+                pltpu.make_async_copy(x, to, sem.at[r, k]) for k, (x, to) in enumerate(todo)
+            ]
+        run(copies)
+
+    def gaps():
+        row8 = rows[pl.ds(pl.multiple_of(base, cap), cap), :]
+        return [sv[r] + row8[r : r + 1, :] for r in range(cap)]
+
+    def make():
+        live_a = lax.broadcasted_iota(i32, (nvd, half), 0)
+        live_b = lax.broadcasted_iota(i32, (nvd, half), 1)
+        for r, gap in enumerate(gaps()):
+            size_i = tbl[HEAD + 2 * n + base + r]
+            size_j = tbl[HEAD + 3 * n + base + r]
+            k = jnp.dot(s0[r], b0[r], preferred_element_type=f32)
+            k += jnp.dot(s1[r], b1[r], preferred_element_type=f32)
+            k = jnp.where((live_a < size_i) & (live_b < size_j), k, 0.0)
+            t = (-k / gap).astype(bf16)
+            st[r] = t
+            if not client:
+                se[r : r + 1, :] = jnp.sum(k * t.astype(f32), axis=0, keepdims=True)
+
+    def take():
+        ready = js[2]
+        copies = [pltpu.make_async_copy(ready.at[r], st.at[r], sem.at[r, 0]) for r in range(cap)]
+        copies += [
+            pltpu.make_async_copy(vcol.at[lax.div(place(r), per_orb)], sv.at[r], sem.at[r, 1])
+            for r in range(cap)
+        ]
+        run(copies)
+        for r, gap in enumerate(gaps()):
+            t = st[r].astype(f32)
+            se[r : r + 1, :] = -jnp.sum(t * t * gap, axis=0, keepdims=True)
+
+    if client:
+
+        @pl.when(middle)
+        def _():
+            load()
+            make()
+            tout[...] = st[...]
+
+        return
+    if mode == "served":
+
+        @pl.when(middle)
+        def _():
+            load()
+            make()
+
+        pl.when(jnp.logical_not(middle))(take)
+    else:
+        load()
+        make()
+    run(
+        [pltpu.make_async_copy(st.at[r], tout.at[place(r)], sem_out.at[r]) for r in range(cap)]
+        + [
+            pltpu.make_async_copy(
+                se, eout.at[pl.ds(pl.multiple_of(base, cap), cap), :], sem_out.at[cap]
+            )
+        ]
+    )
+
+
+def amplitudes(mode, call, per_orb, tables, left, sources, cap, held=(), after=()):
+    tbl, rows, vcol = tables
+    occ, nvd, half = vcol.shape
+    qa = left[0].shape[2]
+    client = mode == "client"
+    operands = (tbl, rows, vcol, *left, *sources, *after)
+    aliases = {len(operands) + k: k for k in range(len(held))}
+    operands += tuple(held)
+    if client:
+        out_shape = jax.ShapeDtypeStruct((cap, nvd, half), bf16)
+        out_specs = VMEM
+    else:
+        out_shape = (
+            jax.ShapeDtypeStruct((occ * per_orb, nvd, half), bf16),
+            jax.ShapeDtypeStruct((occ * per_orb, half), f32),
+        )
+        out_specs = (HBM, HBM)
+    return pl.pallas_call(
+        lambda *refs: amplitudes_kernel(mode, call, per_orb, not held, *refs),
+        out_shape=out_shape,
+        in_specs=[SMEM, VMEM] + [HBM] * (len(operands) - 2),
+        out_specs=out_specs,
+        scratch_shapes=[
+            pltpu.VMEM((cap, nvd, half), f32),
+            pltpu.VMEM((cap, nvd, qa), bf16),
+            pltpu.VMEM((cap, nvd, qa), bf16),
+            pltpu.VMEM((cap, qa, half), bf16),
+            pltpu.VMEM((cap, qa, half), bf16),
+            pltpu.VMEM((cap, nvd, half), bf16),
+            pltpu.VMEM((cap, half), f32),
+            pltpu.SemaphoreType.DMA((cap, 7)),
+            pltpu.SemaphoreType.DMA((cap + 1,)),
+        ],
+        input_output_aliases=aliases,
+        compiler_params=PARAMS,
+        cost_estimate=TINY,
+        name="amplitudes",
+    )(*operands)
+
+
+def density_kernel(start, t, d):
+    count, half = d.shape[:2]
+    per_orb = t.shape[0] // count
+    first = pl.multiple_of(start[0], half)
+    for o in range(count):
+        own = range(o * per_orb, (o + 1) * per_orb)
+        left = jnp.concatenate([t[k, pl.ds(first, half), :] for k in own], axis=1)
+        right = jnp.concatenate([t[k] for k in own], axis=1)
+        d[o] = lax.dot_general(left, right, (((1,), (1,)), ((), ())), preferred_element_type=f32)
+
+
+def density_rows(t_all, start, per_orb, half):
+    npair, nvd, width = t_all.shape
+    occ = npair // per_orb
+    step = 4 if occ % 4 == 0 else 1
+    return pl.pallas_call(
+        density_kernel,
+        out_shape=jax.ShapeDtypeStruct((occ, half, nvd), f32),
+        grid_spec=pltpu.PrefetchScalarGridSpec(
+            num_scalar_prefetch=1,
+            grid=(occ // step,),
+            in_specs=[pl.BlockSpec((step * per_orb, nvd, width), lambda i, s: (i, 0, 0))],
+            out_specs=pl.BlockSpec((step, half, nvd), lambda i, s: (i, 0, 0)),
+        ),
+        compiler_params=pltpu.CompilerParams(vmem_limit_bytes=LIMIT),
+        cost_estimate=TINY,
+        name="density_rows",
+    )(start.reshape(1), t_all)
+
+
+def line_plan(blocks, vir_energy, occ_energy, domain_size, partner_owner, partner_slot):
+    occ, qa, nvd = blocks.shape
+    pair_dev = partner_slot.shape[0]
+    per_orb = pair_dev // occ
+    peers = 8
+    cap = pair_dev // peers
+    half = nvd // 2
+    wide = nvd + 128
+    me, core = lax.axis_index("orb"), lax.axis_index("aux")
+    z, y = me // 2, me % 2
+    lower = z < 2
+    middle = (z == 1) | (z == 2)
+    col0 = core * half
+
+    def pp(x, perm):
+        return lax.ppermute(x, "orb", perm)
+
+    def swap_core(x):
+        return lax.ppermute(x, "aux", [(0, 1), (1, 0)])
+
+    def flip(bit):
+        return [(o, o ^ bit) for o in range(peers)]
+
+    cross = [(2, 4), (3, 5), (4, 2), (5, 3)]
+    outward = [(2, 0), (3, 1), (4, 6), (5, 7)]
+    y_middle = [(2, 3), (3, 2), (4, 5), (5, 4)]
+    y_end = [(0, 1), (1, 0), (6, 7), (7, 6)]
+
+    other = swap_core(blocks)
+    first = lax.dynamic_slice_in_dim(blocks, col0, half, 2)
+    near_first, mid_first = pp(first, flip(2)), pp(first, cross)
+
+    owner = partner_owner[:, 0]
+    target = owner * cap + slot_ranks(owner)
+    pairs = jnp.arange(pair_dev, dtype=i32)
+    hit = target[None, :] == pairs[:, None]
+    order = jnp.sum(jnp.where(hit, pairs[None, :], 0), axis=1)
+    slots = jnp.sum(jnp.where(hit, partner_slot[None, :], 0), axis=1)
+    lists = jnp.concatenate([order, slots]).astype(f32)
+    small = jnp.concatenate(
+        [
+            jnp.concatenate(
+                [
+                    vir_energy,
+                    occ_energy[:, None],
+                    domain_size.astype(f32)[:, None],
+                    jnp.zeros((occ, wide - nvd - 2), f32),
+                ],
+                axis=1,
+            ),
+            jnp.pad(lists[None], ((0, 7), (0, wide - lists.shape[0]))),
+        ]
+    )
+    both = jnp.stack([small, pp(small, flip(1))])
+    every = jnp.concatenate([both] + [pp(both, flip(bit)) for bit in (2, 4, 6)])
+
+    column = jnp.stack([z, z ^ 1, jnp.where(lower, 2, 1), jnp.where(lower, 3, 0)])
+    bases = jnp.concatenate([column * 2 + y, column * 2 + (1 - y)]) * cap
+    head = [bases, middle[None], col0[None]]
+
+    def lists_of(x):
+        found = every[x, occ, : 2 * pair_dev].astype(i32)
+        return found[:pair_dev], found[pair_dev:]
+
+    def tables_of(x):
+        order, slots = lists_of(x)
+        theirs = jnp.take(orbitals, ((pairs // cap) ^ me) * occ + slots, axis=0)
+        mine = jnp.take(every[x, :occ], order // per_orb, axis=0)
+        rows = lax.dynamic_slice_in_dim(theirs, col0, half, 1) - (
+            theirs[:, nvd : nvd + 1] + mine[:, nvd : nvd + 1]
+        )
+        size_i, size_j = mine[:, nvd + 1], theirs[:, nvd + 1].astype(i32) - col0
+        vcol = jnp.broadcast_to(every[x, :occ, :nvd, None], (occ, nvd, half))
+        return table_of(head + [order, slots, size_i, size_j]), rows, vcol
+
+    second = lax.dynamic_slice_in_dim(other, col0, half, 2)
+    every, second = lax.optimization_barrier((every, second))
+    orbitals = every[:, :occ].reshape(peers * occ, wide)
+    tables = tables_of(0)
+    beside_list = table_of(head + [lists_of(1)[1]])
+    relay_list = table_of(head + [lists_of(3)[1]])
+    own = [first, second]
+    near = [near_first, pp(second, flip(2))]
+    mid = [mid_first, pp(second, cross)]
+    far = [pp(x, cross) for x in near]
+    left = turn([blocks, other])
+
+    def own_pairs(k, mode, sources, held=(), after=()):
+        return amplitudes(mode, k, per_orb, tables, left, sources, cap, held, after)
+
+    beside = pp(pack(beside_list, 0, own, cap), flip(1))
+    held = own_pairs(0, "slots", own)
+    packed = pack(beside_list, 1, near, cap, after=(held[1],))
+    beside_near = pp(packed, flip(1))
+    relay = pp(pack(relay_list, 2, mid, cap, only_middle=True, after=(packed,)), outward)
+    across = [swap_core(x) for x in near]
+    held = own_pairs(4, "asked", [beside], held, (packed,))
+    held = own_pairs(1, "slots", near, held)
+    client_left = turn(near + across)
+    client = tables_of(2)
+    gone = amplitudes("client", 2, per_orb, client, client_left, mid, cap, after=(held[1],))
+    ready_2 = pp(gone, outward)
+    held = own_pairs(5, "asked", [beside_near], held, (gone,))
+    packed = pack(beside_list, 2, mid, cap, relayed=relay, after=(held[1],))
+    third = pp(packed, flip(1))
+    relays = []
+    for x in far:
+        packed = pack(relay_list, 3, [x], cap, only_middle=True, after=(packed,))
+        relays.append(pp(packed, outward))
+    gone = amplitudes("client", 3, per_orb, client, client_left, far, cap, after=(packed,))
+    ready_3 = pp(gone, outward)
+    fourth = []
+    packed = gone
+    for x, came in zip(far, relays):
+        packed = pack(beside_list, 3, [x], cap, relayed=came, after=(packed,))
+        fourth.append(pp(packed, flip(1)))
+        if len(fourth) == 1:
+            held = own_pairs(2, "served", mid + [ready_2], held, (packed,))
+            held = own_pairs(6, "asked", [third], held)
+            packed = held[1]
+    held = own_pairs(3, "served", far + [ready_3], held, (packed,))
+    t_all, e_all = own_pairs(7, "asked_two", fourth, held)
+
+    away = swap_core(density_rows(t_all, (1 - core) * half, per_orb, half))
+    density = density_rows(t_all, core * half, per_orb, half) + away
+
+    sums = jnp.sum(e_all, axis=1)
+    energy = jnp.sum(jnp.where(hit, sums[:, None], 0.0), axis=0)
+    energy = (energy + swap_core(energy)) / nvd
+    return (energy, density)
+
+
 def solution(mesh):
     in_specs = (
         P(("mol", "orb"), "aux", None),
@@ -88,5 +503,5 @@
     )
     out_specs = (P(("mol", "orb")), P(("mol", "orb"), "aux", None))
     return jax.shard_map(
-        on_device, mesh=mesh, in_specs=in_specs, out_specs=out_specs, check_vma=False
-    )
+        line_plan if fits_line(mesh) else by_requests, mesh=mesh, in_specs=in_specs, out_specs=out_specs, check_vma=False
+    )

time: 332 us -> 196 us (0.59)
  waiting for transfers between devices: 209 us -> 56 us
  Pallas kernels: 0 us -> 75.5 us
  starting transfers between devices: 15.4 us -> 34.6 us
  matrix products: 19 us -> 0 us
  local copies, waits for them, and re-layouts: 34.2 us -> 16.5 us
  blocking collectives: 16 us -> 0 us
  between operations: 14.2 us -> 1.28 us
  other arithmetic: 22.8 us -> 10 us
    all_to_all x4 -> x0, waiting for transfers between devices: 196 us -> none  [the longest x1 182 us: on_device(): lax.all_to_all(send_blocks, 'orb', split_axis=0, concat_axis=0, tiled=True)]
    pallas_call x0 -> x22, Pallas kernels: none -> 75.5 us  [the longest x10 46.5 us: amplitudes(): pl.pallas_call(lambda *refs: amplitudes_kernel(mode, call, per_orb, not h...]
    ppermute x0 -> x25, waiting for transfers between devices: none -> 56 us  [the longest x20 56 us: pp(): return lax.ppermute(x, 'orb', perm)]
    ppermute x0 -> x25, starting transfers between devices: none -> 34.6 us  [the longest x20 33.3 us: pp(): return lax.ppermute(x, 'orb', perm)]
    gather x12 -> x4, local copies, waits for them, and re-layouts: 31.3 us -> 2.63 us  [the longest x2 1.32 us: tables_of(): mine = jnp.take(every[x, :occ], order // per_orb, axis=0)]
    dot_general x2 -> x0, matrix products: 19 us -> none  [the longest x1 11.5 us: on_device(): jnp.einsum('oqa,opqb->aopb', blocks, partner, preferred_element_type=jnp....]
    all_to_all x4 -> x0, starting transfers between devices: 15.3 us -> none  [the longest x1 5.09 us: on_device(): lax.all_to_all(send_blocks, 'orb', split_axis=0, concat_axis=0, tiled=True)]
    all_to_all x1 -> x0, blocking collectives: 13.5 us -> none  [on_device(): lax.all_to_all(requests, 'orb', split_axis=0, concat_axis=0, tiled=True)]
  transfers between devices with their start and end apart: 6 -> 25, of which waited for: 5 -> 8; matrix products, arithmetic and copies ran while one was open for 3% -> 9% of each run, Pallas kernels for 0% -> 33%
where the time goes in v4:
time: 196 us; the launch traced here: 194 us
  Pallas kernels  75.5 us (39%)
  waiting for transfers between devices  56 us (29%)
  starting transfers between devices  34.6 us (18%)
  local copies, waits for them, and re-layouts  16.5 us (8%)
  other arithmetic  10 us (5%)
    ppermute x20, waiting for transfers between devices, pp(): return lax.ppermute(x, 'orb', perm)  56 us
    pallas_call x10, Pallas kernels, amplitudes(): pl.pallas_call(lambda *refs: amplitudes_kernel(mode, call, per_orb, not h...  46.5 us
    ppermute x20, starting transfers between devices, pp(): return lax.ppermute(x, 'orb', perm)  33.3 us
    pallas_call x8, Pallas kernels, pack(): pl.pallas_call(lambda *refs: pack_kernel(call, only_middle, relayed is no...  14 us
    pallas_call x2, Pallas kernels, density_rows(): pl.pallas_call(density_kernel, out_shape=jax.ShapeDtypeStruct((occ, half,...  7.99 us
    pallas_call x2, Pallas kernels, turn(): pl.pallas_call(turn_kernel, out_shape=[jax.ShapeDtypeStruct((count, cols,...  6.97 us
    unnamed x43, local copies, waits for them, and re-layouts  5.02 us
    broadcast_in_dim x3, local copies, waits for them, and re-layouts, tables_of(): vcol = jnp.broadcast_to(every[x, :occ, :nvd, None], (occ, nvd, half))  3.94 us
  transfers between devices with their start and end apart: 25, of which 8 were waited for; matrix products, arithmetic and copies ran while one was open for 9% of the time, Pallas kernels for 33%

profile of v4, /device:TPU:0, one launch (start us, length us, event | category | flops | bytes accessed | tf_op | source)
XLA Modules:
  0.0 193.9 jit_solution(1891889380278348128)
XLA Ops:
  1.2 2.4 %constant_dynamic-slice_fusion.refs_5_.refs_1_ = bf16[16,256,128]{2,1,0:T(8,128)(2,1)} fusion(bf16[16,256,256]{2,1,0:T(8,128)(2,1)} %refs_0_.1, s32[]{:T(128)S(6)} %select_n.67), kind=kLoop, calls=%fused_computation.67 | loop fusion | bytes 2097156 | tf_op jit(solution)/shard_map/dynamic_slice | solution.py:392
  3.6 2.6 %collective-permute-start.5 = (bf16[16,256,128]{2,1,0:T(8,128)(2,1)}, bf16[16,256,128]{2,1,0:T(8,128)(2,1)}, u32[]{:S(2)}, u32[]{:S(2)}) collective-permute-start(bf16[16,256,128]{2,1,0:T(8,128)(2,1)} %constant_dynamic-slice_fusion.refs_5_.refs_1_), channel_id=1, source_target_pairs={{0,4},{2,6},{4,0},{6,2},{8,12},{10,14},{12,8},{14,10},{1,5},{3,7},... | collective-permute-start | bytes 3145736 | tf_op jit(solution)/shard_map/ppermute | solution.py:378
  8.2 1.5 collective-permute-start
  10.7 1.7 collective-permute-done
  12.4 4.3 %collective-permute-start.1 = (f32[2,24,384]{2,1,0:T(8,128)S(1)}, f32[2,24,384]{2,1,0:T(8,128)S(1)}, u32[]{:S(2)}, u32[]{:S(2)}) collective-permute-start(f32[2,24,384]{2,1,0:T(8,128)S(1)} %pad_maximum_fusion), channel_id=1, source_target_pairs={{0,4},{2,6},{4,0},{6,2},{8,12},{10,14},{12,8},{14,10},{1,5},{3,7},... | collective-permute-start | bytes 221192 | tf_op jit(solution)/shard_map/ppermute | solution.py:378
  16.7 15.1 %collective-permute-done.1 = f32[2,24,384]{2,1,0:T(8,128)S(1)} collective-permute-done((f32[2,24,384]{2,1,0:T(8,128)S(1)}, f32[2,24,384]{2,1,0:T(8,128)S(1)}, u32[]{:S(2)}, u32[]{:S(2)}) %collective-permute-start.1) | collective-permute-done | bytes 73760 | tf_op jit(solution)/shard_map/ppermute | solution.py:378
  31.8 3.8 %collective-permute-start.3 = (f32[2,24,384]{2,1,0:T(8,128)S(1)}, f32[2,24,384]{2,1,0:T(8,128)S(1)}, u32[]{:S(2)}, u32[]{:S(2)}) collective-permute-start(f32[2,24,384]{2,1,0:T(8,128)S(1)} %pad_maximum_fusion), channel_id=1, source_target_pairs={{0,12},{2,14},{4,8},{6,10},{8,4},{10,6},{12,0},{14,2},{1,13},{3,15... | collective-permute-start | bytes 221192 | tf_op jit(solution)/shard_map/ppermute | solution.py:378
  35.6 4.0 %collective-permute-done.2 = f32[2,24,384]{2,1,0:T(8,128)S(1)} collective-permute-done((f32[2,24,384]{2,1,0:T(8,128)S(1)}, f32[2,24,384]{2,1,0:T(8,128)S(1)}, u32[]{:S(2)}, u32[]{:S(2)}) %collective-permute-start.2) | collective-permute-done | bytes 73760 | tf_op jit(solution)/shard_map/ppermute | solution.py:378
  39.7 1.4 constant_dynamic-slice_fusion.1.refs_6_.refs_2_
  41.7 1.7 collective-permute-start.9
  43.4 1.7 collective-permute-start.8
  46.9 3.1 %pack.10 = bf16[2,8,256,128]{3,2,1,0:T(8,128)(2,1)} custom-call(s32[74]{0:T(128)S(1)} %pad_add_fusion.refs_0_, bf16[16,256,128]{2,1,0:T(8,128)(2,1)} %constant_dynamic-slice_fusion.refs_5_.refs_1_, bf16[16,256,128]{2,1,0:T(8,128)(2,1)} %constant_dynamic-slice_fusion.1.refs_6_.refs_2_), custom_call_target="tpu_custom_call" | custom-call | flops 1 | bytes 1 | tf_op jit(solution)/shard_map/pack/pallas_call | solution.py:144
  50.0 1.6 collective-permute-start.14
  51.7 3.5 %turn.2 = (bf16[16,256,256]{2,1,0:T(8,128)(2,1)S(1)}, bf16[16,256,256]{2,1,0:T(8,128)(2,1)S(1)}) custom-call(bf16[16,256,256]{2,1,0:T(8,128)(2,1)} %refs_0_.1, bf16[16,256,256]{2,1,0:T(8,128)(2,1)} %copy-done.7), custom_call_target="tpu_custom_call" | custom-call | flops 1 | bytes 1 | tf_op jit(solution)/shard_map/turn/pallas_call | solution.py:167
  55.2 1.3 copy-done
  56.5 1.4 copy-done.4
  59.1 1.3 slice_bitcast_fusion.2
  61.0 5.2 %amplitudes.10 = (bf16[64,256,128]{2,1,0:T(8,128)(2,1)}, f32[64,128]{1,0:T(8,128)S(1)}) custom-call(s32[266]{0:T(512)S(1)} %concatenate.46.refs_0_, f32[64,128]{1,0:T(8,128)S(1)} %dynamic-slice_subtract_fusion.1.refs_1_, f32[16,256,128]{2,1,0:T(8,128)S(1)} %broadcast_in_dim.88.refs_2_, bf16[16,256,256]{2,1,0:T(8,128)(2,1)} %copy-done, ...), custom_call_target="tpu_custom_call" | custom-call | flops 1 | bytes 1 | tf_op jit(solution)/shard_map/amplitudes/pallas_call | solution.py:310
  67.5 2.9 %pack.8.refs_3_.refs_6_ = bf16[2,8,256,128]{3,2,1,0:T(8,128)(2,1)} custom-call(s32[74]{0:T(128)S(1)} %pad_add_fusion.refs_0_, bf16[16,256,128]{2,1,0:T(8,128)(2,1)} %collective-permute-done.5.refs_1_.refs_0_.refs_5_, bf16[16,256,128]{2,1,0:T(8,128)(2,1)} %collective-permute-done.9.refs_2_.refs_1_.refs_6_, f32[64,128]{1,0:T(8,128)S(1)} %get-tuple-element.32.refs_3_.refs_8_), custom_call_target="tpu_custom_call" | custom-call | flops 1 | bytes 1 | tf_op jit(solution)/shard_map/pack/pallas_call | solution.py:144
  70.5 1.6 collective-permute-start.11
  72.1 1.7 pack.9
  73.8 1.3 collective-permute-start.10
  77.9 1.7 collective-permute-start.6
  79.6 1.7 collective-permute-start.16
  82.6 5.2 %amplitudes.11 = (bf16[64,256,128]{2,1,0:T(8,128)(2,1)}, f32[64,128]{1,0:T(8,128)S(1)}) custom-call(s32[266]{0:T(512)S(1)} %concatenate.46.refs_0_, f32[64,128]{1,0:T(8,128)S(1)} %dynamic-slice_subtract_fusion.1.refs_1_, f32[16,256,128]{2,1,0:T(8,128)S(1)} %broadcast_in_dim.88.refs_2_, ...), custom_call_target="tpu_custom_call", output_to_operand_aliasing={{0}: (7, {}), {1}: (8, {})} | custom-call | flops 1 | bytes 1 | tf_op jit(solution)/shard_map/amplitudes/pallas_call | solution.py:310
  87.8 5.2 %amplitudes.12 = (bf16[64,256,128]{2,1,0:T(8,128)(2,1)}, f32[64,128]{1,0:T(8,128)S(1)}) custom-call(s32[266]{0:T(512)S(1)} %concatenate.46.refs_0_, f32[64,128]{1,0:T(8,128)S(1)} %dynamic-slice_subtract_fusion.1.refs_1_, f32[16,256,128]{2,1,0:T(8,128)S(1)} %broadcast_in_dim.88.refs_2_, ...), custom_call_target="tpu_custom_call", output_to_operand_aliasing={{0}: (7, {}), {1}: (8, {})} | custom-call | flops 1 | bytes 1 | tf_op jit(solution)/shard_map/amplitudes/pallas_call | solution.py:310
  93.0 3.5 %turn.3 = (bf16[16,128,256]{2,1,0:T(8,128)(2,1)S(1)}, bf16[16,128,256]{2,1,0:T(8,128)(2,1)S(1)}, bf16[16,128,256]{2,1,0:T(8,128)(2,1)S(1)}, bf16[16,128,256]{2,1,0:T(8,128)(2,1)S(1)}) custom-call(bf16[16,256,128]{2,1,0:T(8,128)(2,1)} %collective-permute-done.5.refs_1_.refs_0_.refs_5_, bf16[16,256,128]{2,1,0:T(8,128)(2,1)} %collective-permute-done.9.refs_2_.refs_1_.refs_6_, ...), custom_call_target="tpu_custom_call" | custom-call | flops 1 | bytes 1 | tf_op jit(solution)/shard_map/turn/pallas_call | solution.py:167
  96.5 2.0 %broadcast_in_dim.90.refs_2_ = f32[16,256,128]{2,1,0:T(8,128)} broadcast(f32[16,256]{1,0:T(8,128)S(1)} %copy-done.10), dimensions={0,1} | broadcast | bytes 2113536 | tf_op jit(solution)/shard_map/broadcast_in_dim | solution.py:435
  100.1 6.3 %amplitudes.14 = (bf16[64,256,128]{2,1,0:T(8,128)(2,1)}, f32[64,128]{1,0:T(8,128)S(1)}) custom-call(s32[266]{0:T(512)S(1)} %concatenate.46.refs_0_, f32[64,128]{1,0:T(8,128)S(1)} %dynamic-slice_subtract_fusion.1.refs_1_, f32[16,256,128]{2,1,0:T(8,128)S(1)} %broadcast_in_dim.88.refs_2_, ...), custom_call_target="tpu_custom_call", output_to_operand_aliasing={{0}: (7, {}), {1}: (8, {})} | custom-call | flops 1 | bytes 1 | tf_op jit(solution)/shard_map/amplitudes/pallas_call | solution.py:310
  106.5 1.9 pack.11.refs_2_
  109.7 1.3 collective-permute-start.15
  111.0 1.3 collective-permute-start.20
  114.3 2.0 %amplitudes.15.refs_3_ = bf16[8,256,128]{2,1,0:T(8,128)(2,1)} custom-call(s32[266]{0:T(512)S(1)} %concatenate.49.refs_0_, f32[64,128]{1,0:T(8,128)S(1)} %dynamic-slice_subtract_fusion.refs_1_, f32[16,256,128]{2,1,0:T(8,128)} %broadcast_in_dim.90.refs_2_, bf16[16,128,256]{2,1,0:T(8,128)(2,1)S(1)} %get-tuple-element.33.refs_3_, ...), custom_call_target="tpu_custom_call" | custom-call | flops 1 | bytes 1 | tf_op jit(solution)/shard_map/amplitudes/pallas_call | solution.py:310
  116.3 1.5 collective-permute-start.22
  117.8 18.9 %collective-permute-done.15.refs_2_ = bf16[1,8,256,128]{3,2,1,0:T(8,128)(2,1)S(1)} collective-permute-done((bf16[1,8,256,128]{3,2,1,0:T(8,128)(2,1)S(1)}, bf16[1,8,256,128]{3,2,1,0:T(8,128)(2,1)S(1)}, u32[]{:S(2)}, u32[]{:S(2)}) %collective-permute-start.15) | collective-permute-done | bytes 524320 | tf_op jit(solution)/shard_map/ppermute | solution.py:378
  136.7 1.5 pack.14.refs_8_
  138.2 1.6 collective-permute-start.17
  139.8 8.2 %collective-permute-done.20.refs_7_ = bf16[8,256,128]{2,1,0:T(8,128)(2,1)S(1)} collective-permute-done((bf16[8,256,128]{2,1,0:T(8,128)(2,1)S(1)}, bf16[8,256,128]{2,1,0:T(8,128)(2,1)S(1)}, u32[]{:S(2)}, u32[]{:S(2)}) %collective-permute-start.20) | collective-permute-done | bytes 524320 | tf_op jit(solution)/shard_map/ppermute | solution.py:378
  149.8 4.4 %amplitudes.16 = (bf16[64,256,128]{2,1,0:T(8,128)(2,1)}, f32[64,128]{1,0:T(8,128)S(1)}) custom-call(s32[266]{0:T(512)S(1)} %concatenate.46.refs_0_, f32[64,128]{1,0:T(8,128)S(1)} %dynamic-slice_subtract_fusion.1.refs_1_, f32[16,256,128]{2,1,0:T(8,128)S(1)} %broadcast_in_dim.88.refs_2_, ...), custom_call_target="tpu_custom_call", output_to_operand_aliasing={{0}: (9, {}), {1}: (10, {})} | custom-call | flops 1 | bytes 1 | tf_op jit(solution)/shard_map/amplitudes/pallas_call | solution.py:310
  154.2 6.4 %amplitudes.17 = (bf16[64,256,128]{2,1,0:T(8,128)(2,1)}, f32[64,128]{1,0:T(8,128)S(1)}) custom-call(s32[266]{0:T(512)S(1)} %concatenate.46.refs_0_, f32[64,128]{1,0:T(8,128)S(1)} %dynamic-slice_subtract_fusion.1.refs_1_, f32[16,256,128]{2,1,0:T(8,128)S(1)} %broadcast_in_dim.88.refs_2_, ...), custom_call_target="tpu_custom_call", output_to_operand_aliasing={{0}: (6, {}), {1}: (7, {})} | custom-call | flops 1 | bytes 1 | tf_op jit(solution)/shard_map/amplitudes/pallas_call | solution.py:310
  160.6 1.7 pack.15.refs_8_
  162.3 1.6 collective-permute-start.21
  163.8 5.7 %collective-permute-done.22.refs_7_ = bf16[8,256,128]{2,1,0:T(8,128)(2,1)} collective-permute-done((bf16[8,256,128]{2,1,0:T(8,128)(2,1)}, bf16[8,256,128]{2,1,0:T(8,128)(2,1)}, u32[]{:S(2)}, u32[]{:S(2)}) %collective-permute-start.22) | collective-permute-done | bytes 524320 | tf_op jit(solution)/shard_map/ppermute | solution.py:378
  169.5 3.6 %amplitudes.18 = (bf16[64,256,128]{2,1,0:T(8,128)(2,1)}, f32[64,128]{1,0:T(8,128)S(1)}) custom-call(s32[266]{0:T(512)S(1)} %concatenate.46.refs_0_, f32[64,128]{1,0:T(8,128)S(1)} %dynamic-slice_subtract_fusion.1.refs_1_, f32[16,256,128]{2,1,0:T(8,128)S(1)} %broadcast_in_dim.88.refs_2_, ...), custom_call_target="tpu_custom_call", output_to_operand_aliasing={{0}: (9, {}), {1}: (10, {})} | custom-call | flops 1 | bytes 1 | tf_op jit(solution)/shard_map/amplitudes/pallas_call | solution.py:310
  174.3 7.0 %amplitudes.19 = (bf16[64,256,128]{2,1,0:T(8,128)(2,1)}, f32[64,128]{1,0:T(8,128)S(1)}) custom-call(s32[266]{0:T(512)S(1)} %concatenate.46.refs_0_, f32[64,128]{1,0:T(8,128)S(1)} %dynamic-slice_subtract_fusion.1.refs_1_, f32[16,256,128]{2,1,0:T(8,128)S(1)} %broadcast_in_dim.88.refs_2_, ...), custom_call_target="tpu_custom_call", output_to_operand_aliasing={{0}: (7, {}), {1}: (8, {})} | custom-call | flops 1 | bytes 1 | tf_op jit(solution)/shard_map/amplitudes/pallas_call | solution.py:310
  181.4 4.0 %density_rows.3 = f32[16,128,256]{2,1,0:T(8,128)S(1)} custom-call(s32[1]{0:T(128)} %bitcast.26.start, bf16[64,256,128]{2,1,0:T(8,128)(2,1)} %get-tuple-element.51.t), custom_call_target="tpu_custom_call" | custom-call | flops 1 | bytes 1 | tf_op jit(solution)/shard_map/density_rows/pallas_call | solution.py:348
  186.2 4.0 %density_rows.2 = f32[16,128,256]{2,1,0:T(8,128)S(1)} custom-call(s32[1]{0:T(128)} %bitcast.6.start, bf16[64,256,128]{2,1,0:T(8,128)(2,1)} %get-tuple-element.51.t), custom_call_target="tpu_custom_call" | custom-call | flops 1 | bytes 1 | tf_op jit(solution)/shard_map/density_rows/pallas_call | solution.py:348
  190.8 3.2 %add.80 = f32[16,128,256]{2,1,0:T(8,128)} add(f32[16,128,256]{2,1,0:T(8,128)S(1)} %density_rows.2, f32[16,128,256]{2,1,0:T(8,128)} %collective-permute-done.24) | non-fusion elementwise | flops 524288 | bytes 6291456 | tf_op jit(solution)/shard_map/add | solution.py:487
  (121 shorter events, 22.5 us)
Async XLA Ops:
  0.6 6.3 %copy-start.18 = (s32[16]{0:T(128)S(1)}, s32[16]{0:T(128)}, u32[]{:S(2)}) copy-start(s32[16]{0:T(128)} %param.13) | copy-start | bytes 196
  0.6 6.4 %copy-start.14 = (f32[16]{0:T(128)S(1)}, f32[16]{0:T(128)}, u32[]{:S(2)}) copy-start(f32[16]{0:T(128)} %param.12) | copy-start | bytes 196
  0.7 6.5 %copy-start.19 = (s32[64,1]{0,1:T(1,128)S(1)}, s32[64,1]{0,1:T(1,128)}, u32[]{:S(2)}) copy-start(s32[64,1]{0,1:T(1,128)} %param.14) | copy-start | bytes 772
  0.7 6.6 %copy-start.15 = (s32[64]{0:T(128)S(1)}, s32[64]{0:T(128)}, u32[]{:S(2)}) copy-start(s32[64]{0:T(128)} %param.15) | copy-start | bytes 772
  0.7 6.8 %copy-start.11 = (f32[16,256]{1,0:T(8,128)S(1)}, f32[16,256]{1,0:T(8,128)}, u32[]{:S(2)}) copy-start(f32[16,256]{1,0:T(8,128)} %param.11) | copy-start | bytes 49156
  0.7 39.0 %collective-permute-start.4 = (bf16[16,256,256]{2,1,0:T(8,128)(2,1)}, bf16[16,256,256]{2,1,0:T(8,128)(2,1)S(1)}, u32[]{:S(2)}, u32[]{:S(2)}) collective-permute-start(bf16[16,256,256]{2,1,0:T(8,128)(2,1)} %refs_0_.1), channel_id=1, source_target_pairs={{0,1},{1,0},{2,3},{3,2},{4,5},{5,4},{6,7},{7,6},{8,9},{9,8},{10,11... | collective-permute-start | bytes 6291464 | tf_op jit(solution)/shard_map/ppermute | solution.py:381
  3.6 36.0 %collective-permute-start.5 = (bf16[16,256,128]{2,1,0:T(8,128)(2,1)}, bf16[16,256,128]{2,1,0:T(8,128)(2,1)}, u32[]{:S(2)}, u32[]{:S(2)}) collective-permute-start(bf16[16,256,128]{2,1,0:T(8,128)(2,1)} %constant_dynamic-slice_fusion.refs_5_.refs_1_), channel_id=1, source_target_pairs={{0,4},{2,6},{4,0},{6,2},{8,12},{10,14},{12,8},{14,10},{1,5},{3,7},... | collective-permute-start | bytes 3145736 | tf_op jit(solution)/shard_map/ppermute | solution.py:378
  6.2 65.8 %collective-permute-start.7 = (bf16[16,256,128]{2,1,0:T(8,128)(2,1)}, bf16[16,256,128]{2,1,0:T(8,128)(2,1)S(1)}, u32[]{:S(2)}, u32[]{:S(2)}) collective-permute-start(bf16[16,256,128]{2,1,0:T(8,128)(2,1)} %constant_dynamic-slice_fusion.refs_5_.refs_1_), channel_id=1, source_target_pairs={{4,8},{6,10},{8,4},{10,6},{5,9},{7,11},{9,5},{11,7},{20,24},{22,26... | collective-permute-start | bytes 3145736 | tf_op jit(solution)/shard_map/ppermute | solution.py:378
  7.3 0.9 copy-start.16
  8.2 4.2 %collective-permute-start = (f32[24,384]{1,0:T(8,128)}, f32[24,384]{1,0:T(8,128)S(1)}, u32[]{:S(2)}, u32[]{:S(2)}) collective-permute-start(f32[24,384]{1,0:T(8,128)} %get-tuple-element.77), channel_id=1, source_target_pairs={{0,2},{2,0},{4,6},{6,4},{8,10},{10,8},{12,14},{14,12},{1,3},{3,1},... | collective-permute-start | bytes 110600 | tf_op jit(solution)/shard_map/ppermute | solution.py:378
  12.4 19.4 %collective-permute-start.1 = (f32[2,24,384]{2,1,0:T(8,128)S(1)}, f32[2,24,384]{2,1,0:T(8,128)S(1)}, u32[]{:S(2)}, u32[]{:S(2)}) collective-permute-start(f32[2,24,384]{2,1,0:T(8,128)S(1)} %pad_maximum_fusion), channel_id=1, source_target_pairs={{0,4},{2,6},{4,0},{6,2},{8,12},{10,14},{12,8},{14,10},{1,5},{3,7},... | collective-permute-start | bytes 221192 | tf_op jit(solution)/shard_map/ppermute | solution.py:378
  16.7 22.8 %collective-permute-start.2 = (f32[2,24,384]{2,1,0:T(8,128)S(1)}, f32[2,24,384]{2,1,0:T(8,128)S(1)}, u32[]{:S(2)}, u32[]{:S(2)}) collective-permute-start(f32[2,24,384]{2,1,0:T(8,128)S(1)} %pad_maximum_fusion), channel_id=1, source_target_pairs={{0,8},{2,10},{4,12},{6,14},{8,0},{10,2},{12,4},{14,6},{1,9},{3,11}... | collective-permute-start | bytes 221192 | tf_op jit(solution)/shard_map/ppermute | solution.py:378
  31.8 7.8 %collective-permute-start.3 = (f32[2,24,384]{2,1,0:T(8,128)S(1)}, f32[2,24,384]{2,1,0:T(8,128)S(1)}, u32[]{:S(2)}, u32[]{:S(2)}) collective-permute-start(f32[2,24,384]{2,1,0:T(8,128)S(1)} %pad_maximum_fusion), channel_id=1, source_target_pairs={{0,12},{2,14},{4,8},{6,10},{8,4},{10,6},{12,0},{14,2},{1,13},{3,15... | collective-permute-start | bytes 221192 | tf_op jit(solution)/shard_map/ppermute | solution.py:378
  39.6 6.1 %copy-start.8 = (f32[8,24,384]{2,1,0:T(8,128)}, f32[8,24,384]{2,1,0:T(8,128)S(1)}, u32[]{:S(2)}) copy-start(f32[8,24,384]{2,1,0:T(8,128)S(1)} %constant_dynamic-update-slice_fusion) | copy-start | bytes 884740
  39.6 38.3 %collective-permute-start.12 = (bf16[16,256,128]{2,1,0:T(8,128)(2,1)}, bf16[16,256,128]{2,1,0:T(8,128)(2,1)}, u32[]{:S(2)}, u32[]{:S(2)}) collective-permute-start(bf16[16,256,128]{2,1,0:T(8,128)(2,1)} %collective-permute-done.5.refs_1_.refs_0_.refs_5_), channel_id=1, source_target_pairs={{0,1},{1,0},{2,3},{3,2},{4,5},{5,4},{6,7},{7,6},{8,9},{9,8},{10,11... | collective-permute-start | bytes 3145736 | tf_op jit(solution)/shard_map/ppermute | solution.py:381
  39.7 10.3 %copy-start.7 = (bf16[16,256,256]{2,1,0:T(8,128)(2,1)}, bf16[16,256,256]{2,1,0:T(8,128)(2,1)S(1)}, u32[]{:S(2)}) copy-start(bf16[16,256,256]{2,1,0:T(8,128)(2,1)S(1)} %collective-permute-done.4.refs_1_) | copy-start | bytes 6291460
  41.7 25.8 %collective-permute-start.9 = (bf16[16,256,128]{2,1,0:T(8,128)(2,1)}, bf16[16,256,128]{2,1,0:T(8,128)(2,1)}, u32[]{:S(2)}, u32[]{:S(2)}) collective-permute-start(bf16[16,256,128]{2,1,0:T(8,128)(2,1)} %constant_dynamic-slice_fusion.1.refs_6_.refs_2_), channel_id=1, source_target_pairs={{0,4},{2,6},{4,0},{6,2},{8,12},{10,14},{12,8},{14,10},{1,5},{3,7},... | collective-permute-start | bytes 3145736 | tf_op jit(solution)/shard_map/ppermute | solution.py:378
  43.4 28.7 %collective-permute-start.8 = (bf16[16,256,128]{2,1,0:T(8,128)(2,1)}, bf16[16,256,128]{2,1,0:T(8,128)(2,1)}, u32[]{:S(2)}, u32[]{:S(2)}) collective-permute-start(bf16[16,256,128]{2,1,0:T(8,128)(2,1)} %constant_dynamic-slice_fusion.1.refs_6_.refs_2_), channel_id=1, source_target_pairs={{4,8},{6,10},{8,4},{10,6},{5,9},{7,11},{9,5},{11,7},{20,24},{22,26... | collective-permute-start | bytes 3145736 | tf_op jit(solution)/shard_map/ppermute | solution.py:378
  50.0 7.8 %copy-start.9 = (f32[8,24,384]{2,1,0:T(8,128)S(1)}, f32[8,24,384]{2,1,0:T(8,128)}, u32[]{:S(2)}) copy-start(f32[8,24,384]{2,1,0:T(8,128)} %copy-done.8) | copy-start | bytes 884740
  50.0 29.6 %collective-permute-start.14 = (bf16[2,8,256,128]{3,2,1,0:T(8,128)(2,1)}, bf16[2,8,256,128]{3,2,1,0:T(8,128)(2,1)}, u32[]{:S(2)}, u32[]{:S(2)}) collective-permute-start(bf16[2,8,256,128]{3,2,1,0:T(8,128)(2,1)} %pack.10), channel_id=1, source_target_pairs={{0,2},{2,0},{4,6},{6,4},{8,10},{10,8},{12,14},{14,12},{1,3},{3,1},... | collective-permute-start | bytes 3145736 | tf_op jit(solution)/shard_map/ppermute | solution.py:378
  55.2 1.3 copy-start
  56.5 1.4 copy-start.4
  61.0 5.2 %copy-start.13 = (s32[64]{0:T(128)S(1)}, s32[64]{0:T(128)}, u32[]{:S(2)}) copy-start(s32[64]{0:T(128)} %get-tuple-element.55) | copy-start | bytes 772
  70.5 29.2 %collective-permute-start.11 = (bf16[2,8,256,128]{3,2,1,0:T(8,128)(2,1)}, bf16[2,8,256,128]{3,2,1,0:T(8,128)(2,1)}, u32[]{:S(2)}, u32[]{:S(2)}) collective-permute-start(bf16[2,8,256,128]{3,2,1,0:T(8,128)(2,1)} %pack.8.refs_3_.refs_6_), channel_id=1, source_target_pairs={{0,2},{2,0},{4,6},{6,4},{8,10},{10,8},{12,14},{14,12},{1,3},{3,1},... | collective-permute-start | bytes 3145736 | tf_op jit(solution)/shard_map/ppermute | solution.py:378
  72.1 3.1 %copy-start.12 = (s32[64]{0:T(128)S(1)}, s32[64]{0:T(128)}, u32[]{:S(2)}) copy-start(s32[64]{0:T(128)} %get-tuple-element.79) | copy-start | bytes 772
  73.8 32.7 %collective-permute-start.10 = (bf16[2,8,256,128]{3,2,1,0:T(8,128)(2,1)}, bf16[2,8,256,128]{3,2,1,0:T(8,128)(2,1)}, u32[]{:S(2)}, u32[]{:S(2)}) collective-permute-start(bf16[2,8,256,128]{3,2,1,0:T(8,128)(2,1)} %pack.9), channel_id=1, source_target_pairs={{4,0},{6,2},{8,12},{10,14},{5,1},{7,3},{9,13},{11,15},{20,16},{22,... | collective-permute-start | bytes 3145736 | tf_op jit(solution)/shard_map/ppermute | solution.py:378
  75.1 17.9 %collective-permute-start.13 = (bf16[16,256,128]{2,1,0:T(8,128)(2,1)}, bf16[16,256,128]{2,1,0:T(8,128)(2,1)}, u32[]{:S(2)}, u32[]{:S(2)}) collective-permute-start(bf16[16,256,128]{2,1,0:T(8,128)(2,1)} %collective-permute-done.9.refs_2_.refs_1_.refs_6_), channel_id=1, source_target_pairs={{0,1},{1,0},{2,3},{3,2},{4,5},{5,4},{6,7},{7,6},{8,9},{9,8},{10,11... | collective-permute-start | bytes 3145736 | tf_op jit(solution)/shard_map/ppermute | solution.py:381
  77.9 31.1 %collective-permute-start.6 = (bf16[16,256,128]{2,1,0:T(8,128)(2,1)}, bf16[16,256,128]{2,1,0:T(8,128)(2,1)}, u32[]{:S(2)}, u32[]{:S(2)}) collective-permute-start(bf16[16,256,128]{2,1,0:T(8,128)(2,1)} %collective-permute-done.5.refs_1_.refs_0_.refs_5_), channel_id=1, source_target_pairs={{4,8},{6,10},{8,4},{10,6},{5,9},{7,11},{9,5},{11,7},{20,24},{22,26... | collective-permute-start | bytes 3145736 | tf_op jit(solution)/shard_map/ppermute | solution.py:378
  79.6 32.7 %collective-permute-start.16 = (bf16[16,256,128]{2,1,0:T(8,128)(2,1)}, bf16[16,256,128]{2,1,0:T(8,128)(2,1)}, u32[]{:S(2)}, u32[]{:S(2)}) collective-permute-start(bf16[16,256,128]{2,1,0:T(8,128)(2,1)} %collective-permute-done.9.refs_2_.refs_1_.refs_6_), channel_id=1, source_target_pairs={{4,8},{6,10},{8,4},{10,6},{5,9},{7,11},{9,5},{11,7},{20,24},{22,26... | collective-permute-start | bytes 3145736 | tf_op jit(solution)/shard_map/ppermute | solution.py:378
  93.0 3.5 %copy-start.10 = (f32[16,256]{1,0:T(8,128)S(1)}, f32[16,256]{1,0:T(8,128)}, u32[]{:S(2)}) copy-start(f32[16,256]{1,0:T(8,128)} %get-tuple-element.66) | copy-start | bytes 49156
  98.5 1.6 copy-start.1
  108.4 45.8 %collective-permute-start.19 = (bf16[2,8,256,128]{3,2,1,0:T(8,128)(2,1)S(1)}, bf16[2,8,256,128]{3,2,1,0:T(8,128)(2,1)}, u32[]{:S(2)}, u32[]{:S(2)}) collective-permute-start(bf16[2,8,256,128]{3,2,1,0:T(8,128)(2,1)S(1)} %pack.11.refs_2_), channel_id=1, source_target_pairs={{0,2},{2,0},{4,6},{6,4},{8,10},{10,8},{12,14},{14,12},{1,3},{3,1},... | collective-permute-start | bytes 3145736 | tf_op jit(solution)/shard_map/ppermute | solution.py:378
  109.7 27.0 %collective-permute-start.15 = (bf16[1,8,256,128]{3,2,1,0:T(8,128)(2,1)S(1)}, bf16[1,8,256,128]{3,2,1,0:T(8,128)(2,1)S(1)}, u32[]{:S(2)}, u32[]{:S(2)}) collective-permute-start(bf16[1,8,256,128]{3,2,1,0:T(8,128)(2,1)S(1)} %pack.12.refs_2_), channel_id=1, source_target_pairs={{4,0},{6,2},{8,12},{10,14},{5,1},{7,3},{9,13},{11,15},{20,16},{22,... | collective-permute-start | bytes 1572872 | tf_op jit(solution)/shard_map/ppermute | solution.py:378
  111.0 36.9 %collective-permute-start.20 = (bf16[8,256,128]{2,1,0:T(8,128)(2,1)S(1)}, bf16[8,256,128]{2,1,0:T(8,128)(2,1)S(1)}, u32[]{:S(2)}, u32[]{:S(2)}) collective-permute-start(bf16[8,256,128]{2,1,0:T(8,128)(2,1)S(1)} %amplitudes.13.refs_6_), channel_id=1, source_target_pairs={{4,0},{6,2},{8,12},{10,14},{5,1},{7,3},{9,13},{11,15},{20,16},{22,... | collective-permute-start | bytes 1572872 | tf_op jit(solution)/shard_map/ppermute | solution.py:378
  113.0 47.6 %collective-permute-start.18 = (bf16[1,8,256,128]{3,2,1,0:T(8,128)(2,1)S(1)}, bf16[1,8,256,128]{3,2,1,0:T(8,128)(2,1)}, u32[]{:S(2)}, u32[]{:S(2)}) collective-permute-start(bf16[1,8,256,128]{3,2,1,0:T(8,128)(2,1)S(1)} %pack.13.refs_9_), channel_id=1, source_target_pairs={{4,0},{6,2},{8,12},{10,14},{5,1},{7,3},{9,13},{11,15},{20,16},{22,... | collective-permute-start | bytes 1572872 | tf_op jit(solution)/shard_map/ppermute | solution.py:378
  116.3 53.2 %collective-permute-start.22 = (bf16[8,256,128]{2,1,0:T(8,128)(2,1)}, bf16[8,256,128]{2,1,0:T(8,128)(2,1)}, u32[]{:S(2)}, u32[]{:S(2)}) collective-permute-start(bf16[8,256,128]{2,1,0:T(8,128)(2,1)} %amplitudes.15.refs_3_), channel_id=1, source_target_pairs={{4,0},{6,2},{8,12},{10,14},{5,1},{7,3},{9,13},{11,15},{20,16},{22,... | collective-permute-start | bytes 1572872 | tf_op jit(solution)/shard_map/ppermute | solution.py:378
  138.2 34.9 %collective-permute-start.17 = (bf16[1,8,256,128]{3,2,1,0:T(8,128)(2,1)}, bf16[1,8,256,128]{3,2,1,0:T(8,128)(2,1)}, u32[]{:S(2)}, u32[]{:S(2)}) collective-permute-start(bf16[1,8,256,128]{3,2,1,0:T(8,128)(2,1)} %pack.14.refs_8_), channel_id=1, source_target_pairs={{0,2},{2,0},{4,6},{6,4},{8,10},{10,8},{12,14},{14,12},{1,3},{3,1},... | collective-permute-start | bytes 1572872 | tf_op jit(solution)/shard_map/ppermute | solution.py:378
  147.9 0.8 copy-start.5
  148.7 1.0 copy-start.6
  149.8 4.4 %copy-start.2 = (bf16[16,256,256]{2,1,0:T(8,128)(2,1)S(1)}, bf16[16,256,256]{2,1,0:T(8,128)(2,1)}, u32[]{:S(2)}) copy-start(bf16[16,256,256]{2,1,0:T(8,128)(2,1)} %copy-done) | copy-start | bytes 6291460
  162.3 12.1 %collective-permute-start.21 = (bf16[1,8,256,128]{3,2,1,0:T(8,128)(2,1)S(1)}, bf16[1,8,256,128]{3,2,1,0:T(8,128)(2,1)S(1)}, u32[]{:S(2)}, u32[]{:S(2)}) collective-permute-start(bf16[1,8,256,128]{3,2,1,0:T(8,128)(2,1)S(1)} %pack.15.refs_8_), channel_id=1, source_target_pairs={{0,2},{2,0},{4,6},{6,4},{8,10},{10,8},{12,14},{14,12},{1,3},{3,1},... | collective-permute-start | bytes 1572872 | tf_op jit(solution)/shard_map/ppermute | solution.py:378
  169.5 4.8 %copy-start.3 = (bf16[16,256,256]{2,1,0:T(8,128)(2,1)S(1)}, bf16[16,256,256]{2,1,0:T(8,128)(2,1)}, u32[]{:S(2)}) copy-start(bf16[16,256,256]{2,1,0:T(8,128)(2,1)} %copy-done) | copy-start | bytes 6291460
  181.4 4.2 %copy-start.17 = (s32[64]{0:T(128)S(1)}, s32[64]{0:T(128)}, u32[]{:S(2)}) copy-start(s32[64]{0:T(128)} %copy-done.16) | copy-start | bytes 772
  185.4 5.4 %collective-permute-start.24 = (f32[16,128,256]{2,1,0:T(8,128)S(1)}, f32[16,128,256]{2,1,0:T(8,128)}, u32[]{:S(2)}, u32[]{:S(2)}) collective-permute-start(f32[16,128,256]{2,1,0:T(8,128)S(1)} %density_rows.3), channel_id=1, source_target_pairs={{0,1},{1,0},{2,3},{3,2},{4,5},{5,4},{6,7},{7,6},{8,9},{9,8},{10,11... | collective-permute-start | bytes 6291464 | tf_op jit(solution)/shard_map/ppermute | solution.py:381
  185.7 4.6 %collective-permute-start.23 = (f32[64]{0:T(128)S(1)}, f32[64]{0:T(128)S(1)}, u32[]{:S(2)}, u32[]{:S(2)}) collective-permute-start(f32[64]{0:T(128)S(1)} %select_reduce_fusion), channel_id=1, source_target_pairs={{0,1},{1,0},{2,3},{3,2},{4,5},{5,4},{6,7},{7,6},{8,9},{9,8},{10,11... | collective-permute-start | bytes 776 | tf_op jit(solution)/shard_map/ppermute | solution.py:381

commit v5 on v4

--- a/solution.py
+++ b/solution.py
@@ -89,22 +89,128 @@
     return mesh.shape["orb"] == 8 and mesh.shape["aux"] == 2
 
 
-HEAD = 10
-
-
-def table_of(fields):
-    return jnp.concatenate([x.astype(i32) for x in fields])
-
-
 TINY = pl.CostEstimate(flops=1, bytes_accessed=1, transcendentals=0)
 PARAMS = pltpu.CompilerParams(vmem_limit_bytes=LIMIT)
+
+
+def lists_kernel(cap, vir, occ, size, owner, slot, small, hit):
+    n, (count, nvd) = hit.shape[0], vir.shape
+
+    def column(row, m):
+        eye = lax.broadcasted_iota(i32, (m, m), 0) == lax.broadcasted_iota(i32, (m, m), 1)
+        return jnp.sum(jnp.where(eye, row, 0.0), axis=1, keepdims=True)
+
+    down = lax.broadcasted_iota(i32, (n, n), 0).astype(f32)
+    along = lax.broadcasted_iota(i32, (n, n), 1).astype(f32)
+    owner_row = owner[...].astype(f32)
+    owner_col = column(owner_row, n)
+    before = (owner_col == owner_row) & (along < down)
+    target = owner_col * cap + jnp.sum(jnp.where(before, 1.0, 0.0), axis=1, keepdims=True)
+    found = target == along
+    hit[...] = jnp.where(found, 1.0, 0.0)
+    small[...] = jnp.zeros_like(small)
+    small[:count, :nvd] = vir[...]
+    lane = lax.broadcasted_iota(i32, (count, 128), 1)
+    occ_col, size_col = column(occ[...], count), column(size[...].astype(f32), count)
+    small[:count, nvd:] = jnp.where(lane == 0, occ_col, jnp.where(lane == 1, size_col, 0.0))
+    small[count : count + 1, :n] = jnp.sum(jnp.where(found, down, 0.0), axis=0, keepdims=True)
+    slot_col = column(slot[...].astype(f32), n)
+    small[count : count + 1, 128 : 128 + n] = jnp.sum(
+        jnp.where(found, slot_col, 0.0), axis=0, keepdims=True
+    )
+
+
+def lists(vir, occ, size, owner, slot, cap):
+    count, nvd = vir.shape
+    n = slot.shape[0]
+    return pl.pallas_call(
+        lambda *refs: lists_kernel(cap, *refs),
+        out_shape=(
+            jax.ShapeDtypeStruct((count + 8, nvd + 128), f32),
+            jax.ShapeDtypeStruct((n, n), f32),
+        ),
+        in_specs=[VMEM] * 5,
+        out_specs=(VMEM, VMEM),
+        compiler_params=PARAMS,
+        cost_estimate=TINY,
+        name="lists",
+    )(vir, occ.reshape(1, -1), size.reshape(1, -1), owner.reshape(1, -1), slot.reshape(1, -1))
+
+
+ORDER, SLOT, SIZE_I, SIZE_J, HEAD = range(5)
+MIDDLE, COLUMN = 8, 9
+
+
+def pick(one, values):
+    return lax.dot_general(
+        one, values, (((0,), (0,)), ((), ())),
+        precision=lax.Precision.HIGHEST, preferred_element_type=f32,
+    )
+
+
+def tables_kernel(cap, per_orb, meta, *refs):
+    smalls, outs = refs[:8], refs[8:]
+    count, nvd = smalls[0].shape[0] - 8, smalls[0].shape[1] - 128
+    n = 8 * cap
+    me, col0 = meta[0], meta[1]
+    z, y = me // 2, me % 2
+    lower = z < 2
+    middle = jnp.where((z == 1) | (z == 2), 1, 0)
+    places = [z, z ^ 1, jnp.where(lower, 2, 1), jnp.where(lower, 3, 0)]
+    head = [(2 * p + y) * cap for p in places] + [(2 * p + 1 - y) * cap for p in places]
+    lane = lax.broadcasted_iota(i32, (1, 128), 1)
+    head_row = jnp.zeros((1, 128), i32)
+    for k, value in enumerate(head + [middle, col0]):
+        head_row = jnp.where(lane == k, value, head_row)
+    orbitals = jnp.concatenate([x[:count, :] for x in smalls], axis=0)
+    columns = jnp.where(col0 == 0, orbitals[:, : nvd // 2], orbitals[:, nvd // 2 : nvd])
+    extra = orbitals[:, nvd:]
+
+    def build(x, tbl, rows=None):
+        order = smalls[x][count : count + 1, :n].astype(i32)
+        slots = smalls[x][count : count + 1, 128 : 128 + n].astype(i32)
+        tbl[...] = jnp.zeros_like(tbl)
+        tbl[HEAD : HEAD + 1, :] = head_row
+        tbl[SLOT : SLOT + 1, :n] = slots
+        if rows is None:
+            return
+        tbl[ORDER : ORDER + 1, :n] = order
+        pair = lax.broadcasted_iota(i32, (1, n), 1)
+        owner = sum(jnp.where(pair >= k * cap, 1, 0) for k in range(1, 8))
+        index = (owner ^ me) * count + slots
+        theirs = jnp.where(lax.broadcasted_iota(i32, (8 * count, n), 0) == index, 1.0, 0.0)
+        first = sum(jnp.where(order >= k * per_orb, 1, 0) for k in range(1, count))
+        mine = jnp.where(lax.broadcasted_iota(i32, (count, n), 0) == first, 1.0, 0.0)
+        own = smalls[x][:count, nvd:]
+        rows[...] = pick(theirs, columns) - (pick(theirs, extra)[:, :1] + pick(mine, own)[:, :1])
+        tbl[SIZE_I : SIZE_I + 1, :n] = pick(own, mine)[1:2, :].astype(i32)
+        tbl[SIZE_J : SIZE_J + 1, :n] = pick(extra, theirs)[1:2, :].astype(i32) - col0
+
+    build(0, outs[0], outs[1])
+    build(2, outs[2], outs[3])
+    build(1, outs[4])
+    build(3, outs[5])
+
+
+def tables_of(meta, smalls, cap, per_orb, half):
+    table = jax.ShapeDtypeStruct((8, 128), i32)
+    rows = jax.ShapeDtypeStruct((8 * cap, half), f32)
+    return pl.pallas_call(
+        lambda *refs: tables_kernel(cap, per_orb, *refs),
+        out_shape=(table, rows, table, rows, table, table),
+        in_specs=[SMEM] + [VMEM] * 8,
+        out_specs=[VMEM] * 6,
+        compiler_params=PARAMS,
+        cost_estimate=TINY,
+        name="tables",
+    )(meta, *smalls)
 
 
 def pack_kernel(call, only_middle, relayed, after, tbl, *refs):
     out, sems = refs[-2:]
     halves, cap = out.shape[:2]
-    base = tbl[call]
-    middle = tbl[8] == 1
+    base = tbl[HEAD, call]
+    middle = tbl[HEAD, MIDDLE] == 1
 
     def run(copies):
         for copy in copies:
@@ -116,7 +222,7 @@
         run(
             [
                 pltpu.make_async_copy(
-                    refs[q].at[tbl[HEAD + base + r]], out.at[q, r], sems.at[q, r]
+                    refs[q].at[tbl[SLOT, base + r]], out.at[q, r], sems.at[q, r]
                 )
                 for q in range(halves)
                 for r in range(cap)
@@ -190,13 +296,12 @@
     if mode == "asked_two":
         js = (js[0].at[0], js[1].at[0])
     cap = sv.shape[0]
-    n = rows.shape[0]
     nvd, half = sv.shape[1], sv.shape[2]
-    base = tbl[call]
-    middle = tbl[8] == 1
+    base = tbl[HEAD, call]
+    middle = tbl[HEAD, MIDDLE] == 1
 
     def place(r):
-        return tbl[HEAD + base + r]
+        return tbl[ORDER, base + r]
 
     def run(copies):
         for copy in copies:
@@ -208,15 +313,15 @@
         copies = []
         for r in range(cap):
             i = lax.div(place(r), per_orb)
-            slot = r if mode.startswith("asked") else tbl[HEAD + n + base + r]
+            slot = r if mode.startswith("asked") else tbl[SLOT, base + r]
             todo = [
                 (vcol.at[i], sv.at[r]),
                 (js[0].at[slot], b0.at[r]),
                 (js[1].at[slot], b1.at[r]),
             ]
             if client:
-                here = pl.ds(pl.multiple_of(tbl[9], half), half)
-                there = pl.ds(pl.multiple_of(half - tbl[9], half), half)
+                here = pl.ds(pl.multiple_of(tbl[HEAD, COLUMN], half), half)
+                there = pl.ds(pl.multiple_of(half - tbl[HEAD, COLUMN], half), half)
                 todo += [
                     (left[0].at[i], s0.at[r, here, :]),
                     (left[1].at[i], s1.at[r, here, :]),
@@ -238,8 +343,8 @@
         live_a = lax.broadcasted_iota(i32, (nvd, half), 0)
         live_b = lax.broadcasted_iota(i32, (nvd, half), 1)
         for r, gap in enumerate(gaps()):
-            size_i = tbl[HEAD + 2 * n + base + r]
-            size_j = tbl[HEAD + 3 * n + base + r]
+            size_i = tbl[SIZE_I, base + r]
+            size_j = tbl[SIZE_J, base + r]
             k = jnp.dot(s0[r], b0[r], preferred_element_type=f32)
             k += jnp.dot(s1[r], b1[r], preferred_element_type=f32)
             k = jnp.where((live_a < size_i) & (live_b < size_j), k, 0.0)
@@ -367,11 +472,7 @@
     peers = 8
     cap = pair_dev // peers
     half = nvd // 2
-    wide = nvd + 128
     me, core = lax.axis_index("orb"), lax.axis_index("aux")
-    z, y = me // 2, me % 2
-    lower = z < 2
-    middle = (z == 1) | (z == 2)
     col0 = core * half
 
     def pp(x, perm):
@@ -380,114 +481,76 @@
     def swap_core(x):
         return lax.ppermute(x, "aux", [(0, 1), (1, 0)])
 
-    def flip(bit):
-        return [(o, o ^ bit) for o in range(peers)]
+    def flip(bits):
+        return [(o, o ^ bits) for o in range(peers)]
 
     cross = [(2, 4), (3, 5), (4, 2), (5, 3)]
     outward = [(2, 0), (3, 1), (4, 6), (5, 7)]
-    y_middle = [(2, 3), (3, 2), (4, 5), (5, 4)]
-    y_end = [(0, 1), (1, 0), (6, 7), (7, 6)]
+
+    small, hit = lists(vir_energy, occ_energy, domain_size, partner_owner, partner_slot, cap)
+    smalls = [small] + [pp(small, flip(bits)) for bits in range(1, peers)]
 
     other = swap_core(blocks)
-    first = lax.dynamic_slice_in_dim(blocks, col0, half, 2)
-    near_first, mid_first = pp(first, flip(2)), pp(first, cross)
-
-    owner = partner_owner[:, 0]
-    target = owner * cap + slot_ranks(owner)
-    pairs = jnp.arange(pair_dev, dtype=i32)
-    hit = target[None, :] == pairs[:, None]
-    order = jnp.sum(jnp.where(hit, pairs[None, :], 0), axis=1)
-    slots = jnp.sum(jnp.where(hit, partner_slot[None, :], 0), axis=1)
-    lists = jnp.concatenate([order, slots]).astype(f32)
-    small = jnp.concatenate(
-        [
-            jnp.concatenate(
-                [
-                    vir_energy,
-                    occ_energy[:, None],
-                    domain_size.astype(f32)[:, None],
-                    jnp.zeros((occ, wide - nvd - 2), f32),
-                ],
-                axis=1,
-            ),
-            jnp.pad(lists[None], ((0, 7), (0, wide - lists.shape[0]))),
-        ]
-    )
-    both = jnp.stack([small, pp(small, flip(1))])
-    every = jnp.concatenate([both] + [pp(both, flip(bit)) for bit in (2, 4, 6)])
-
-    column = jnp.stack([z, z ^ 1, jnp.where(lower, 2, 1), jnp.where(lower, 3, 0)])
-    bases = jnp.concatenate([column * 2 + y, column * 2 + (1 - y)]) * cap
-    head = [bases, middle[None], col0[None]]
-
-    def lists_of(x):
-        found = every[x, occ, : 2 * pair_dev].astype(i32)
-        return found[:pair_dev], found[pair_dev:]
-
-    def tables_of(x):
-        order, slots = lists_of(x)
-        theirs = jnp.take(orbitals, ((pairs // cap) ^ me) * occ + slots, axis=0)
-        mine = jnp.take(every[x, :occ], order // per_orb, axis=0)
-        rows = lax.dynamic_slice_in_dim(theirs, col0, half, 1) - (
-            theirs[:, nvd : nvd + 1] + mine[:, nvd : nvd + 1]
-        )
-        size_i, size_j = mine[:, nvd + 1], theirs[:, nvd + 1].astype(i32) - col0
-        vcol = jnp.broadcast_to(every[x, :occ, :nvd, None], (occ, nvd, half))
-        return table_of(head + [order, slots, size_i, size_j]), rows, vcol
-
-    second = lax.dynamic_slice_in_dim(other, col0, half, 2)
-    every, second = lax.optimization_barrier((every, second))
-    orbitals = every[:, :occ].reshape(peers * occ, wide)
-    tables = tables_of(0)
-    beside_list = table_of(head + [lists_of(1)[1]])
-    relay_list = table_of(head + [lists_of(3)[1]])
-    own = [first, second]
-    near = [near_first, pp(second, flip(2))]
-    mid = [mid_first, pp(second, cross)]
-    far = [pp(x, cross) for x in near]
-    left = turn([blocks, other])
+    own = [lax.dynamic_slice_in_dim(x, col0, half, 2) for x in (blocks, other)]
+    sent, smalls = lax.optimization_barrier((own[0], smalls))
+    near = [pp(x, flip(2)) for x in (sent, own[1])]
+    mid = [pp(x, cross) for x in (sent, own[1])]
+    tbl, rows, client_tbl, client_rows, beside_list, relay_list = tables_of(
+        jnp.stack([me, col0]), smalls, cap, per_orb, half
+    )
+
+    def spread(vir):
+        return jnp.broadcast_to(vir[:, :, None], (occ, nvd, half))
+
+    tables = (tbl, rows, spread(vir_energy))
+    client = (client_tbl, client_rows, spread(smalls[2][:occ, :nvd]))
 
     def own_pairs(k, mode, sources, held=(), after=()):
         return amplitudes(mode, k, per_orb, tables, left, sources, cap, held, after)
 
-    beside = pp(pack(beside_list, 0, own, cap), flip(1))
-    held = own_pairs(0, "slots", own)
-    packed = pack(beside_list, 1, near, cap, after=(held[1],))
+    packed = pack(beside_list, 0, own, cap)
+    beside = pp(packed, flip(1))
+    left = turn([blocks, other])
+    held = own_pairs(0, "slots", own, after=(packed,))
+    first, held = lax.optimization_barrier((near[0], held))
+    far = [pp(first, cross)]
+    across = [swap_core(first)]
+    held = own_pairs(4, "asked", [beside], held)
+    second, held = lax.optimization_barrier((near[1], held))
+    far.append(pp(second, cross))
+    across.append(swap_core(second))
+    near = [first, second]
+    packed = pack(relay_list, 2, mid, cap, only_middle=True, after=(held[1],))
+    relay = pp(packed, outward)
+    packed = pack(beside_list, 1, near, cap, after=(packed,))
     beside_near = pp(packed, flip(1))
-    relay = pp(pack(relay_list, 2, mid, cap, only_middle=True, after=(packed,)), outward)
-    across = [swap_core(x) for x in near]
-    held = own_pairs(4, "asked", [beside], held, (packed,))
-    held = own_pairs(1, "slots", near, held)
     client_left = turn(near + across)
-    client = tables_of(2)
-    gone = amplitudes("client", 2, per_orb, client, client_left, mid, cap, after=(held[1],))
+    gone = amplitudes("client", 2, per_orb, client, client_left, mid, cap, after=(packed,))
     ready_2 = pp(gone, outward)
-    held = own_pairs(5, "asked", [beside_near], held, (gone,))
-    packed = pack(beside_list, 2, mid, cap, relayed=relay, after=(held[1],))
+    held = own_pairs(1, "slots", near, held, (gone,))
+    relays = []
+    packed = pack(relay_list, 3, far[:1], cap, only_middle=True, after=(held[1],))
+    relays.append(pp(packed, outward))
+    packed = pack(beside_list, 2, mid, cap, relayed=relay, after=(packed,))
     third = pp(packed, flip(1))
-    relays = []
-    for x in far:
-        packed = pack(relay_list, 3, [x], cap, only_middle=True, after=(packed,))
-        relays.append(pp(packed, outward))
+    held = own_pairs(5, "asked", [beside_near], held, (packed,))
+    packed = pack(relay_list, 3, far[1:], cap, only_middle=True, after=(held[1],))
+    relays.append(pp(packed, outward))
     gone = amplitudes("client", 3, per_orb, client, client_left, far, cap, after=(packed,))
     ready_3 = pp(gone, outward)
-    fourth = []
-    packed = gone
-    for x, came in zip(far, relays):
-        packed = pack(beside_list, 3, [x], cap, relayed=came, after=(packed,))
-        fourth.append(pp(packed, flip(1)))
-        if len(fourth) == 1:
-            held = own_pairs(2, "served", mid + [ready_2], held, (packed,))
-            held = own_pairs(6, "asked", [third], held)
-            packed = held[1]
+    packed = pack(beside_list, 3, far[:1], cap, relayed=relays[0], after=(gone,))
+    fourth = [pp(packed, flip(1))]
+    held = own_pairs(2, "served", mid + [ready_2], held, (packed,))
+    held = own_pairs(6, "asked", [third], held)
+    packed = pack(beside_list, 3, far[1:], cap, relayed=relays[1], after=(held[1],))
+    fourth.append(pp(packed, flip(1)))
     held = own_pairs(3, "served", far + [ready_3], held, (packed,))
     t_all, e_all = own_pairs(7, "asked_two", fourth, held)
 
     away = swap_core(density_rows(t_all, (1 - core) * half, per_orb, half))
     density = density_rows(t_all, core * half, per_orb, half) + away
 
-    sums = jnp.sum(e_all, axis=1)
-    energy = jnp.sum(jnp.where(hit, sums[:, None], 0.0), axis=0)
+    energy = jnp.sum(hit * jnp.sum(e_all, axis=1)[None, :], axis=1)
     energy = (energy + swap_core(energy)) / nvd
     return (energy, density)
 

time: 196 us -> 186 us (0.949)
  other arithmetic: 10 us -> 4 us
  waiting for transfers between devices: 56 us -> 50.8 us
  starting transfers between devices: 34.6 us -> 31.5 us
    unnamed x43 -> x60, local copies, waits for them, and re-layouts: 5.02 us -> 12.7 us
    ppermute x20 -> x23, waiting for transfers between devices: 56 us -> 50.8 us  [pp(): return lax.ppermute(x, 'orb', perm)]
    ppermute x20 -> x23, starting transfers between devices: 33.3 us -> 30.4 us  [pp(): return lax.ppermute(x, 'orb', perm)]
    gather x4 -> x0, local copies, waits for them, and re-layouts: 2.63 us -> none  [the longest x2 1.32 us: tables_of(): mine = jnp.take(every[x, :occ], order // per_orb, axis=0)]
    broadcast_in_dim x6 -> x2, local copies, waits for them, and re-layouts: 4.11 us -> 2.59 us  [spread(): return jnp.broadcast_to(vir[:, :, None], (occ, nvd, half))]
  transfers between devices with their start and end apart: 25 -> 28, of which waited for: 8 -> 9; matrix products, arithmetic and copies ran while one was open for 9% -> 3% of each run, Pallas kernels for 33% -> 37%
where the time goes in v5:
time: 186 us; the launch traced here: 182 us
  Pallas kernels  77.1 us (41%)
  waiting for transfers between devices  50.8 us (27%)
  starting transfers between devices  31.5 us (17%)
  local copies, waits for them, and re-layouts  17.8 us (10%)
  other arithmetic  4 us (2%)
    ppermute x23, waiting for transfers between devices, pp(): return lax.ppermute(x, 'orb', perm)  50.8 us
    pallas_call x10, Pallas kernels, amplitudes(): pl.pallas_call(lambda *refs: amplitudes_kernel(mode, call, per_orb, not h...  48 us
    ppermute x23, starting transfers between devices, pp(): return lax.ppermute(x, 'orb', perm)  30.4 us
    unnamed x60, local copies, waits for them, and re-layouts  12.7 us
    pallas_call x8, Pallas kernels, pack(): pl.pallas_call(lambda *refs: pack_kernel(call, only_middle, relayed is no...  12.7 us
    pallas_call x2, Pallas kernels, density_rows(): pl.pallas_call(density_kernel, out_shape=jax.ShapeDtypeStruct((occ, half,...  7.99 us
    pallas_call x2, Pallas kernels, turn(): pl.pallas_call(turn_kernel, out_shape=[jax.ShapeDtypeStruct((count, cols,...  6.97 us
  transfers between devices with their start and end apart: 28, of which 9 were waited for; matrix products, arithmetic and copies ran while one was open for 3% of the time, Pallas kernels for 37%

profile of v5, /device:TPU:0, one launch (start us, length us, event | category | flops | bytes accessed | tf_op | source)
XLA Modules:
  0.0 182.4 jit_solution(12295215954148526323)
XLA Ops:
  4.7 2.6 %collective-permute-start = (f32[24,384]{1,0:T(8,128)S(1)}, f32[24,384]{1,0:T(8,128)S(1)}, u32[]{:S(2)}, u32[]{:S(2)}) collective-permute-start(f32[24,384]{1,0:T(8,128)S(1)} %get-tuple-element.49.refs_1_), channel_id=1, source_target_pairs={{0,2},{2,0},{4,6},{6,4},{8,10},{10,8},{12,14},{14,12},{1,3},{3,1},... | collective-permute-start | bytes 110600 | tf_op jit(solution)/shard_map/ppermute | solution.py:479
  7.3 1.6 collective-permute-start.1
  8.9 3.0 %collective-permute-start.3 = (f32[24,384]{1,0:T(8,128)S(1)}, f32[24,384]{1,0:T(8,128)S(1)}, u32[]{:S(2)}, u32[]{:S(2)}) collective-permute-start(f32[24,384]{1,0:T(8,128)S(1)} %get-tuple-element.49.refs_1_), channel_id=1, source_target_pairs={{0,8},{2,10},{4,12},{6,14},{8,0},{10,2},{12,4},{14,6},{1,9},{3,11}... | collective-permute-start | bytes 110600 | tf_op jit(solution)/shard_map/ppermute | solution.py:479
  11.8 1.4 collective-permute-start.4
  13.3 3.5 %collective-permute-start.5 = (f32[24,384]{1,0:T(8,128)S(1)}, f32[24,384]{1,0:T(8,128)S(1)}, u32[]{:S(2)}, u32[]{:S(2)}) collective-permute-start(f32[24,384]{1,0:T(8,128)S(1)} %get-tuple-element.49.refs_1_), channel_id=1, source_target_pairs={{0,12},{2,14},{4,8},{6,10},{8,4},{10,6},{12,0},{14,2},{1,13},{3,15... | collective-permute-start | bytes 110600 | tf_op jit(solution)/shard_map/ppermute | solution.py:479
  17.0 2.3 %constant_dynamic-slice_fusion.1.refs_1_.refs_5_ = bf16[16,256,128]{2,1,0:T(8,128)(2,1)} fusion(bf16[16,256,256]{2,1,0:T(8,128)(2,1)} %refs_0_.3, s32[]{:T(128)S(6)} %select_n.4), kind=kLoop, calls=%fused_computation.4 | loop fusion | bytes 2097156 | tf_op jit(solution)/shard_map/dynamic_slice | solution.py:494
  19.4 4.0 %collective-permute-done.6.refs_8_ = f32[24,384]{1,0:T(8,128)S(1)} collective-permute-done((f32[24,384]{1,0:T(8,128)S(1)}, f32[24,384]{1,0:T(8,128)S(1)}, u32[]{:S(2)}, u32[]{:S(2)}) %collective-permute-start.6) | collective-permute-done | bytes 36896 | tf_op jit(solution)/shard_map/ppermute | solution.py:479
  23.5 1.3 tables.1
  26.1 1.8 %pack.8.refs_7_ = bf16[2,8,256,128]{3,2,1,0:T(8,128)(2,1)S(1)} custom-call(s32[8,128]{1,0:T(8,128)S(1)} %get-tuple-element.61.refs_0_, bf16[16,256,128]{2,1,0:T(8,128)(2,1)} %constant_dynamic-slice_fusion.1.refs_1_.refs_5_, bf16[16,256,128]{2,1,0:T(8,128)(2,1)S(1)} %constant_dynamic-slice_fusion.refs_2_.refs_6_), custom_call_target="tpu_custom_call" | custom-call | flops 1 | bytes 1 | tf_op jit(solution)/shard_map/pack/pallas_call | solution.py:250
  28.5 2.0 %collective-permute-start.10 = (bf16[16,256,128]{2,1,0:T(8,128)(2,1)S(1)}, bf16[16,256,128]{2,1,0:T(8,128)(2,1)S(1)}, u32[]{:S(2)}, u32[]{:S(2)}) collective-permute-start(bf16[16,256,128]{2,1,0:T(8,128)(2,1)S(1)} %constant_dynamic-slice_fusion.refs_2_.refs_6_), channel_id=1, source_target_pairs={{0,4},{2,6},{4,0},{6,2},{8,12},{10,14},{12,8},{14,10},{1,5},{3,7},... | collective-permute-start | bytes 3145736 | tf_op jit(solution)/shard_map/ppermute | solution.py:479
  32.0 3.5 %turn.2 = (bf16[16,256,256]{2,1,0:T(8,128)(2,1)S(1)}, bf16[16,256,256]{2,1,0:T(8,128)(2,1)S(1)}) custom-call(bf16[16,256,256]{2,1,0:T(8,128)(2,1)} %refs_0_.3, bf16[16,256,256]{2,1,0:T(8,128)(2,1)} %copy-done.28), custom_call_target="tpu_custom_call" | custom-call | flops 1 | bytes 1 | tf_op jit(solution)/shard_map/turn/pallas_call | solution.py:273
  35.5 1.3 copy-done
  36.8 1.4 copy-done.4
  38.8 5.9 %amplitudes.10 = (bf16[64,256,128]{2,1,0:T(8,128)(2,1)}, f32[64,128]{1,0:T(8,128)S(1)}) custom-call(s32[8,128]{1,0:T(8,128)S(1)} %get-tuple-element.57.refs_0_, f32[64,128]{1,0:T(8,128)S(1)} %get-tuple-element.58.refs_1_, f32[16,256,128]{2,1,0:T(8,128)S(1)} %broadcast_in_dim.4.refs_2_, bf16[16,256,256]{2,1,0:T(8,128)(2,1)} %copy-done, ...), custom_call_target="tpu_custom_call" | custom-call | flops 1 | bytes 1 | tf_op jit(solution)/shard_map/amplitudes/pallas_call | solution.py:415
  44.7 5.1 %collective-permute-done.8.refs_0_.refs_1_.refs_5_ = bf16[16,256,128]{2,1,0:T(8,128)(2,1)} collective-permute-done((bf16[16,256,128]{2,1,0:T(8,128)(2,1)}, bf16[16,256,128]{2,1,0:T(8,128)(2,1)}, u32[]{:S(2)}, u32[]{:S(2)}) %collective-permute-start.8) | collective-permute-done | bytes 1048608 | tf_op jit(solution)/shard_map/ppermute | solution.py:479
  50.7 7.7 %amplitudes.11 = (bf16[64,256,128]{2,1,0:T(8,128)(2,1)}, f32[64,128]{1,0:T(8,128)S(1)}) custom-call(s32[8,128]{1,0:T(8,128)S(1)} %get-tuple-element.57.refs_0_, f32[64,128]{1,0:T(8,128)S(1)} %get-tuple-element.58.refs_1_, f32[16,256,128]{2,1,0:T(8,128)S(1)} %broadcast_in_dim.4.refs_2_, ...), custom_call_target="tpu_custom_call", output_to_operand_aliasing={{0}: (6, {}), {1}: (7, {})} | custom-call | flops 1 | bytes 1 | tf_op jit(solution)/shard_map/amplitudes/pallas_call | solution.py:415
  58.4 10.4 %collective-permute-done.10.refs_1_.refs_2_.refs_6_ = bf16[16,256,128]{2,1,0:T(8,128)(2,1)S(1)} collective-permute-done((bf16[16,256,128]{2,1,0:T(8,128)(2,1)S(1)}, bf16[16,256,128]{2,1,0:T(8,128)(2,1)S(1)}, u32[]{:S(2)}, u32[]{:S(2)}) %collective-permute-start.10) | collective-permute-done | bytes 1048608 | tf_op jit(solution)/shard_map/ppermute | solution.py:479
  69.6 1.8 pack.9.refs_3_
  71.4 1.3 collective-permute-start.19
  72.7 2.8 %pack.10.refs_9_ = bf16[2,8,256,128]{3,2,1,0:T(8,128)(2,1)} custom-call(s32[8,128]{1,0:T(8,128)S(1)} %get-tuple-element.61.refs_0_, bf16[16,256,128]{2,1,0:T(8,128)(2,1)} %collective-permute-done.8.refs_0_.refs_1_.refs_5_, bf16[16,256,128]{2,1,0:T(8,128)(2,1)S(1)} %collective-permute-done.10.refs_1_.refs_2_.refs_6_, bf16[2,8,256,128]{3,2,1,0:T(8,128)(2,1)} %pack.9.refs_3_), custom_call_target="tpu_custom_call" | custom-call | flops 1 | bytes 1 | tf_op jit(solution)/shard_map/pack/pallas_call | solution.py:250
  77.0 3.5 %turn.3 = (bf16[16,128,256]{2,1,0:T(8,128)(2,1)S(1)}, bf16[16,128,256]{2,1,0:T(8,128)(2,1)S(1)}, bf16[16,128,256]{2,1,0:T(8,128)(2,1)S(1)}, bf16[16,128,256]{2,1,0:T(8,128)(2,1)S(1)}) custom-call(bf16[16,256,128]{2,1,0:T(8,128)(2,1)} %collective-permute-done.8.refs_0_.refs_1_.refs_5_, bf16[16,256,128]{2,1,0:T(8,128)(2,1)} %copy-done.12, ...), custom_call_target="tpu_custom_call" | custom-call | flops 1 | bytes 1 | tf_op jit(solution)/shard_map/turn/pallas_call | solution.py:273
  80.5 2.0 %broadcast_in_dim.5.refs_2_ = f32[16,256,128]{2,1,0:T(8,128)} broadcast(f32[16,256]{1,0:T(8,128)S(1)} %slice.3), dimensions={0,1} | broadcast | bytes 2113536 | tf_op jit(solution)/shard_map/broadcast_in_dim | solution.py:503
  83.8 5.9 %amplitudes.13 = (bf16[64,256,128]{2,1,0:T(8,128)(2,1)}, f32[64,128]{1,0:T(8,128)S(1)}) custom-call(s32[8,128]{1,0:T(8,128)S(1)} %get-tuple-element.57.refs_0_, f32[64,128]{1,0:T(8,128)S(1)} %get-tuple-element.58.refs_1_, f32[16,256,128]{2,1,0:T(8,128)S(1)} %broadcast_in_dim.4.refs_2_, ...), custom_call_target="tpu_custom_call", output_to_operand_aliasing={{0}: (8, {}), {1}: (9, {})} | custom-call | flops 1 | bytes 1 | tf_op jit(solution)/shard_map/amplitudes/pallas_call | solution.py:415
  90.3 11.1 %collective-permute-done.19.refs_3_ = bf16[2,8,256,128]{3,2,1,0:T(8,128)(2,1)S(1)} collective-permute-done((bf16[2,8,256,128]{3,2,1,0:T(8,128)(2,1)}, bf16[2,8,256,128]{3,2,1,0:T(8,128)(2,1)S(1)}, u32[]{:S(2)}, u32[]{:S(2)}) %collective-permute-start.19) | collective-permute-done | bytes 1048608 | tf_op jit(solution)/shard_map/ppermute | solution.py:479
  102.4 1.2 copy-done.19
  103.6 1.9 %pack.12.refs_6_ = bf16[2,8,256,128]{3,2,1,0:T(8,128)(2,1)} custom-call(s32[8,128]{1,0:T(8,128)S(1)} %get-tuple-element.61.refs_0_, bf16[16,256,128]{2,1,0:T(8,128)(2,1)S(1)} %collective-permute-done.14.refs_1_.refs_7_.refs_5_, bf16[16,256,128]{2,1,0:T(8,128)(2,1)S(1)} %copy-done.11, bf16[2,8,256,128]{3,2,1,0:T(8,128)(2,1)S(1)} %copy-done.19, ...), custom_call_target="tpu_custom_call" | custom-call | flops 1 | bytes 1 | tf_op jit(solution)/shard_map/pack/pallas_call | solution.py:250
  105.5 1.6 collective-permute-start.22
  107.1 1.3 collective-permute-start.16
  108.4 1.3 collective-permute-start.23
  109.7 5.2 %amplitudes.14 = (bf16[64,256,128]{2,1,0:T(8,128)(2,1)}, f32[64,128]{1,0:T(8,128)S(1)}) custom-call(s32[8,128]{1,0:T(8,128)S(1)} %get-tuple-element.57.refs_0_, f32[64,128]{1,0:T(8,128)S(1)} %get-tuple-element.58.refs_1_, f32[16,256,128]{2,1,0:T(8,128)S(1)} %broadcast_in_dim.4.refs_2_, ...), custom_call_target="tpu_custom_call", output_to_operand_aliasing={{0}: (7, {}), {1}: (8, {})} | custom-call | flops 1 | bytes 1 | tf_op jit(solution)/shard_map/amplitudes/pallas_call | solution.py:415
  115.7 1.4 collective-permute-start.21
  117.1 2.2 %amplitudes.15.refs_3_ = bf16[8,256,128]{2,1,0:T(8,128)(2,1)} custom-call(s32[8,128]{1,0:T(8,128)S(1)} %get-tuple-element.72.refs_0_, f32[64,128]{1,0:T(8,128)S(1)} %get-tuple-element.73.refs_1_, f32[16,256,128]{2,1,0:T(8,128)} %broadcast_in_dim.5.refs_2_, bf16[16,128,256]{2,1,0:T(8,128)(2,1)S(1)} %get-tuple-element.74.refs_3_, ...), custom_call_target="tpu_custom_call" | custom-call | flops 1 | bytes 1 | tf_op jit(solution)/shard_map/amplitudes/pallas_call | solution.py:415
  119.3 1.3 collective-permute-start.25
  120.6 10.3 %collective-permute-done.16.refs_2_ = bf16[1,8,256,128]{3,2,1,0:T(8,128)(2,1)S(1)} collective-permute-done((bf16[1,8,256,128]{3,2,1,0:T(8,128)(2,1)S(1)}, bf16[1,8,256,128]{3,2,1,0:T(8,128)(2,1)S(1)}, u32[]{:S(2)}, u32[]{:S(2)}) %collective-permute-start.16) | collective-permute-done | bytes 524320 | tf_op jit(solution)/shard_map/ppermute | solution.py:479
  132.7 1.5 pack.14.refs_8_
  134.2 1.9 %collective-permute-start.20 = (bf16[1,8,256,128]{3,2,1,0:T(8,128)(2,1)}, bf16[1,8,256,128]{3,2,1,0:T(8,128)(2,1)}, u32[]{:S(2)}, u32[]{:S(2)}) collective-permute-start(bf16[1,8,256,128]{3,2,1,0:T(8,128)(2,1)} %pack.14.refs_8_), channel_id=1, source_target_pairs={{0,2},{2,0},{4,6},{6,4},{8,10},{10,8},{12,14},{14,12},{1,3},{3,1},... | collective-permute-start | bytes 1572872 | tf_op jit(solution)/shard_map/ppermute | solution.py:479
  136.1 6.1 %collective-permute-done.23.refs_7_ = bf16[8,256,128]{2,1,0:T(8,128)(2,1)} collective-permute-done((bf16[8,256,128]{2,1,0:T(8,128)(2,1)S(1)}, bf16[8,256,128]{2,1,0:T(8,128)(2,1)}, u32[]{:S(2)}, u32[]{:S(2)}) %collective-permute-start.23) | collective-permute-done | bytes 524320 | tf_op jit(solution)/shard_map/ppermute | solution.py:479
  142.2 3.6 %amplitudes.16 = (bf16[64,256,128]{2,1,0:T(8,128)(2,1)}, f32[64,128]{1,0:T(8,128)S(1)}) custom-call(s32[8,128]{1,0:T(8,128)S(1)} %get-tuple-element.57.refs_0_, f32[64,128]{1,0:T(8,128)S(1)} %get-tuple-element.58.refs_1_, f32[16,256,128]{2,1,0:T(8,128)S(1)} %broadcast_in_dim.4.refs_2_, ...), custom_call_target="tpu_custom_call", output_to_operand_aliasing={{0}: (9, {}), {1}: (10, {})} | custom-call | flops 1 | bytes 1 | tf_op jit(solution)/shard_map/amplitudes/pallas_call | solution.py:415
  145.8 6.4 %amplitudes.17 = (bf16[64,256,128]{2,1,0:T(8,128)(2,1)}, f32[64,128]{1,0:T(8,128)S(1)}) custom-call(s32[8,128]{1,0:T(8,128)S(1)} %get-tuple-element.57.refs_0_, f32[64,128]{1,0:T(8,128)S(1)} %get-tuple-element.58.refs_1_, f32[16,256,128]{2,1,0:T(8,128)S(1)} %broadcast_in_dim.4.refs_2_, ...), custom_call_target="tpu_custom_call", output_to_operand_aliasing={{0}: (6, {}), {1}: (7, {})} | custom-call | flops 1 | bytes 1 | tf_op jit(solution)/shard_map/amplitudes/pallas_call | solution.py:415
  152.3 1.5 pack.15.refs_8_
  153.8 1.9 %collective-permute-start.24 = (bf16[1,8,256,128]{3,2,1,0:T(8,128)(2,1)}, bf16[1,8,256,128]{3,2,1,0:T(8,128)(2,1)}, u32[]{:S(2)}, u32[]{:S(2)}) collective-permute-start(bf16[1,8,256,128]{3,2,1,0:T(8,128)(2,1)} %pack.15.refs_8_), channel_id=1, source_target_pairs={{0,2},{2,0},{4,6},{6,4},{8,10},{10,8},{12,14},{14,12},{1,3},{3,1},... | collective-permute-start | bytes 1572872 | tf_op jit(solution)/shard_map/ppermute | solution.py:479
  156.6 1.2 copy-done.9
  157.9 3.6 %amplitudes.18 = (bf16[64,256,128]{2,1,0:T(8,128)(2,1)}, f32[64,128]{1,0:T(8,128)S(1)}) custom-call(s32[8,128]{1,0:T(8,128)S(1)} %get-tuple-element.57.refs_0_, f32[64,128]{1,0:T(8,128)S(1)} %get-tuple-element.58.refs_1_, f32[16,256,128]{2,1,0:T(8,128)S(1)} %broadcast_in_dim.4.refs_2_, ...), custom_call_target="tpu_custom_call", output_to_operand_aliasing={{0}: (9, {}), {1}: (10, {})} | custom-call | flops 1 | bytes 1 | tf_op jit(solution)/shard_map/amplitudes/pallas_call | solution.py:415
  161.5 1.9 %collective-permute-done.24.refs_6_ = bf16[1,8,256,128]{3,2,1,0:T(8,128)(2,1)} collective-permute-done((bf16[1,8,256,128]{3,2,1,0:T(8,128)(2,1)}, bf16[1,8,256,128]{3,2,1,0:T(8,128)(2,1)}, u32[]{:S(2)}, u32[]{:S(2)}) %collective-permute-start.24) | collective-permute-done | bytes 524320 | tf_op jit(solution)/shard_map/ppermute | solution.py:479
  163.4 6.4 %amplitudes.19 = (bf16[64,256,128]{2,1,0:T(8,128)(2,1)}, f32[64,128]{1,0:T(8,128)S(1)}) custom-call(s32[8,128]{1,0:T(8,128)S(1)} %get-tuple-element.57.refs_0_, f32[64,128]{1,0:T(8,128)S(1)} %get-tuple-element.58.refs_1_, f32[16,256,128]{2,1,0:T(8,128)S(1)} %broadcast_in_dim.4.refs_2_, ...), custom_call_target="tpu_custom_call", output_to_operand_aliasing={{0}: (7, {}), {1}: (8, {})} | custom-call | flops 1 | bytes 1 | tf_op jit(solution)/shard_map/amplitudes/pallas_call | solution.py:415
  169.8 4.0 %density_rows.3 = f32[16,128,256]{2,1,0:T(8,128)S(1)} custom-call(s32[1]{0:T(128)} %bitcast.6.start, bf16[64,256,128]{2,1,0:T(8,128)(2,1)} %get-tuple-element.91.t), custom_call_target="tpu_custom_call" | custom-call | flops 1 | bytes 1 | tf_op jit(solution)/shard_map/density_rows/pallas_call | solution.py:453
  174.7 4.0 %density_rows.2 = f32[16,128,256]{2,1,0:T(8,128)S(1)} custom-call(s32[1]{0:T(128)} %bitcast.5.start, bf16[64,256,128]{2,1,0:T(8,128)(2,1)} %get-tuple-element.91.t), custom_call_target="tpu_custom_call" | custom-call | flops 1 | bytes 1 | tf_op jit(solution)/shard_map/density_rows/pallas_call | solution.py:453
  179.2 3.2 %add.12 = f32[16,128,256]{2,1,0:T(8,128)} add(f32[16,128,256]{2,1,0:T(8,128)S(1)} %density_rows.2, f32[16,128,256]{2,1,0:T(8,128)} %collective-permute-done.27) | non-fusion elementwise | flops 524288 | bytes 6291456 | tf_op jit(solution)/shard_map/add | solution.py:551
  (102 shorter events, 19.2 us)
Async XLA Ops:
  0.6 24.1 %collective-permute-start.7 = (bf16[16,256,256]{2,1,0:T(8,128)(2,1)}, bf16[16,256,256]{2,1,0:T(8,128)(2,1)S(1)}, u32[]{:S(2)}, u32[]{:S(2)}) collective-permute-start(bf16[16,256,256]{2,1,0:T(8,128)(2,1)} %refs_0_.3), channel_id=1, source_target_pairs={{0,1},{1,0},{2,3},{3,2},{4,5},{5,4},{6,7},{7,6},{8,9},{9,8},{10,11... | collective-permute-start | bytes 6291464 | tf_op jit(solution)/shard_map/ppermute | solution.py:482
  4.7 7.2 %collective-permute-start = (f32[24,384]{1,0:T(8,128)S(1)}, f32[24,384]{1,0:T(8,128)S(1)}, u32[]{:S(2)}, u32[]{:S(2)}) collective-permute-start(f32[24,384]{1,0:T(8,128)S(1)} %get-tuple-element.49.refs_1_), channel_id=1, source_target_pairs={{0,2},{2,0},{4,6},{6,4},{8,10},{10,8},{12,14},{14,12},{1,3},{3,1},... | collective-permute-start | bytes 110600 | tf_op jit(solution)/shard_map/ppermute | solution.py:479
  7.3 6.0 %collective-permute-start.1 = (f32[24,384]{1,0:T(8,128)S(1)}, f32[24,384]{1,0:T(8,128)S(1)}, u32[]{:S(2)}, u32[]{:S(2)}) collective-permute-start(f32[24,384]{1,0:T(8,128)S(1)} %get-tuple-element.49.refs_1_), channel_id=1, source_target_pairs={{0,4},{2,6},{4,0},{6,2},{8,12},{10,14},{12,8},{14,10},{1,5},{3,7},... | collective-permute-start | bytes 110600 | tf_op jit(solution)/shard_map/ppermute | solution.py:479
  8.8 7.9 %collective-permute-start.2 = (f32[24,384]{1,0:T(8,128)S(1)}, f32[24,384]{1,0:T(8,128)S(1)}, u32[]{:S(2)}, u32[]{:S(2)}) collective-permute-start(f32[24,384]{1,0:T(8,128)S(1)} %get-tuple-element.49.refs_1_), channel_id=1, source_target_pairs={{0,6},{2,4},{4,2},{6,0},{8,14},{10,12},{12,10},{14,8},{1,7},{3,5},... | collective-permute-start | bytes 110600 | tf_op jit(solution)/shard_map/ppermute | solution.py:479
  8.9 10.5 %collective-permute-start.3 = (f32[24,384]{1,0:T(8,128)S(1)}, f32[24,384]{1,0:T(8,128)S(1)}, u32[]{:S(2)}, u32[]{:S(2)}) collective-permute-start(f32[24,384]{1,0:T(8,128)S(1)} %get-tuple-element.49.refs_1_), channel_id=1, source_target_pairs={{0,8},{2,10},{4,12},{6,14},{8,0},{10,2},{12,4},{14,6},{1,9},{3,11}... | collective-permute-start | bytes 110600 | tf_op jit(solution)/shard_map/ppermute | solution.py:479
  11.8 7.5 %collective-permute-start.4 = (f32[24,384]{1,0:T(8,128)S(1)}, f32[24,384]{1,0:T(8,128)S(1)}, u32[]{:S(2)}, u32[]{:S(2)}) collective-permute-start(f32[24,384]{1,0:T(8,128)S(1)} %get-tuple-element.49.refs_1_), channel_id=1, source_target_pairs={{0,10},{2,8},{4,14},{6,12},{8,2},{10,0},{12,6},{14,4},{1,11},{3,9}... | collective-permute-start | bytes 110600 | tf_op jit(solution)/shard_map/ppermute | solution.py:479
  13.3 6.1 %collective-permute-start.5 = (f32[24,384]{1,0:T(8,128)S(1)}, f32[24,384]{1,0:T(8,128)S(1)}, u32[]{:S(2)}, u32[]{:S(2)}) collective-permute-start(f32[24,384]{1,0:T(8,128)S(1)} %get-tuple-element.49.refs_1_), channel_id=1, source_target_pairs={{0,12},{2,14},{4,8},{6,10},{8,4},{10,6},{12,0},{14,2},{1,13},{3,15... | collective-permute-start | bytes 110600 | tf_op jit(solution)/shard_map/ppermute | solution.py:479
  16.7 6.7 %collective-permute-start.6 = (f32[24,384]{1,0:T(8,128)S(1)}, f32[24,384]{1,0:T(8,128)S(1)}, u32[]{:S(2)}, u32[]{:S(2)}) collective-permute-start(f32[24,384]{1,0:T(8,128)S(1)} %get-tuple-element.49.refs_1_), channel_id=1, source_target_pairs={{0,14},{2,12},{4,10},{6,8},{8,6},{10,4},{12,2},{14,0},{1,15},{3,13... | collective-permute-start | bytes 110600 | tf_op jit(solution)/shard_map/ppermute | solution.py:479
  23.4 26.4 %collective-permute-start.8 = (bf16[16,256,128]{2,1,0:T(8,128)(2,1)}, bf16[16,256,128]{2,1,0:T(8,128)(2,1)}, u32[]{:S(2)}, u32[]{:S(2)}) collective-permute-start(bf16[16,256,128]{2,1,0:T(8,128)(2,1)} %constant_dynamic-slice_fusion.1.refs_1_.refs_5_), channel_id=1, source_target_pairs={{0,4},{2,6},{4,0},{6,2},{8,12},{10,14},{12,8},{14,10},{1,5},{3,7},... | collective-permute-start | bytes 3145736 | tf_op jit(solution)/shard_map/ppermute | solution.py:479
  24.8 1.3 copy-start.28
  27.9 10.2 %copy-start.23 = (f32[16,256]{1,0:T(8,128)S(1)}, f32[16,256]{1,0:T(8,128)}, u32[]{:S(2)}) copy-start(f32[16,256]{1,0:T(8,128)} %refs_0_.2) | copy-start | bytes 49156
  27.9 22.8 %collective-permute-start.11 = (bf16[2,8,256,128]{3,2,1,0:T(8,128)(2,1)S(1)}, bf16[2,8,256,128]{3,2,1,0:T(8,128)(2,1)S(1)}, u32[]{:S(2)}, u32[]{:S(2)}) collective-permute-start(bf16[2,8,256,128]{3,2,1,0:T(8,128)(2,1)S(1)} %pack.8.refs_7_), channel_id=1, source_target_pairs={{0,2},{2,0},{4,6},{6,4},{8,10},{10,8},{12,14},{14,12},{1,3},{3,1},... | collective-permute-start | bytes 3145736 | tf_op jit(solution)/shard_map/ppermute | solution.py:479
  28.5 40.3 %collective-permute-start.10 = (bf16[16,256,128]{2,1,0:T(8,128)(2,1)S(1)}, bf16[16,256,128]{2,1,0:T(8,128)(2,1)S(1)}, u32[]{:S(2)}, u32[]{:S(2)}) collective-permute-start(bf16[16,256,128]{2,1,0:T(8,128)(2,1)S(1)} %constant_dynamic-slice_fusion.refs_2_.refs_6_), channel_id=1, source_target_pairs={{0,4},{2,6},{4,0},{6,2},{8,12},{10,14},{12,8},{14,10},{1,5},{3,7},... | collective-permute-start | bytes 3145736 | tf_op jit(solution)/shard_map/ppermute | solution.py:479
  30.5 39.0 %collective-permute-start.14 = (bf16[16,256,128]{2,1,0:T(8,128)(2,1)}, bf16[16,256,128]{2,1,0:T(8,128)(2,1)S(1)}, u32[]{:S(2)}, u32[]{:S(2)}) collective-permute-start(bf16[16,256,128]{2,1,0:T(8,128)(2,1)} %constant_dynamic-slice_fusion.1.refs_1_.refs_5_), channel_id=1, source_target_pairs={{4,8},{6,10},{8,4},{10,6},{5,9},{7,11},{9,5},{11,7},{20,24},{22,26... | collective-permute-start | bytes 3145736 | tf_op jit(solution)/shard_map/ppermute | solution.py:479
  31.2 38.3 %collective-permute-start.15 = (bf16[16,256,128]{2,1,0:T(8,128)(2,1)S(1)}, bf16[16,256,128]{2,1,0:T(8,128)(2,1)S(1)}, u32[]{:S(2)}, u32[]{:S(2)}) collective-permute-start(bf16[16,256,128]{2,1,0:T(8,128)(2,1)S(1)} %constant_dynamic-slice_fusion.refs_2_.refs_6_), channel_id=1, source_target_pairs={{4,8},{6,10},{8,4},{10,6},{5,9},{7,11},{9,5},{11,7},{20,24},{22,26... | collective-permute-start | bytes 3145736 | tf_op jit(solution)/shard_map/ppermute | solution.py:479
  35.5 1.3 copy-start
  36.8 1.4 copy-start.4
  38.8 12.0 %copy-start.1 = (bf16[16,256,256]{2,1,0:T(8,128)(2,1)S(1)}, bf16[16,256,256]{2,1,0:T(8,128)(2,1)}, u32[]{:S(2)}) copy-start(bf16[16,256,256]{2,1,0:T(8,128)(2,1)} %copy-done) | copy-start | bytes 6291460
  49.8 26.2 %collective-permute-start.12 = (bf16[16,256,128]{2,1,0:T(8,128)(2,1)}, bf16[16,256,128]{2,1,0:T(8,128)(2,1)S(1)}, u32[]{:S(2)}, u32[]{:S(2)}) collective-permute-start(bf16[16,256,128]{2,1,0:T(8,128)(2,1)} %collective-permute-done.8.refs_0_.refs_1_.refs_5_), channel_id=1, source_target_pairs={{0,1},{1,0},{2,3},{3,2},{4,5},{5,4},{6,7},{7,6},{8,9},{9,8},{10,11... | collective-permute-start | bytes 3145736 | tf_op jit(solution)/shard_map/ppermute | solution.py:482
  68.8 7.2 %copy-start.12 = (bf16[16,256,128]{2,1,0:T(8,128)(2,1)}, bf16[16,256,128]{2,1,0:T(8,128)(2,1)S(1)}, u32[]{:S(2)}) copy-start(bf16[16,256,128]{2,1,0:T(8,128)(2,1)S(1)} %collective-permute-done.10.refs_1_.refs_2_.refs_6_) | copy-start | bytes 3145732
  68.8 8.2 %collective-permute-start.13 = (bf16[16,256,128]{2,1,0:T(8,128)(2,1)S(1)}, bf16[16,256,128]{2,1,0:T(8,128)(2,1)}, u32[]{:S(2)}, u32[]{:S(2)}) collective-permute-start(bf16[16,256,128]{2,1,0:T(8,128)(2,1)S(1)} %collective-permute-done.10.refs_1_.refs_2_.refs_6_), channel_id=1, source_target_pairs={{0,1},{1,0},{2,3},{3,2},{4,5},{5,4},{6,7},{7,6},{8,9},{9,8},{10,11... | collective-permute-start | bytes 3145736 | tf_op jit(solution)/shard_map/ppermute | solution.py:482
  68.8 20.8 %collective-permute-start.9 = (bf16[16,256,128]{2,1,0:T(8,128)(2,1)}, bf16[16,256,128]{2,1,0:T(8,128)(2,1)S(1)}, u32[]{:S(2)}, u32[]{:S(2)}) collective-permute-start(bf16[16,256,128]{2,1,0:T(8,128)(2,1)} %collective-permute-done.8.refs_0_.refs_1_.refs_5_), channel_id=1, source_target_pairs={{4,8},{6,10},{8,4},{10,6},{5,9},{7,11},{9,5},{11,7},{20,24},{22,26... | collective-permute-start | bytes 3145736 | tf_op jit(solution)/shard_map/ppermute | solution.py:479
  69.6 5.9 %copy-start.10 = (bf16[16,256,128]{2,1,0:T(8,128)(2,1)}, bf16[16,256,128]{2,1,0:T(8,128)(2,1)S(1)}, u32[]{:S(2)}) copy-start(bf16[16,256,128]{2,1,0:T(8,128)(2,1)S(1)} %collective-permute-done.15.refs_2_.refs_8_.refs_6_) | copy-start | bytes 3145732
  71.4 30.1 %collective-permute-start.19 = (bf16[2,8,256,128]{3,2,1,0:T(8,128)(2,1)}, bf16[2,8,256,128]{3,2,1,0:T(8,128)(2,1)S(1)}, u32[]{:S(2)}, u32[]{:S(2)}) collective-permute-start(bf16[2,8,256,128]{3,2,1,0:T(8,128)(2,1)} %pack.9.refs_3_), channel_id=1, source_target_pairs={{4,0},{6,2},{8,12},{10,14},{5,1},{7,3},{9,13},{11,15},{20,16},{22,... | collective-permute-start | bytes 3145736 | tf_op jit(solution)/shard_map/ppermute | solution.py:479
  75.5 34.2 %collective-permute-start.18 = (bf16[2,8,256,128]{3,2,1,0:T(8,128)(2,1)}, bf16[2,8,256,128]{3,2,1,0:T(8,128)(2,1)}, u32[]{:S(2)}, u32[]{:S(2)}) collective-permute-start(bf16[2,8,256,128]{3,2,1,0:T(8,128)(2,1)} %pack.10.refs_9_), channel_id=1, source_target_pairs={{0,2},{2,0},{4,6},{6,4},{8,10},{10,8},{12,14},{14,12},{1,3},{3,1},... | collective-permute-start | bytes 3145736 | tf_op jit(solution)/shard_map/ppermute | solution.py:479
  76.0 38.9 %collective-permute-start.17 = (bf16[16,256,128]{2,1,0:T(8,128)(2,1)S(1)}, bf16[16,256,128]{2,1,0:T(8,128)(2,1)S(1)}, u32[]{:S(2)}, u32[]{:S(2)}) collective-permute-start(bf16[16,256,128]{2,1,0:T(8,128)(2,1)S(1)} %collective-permute-done.10.refs_1_.refs_2_.refs_6_), channel_id=1, source_target_pairs={{4,8},{6,10},{8,4},{10,6},{5,9},{7,11},{9,5},{11,7},{20,24},{22,26... | collective-permute-start | bytes 3145736 | tf_op jit(solution)/shard_map/ppermute | solution.py:479
  80.5 2.0 %copy-start.16 = (bf16[16,128,256]{2,1,0:T(8,128)(2,1)}, bf16[16,128,256]{2,1,0:T(8,128)(2,1)S(1)}, u32[]{:S(2)}) copy-start(bf16[16,128,256]{2,1,0:T(8,128)(2,1)S(1)} %get-tuple-element.77.refs_6_) | copy-start | bytes 3145732
  80.5 3.2 %copy-start.14 = (bf16[16,128,256]{2,1,0:T(8,128)(2,1)}, bf16[16,128,256]{2,1,0:T(8,128)(2,1)S(1)}, u32[]{:S(2)}) copy-start(bf16[16,128,256]{2,1,0:T(8,128)(2,1)S(1)} %get-tuple-element.76.refs_5_) | copy-start | bytes 3145732
  82.5 1.2 copy-start.13
  89.6 12.8 %copy-start.11 = (bf16[16,256,128]{2,1,0:T(8,128)(2,1)S(1)}, bf16[16,256,128]{2,1,0:T(8,128)(2,1)}, u32[]{:S(2)}) copy-start(bf16[16,256,128]{2,1,0:T(8,128)(2,1)} %copy-done.10) | copy-start | bytes 3145732
  89.6 15.8 %copy-start.5 = (bf16[16,256,128]{2,1,0:T(8,128)(2,1)}, bf16[16,256,128]{2,1,0:T(8,128)(2,1)S(1)}, u32[]{:S(2)}) copy-start(bf16[16,256,128]{2,1,0:T(8,128)(2,1)S(1)} %collective-permute-done.9.refs_1_.refs_7_.refs_5_) | copy-start | bytes 3145732
  102.4 1.2 copy-start.19
  105.5 40.3 %collective-permute-start.22 = (bf16[2,8,256,128]{3,2,1,0:T(8,128)(2,1)}, bf16[2,8,256,128]{3,2,1,0:T(8,128)(2,1)}, u32[]{:S(2)}, u32[]{:S(2)}) collective-permute-start(bf16[2,8,256,128]{3,2,1,0:T(8,128)(2,1)} %pack.12.refs_6_), channel_id=1, source_target_pairs={{0,2},{2,0},{4,6},{6,4},{8,10},{10,8},{12,14},{14,12},{1,3},{3,1},... | collective-permute-start | bytes 3145736 | tf_op jit(solution)/shard_map/ppermute | solution.py:479
  107.1 23.8 %collective-permute-start.16 = (bf16[1,8,256,128]{3,2,1,0:T(8,128)(2,1)S(1)}, bf16[1,8,256,128]{3,2,1,0:T(8,128)(2,1)S(1)}, u32[]{:S(2)}, u32[]{:S(2)}) collective-permute-start(bf16[1,8,256,128]{3,2,1,0:T(8,128)(2,1)S(1)} %pack.11.refs_4_), channel_id=1, source_target_pairs={{4,0},{6,2},{8,12},{10,14},{5,1},{7,3},{9,13},{11,15},{20,16},{22,... | collective-permute-start | bytes 1572872 | tf_op jit(solution)/shard_map/ppermute | solution.py:479
  108.4 33.8 %collective-permute-start.23 = (bf16[8,256,128]{2,1,0:T(8,128)(2,1)S(1)}, bf16[8,256,128]{2,1,0:T(8,128)(2,1)}, u32[]{:S(2)}, u32[]{:S(2)}) collective-permute-start(bf16[8,256,128]{2,1,0:T(8,128)(2,1)S(1)} %amplitudes.12.refs_7_), channel_id=1, source_target_pairs={{4,0},{6,2},{8,12},{10,14},{5,1},{7,3},{9,13},{11,15},{20,16},{22,... | collective-permute-start | bytes 1572872 | tf_op jit(solution)/shard_map/ppermute | solution.py:479
  109.7 7.4 %copy-start.17 = (bf16[16,128,256]{2,1,0:T(8,128)(2,1)S(1)}, bf16[16,128,256]{2,1,0:T(8,128)(2,1)}, u32[]{:S(2)}) copy-start(bf16[16,128,256]{2,1,0:T(8,128)(2,1)} %copy-done.16) | copy-start | bytes 3145732
  114.9 2.2 %copy-start.15 = (bf16[16,128,256]{2,1,0:T(8,128)(2,1)S(1)}, bf16[16,128,256]{2,1,0:T(8,128)(2,1)}, u32[]{:S(2)}) copy-start(bf16[16,128,256]{2,1,0:T(8,128)(2,1)} %copy-done.14) | copy-start | bytes 3145732
  115.0 2.1 %copy-start.7 = (bf16[16,256,128]{2,1,0:T(8,128)(2,1)}, bf16[16,256,128]{2,1,0:T(8,128)(2,1)S(1)}, u32[]{:S(2)}) copy-start(bf16[16,256,128]{2,1,0:T(8,128)(2,1)S(1)} %collective-permute-done.17.refs_1_.refs_8_.refs_6_) | copy-start | bytes 3145732
  115.7 16.0 %copy-start.6 = (bf16[16,256,128]{2,1,0:T(8,128)(2,1)S(1)}, bf16[16,256,128]{2,1,0:T(8,128)(2,1)}, u32[]{:S(2)}) copy-start(bf16[16,256,128]{2,1,0:T(8,128)(2,1)} %copy-done.5) | copy-start | bytes 3145732
  115.7 36.6 %collective-permute-start.21 = (bf16[1,8,256,128]{3,2,1,0:T(8,128)(2,1)S(1)}, bf16[1,8,256,128]{3,2,1,0:T(8,128)(2,1)S(1)}, u32[]{:S(2)}, u32[]{:S(2)}) collective-permute-start(bf16[1,8,256,128]{3,2,1,0:T(8,128)(2,1)S(1)} %pack.13.refs_9_), channel_id=1, source_target_pairs={{4,0},{6,2},{8,12},{10,14},{5,1},{7,3},{9,13},{11,15},{20,16},{22,... | collective-permute-start | bytes 1572872 | tf_op jit(solution)/shard_map/ppermute | solution.py:479
  119.3 37.4 %collective-permute-start.25 = (bf16[8,256,128]{2,1,0:T(8,128)(2,1)}, bf16[8,256,128]{2,1,0:T(8,128)(2,1)}, u32[]{:S(2)}, u32[]{:S(2)}) collective-permute-start(bf16[8,256,128]{2,1,0:T(8,128)(2,1)} %amplitudes.15.refs_3_), channel_id=1, source_target_pairs={{4,0},{6,2},{8,12},{10,14},{5,1},{7,3},{9,13},{11,15},{20,16},{22,... | collective-permute-start | bytes 1572872 | tf_op jit(solution)/shard_map/ppermute | solution.py:479
  134.2 27.3 %collective-permute-start.20 = (bf16[1,8,256,128]{3,2,1,0:T(8,128)(2,1)}, bf16[1,8,256,128]{3,2,1,0:T(8,128)(2,1)}, u32[]{:S(2)}, u32[]{:S(2)}) collective-permute-start(bf16[1,8,256,128]{3,2,1,0:T(8,128)(2,1)} %pack.14.refs_8_), channel_id=1, source_target_pairs={{0,2},{2,0},{4,6},{6,4},{8,10},{10,8},{12,14},{14,12},{1,3},{3,1},... | collective-permute-start | bytes 1572872 | tf_op jit(solution)/shard_map/ppermute | solution.py:479
  142.2 3.6 %copy-start.2 = (bf16[16,256,256]{2,1,0:T(8,128)(2,1)S(1)}, bf16[16,256,256]{2,1,0:T(8,128)(2,1)}, u32[]{:S(2)}) copy-start(bf16[16,256,256]{2,1,0:T(8,128)(2,1)} %copy-done) | copy-start | bytes 6291460
  145.8 6.5 %copy-start.8 = (bf16[16,256,128]{2,1,0:T(8,128)(2,1)S(1)}, bf16[16,256,128]{2,1,0:T(8,128)(2,1)}, u32[]{:S(2)}) copy-start(bf16[16,256,128]{2,1,0:T(8,128)(2,1)} %copy-done.7) | copy-start | bytes 3145732
  153.8 9.6 %collective-permute-start.24 = (bf16[1,8,256,128]{3,2,1,0:T(8,128)(2,1)}, bf16[1,8,256,128]{3,2,1,0:T(8,128)(2,1)}, u32[]{:S(2)}, u32[]{:S(2)}) collective-permute-start(bf16[1,8,256,128]{3,2,1,0:T(8,128)(2,1)} %pack.15.refs_8_), channel_id=1, source_target_pairs={{0,2},{2,0},{4,6},{6,4},{8,10},{10,8},{12,14},{14,12},{1,3},{3,1},... | collective-permute-start | bytes 1572872 | tf_op jit(solution)/shard_map/ppermute | solution.py:479
  157.9 5.5 %copy-start.3 = (bf16[16,256,256]{2,1,0:T(8,128)(2,1)S(1)}, bf16[16,256,256]{2,1,0:T(8,128)(2,1)}, u32[]{:S(2)}) copy-start(bf16[16,256,256]{2,1,0:T(8,128)(2,1)} %copy-done) | copy-start | bytes 6291460
  173.8 5.4 %collective-permute-start.27 = (f32[16,128,256]{2,1,0:T(8,128)S(1)}, f32[16,128,256]{2,1,0:T(8,128)}, u32[]{:S(2)}, u32[]{:S(2)}) collective-permute-start(f32[16,128,256]{2,1,0:T(8,128)S(1)} %density_rows.3), channel_id=1, source_target_pairs={{0,1},{1,0},{2,3},{3,2},{4,5},{5,4},{6,7},{7,6},{8,9},{9,8},{10,11... | collective-permute-start | bytes 6291464 | tf_op jit(solution)/shard_map/ppermute | solution.py:482
  174.1 4.6 %collective-permute-start.26 = (f32[64]{0:T(128)S(1)}, f32[64]{0:T(128)S(1)}, u32[]{:S(2)}, u32[]{:S(2)}) collective-permute-start(f32[64]{0:T(128)S(1)} %multiply_reduce_fusion), channel_id=1, source_target_pairs={{0,1},{1,0},{2,3},{3,2},{4,5},{5,4},{6,7},{7,6},{8,9},{9,8},{10,11... | collective-permute-start | bytes 776 | tf_op jit(solution)/shard_map/ppermute | solution.py:482
  (10 other events, 8.4 us)

commit v6 on v5

--- a/solution.py
+++ b/solution.py
@@ -234,19 +234,21 @@
     else:
         pl.when(middle)(gather)
     if relayed:
-        came = refs[halves]
 
         @pl.when(jnp.logical_not(middle))
         def _():
             run(
-                [pltpu.make_async_copy(came.at[q], out.at[q], sems.at[q, 0]) for q in range(halves)]
+                [
+                    pltpu.make_async_copy(refs[halves + q].at[0], out.at[q], sems.at[q, 0])
+                    for q in range(halves)
+                ]
             )
 
 
 def pack(tbl, call, sources, cap, only_middle=False, relayed=None, after=()):
     halves = len(sources)
     shape = (halves, cap) + sources[0].shape[1:]
-    operands = (*sources, *(() if relayed is None else (relayed,)), *after)
+    operands = (*sources, *(relayed or ()), *after)
     return pl.pallas_call(
         lambda *refs: pack_kernel(call, only_middle, relayed is not None, len(after), *refs),
         out_shape=jax.ShapeDtypeStruct(shape, bf16),
@@ -285,6 +287,7 @@
 def amplitudes_kernel(mode, call, per_orb, first, tbl, rows, vcol, *refs):
     sv, s0, s1, b0, b1, st, se, sem, sem_out = refs[-9:]
     client = mode == "client"
+    elsewhere = None
     if client:
         tout = refs[-10]
         left, js = refs[:4], refs[4:6]
@@ -294,7 +297,7 @@
     if mode == "asked":
         js = (js[0].at[0], js[0].at[1])
     if mode == "asked_two":
-        js = (js[0].at[0], js[1].at[0])
+        js, elsewhere = [[x.at[0] for x in refs[k : k + 2]] for k in (2, 4)]
     cap = sv.shape[0]
     nvd, half = sv.shape[1], sv.shape[2]
     base = tbl[HEAD, call]
@@ -309,7 +312,7 @@
         for copy in copies:
             copy.wait()
 
-    def load():
+    def load(js=js):
         copies = []
         for r in range(cap):
             i = lax.div(place(r), per_orb)
@@ -382,6 +385,10 @@
             make()
 
         pl.when(jnp.logical_not(middle))(take)
+    elif elsewhere is not None:
+        pl.when(middle)(load)
+        pl.when(jnp.logical_not(middle))(lambda: load(elsewhere))
+        make()
     else:
         load()
         make()
@@ -486,6 +493,8 @@
 
     cross = [(2, 4), (3, 5), (4, 2), (5, 3)]
     outward = [(2, 0), (3, 1), (4, 6), (5, 7)]
+    outward_diagonal = [(2, 1), (3, 0), (4, 7), (5, 6)]
+    y_middle = [(2, 3), (3, 2), (4, 5), (5, 4)]
 
     small, hit = lists(vir_energy, occ_energy, domain_size, partner_owner, partner_slot, cap)
     smalls = [small] + [pp(small, flip(bits)) for bits in range(1, peers)]
@@ -515,37 +524,41 @@
     first, held = lax.optimization_barrier((near[0], held))
     far = [pp(first, cross)]
     across = [swap_core(first)]
-    held = own_pairs(4, "asked", [beside], held)
+    packed = pack(relay_list, 2, mid[:1], cap, only_middle=True, after=(held[1],))
+    relays = [pp(packed, outward)]
+    held = own_pairs(4, "asked", [beside], held, (packed,))
     second, held = lax.optimization_barrier((near[1], held))
     far.append(pp(second, cross))
     across.append(swap_core(second))
     near = [first, second]
-    packed = pack(relay_list, 2, mid, cap, only_middle=True, after=(held[1],))
-    relay = pp(packed, outward)
+    packed = pack(relay_list, 2, mid[1:], cap, only_middle=True, after=(held[1],))
+    relays.append(pp(packed, outward))
     packed = pack(beside_list, 1, near, cap, after=(packed,))
     beside_near = pp(packed, flip(1))
     client_left = turn(near + across)
-    gone = amplitudes("client", 2, per_orb, client, client_left, mid, cap, after=(packed,))
+    gone = amplitudes("client", 2, per_orb, client, client_left, mid, cap, after=(packed, relays[0]))
     ready_2 = pp(gone, outward)
-    held = own_pairs(1, "slots", near, held, (gone,))
-    relays = []
-    packed = pack(relay_list, 3, far[:1], cap, only_middle=True, after=(held[1],))
-    relays.append(pp(packed, outward))
-    packed = pack(beside_list, 2, mid, cap, relayed=relay, after=(packed,))
+    held = own_pairs(1, "slots", near, held, (gone, relays[1]))
+    diagonal, fourth = [], []
+
+    def send_far(q, token):
+        packed = pack(relay_list, 3, far[q : q + 1], cap, only_middle=True, after=(token,))
+        diagonal.append(pp(packed, outward_diagonal))
+        packed = pack(beside_list, 3, far[q : q + 1], cap, only_middle=True, after=(packed,))
+        fourth.append(pp(packed, y_middle))
+        return packed
+
+    packed = send_far(0, held[1])
+    held = own_pairs(2, "served", mid + [ready_2], held, (packed, beside_near))
+    packed = pack(beside_list, 2, mid, cap, relayed=relays, after=(held[1],))
     third = pp(packed, flip(1))
-    held = own_pairs(5, "asked", [beside_near], held, (packed,))
-    packed = pack(relay_list, 3, far[1:], cap, only_middle=True, after=(held[1],))
-    relays.append(pp(packed, outward))
-    gone = amplitudes("client", 3, per_orb, client, client_left, far, cap, after=(packed,))
+    held = own_pairs(5, "asked", [beside_near], held, (packed, diagonal[0]))
+    packed = send_far(1, held[1])
+    gone = amplitudes("client", 3, per_orb, client, client_left, far, cap, after=(packed, diagonal[0], fourth[0]))
     ready_3 = pp(gone, outward)
-    packed = pack(beside_list, 3, far[:1], cap, relayed=relays[0], after=(gone,))
-    fourth = [pp(packed, flip(1))]
-    held = own_pairs(2, "served", mid + [ready_2], held, (packed,))
-    held = own_pairs(6, "asked", [third], held)
-    packed = pack(beside_list, 3, far[1:], cap, relayed=relays[1], after=(held[1],))
-    fourth.append(pp(packed, flip(1)))
-    held = own_pairs(3, "served", far + [ready_3], held, (packed,))
-    t_all, e_all = own_pairs(7, "asked_two", fourth, held)
+    held = own_pairs(6, "asked", [third], held, (gone,))
+    held = own_pairs(7, "asked_two", fourth + diagonal, held)
+    t_all, e_all = own_pairs(3, "served", far + [ready_3], held)
 
     away = swap_core(density_rows(t_all, (1 - core) * half, per_orb, half))
     density = density_rows(t_all, core * half, per_orb, half) + away

time: 186 us -> 198 us (1.065)
  the two profiles are of different devices: /device:TPU:0 before, /device:TPU:9 now
where the time goes in v6:
time: 198 us; the launch traced here: 197 us
  Pallas kernels  94.1 us (48%)
  starting transfers between devices  55.3 us (28%)
  waiting for transfers between devices  27.1 us (14%)
  local copies, waits for them, and re-layouts  14.6 us (7%)
  other arithmetic  4.18 us (2%)
    pallas_call x10, Pallas kernels, amplitudes(): pl.pallas_call(lambda *refs: amplitudes_kernel(mode, call, per_orb, not h...  59.2 us
    ppermute x24, starting transfers between devices, pp(): return lax.ppermute(x, 'orb', perm)  41.3 us
    ppermute x24, waiting for transfers between devices, pp(): return lax.ppermute(x, 'orb', perm)  27.1 us
    pallas_call x9, Pallas kernels, pack(): pl.pallas_call(lambda *refs: pack_kernel(call, only_middle, relayed is no...  18.4 us
    ppermute x5, starting transfers between devices, swap_core(): return lax.ppermute(x, 'aux', [(0, 1), (1, 0)])  14 us
    unnamed x70, local copies, waits for them, and re-layouts  10.6 us
    pallas_call x2, Pallas kernels, density_rows(): pl.pallas_call(density_kernel, out_shape=jax.ShapeDtypeStruct((occ, half,...  7.99 us
    pallas_call x2, Pallas kernels, turn(): pl.pallas_call(turn_kernel, out_shape=[jax.ShapeDtypeStruct((count, cols,...  6.97 us
  transfers between devices with their start and end apart: 29, of which 5 were waited for; matrix products, arithmetic and copies ran while one was open for 2% of the time, Pallas kernels for 43%

profile of v6, /device:TPU:9, one launch (start us, length us, event | category | flops | bytes accessed | tf_op | source)
XLA Modules:
  0.0 196.6 jit_solution(10989497318629735065)
XLA Ops:
  7.6 2.3 %collective-permute-start.3 = (f32[24,384]{1,0:T(8,128)S(1)}, f32[24,384]{1,0:T(8,128)S(1)}, u32[]{:S(2)}, u32[]{:S(2)}) collective-permute-start(f32[24,384]{1,0:T(8,128)S(1)} %get-tuple-element.49.refs_1_), channel_id=1, source_target_pairs={{0,8},{2,10},{4,12},{6,14},{8,0},{10,2},{12,4},{14,6},{1,9},{3,11}... | collective-permute-start | bytes 110600 | tf_op jit(solution)/shard_map/ppermute | solution.py:486
  13.9 2.0 %collective-permute-done.4.refs_6_ = f32[24,384]{1,0:T(8,128)S(1)} collective-permute-done((f32[24,384]{1,0:T(8,128)S(1)}, f32[24,384]{1,0:T(8,128)S(1)}, u32[]{:S(2)}, u32[]{:S(2)}) %collective-permute-start.4) | collective-permute-done | bytes 36896 | tf_op jit(solution)/shard_map/ppermute | solution.py:486
  15.9 2.4 %collective-permute-done.6.refs_8_ = f32[24,384]{1,0:T(8,128)S(1)} collective-permute-done((f32[24,384]{1,0:T(8,128)S(1)}, f32[24,384]{1,0:T(8,128)S(1)}, u32[]{:S(2)}, u32[]{:S(2)}) %collective-permute-start.6) | collective-permute-done | bytes 36896 | tf_op jit(solution)/shard_map/ppermute | solution.py:486
  18.3 3.0 %collective-permute-start.8 = (bf16[16,256,128]{2,1,0:T(8,128)(2,1)S(1)}, bf16[16,256,128]{2,1,0:T(8,128)(2,1)}, u32[]{:S(2)}, u32[]{:S(2)}) collective-permute-start(bf16[16,256,128]{2,1,0:T(8,128)(2,1)S(1)} %constant_dynamic-slice_fusion.1.refs_1_.refs_5_), channel_id=1, source_target_pairs={{0,4},{2,6},{4,0},{6,2},{8,12},{10,14},{12,8},{14,10},{1,5},{3,7},... | collective-permute-start | bytes 3145736 | tf_op jit(solution)/shard_map/ppermute | solution.py:486
  21.3 1.9 collective-permute-start.12
  24.7 2.1 %pack.9.refs_7_ = bf16[2,8,256,128]{3,2,1,0:T(8,128)(2,1)S(1)} custom-call(s32[8,128]{1,0:T(8,128)S(1)} %get-tuple-element.62.refs_0_, bf16[16,256,128]{2,1,0:T(8,128)(2,1)S(1)} %constant_dynamic-slice_fusion.1.refs_1_.refs_5_, bf16[16,256,128]{2,1,0:T(8,128)(2,1)S(1)} %constant_dynamic-slice_fusion.refs_2_.refs_6_), custom_call_target="tpu_custom_call" | custom-call | flops 1 | bytes 1 | tf_op jit(solution)/shard_map/pack/pallas_call | solution.py:252
  27.2 3.4 %collective-permute-start.16 = (bf16[16,256,128]{2,1,0:T(8,128)(2,1)S(1)}, bf16[16,256,128]{2,1,0:T(8,128)(2,1)S(1)}, u32[]{:S(2)}, u32[]{:S(2)}) collective-permute-start(bf16[16,256,128]{2,1,0:T(8,128)(2,1)S(1)} %constant_dynamic-slice_fusion.refs_2_.refs_6_), channel_id=1, source_target_pairs={{4,8},{6,10},{8,4},{10,6},{5,9},{7,11},{9,5},{11,7},{20,24},{22,26... | collective-permute-start | bytes 3145736 | tf_op jit(solution)/shard_map/ppermute | solution.py:486
  30.6 3.5 %turn.2 = (bf16[16,256,256]{2,1,0:T(8,128)(2,1)S(1)}, bf16[16,256,256]{2,1,0:T(8,128)(2,1)S(1)}) custom-call(bf16[16,256,256]{2,1,0:T(8,128)(2,1)} %refs_0_.3, bf16[16,256,256]{2,1,0:T(8,128)(2,1)} %copy-done.32), custom_call_target="tpu_custom_call" | custom-call | flops 1 | bytes 1 | tf_op jit(solution)/shard_map/turn/pallas_call | solution.py:275
  34.1 1.4 copy-done.2
  35.4 1.4 copy-done.5
  37.5 6.5 %amplitudes.10 = (bf16[64,256,128]{2,1,0:T(8,128)(2,1)}, f32[64,128]{1,0:T(8,128)S(1)}) custom-call(s32[8,128]{1,0:T(8,128)S(1)} %get-tuple-element.57.refs_0_, f32[64,128]{1,0:T(8,128)S(1)} %get-tuple-element.58.refs_1_, f32[16,256,128]{2,1,0:T(8,128)S(1)} %broadcast_in_dim.4.refs_2_, bf16[16,256,256]{2,1,0:T(8,128)(2,1)} %copy-done.2, ...), custom_call_target="tpu_custom_call" | custom-call | flops 1 | bytes 1 | tf_op jit(solution)/shard_map/amplitudes/pallas_call | solution.py:422
  44.0 5.1 %collective-permute-start.14 = (bf16[16,256,128]{2,1,0:T(8,128)(2,1)}, bf16[16,256,128]{2,1,0:T(8,128)(2,1)S(1)}, u32[]{:S(2)}, u32[]{:S(2)}) collective-permute-start(bf16[16,256,128]{2,1,0:T(8,128)(2,1)} %collective-permute-done.8.refs_0_.refs_1_.refs_5_), channel_id=1, source_target_pairs={{0,1},{1,0},{2,3},{3,2},{4,5},{5,4},{6,7},{7,6},{8,9},{9,8},{10,11... | collective-permute-start | bytes 3145736 | tf_op jit(solution)/shard_map/ppermute | solution.py:489
  49.0 2.2 %pack.10.refs_6_ = bf16[1,8,256,128]{3,2,1,0:T(8,128)(2,1)} custom-call(s32[8,128]{1,0:T(8,128)S(1)} %get-tuple-element.66.refs_0_, bf16[16,256,128]{2,1,0:T(8,128)(2,1)S(1)} %collective-permute-done.12.refs_1_.refs_7_.refs_5_, f32[64,128]{1,0:T(8,128)S(1)} %get-tuple-element.67.refs_2_.refs_8_), custom_call_target="tpu_custom_call" | custom-call | flops 1 | bytes 1 | tf_op jit(solution)/shard_map/pack/pallas_call | solution.py:252
  51.3 6.4 %amplitudes.11 = (bf16[64,256,128]{2,1,0:T(8,128)(2,1)}, f32[64,128]{1,0:T(8,128)S(1)}) custom-call(s32[8,128]{1,0:T(8,128)S(1)} %get-tuple-element.57.refs_0_, f32[64,128]{1,0:T(8,128)S(1)} %get-tuple-element.58.refs_1_, f32[16,256,128]{2,1,0:T(8,128)S(1)} %broadcast_in_dim.4.refs_2_, ...), custom_call_target="tpu_custom_call", output_to_operand_aliasing={{0}: (7, {}), {1}: (8, {})} | custom-call | flops 1 | bytes 1 | tf_op jit(solution)/shard_map/amplitudes/pallas_call | solution.py:422
  57.7 6.3 %collective-permute-done.10.refs_1_.refs_2_.refs_6_ = bf16[16,256,128]{2,1,0:T(8,128)(2,1)S(1)} collective-permute-done((bf16[16,256,128]{2,1,0:T(8,128)(2,1)S(1)}, bf16[16,256,128]{2,1,0:T(8,128)(2,1)S(1)}, u32[]{:S(2)}, u32[]{:S(2)}) %collective-permute-start.10) | collective-permute-done | bytes 1048608 | tf_op jit(solution)/shard_map/ppermute | solution.py:486
  64.0 3.9 %collective-permute-start.15 = (bf16[16,256,128]{2,1,0:T(8,128)(2,1)S(1)}, bf16[16,256,128]{2,1,0:T(8,128)(2,1)S(1)}, u32[]{:S(2)}, u32[]{:S(2)}) collective-permute-start(bf16[16,256,128]{2,1,0:T(8,128)(2,1)S(1)} %collective-permute-done.10.refs_1_.refs_2_.refs_6_), channel_id=1, source_target_pairs={{0,1},{1,0},{2,3},{3,2},{4,5},{5,4},{6,7},{7,6},{8,9},{9,8},{10,11... | collective-permute-start | bytes 3145736 | tf_op jit(solution)/shard_map/ppermute | solution.py:489
  67.9 3.4 %collective-permute-start.18 = (bf16[1,8,256,128]{3,2,1,0:T(8,128)(2,1)}, bf16[1,8,256,128]{3,2,1,0:T(8,128)(2,1)S(1)}, u32[]{:S(2)}, u32[]{:S(2)}) collective-permute-start(bf16[1,8,256,128]{3,2,1,0:T(8,128)(2,1)} %pack.10.refs_6_), channel_id=1, source_target_pairs={{4,0},{6,2},{8,12},{10,14},{5,1},{7,3},{9,13},{11,15},{20,16},{22,... | collective-permute-start | bytes 1572872 | tf_op jit(solution)/shard_map/ppermute | solution.py:486
  71.3 1.9 collective-permute-start.9
  73.2 1.4 pack.11.refs_3_
  74.6 1.8 pack.12.refs_9_
  79.2 3.5 %turn.3 = (bf16[16,128,256]{2,1,0:T(8,128)(2,1)S(1)}, bf16[16,128,256]{2,1,0:T(8,128)(2,1)S(1)}, bf16[16,128,256]{2,1,0:T(8,128)(2,1)S(1)}, bf16[16,128,256]{2,1,0:T(8,128)(2,1)S(1)}) custom-call(bf16[16,256,128]{2,1,0:T(8,128)(2,1)} %collective-permute-done.8.refs_0_.refs_1_.refs_5_, bf16[16,256,128]{2,1,0:T(8,128)(2,1)} %copy-done.14, ...), custom_call_target="tpu_custom_call" | custom-call | flops 1 | bytes 1 | tf_op jit(solution)/shard_map/turn/pallas_call | solution.py:275
  82.9 1.9 broadcast_in_dim.5.refs_2_
  84.8 5.5 %amplitudes.12.refs_7_ = bf16[8,256,128]{2,1,0:T(8,128)(2,1)S(1)} custom-call(s32[8,128]{1,0:T(8,128)S(1)} %get-tuple-element.72.refs_0_, f32[64,128]{1,0:T(8,128)S(1)} %get-tuple-element.73.refs_1_, f32[16,256,128]{2,1,0:T(8,128)} %broadcast_in_dim.5.refs_2_, bf16[16,128,256]{2,1,0:T(8,128)(2,1)S(1)} %get-tuple-element.74.refs_3_, ...), custom_call_target="tpu_custom_call" | custom-call | flops 1 | bytes 1 | tf_op jit(solution)/shard_map/amplitudes/pallas_call | solution.py:422
  90.3 1.3 collective-permute-start.20
  91.7 3.2 %collective-permute-start.13 = (bf16[16,256,128]{2,1,0:T(8,128)(2,1)S(1)}, bf16[16,256,128]{2,1,0:T(8,128)(2,1)S(1)}, u32[]{:S(2)}, u32[]{:S(2)}) collective-permute-start(bf16[16,256,128]{2,1,0:T(8,128)(2,1)S(1)} %copy-done.15), channel_id=1, source_target_pairs={{4,8},{6,10},{8,4},{10,6},{5,9},{7,11},{9,5},{11,7},{20,24},{22,26... | collective-permute-start | bytes 3145736 | tf_op jit(solution)/shard_map/ppermute | solution.py:486
  94.9 5.8 %amplitudes.13 = (bf16[64,256,128]{2,1,0:T(8,128)(2,1)}, f32[64,128]{1,0:T(8,128)S(1)}) custom-call(s32[8,128]{1,0:T(8,128)S(1)} %get-tuple-element.57.refs_0_, f32[64,128]{1,0:T(8,128)S(1)} %get-tuple-element.58.refs_1_, f32[16,256,128]{2,1,0:T(8,128)S(1)} %broadcast_in_dim.4.refs_2_, ...), custom_call_target="tpu_custom_call", output_to_operand_aliasing={{0}: (9, {}), {1}: (10, {})} | custom-call | flops 1 | bytes 1 | tf_op jit(solution)/shard_map/amplitudes/pallas_call | solution.py:422
  100.8 2.2 %pack.13.refs_2_ = bf16[1,8,256,128]{3,2,1,0:T(8,128)(2,1)} custom-call(s32[8,128]{1,0:T(8,128)S(1)} %get-tuple-element.66.refs_0_, bf16[16,256,128]{2,1,0:T(8,128)(2,1)S(1)} %collective-permute-done.9.refs_1_.refs_7_.refs_5_, f32[64,128]{1,0:T(8,128)S(1)} %get-tuple-element.80.refs_2_.refs_11_), custom_call_target="tpu_custom_call" | custom-call | flops 1 | bytes 1 | tf_op jit(solution)/shard_map/pack/pallas_call | solution.py:252
  103.0 2.7 %collective-permute-start.21 = (bf16[1,8,256,128]{3,2,1,0:T(8,128)(2,1)}, bf16[1,8,256,128]{3,2,1,0:T(8,128)(2,1)S(1)}, u32[]{:S(2)}, u32[]{:S(2)}) collective-permute-start(bf16[1,8,256,128]{3,2,1,0:T(8,128)(2,1)} %pack.13.refs_2_), channel_id=1, source_target_pairs={{4,2},{6,0},{8,14},{10,12},{5,3},{7,1},{9,15},{11,13},{20,18},{22,... | collective-permute-start | bytes 1572872 | tf_op jit(solution)/shard_map/ppermute | solution.py:486
  105.7 2.2 %pack.14.refs_8_ = bf16[1,8,256,128]{3,2,1,0:T(8,128)(2,1)} custom-call(s32[8,128]{1,0:T(8,128)S(1)} %get-tuple-element.62.refs_0_, bf16[16,256,128]{2,1,0:T(8,128)(2,1)S(1)} %collective-permute-done.9.refs_1_.refs_7_.refs_5_, bf16[1,8,256,128]{3,2,1,0:T(8,128)(2,1)} %pack.13.refs_2_), custom_call_target="tpu_custom_call" | custom-call | flops 1 | bytes 1 | tf_op jit(solution)/shard_map/pack/pallas_call | solution.py:252
  109.8 5.2 %amplitudes.14 = (bf16[64,256,128]{2,1,0:T(8,128)(2,1)}, f32[64,128]{1,0:T(8,128)S(1)}) custom-call(s32[8,128]{1,0:T(8,128)S(1)} %get-tuple-element.57.refs_0_, f32[64,128]{1,0:T(8,128)S(1)} %get-tuple-element.58.refs_1_, f32[16,256,128]{2,1,0:T(8,128)} %copy-done, bf16[16,256,256]{2,1,0:T(8,128)(2,1)} %copy-done.2, ...), custom_call_target="tpu_custom_call", output_to_operand_aliasing={{0}: (10, {}), {1}: (11, {})} | custom-call | flops 1 | bytes 1 | tf_op jit(solution)/shard_map/amplitudes/pallas_call | solution.py:422
  115.0 2.2 %pack.15.refs_6_ = bf16[2,8,256,128]{3,2,1,0:T(8,128)(2,1)S(1)} custom-call(s32[8,128]{1,0:T(8,128)S(1)} %get-tuple-element.62.refs_0_, bf16[16,256,128]{2,1,0:T(8,128)(2,1)S(1)} %copy-done.11, bf16[16,256,128]{2,1,0:T(8,128)(2,1)S(1)} %copy-done.13, bf16[1,8,256,128]{3,2,1,0:T(8,128)(2,1)S(1)} %collective-permute-done.18.refs_10_.refs_3_, ...), custom_call_target="tpu_custom_call" | custom-call | flops 1 | bytes 1 | tf_op jit(solution)/shard_map/pack/pallas_call | solution.py:252
  118.5 2.3 %collective-permute-start.22 = (bf16[1,8,256,128]{3,2,1,0:T(8,128)(2,1)}, bf16[1,8,256,128]{3,2,1,0:T(8,128)(2,1)S(1)}, u32[]{:S(2)}, u32[]{:S(2)}) collective-permute-start(bf16[1,8,256,128]{3,2,1,0:T(8,128)(2,1)} %pack.14.refs_8_), channel_id=1, source_target_pairs={{4,6},{6,4},{8,10},{10,8},{5,7},{7,5},{9,11},{11,9},{20,22},{22,20... | collective-permute-start | bytes 1572872 | tf_op jit(solution)/shard_map/ppermute | solution.py:486
  120.8 5.2 %amplitudes.15 = (bf16[64,256,128]{2,1,0:T(8,128)(2,1)}, f32[64,128]{1,0:T(8,128)S(1)}) custom-call(s32[8,128]{1,0:T(8,128)S(1)} %get-tuple-element.57.refs_0_, f32[64,128]{1,0:T(8,128)S(1)} %get-tuple-element.58.refs_1_, f32[16,256,128]{2,1,0:T(8,128)S(1)} %copy-done.1, ...), custom_call_target="tpu_custom_call", output_to_operand_aliasing={{0}: (8, {}), {1}: (9, {})} | custom-call | flops 1 | bytes 1 | tf_op jit(solution)/shard_map/amplitudes/pallas_call | solution.py:422
  126.1 2.2 %pack.16.refs_2_ = bf16[1,8,256,128]{3,2,1,0:T(8,128)(2,1)} custom-call(s32[8,128]{1,0:T(8,128)S(1)} %get-tuple-element.66.refs_0_, bf16[16,256,128]{2,1,0:T(8,128)(2,1)S(1)} %collective-permute-done.13.refs_1_.refs_8_.refs_6_, f32[64,128]{1,0:T(8,128)S(1)} %get-tuple-element.84.refs_2_.refs_8_), custom_call_target="tpu_custom_call" | custom-call | flops 1 | bytes 1 | tf_op jit(solution)/shard_map/pack/pallas_call | solution.py:252
  128.3 2.2 %pack.17.refs_9_ = bf16[1,8,256,128]{3,2,1,0:T(8,128)(2,1)} custom-call(s32[8,128]{1,0:T(8,128)S(1)} %get-tuple-element.62.refs_0_, bf16[16,256,128]{2,1,0:T(8,128)(2,1)S(1)} %collective-permute-done.13.refs_1_.refs_8_.refs_6_, bf16[1,8,256,128]{3,2,1,0:T(8,128)(2,1)} %pack.16.refs_2_), custom_call_target="tpu_custom_call" | custom-call | flops 1 | bytes 1 | tf_op jit(solution)/shard_map/pack/pallas_call | solution.py:252
  130.5 3.1 %collective-permute-start.24 = (bf16[1,8,256,128]{3,2,1,0:T(8,128)(2,1)}, bf16[1,8,256,128]{3,2,1,0:T(8,128)(2,1)}, u32[]{:S(2)}, u32[]{:S(2)}) collective-permute-start(bf16[1,8,256,128]{3,2,1,0:T(8,128)(2,1)} %pack.17.refs_9_), channel_id=1, source_target_pairs={{4,6},{6,4},{8,10},{10,8},{5,7},{7,5},{9,11},{11,9},{20,22},{22,20... | collective-permute-start | bytes 1572872 | tf_op jit(solution)/shard_map/ppermute | solution.py:486
  133.6 2.1 %collective-permute-start.25 = (bf16[1,8,256,128]{3,2,1,0:T(8,128)(2,1)}, bf16[1,8,256,128]{3,2,1,0:T(8,128)(2,1)}, u32[]{:S(2)}, u32[]{:S(2)}) collective-permute-start(bf16[1,8,256,128]{3,2,1,0:T(8,128)(2,1)} %pack.16.refs_2_), channel_id=1, source_target_pairs={{4,2},{6,0},{8,14},{10,12},{5,3},{7,1},{9,15},{11,13},{20,18},{22,... | collective-permute-start | bytes 1572872 | tf_op jit(solution)/shard_map/ppermute | solution.py:486
  135.7 16.1 %collective-permute-done.22.refs_11_.refs_5_ = bf16[1,8,256,128]{3,2,1,0:T(8,128)(2,1)S(1)} collective-permute-done((bf16[1,8,256,128]{3,2,1,0:T(8,128)(2,1)}, bf16[1,8,256,128]{3,2,1,0:T(8,128)(2,1)S(1)}, u32[]{:S(2)}, u32[]{:S(2)}) %collective-permute-start.22) | collective-permute-done | bytes 524320 | tf_op jit(solution)/shard_map/ppermute | solution.py:486
  151.8 5.9 %amplitudes.16.refs_6_ = bf16[8,256,128]{2,1,0:T(8,128)(2,1)} custom-call(s32[8,128]{1,0:T(8,128)S(1)} %get-tuple-element.72.refs_0_, f32[64,128]{1,0:T(8,128)S(1)} %get-tuple-element.73.refs_1_, f32[16,256,128]{2,1,0:T(8,128)} %broadcast_in_dim.5.refs_2_, bf16[16,128,256]{2,1,0:T(8,128)(2,1)S(1)} %get-tuple-element.74.refs_3_, ...), custom_call_target="tpu_custom_call" | custom-call | flops 1 | bytes 1 | tf_op jit(solution)/shard_map/amplitudes/pallas_call | solution.py:422
  157.7 2.1 %collective-permute-start.23 = (bf16[8,256,128]{2,1,0:T(8,128)(2,1)}, bf16[8,256,128]{2,1,0:T(8,128)(2,1)}, u32[]{:S(2)}, u32[]{:S(2)}) collective-permute-start(bf16[8,256,128]{2,1,0:T(8,128)(2,1)} %amplitudes.16.refs_6_), channel_id=1, source_target_pairs={{4,0},{6,2},{8,12},{10,14},{5,1},{7,3},{9,13},{11,15},{20,16},{22,... | collective-permute-start | bytes 1572872 | tf_op jit(solution)/shard_map/ppermute | solution.py:486
  159.8 1.6 copy-done.4
  161.4 6.4 %amplitudes.17 = (bf16[64,256,128]{2,1,0:T(8,128)(2,1)}, f32[64,128]{1,0:T(8,128)S(1)}) custom-call(s32[8,128]{1,0:T(8,128)S(1)} %get-tuple-element.57.refs_0_, f32[64,128]{1,0:T(8,128)S(1)} %get-tuple-element.58.refs_1_, f32[16,256,128]{2,1,0:T(8,128)S(1)} %copy-done.1, ...), custom_call_target="tpu_custom_call", output_to_operand_aliasing={{0}: (7, {}), {1}: (8, {})} | custom-call | flops 1 | bytes 1 | tf_op jit(solution)/shard_map/amplitudes/pallas_call | solution.py:422
  167.9 5.8 %amplitudes.18 = (bf16[64,256,128]{2,1,0:T(8,128)(2,1)}, f32[64,128]{1,0:T(8,128)S(1)}) custom-call(s32[8,128]{1,0:T(8,128)S(1)} %get-tuple-element.57.refs_0_, f32[64,128]{1,0:T(8,128)S(1)} %get-tuple-element.58.refs_1_, f32[16,256,128]{2,1,0:T(8,128)S(1)} %copy-done.1, ...), custom_call_target="tpu_custom_call", output_to_operand_aliasing={{0}: (9, {}), {1}: (10, {})} | custom-call | flops 1 | bytes 1 | tf_op jit(solution)/shard_map/amplitudes/pallas_call | solution.py:422
  173.7 6.5 %amplitudes.19 = (bf16[64,256,128]{2,1,0:T(8,128)(2,1)}, f32[64,128]{1,0:T(8,128)S(1)}) custom-call(s32[8,128]{1,0:T(8,128)S(1)} %get-tuple-element.57.refs_0_, f32[64,128]{1,0:T(8,128)S(1)} %get-tuple-element.58.refs_1_, f32[16,256,128]{2,1,0:T(8,128)S(1)} %copy-done.1, ...), custom_call_target="tpu_custom_call", output_to_operand_aliasing={{0}: (8, {}), {1}: (9, {})} | custom-call | flops 1 | bytes 1 | tf_op jit(solution)/shard_map/amplitudes/pallas_call | solution.py:422
  180.2 4.0 %density_rows.3 = f32[16,128,256]{2,1,0:T(8,128)S(1)} custom-call(s32[1]{0:T(128)} %bitcast.6.start, bf16[64,256,128]{2,1,0:T(8,128)(2,1)} %get-tuple-element.91.t), custom_call_target="tpu_custom_call" | custom-call | flops 1 | bytes 1 | tf_op jit(solution)/shard_map/density_rows/pallas_call | solution.py:460
  184.2 4.2 %collective-permute-start.28 = (f32[16,128,256]{2,1,0:T(8,128)S(1)}, f32[16,128,256]{2,1,0:T(8,128)}, u32[]{:S(2)}, u32[]{:S(2)}) collective-permute-start(f32[16,128,256]{2,1,0:T(8,128)S(1)} %density_rows.3), channel_id=1, source_target_pairs={{0,1},{1,0},{2,3},{3,2},{4,5},{5,4},{6,7},{7,6},{8,9},{9,8},{10,11... | collective-permute-start | bytes 6291464 | tf_op jit(solution)/shard_map/ppermute | solution.py:489
  188.7 4.0 %density_rows.2 = f32[16,128,256]{2,1,0:T(8,128)S(1)} custom-call(s32[1]{0:T(128)} %bitcast.5.start, bf16[64,256,128]{2,1,0:T(8,128)(2,1)} %get-tuple-element.91.t), custom_call_target="tpu_custom_call" | custom-call | flops 1 | bytes 1 | tf_op jit(solution)/shard_map/density_rows/pallas_call | solution.py:460
  193.3 3.4 %add.12 = f32[16,128,256]{2,1,0:T(8,128)} add(f32[16,128,256]{2,1,0:T(8,128)S(1)} %density_rows.2, f32[16,128,256]{2,1,0:T(8,128)} %collective-permute-done.28) | non-fusion elementwise | flops 524288 | bytes 6291456 | tf_op jit(solution)/shard_map/add | solution.py:564
  (115 shorter events, 20.2 us)
Async XLA Ops:
  0.6 23.9 %collective-permute-start.7 = (bf16[16,256,256]{2,1,0:T(8,128)(2,1)}, bf16[16,256,256]{2,1,0:T(8,128)(2,1)S(1)}, u32[]{:S(2)}, u32[]{:S(2)}) collective-permute-start(bf16[16,256,256]{2,1,0:T(8,128)(2,1)} %refs_0_.3), channel_id=1, source_target_pairs={{0,1},{1,0},{2,3},{3,2},{4,5},{5,4},{6,7},{7,6},{8,9},{9,8},{10,11... | collective-permute-start | bytes 6291464 | tf_op jit(solution)/shard_map/ppermute | solution.py:489
  4.9 6.3 %collective-permute-start = (f32[24,384]{1,0:T(8,128)S(1)}, f32[24,384]{1,0:T(8,128)S(1)}, u32[]{:S(2)}, u32[]{:S(2)}) collective-permute-start(f32[24,384]{1,0:T(8,128)S(1)} %get-tuple-element.49.refs_1_), channel_id=1, source_target_pairs={{0,2},{2,0},{4,6},{6,4},{8,10},{10,8},{12,14},{14,12},{1,3},{3,1},... | collective-permute-start | bytes 110600 | tf_op jit(solution)/shard_map/ppermute | solution.py:486
  6.2 6.1 %collective-permute-start.1 = (f32[24,384]{1,0:T(8,128)S(1)}, f32[24,384]{1,0:T(8,128)S(1)}, u32[]{:S(2)}, u32[]{:S(2)}) collective-permute-start(f32[24,384]{1,0:T(8,128)S(1)} %get-tuple-element.49.refs_1_), channel_id=1, source_target_pairs={{0,4},{2,6},{4,0},{6,2},{8,12},{10,14},{12,8},{14,10},{1,5},{3,7},... | collective-permute-start | bytes 110600 | tf_op jit(solution)/shard_map/ppermute | solution.py:486
  6.4 7.2 %collective-permute-start.2 = (f32[24,384]{1,0:T(8,128)S(1)}, f32[24,384]{1,0:T(8,128)S(1)}, u32[]{:S(2)}, u32[]{:S(2)}) collective-permute-start(f32[24,384]{1,0:T(8,128)S(1)} %get-tuple-element.49.refs_1_), channel_id=1, source_target_pairs={{0,6},{2,4},{4,2},{6,0},{8,14},{10,12},{12,10},{14,8},{1,7},{3,5},... | collective-permute-start | bytes 110600 | tf_op jit(solution)/shard_map/ppermute | solution.py:486
  7.6 6.3 %collective-permute-start.3 = (f32[24,384]{1,0:T(8,128)S(1)}, f32[24,384]{1,0:T(8,128)S(1)}, u32[]{:S(2)}, u32[]{:S(2)}) collective-permute-start(f32[24,384]{1,0:T(8,128)S(1)} %get-tuple-element.49.refs_1_), channel_id=1, source_target_pairs={{0,8},{2,10},{4,12},{6,14},{8,0},{10,2},{12,4},{14,6},{1,9},{3,11}... | collective-permute-start | bytes 110600 | tf_op jit(solution)/shard_map/ppermute | solution.py:486
  11.2 4.7 %collective-permute-start.4 = (f32[24,384]{1,0:T(8,128)S(1)}, f32[24,384]{1,0:T(8,128)S(1)}, u32[]{:S(2)}, u32[]{:S(2)}) collective-permute-start(f32[24,384]{1,0:T(8,128)S(1)} %get-tuple-element.49.refs_1_), channel_id=1, source_target_pairs={{0,10},{2,8},{4,14},{6,12},{8,2},{10,0},{12,6},{14,4},{1,11},{3,9}... | collective-permute-start | bytes 110600 | tf_op jit(solution)/shard_map/ppermute | solution.py:486
  12.3 3.6 %collective-permute-start.5 = (f32[24,384]{1,0:T(8,128)S(1)}, f32[24,384]{1,0:T(8,128)S(1)}, u32[]{:S(2)}, u32[]{:S(2)}) collective-permute-start(f32[24,384]{1,0:T(8,128)S(1)} %get-tuple-element.49.refs_1_), channel_id=1, source_target_pairs={{0,12},{2,14},{4,8},{6,10},{8,4},{10,6},{12,0},{14,2},{1,13},{3,15... | collective-permute-start | bytes 110600 | tf_op jit(solution)/shard_map/ppermute | solution.py:486
  13.6 4.7 %collective-permute-start.6 = (f32[24,384]{1,0:T(8,128)S(1)}, f32[24,384]{1,0:T(8,128)S(1)}, u32[]{:S(2)}, u32[]{:S(2)}) collective-permute-start(f32[24,384]{1,0:T(8,128)S(1)} %get-tuple-element.49.refs_1_), channel_id=1, source_target_pairs={{0,14},{2,12},{4,10},{6,8},{8,6},{10,4},{12,2},{14,0},{1,15},{3,13... | collective-permute-start | bytes 110600 | tf_op jit(solution)/shard_map/ppermute | solution.py:486
  18.3 25.7 %collective-permute-start.8 = (bf16[16,256,128]{2,1,0:T(8,128)(2,1)S(1)}, bf16[16,256,128]{2,1,0:T(8,128)(2,1)}, u32[]{:S(2)}, u32[]{:S(2)}) collective-permute-start(bf16[16,256,128]{2,1,0:T(8,128)(2,1)S(1)} %constant_dynamic-slice_fusion.1.refs_1_.refs_5_), channel_id=1, source_target_pairs={{0,4},{2,6},{4,0},{6,2},{8,12},{10,14},{12,8},{14,10},{1,5},{3,7},... | collective-permute-start | bytes 3145736 | tf_op jit(solution)/shard_map/ppermute | solution.py:486
  21.3 27.7 %collective-permute-start.12 = (bf16[16,256,128]{2,1,0:T(8,128)(2,1)S(1)}, bf16[16,256,128]{2,1,0:T(8,128)(2,1)S(1)}, u32[]{:S(2)}, u32[]{:S(2)}) collective-permute-start(bf16[16,256,128]{2,1,0:T(8,128)(2,1)S(1)} %constant_dynamic-slice_fusion.1.refs_1_.refs_5_), channel_id=1, source_target_pairs={{4,8},{6,10},{8,4},{10,6},{5,9},{7,11},{9,5},{11,7},{20,24},{22,26... | collective-permute-start | bytes 3145736 | tf_op jit(solution)/shard_map/ppermute | solution.py:486
  26.9 9.9 %copy-start.27 = (f32[16,256]{1,0:T(8,128)S(1)}, f32[16,256]{1,0:T(8,128)}, u32[]{:S(2)}) copy-start(f32[16,256]{1,0:T(8,128)} %refs_0_.2) | copy-start | bytes 49156
  26.9 24.3 %collective-permute-start.11 = (bf16[2,8,256,128]{3,2,1,0:T(8,128)(2,1)S(1)}, bf16[2,8,256,128]{3,2,1,0:T(8,128)(2,1)}, u32[]{:S(2)}, u32[]{:S(2)}) collective-permute-start(bf16[2,8,256,128]{3,2,1,0:T(8,128)(2,1)S(1)} %pack.9.refs_7_), channel_id=1, source_target_pairs={{0,2},{2,0},{4,6},{6,4},{8,10},{10,8},{12,14},{14,12},{1,3},{3,1},... | collective-permute-start | bytes 3145736 | tf_op jit(solution)/shard_map/ppermute | solution.py:486
  27.2 36.8 %collective-permute-start.10 = (bf16[16,256,128]{2,1,0:T(8,128)(2,1)S(1)}, bf16[16,256,128]{2,1,0:T(8,128)(2,1)S(1)}, u32[]{:S(2)}, u32[]{:S(2)}) collective-permute-start(bf16[16,256,128]{2,1,0:T(8,128)(2,1)S(1)} %constant_dynamic-slice_fusion.refs_2_.refs_6_), channel_id=1, source_target_pairs={{0,4},{2,6},{4,0},{6,2},{8,12},{10,14},{12,8},{14,10},{1,5},{3,7},... | collective-permute-start | bytes 3145736 | tf_op jit(solution)/shard_map/ppermute | solution.py:486
  27.2 46.0 %collective-permute-start.16 = (bf16[16,256,128]{2,1,0:T(8,128)(2,1)S(1)}, bf16[16,256,128]{2,1,0:T(8,128)(2,1)S(1)}, u32[]{:S(2)}, u32[]{:S(2)}) collective-permute-start(bf16[16,256,128]{2,1,0:T(8,128)(2,1)S(1)} %constant_dynamic-slice_fusion.refs_2_.refs_6_), channel_id=1, source_target_pairs={{4,8},{6,10},{8,4},{10,6},{5,9},{7,11},{9,5},{11,7},{20,24},{22,26... | collective-permute-start | bytes 3145736 | tf_op jit(solution)/shard_map/ppermute | solution.py:486
  37.4 57.4 %copy-start = (f32[16,256,128]{2,1,0:T(8,128)}, f32[16,256,128]{2,1,0:T(8,128)S(1)}, u32[]{:S(2)}) copy-start(f32[16,256,128]{2,1,0:T(8,128)S(1)} %broadcast_in_dim.4.refs_2_) | copy-start | bytes 6291460
  37.4 13.8 %copy-start.3 = (bf16[16,256,256]{2,1,0:T(8,128)(2,1)S(1)}, bf16[16,256,256]{2,1,0:T(8,128)(2,1)}, u32[]{:S(2)}) copy-start(bf16[16,256,256]{2,1,0:T(8,128)(2,1)} %copy-done.2) | copy-start | bytes 6291460
  44.0 32.9 %collective-permute-start.14 = (bf16[16,256,128]{2,1,0:T(8,128)(2,1)}, bf16[16,256,128]{2,1,0:T(8,128)(2,1)S(1)}, u32[]{:S(2)}, u32[]{:S(2)}) collective-permute-start(bf16[16,256,128]{2,1,0:T(8,128)(2,1)} %collective-permute-done.8.refs_0_.refs_1_.refs_5_), channel_id=1, source_target_pairs={{0,1},{1,0},{2,3},{3,2},{4,5},{5,4},{6,7},{7,6},{8,9},{9,8},{10,11... | collective-permute-start | bytes 3145736 | tf_op jit(solution)/shard_map/ppermute | solution.py:489
  49.0 8.6 %copy-start.10 = (bf16[16,256,128]{2,1,0:T(8,128)(2,1)}, bf16[16,256,128]{2,1,0:T(8,128)(2,1)S(1)}, u32[]{:S(2)}) copy-start(bf16[16,256,128]{2,1,0:T(8,128)(2,1)S(1)} %collective-permute-done.12.refs_1_.refs_7_.refs_5_) | copy-start | bytes 3145732
  64.0 12.5 %copy-start.14 = (bf16[16,256,128]{2,1,0:T(8,128)(2,1)}, bf16[16,256,128]{2,1,0:T(8,128)(2,1)S(1)}, u32[]{:S(2)}) copy-start(bf16[16,256,128]{2,1,0:T(8,128)(2,1)S(1)} %collective-permute-done.10.refs_1_.refs_2_.refs_6_) | copy-start | bytes 3145732
  64.0 14.2 %collective-permute-start.15 = (bf16[16,256,128]{2,1,0:T(8,128)(2,1)S(1)}, bf16[16,256,128]{2,1,0:T(8,128)(2,1)S(1)}, u32[]{:S(2)}, u32[]{:S(2)}) collective-permute-start(bf16[16,256,128]{2,1,0:T(8,128)(2,1)S(1)} %collective-permute-done.10.refs_1_.refs_2_.refs_6_), channel_id=1, source_target_pairs={{0,1},{1,0},{2,3},{3,2},{4,5},{5,4},{6,7},{7,6},{8,9},{9,8},{10,11... | collective-permute-start | bytes 3145736 | tf_op jit(solution)/shard_map/ppermute | solution.py:489
  67.9 15.0 %collective-permute-start.18 = (bf16[1,8,256,128]{3,2,1,0:T(8,128)(2,1)}, bf16[1,8,256,128]{3,2,1,0:T(8,128)(2,1)S(1)}, u32[]{:S(2)}, u32[]{:S(2)}) collective-permute-start(bf16[1,8,256,128]{3,2,1,0:T(8,128)(2,1)} %pack.10.refs_6_), channel_id=1, source_target_pairs={{4,0},{6,2},{8,12},{10,14},{5,1},{7,3},{9,13},{11,15},{20,16},{22,... | collective-permute-start | bytes 1572872 | tf_op jit(solution)/shard_map/ppermute | solution.py:486
  71.3 29.5 %collective-permute-start.9 = (bf16[16,256,128]{2,1,0:T(8,128)(2,1)}, bf16[16,256,128]{2,1,0:T(8,128)(2,1)S(1)}, u32[]{:S(2)}, u32[]{:S(2)}) collective-permute-start(bf16[16,256,128]{2,1,0:T(8,128)(2,1)} %collective-permute-done.8.refs_0_.refs_1_.refs_5_), channel_id=1, source_target_pairs={{4,8},{6,10},{8,4},{10,6},{5,9},{7,11},{9,5},{11,7},{20,24},{22,26... | collective-permute-start | bytes 3145736 | tf_op jit(solution)/shard_map/ppermute | solution.py:486
  76.5 6.2 %copy-start.19 = (bf16[2,8,256,128]{3,2,1,0:T(8,128)(2,1)}, bf16[2,8,256,128]{3,2,1,0:T(8,128)(2,1)S(1)}, u32[]{:S(2)}) copy-start(bf16[2,8,256,128]{3,2,1,0:T(8,128)(2,1)S(1)} %pack.12.refs_9_) | copy-start | bytes 3145732
  76.5 31.4 %collective-permute-start.17 = (bf16[2,8,256,128]{3,2,1,0:T(8,128)(2,1)S(1)}, bf16[2,8,256,128]{3,2,1,0:T(8,128)(2,1)}, u32[]{:S(2)}, u32[]{:S(2)}) collective-permute-start(bf16[2,8,256,128]{3,2,1,0:T(8,128)(2,1)S(1)} %pack.12.refs_9_), channel_id=1, source_target_pairs={{0,2},{2,0},{4,6},{6,4},{8,10},{10,8},{12,14},{14,12},{1,3},{3,1},... | collective-permute-start | bytes 3145736 | tf_op jit(solution)/shard_map/ppermute | solution.py:486
  76.9 18.0 %collective-permute-start.19 = (bf16[1,8,256,128]{3,2,1,0:T(8,128)(2,1)S(1)}, bf16[1,8,256,128]{3,2,1,0:T(8,128)(2,1)S(1)}, u32[]{:S(2)}, u32[]{:S(2)}) collective-permute-start(bf16[1,8,256,128]{3,2,1,0:T(8,128)(2,1)S(1)} %pack.11.refs_3_), channel_id=1, source_target_pairs={{4,0},{6,2},{8,12},{10,14},{5,1},{7,3},{9,13},{11,15},{20,16},{22,... | collective-permute-start | bytes 1572872 | tf_op jit(solution)/shard_map/ppermute | solution.py:486
  82.7 7.6 %copy-start.18 = (bf16[16,128,256]{2,1,0:T(8,128)(2,1)}, bf16[16,128,256]{2,1,0:T(8,128)(2,1)S(1)}, u32[]{:S(2)}) copy-start(bf16[16,128,256]{2,1,0:T(8,128)(2,1)S(1)} %get-tuple-element.77.refs_6_) | copy-start | bytes 3145732
  84.8 6.8 %copy-start.15 = (bf16[16,256,128]{2,1,0:T(8,128)(2,1)S(1)}, bf16[16,256,128]{2,1,0:T(8,128)(2,1)}, u32[]{:S(2)}) copy-start(bf16[16,256,128]{2,1,0:T(8,128)(2,1)} %copy-done.14) | copy-start | bytes 3145732
  90.3 17.6 %collective-permute-start.20 = (bf16[8,256,128]{2,1,0:T(8,128)(2,1)S(1)}, bf16[8,256,128]{2,1,0:T(8,128)(2,1)S(1)}, u32[]{:S(2)}, u32[]{:S(2)}) collective-permute-start(bf16[8,256,128]{2,1,0:T(8,128)(2,1)S(1)} %amplitudes.12.refs_7_), channel_id=1, source_target_pairs={{4,0},{6,2},{8,12},{10,14},{5,1},{7,3},{9,13},{11,15},{20,16},{22,... | collective-permute-start | bytes 1572872 | tf_op jit(solution)/shard_map/ppermute | solution.py:486
  91.7 34.4 %collective-permute-start.13 = (bf16[16,256,128]{2,1,0:T(8,128)(2,1)S(1)}, bf16[16,256,128]{2,1,0:T(8,128)(2,1)S(1)}, u32[]{:S(2)}, u32[]{:S(2)}) collective-permute-start(bf16[16,256,128]{2,1,0:T(8,128)(2,1)S(1)} %copy-done.15), channel_id=1, source_target_pairs={{4,8},{6,10},{8,4},{10,6},{5,9},{7,11},{9,5},{11,7},{20,24},{22,26... | collective-permute-start | bytes 3145736 | tf_op jit(solution)/shard_map/ppermute | solution.py:486
  94.9 5.9 %copy-start.22 = (bf16[1,8,256,128]{3,2,1,0:T(8,128)(2,1)}, bf16[1,8,256,128]{3,2,1,0:T(8,128)(2,1)S(1)}, u32[]{:S(2)}) copy-start(bf16[1,8,256,128]{3,2,1,0:T(8,128)(2,1)S(1)} %collective-permute-done.19.refs_8_.refs_4_) | copy-start | bytes 1572868
  100.7 8.0 %copy-start.11 = (bf16[16,256,128]{2,1,0:T(8,128)(2,1)S(1)}, bf16[16,256,128]{2,1,0:T(8,128)(2,1)}, u32[]{:S(2)}) copy-start(bf16[16,256,128]{2,1,0:T(8,128)(2,1)} %copy-done.10) | copy-start | bytes 3145732
  100.8 8.0 %copy-start.13 = (bf16[16,256,128]{2,1,0:T(8,128)(2,1)S(1)}, bf16[16,256,128]{2,1,0:T(8,128)(2,1)}, u32[]{:S(2)}) copy-start(bf16[16,256,128]{2,1,0:T(8,128)(2,1)} %copy-done.12) | copy-start | bytes 3145732
  100.8 14.2 %copy-start.6 = (bf16[16,256,128]{2,1,0:T(8,128)(2,1)}, bf16[16,256,128]{2,1,0:T(8,128)(2,1)S(1)}, u32[]{:S(2)}) copy-start(bf16[16,256,128]{2,1,0:T(8,128)(2,1)S(1)} %collective-permute-done.9.refs_1_.refs_7_.refs_5_) | copy-start | bytes 3145732
  103.0 17.8 %collective-permute-start.21 = (bf16[1,8,256,128]{3,2,1,0:T(8,128)(2,1)}, bf16[1,8,256,128]{3,2,1,0:T(8,128)(2,1)S(1)}, u32[]{:S(2)}, u32[]{:S(2)}) collective-permute-start(bf16[1,8,256,128]{3,2,1,0:T(8,128)(2,1)} %pack.13.refs_2_), channel_id=1, source_target_pairs={{4,2},{6,0},{8,14},{10,12},{5,3},{7,1},{9,15},{11,13},{20,18},{22,... | collective-permute-start | bytes 1572872 | tf_op jit(solution)/shard_map/ppermute | solution.py:486
  117.2 42.6 %collective-permute-start.26 = (bf16[2,8,256,128]{3,2,1,0:T(8,128)(2,1)S(1)}, bf16[2,8,256,128]{3,2,1,0:T(8,128)(2,1)}, u32[]{:S(2)}, u32[]{:S(2)}) collective-permute-start(bf16[2,8,256,128]{3,2,1,0:T(8,128)(2,1)S(1)} %pack.15.refs_6_), channel_id=1, source_target_pairs={{0,2},{2,0},{4,6},{6,4},{8,10},{10,8},{12,14},{14,12},{1,3},{3,1},... | collective-permute-start | bytes 3145736 | tf_op jit(solution)/shard_map/ppermute | solution.py:486
  118.5 33.4 %collective-permute-start.22 = (bf16[1,8,256,128]{3,2,1,0:T(8,128)(2,1)}, bf16[1,8,256,128]{3,2,1,0:T(8,128)(2,1)S(1)}, u32[]{:S(2)}, u32[]{:S(2)}) collective-permute-start(bf16[1,8,256,128]{3,2,1,0:T(8,128)(2,1)} %pack.14.refs_8_), channel_id=1, source_target_pairs={{4,6},{6,4},{8,10},{10,8},{5,7},{7,5},{9,11},{11,9},{20,22},{22,20... | collective-permute-start | bytes 1572872 | tf_op jit(solution)/shard_map/ppermute | solution.py:486
  120.8 31.0 %copy-start.16 = (bf16[1,8,256,128]{3,2,1,0:T(8,128)(2,1)}, bf16[1,8,256,128]{3,2,1,0:T(8,128)(2,1)S(1)}, u32[]{:S(2)}) copy-start(bf16[1,8,256,128]{3,2,1,0:T(8,128)(2,1)S(1)} %collective-permute-done.21.refs_7_.refs_10_) | copy-start | bytes 1572868
  126.1 25.7 %copy-start.8 = (bf16[16,256,128]{2,1,0:T(8,128)(2,1)}, bf16[16,256,128]{2,1,0:T(8,128)(2,1)S(1)}, u32[]{:S(2)}) copy-start(bf16[16,256,128]{2,1,0:T(8,128)(2,1)S(1)} %collective-permute-done.13.refs_1_.refs_8_.refs_6_) | copy-start | bytes 3145732
  130.5 37.3 %collective-permute-start.24 = (bf16[1,8,256,128]{3,2,1,0:T(8,128)(2,1)}, bf16[1,8,256,128]{3,2,1,0:T(8,128)(2,1)}, u32[]{:S(2)}, u32[]{:S(2)}) collective-permute-start(bf16[1,8,256,128]{3,2,1,0:T(8,128)(2,1)} %pack.17.refs_9_), channel_id=1, source_target_pairs={{4,6},{6,4},{8,10},{10,8},{5,7},{7,5},{9,11},{11,9},{20,22},{22,20... | collective-permute-start | bytes 1572872 | tf_op jit(solution)/shard_map/ppermute | solution.py:486
  133.6 34.2 %collective-permute-start.25 = (bf16[1,8,256,128]{3,2,1,0:T(8,128)(2,1)}, bf16[1,8,256,128]{3,2,1,0:T(8,128)(2,1)}, u32[]{:S(2)}, u32[]{:S(2)}) collective-permute-start(bf16[1,8,256,128]{3,2,1,0:T(8,128)(2,1)} %pack.16.refs_2_), channel_id=1, source_target_pairs={{4,2},{6,0},{8,14},{10,12},{5,3},{7,1},{9,15},{11,13},{20,18},{22,... | collective-permute-start | bytes 1572872 | tf_op jit(solution)/shard_map/ppermute | solution.py:486
  151.8 5.9 %copy-start.20 = (bf16[1,8,256,128]{3,2,1,0:T(8,128)(2,1)}, bf16[1,8,256,128]{3,2,1,0:T(8,128)(2,1)S(1)}, u32[]{:S(2)}) copy-start(bf16[1,8,256,128]{3,2,1,0:T(8,128)(2,1)S(1)} %collective-permute-done.22.refs_11_.refs_5_) | copy-start | bytes 1572868
  157.7 16.0 %collective-permute-start.23 = (bf16[8,256,128]{2,1,0:T(8,128)(2,1)}, bf16[8,256,128]{2,1,0:T(8,128)(2,1)}, u32[]{:S(2)}, u32[]{:S(2)}) collective-permute-start(bf16[8,256,128]{2,1,0:T(8,128)(2,1)} %amplitudes.16.refs_6_), channel_id=1, source_target_pairs={{4,0},{6,2},{8,12},{10,14},{5,1},{7,3},{9,13},{11,15},{20,16},{22,... | collective-permute-start | bytes 1572872 | tf_op jit(solution)/shard_map/ppermute | solution.py:486
  161.4 6.4 %copy-start.17 = (bf16[1,8,256,128]{3,2,1,0:T(8,128)(2,1)S(1)}, bf16[1,8,256,128]{3,2,1,0:T(8,128)(2,1)}, u32[]{:S(2)}) copy-start(bf16[1,8,256,128]{3,2,1,0:T(8,128)(2,1)} %copy-done.16) | copy-start | bytes 1572868
  161.4 6.4 %copy-start.21 = (bf16[1,8,256,128]{3,2,1,0:T(8,128)(2,1)S(1)}, bf16[1,8,256,128]{3,2,1,0:T(8,128)(2,1)}, u32[]{:S(2)}) copy-start(bf16[1,8,256,128]{3,2,1,0:T(8,128)(2,1)} %copy-done.20) | copy-start | bytes 1572868
  167.9 5.9 %copy-start.7 = (bf16[16,256,128]{2,1,0:T(8,128)(2,1)S(1)}, bf16[16,256,128]{2,1,0:T(8,128)(2,1)}, u32[]{:S(2)}) copy-start(bf16[16,256,128]{2,1,0:T(8,128)(2,1)} %copy-done.6) | copy-start | bytes 3145732
  167.9 5.9 %copy-start.9 = (bf16[16,256,128]{2,1,0:T(8,128)(2,1)S(1)}, bf16[16,256,128]{2,1,0:T(8,128)(2,1)}, u32[]{:S(2)}) copy-start(bf16[16,256,128]{2,1,0:T(8,128)(2,1)} %copy-done.8) | copy-start | bytes 3145732
  184.2 9.0 %collective-permute-start.28 = (f32[16,128,256]{2,1,0:T(8,128)S(1)}, f32[16,128,256]{2,1,0:T(8,128)}, u32[]{:S(2)}, u32[]{:S(2)}) collective-permute-start(f32[16,128,256]{2,1,0:T(8,128)S(1)} %density_rows.3), channel_id=1, source_target_pairs={{0,1},{1,0},{2,3},{3,2},{4,5},{5,4},{6,7},{7,6},{8,9},{9,8},{10,11... | collective-permute-start | bytes 6291464 | tf_op jit(solution)/shard_map/ppermute | solution.py:489
  188.6 4.1 %collective-permute-start.27 = (f32[64]{0:T(128)S(1)}, f32[64]{0:T(128)S(1)}, u32[]{:S(2)}, u32[]{:S(2)}) collective-permute-start(f32[64]{0:T(128)S(1)} %multiply_reduce_fusion), channel_id=1, source_target_pairs={{0,1},{1,0},{2,3},{3,2},{4,5},{5,4},{6,7},{7,6},{8,9},{9,8},{10,11... | collective-permute-start | bytes 776 | tf_op jit(solution)/shard_map/ppermute | solution.py:489
  (16 other events, 28.5 us)

commit v7 on v6

--- a/solution.py
+++ b/solution.py
@@ -93,7 +93,18 @@
 PARAMS = pltpu.CompilerParams(vmem_limit_bytes=LIMIT)
 
 
-def lists_kernel(cap, vir, occ, size, owner, slot, small, hit):
+def lists_kernel(cap, *refs):
+    small, hit = refs[5:7]
+    sems = refs[-1]
+    copies = [
+        pltpu.make_async_copy(x, to, sems.at[k])
+        for k, (x, to) in enumerate(zip(refs[:5], refs[7:12]))
+    ]
+    for copy in copies:
+        copy.start()
+    for copy in copies:
+        copy.wait()
+    vir, occ, size, owner, slot = refs[7:12]
     n, (count, nvd) = hit.shape[0], vir.shape
 
     def column(row, m):
@@ -129,8 +140,16 @@
             jax.ShapeDtypeStruct((count + 8, nvd + 128), f32),
             jax.ShapeDtypeStruct((n, n), f32),
         ),
-        in_specs=[VMEM] * 5,
+        in_specs=[HBM] * 5,
         out_specs=(VMEM, VMEM),
+        scratch_shapes=[
+            pltpu.VMEM((count, nvd), f32),
+            pltpu.VMEM((1, count), f32),
+            pltpu.VMEM((1, count), i32),
+            pltpu.VMEM((1, n), i32),
+            pltpu.VMEM((1, n), i32),
+            pltpu.SemaphoreType.DMA((5,)),
+        ],
         compiler_params=PARAMS,
         cost_estimate=TINY,
         name="lists",
@@ -148,9 +167,8 @@
     )
 
 
-def tables_kernel(cap, per_orb, meta, *refs):
-    smalls, outs = refs[:8], refs[8:]
-    count, nvd = smalls[0].shape[0] - 8, smalls[0].shape[1] - 128
+def tables_kernel(cap, per_orb, meta, every, *outs):
+    count, nvd = every.shape[1] - 8, every.shape[2] - 128
     n = 8 * cap
     me, col0 = meta[0], meta[1]
     z, y = me // 2, me % 2
@@ -162,13 +180,14 @@
     head_row = jnp.zeros((1, 128), i32)
     for k, value in enumerate(head + [middle, col0]):
         head_row = jnp.where(lane == k, value, head_row)
-    orbitals = jnp.concatenate([x[:count, :] for x in smalls], axis=0)
+    orbitals = jnp.concatenate([every[d, :count, :] for d in range(8)], axis=0)
     columns = jnp.where(col0 == 0, orbitals[:, : nvd // 2], orbitals[:, nvd // 2 : nvd])
     extra = orbitals[:, nvd:]
 
     def build(x, tbl, rows=None):
-        order = smalls[x][count : count + 1, :n].astype(i32)
-        slots = smalls[x][count : count + 1, 128 : 128 + n].astype(i32)
+        packet = every[me ^ x]
+        order = packet[count : count + 1, :n].astype(i32)
+        slots = packet[count : count + 1, 128 : 128 + n].astype(i32)
         tbl[...] = jnp.zeros_like(tbl)
         tbl[HEAD : HEAD + 1, :] = head_row
         tbl[SLOT : SLOT + 1, :n] = slots
@@ -177,11 +196,11 @@
         tbl[ORDER : ORDER + 1, :n] = order
         pair = lax.broadcasted_iota(i32, (1, n), 1)
         owner = sum(jnp.where(pair >= k * cap, 1, 0) for k in range(1, 8))
-        index = (owner ^ me) * count + slots
+        index = owner * count + slots
         theirs = jnp.where(lax.broadcasted_iota(i32, (8 * count, n), 0) == index, 1.0, 0.0)
         first = sum(jnp.where(order >= k * per_orb, 1, 0) for k in range(1, count))
         mine = jnp.where(lax.broadcasted_iota(i32, (count, n), 0) == first, 1.0, 0.0)
-        own = smalls[x][:count, nvd:]
+        own = packet[:count, nvd:]
         rows[...] = pick(theirs, columns) - (pick(theirs, extra)[:, :1] + pick(mine, own)[:, :1])
         tbl[SIZE_I : SIZE_I + 1, :n] = pick(own, mine)[1:2, :].astype(i32)
         tbl[SIZE_J : SIZE_J + 1, :n] = pick(extra, theirs)[1:2, :].astype(i32) - col0
@@ -192,73 +211,66 @@
     build(3, outs[5])
 
 
-def tables_of(meta, smalls, cap, per_orb, half):
+def tables_of(meta, every, cap, per_orb, half):
     table = jax.ShapeDtypeStruct((8, 128), i32)
     rows = jax.ShapeDtypeStruct((8 * cap, half), f32)
     return pl.pallas_call(
         lambda *refs: tables_kernel(cap, per_orb, *refs),
         out_shape=(table, rows, table, rows, table, table),
-        in_specs=[SMEM] + [VMEM] * 8,
+        in_specs=[SMEM, VMEM],
         out_specs=[VMEM] * 6,
         compiler_params=PARAMS,
         cost_estimate=TINY,
         name="tables",
-    )(meta, *smalls)
-
-
-def pack_kernel(call, only_middle, relayed, after, tbl, *refs):
-    out, sems = refs[-2:]
-    halves, cap = out.shape[:2]
-    base = tbl[HEAD, call]
-    middle = tbl[HEAD, MIDDLE] == 1
-
-    def run(copies):
-        for copy in copies:
+    )(meta, every)
+
+
+def pack_kernel(jobs, tables, after, *refs):
+    tbls, sources = refs[:tables], refs[tables : tables + len(jobs)]
+    outs, sems = refs[tables + len(jobs) + after : -1], refs[-1]
+
+    def copies(only_middle):
+        made = []
+        for k, (table, call, middle) in enumerate(jobs):
+            if middle == only_middle:
+                base = tbls[table][HEAD, call]
+                for r in range(outs[k].shape[0]):
+                    slot = tbls[table][SLOT, base + r]
+                    made.append(
+                        pltpu.make_async_copy(sources[k].at[slot], outs[k].at[r], sems.at[k, r])
+                    )
+        return made
+
+    everywhere = copies(False)
+    for copy in everywhere:
+        copy.start()
+
+    @pl.when(tbls[0][HEAD, MIDDLE] == 1)
+    def _():
+        some = copies(True)
+        for copy in some:
             copy.start()
-        for copy in copies:
+        for copy in some:
             copy.wait()
 
-    def gather():
-        run(
-            [
-                pltpu.make_async_copy(
-                    refs[q].at[tbl[SLOT, base + r]], out.at[q, r], sems.at[q, r]
-                )
-                for q in range(halves)
-                for r in range(cap)
-            ]
-        )
-
-    if not only_middle and not relayed:
-        gather()
-    else:
-        pl.when(middle)(gather)
-    if relayed:
-
-        @pl.when(jnp.logical_not(middle))
-        def _():
-            run(
-                [
-                    pltpu.make_async_copy(refs[halves + q].at[0], out.at[q], sems.at[q, 0])
-                    for q in range(halves)
-                ]
-            )
-
-
-def pack(tbl, call, sources, cap, only_middle=False, relayed=None, after=()):
-    halves = len(sources)
-    shape = (halves, cap) + sources[0].shape[1:]
-    operands = (*sources, *(relayed or ()), *after)
+    for copy in everywhere:
+        copy.wait()
+
+
+def pack(tbls, jobs, cap, after=()):
+    sources = [source for _, _, source, _ in jobs]
+    shape = jax.ShapeDtypeStruct((cap,) + sources[0].shape[1:], bf16)
+    kinds = [(table, call, middle) for table, call, _, middle in jobs]
     return pl.pallas_call(
-        lambda *refs: pack_kernel(call, only_middle, relayed is not None, len(after), *refs),
-        out_shape=jax.ShapeDtypeStruct(shape, bf16),
-        in_specs=[SMEM] + [HBM] * len(operands),
-        out_specs=VMEM,
-        scratch_shapes=[pltpu.SemaphoreType.DMA((halves, cap))],
+        lambda *refs: pack_kernel(kinds, len(tbls), len(after), *refs),
+        out_shape=[shape] * len(jobs),
+        in_specs=[SMEM] * len(tbls) + [HBM] * (len(jobs) + len(after)),
+        out_specs=[VMEM] * len(jobs),
+        scratch_shapes=[pltpu.SemaphoreType.DMA((len(jobs), cap))],
         compiler_params=PARAMS,
         cost_estimate=TINY,
         name="pack",
-    )(tbl, *operands)
+    )(*tbls, *sources, *after)
 
 
 def turn_kernel(*refs):
@@ -294,10 +306,8 @@
     else:
         tout, eout = refs[-11:-9]
         left, js = refs[:2], refs[2:5]
-    if mode == "asked":
-        js = (js[0].at[0], js[0].at[1])
     if mode == "asked_two":
-        js, elsewhere = [[x.at[0] for x in refs[k : k + 2]] for k in (2, 4)]
+        js, elsewhere = refs[2:4], refs[4:6]
     cap = sv.shape[0]
     nvd, half = sv.shape[1], sv.shape[2]
     base = tbl[HEAD, call]
@@ -493,71 +503,77 @@
 
     cross = [(2, 4), (3, 5), (4, 2), (5, 3)]
     outward = [(2, 0), (3, 1), (4, 6), (5, 7)]
-    outward_diagonal = [(2, 1), (3, 0), (4, 7), (5, 6)]
+    diagonal = [(2, 1), (3, 0), (4, 7), (5, 6)]
     y_middle = [(2, 3), (3, 2), (4, 5), (5, 4)]
 
     small, hit = lists(vir_energy, occ_energy, domain_size, partner_owner, partner_slot, cap)
-    smalls = [small] + [pp(small, flip(bits)) for bits in range(1, peers)]
+    every = lax.all_gather(small, "orb")
 
     other = swap_core(blocks)
     own = [lax.dynamic_slice_in_dim(x, col0, half, 2) for x in (blocks, other)]
-    sent, smalls = lax.optimization_barrier((own[0], smalls))
+    sent, every = lax.optimization_barrier((own[0], every))
     near = [pp(x, flip(2)) for x in (sent, own[1])]
     mid = [pp(x, cross) for x in (sent, own[1])]
     tbl, rows, client_tbl, client_rows, beside_list, relay_list = tables_of(
-        jnp.stack([me, col0]), smalls, cap, per_orb, half
+        jnp.stack([me, col0]), every, cap, per_orb, half
     )
 
     def spread(vir):
         return jnp.broadcast_to(vir[:, :, None], (occ, nvd, half))
 
     tables = (tbl, rows, spread(vir_energy))
-    client = (client_tbl, client_rows, spread(smalls[2][:occ, :nvd]))
+    client_vir = lax.dynamic_index_in_dim(every, me ^ 2, 0, keepdims=False)[:occ, :nvd]
+    client = (client_tbl, client_rows, spread(client_vir))
+    lists_of = [beside_list, relay_list]
 
     def own_pairs(k, mode, sources, held=(), after=()):
         return amplitudes(mode, k, per_orb, tables, left, sources, cap, held, after)
 
-    packed = pack(beside_list, 0, own, cap)
-    beside = pp(packed, flip(1))
+    packed = pack(lists_of, [(0, 0, x, False) for x in own], cap)
+    beside = [pp(x, flip(1)) for x in packed]
     left = turn([blocks, other])
-    held = own_pairs(0, "slots", own, after=(packed,))
+    held = own_pairs(0, "slots", own, after=(packed[1],))
+
+    def send_on(x, y, token):
+        jobs = [(0, 1, x, False), (1, 2, y, True), (0, 2, y, True)]
+        packed = pack(lists_of, jobs, cap, after=(token,))
+        perms = (flip(1), diagonal, y_middle)
+        return packed[0], [pp(part, perm) for part, perm in zip(packed, perms)]
+
     first, held = lax.optimization_barrier((near[0], held))
     far = [pp(first, cross)]
     across = [swap_core(first)]
-    packed = pack(relay_list, 2, mid[:1], cap, only_middle=True, after=(held[1],))
-    relays = [pp(packed, outward)]
-    held = own_pairs(4, "asked", [beside], held, (packed,))
+    packed, sent_first = send_on(first, mid[0], held[1])
+    held = own_pairs(4, "asked", beside, held, (packed,))
     second, held = lax.optimization_barrier((near[1], held))
     far.append(pp(second, cross))
     across.append(swap_core(second))
     near = [first, second]
-    packed = pack(relay_list, 2, mid[1:], cap, only_middle=True, after=(held[1],))
-    relays.append(pp(packed, outward))
-    packed = pack(beside_list, 1, near, cap, after=(packed,))
-    beside_near = pp(packed, flip(1))
+    packed, sent_second = send_on(second, mid[1], held[1])
+    beside_near, third_diagonal, third = zip(sent_first, sent_second)
     client_left = turn(near + across)
-    gone = amplitudes("client", 2, per_orb, client, client_left, mid, cap, after=(packed, relays[0]))
+    gone = amplitudes(
+        "client", 2, per_orb, client, client_left, mid, cap, after=(packed, third_diagonal[0], third[0])
+    )
     ready_2 = pp(gone, outward)
-    held = own_pairs(1, "slots", near, held, (gone, relays[1]))
-    diagonal, fourth = [], []
+    held = own_pairs(1, "slots", near, held, (gone, third_diagonal[1], beside_near[0]))
+    fourth_diagonal, fourth = [], []
 
     def send_far(q, token):
-        packed = pack(relay_list, 3, far[q : q + 1], cap, only_middle=True, after=(token,))
-        diagonal.append(pp(packed, outward_diagonal))
-        packed = pack(beside_list, 3, far[q : q + 1], cap, only_middle=True, after=(packed,))
-        fourth.append(pp(packed, y_middle))
-        return packed
+        jobs = [(1, 3, far[q], True), (0, 3, far[q], True)]
+        packed = pack(lists_of, jobs, cap, after=(token,))
+        fourth_diagonal.append(pp(packed[0], diagonal))
+        fourth.append(pp(packed[1], y_middle))
+        return packed[0]
 
     packed = send_far(0, held[1])
-    held = own_pairs(2, "served", mid + [ready_2], held, (packed, beside_near))
-    packed = pack(beside_list, 2, mid, cap, relayed=relays, after=(held[1],))
-    third = pp(packed, flip(1))
-    held = own_pairs(5, "asked", [beside_near], held, (packed, diagonal[0]))
+    held = own_pairs(2, "served", mid + [ready_2], held, (packed, third[1]))
+    held = own_pairs(5, "asked", beside_near, held, (fourth_diagonal[0],))
+    held = own_pairs(6, "asked_two", third + third_diagonal, held)
     packed = send_far(1, held[1])
-    gone = amplitudes("client", 3, per_orb, client, client_left, far, cap, after=(packed, diagonal[0], fourth[0]))
+    gone = amplitudes("client", 3, per_orb, client, client_left, far, cap, after=(packed,))
     ready_3 = pp(gone, outward)
-    held = own_pairs(6, "asked", [third], held, (gone,))
-    held = own_pairs(7, "asked_two", fourth + diagonal, held)
+    held = own_pairs(7, "asked_two", fourth + fourth_diagonal, held, (gone,))
     t_all, e_all = own_pairs(3, "served", far + [ready_3], held)
 
     away = swap_core(density_rows(t_all, (1 - core) * half, per_orb, half))

time: 198 us -> 225 us (1.14)
  the two profiles are of different devices: /device:TPU:9 before, /device:TPU:0 now
where the time goes in v7:
time: 225 us; the launch traced here: 224 us
  Pallas kernels  76.7 us (34%)
  waiting for transfers between devices  63.3 us (28%)
  blocking collectives  32.2 us (14%)
  starting transfers between devices  28.1 us (12%)
  local copies, waits for them, and re-layouts  18.4 us (8%)
  other arithmetic  3.99 us (2%)
    ppermute x20, waiting for transfers between devices, pp(): return lax.ppermute(x, 'orb', perm)  63.3 us
    pallas_call x10, Pallas kernels, amplitudes(): pl.pallas_call(lambda *refs: amplitudes_kernel(mode, call, per_orb, not h...  48.7 us
    all_gather x1, blocking collectives, line_plan(): every = lax.all_gather(small, 'orb')  32.2 us
    ppermute x20, starting transfers between devices, pp(): return lax.ppermute(x, 'orb', perm)  26.5 us
    pallas_call x5, Pallas kernels, pack(): pl.pallas_call(lambda *refs: pack_kernel(kinds, len(tbls), len(after), *r...  11.4 us
    unnamed x56, local copies, waits for them, and re-layouts  11.2 us
    pallas_call x2, Pallas kernels, density_rows(): pl.pallas_call(density_kernel, out_shape=jax.ShapeDtypeStruct((occ, half,...  7.99 us
    pallas_call x2, Pallas kernels, turn(): pl.pallas_call(turn_kernel, out_shape=[jax.ShapeDtypeStruct((count, cols,...  7.04 us
  transfers between devices with their start and end apart: 25, of which 7 were waited for; matrix products, arithmetic and copies ran while one was open for 4% of the time, Pallas kernels for 30%

profile of v7, /device:TPU:0, one launch (start us, length us, event | category | flops | bytes accessed | tf_op | source)
XLA Modules:
  0.0 223.9 jit_solution(7975165587137618440)
XLA Ops:
  5.3 32.2 %all-gather = f32[192,384]{1,0:T(8,128)S(1)} all-gather(f32[24,384]{1,0:T(8,128)S(1)} %get-tuple-element.53), channel_id=2, replica_groups=mesh['mol'=2,'orb'=8,'aux'=2] {'orb'}, dimensions={0}, use_global_device_ids=true | all-gather | bytes 331776 | tf_op jit(solution)/shard_map/all_gather | solution.py:510
  37.6 2.3 %constant_dynamic-slice_fusion.1.refs_2_.refs_5_ = bf16[16,256,128]{2,1,0:T(8,128)(2,1)} fusion(bf16[16,256,256]{2,1,0:T(8,128)(2,1)} %refs_0_.3, s32[]{:T(128)S(6)} %select_n.8), kind=kLoop, calls=%fused_computation.3 | loop fusion | bytes 2097156 | tf_op jit(solution)/shard_map/dynamic_slice | solution.py:513
  40.6 2.3 %constant_dynamic-slice_fusion.refs_3_.refs_6_ = bf16[16,256,128]{2,1,0:T(8,128)(2,1)} fusion(bf16[16,256,256]{2,1,0:T(8,128)(2,1)} %collective-permute-done.refs_1_, s32[]{:T(128)S(6)} %select_n.8), kind=kLoop, calls=%fused_computation.2 | loop fusion | bytes 2097156 | tf_op jit(solution)/shard_map/dynamic_slice | solution.py:513
  43.0 3.2 %collective-permute-start.3 = (bf16[16,256,128]{2,1,0:T(8,128)(2,1)}, bf16[16,256,128]{2,1,0:T(8,128)(2,1)}, u32[]{:S(2)}, u32[]{:S(2)}) collective-permute-start(bf16[16,256,128]{2,1,0:T(8,128)(2,1)} %constant_dynamic-slice_fusion.refs_3_.refs_6_), channel_id=1, source_target_pairs={{0,4},{2,6},{4,0},{6,2},{8,12},{10,14},{12,8},{14,10},{1,5},{3,7},... | collective-permute-start | bytes 3145736 | tf_op jit(solution)/shard_map/ppermute | solution.py:496
  46.2 1.3 tables.1
  47.5 2.0 pack.5
  49.6 4.1 %collective-permute-start.5 = (bf16[8,256,128]{2,1,0:T(8,128)(2,1)S(1)}, bf16[8,256,128]{2,1,0:T(8,128)(2,1)S(1)}, u32[]{:S(2)}, u32[]{:S(2)}) collective-permute-start(bf16[8,256,128]{2,1,0:T(8,128)(2,1)S(1)} %get-tuple-element.62.refs_7_), channel_id=1, source_target_pairs={{0,2},{2,0},{4,6},{6,4},{8,10},{10,8},{12,14},{14,12},{1,3},{3,1},... | collective-permute-start | bytes 1572872 | tf_op jit(solution)/shard_map/ppermute | solution.py:496
  53.8 12.5 %collective-permute-done.1.refs_2_.refs_0_.refs_5_ = bf16[16,256,128]{2,1,0:T(8,128)(2,1)} collective-permute-done((bf16[16,256,128]{2,1,0:T(8,128)(2,1)}, bf16[16,256,128]{2,1,0:T(8,128)(2,1)}, u32[]{:S(2)}, u32[]{:S(2)}) %collective-permute-start.1) | collective-permute-done | bytes 1048608 | tf_op jit(solution)/shard_map/ppermute | solution.py:496
  67.0 3.5 %turn.2 = (bf16[16,256,256]{2,1,0:T(8,128)(2,1)S(1)}, bf16[16,256,256]{2,1,0:T(8,128)(2,1)S(1)}) custom-call(bf16[16,256,256]{2,1,0:T(8,128)(2,1)} %refs_0_.3, bf16[16,256,256]{2,1,0:T(8,128)(2,1)} %collective-permute-done.refs_1_), custom_call_target="tpu_custom_call" | custom-call | flops 1 | bytes 1 | tf_op jit(solution)/shard_map/turn/pallas_call | solution.py:287
  70.6 1.3 copy-done
  71.9 1.4 copy-done.3
  73.8 5.3 %amplitudes.10 = (bf16[64,256,128]{2,1,0:T(8,128)(2,1)}, f32[64,128]{1,0:T(8,128)S(1)}) custom-call(s32[8,128]{1,0:T(8,128)S(1)} %get-tuple-element.55.refs_0_, f32[64,128]{1,0:T(8,128)S(1)} %get-tuple-element.56.refs_1_, f32[16,256,128]{2,1,0:T(8,128)S(1)} %broadcast_in_dim.4.refs_2_, bf16[16,256,256]{2,1,0:T(8,128)(2,1)} %copy-done, ...), custom_call_target="tpu_custom_call" | custom-call | flops 1 | bytes 1 | tf_op jit(solution)/shard_map/amplitudes/pallas_call | solution.py:432
  79.2 3.2 %pack.6 = (bf16[8,256,128]{2,1,0:T(8,128)(2,1)}, bf16[8,256,128]{2,1,0:T(8,128)(2,1)}, bf16[8,256,128]{2,1,0:T(8,128)(2,1)S(1)}) custom-call(s32[8,128]{1,0:T(8,128)S(1)} %get-tuple-element.60.refs_0_, s32[8,128]{1,0:T(8,128)S(1)} %get-tuple-element.61.refs_1_, bf16[16,256,128]{2,1,0:T(8,128)(2,1)} %collective-permute-done.1.refs_2_.refs_0_.refs_5_, ...), custom_call_target="tpu_custom_call" | custom-call | flops 1 | bytes 1 | tf_op jit(solution)/shard_map/pack/pallas_call | solution.py:264
  82.4 7.7 %amplitudes.11 = (bf16[64,256,128]{2,1,0:T(8,128)(2,1)}, f32[64,128]{1,0:T(8,128)S(1)}) custom-call(s32[8,128]{1,0:T(8,128)S(1)} %get-tuple-element.55.refs_0_, f32[64,128]{1,0:T(8,128)S(1)} %get-tuple-element.56.refs_1_, f32[16,256,128]{2,1,0:T(8,128)S(1)} %broadcast_in_dim.4.refs_2_, ...), custom_call_target="tpu_custom_call", output_to_operand_aliasing={{0}: (8, {}), {1}: (9, {})} | custom-call | flops 1 | bytes 1 | tf_op jit(solution)/shard_map/amplitudes/pallas_call | solution.py:432
  91.9 1.3 collective-permute-start.13
  93.2 2.8 %pack.7 = (bf16[8,256,128]{2,1,0:T(8,128)(2,1)S(1)}, bf16[8,256,128]{2,1,0:T(8,128)(2,1)}, bf16[8,256,128]{2,1,0:T(8,128)(2,1)S(1)}) custom-call(s32[8,128]{1,0:T(8,128)S(1)} %get-tuple-element.60.refs_0_, s32[8,128]{1,0:T(8,128)S(1)} %get-tuple-element.61.refs_1_, bf16[16,256,128]{2,1,0:T(8,128)(2,1)} %collective-permute-done.3.refs_1_.refs_2_.refs_6_, ...), custom_call_target="tpu_custom_call" | custom-call | flops 1 | bytes 1 | tf_op jit(solution)/shard_map/pack/pallas_call | solution.py:264
  99.5 1.5 collective-permute-start.15
  101.0 1.3 collective-permute-start.14
  102.3 1.6 collective-permute-start.7
  103.9 3.5 %turn.3 = (bf16[16,128,256]{2,1,0:T(8,128)(2,1)S(1)}, bf16[16,128,256]{2,1,0:T(8,128)(2,1)S(1)}, bf16[16,128,256]{2,1,0:T(8,128)(2,1)S(1)}, bf16[16,128,256]{2,1,0:T(8,128)(2,1)S(1)}) custom-call(bf16[16,256,128]{2,1,0:T(8,128)(2,1)} %collective-permute-done.1.refs_2_.refs_0_.refs_5_, bf16[16,256,128]{2,1,0:T(8,128)(2,1)} %collective-permute-done.3.refs_1_.refs_2_.refs_6_, ...), custom_call_target="tpu_custom_call" | custom-call | flops 1 | bytes 1 | tf_op jit(solution)/shard_map/turn/pallas_call | solution.py:287
  107.5 5.8 %collective-permute-done.13.refs_10_.refs_7_ = bf16[8,256,128]{2,1,0:T(8,128)(2,1)} collective-permute-done((bf16[8,256,128]{2,1,0:T(8,128)(2,1)}, bf16[8,256,128]{2,1,0:T(8,128)(2,1)}, u32[]{:S(2)}, u32[]{:S(2)}) %collective-permute-start.13) | collective-permute-done | bytes 524320 | tf_op jit(solution)/shard_map/ppermute | solution.py:496
  113.4 1.7 collective-permute-start.16
  115.1 2.0 broadcast_in_dim.5.refs_2_
  117.1 1.2 amplitudes.12.refs_7_
  118.3 17.5 %collective-permute-done.15.refs_9_.refs_5_ = bf16[8,256,128]{2,1,0:T(8,128)(2,1)} collective-permute-done((bf16[8,256,128]{2,1,0:T(8,128)(2,1)}, bf16[8,256,128]{2,1,0:T(8,128)(2,1)}, u32[]{:S(2)}, u32[]{:S(2)}) %collective-permute-start.15) | collective-permute-done | bytes 524320 | tf_op jit(solution)/shard_map/ppermute | solution.py:496
  136.5 1.3 collective-permute-start.18
  137.8 5.2 %amplitudes.13 = (bf16[64,256,128]{2,1,0:T(8,128)(2,1)}, f32[64,128]{1,0:T(8,128)S(1)}) custom-call(s32[8,128]{1,0:T(8,128)S(1)} %get-tuple-element.55.refs_0_, f32[64,128]{1,0:T(8,128)S(1)} %get-tuple-element.56.refs_1_, f32[16,256,128]{2,1,0:T(8,128)S(1)} %broadcast_in_dim.4.refs_2_, ...), custom_call_target="tpu_custom_call", output_to_operand_aliasing={{0}: (10, {}), {1}: (11, {})} | custom-call | flops 1 | bytes 1 | tf_op jit(solution)/shard_map/amplitudes/pallas_call | solution.py:432
  143.1 1.6 pack.8
  144.7 1.3 collective-permute-start.17
  146.0 1.5 collective-permute-start.20
  147.5 5.7 %collective-permute-done.18.refs_7_ = bf16[8,256,128]{2,1,0:T(8,128)(2,1)S(1)} collective-permute-done((bf16[8,256,128]{2,1,0:T(8,128)(2,1)S(1)}, bf16[8,256,128]{2,1,0:T(8,128)(2,1)S(1)}, u32[]{:S(2)}, u32[]{:S(2)}) %collective-permute-start.18) | collective-permute-done | bytes 524320 | tf_op jit(solution)/shard_map/ppermute | solution.py:496
  153.2 4.6 %amplitudes.14 = (bf16[64,256,128]{2,1,0:T(8,128)(2,1)}, f32[64,128]{1,0:T(8,128)S(1)}) custom-call(s32[8,128]{1,0:T(8,128)S(1)} %get-tuple-element.55.refs_0_, f32[64,128]{1,0:T(8,128)S(1)} %get-tuple-element.56.refs_1_, f32[16,256,128]{2,1,0:T(8,128)S(1)} %broadcast_in_dim.4.refs_2_, ...), custom_call_target="tpu_custom_call", output_to_operand_aliasing={{0}: (10, {}), {1}: (11, {})} | custom-call | flops 1 | bytes 1 | tf_op jit(solution)/shard_map/amplitudes/pallas_call | solution.py:432
  157.8 6.8 %collective-permute-done.17.refs_7_ = bf16[8,256,128]{2,1,0:T(8,128)(2,1)S(1)} collective-permute-done((bf16[8,256,128]{2,1,0:T(8,128)(2,1)S(1)}, bf16[8,256,128]{2,1,0:T(8,128)(2,1)S(1)}, u32[]{:S(2)}, u32[]{:S(2)}) %collective-permute-start.17) | collective-permute-done | bytes 524320 | tf_op jit(solution)/shard_map/ppermute | solution.py:496
  164.6 7.1 %amplitudes.15 = (bf16[64,256,128]{2,1,0:T(8,128)(2,1)}, f32[64,128]{1,0:T(8,128)S(1)}) custom-call(s32[8,128]{1,0:T(8,128)S(1)} %get-tuple-element.55.refs_0_, f32[64,128]{1,0:T(8,128)S(1)} %get-tuple-element.56.refs_1_, f32[16,256,128]{2,1,0:T(8,128)S(1)} %broadcast_in_dim.4.refs_2_, ...), custom_call_target="tpu_custom_call", output_to_operand_aliasing={{0}: (8, {}), {1}: (9, {})} | custom-call | flops 1 | bytes 1 | tf_op jit(solution)/shard_map/amplitudes/pallas_call | solution.py:432
  171.7 5.2 %amplitudes.16 = (bf16[64,256,128]{2,1,0:T(8,128)(2,1)}, f32[64,128]{1,0:T(8,128)S(1)}) custom-call(s32[8,128]{1,0:T(8,128)S(1)} %get-tuple-element.55.refs_0_, f32[64,128]{1,0:T(8,128)S(1)} %get-tuple-element.56.refs_1_, f32[16,256,128]{2,1,0:T(8,128)S(1)} %broadcast_in_dim.4.refs_2_, ...), custom_call_target="tpu_custom_call", output_to_operand_aliasing={{0}: (9, {}), {1}: (10, {})} | custom-call | flops 1 | bytes 1 | tf_op jit(solution)/shard_map/amplitudes/pallas_call | solution.py:432
  177.0 1.8 pack.9
  178.8 1.5 collective-permute-start.21
  180.3 1.3 collective-permute-start.22
  181.6 2.0 amplitudes.17.refs_9_
  183.6 1.3 collective-permute-start.19
  184.9 13.3 %collective-permute-done.22.refs_8_ = bf16[8,256,128]{2,1,0:T(8,128)(2,1)} collective-permute-done((bf16[8,256,128]{2,1,0:T(8,128)(2,1)}, bf16[8,256,128]{2,1,0:T(8,128)(2,1)}, u32[]{:S(2)}, u32[]{:S(2)}) %collective-permute-start.22) | collective-permute-done | bytes 524320 | tf_op jit(solution)/shard_map/ppermute | solution.py:496
  198.3 1.0 copy-done.15
  199.3 6.0 %amplitudes.18 = (bf16[64,256,128]{2,1,0:T(8,128)(2,1)}, f32[64,128]{1,0:T(8,128)S(1)}) custom-call(s32[8,128]{1,0:T(8,128)S(1)} %get-tuple-element.55.refs_0_, f32[64,128]{1,0:T(8,128)S(1)} %get-tuple-element.56.refs_1_, f32[16,256,128]{2,1,0:T(8,128)S(1)} %broadcast_in_dim.4.refs_2_, ...), custom_call_target="tpu_custom_call", output_to_operand_aliasing={{0}: (10, {}), {1}: (11, {})} | custom-call | flops 1 | bytes 1 | tf_op jit(solution)/shard_map/amplitudes/pallas_call | solution.py:432
  205.3 1.6 collective-permute-done.19.refs_7_
  206.9 4.4 %amplitudes.19 = (bf16[64,256,128]{2,1,0:T(8,128)(2,1)}, f32[64,128]{1,0:T(8,128)S(1)}) custom-call(s32[8,128]{1,0:T(8,128)S(1)} %get-tuple-element.55.refs_0_, f32[64,128]{1,0:T(8,128)S(1)} %get-tuple-element.56.refs_1_, f32[16,256,128]{2,1,0:T(8,128)S(1)} %broadcast_in_dim.4.refs_2_, ...), custom_call_target="tpu_custom_call", output_to_operand_aliasing={{0}: (8, {}), {1}: (9, {})} | custom-call | flops 1 | bytes 1 | tf_op jit(solution)/shard_map/amplitudes/pallas_call | solution.py:432
  211.3 4.0 %density_rows.3 = f32[16,128,256]{2,1,0:T(8,128)S(1)} custom-call(s32[1]{0:T(128)} %bitcast.8.start, bf16[64,256,128]{2,1,0:T(8,128)(2,1)} %get-tuple-element.101.t), custom_call_target="tpu_custom_call" | custom-call | flops 1 | bytes 1 | tf_op jit(solution)/shard_map/density_rows/pallas_call | solution.py:470
  216.2 4.0 %density_rows.2 = f32[16,128,256]{2,1,0:T(8,128)S(1)} custom-call(s32[1]{0:T(128)} %bitcast.5.start, bf16[64,256,128]{2,1,0:T(8,128)(2,1)} %get-tuple-element.101.t), custom_call_target="tpu_custom_call" | custom-call | flops 1 | bytes 1 | tf_op jit(solution)/shard_map/density_rows/pallas_call | solution.py:470
  220.7 3.2 %add.17 = f32[16,128,256]{2,1,0:T(8,128)} add(f32[16,128,256]{2,1,0:T(8,128)S(1)} %density_rows.2, f32[16,128,256]{2,1,0:T(8,128)} %collective-permute-done.24) | non-fusion elementwise | flops 524288 | bytes 6291456 | tf_op jit(solution)/shard_map/add | solution.py:580
  (91 shorter events, 14.3 us)
Async XLA Ops:
  0.6 40.0 %collective-permute-start = (bf16[16,256,256]{2,1,0:T(8,128)(2,1)}, bf16[16,256,256]{2,1,0:T(8,128)(2,1)}, u32[]{:S(2)}, u32[]{:S(2)}) collective-permute-start(bf16[16,256,256]{2,1,0:T(8,128)(2,1)} %refs_0_.3), channel_id=1, source_target_pairs={{0,1},{1,0},{2,3},{3,2},{4,5},{5,4},{6,7},{7,6},{8,9},{9,8},{10,11... | collective-permute-start | bytes 6291464 | tf_op jit(solution)/shard_map/ppermute | solution.py:499
  1.1 0.7 copy-start.18
  39.9 26.4 %collective-permute-start.1 = (bf16[16,256,128]{2,1,0:T(8,128)(2,1)}, bf16[16,256,128]{2,1,0:T(8,128)(2,1)}, u32[]{:S(2)}, u32[]{:S(2)}) collective-permute-start(bf16[16,256,128]{2,1,0:T(8,128)(2,1)} %constant_dynamic-slice_fusion.1.refs_2_.refs_5_), channel_id=1, source_target_pairs={{0,4},{2,6},{4,0},{6,2},{8,12},{10,14},{12,8},{14,10},{1,5},{3,7},... | collective-permute-start | bytes 3145736 | tf_op jit(solution)/shard_map/ppermute | solution.py:496
  39.9 39.2 %collective-permute-start.6 = (bf16[16,256,128]{2,1,0:T(8,128)(2,1)}, bf16[16,256,128]{2,1,0:T(8,128)(2,1)S(1)}, u32[]{:S(2)}, u32[]{:S(2)}) collective-permute-start(bf16[16,256,128]{2,1,0:T(8,128)(2,1)} %constant_dynamic-slice_fusion.1.refs_2_.refs_5_), channel_id=1, source_target_pairs={{4,8},{6,10},{8,4},{10,6},{5,9},{7,11},{9,5},{11,7},{20,24},{22,26... | collective-permute-start | bytes 3145736 | tf_op jit(solution)/shard_map/ppermute | solution.py:496
  43.0 47.2 %collective-permute-start.3 = (bf16[16,256,128]{2,1,0:T(8,128)(2,1)}, bf16[16,256,128]{2,1,0:T(8,128)(2,1)}, u32[]{:S(2)}, u32[]{:S(2)}) collective-permute-start(bf16[16,256,128]{2,1,0:T(8,128)(2,1)} %constant_dynamic-slice_fusion.refs_3_.refs_6_), channel_id=1, source_target_pairs={{0,4},{2,6},{4,0},{6,2},{8,12},{10,14},{12,8},{14,10},{1,5},{3,7},... | collective-permute-start | bytes 3145736 | tf_op jit(solution)/shard_map/ppermute | solution.py:496
  49.6 32.8 %collective-permute-start.5 = (bf16[8,256,128]{2,1,0:T(8,128)(2,1)S(1)}, bf16[8,256,128]{2,1,0:T(8,128)(2,1)S(1)}, u32[]{:S(2)}, u32[]{:S(2)}) collective-permute-start(bf16[8,256,128]{2,1,0:T(8,128)(2,1)S(1)} %get-tuple-element.62.refs_7_), channel_id=1, source_target_pairs={{0,2},{2,0},{4,6},{6,4},{8,10},{10,8},{12,14},{14,12},{1,3},{3,1},... | collective-permute-start | bytes 1572872 | tf_op jit(solution)/shard_map/ppermute | solution.py:496
  53.7 19.5 %copy-start.19 = (f32[16,256]{1,0:T(8,128)S(1)}, f32[16,256]{1,0:T(8,128)}, u32[]{:S(2)}) copy-start(f32[16,256]{1,0:T(8,128)} %refs_0_.2) | copy-start | bytes 49156
  53.7 28.7 %collective-permute-start.4 = (bf16[8,256,128]{2,1,0:T(8,128)(2,1)S(1)}, bf16[8,256,128]{2,1,0:T(8,128)(2,1)S(1)}, u32[]{:S(2)}, u32[]{:S(2)}) collective-permute-start(bf16[8,256,128]{2,1,0:T(8,128)(2,1)S(1)} %get-tuple-element.66), channel_id=1, source_target_pairs={{0,2},{2,0},{4,6},{6,4},{8,10},{10,8},{12,14},{14,12},{1,3},{3,1},... | collective-permute-start | bytes 1572872 | tf_op jit(solution)/shard_map/ppermute | solution.py:496
  66.3 25.6 %collective-permute-start.11 = (bf16[16,256,128]{2,1,0:T(8,128)(2,1)}, bf16[16,256,128]{2,1,0:T(8,128)(2,1)S(1)}, u32[]{:S(2)}, u32[]{:S(2)}) collective-permute-start(bf16[16,256,128]{2,1,0:T(8,128)(2,1)} %constant_dynamic-slice_fusion.refs_3_.refs_6_), channel_id=1, source_target_pairs={{4,8},{6,10},{8,4},{10,6},{5,9},{7,11},{9,5},{11,7},{20,24},{22,26... | collective-permute-start | bytes 3145736 | tf_op jit(solution)/shard_map/ppermute | solution.py:496
  70.5 1.3 copy-start
  71.9 1.4 copy-start.3
  79.1 3.3 %copy-start.1 = (bf16[16,256,256]{2,1,0:T(8,128)(2,1)S(1)}, bf16[16,256,256]{2,1,0:T(8,128)(2,1)}, u32[]{:S(2)}) copy-start(bf16[16,256,256]{2,1,0:T(8,128)(2,1)} %copy-done) | copy-start | bytes 6291460
  79.1 11.0 %copy-start.6 = (bf16[16,256,128]{2,1,0:T(8,128)(2,1)}, bf16[16,256,128]{2,1,0:T(8,128)(2,1)S(1)}, u32[]{:S(2)}) copy-start(bf16[16,256,128]{2,1,0:T(8,128)(2,1)S(1)} %collective-permute-done.6.refs_3_.refs_4_.refs_7_.refs_5_) | copy-start | bytes 3145732
  79.2 21.8 %collective-permute-start.8 = (bf16[16,256,128]{2,1,0:T(8,128)(2,1)}, bf16[16,256,128]{2,1,0:T(8,128)(2,1)}, u32[]{:S(2)}, u32[]{:S(2)}) collective-permute-start(bf16[16,256,128]{2,1,0:T(8,128)(2,1)} %collective-permute-done.1.refs_2_.refs_0_.refs_5_), channel_id=1, source_target_pairs={{0,1},{1,0},{2,3},{3,2},{4,5},{5,4},{6,7},{7,6},{8,9},{9,8},{10,11... | collective-permute-start | bytes 3145736 | tf_op jit(solution)/shard_map/ppermute | solution.py:499
  90.2 12.1 %collective-permute-start.9 = (bf16[16,256,128]{2,1,0:T(8,128)(2,1)}, bf16[16,256,128]{2,1,0:T(8,128)(2,1)}, u32[]{:S(2)}, u32[]{:S(2)}) collective-permute-start(bf16[16,256,128]{2,1,0:T(8,128)(2,1)} %collective-permute-done.3.refs_1_.refs_2_.refs_6_), channel_id=1, source_target_pairs={{0,1},{1,0},{2,3},{3,2},{4,5},{5,4},{6,7},{7,6},{8,9},{9,8},{10,11... | collective-permute-start | bytes 3145736 | tf_op jit(solution)/shard_map/ppermute | solution.py:499
  90.5 8.2 %collective-permute-start.10 = (bf16[8,256,128]{2,1,0:T(8,128)(2,1)S(1)}, bf16[8,256,128]{2,1,0:T(8,128)(2,1)S(1)}, u32[]{:S(2)}, u32[]{:S(2)}) collective-permute-start(bf16[8,256,128]{2,1,0:T(8,128)(2,1)S(1)} %get-tuple-element.79), channel_id=1, source_target_pairs={{4,6},{6,4},{8,10},{10,8},{5,7},{7,5},{9,11},{11,9},{20,22},{22,20... | collective-permute-start | bytes 1572872 | tf_op jit(solution)/shard_map/ppermute | solution.py:496
  91.2 51.9 %collective-permute-start.2 = (bf16[16,256,128]{2,1,0:T(8,128)(2,1)}, bf16[16,256,128]{2,1,0:T(8,128)(2,1)S(1)}, u32[]{:S(2)}, u32[]{:S(2)}) collective-permute-start(bf16[16,256,128]{2,1,0:T(8,128)(2,1)} %collective-permute-done.1.refs_2_.refs_0_.refs_5_), channel_id=1, source_target_pairs={{4,8},{6,10},{8,4},{10,6},{5,9},{7,11},{9,5},{11,7},{20,24},{22,26... | collective-permute-start | bytes 3145736 | tf_op jit(solution)/shard_map/ppermute | solution.py:496
  91.9 21.4 %collective-permute-start.13 = (bf16[8,256,128]{2,1,0:T(8,128)(2,1)}, bf16[8,256,128]{2,1,0:T(8,128)(2,1)}, u32[]{:S(2)}, u32[]{:S(2)}) collective-permute-start(bf16[8,256,128]{2,1,0:T(8,128)(2,1)} %get-tuple-element.82), channel_id=1, source_target_pairs={{4,2},{6,0},{8,14},{10,12},{5,3},{7,1},{9,15},{11,13},{20,18},{22,... | collective-permute-start | bytes 1572872 | tf_op jit(solution)/shard_map/ppermute | solution.py:496
  96.0 1.0 copy-start.8
  97.0 0.9 copy-start.16
  97.9 0.8 copy-start.26
  98.7 0.8 copy-start.12
  99.5 36.3 %collective-permute-start.15 = (bf16[8,256,128]{2,1,0:T(8,128)(2,1)}, bf16[8,256,128]{2,1,0:T(8,128)(2,1)}, u32[]{:S(2)}, u32[]{:S(2)}) collective-permute-start(bf16[8,256,128]{2,1,0:T(8,128)(2,1)} %get-tuple-element.68.refs_7_), channel_id=1, source_target_pairs={{0,2},{2,0},{4,6},{6,4},{8,10},{10,8},{12,14},{14,12},{1,3},{3,1},... | collective-permute-start | bytes 1572872 | tf_op jit(solution)/shard_map/ppermute | solution.py:496
  101.0 35.5 %collective-permute-start.14 = (bf16[8,256,128]{2,1,0:T(8,128)(2,1)}, bf16[8,256,128]{2,1,0:T(8,128)(2,1)}, u32[]{:S(2)}, u32[]{:S(2)}) collective-permute-start(bf16[8,256,128]{2,1,0:T(8,128)(2,1)} %get-tuple-element.83), channel_id=1, source_target_pairs={{4,2},{6,0},{8,14},{10,12},{5,3},{7,1},{9,15},{11,13},{20,18},{22,... | collective-permute-start | bytes 1572872 | tf_op jit(solution)/shard_map/ppermute | solution.py:496
  102.3 74.7 %collective-permute-start.7 = (bf16[16,256,128]{2,1,0:T(8,128)(2,1)}, bf16[16,256,128]{2,1,0:T(8,128)(2,1)}, u32[]{:S(2)}, u32[]{:S(2)}) collective-permute-start(bf16[16,256,128]{2,1,0:T(8,128)(2,1)} %collective-permute-done.3.refs_1_.refs_2_.refs_6_), channel_id=1, source_target_pairs={{4,8},{6,10},{8,4},{10,6},{5,9},{7,11},{9,5},{11,7},{20,24},{22,26... | collective-permute-start | bytes 3145736 | tf_op jit(solution)/shard_map/ppermute | solution.py:496
  103.9 9.4 %copy-start.17 = (bf16[8,256,128]{2,1,0:T(8,128)(2,1)S(1)}, bf16[8,256,128]{2,1,0:T(8,128)(2,1)}, u32[]{:S(2)}) copy-start(bf16[8,256,128]{2,1,0:T(8,128)(2,1)} %copy-done.16) | copy-start | bytes 1572868
  107.5 9.6 %copy-start.10 = (bf16[16,128,256]{2,1,0:T(8,128)(2,1)}, bf16[16,128,256]{2,1,0:T(8,128)(2,1)S(1)}, u32[]{:S(2)}) copy-start(bf16[16,128,256]{2,1,0:T(8,128)(2,1)S(1)} %get-tuple-element.78.refs_6_) | copy-start | bytes 3145732
  107.5 9.6 %copy-start.13 = (bf16[8,256,128]{2,1,0:T(8,128)(2,1)S(1)}, bf16[8,256,128]{2,1,0:T(8,128)(2,1)}, u32[]{:S(2)}) copy-start(bf16[8,256,128]{2,1,0:T(8,128)(2,1)} %copy-done.12) | copy-start | bytes 1572868
  113.4 44.4 %collective-permute-start.16 = (bf16[8,256,128]{2,1,0:T(8,128)(2,1)S(1)}, bf16[8,256,128]{2,1,0:T(8,128)(2,1)S(1)}, u32[]{:S(2)}, u32[]{:S(2)}) collective-permute-start(bf16[8,256,128]{2,1,0:T(8,128)(2,1)S(1)} %copy-done.17), channel_id=1, source_target_pairs={{0,2},{2,0},{4,6},{6,4},{8,10},{10,8},{12,14},{14,12},{1,3},{3,1},... | collective-permute-start | bytes 1572872 | tf_op jit(solution)/shard_map/ppermute | solution.py:496
  117.1 18.7 %copy-start.27 = (bf16[8,256,128]{2,1,0:T(8,128)(2,1)S(1)}, bf16[8,256,128]{2,1,0:T(8,128)(2,1)}, u32[]{:S(2)}) copy-start(bf16[8,256,128]{2,1,0:T(8,128)(2,1)} %copy-done.26) | copy-start | bytes 1572868
  135.8 10.2 %collective-permute-start.12 = (bf16[8,256,128]{2,1,0:T(8,128)(2,1)S(1)}, bf16[8,256,128]{2,1,0:T(8,128)(2,1)S(1)}, u32[]{:S(2)}, u32[]{:S(2)}) collective-permute-start(bf16[8,256,128]{2,1,0:T(8,128)(2,1)S(1)} %copy-done.27), channel_id=1, source_target_pairs={{4,6},{6,4},{8,10},{10,8},{5,7},{7,5},{9,11},{11,9},{20,22},{22,20... | collective-permute-start | bytes 1572872 | tf_op jit(solution)/shard_map/ppermute | solution.py:496
  136.5 16.7 %collective-permute-start.18 = (bf16[8,256,128]{2,1,0:T(8,128)(2,1)S(1)}, bf16[8,256,128]{2,1,0:T(8,128)(2,1)S(1)}, u32[]{:S(2)}, u32[]{:S(2)}) collective-permute-start(bf16[8,256,128]{2,1,0:T(8,128)(2,1)S(1)} %amplitudes.12.refs_7_), channel_id=1, source_target_pairs={{4,0},{6,2},{8,12},{10,14},{5,1},{7,3},{9,13},{11,15},{20,16},{22,... | collective-permute-start | bytes 1572872 | tf_op jit(solution)/shard_map/ppermute | solution.py:496
  143.0 10.1 %copy-start.7 = (bf16[16,256,128]{2,1,0:T(8,128)(2,1)S(1)}, bf16[16,256,128]{2,1,0:T(8,128)(2,1)}, u32[]{:S(2)}) copy-start(bf16[16,256,128]{2,1,0:T(8,128)(2,1)} %copy-done.6) | copy-start | bytes 3145732
  143.0 10.1 %copy-start.9 = (bf16[16,256,128]{2,1,0:T(8,128)(2,1)S(1)}, bf16[16,256,128]{2,1,0:T(8,128)(2,1)}, u32[]{:S(2)}) copy-start(bf16[16,256,128]{2,1,0:T(8,128)(2,1)} %copy-done.8) | copy-start | bytes 3145732
  143.1 14.7 %copy-start.4 = (bf16[16,256,128]{2,1,0:T(8,128)(2,1)}, bf16[16,256,128]{2,1,0:T(8,128)(2,1)S(1)}, u32[]{:S(2)}) copy-start(bf16[16,256,128]{2,1,0:T(8,128)(2,1)S(1)} %collective-permute-done.2.refs_2_.refs_3_.refs_7_.refs_5_) | copy-start | bytes 3145732
  144.7 19.9 %collective-permute-start.17 = (bf16[8,256,128]{2,1,0:T(8,128)(2,1)S(1)}, bf16[8,256,128]{2,1,0:T(8,128)(2,1)S(1)}, u32[]{:S(2)}, u32[]{:S(2)}) collective-permute-start(bf16[8,256,128]{2,1,0:T(8,128)(2,1)S(1)} %get-tuple-element.87.refs_8_), channel_id=1, source_target_pairs={{4,2},{6,0},{8,14},{10,12},{5,3},{7,1},{9,15},{11,13},{20,18},{22,... | collective-permute-start | bytes 1572872 | tf_op jit(solution)/shard_map/ppermute | solution.py:496
  146.0 38.9 %collective-permute-start.20 = (bf16[8,256,128]{2,1,0:T(8,128)(2,1)}, bf16[8,256,128]{2,1,0:T(8,128)(2,1)}, u32[]{:S(2)}, u32[]{:S(2)}) collective-permute-start(bf16[8,256,128]{2,1,0:T(8,128)(2,1)} %get-tuple-element.95), channel_id=1, source_target_pairs={{4,6},{6,4},{8,10},{10,8},{5,7},{7,5},{9,11},{11,9},{20,22},{22,20... | collective-permute-start | bytes 1572872 | tf_op jit(solution)/shard_map/ppermute | solution.py:496
  153.2 11.4 %copy-start.2 = (bf16[16,256,256]{2,1,0:T(8,128)(2,1)S(1)}, bf16[16,256,256]{2,1,0:T(8,128)(2,1)}, u32[]{:S(2)}) copy-start(bf16[16,256,256]{2,1,0:T(8,128)(2,1)} %copy-done) | copy-start | bytes 6291460
  164.6 7.1 %copy-start.14 = (bf16[8,256,128]{2,1,0:T(8,128)(2,1)}, bf16[8,256,128]{2,1,0:T(8,128)(2,1)S(1)}, u32[]{:S(2)}) copy-start(bf16[8,256,128]{2,1,0:T(8,128)(2,1)S(1)} %collective-permute-done.17.refs_7_) | copy-start | bytes 1572868
  177.0 4.6 %copy-start.11 = (bf16[16,128,256]{2,1,0:T(8,128)(2,1)S(1)}, bf16[16,128,256]{2,1,0:T(8,128)(2,1)}, u32[]{:S(2)}) copy-start(bf16[16,128,256]{2,1,0:T(8,128)(2,1)} %copy-done.10) | copy-start | bytes 3145732
  178.8 6.1 %collective-permute-start.21 = (bf16[8,256,128]{2,1,0:T(8,128)(2,1)}, bf16[8,256,128]{2,1,0:T(8,128)(2,1)}, u32[]{:S(2)}, u32[]{:S(2)}) collective-permute-start(bf16[8,256,128]{2,1,0:T(8,128)(2,1)} %get-tuple-element.96), channel_id=1, source_target_pairs={{4,6},{6,4},{8,10},{10,8},{5,7},{7,5},{9,11},{11,9},{20,22},{22,20... | collective-permute-start | bytes 1572872 | tf_op jit(solution)/shard_map/ppermute | solution.py:496
  180.3 18.0 %collective-permute-start.22 = (bf16[8,256,128]{2,1,0:T(8,128)(2,1)}, bf16[8,256,128]{2,1,0:T(8,128)(2,1)}, u32[]{:S(2)}, u32[]{:S(2)}) collective-permute-start(bf16[8,256,128]{2,1,0:T(8,128)(2,1)} %get-tuple-element.94.refs_9_), channel_id=1, source_target_pairs={{4,2},{6,0},{8,14},{10,12},{5,3},{7,1},{9,15},{11,13},{20,18},{22,... | collective-permute-start | bytes 1572872 | tf_op jit(solution)/shard_map/ppermute | solution.py:496
  183.6 23.3 %collective-permute-start.19 = (bf16[8,256,128]{2,1,0:T(8,128)(2,1)}, bf16[8,256,128]{2,1,0:T(8,128)(2,1)S(1)}, u32[]{:S(2)}, u32[]{:S(2)}) collective-permute-start(bf16[8,256,128]{2,1,0:T(8,128)(2,1)} %amplitudes.17.refs_9_), channel_id=1, source_target_pairs={{4,0},{6,2},{8,12},{10,14},{5,1},{7,3},{9,13},{11,15},{20,16},{22,... | collective-permute-start | bytes 1572872 | tf_op jit(solution)/shard_map/ppermute | solution.py:496
  198.3 1.0 copy-start.15
  199.3 7.6 %copy-start.5 = (bf16[16,256,128]{2,1,0:T(8,128)(2,1)S(1)}, bf16[16,256,128]{2,1,0:T(8,128)(2,1)}, u32[]{:S(2)}) copy-start(bf16[16,256,128]{2,1,0:T(8,128)(2,1)} %copy-done.4) | copy-start | bytes 3145732
  211.3 4.2 %copy-start.21 = (f32[64,64]{1,0:T(8,128)S(1)}, f32[64,64]{1,0:T(8,128)}, u32[]{:S(2)}) copy-start(f32[64,64]{1,0:T(8,128)} %copy-done.20) | copy-start | bytes 49156
  215.3 5.4 %collective-permute-start.24 = (f32[16,128,256]{2,1,0:T(8,128)S(1)}, f32[16,128,256]{2,1,0:T(8,128)}, u32[]{:S(2)}, u32[]{:S(2)}) collective-permute-start(f32[16,128,256]{2,1,0:T(8,128)S(1)} %density_rows.3), channel_id=1, source_target_pairs={{0,1},{1,0},{2,3},{3,2},{4,5},{5,4},{6,7},{7,6},{8,9},{9,8},{10,11... | collective-permute-start | bytes 6291464 | tf_op jit(solution)/shard_map/ppermute | solution.py:499
  215.6 4.6 %collective-permute-start.23 = (f32[64]{0:T(128)S(1)}, f32[64]{0:T(128)S(1)}, u32[]{:S(2)}, u32[]{:S(2)}) collective-permute-start(f32[64]{0:T(128)S(1)} %multiply_reduce_fusion), channel_id=1, source_target_pairs={{0,1},{1,0},{2,3},{3,2},{4,5},{5,4},{6,7},{7,6},{8,9},{9,8},{10,11... | collective-permute-start | bytes 776 | tf_op jit(solution)/shard_map/ppermute | solution.py:499
  (5 other events, 3.2 us)

commit v8 on v7

--- a/solution.py
+++ b/solution.py
@@ -167,8 +167,9 @@
     )
 
 
-def tables_kernel(cap, per_orb, meta, every, *outs):
-    count, nvd = every.shape[1] - 8, every.shape[2] - 128
+def tables_kernel(cap, per_orb, meta, *refs):
+    smalls, outs = refs[:8], refs[8:]
+    count, nvd = smalls[0].shape[0] - 8, smalls[0].shape[1] - 128
     n = 8 * cap
     me, col0 = meta[0], meta[1]
     z, y = me // 2, me % 2
@@ -180,12 +181,12 @@
     head_row = jnp.zeros((1, 128), i32)
     for k, value in enumerate(head + [middle, col0]):
         head_row = jnp.where(lane == k, value, head_row)
-    orbitals = jnp.concatenate([every[d, :count, :] for d in range(8)], axis=0)
+    orbitals = jnp.concatenate([x[:count, :] for x in smalls], axis=0)
     columns = jnp.where(col0 == 0, orbitals[:, : nvd // 2], orbitals[:, nvd // 2 : nvd])
     extra = orbitals[:, nvd:]
 
     def build(x, tbl, rows=None):
-        packet = every[me ^ x]
+        packet = smalls[x]
         order = packet[count : count + 1, :n].astype(i32)
         slots = packet[count : count + 1, 128 : 128 + n].astype(i32)
         tbl[...] = jnp.zeros_like(tbl)
@@ -196,7 +197,7 @@
         tbl[ORDER : ORDER + 1, :n] = order
         pair = lax.broadcasted_iota(i32, (1, n), 1)
         owner = sum(jnp.where(pair >= k * cap, 1, 0) for k in range(1, 8))
-        index = owner * count + slots
+        index = (owner ^ me) * count + slots
         theirs = jnp.where(lax.broadcasted_iota(i32, (8 * count, n), 0) == index, 1.0, 0.0)
         first = sum(jnp.where(order >= k * per_orb, 1, 0) for k in range(1, count))
         mine = jnp.where(lax.broadcasted_iota(i32, (count, n), 0) == first, 1.0, 0.0)
@@ -211,18 +212,18 @@
     build(3, outs[5])
 
 
-def tables_of(meta, every, cap, per_orb, half):
+def tables_of(meta, smalls, cap, per_orb, half):
     table = jax.ShapeDtypeStruct((8, 128), i32)
     rows = jax.ShapeDtypeStruct((8 * cap, half), f32)
     return pl.pallas_call(
         lambda *refs: tables_kernel(cap, per_orb, *refs),
         out_shape=(table, rows, table, rows, table, table),
-        in_specs=[SMEM, VMEM],
+        in_specs=[SMEM] + [VMEM] * 8,
         out_specs=[VMEM] * 6,
         compiler_params=PARAMS,
         cost_estimate=TINY,
         name="tables",
-    )(meta, every)
+    )(meta, *smalls)
 
 
 def pack_kernel(jobs, tables, after, *refs):
@@ -234,11 +235,15 @@
         for k, (table, call, middle) in enumerate(jobs):
             if middle == only_middle:
                 base = tbls[table][HEAD, call]
-                for r in range(outs[k].shape[0]):
+                halves, cap = outs[k].shape[:2]
+                for r in range(cap):
                     slot = tbls[table][SLOT, base + r]
-                    made.append(
-                        pltpu.make_async_copy(sources[k].at[slot], outs[k].at[r], sems.at[k, r])
-                    )
+                    made += [
+                        pltpu.make_async_copy(
+                            sources[k].at[q, slot], outs[k].at[q, r], sems.at[k, q, r]
+                        )
+                        for q in range(halves)
+                    ]
         return made
 
     everywhere = copies(False)
@@ -259,14 +264,15 @@
 
 def pack(tbls, jobs, cap, after=()):
     sources = [source for _, _, source, _ in jobs]
-    shape = jax.ShapeDtypeStruct((cap,) + sources[0].shape[1:], bf16)
+    halves, _, *block = sources[0].shape
+    shape = jax.ShapeDtypeStruct((halves, cap, *block), bf16)
     kinds = [(table, call, middle) for table, call, _, middle in jobs]
     return pl.pallas_call(
         lambda *refs: pack_kernel(kinds, len(tbls), len(after), *refs),
         out_shape=[shape] * len(jobs),
         in_specs=[SMEM] * len(tbls) + [HBM] * (len(jobs) + len(after)),
         out_specs=[VMEM] * len(jobs),
-        scratch_shapes=[pltpu.SemaphoreType.DMA((len(jobs), cap))],
+        scratch_shapes=[pltpu.SemaphoreType.DMA((len(jobs), halves, cap))],
         compiler_params=PARAMS,
         cost_estimate=TINY,
         name="pack",
@@ -282,7 +288,7 @@
 
 def turn(arrays):
     count, rows, cols = arrays[0].shape
-    step = 4 if count % 4 == 0 else 1
+    step = count // 4
     n = len(arrays)
     return pl.pallas_call(
         turn_kernel,
@@ -296,18 +302,19 @@
     )(*arrays)
 
 
-def amplitudes_kernel(mode, call, per_orb, first, tbl, rows, vcol, *refs):
+def amplitudes_kernel(mode, call, per_orb, groups, tbl, rows, vcol, *refs):
     sv, s0, s1, b0, b1, st, se, sem, sem_out = refs[-9:]
     client = mode == "client"
-    elsewhere = None
     if client:
         tout = refs[-10]
-        left, js = refs[:4], refs[4:6]
+        left, rest = refs[:1], refs[1:]
     else:
         tout, eout = refs[-11:-9]
-        left, js = refs[:2], refs[2:5]
-    if mode == "asked_two":
-        js, elsewhere = refs[2:4], refs[4:6]
+        left, rest = refs[:2], refs[2:]
+    places = []
+    for arrays in groups:
+        places.append([rest[0].at[0], rest[arrays - 1].at[2 - arrays]])
+        rest = rest[arrays:]
     cap = sv.shape[0]
     nvd, half = sv.shape[1], sv.shape[2]
     base = tbl[HEAD, call]
@@ -322,25 +329,24 @@
         for copy in copies:
             copy.wait()
 
-    def load(js=js):
+    def load(js):
         copies = []
         for r in range(cap):
             i = lax.div(place(r), per_orb)
-            slot = r if mode.startswith("asked") else tbl[SLOT, base + r]
+            slot = r if mode == "asked" else tbl[SLOT, base + r]
             todo = [
                 (vcol.at[i], sv.at[r]),
                 (js[0].at[slot], b0.at[r]),
                 (js[1].at[slot], b1.at[r]),
             ]
             if client:
-                here = pl.ds(pl.multiple_of(tbl[HEAD, COLUMN], half), half)
-                there = pl.ds(pl.multiple_of(half - tbl[HEAD, COLUMN], half), half)
-                todo += [
-                    (left[0].at[i], s0.at[r, here, :]),
-                    (left[1].at[i], s1.at[r, here, :]),
-                    (left[2].at[i], s1.at[r, there, :]),
-                    (left[3].at[i], s0.at[r, there, :]),
-                ]
+                core = lax.div(tbl[HEAD, COLUMN], half)
+                for c, swapped in ((0, core), (1, 1 - core)):
+                    rows_c = pl.ds(c * half, half)
+                    todo += [
+                        (left[0].at[2 * c + swapped, i], s0.at[r, rows_c, :]),
+                        (left[0].at[2 * c + 1 - swapped, i], s1.at[r, rows_c, :]),
+                    ]
             else:
                 todo += [(left[0].at[i], s0.at[r]), (left[1].at[i], s1.at[r])]
             copies += [
@@ -367,7 +373,7 @@
                 se[r : r + 1, :] = jnp.sum(k * t.astype(f32), axis=0, keepdims=True)
 
     def take():
-        ready = js[2]
+        ready = rest[0]
         copies = [pltpu.make_async_copy(ready.at[r], st.at[r], sem.at[r, 0]) for r in range(cap)]
         copies += [
             pltpu.make_async_copy(vcol.at[lax.div(place(r), per_orb)], sv.at[r], sem.at[r, 1])
@@ -382,7 +388,7 @@
 
         @pl.when(middle)
         def _():
-            load()
+            load(places[0])
             make()
             tout[...] = st[...]
 
@@ -391,16 +397,16 @@
 
         @pl.when(middle)
         def _():
-            load()
+            load(places[0])
             make()
 
         pl.when(jnp.logical_not(middle))(take)
-    elif elsewhere is not None:
-        pl.when(middle)(load)
-        pl.when(jnp.logical_not(middle))(lambda: load(elsewhere))
+    elif len(places) == 2:
+        pl.when(middle)(lambda: load(places[0]))
+        pl.when(jnp.logical_not(middle))(lambda: load(places[1]))
         make()
     else:
-        load()
+        load(places[0])
         make()
     run(
         [pltpu.make_async_copy(st.at[r], tout.at[place(r)], sem_out.at[r]) for r in range(cap)]
@@ -412,10 +418,11 @@
     )
 
 
-def amplitudes(mode, call, per_orb, tables, left, sources, cap, held=(), after=()):
+def amplitudes(mode, call, per_orb, tables, left, groups, cap, held=(), after=()):
     tbl, rows, vcol = tables
     occ, nvd, half = vcol.shape
-    qa = left[0].shape[2]
+    qa = left[0].shape[-1]
+    sources = [x for group in groups for x in group]
     client = mode == "client"
     operands = (tbl, rows, vcol, *left, *sources, *after)
     aliases = {len(operands) + k: k for k in range(len(held))}
@@ -430,7 +437,7 @@
         )
         out_specs = (HBM, HBM)
     return pl.pallas_call(
-        lambda *refs: amplitudes_kernel(mode, call, per_orb, not held, *refs),
+        lambda *refs: amplitudes_kernel(mode, call, per_orb, [len(g) for g in groups], *refs),
         out_shape=out_shape,
         in_specs=[SMEM, VMEM] + [HBM] * (len(operands) - 2),
         out_specs=out_specs,
@@ -507,74 +514,63 @@
     y_middle = [(2, 3), (3, 2), (4, 5), (5, 4)]
 
     small, hit = lists(vir_energy, occ_energy, domain_size, partner_owner, partner_slot, cap)
-    every = lax.all_gather(small, "orb")
+    smalls = [small] + [pp(small, flip(bits)) for bits in range(1, peers)]
 
     other = swap_core(blocks)
-    own = [lax.dynamic_slice_in_dim(x, col0, half, 2) for x in (blocks, other)]
-    sent, every = lax.optimization_barrier((own[0], every))
-    near = [pp(x, flip(2)) for x in (sent, own[1])]
-    mid = [pp(x, cross) for x in (sent, own[1])]
+    own = jnp.stack([lax.dynamic_slice_in_dim(x, col0, half, 2) for x in (blocks, other)])
+    sent, smalls = lax.optimization_barrier((own, smalls))
+    near, mid = pp(sent, flip(2)), pp(sent, cross)
+
     tbl, rows, client_tbl, client_rows, beside_list, relay_list = tables_of(
-        jnp.stack([me, col0]), every, cap, per_orb, half
+        jnp.stack([me, col0]), smalls, cap, per_orb, half
     )
 
     def spread(vir):
         return jnp.broadcast_to(vir[:, :, None], (occ, nvd, half))
 
     tables = (tbl, rows, spread(vir_energy))
-    client_vir = lax.dynamic_index_in_dim(every, me ^ 2, 0, keepdims=False)[:occ, :nvd]
-    client = (client_tbl, client_rows, spread(client_vir))
+    client = (client_tbl, client_rows, spread(smalls[2][:occ, :nvd]))
     lists_of = [beside_list, relay_list]
 
-    def own_pairs(k, mode, sources, held=(), after=()):
-        return amplitudes(mode, k, per_orb, tables, left, sources, cap, held, after)
-
-    packed = pack(lists_of, [(0, 0, x, False) for x in own], cap)
-    beside = [pp(x, flip(1)) for x in packed]
+    def own_pairs(k, mode, groups, held=(), after=()):
+        return amplitudes(mode, k, per_orb, tables, left, groups, cap, held, after)
+
+    (packed,) = pack(lists_of, [(0, 0, own, False)], cap)
+    beside = pp(packed, flip(1))
     left = turn([blocks, other])
-    held = own_pairs(0, "slots", own, after=(packed[1],))
-
-    def send_on(x, y, token):
-        jobs = [(0, 1, x, False), (1, 2, y, True), (0, 2, y, True)]
-        packed = pack(lists_of, jobs, cap, after=(token,))
-        perms = (flip(1), diagonal, y_middle)
-        return packed[0], [pp(part, perm) for part, perm in zip(packed, perms)]
-
-    first, held = lax.optimization_barrier((near[0], held))
-    far = [pp(first, cross)]
-    across = [swap_core(first)]
-    packed, sent_first = send_on(first, mid[0], held[1])
-    held = own_pairs(4, "asked", beside, held, (packed,))
-    second, held = lax.optimization_barrier((near[1], held))
-    far.append(pp(second, cross))
-    across.append(swap_core(second))
-    near = [first, second]
-    packed, sent_second = send_on(second, mid[1], held[1])
-    beside_near, third_diagonal, third = zip(sent_first, sent_second)
-    client_left = turn(near + across)
+    held = own_pairs(0, "slots", [[own]], after=(packed,))
+    held = own_pairs(4, "asked", [[beside]], held)
+    near, held = lax.optimization_barrier((near, held))
+    far = [pp(near[q : q + 1], cross) for q in range(2)]
+    columns = lax.all_gather(near, "aux").reshape(4 * occ, qa, half)
+    (packed,) = pack(lists_of, [(0, 1, near, False)], cap, after=(held[1],))
+    beside_near = pp(packed, flip(1))
+    packed = pack(lists_of, [(1, 2, mid, True), (0, 2, mid, True)], cap, after=(packed,))
+    third_diagonal = pp(packed[0], diagonal)
+    third = pp(packed[1], y_middle)
+    client_left = [x.reshape(4, occ, half, qa) for x in turn([columns])]
     gone = amplitudes(
-        "client", 2, per_orb, client, client_left, mid, cap, after=(packed, third_diagonal[0], third[0])
+        "client", 2, per_orb, client, client_left, [[mid]], cap, after=(packed[0],)
     )
     ready_2 = pp(gone, outward)
-    held = own_pairs(1, "slots", near, held, (gone, third_diagonal[1], beside_near[0]))
+    held = own_pairs(1, "slots", [[near]], held, (gone, third_diagonal))
     fourth_diagonal, fourth = [], []
 
     def send_far(q, token):
-        jobs = [(1, 3, far[q], True), (0, 3, far[q], True)]
-        packed = pack(lists_of, jobs, cap, after=(token,))
+        packed = pack(lists_of, [(1, 3, far[q], True), (0, 3, far[q], True)], cap, after=(token,))
         fourth_diagonal.append(pp(packed[0], diagonal))
         fourth.append(pp(packed[1], y_middle))
         return packed[0]
 
     packed = send_far(0, held[1])
-    held = own_pairs(2, "served", mid + [ready_2], held, (packed, third[1]))
-    held = own_pairs(5, "asked", beside_near, held, (fourth_diagonal[0],))
-    held = own_pairs(6, "asked_two", third + third_diagonal, held)
+    held = own_pairs(2, "served", [[mid]], held, (ready_2, packed))
+    held = own_pairs(5, "asked", [[beside_near]], held)
+    held = own_pairs(6, "asked", [[third], [third_diagonal]], held, (fourth_diagonal[0],))
     packed = send_far(1, held[1])
-    gone = amplitudes("client", 3, per_orb, client, client_left, far, cap, after=(packed,))
+    gone = amplitudes("client", 3, per_orb, client, client_left, [far], cap, after=(packed,))
     ready_3 = pp(gone, outward)
-    held = own_pairs(7, "asked_two", fourth + fourth_diagonal, held, (gone,))
-    t_all, e_all = own_pairs(3, "served", far + [ready_3], held)
+    held = own_pairs(7, "asked", [fourth, fourth_diagonal], held, (gone,))
+    t_all, e_all = own_pairs(3, "served", [far], held, (ready_3,))
 
     away = swap_core(density_rows(t_all, (1 - core) * half, per_orb, half))
     density = density_rows(t_all, core * half, per_orb, half) + away

time: 225 us -> 244 us (1.084)
  waiting for transfers between devices: 63.3 us -> 100 us
  blocking collectives: 32.2 us -> 0 us
  between operations: 1.21 us -> 14.5 us
  local copies, waits for them, and re-layouts: 18.4 us -> 14.8 us
    ppermute x20 -> x21, waiting for transfers between devices: 63.3 us -> 100 us  [pp(): return lax.ppermute(x, 'orb', perm)]
    all_gather x1 -> x0, blocking collectives: 32.2 us -> none  [line_plan(): every = lax.all_gather(small, 'orb')]
    dynamic_slice x2 -> x0, local copies, waits for them, and re-layouts: 4.63 us -> none  [line_plan(): own = [lax.dynamic_slice_in_dim(x, col0, half, 2) for x in (blocks, other)]]
    slice x1 -> x2, local copies, waits for them, and re-layouts: 0.01 us -> 3.42 us  [the longest x1 3.42 us: line_plan(): far = [pp(near[q:q + 1], cross) for q in range(2)]]
    unnamed x56 -> x30, local copies, waits for them, and re-layouts: 11.2 us -> 8.66 us
    ppermute x20 -> x21, starting transfers between devices: 26.5 us -> 28.7 us  [pp(): return lax.ppermute(x, 'orb', perm)]
  transfers between devices with their start and end apart: 25 -> 25, of which waited for: 7 -> 7; matrix products, arithmetic and copies ran while one was open for 4% -> 3% of each run, Pallas kernels for 30% -> 29%
where the time goes in v8:
time: 244 us; the launch traced here: 242 us
  waiting for transfers between devices  100 us (41%)
  Pallas kernels  76.9 us (32%)
  starting transfers between devices  29.8 us (12%)
  local copies, waits for them, and re-layouts  14.8 us (6%)
  between operations  14.5 us (6%)
  other arithmetic  5.48 us (2%)
    ppermute x21, waiting for transfers between devices, pp(): return lax.ppermute(x, 'orb', perm)  100 us
    pallas_call x10, Pallas kernels, amplitudes(): pl.pallas_call(lambda *refs: amplitudes_kernel(mode, call, per_orb, [len(...  49.6 us
    ppermute x21, starting transfers between devices, pp(): return lax.ppermute(x, 'orb', perm)  28.7 us
    pallas_call x5, Pallas kernels, pack(): pl.pallas_call(lambda *refs: pack_kernel(kinds, len(tbls), len(after), *r...  10.8 us
    unnamed x30, local copies, waits for them, and re-layouts  8.66 us
    pallas_call x2, Pallas kernels, density_rows(): pl.pallas_call(density_kernel, out_shape=jax.ShapeDtypeStruct((occ, half,...  8 us
    pallas_call x2, Pallas kernels, turn(): pl.pallas_call(turn_kernel, out_shape=[jax.ShapeDtypeStruct((count, cols,...  7.01 us
  transfers between devices with their start and end apart: 25, of which 7 were waited for; matrix products, arithmetic and copies ran while one was open for 3% of the time, Pallas kernels for 29%

profile of v8, /device:TPU:0, one launch (start us, length us, event | category | flops | bytes accessed | tf_op | source)
XLA Modules:
  0.0 242.0 jit_solution(3075096875820044680)
XLA Ops:
  11.3 5.6 %collective-permute-start.7 = (f32[24,384]{1,0:T(8,128)S(1)}, f32[24,384]{1,0:T(8,128)S(1)}, u32[]{:S(2)}, u32[]{:S(2)}) collective-permute-start(f32[24,384]{1,0:T(8,128)S(1)} %get-tuple-element.48.refs_1_), channel_id=1, source_target_pairs={{0,14},{2,12},{4,10},{6,8},{8,6},{10,4},{12,2},{14,0},{1,15},{3,13... | collective-permute-start | bytes 110600 | tf_op jit(solution)/shard_map/ppermute | solution.py:503
  17.9 2.0 collective-permute-start.4
  20.0 1.3 dynamic-slice_bitcast_fusion.1
  21.3 2.4 collective-permute-start.3
  23.8 0.8 collective-permute-start.2
  25.1 1.5 pad_maximum_fusion.refs_2_.refs_5_
  26.6 1.3 collective-permute-done.2.refs_3_
  28.7 1.2 collective-permute-start.8
  30.0 1.3 tables.1
  31.3 2.1 pack.5.refs_6_
  34.0 3.5 %turn.2 = (bf16[16,256,256]{2,1,0:T(8,128)(2,1)S(1)}, bf16[16,256,256]{2,1,0:T(8,128)(2,1)S(1)}) custom-call(bf16[16,256,256]{2,1,0:T(8,128)(2,1)} %refs_0_.3, bf16[16,256,256]{2,1,0:T(8,128)(2,1)} %copy-done.14), custom_call_target="tpu_custom_call" | custom-call | flops 1 | bytes 1 | tf_op jit(solution)/shard_map/turn/pallas_call | solution.py:293
  37.5 1.3 copy-done.2
  39.4 6.4 %amplitudes.10 = (bf16[64,256,128]{2,1,0:T(8,128)(2,1)}, f32[64,128]{1,0:T(8,128)S(1)}) custom-call(s32[8,128]{1,0:T(8,128)S(1)} %get-tuple-element.56.refs_0_, f32[64,128]{1,0:T(8,128)S(1)} %get-tuple-element.57.refs_1_, f32[16,256,128]{2,1,0:T(8,128)S(1)} %broadcast_in_dim.4.refs_2_, bf16[16,256,256]{2,1,0:T(8,128)(2,1)S(1)} %get-tuple-element.58.refs_3_, ...), custom_call_target="tpu_custom_call" | custom-call | flops 1 | bytes 1 | tf_op jit(solution)/shard_map/amplitudes/pallas_call | solution.py:439
  45.8 10.3 %collective-permute-done.9.refs_5_ = bf16[2,8,256,128]{3,2,1,0:T(8,128)(2,1)S(1)} collective-permute-done((bf16[2,8,256,128]{3,2,1,0:T(8,128)(2,1)S(1)}, bf16[2,8,256,128]{3,2,1,0:T(8,128)(2,1)S(1)}, u32[]{:S(2)}, u32[]{:S(2)}) %collective-permute-start.9) | collective-permute-done | bytes 1048608 | tf_op jit(solution)/shard_map/ppermute | solution.py:503
  56.1 7.7 %amplitudes.11 = (bf16[64,256,128]{2,1,0:T(8,128)(2,1)}, f32[64,128]{1,0:T(8,128)S(1)}) custom-call(s32[8,128]{1,0:T(8,128)S(1)} %get-tuple-element.56.refs_0_, f32[64,128]{1,0:T(8,128)S(1)} %get-tuple-element.57.refs_1_, f32[16,256,128]{2,1,0:T(8,128)S(1)} %broadcast_in_dim.4.refs_2_, ...), custom_call_target="tpu_custom_call", output_to_operand_aliasing={{0}: (6, {}), {1}: (7, {})} | custom-call | flops 1 | bytes 1 | tf_op jit(solution)/shard_map/amplitudes/pallas_call | solution.py:439
  63.9 10.7 %collective-permute-done.8.refs_2_.refs_5_ = bf16[2,16,256,128]{3,2,1,0:T(8,128)(2,1)} collective-permute-done((bf16[2,16,256,128]{3,2,1,0:T(8,128)(2,1)}, bf16[2,16,256,128]{3,2,1,0:T(8,128)(2,1)}, u32[]{:S(2)}, u32[]{:S(2)}) %collective-permute-start.8) | collective-permute-done | bytes 2097184 | tf_op jit(solution)/shard_map/ppermute | solution.py:503
  75.3 3.0 %pack.6.refs_4_ = bf16[2,8,256,128]{3,2,1,0:T(8,128)(2,1)} custom-call(s32[8,128]{1,0:T(8,128)S(1)} %get-tuple-element.61.refs_0_, s32[8,128]{1,0:T(8,128)S(1)} %get-tuple-element.62.refs_1_, bf16[2,16,256,128]{3,2,1,0:T(8,128)(2,1)} %collective-permute-done.8.refs_2_.refs_5_, f32[64,128]{1,0:T(8,128)S(1)} %get-tuple-element.70.refs_3_.refs_9_), custom_call_target="tpu_custom_call" | custom-call | flops 1 | bytes 1 | tf_op jit(solution)/shard_map/pack/pallas_call | solution.py:270
  78.4 2.3 pack.7
  80.7 1.3 collective-permute-start.14
  82.0 3.4 %fusion = (bf16[1,16,256,128]{3,2,1,0:T(8,128)(2,1)}, bf16[1,16,256,128]{3,2,1,0:T(8,128)(2,1)}) fusion(bf16[2,16,256,128]{3,2,1,0:T(8,128)(2,1)} %collective-permute-done.8.refs_2_.refs_5_), kind=kLoop, calls=%fused_computation.6 | loop fusion | bytes 4194304 | tf_op jit(solution)/shard_map/slice | solution.py:544
  86.5 1.6 collective-permute-start.13
  88.1 1.7 collective-permute-start.11
  89.8 3.5 %turn.3 = bf16[64,128,256]{2,1,0:T(8,128)(2,1)S(1)} custom-call(bf16[64,256,128]{2,1,0:T(8,128)(2,1)} %bitcast.19), custom_call_target="tpu_custom_call" | custom-call | flops 1 | bytes 1 | tf_op jit(solution)/shard_map/turn/pallas_call | solution.py:293
  93.4 2.0 copy-done.3
  95.9 1.0 copy-done.5
  96.9 1.2 amplitudes.12.refs_6_
  98.1 50.7 %collective-permute-done.14.refs_7_.refs_6_ = bf16[2,8,256,128]{3,2,1,0:T(8,128)(2,1)} collective-permute-done((bf16[2,8,256,128]{3,2,1,0:T(8,128)(2,1)}, bf16[2,8,256,128]{3,2,1,0:T(8,128)(2,1)}, u32[]{:S(2)}, u32[]{:S(2)}) %collective-permute-start.14) | collective-permute-done | bytes 1048608 | tf_op jit(solution)/shard_map/ppermute | solution.py:503
  148.8 1.3 collective-permute-start.17
  150.1 6.4 %amplitudes.13 = (bf16[64,256,128]{2,1,0:T(8,128)(2,1)}, f32[64,128]{1,0:T(8,128)S(1)}) custom-call(s32[8,128]{1,0:T(8,128)S(1)} %get-tuple-element.56.refs_0_, f32[64,128]{1,0:T(8,128)S(1)} %get-tuple-element.57.refs_1_, f32[16,256,128]{2,1,0:T(8,128)S(1)} %broadcast_in_dim.4.refs_2_, ...), custom_call_target="tpu_custom_call", output_to_operand_aliasing={{0}: (8, {}), {1}: (9, {})} | custom-call | flops 1 | bytes 1 | tf_op jit(solution)/shard_map/amplitudes/pallas_call | solution.py:439
  156.5 1.6 pack.8
  158.2 1.3 collective-permute-start.15
  159.5 6.2 %collective-permute-done.17.refs_6_ = bf16[8,256,128]{2,1,0:T(8,128)(2,1)S(1)} collective-permute-done((bf16[8,256,128]{2,1,0:T(8,128)(2,1)S(1)}, bf16[8,256,128]{2,1,0:T(8,128)(2,1)S(1)}, u32[]{:S(2)}, u32[]{:S(2)}) %collective-permute-start.17) | collective-permute-done | bytes 524320 | tf_op jit(solution)/shard_map/ppermute | solution.py:503
  165.7 1.4 collective-permute-start.19
  167.1 4.6 %amplitudes.14 = (bf16[64,256,128]{2,1,0:T(8,128)(2,1)}, f32[64,128]{1,0:T(8,128)S(1)}) custom-call(s32[8,128]{1,0:T(8,128)S(1)} %get-tuple-element.56.refs_0_, f32[64,128]{1,0:T(8,128)S(1)} %get-tuple-element.57.refs_1_, f32[16,256,128]{2,1,0:T(8,128)S(1)} %broadcast_in_dim.4.refs_2_, ...), custom_call_target="tpu_custom_call", output_to_operand_aliasing={{0}: (8, {}), {1}: (9, {})} | custom-call | flops 1 | bytes 1 | tf_op jit(solution)/shard_map/amplitudes/pallas_call | solution.py:439
  171.7 6.4 %amplitudes.15 = (bf16[64,256,128]{2,1,0:T(8,128)(2,1)}, f32[64,128]{1,0:T(8,128)S(1)}) custom-call(s32[8,128]{1,0:T(8,128)S(1)} %get-tuple-element.56.refs_0_, f32[64,128]{1,0:T(8,128)S(1)} %get-tuple-element.57.refs_1_, f32[16,256,128]{2,1,0:T(8,128)S(1)} %broadcast_in_dim.4.refs_2_, ...), custom_call_target="tpu_custom_call", output_to_operand_aliasing={{0}: (6, {}), {1}: (7, {})} | custom-call | flops 1 | bytes 1 | tf_op jit(solution)/shard_map/amplitudes/pallas_call | solution.py:439
  178.2 5.2 %amplitudes.16 = (bf16[64,256,128]{2,1,0:T(8,128)(2,1)}, f32[64,128]{1,0:T(8,128)S(1)}) custom-call(s32[8,128]{1,0:T(8,128)S(1)} %get-tuple-element.56.refs_0_, f32[64,128]{1,0:T(8,128)S(1)} %get-tuple-element.57.refs_1_, f32[16,256,128]{2,1,0:T(8,128)S(1)} %broadcast_in_dim.4.refs_2_, ...), custom_call_target="tpu_custom_call", output_to_operand_aliasing={{0}: (8, {}), {1}: (9, {})} | custom-call | flops 1 | bytes 1 | tf_op jit(solution)/shard_map/amplitudes/pallas_call | solution.py:439
  183.4 1.9 pack.9
  185.3 1.5 collective-permute-start.20
  186.8 1.3 collective-permute-start.21
  188.1 2.0 amplitudes.17.refs_9_
  190.1 1.3 collective-permute-start.18
  191.4 20.5 %collective-permute-done.21.refs_8_ = bf16[1,8,256,128]{3,2,1,0:T(8,128)(2,1)} collective-permute-done((bf16[1,8,256,128]{3,2,1,0:T(8,128)(2,1)}, bf16[1,8,256,128]{3,2,1,0:T(8,128)(2,1)}, u32[]{:S(2)}, u32[]{:S(2)}) %collective-permute-start.21) | collective-permute-done | bytes 524320 | tf_op jit(solution)/shard_map/ppermute | solution.py:503
  211.9 1.0 copy-done.7
  212.9 6.0 %amplitudes.18 = (bf16[64,256,128]{2,1,0:T(8,128)(2,1)}, f32[64,128]{1,0:T(8,128)S(1)}) custom-call(s32[8,128]{1,0:T(8,128)S(1)} %get-tuple-element.56.refs_0_, f32[64,128]{1,0:T(8,128)S(1)} %get-tuple-element.57.refs_1_, f32[16,256,128]{2,1,0:T(8,128)S(1)} %broadcast_in_dim.4.refs_2_, ...), custom_call_target="tpu_custom_call", output_to_operand_aliasing={{0}: (10, {}), {1}: (11, {})} | custom-call | flops 1 | bytes 1 | tf_op jit(solution)/shard_map/amplitudes/pallas_call | solution.py:439
  218.9 3.6 %amplitudes.19 = (bf16[64,256,128]{2,1,0:T(8,128)(2,1)}, f32[64,128]{1,0:T(8,128)S(1)}) custom-call(s32[8,128]{1,0:T(8,128)S(1)} %get-tuple-element.56.refs_0_, f32[64,128]{1,0:T(8,128)S(1)} %get-tuple-element.57.refs_1_, f32[16,256,128]{2,1,0:T(8,128)S(1)} %broadcast_in_dim.4.refs_2_, ...), custom_call_target="tpu_custom_call", output_to_operand_aliasing={{0}: (8, {}), {1}: (9, {})} | custom-call | flops 1 | bytes 1 | tf_op jit(solution)/shard_map/amplitudes/pallas_call | solution.py:439
  222.5 4.0 %density_rows.3 = f32[16,128,256]{2,1,0:T(8,128)S(1)} custom-call(s32[1]{0:T(128)} %bitcast.10.start, bf16[64,256,128]{2,1,0:T(8,128)(2,1)} %get-tuple-element.89.t), custom_call_target="tpu_custom_call" | custom-call | flops 1 | bytes 1 | tf_op jit(solution)/shard_map/density_rows/pallas_call | solution.py:477
  227.4 4.0 %density_rows.2 = f32[16,128,256]{2,1,0:T(8,128)S(1)} custom-call(s32[1]{0:T(128)} %bitcast.5.start, bf16[64,256,128]{2,1,0:T(8,128)(2,1)} %get-tuple-element.89.t), custom_call_target="tpu_custom_call" | custom-call | flops 1 | bytes 1 | tf_op jit(solution)/shard_map/density_rows/pallas_call | solution.py:477
  231.9 3.2 %add.12 = f32[16,128,256]{2,1,0:T(8,128)} add(f32[16,128,256]{2,1,0:T(8,128)S(1)} %density_rows.2, f32[16,128,256]{2,1,0:T(8,128)} %collective-permute-done.23) | non-fusion elementwise | flops 524288 | bytes 6291456 | tf_op jit(solution)/shard_map/add | solution.py:576
  (66 shorter events, 11.7 us)
Async XLA Ops:
  7.2 82.6 %all-gather.3.cloned.1.call-start = ((), (), s32[]{:S(2)}) async-start(), calls=%async_computation | async-start | bytes 6291456 | tf_op jit(solution)/shard_map/all_gather | solution.py:545
  7.2 14.1 %collective-permute-start = (bf16[16,256,256]{2,1,0:T(8,128)(2,1)}, bf16[16,256,256]{2,1,0:T(8,128)(2,1)S(1)}, u32[]{:S(2)}, u32[]{:S(2)}) collective-permute-start(bf16[16,256,256]{2,1,0:T(8,128)(2,1)} %refs_0_.3), channel_id=1, source_target_pairs={{0,1},{1,0},{2,3},{3,2},{4,5},{5,4},{6,7},{7,6},{8,9},{9,8},{10,11... | collective-permute-start | bytes 6291464 | tf_op jit(solution)/shard_map/ppermute | solution.py:506
  7.7 0.7 copy-start.8
  8.4 0.7 copy-start.10
  9.1 0.7 copy-start.11
  9.8 0.7 copy-start.12
  10.4 0.7 copy-start.13
  11.3 12.5 %collective-permute-start.7 = (f32[24,384]{1,0:T(8,128)S(1)}, f32[24,384]{1,0:T(8,128)S(1)}, u32[]{:S(2)}, u32[]{:S(2)}) collective-permute-start(f32[24,384]{1,0:T(8,128)S(1)} %get-tuple-element.48.refs_1_), channel_id=1, source_target_pairs={{0,14},{2,12},{4,10},{6,8},{8,6},{10,4},{12,2},{14,0},{1,15},{3,13... | collective-permute-start | bytes 110600 | tf_op jit(solution)/shard_map/ppermute | solution.py:503
  17.0 7.7 %collective-permute-start.6 = (f32[24,384]{1,0:T(8,128)S(1)}, f32[24,384]{1,0:T(8,128)S(1)}, u32[]{:S(2)}, u32[]{:S(2)}) collective-permute-start(f32[24,384]{1,0:T(8,128)S(1)} %get-tuple-element.48.refs_1_), channel_id=1, source_target_pairs={{0,12},{2,14},{4,8},{6,10},{8,4},{10,6},{12,0},{14,2},{1,13},{3,15... | collective-permute-start | bytes 110600 | tf_op jit(solution)/shard_map/ppermute | solution.py:503
  17.2 9.4 %collective-permute-start.5 = (f32[24,384]{1,0:T(8,128)S(1)}, f32[24,384]{1,0:T(8,128)S(1)}, u32[]{:S(2)}, u32[]{:S(2)}) collective-permute-start(f32[24,384]{1,0:T(8,128)S(1)} %get-tuple-element.48.refs_1_), channel_id=1, source_target_pairs={{0,10},{2,8},{4,14},{6,12},{8,2},{10,0},{12,6},{14,4},{1,11},{3,9}... | collective-permute-start | bytes 110600 | tf_op jit(solution)/shard_map/ppermute | solution.py:503
  17.9 8.7 %collective-permute-start.4 = (f32[24,384]{1,0:T(8,128)S(1)}, f32[24,384]{1,0:T(8,128)S(1)}, u32[]{:S(2)}, u32[]{:S(2)}) collective-permute-start(f32[24,384]{1,0:T(8,128)S(1)} %get-tuple-element.48.refs_1_), channel_id=1, source_target_pairs={{0,8},{2,10},{4,12},{6,14},{8,0},{10,2},{12,4},{14,6},{1,9},{3,11}... | collective-permute-start | bytes 110600 | tf_op jit(solution)/shard_map/ppermute | solution.py:503
  21.3 3.4 %copy-start.14 = (bf16[16,256,256]{2,1,0:T(8,128)(2,1)}, bf16[16,256,256]{2,1,0:T(8,128)(2,1)S(1)}, u32[]{:S(2)}) copy-start(bf16[16,256,256]{2,1,0:T(8,128)(2,1)S(1)} %collective-permute-done.refs_1_) | copy-start | bytes 6291460
  21.3 5.3 %collective-permute-start.3 = (f32[24,384]{1,0:T(8,128)S(1)}, f32[24,384]{1,0:T(8,128)S(1)}, u32[]{:S(2)}, u32[]{:S(2)}) collective-permute-start(f32[24,384]{1,0:T(8,128)S(1)} %get-tuple-element.48.refs_1_), channel_id=1, source_target_pairs={{0,6},{2,4},{4,2},{6,0},{8,14},{10,12},{12,10},{14,8},{1,7},{3,5},... | collective-permute-start | bytes 110600 | tf_op jit(solution)/shard_map/ppermute | solution.py:503
  23.8 4.0 %collective-permute-start.2 = (f32[24,384]{1,0:T(8,128)S(1)}, f32[24,384]{1,0:T(8,128)S(1)}, u32[]{:S(2)}, u32[]{:S(2)}) collective-permute-start(f32[24,384]{1,0:T(8,128)S(1)} %get-tuple-element.48.refs_1_), channel_id=1, source_target_pairs={{0,4},{2,6},{4,0},{6,2},{8,12},{10,14},{12,8},{14,10},{1,5},{3,7},... | collective-permute-start | bytes 110600 | tf_op jit(solution)/shard_map/ppermute | solution.py:503
  24.7 4.0 %collective-permute-start.1 = (f32[24,384]{1,0:T(8,128)S(1)}, f32[24,384]{1,0:T(8,128)S(1)}, u32[]{:S(2)}, u32[]{:S(2)}) collective-permute-start(f32[24,384]{1,0:T(8,128)S(1)} %get-tuple-element.48.refs_1_), channel_id=1, source_target_pairs={{0,2},{2,0},{4,6},{6,4},{8,10},{10,8},{12,14},{14,12},{1,3},{3,1},... | collective-permute-start | bytes 110600 | tf_op jit(solution)/shard_map/ppermute | solution.py:503
  28.7 45.9 %collective-permute-start.8 = (bf16[2,16,256,128]{3,2,1,0:T(8,128)(2,1)}, bf16[2,16,256,128]{3,2,1,0:T(8,128)(2,1)}, u32[]{:S(2)}, u32[]{:S(2)}) collective-permute-start(bf16[2,16,256,128]{3,2,1,0:T(8,128)(2,1)} %pad_maximum_fusion.refs_2_.refs_5_), channel_id=1, source_target_pairs={{0,4},{2,6},{4,0},{6,2},{8,12},{10,14},{12,8},{14,10},{1,5},{3,7},... | collective-permute-start | bytes 6291464 | tf_op jit(solution)/shard_map/ppermute | solution.py:503
  33.3 5.4 %copy-start.9 = (f32[16,256]{1,0:T(8,128)S(1)}, f32[16,256]{1,0:T(8,128)}, u32[]{:S(2)}) copy-start(f32[16,256]{1,0:T(8,128)} %refs_0_.2) | copy-start | bytes 49156
  33.3 22.8 %collective-permute-start.9 = (bf16[2,8,256,128]{3,2,1,0:T(8,128)(2,1)S(1)}, bf16[2,8,256,128]{3,2,1,0:T(8,128)(2,1)S(1)}, u32[]{:S(2)}, u32[]{:S(2)}) collective-permute-start(bf16[2,8,256,128]{3,2,1,0:T(8,128)(2,1)S(1)} %pack.5.refs_6_), channel_id=1, source_target_pairs={{0,2},{2,0},{4,6},{6,4},{8,10},{10,8},{12,14},{14,12},{1,3},{3,1},... | collective-permute-start | bytes 3145736 | tf_op jit(solution)/shard_map/ppermute | solution.py:503
  37.4 1.3 copy-start.2
  38.8 17.4 %copy-start = (bf16[16,256,256]{2,1,0:T(8,128)(2,1)}, bf16[16,256,256]{2,1,0:T(8,128)(2,1)S(1)}, u32[]{:S(2)}) copy-start(bf16[16,256,256]{2,1,0:T(8,128)(2,1)S(1)} %get-tuple-element.58.refs_3_) | copy-start | bytes 6291460
  74.5 3.9 %collective-permute-start.12 = (bf16[2,16,256,128]{3,2,1,0:T(8,128)(2,1)}, bf16[2,16,256,128]{3,2,1,0:T(8,128)(2,1)S(1)}, u32[]{:S(2)}, u32[]{:S(2)}) collective-permute-start(bf16[2,16,256,128]{3,2,1,0:T(8,128)(2,1)} %pad_maximum_fusion.refs_2_.refs_5_), channel_id=1, source_target_pairs={{4,8},{6,10},{8,4},{10,6},{5,9},{7,11},{9,5},{11,7},{20,24},{22,26... | collective-permute-start | bytes 6291464 | tf_op jit(solution)/shard_map/ppermute | solution.py:503
  78.4 2.3 copy-start.4
  80.7 68.1 %collective-permute-start.14 = (bf16[2,8,256,128]{3,2,1,0:T(8,128)(2,1)}, bf16[2,8,256,128]{3,2,1,0:T(8,128)(2,1)}, u32[]{:S(2)}, u32[]{:S(2)}) collective-permute-start(bf16[2,8,256,128]{3,2,1,0:T(8,128)(2,1)} %get-tuple-element.72.refs_5_), channel_id=1, source_target_pairs={{4,2},{6,0},{8,14},{10,12},{5,3},{7,1},{9,15},{11,13},{20,18},{22,... | collective-permute-start | bytes 3145736 | tf_op jit(solution)/shard_map/ppermute | solution.py:503
  85.4 71.1 %collective-permute-start.10 = (bf16[1,16,256,128]{3,2,1,0:T(8,128)(2,1)}, bf16[1,16,256,128]{3,2,1,0:T(8,128)(2,1)S(1)}, u32[]{:S(2)}, u32[]{:S(2)}) collective-permute-start(bf16[1,16,256,128]{3,2,1,0:T(8,128)(2,1)} %get-tuple-element.91), channel_id=1, source_target_pairs={{4,8},{6,10},{8,4},{10,6},{5,9},{7,11},{9,5},{11,7},{20,24},{22,26... | collective-permute-start | bytes 3145736 | tf_op jit(solution)/shard_map/ppermute | solution.py:503
  86.1 85.6 %collective-permute-start.16 = (bf16[2,8,256,128]{3,2,1,0:T(8,128)(2,1)}, bf16[2,8,256,128]{3,2,1,0:T(8,128)(2,1)}, u32[]{:S(2)}, u32[]{:S(2)}) collective-permute-start(bf16[2,8,256,128]{3,2,1,0:T(8,128)(2,1)} %pack.6.refs_4_), channel_id=1, source_target_pairs={{0,2},{2,0},{4,6},{6,4},{8,10},{10,8},{12,14},{14,12},{1,3},{3,1},... | collective-permute-start | bytes 3145736 | tf_op jit(solution)/shard_map/ppermute | solution.py:503
  86.5 91.6 %collective-permute-start.13 = (bf16[2,8,256,128]{3,2,1,0:T(8,128)(2,1)}, bf16[2,8,256,128]{3,2,1,0:T(8,128)(2,1)}, u32[]{:S(2)}, u32[]{:S(2)}) collective-permute-start(bf16[2,8,256,128]{3,2,1,0:T(8,128)(2,1)} %get-tuple-element.71), channel_id=1, source_target_pairs={{4,6},{6,4},{8,10},{10,8},{5,7},{7,5},{9,11},{11,9},{20,22},{22,20... | collective-permute-start | bytes 3145736 | tf_op jit(solution)/shard_map/ppermute | solution.py:503
  88.1 95.3 %collective-permute-start.11 = (bf16[1,16,256,128]{3,2,1,0:T(8,128)(2,1)}, bf16[1,16,256,128]{3,2,1,0:T(8,128)(2,1)}, u32[]{:S(2)}, u32[]{:S(2)}) collective-permute-start(bf16[1,16,256,128]{3,2,1,0:T(8,128)(2,1)} %get-tuple-element.90), channel_id=1, source_target_pairs={{4,8},{6,10},{8,4},{10,6},{5,9},{7,11},{9,5},{11,7},{20,24},{22,26... | collective-permute-start | bytes 3145736 | tf_op jit(solution)/shard_map/ppermute | solution.py:503
  93.3 2.0 copy-start.3
  95.3 1.6 copy-start.5
  96.9 53.2 %copy-start.1 = (bf16[16,256,256]{2,1,0:T(8,128)(2,1)S(1)}, bf16[16,256,256]{2,1,0:T(8,128)(2,1)}, u32[]{:S(2)}) copy-start(bf16[16,256,256]{2,1,0:T(8,128)(2,1)} %copy-done) | copy-start | bytes 6291460
  148.8 16.8 %collective-permute-start.17 = (bf16[8,256,128]{2,1,0:T(8,128)(2,1)S(1)}, bf16[8,256,128]{2,1,0:T(8,128)(2,1)S(1)}, u32[]{:S(2)}, u32[]{:S(2)}) collective-permute-start(bf16[8,256,128]{2,1,0:T(8,128)(2,1)S(1)} %amplitudes.12.refs_6_), channel_id=1, source_target_pairs={{4,0},{6,2},{8,12},{10,14},{5,1},{7,3},{9,13},{11,15},{20,16},{22,... | collective-permute-start | bytes 1572872 | tf_op jit(solution)/shard_map/ppermute | solution.py:503
  158.2 20.0 %collective-permute-start.15 = (bf16[1,8,256,128]{3,2,1,0:T(8,128)(2,1)S(1)}, bf16[1,8,256,128]{3,2,1,0:T(8,128)(2,1)S(1)}, u32[]{:S(2)}, u32[]{:S(2)}) collective-permute-start(bf16[1,8,256,128]{3,2,1,0:T(8,128)(2,1)S(1)} %get-tuple-element.75.refs_7_), channel_id=1, source_target_pairs={{4,2},{6,0},{8,14},{10,12},{5,3},{7,1},{9,15},{11,13},{20,18},{22,... | collective-permute-start | bytes 1572872 | tf_op jit(solution)/shard_map/ppermute | solution.py:503
  165.7 25.7 %collective-permute-start.19 = (bf16[1,8,256,128]{3,2,1,0:T(8,128)(2,1)}, bf16[1,8,256,128]{3,2,1,0:T(8,128)(2,1)}, u32[]{:S(2)}, u32[]{:S(2)}) collective-permute-start(bf16[1,8,256,128]{3,2,1,0:T(8,128)(2,1)} %get-tuple-element.83), channel_id=1, source_target_pairs={{4,6},{6,4},{8,10},{10,8},{5,7},{7,5},{9,11},{11,9},{20,22},{22,20... | collective-permute-start | bytes 1572872 | tf_op jit(solution)/shard_map/ppermute | solution.py:503
  178.2 5.3 %copy-start.6 = (bf16[1,8,256,128]{3,2,1,0:T(8,128)(2,1)}, bf16[1,8,256,128]{3,2,1,0:T(8,128)(2,1)S(1)}, u32[]{:S(2)}) copy-start(bf16[1,8,256,128]{3,2,1,0:T(8,128)(2,1)S(1)} %collective-permute-done.15.refs_7_) | copy-start | bytes 1572868
  185.3 6.1 %collective-permute-start.20 = (bf16[1,8,256,128]{3,2,1,0:T(8,128)(2,1)}, bf16[1,8,256,128]{3,2,1,0:T(8,128)(2,1)}, u32[]{:S(2)}, u32[]{:S(2)}) collective-permute-start(bf16[1,8,256,128]{3,2,1,0:T(8,128)(2,1)} %get-tuple-element.84), channel_id=1, source_target_pairs={{4,6},{6,4},{8,10},{10,8},{5,7},{7,5},{9,11},{11,9},{20,22},{22,20... | collective-permute-start | bytes 1572872 | tf_op jit(solution)/shard_map/ppermute | solution.py:503
  186.8 25.1 %collective-permute-start.21 = (bf16[1,8,256,128]{3,2,1,0:T(8,128)(2,1)}, bf16[1,8,256,128]{3,2,1,0:T(8,128)(2,1)}, u32[]{:S(2)}, u32[]{:S(2)}) collective-permute-start(bf16[1,8,256,128]{3,2,1,0:T(8,128)(2,1)} %get-tuple-element.82.refs_6_), channel_id=1, source_target_pairs={{4,2},{6,0},{8,14},{10,12},{5,3},{7,1},{9,15},{11,13},{20,18},{22,... | collective-permute-start | bytes 1572872 | tf_op jit(solution)/shard_map/ppermute | solution.py:503
  190.1 28.9 %collective-permute-start.18 = (bf16[8,256,128]{2,1,0:T(8,128)(2,1)}, bf16[8,256,128]{2,1,0:T(8,128)(2,1)}, u32[]{:S(2)}, u32[]{:S(2)}) collective-permute-start(bf16[8,256,128]{2,1,0:T(8,128)(2,1)} %amplitudes.17.refs_9_), channel_id=1, source_target_pairs={{4,0},{6,2},{8,12},{10,14},{5,1},{7,3},{9,13},{11,15},{20,16},{22,... | collective-permute-start | bytes 1572872 | tf_op jit(solution)/shard_map/ppermute | solution.py:503
  211.9 1.0 copy-start.7
  226.5 5.4 %collective-permute-start.23 = (f32[16,128,256]{2,1,0:T(8,128)S(1)}, f32[16,128,256]{2,1,0:T(8,128)}, u32[]{:S(2)}, u32[]{:S(2)}) collective-permute-start(f32[16,128,256]{2,1,0:T(8,128)S(1)} %density_rows.3), channel_id=1, source_target_pairs={{0,1},{1,0},{2,3},{3,2},{4,5},{5,4},{6,7},{7,6},{8,9},{9,8},{10,11... | collective-permute-start | bytes 6291464 | tf_op jit(solution)/shard_map/ppermute | solution.py:506
  226.9 4.6 %collective-permute-start.22 = (f32[64]{0:T(128)S(1)}, f32[64]{0:T(128)S(1)}, u32[]{:S(2)}, u32[]{:S(2)}) collective-permute-start(f32[64]{0:T(128)S(1)} %multiply_reduce_fusion), channel_id=1, source_target_pairs={{0,1},{1,0},{2,3},{3,2},{4,5},{5,4},{6,7},{7,6},{8,9},{9,8},{10,11... | collective-permute-start | bytes 776 | tf_op jit(solution)/shard_map/ppermute | solution.py:506
Sparse Core Ops, SparseCore 0:
  74.7 14.0 all-gather.2

commit v9 on v6

--- a/solution.py
+++ b/solution.py
@@ -9,7 +9,7 @@
 HBM = pl.BlockSpec(memory_space=pltpu.HBM)
 SMEM = pl.BlockSpec(memory_space=pltpu.SMEM)
 VMEM = pl.BlockSpec(memory_space=pltpu.VMEM)
-LIMIT = 48 * 1024 * 1024
+LIMIT = 24 * 1024 * 1024
 
 
 def slot_ranks(owner):
@@ -206,28 +206,16 @@
     )(meta, *smalls)
 
 
-def pack_kernel(call, only_middle, relayed, after, tbl, *refs):
-    out, sems = refs[-2:]
+def pack_kernel(call, only_middle, relayed, tbl, *refs):
+    out = refs[-1]
     halves, cap = out.shape[:2]
     base = tbl[HEAD, call]
     middle = tbl[HEAD, MIDDLE] == 1
 
-    def run(copies):
-        for copy in copies:
-            copy.start()
-        for copy in copies:
-            copy.wait()
-
     def gather():
-        run(
-            [
-                pltpu.make_async_copy(
-                    refs[q].at[tbl[SLOT, base + r]], out.at[q, r], sems.at[q, r]
-                )
-                for q in range(halves)
-                for r in range(cap)
-            ]
-        )
+        for q in range(halves):
+            for r in range(cap):
+                out[q, r] = refs[q][tbl[SLOT, base + r]]
 
     if not only_middle and not relayed:
         gather()
@@ -237,28 +225,23 @@
 
         @pl.when(jnp.logical_not(middle))
         def _():
-            run(
-                [
-                    pltpu.make_async_copy(refs[halves + q].at[0], out.at[q], sems.at[q, 0])
-                    for q in range(halves)
-                ]
-            )
+            for q in range(halves):
+                out[q] = refs[halves + q][0]
 
 
 def pack(tbl, call, sources, cap, only_middle=False, relayed=None, after=()):
     halves = len(sources)
     shape = (halves, cap) + sources[0].shape[1:]
-    operands = (*sources, *(relayed or ()), *after)
+    operands = (*sources, *(relayed or ()))
     return pl.pallas_call(
-        lambda *refs: pack_kernel(call, only_middle, relayed is not None, len(after), *refs),
+        lambda *refs: pack_kernel(call, only_middle, relayed is not None, *refs),
         out_shape=jax.ShapeDtypeStruct(shape, bf16),
-        in_specs=[SMEM] + [HBM] * len(operands),
+        in_specs=[SMEM] + [VMEM] * len(operands) + [HBM] * len(after),
         out_specs=VMEM,
-        scratch_shapes=[pltpu.SemaphoreType.DMA((halves, cap))],
         compiler_params=PARAMS,
         cost_estimate=TINY,
         name="pack",
-    )(tbl, *operands)
+    )(tbl, *operands, *after)
 
 
 def turn_kernel(*refs):
@@ -284,132 +267,93 @@
     )(*arrays)
 
 
-def amplitudes_kernel(mode, call, per_orb, first, tbl, rows, vcol, *refs):
-    sv, s0, s1, b0, b1, st, se, sem, sem_out = refs[-9:]
+def amplitudes_kernel(mode, call, per_orb, groups, tbl, rows, vcol, *refs):
     client = mode == "client"
-    elsewhere = None
     if client:
-        tout = refs[-10]
-        left, js = refs[:4], refs[4:6]
+        tout = refs[-1]
+        left, rest = refs[:4], refs[4:]
     else:
-        tout, eout = refs[-11:-9]
-        left, js = refs[:2], refs[2:5]
-    if mode == "asked":
-        js = (js[0].at[0], js[0].at[1])
-    if mode == "asked_two":
-        js, elsewhere = [[x.at[0] for x in refs[k : k + 2]] for k in (2, 4)]
-    cap = sv.shape[0]
-    nvd, half = sv.shape[1], sv.shape[2]
-    base = tbl[HEAD, call]
+        tout, eout = refs[-2:]
+        left, rest = refs[:2], refs[2:]
+    places = []
+    for arrays in groups:
+        if arrays == 1:
+            places.append([rest[0].at[0], rest[0].at[1]])
+        elif len(rest[0].shape) == 4:
+            places.append([rest[0].at[0], rest[1].at[0]])
+        else:
+            places.append(rest[:2])
+        rest = rest[arrays:]
+    cap = rows.shape[0] // 8
+    nvd, half = vcol.shape[1:]
+    base = pl.multiple_of(tbl[HEAD, call], cap)
     middle = tbl[HEAD, MIDDLE] == 1
-
-    def place(r):
-        return tbl[ORDER, base + r]
-
-    def run(copies):
-        for copy in copies:
-            copy.start()
-        for copy in copies:
-            copy.wait()
-
-    def load(js=js):
-        copies = []
-        for r in range(cap):
-            i = lax.div(place(r), per_orb)
-            slot = r if mode.startswith("asked") else tbl[SLOT, base + r]
-            todo = [
-                (vcol.at[i], sv.at[r]),
-                (js[0].at[slot], b0.at[r]),
-                (js[1].at[slot], b1.at[r]),
-            ]
-            if client:
-                here = pl.ds(pl.multiple_of(tbl[HEAD, COLUMN], half), half)
-                there = pl.ds(pl.multiple_of(half - tbl[HEAD, COLUMN], half), half)
-                todo += [
-                    (left[0].at[i], s0.at[r, here, :]),
-                    (left[1].at[i], s1.at[r, here, :]),
-                    (left[2].at[i], s1.at[r, there, :]),
-                    (left[3].at[i], s0.at[r, there, :]),
-                ]
-            else:
-                todo += [(left[0].at[i], s0.at[r]), (left[1].at[i], s1.at[r])]
-            copies += [
-                pltpu.make_async_copy(x, to, sem.at[r, k]) for k, (x, to) in enumerate(todo)
-            ]
-        run(copies)
-
-    def gaps():
-        row8 = rows[pl.ds(pl.multiple_of(base, cap), cap), :]
-        return [sv[r] + row8[r : r + 1, :] for r in range(cap)]
-
-    def make():
+    row8 = rows[pl.ds(base, cap), :]
+
+    def gap(r, i):
+        return vcol[i] + row8[r : r + 1, :]
+
+    def make(r):
+        p = tbl[ORDER, base + r]
+        i = lax.div(p, per_orb)
+        slot = r if mode == "asked" else tbl[SLOT, base + r]
+        b0, b1 = [x[slot] for x in places[0]]
+        if len(places) == 2:
+            b0, b1 = [jnp.where(middle, b, x[slot]) for b, x in zip((b0, b1), places[1])]
+
+        def product(x0, x1):
+            return jnp.dot(x0[i], b0, preferred_element_type=f32) + jnp.dot(
+                x1[i], b1, preferred_element_type=f32
+            )
+
+        if client:
+            here, there = product(left[0], left[1]), product(left[3], left[2])
+            first = tbl[HEAD, COLUMN] == 0
+            k = jnp.concatenate(
+                [jnp.where(first, here, there), jnp.where(first, there, here)], axis=0
+            )
+        else:
+            k = product(left[0], left[1])
         live_a = lax.broadcasted_iota(i32, (nvd, half), 0)
         live_b = lax.broadcasted_iota(i32, (nvd, half), 1)
-        for r, gap in enumerate(gaps()):
-            size_i = tbl[SIZE_I, base + r]
-            size_j = tbl[SIZE_J, base + r]
-            k = jnp.dot(s0[r], b0[r], preferred_element_type=f32)
-            k += jnp.dot(s1[r], b1[r], preferred_element_type=f32)
-            k = jnp.where((live_a < size_i) & (live_b < size_j), k, 0.0)
-            t = (-k / gap).astype(bf16)
-            st[r] = t
-            if not client:
-                se[r : r + 1, :] = jnp.sum(k * t.astype(f32), axis=0, keepdims=True)
-
-    def take():
-        ready = js[2]
-        copies = [pltpu.make_async_copy(ready.at[r], st.at[r], sem.at[r, 0]) for r in range(cap)]
-        copies += [
-            pltpu.make_async_copy(vcol.at[lax.div(place(r), per_orb)], sv.at[r], sem.at[r, 1])
-            for r in range(cap)
-        ]
-        run(copies)
-        for r, gap in enumerate(gaps()):
-            t = st[r].astype(f32)
-            se[r : r + 1, :] = -jnp.sum(t * t * gap, axis=0, keepdims=True)
-
-    if client:
-
-        @pl.when(middle)
-        def _():
-            load()
-            make()
-            tout[...] = st[...]
-
-        return
+        live = (live_a < tbl[SIZE_I, base + r]) & (live_b < tbl[SIZE_J, base + r])
+        k = jnp.where(live, k, 0.0)
+        t = (-k / gap(r, i)).astype(bf16)
+        if client:
+            tout[r] = t
+            return None
+        tout[p] = t
+        return jnp.sum(k * t.astype(f32), axis=0, keepdims=True)
+
+    def take(r):
+        p = tbl[ORDER, base + r]
+        ready = rest[0][r]
+        tout[p] = ready
+        t = ready.astype(f32)
+        return -jnp.sum(t * t * gap(r, lax.div(p, per_orb)), axis=0, keepdims=True)
+
+    def each(step):
+        parts = [step(r) for r in range(cap)]
+        if not client:
+            eout[pl.ds(base, cap), :] = jnp.concatenate(parts, axis=0)
+
     if mode == "served":
-
-        @pl.when(middle)
-        def _():
-            load()
-            make()
-
-        pl.when(jnp.logical_not(middle))(take)
-    elif elsewhere is not None:
-        pl.when(middle)(load)
-        pl.when(jnp.logical_not(middle))(lambda: load(elsewhere))
-        make()
+        pl.when(middle)(lambda: each(make))
+        pl.when(jnp.logical_not(middle))(lambda: each(take))
+    elif client:
+        pl.when(middle)(lambda: each(make))
     else:
-        load()
-        make()
-    run(
-        [pltpu.make_async_copy(st.at[r], tout.at[place(r)], sem_out.at[r]) for r in range(cap)]
-        + [
-            pltpu.make_async_copy(
-                se, eout.at[pl.ds(pl.multiple_of(base, cap), cap), :], sem_out.at[cap]
-            )
-        ]
-    )
-
-
-def amplitudes(mode, call, per_orb, tables, left, sources, cap, held=(), after=()):
+        each(make)
+
+
+def amplitudes(mode, call, per_orb, tables, left, groups, cap, held=(), after=(), ready=()):
     tbl, rows, vcol = tables
     occ, nvd, half = vcol.shape
-    qa = left[0].shape[2]
     client = mode == "client"
-    operands = (tbl, rows, vcol, *left, *sources, *after)
+    sources = [x for group in groups for x in group]
+    blocks = (rows, vcol, *left, *sources, *ready)
+    operands = (tbl, *blocks, *after)
     aliases = {len(operands) + k: k for k in range(len(held))}
-    operands += tuple(held)
     if client:
         out_shape = jax.ShapeDtypeStruct((cap, nvd, half), bf16)
         out_specs = VMEM
@@ -418,28 +362,17 @@
             jax.ShapeDtypeStruct((occ * per_orb, nvd, half), bf16),
             jax.ShapeDtypeStruct((occ * per_orb, half), f32),
         )
-        out_specs = (HBM, HBM)
+        out_specs = (VMEM, VMEM)
     return pl.pallas_call(
-        lambda *refs: amplitudes_kernel(mode, call, per_orb, not held, *refs),
+        lambda *refs: amplitudes_kernel(mode, call, per_orb, [len(g) for g in groups], *refs),
         out_shape=out_shape,
-        in_specs=[SMEM, VMEM] + [HBM] * (len(operands) - 2),
+        in_specs=[SMEM] + [VMEM] * len(blocks) + [HBM] * len(after) + [VMEM] * len(held),
         out_specs=out_specs,
-        scratch_shapes=[
-            pltpu.VMEM((cap, nvd, half), f32),
-            pltpu.VMEM((cap, nvd, qa), bf16),
-            pltpu.VMEM((cap, nvd, qa), bf16),
-            pltpu.VMEM((cap, qa, half), bf16),
-            pltpu.VMEM((cap, qa, half), bf16),
-            pltpu.VMEM((cap, nvd, half), bf16),
-            pltpu.VMEM((cap, half), f32),
-            pltpu.SemaphoreType.DMA((cap, 7)),
-            pltpu.SemaphoreType.DMA((cap + 1,)),
-        ],
         input_output_aliases=aliases,
         compiler_params=PARAMS,
         cost_estimate=TINY,
         name="amplitudes",
-    )(*operands)
+    )(*operands, *held)
 
 
 def density_kernel(start, t, d):
@@ -493,7 +426,7 @@
 
     cross = [(2, 4), (3, 5), (4, 2), (5, 3)]
     outward = [(2, 0), (3, 1), (4, 6), (5, 7)]
-    outward_diagonal = [(2, 1), (3, 0), (4, 7), (5, 6)]
+    diagonal = [(2, 1), (3, 0), (4, 7), (5, 6)]
     y_middle = [(2, 3), (3, 2), (4, 5), (5, 4)]
 
     small, hit = lists(vir_energy, occ_energy, domain_size, partner_owner, partner_slot, cap)
@@ -514,19 +447,19 @@
     tables = (tbl, rows, spread(vir_energy))
     client = (client_tbl, client_rows, spread(smalls[2][:occ, :nvd]))
 
-    def own_pairs(k, mode, sources, held=(), after=()):
-        return amplitudes(mode, k, per_orb, tables, left, sources, cap, held, after)
+    def own_pairs(k, mode, groups, held=(), after=(), ready=()):
+        return amplitudes(mode, k, per_orb, tables, left, groups, cap, held, after, ready)
 
     packed = pack(beside_list, 0, own, cap)
     beside = pp(packed, flip(1))
     left = turn([blocks, other])
-    held = own_pairs(0, "slots", own, after=(packed,))
+    held = own_pairs(0, "slots", [own], after=(packed,))
     first, held = lax.optimization_barrier((near[0], held))
     far = [pp(first, cross)]
     across = [swap_core(first)]
     packed = pack(relay_list, 2, mid[:1], cap, only_middle=True, after=(held[1],))
     relays = [pp(packed, outward)]
-    held = own_pairs(4, "asked", [beside], held, (packed,))
+    held = own_pairs(4, "asked", [[beside]], held, (packed,))
     second, held = lax.optimization_barrier((near[1], held))
     far.append(pp(second, cross))
     across.append(swap_core(second))
@@ -536,29 +469,31 @@
     packed = pack(beside_list, 1, near, cap, after=(packed,))
     beside_near = pp(packed, flip(1))
     client_left = turn(near + across)
-    gone = amplitudes("client", 2, per_orb, client, client_left, mid, cap, after=(packed, relays[0]))
+    gone = amplitudes(
+        "client", 2, per_orb, client, client_left, [mid], cap, after=(packed, relays[0])
+    )
     ready_2 = pp(gone, outward)
-    held = own_pairs(1, "slots", near, held, (gone, relays[1]))
-    diagonal, fourth = [], []
+    held = own_pairs(1, "slots", [near], held, (gone,))
+    packed = pack(beside_list, 2, mid, cap, relayed=relays, after=(held[1],))
+    third = pp(packed, flip(1))
+    fourth_diagonal, fourth = [], []
 
     def send_far(q, token):
         packed = pack(relay_list, 3, far[q : q + 1], cap, only_middle=True, after=(token,))
-        diagonal.append(pp(packed, outward_diagonal))
+        fourth_diagonal.append(pp(packed, diagonal))
         packed = pack(beside_list, 3, far[q : q + 1], cap, only_middle=True, after=(packed,))
         fourth.append(pp(packed, y_middle))
         return packed
 
-    packed = send_far(0, held[1])
-    held = own_pairs(2, "served", mid + [ready_2], held, (packed, beside_near))
-    packed = pack(beside_list, 2, mid, cap, relayed=relays, after=(held[1],))
-    third = pp(packed, flip(1))
-    held = own_pairs(5, "asked", [beside_near], held, (packed, diagonal[0]))
+    packed = send_far(0, packed)
+    held = own_pairs(2, "served", [mid], held, (packed, beside_near), (ready_2,))
+    held = own_pairs(5, "asked", [[beside_near]], held, (fourth_diagonal[0],))
     packed = send_far(1, held[1])
-    gone = amplitudes("client", 3, per_orb, client, client_left, far, cap, after=(packed, diagonal[0], fourth[0]))
+    gone = amplitudes("client", 3, per_orb, client, client_left, [far], cap, after=(packed,))
     ready_3 = pp(gone, outward)
-    held = own_pairs(6, "asked", [third], held, (gone,))
-    held = own_pairs(7, "asked_two", fourth + diagonal, held)
-    t_all, e_all = own_pairs(3, "served", far + [ready_3], held)
+    held = own_pairs(6, "asked", [[third]], held, (gone,))
+    held = own_pairs(7, "asked", [fourth, fourth_diagonal], held)
+    t_all, e_all = own_pairs(3, "served", [far], held, ready=(ready_3,))
 
     away = swap_core(density_rows(t_all, (1 - core) * half, per_orb, half))
     density = density_rows(t_all, core * half, per_orb, half) + away

time: 198 us -> 172 us (0.87)
  the two profiles are of different devices: /device:TPU:9 before, /device:TPU:0 now
where the time goes in v9:
time: 172 us; the launch traced here: 171 us
  waiting for transfers between devices  89.1 us (52%)
  starting transfers between devices  31.9 us (19%)
  Pallas kernels  31.4 us (18%)
  local copies, waits for them, and re-layouts  13.6 us (8%)
  other arithmetic  4 us (2%)
    ppermute x24, waiting for transfers between devices, pp(): return lax.ppermute(x, 'orb', perm)  89.1 us
    ppermute x24, starting transfers between devices, pp(): return lax.ppermute(x, 'orb', perm)  30.7 us
    pallas_call x10, Pallas kernels, amplitudes(): pl.pallas_call(lambda *refs: amplitudes_kernel(mode, call, per_orb, [len(...  13.9 us
    unnamed x38, local copies, waits for them, and re-layouts  11 us
    pallas_call x9, Pallas kernels, pack(): pl.pallas_call(lambda *refs: pack_kernel(call, only_middle, relayed is no...  9.49 us
    pallas_call x2, Pallas kernels, density_rows(): pl.pallas_call(density_kernel, out_shape=jax.ShapeDtypeStruct((occ, half,...  3.88 us
  transfers between devices with their start and end apart: 29, of which 10 were waited for; matrix products, arithmetic and copies ran while one was open for 2% of the time, Pallas kernels for 16%

profile of v9, /device:TPU:0, one launch (start us, length us, event | category | flops | bytes accessed | tf_op | source)
XLA Modules:
  0.0 171.1 jit_solution(7500927446732803364)
XLA Ops:
  4.7 2.6 %collective-permute-start = (f32[24,384]{1,0:T(8,128)S(1)}, f32[24,384]{1,0:T(8,128)S(1)}, u32[]{:S(2)}, u32[]{:S(2)}) collective-permute-start(f32[24,384]{1,0:T(8,128)S(1)} %get-tuple-element.49.refs_1_), channel_id=1, source_target_pairs={{0,2},{2,0},{4,6},{6,4},{8,10},{10,8},{12,14},{14,12},{1,3},{3,1},... | collective-permute-start | bytes 110600 | tf_op jit(solution)/shard_map/ppermute | solution.py:419
  7.3 1.6 collective-permute-start.1
  8.9 3.0 %collective-permute-start.3 = (f32[24,384]{1,0:T(8,128)S(1)}, f32[24,384]{1,0:T(8,128)S(1)}, u32[]{:S(2)}, u32[]{:S(2)}) collective-permute-start(f32[24,384]{1,0:T(8,128)S(1)} %get-tuple-element.49.refs_1_), channel_id=1, source_target_pairs={{0,8},{2,10},{4,12},{6,14},{8,0},{10,2},{12,4},{14,6},{1,9},{3,11}... | collective-permute-start | bytes 110600 | tf_op jit(solution)/shard_map/ppermute | solution.py:419
  11.8 1.3 constant_dynamic-slice_fusion.1.refs_1_.refs_5_
  13.1 1.4 collective-permute-start.4
  14.5 3.6 %collective-permute-start.5 = (f32[24,384]{1,0:T(8,128)S(1)}, f32[24,384]{1,0:T(8,128)S(1)}, u32[]{:S(2)}, u32[]{:S(2)}) collective-permute-start(f32[24,384]{1,0:T(8,128)S(1)} %get-tuple-element.49.refs_1_), channel_id=1, source_target_pairs={{0,12},{2,14},{4,8},{6,10},{8,4},{10,6},{12,0},{14,2},{1,13},{3,15... | collective-permute-start | bytes 110600 | tf_op jit(solution)/shard_map/ppermute | solution.py:419
  18.2 1.0 collective-permute-done.4.refs_6_
  19.2 1.4 collective-permute-done.5.refs_7_
  20.5 4.6 %collective-permute-done.6.refs_8_ = f32[24,384]{1,0:T(8,128)S(1)} collective-permute-done((f32[24,384]{1,0:T(8,128)S(1)}, f32[24,384]{1,0:T(8,128)S(1)}, u32[]{:S(2)}, u32[]{:S(2)}) %collective-permute-start.6) | collective-permute-done | bytes 36896 | tf_op jit(solution)/shard_map/ppermute | solution.py:419
  25.9 1.3 tables.1
  28.5 3.2 %collective-permute-start.10 = (bf16[16,256,128]{2,1,0:T(8,128)(2,1)S(1)}, bf16[16,256,128]{2,1,0:T(8,128)(2,1)S(1)}, u32[]{:S(2)}, u32[]{:S(2)}) collective-permute-start(bf16[16,256,128]{2,1,0:T(8,128)(2,1)S(1)} %constant_dynamic-slice_fusion.refs_2_.refs_6_), channel_id=1, source_target_pairs={{0,4},{2,6},{4,0},{6,2},{8,12},{10,14},{12,8},{14,10},{1,5},{3,7},... | collective-permute-start | bytes 3145736 | tf_op jit(solution)/shard_map/ppermute | solution.py:419
  32.4 1.3 turn.2
  34.4 1.3 amplitudes.10
  35.7 15.5 %collective-permute-done.8.refs_0_.refs_1_.refs_5_ = bf16[16,256,128]{2,1,0:T(8,128)(2,1)S(1)} collective-permute-done((bf16[16,256,128]{2,1,0:T(8,128)(2,1)S(1)}, bf16[16,256,128]{2,1,0:T(8,128)(2,1)S(1)}, u32[]{:S(2)}, u32[]{:S(2)}) %collective-permute-start.8) | collective-permute-done | bytes 1048608 | tf_op jit(solution)/shard_map/ppermute | solution.py:419
  51.9 1.3 amplitudes.11
  53.2 16.7 %collective-permute-done.10.refs_1_.refs_2_.refs_6_ = bf16[16,256,128]{2,1,0:T(8,128)(2,1)S(1)} collective-permute-done((bf16[16,256,128]{2,1,0:T(8,128)(2,1)S(1)}, bf16[16,256,128]{2,1,0:T(8,128)(2,1)S(1)}, u32[]{:S(2)}, u32[]{:S(2)}) %collective-permute-start.10) | collective-permute-done | bytes 1048608 | tf_op jit(solution)/shard_map/ppermute | solution.py:419
  70.7 1.3 collective-permute-start.18
  73.3 1.3 collective-permute-start.19
  76.0 1.3 turn.3
  77.4 9.9 %collective-permute-done.18.refs_10_.refs_3_ = bf16[1,8,256,128]{3,2,1,0:T(8,128)(2,1)S(1)} collective-permute-done((bf16[1,8,256,128]{3,2,1,0:T(8,128)(2,1)S(1)}, bf16[1,8,256,128]{3,2,1,0:T(8,128)(2,1)S(1)}, u32[]{:S(2)}, u32[]{:S(2)}) %collective-permute-start.18) | collective-permute-done | bytes 524320 | tf_op jit(solution)/shard_map/ppermute | solution.py:419
  88.5 1.3 collective-permute-start.21
  89.8 1.3 amplitudes.13
  91.2 7.4 %collective-permute-done.19.refs_4_ = bf16[1,8,256,128]{3,2,1,0:T(8,128)(2,1)S(1)} collective-permute-done((bf16[1,8,256,128]{3,2,1,0:T(8,128)(2,1)S(1)}, bf16[1,8,256,128]{3,2,1,0:T(8,128)(2,1)S(1)}, u32[]{:S(2)}, u32[]{:S(2)}) %collective-permute-start.19) | collective-permute-done | bytes 524320 | tf_op jit(solution)/shard_map/ppermute | solution.py:419
  98.5 1.6 pack.13.refs_2_
  100.8 1.3 collective-permute-start.20
  102.8 1.4 pack.15.refs_8_
  104.2 5.6 %collective-permute-done.21.refs_7_ = bf16[8,256,128]{2,1,0:T(8,128)(2,1)S(1)} collective-permute-done((bf16[8,256,128]{2,1,0:T(8,128)(2,1)S(1)}, bf16[8,256,128]{2,1,0:T(8,128)(2,1)S(1)}, u32[]{:S(2)}, u32[]{:S(2)}) %collective-permute-start.21) | collective-permute-done | bytes 524320 | tf_op jit(solution)/shard_map/ppermute | solution.py:419
  109.8 0.9 amplitudes.14
  110.7 10.1 %collective-permute-done.20.refs_6_.refs_7_ = bf16[1,8,256,128]{3,2,1,0:T(8,128)(2,1)S(1)} collective-permute-done((bf16[1,8,256,128]{3,2,1,0:T(8,128)(2,1)S(1)}, bf16[1,8,256,128]{3,2,1,0:T(8,128)(2,1)S(1)}, u32[]{:S(2)}, u32[]{:S(2)}) %collective-permute-start.20) | collective-permute-done | bytes 524320 | tf_op jit(solution)/shard_map/ppermute | solution.py:419
  120.8 1.3 amplitudes.15
  122.2 1.8 %pack.16.refs_2_ = bf16[1,8,256,128]{3,2,1,0:T(8,128)(2,1)} custom-call(s32[8,128]{1,0:T(8,128)S(1)} %get-tuple-element.66.refs_0_, bf16[16,256,128]{2,1,0:T(8,128)(2,1)S(1)} %collective-permute-done.13.refs_1_.refs_8_.refs_6_, f32[64,128]{1,0:T(8,128)S(1)} %get-tuple-element.84.refs_2_.refs_8_), custom_call_target="tpu_custom_call" | custom-call | flops 1 | bytes 1 | tf_op jit(solution)/shard_map/pack/pallas_call | solution.py:236
  124.0 1.5 collective-permute-start.23
  125.5 1.4 pack.17.refs_9_
  126.9 1.5 collective-permute-start.24
  128.3 1.3 collective-permute-start.25
  129.6 1.5 amplitudes.16.refs_6_
  131.1 1.5 collective-permute-start.22
  132.6 16.8 %collective-permute-done.26.refs_5_ = bf16[2,8,256,128]{3,2,1,0:T(8,128)(2,1)} collective-permute-done((bf16[2,8,256,128]{3,2,1,0:T(8,128)(2,1)}, bf16[2,8,256,128]{3,2,1,0:T(8,128)(2,1)}, u32[]{:S(2)}, u32[]{:S(2)}) %collective-permute-start.26) | collective-permute-done | bytes 1048608 | tf_op jit(solution)/shard_map/ppermute | solution.py:419
  149.4 2.2 %copy-done.1 = bf16[64,256,128]{2,1,0:T(8,128)(2,1)S(1)} copy-done((bf16[64,256,128]{2,1,0:T(8,128)(2,1)S(1)}, bf16[64,256,128]{2,1,0:T(8,128)(2,1)}, u32[]{:S(2)}) %copy-start.1) | copy-done | bytes 4194328
  151.5 1.6 copy-done.5
  153.1 1.6 copy-done.7
  154.7 2.0 %amplitudes.17 = (bf16[64,256,128]{2,1,0:T(8,128)(2,1)S(1)}, f32[64,128]{1,0:T(8,128)S(1)}) custom-call(s32[8,128]{1,0:T(8,128)S(1)} %get-tuple-element.57.refs_0_, f32[64,128]{1,0:T(8,128)S(1)} %get-tuple-element.58.refs_1_, f32[16,256,128]{2,1,0:T(8,128)S(1)} %broadcast_in_dim.4.refs_2_, ...), custom_call_target="tpu_custom_call", output_to_operand_aliasing={{0}: (7, {}), {1}: (8, {})} | custom-call | flops 1 | bytes 1 | tf_op jit(solution)/shard_map/amplitudes/pallas_call | solution.py:366
  156.8 2.3 %amplitudes.18 = (bf16[64,256,128]{2,1,0:T(8,128)(2,1)S(1)}, f32[64,128]{1,0:T(8,128)S(1)}) custom-call(s32[8,128]{1,0:T(8,128)S(1)} %get-tuple-element.57.refs_0_, f32[64,128]{1,0:T(8,128)S(1)} %get-tuple-element.58.refs_1_, f32[16,256,128]{2,1,0:T(8,128)S(1)} %broadcast_in_dim.4.refs_2_, ...), custom_call_target="tpu_custom_call", output_to_operand_aliasing={{0}: (9, {}), {1}: (10, {})} | custom-call | flops 1 | bytes 1 | tf_op jit(solution)/shard_map/amplitudes/pallas_call | solution.py:366
  159.1 1.4 amplitudes.19
  160.4 2.0 %density_rows.3 = f32[16,128,256]{2,1,0:T(8,128)S(1)} custom-call(s32[1]{0:T(128)} %bitcast.6.start, bf16[64,256,128]{2,1,0:T(8,128)(2,1)S(1)} %get-tuple-element.91.t), custom_call_target="tpu_custom_call" | custom-call | flops 1 | bytes 1 | tf_op jit(solution)/shard_map/density_rows/pallas_call | solution.py:393
  163.3 2.2 %copy-done.3 = bf16[64,256,128]{2,1,0:T(8,128)(2,1)S(1)} copy-done((bf16[64,256,128]{2,1,0:T(8,128)(2,1)S(1)}, bf16[64,256,128]{2,1,0:T(8,128)(2,1)}, u32[]{:S(2)}) %copy-start.3) | copy-done | bytes 4194328
  165.5 1.9 %density_rows.2 = f32[16,128,256]{2,1,0:T(8,128)S(1)} custom-call(s32[1]{0:T(128)} %bitcast.5.start, bf16[64,256,128]{2,1,0:T(8,128)(2,1)S(1)} %copy-done.3), custom_call_target="tpu_custom_call" | custom-call | flops 1 | bytes 1 | tf_op jit(solution)/shard_map/density_rows/pallas_call | solution.py:393
  167.9 3.2 %add.12 = f32[16,128,256]{2,1,0:T(8,128)} add(f32[16,128,256]{2,1,0:T(8,128)S(1)} %density_rows.2, f32[16,128,256]{2,1,0:T(8,128)} %collective-permute-done.28) | non-fusion elementwise | flops 524288 | bytes 6291456 | tf_op jit(solution)/shard_map/add | solution.py:499
  (83 shorter events, 15.4 us)
Async XLA Ops:
  0.6 26.5 %collective-permute-start.7 = (bf16[16,256,256]{2,1,0:T(8,128)(2,1)}, bf16[16,256,256]{2,1,0:T(8,128)(2,1)S(1)}, u32[]{:S(2)}, u32[]{:S(2)}) collective-permute-start(bf16[16,256,256]{2,1,0:T(8,128)(2,1)} %refs_0_.3), channel_id=1, source_target_pairs={{0,1},{1,0},{2,3},{3,2},{4,5},{5,4},{6,7},{7,6},{8,9},{9,8},{10,11... | collective-permute-start | bytes 6291464 | tf_op jit(solution)/shard_map/ppermute | solution.py:422
  1.1 0.7 copy-start.13
  1.9 0.7 copy-start.15
  2.5 0.7 copy-start.16
  3.2 0.7 copy-start.17
  3.8 0.7 copy-start.18
  4.7 8.5 %collective-permute-start = (f32[24,384]{1,0:T(8,128)S(1)}, f32[24,384]{1,0:T(8,128)S(1)}, u32[]{:S(2)}, u32[]{:S(2)}) collective-permute-start(f32[24,384]{1,0:T(8,128)S(1)} %get-tuple-element.49.refs_1_), channel_id=1, source_target_pairs={{0,2},{2,0},{4,6},{6,4},{8,10},{10,8},{12,14},{14,12},{1,3},{3,1},... | collective-permute-start | bytes 110600 | tf_op jit(solution)/shard_map/ppermute | solution.py:419
  7.3 7.2 %collective-permute-start.1 = (f32[24,384]{1,0:T(8,128)S(1)}, f32[24,384]{1,0:T(8,128)S(1)}, u32[]{:S(2)}, u32[]{:S(2)}) collective-permute-start(f32[24,384]{1,0:T(8,128)S(1)} %get-tuple-element.49.refs_1_), channel_id=1, source_target_pairs={{0,4},{2,6},{4,0},{6,2},{8,12},{10,14},{12,8},{14,10},{1,5},{3,7},... | collective-permute-start | bytes 110600 | tf_op jit(solution)/shard_map/ppermute | solution.py:419
  8.8 9.3 %collective-permute-start.2 = (f32[24,384]{1,0:T(8,128)S(1)}, f32[24,384]{1,0:T(8,128)S(1)}, u32[]{:S(2)}, u32[]{:S(2)}) collective-permute-start(f32[24,384]{1,0:T(8,128)S(1)} %get-tuple-element.49.refs_1_), channel_id=1, source_target_pairs={{0,6},{2,4},{4,2},{6,0},{8,14},{10,12},{12,10},{14,8},{1,7},{3,5},... | collective-permute-start | bytes 110600 | tf_op jit(solution)/shard_map/ppermute | solution.py:419
  8.9 9.4 %collective-permute-start.3 = (f32[24,384]{1,0:T(8,128)S(1)}, f32[24,384]{1,0:T(8,128)S(1)}, u32[]{:S(2)}, u32[]{:S(2)}) collective-permute-start(f32[24,384]{1,0:T(8,128)S(1)} %get-tuple-element.49.refs_1_), channel_id=1, source_target_pairs={{0,8},{2,10},{4,12},{6,14},{8,0},{10,2},{12,4},{14,6},{1,9},{3,11}... | collective-permute-start | bytes 110600 | tf_op jit(solution)/shard_map/ppermute | solution.py:419
  13.1 6.0 %collective-permute-start.4 = (f32[24,384]{1,0:T(8,128)S(1)}, f32[24,384]{1,0:T(8,128)S(1)}, u32[]{:S(2)}, u32[]{:S(2)}) collective-permute-start(f32[24,384]{1,0:T(8,128)S(1)} %get-tuple-element.49.refs_1_), channel_id=1, source_target_pairs={{0,10},{2,8},{4,14},{6,12},{8,2},{10,0},{12,6},{14,4},{1,11},{3,9}... | collective-permute-start | bytes 110600 | tf_op jit(solution)/shard_map/ppermute | solution.py:419
  14.5 6.0 %collective-permute-start.5 = (f32[24,384]{1,0:T(8,128)S(1)}, f32[24,384]{1,0:T(8,128)S(1)}, u32[]{:S(2)}, u32[]{:S(2)}) collective-permute-start(f32[24,384]{1,0:T(8,128)S(1)} %get-tuple-element.49.refs_1_), channel_id=1, source_target_pairs={{0,12},{2,14},{4,8},{6,10},{8,4},{10,6},{12,0},{14,2},{1,13},{3,15... | collective-permute-start | bytes 110600 | tf_op jit(solution)/shard_map/ppermute | solution.py:419
  18.1 7.0 %collective-permute-start.6 = (f32[24,384]{1,0:T(8,128)S(1)}, f32[24,384]{1,0:T(8,128)S(1)}, u32[]{:S(2)}, u32[]{:S(2)}) collective-permute-start(f32[24,384]{1,0:T(8,128)S(1)} %get-tuple-element.49.refs_1_), channel_id=1, source_target_pairs={{0,14},{2,12},{4,10},{6,8},{8,6},{10,4},{12,2},{14,0},{1,15},{3,13... | collective-permute-start | bytes 110600 | tf_op jit(solution)/shard_map/ppermute | solution.py:419
  25.2 26.1 %collective-permute-start.8 = (bf16[16,256,128]{2,1,0:T(8,128)(2,1)S(1)}, bf16[16,256,128]{2,1,0:T(8,128)(2,1)S(1)}, u32[]{:S(2)}, u32[]{:S(2)}) collective-permute-start(bf16[16,256,128]{2,1,0:T(8,128)(2,1)S(1)} %constant_dynamic-slice_fusion.1.refs_1_.refs_5_), channel_id=1, source_target_pairs={{0,4},{2,6},{4,0},{6,2},{8,12},{10,14},{12,8},{14,10},{1,5},{3,7},... | collective-permute-start | bytes 3145736 | tf_op jit(solution)/shard_map/ppermute | solution.py:419
  25.2 26.1 %collective-permute-start.12 = (bf16[16,256,128]{2,1,0:T(8,128)(2,1)S(1)}, bf16[16,256,128]{2,1,0:T(8,128)(2,1)S(1)}, u32[]{:S(2)}, u32[]{:S(2)}) collective-permute-start(bf16[16,256,128]{2,1,0:T(8,128)(2,1)S(1)} %constant_dynamic-slice_fusion.1.refs_1_.refs_5_), channel_id=1, source_target_pairs={{4,8},{6,10},{8,4},{10,6},{5,9},{7,11},{9,5},{11,7},{20,24},{22,26... | collective-permute-start | bytes 3145736 | tf_op jit(solution)/shard_map/ppermute | solution.py:419
  27.4 5.0 %copy-start.10 = (bf16[16,256,256]{2,1,0:T(8,128)(2,1)S(1)}, bf16[16,256,256]{2,1,0:T(8,128)(2,1)}, u32[]{:S(2)}) copy-start(bf16[16,256,256]{2,1,0:T(8,128)(2,1)} %refs_0_.3) | copy-start | bytes 6291460
  28.1 5.7 %copy-start.14 = (f32[16,256]{1,0:T(8,128)S(1)}, f32[16,256]{1,0:T(8,128)}, u32[]{:S(2)}) copy-start(f32[16,256]{1,0:T(8,128)} %refs_0_.2) | copy-start | bytes 49156
  28.1 23.8 %collective-permute-start.11 = (bf16[2,8,256,128]{3,2,1,0:T(8,128)(2,1)S(1)}, bf16[2,8,256,128]{3,2,1,0:T(8,128)(2,1)S(1)}, u32[]{:S(2)}, u32[]{:S(2)}) collective-permute-start(bf16[2,8,256,128]{3,2,1,0:T(8,128)(2,1)S(1)} %pack.9.refs_7_), channel_id=1, source_target_pairs={{0,2},{2,0},{4,6},{6,4},{8,10},{10,8},{12,14},{14,12},{1,3},{3,1},... | collective-permute-start | bytes 3145736 | tf_op jit(solution)/shard_map/ppermute | solution.py:419
  28.5 41.5 %collective-permute-start.10 = (bf16[16,256,128]{2,1,0:T(8,128)(2,1)S(1)}, bf16[16,256,128]{2,1,0:T(8,128)(2,1)S(1)}, u32[]{:S(2)}, u32[]{:S(2)}) collective-permute-start(bf16[16,256,128]{2,1,0:T(8,128)(2,1)S(1)} %constant_dynamic-slice_fusion.refs_2_.refs_6_), channel_id=1, source_target_pairs={{0,4},{2,6},{4,0},{6,2},{8,12},{10,14},{12,8},{14,10},{1,5},{3,7},... | collective-permute-start | bytes 3145736 | tf_op jit(solution)/shard_map/ppermute | solution.py:419
  31.7 40.3 %collective-permute-start.16 = (bf16[16,256,128]{2,1,0:T(8,128)(2,1)S(1)}, bf16[16,256,128]{2,1,0:T(8,128)(2,1)S(1)}, u32[]{:S(2)}, u32[]{:S(2)}) collective-permute-start(bf16[16,256,128]{2,1,0:T(8,128)(2,1)S(1)} %constant_dynamic-slice_fusion.refs_2_.refs_6_), channel_id=1, source_target_pairs={{4,8},{6,10},{8,4},{10,6},{5,9},{7,11},{9,5},{11,7},{20,24},{22,26... | collective-permute-start | bytes 3145736 | tf_op jit(solution)/shard_map/ppermute | solution.py:419
  33.8 87.0 %copy-start.4 = (bf16[16,256,256]{2,1,0:T(8,128)(2,1)}, bf16[16,256,256]{2,1,0:T(8,128)(2,1)S(1)}, u32[]{:S(2)}) copy-start(bf16[16,256,256]{2,1,0:T(8,128)(2,1)S(1)} %get-tuple-element.59.refs_3_) | copy-start | bytes 6291460
  33.8 87.0 %copy-start.6 = (bf16[16,256,256]{2,1,0:T(8,128)(2,1)}, bf16[16,256,256]{2,1,0:T(8,128)(2,1)S(1)}, u32[]{:S(2)}) copy-start(bf16[16,256,256]{2,1,0:T(8,128)(2,1)S(1)} %get-tuple-element.60.refs_4_) | copy-start | bytes 6291460
  51.3 23.4 %collective-permute-start.14 = (bf16[16,256,128]{2,1,0:T(8,128)(2,1)S(1)}, bf16[16,256,128]{2,1,0:T(8,128)(2,1)S(1)}, u32[]{:S(2)}, u32[]{:S(2)}) collective-permute-start(bf16[16,256,128]{2,1,0:T(8,128)(2,1)S(1)} %collective-permute-done.8.refs_0_.refs_1_.refs_5_), channel_id=1, source_target_pairs={{0,1},{1,0},{2,3},{3,2},{4,5},{5,4},{6,7},{7,6},{8,9},{9,8},{10,11... | collective-permute-start | bytes 3145736 | tf_op jit(solution)/shard_map/ppermute | solution.py:422
  70.0 5.3 %collective-permute-start.15 = (bf16[16,256,128]{2,1,0:T(8,128)(2,1)S(1)}, bf16[16,256,128]{2,1,0:T(8,128)(2,1)S(1)}, u32[]{:S(2)}, u32[]{:S(2)}) collective-permute-start(bf16[16,256,128]{2,1,0:T(8,128)(2,1)S(1)} %collective-permute-done.10.refs_1_.refs_2_.refs_6_), channel_id=1, source_target_pairs={{0,1},{1,0},{2,3},{3,2},{4,5},{5,4},{6,7},{7,6},{8,9},{9,8},{10,11... | collective-permute-start | bytes 3145736 | tf_op jit(solution)/shard_map/ppermute | solution.py:422
  70.0 30.2 %collective-permute-start.9 = (bf16[16,256,128]{2,1,0:T(8,128)(2,1)S(1)}, bf16[16,256,128]{2,1,0:T(8,128)(2,1)S(1)}, u32[]{:S(2)}, u32[]{:S(2)}) collective-permute-start(bf16[16,256,128]{2,1,0:T(8,128)(2,1)S(1)} %collective-permute-done.8.refs_0_.refs_1_.refs_5_), channel_id=1, source_target_pairs={{4,8},{6,10},{8,4},{10,6},{5,9},{7,11},{9,5},{11,7},{20,24},{22,26... | collective-permute-start | bytes 3145736 | tf_op jit(solution)/shard_map/ppermute | solution.py:419
  70.7 16.6 %collective-permute-start.18 = (bf16[1,8,256,128]{3,2,1,0:T(8,128)(2,1)S(1)}, bf16[1,8,256,128]{3,2,1,0:T(8,128)(2,1)S(1)}, u32[]{:S(2)}, u32[]{:S(2)}) collective-permute-start(bf16[1,8,256,128]{3,2,1,0:T(8,128)(2,1)S(1)} %pack.10.refs_6_), channel_id=1, source_target_pairs={{4,0},{6,2},{8,12},{10,14},{5,1},{7,3},{9,13},{11,15},{20,16},{22,... | collective-permute-start | bytes 1572872 | tf_op jit(solution)/shard_map/ppermute | solution.py:419
  73.3 25.2 %collective-permute-start.19 = (bf16[1,8,256,128]{3,2,1,0:T(8,128)(2,1)S(1)}, bf16[1,8,256,128]{3,2,1,0:T(8,128)(2,1)S(1)}, u32[]{:S(2)}, u32[]{:S(2)}) collective-permute-start(bf16[1,8,256,128]{3,2,1,0:T(8,128)(2,1)S(1)} %pack.11.refs_3_), channel_id=1, source_target_pairs={{4,0},{6,2},{8,12},{10,14},{5,1},{7,3},{9,13},{11,15},{20,16},{22,... | collective-permute-start | bytes 1572872 | tf_op jit(solution)/shard_map/ppermute | solution.py:419
  74.6 29.6 %collective-permute-start.17 = (bf16[2,8,256,128]{3,2,1,0:T(8,128)(2,1)S(1)}, bf16[2,8,256,128]{3,2,1,0:T(8,128)(2,1)S(1)}, u32[]{:S(2)}, u32[]{:S(2)}) collective-permute-start(bf16[2,8,256,128]{3,2,1,0:T(8,128)(2,1)S(1)} %pack.12.refs_9_), channel_id=1, source_target_pairs={{0,2},{2,0},{4,6},{6,4},{8,10},{10,8},{12,14},{14,12},{1,3},{3,1},... | collective-permute-start | bytes 3145736 | tf_op jit(solution)/shard_map/ppermute | solution.py:419
  75.3 46.8 %collective-permute-start.13 = (bf16[16,256,128]{2,1,0:T(8,128)(2,1)S(1)}, bf16[16,256,128]{2,1,0:T(8,128)(2,1)S(1)}, u32[]{:S(2)}, u32[]{:S(2)}) collective-permute-start(bf16[16,256,128]{2,1,0:T(8,128)(2,1)S(1)} %collective-permute-done.10.refs_1_.refs_2_.refs_6_), channel_id=1, source_target_pairs={{4,8},{6,10},{8,4},{10,6},{5,9},{7,11},{9,5},{11,7},{20,24},{22,26... | collective-permute-start | bytes 3145736 | tf_op jit(solution)/shard_map/ppermute | solution.py:419
  88.5 21.2 %collective-permute-start.21 = (bf16[8,256,128]{2,1,0:T(8,128)(2,1)S(1)}, bf16[8,256,128]{2,1,0:T(8,128)(2,1)S(1)}, u32[]{:S(2)}, u32[]{:S(2)}) collective-permute-start(bf16[8,256,128]{2,1,0:T(8,128)(2,1)S(1)} %amplitudes.12.refs_7_), channel_id=1, source_target_pairs={{4,0},{6,2},{8,12},{10,14},{5,1},{7,3},{9,13},{11,15},{20,16},{22,... | collective-permute-start | bytes 1572872 | tf_op jit(solution)/shard_map/ppermute | solution.py:419
  100.8 20.0 %collective-permute-start.20 = (bf16[1,8,256,128]{3,2,1,0:T(8,128)(2,1)S(1)}, bf16[1,8,256,128]{3,2,1,0:T(8,128)(2,1)S(1)}, u32[]{:S(2)}, u32[]{:S(2)}) collective-permute-start(bf16[1,8,256,128]{3,2,1,0:T(8,128)(2,1)S(1)} %pack.14.refs_2_), channel_id=1, source_target_pairs={{4,2},{6,0},{8,14},{10,12},{5,3},{7,1},{9,15},{11,13},{20,18},{22,... | collective-permute-start | bytes 1572872 | tf_op jit(solution)/shard_map/ppermute | solution.py:419
  102.1 47.3 %collective-permute-start.26 = (bf16[2,8,256,128]{3,2,1,0:T(8,128)(2,1)}, bf16[2,8,256,128]{3,2,1,0:T(8,128)(2,1)}, u32[]{:S(2)}, u32[]{:S(2)}) collective-permute-start(bf16[2,8,256,128]{3,2,1,0:T(8,128)(2,1)} %pack.13.refs_2_), channel_id=1, source_target_pairs={{0,2},{2,0},{4,6},{6,4},{8,10},{10,8},{12,14},{14,12},{1,3},{3,1},... | collective-permute-start | bytes 3145736 | tf_op jit(solution)/shard_map/ppermute | solution.py:419
  120.8 1.3 copy-start.11
  122.1 9.0 %copy-start = (bf16[64,256,128]{2,1,0:T(8,128)(2,1)}, bf16[64,256,128]{2,1,0:T(8,128)(2,1)S(1)}, u32[]{:S(2)}) copy-start(bf16[64,256,128]{2,1,0:T(8,128)(2,1)S(1)} %get-tuple-element.85.refs_7_) | copy-start | bytes 12582916
  122.1 8.9 %copy-start.8 = (bf16[16,256,128]{2,1,0:T(8,128)(2,1)}, bf16[16,256,128]{2,1,0:T(8,128)(2,1)S(1)}, u32[]{:S(2)}) copy-start(bf16[16,256,128]{2,1,0:T(8,128)(2,1)S(1)} %collective-permute-done.13.refs_1_.refs_8_.refs_6_) | copy-start | bytes 3145732
  124.0 32.7 %collective-permute-start.23 = (bf16[1,8,256,128]{3,2,1,0:T(8,128)(2,1)}, bf16[1,8,256,128]{3,2,1,0:T(8,128)(2,1)}, u32[]{:S(2)}, u32[]{:S(2)}) collective-permute-start(bf16[1,8,256,128]{3,2,1,0:T(8,128)(2,1)} %pack.15.refs_8_), channel_id=1, source_target_pairs={{4,6},{6,4},{8,10},{10,8},{5,7},{7,5},{9,11},{11,9},{20,22},{22,20... | collective-permute-start | bytes 1572872 | tf_op jit(solution)/shard_map/ppermute | solution.py:419
  126.9 29.9 %collective-permute-start.24 = (bf16[1,8,256,128]{3,2,1,0:T(8,128)(2,1)}, bf16[1,8,256,128]{3,2,1,0:T(8,128)(2,1)}, u32[]{:S(2)}, u32[]{:S(2)}) collective-permute-start(bf16[1,8,256,128]{3,2,1,0:T(8,128)(2,1)} %pack.17.refs_9_), channel_id=1, source_target_pairs={{4,6},{6,4},{8,10},{10,8},{5,7},{7,5},{9,11},{11,9},{20,22},{22,20... | collective-permute-start | bytes 1572872 | tf_op jit(solution)/shard_map/ppermute | solution.py:419
  128.3 28.4 %collective-permute-start.25 = (bf16[1,8,256,128]{3,2,1,0:T(8,128)(2,1)}, bf16[1,8,256,128]{3,2,1,0:T(8,128)(2,1)}, u32[]{:S(2)}, u32[]{:S(2)}) collective-permute-start(bf16[1,8,256,128]{3,2,1,0:T(8,128)(2,1)} %pack.16.refs_2_), channel_id=1, source_target_pairs={{4,2},{6,0},{8,14},{10,12},{5,3},{7,1},{9,15},{11,13},{20,18},{22,... | collective-permute-start | bytes 1572872 | tf_op jit(solution)/shard_map/ppermute | solution.py:419
  131.1 28.0 %collective-permute-start.22 = (bf16[8,256,128]{2,1,0:T(8,128)(2,1)}, bf16[8,256,128]{2,1,0:T(8,128)(2,1)}, u32[]{:S(2)}, u32[]{:S(2)}) collective-permute-start(bf16[8,256,128]{2,1,0:T(8,128)(2,1)} %amplitudes.16.refs_6_), channel_id=1, source_target_pairs={{4,0},{6,2},{8,12},{10,14},{5,1},{7,3},{9,13},{11,15},{20,16},{22,... | collective-permute-start | bytes 1572872 | tf_op jit(solution)/shard_map/ppermute | solution.py:419
  149.4 2.2 %copy-start.1 = (bf16[64,256,128]{2,1,0:T(8,128)(2,1)S(1)}, bf16[64,256,128]{2,1,0:T(8,128)(2,1)}, u32[]{:S(2)}) copy-start(bf16[64,256,128]{2,1,0:T(8,128)(2,1)} %copy-done) | copy-start | bytes 12582916
  151.5 1.6 copy-start.5
  153.1 1.6 copy-start.7
  154.7 2.0 %copy-start.12 = (bf16[1,8,256,128]{3,2,1,0:T(8,128)(2,1)S(1)}, bf16[1,8,256,128]{3,2,1,0:T(8,128)(2,1)}, u32[]{:S(2)}) copy-start(bf16[1,8,256,128]{3,2,1,0:T(8,128)(2,1)} %copy-done.11) | copy-start | bytes 1572868
  156.8 2.3 %copy-start.9 = (bf16[16,256,128]{2,1,0:T(8,128)(2,1)S(1)}, bf16[16,256,128]{2,1,0:T(8,128)(2,1)}, u32[]{:S(2)}) copy-start(bf16[16,256,128]{2,1,0:T(8,128)(2,1)} %copy-done.8) | copy-start | bytes 3145732
  160.4 2.0 %copy-start.2 = (bf16[64,256,128]{2,1,0:T(8,128)(2,1)}, bf16[64,256,128]{2,1,0:T(8,128)(2,1)S(1)}, u32[]{:S(2)}) copy-start(bf16[64,256,128]{2,1,0:T(8,128)(2,1)S(1)} %get-tuple-element.91.t) | copy-start | bytes 12582916
  162.4 5.5 %collective-permute-start.28 = (f32[16,128,256]{2,1,0:T(8,128)S(1)}, f32[16,128,256]{2,1,0:T(8,128)}, u32[]{:S(2)}, u32[]{:S(2)}) collective-permute-start(f32[16,128,256]{2,1,0:T(8,128)S(1)} %density_rows.3), channel_id=1, source_target_pairs={{0,1},{1,0},{2,3},{3,2},{4,5},{5,4},{6,7},{7,6},{8,9},{9,8},{10,11... | collective-permute-start | bytes 6291464 | tf_op jit(solution)/shard_map/ppermute | solution.py:422
  162.7 4.7 %collective-permute-start.27 = (f32[64]{0:T(128)S(1)}, f32[64]{0:T(128)S(1)}, u32[]{:S(2)}, u32[]{:S(2)}) collective-permute-start(f32[64]{0:T(128)S(1)} %multiply_reduce_fusion), channel_id=1, source_target_pairs={{0,1},{1,0},{2,3},{3,2},{4,5},{5,4},{6,7},{7,6},{8,9},{9,8},{10,11... | collective-permute-start | bytes 776 | tf_op jit(solution)/shard_map/ppermute | solution.py:422
  163.3 2.2 %copy-start.3 = (bf16[64,256,128]{2,1,0:T(8,128)(2,1)S(1)}, bf16[64,256,128]{2,1,0:T(8,128)(2,1)}, u32[]{:S(2)}) copy-start(bf16[64,256,128]{2,1,0:T(8,128)(2,1)} %copy-done.2) | copy-start | bytes 12582916

commit v10 on v9

--- a/solution.py
+++ b/solution.py
@@ -1,3 +1,5 @@
+import functools
+
 import jax
 import jax.numpy as jnp
 from jax import lax
@@ -9,7 +11,7 @@
 HBM = pl.BlockSpec(memory_space=pltpu.HBM)
 SMEM = pl.BlockSpec(memory_space=pltpu.SMEM)
 VMEM = pl.BlockSpec(memory_space=pltpu.VMEM)
-LIMIT = 24 * 1024 * 1024
+LIMIT = 12 * 1024 * 1024
 
 
 def slot_ranks(owner):
@@ -206,42 +208,38 @@
     )(meta, *smalls)
 
 
-def pack_kernel(call, only_middle, relayed, tbl, *refs):
-    out = refs[-1]
-    halves, cap = out.shape[:2]
-    base = tbl[HEAD, call]
-    middle = tbl[HEAD, MIDDLE] == 1
-
-    def gather():
-        for q in range(halves):
-            for r in range(cap):
-                out[q, r] = refs[q][tbl[SLOT, base + r]]
-
-    if not only_middle and not relayed:
-        gather()
-    else:
-        pl.when(middle)(gather)
-    if relayed:
-
-        @pl.when(jnp.logical_not(middle))
-        def _():
-            for q in range(halves):
-                out[q] = refs[halves + q][0]
-
-
-def pack(tbl, call, sources, cap, only_middle=False, relayed=None, after=()):
-    halves = len(sources)
-    shape = (halves, cap) + sources[0].shape[1:]
-    operands = (*sources, *(relayed or ()))
+def pack_kernel(jobs, tables, *refs):
+    tbls, rest = refs[:tables], refs[tables:]
+    outs = refs[-len(jobs) :]
+    middle = tbls[0][HEAD, MIDDLE] == 1
+
+    def gather(out, sources, tbl, call):
+        base = tbl[HEAD, call]
+        for q in range(out.shape[0]):
+            for r in range(out.shape[1]):
+                out[q, r] = sources[q][tbl[SLOT, base + r]]
+
+    for out, (table, call, halves, only_middle) in zip(outs, jobs):
+        sources, rest = rest[:halves], rest[halves:]
+        if only_middle:
+            pl.when(middle)(functools.partial(gather, out, sources, tbls[table], call))
+        else:
+            gather(out, sources, tbls[table], call)
+
+
+def pack(tbls, jobs, cap, after=()):
+    operands = [x for _, _, sources, _ in jobs for x in sources]
+    kinds = [(table, call, len(sources), middle) for table, call, sources, middle in jobs]
+    block = operands[0].shape[1:]
     return pl.pallas_call(
-        lambda *refs: pack_kernel(call, only_middle, relayed is not None, *refs),
-        out_shape=jax.ShapeDtypeStruct(shape, bf16),
-        in_specs=[SMEM] + [VMEM] * len(operands) + [HBM] * len(after),
-        out_specs=VMEM,
+        lambda *refs: pack_kernel(kinds, len(tbls), *refs),
+        out_shape=[jax.ShapeDtypeStruct((k[2], cap) + block, bf16) for k in kinds],
+        in_specs=[SMEM] * len(tbls) + [VMEM] * len(operands) + [HBM] * len(after),
+        out_specs=[VMEM] * len(jobs),
         compiler_params=PARAMS,
         cost_estimate=TINY,
         name="pack",
-    )(tbl, *operands, *after)
+    )(*tbls, *operands, *after)
 
 
 def turn_kernel(*refs):
@@ -435,11 +433,12 @@
     other = swap_core(blocks)
     own = [lax.dynamic_slice_in_dim(x, col0, half, 2) for x in (blocks, other)]
     sent, smalls = lax.optimization_barrier((own[0], smalls))
+    mid = [pp(x, cross) for x in (sent, own[1])]
     near = [pp(x, flip(2)) for x in (sent, own[1])]
-    mid = [pp(x, cross) for x in (sent, own[1])]
     tbl, rows, client_tbl, client_rows, beside_list, relay_list = tables_of(
         jnp.stack([me, col0]), smalls, cap, per_orb, half
     )
+    lists_of = [beside_list, relay_list]
 
     def spread(vir):
         return jnp.broadcast_to(vir[:, :, None], (occ, nvd, half))
@@ -450,49 +449,47 @@
     def own_pairs(k, mode, groups, held=(), after=(), ready=()):
         return amplitudes(mode, k, per_orb, tables, left, groups, cap, held, after, ready)
 
-    packed = pack(beside_list, 0, own, cap)
+    (packed,) = pack(lists_of, [(0, 0, own, False)], cap)
     beside = pp(packed, flip(1))
     left = turn([blocks, other])
     held = own_pairs(0, "slots", [own], after=(packed,))
     first, held = lax.optimization_barrier((near[0], held))
     far = [pp(first, cross)]
     across = [swap_core(first)]
-    packed = pack(relay_list, 2, mid[:1], cap, only_middle=True, after=(held[1],))
-    relays = [pp(packed, outward)]
-    held = own_pairs(4, "asked", [[beside]], held, (packed,))
+    (packed,) = pack(lists_of, [(0, 1, [first], False)], cap, after=(held[1], mid[0]))
+    beside_near = [pp(packed, flip(1))]
+    held = own_pairs(4, "asked", [[beside]], held, (packed, beside_near[0]))
     second, held = lax.optimization_barrier((near[1], held))
     far.append(pp(second, cross))
     across.append(swap_core(second))
     near = [first, second]
-    packed = pack(relay_list, 2, mid[1:], cap, only_middle=True, after=(held[1],))
-    relays.append(pp(packed, outward))
-    packed = pack(beside_list, 1, near, cap, after=(packed,))
-    beside_near = pp(packed, flip(1))
+    packed = pack(lists_of, [(1, 2, mid, True), (0, 2, mid, True)], cap, after=(held[1],))
+    third_diagonal, third = pp(packed[0], diagonal), pp(packed[1], y_middle)
+    (packed,) = pack(lists_of, [(0, 1, [second], False)], cap, after=(packed[0],))
+    beside_near.append(pp(packed, flip(1)))
     client_left = turn(near + across)
-    gone = amplitudes(
-        "client", 2, per_orb, client, client_left, [mid], cap, after=(packed, relays[0])
-    )
+    gone = amplitudes("client", 2, per_orb, client, client_left, [mid], cap, after=(packed,))
     ready_2 = pp(gone, outward)
-    held = own_pairs(1, "slots", [near], held, (gone,))
-    packed = pack(beside_list, 2, mid, cap, relayed=relays, after=(held[1],))
-    third = pp(packed, flip(1))
+    held = own_pairs(1, "slots", [near], held, (gone, third_diagonal))
+    held = own_pairs(5, "asked", [beside_near], held)
     fourth_diagonal, fourth = [], []
 
     def send_far(q, token):
-        packed = pack(relay_list, 3, far[q : q + 1], cap, only_middle=True, after=(token,))
-        fourth_diagonal.append(pp(packed, diagonal))
-        packed = pack(beside_list, 3, far[q : q + 1], cap, only_middle=True, after=(packed,))
-        fourth.append(pp(packed, y_middle))
-        return packed
-
-    packed = send_far(0, packed)
-    held = own_pairs(2, "served", [mid], held, (packed, beside_near), (ready_2,))
-    held = own_pairs(5, "asked", [[beside_near]], held, (fourth_diagonal[0],))
+        jobs = [(1, 3, far[q : q + 1], True), (0, 3, far[q : q + 1], True)]
+        packed = pack(lists_of, jobs, cap, after=(token,))
+        fourth_diagonal.append(pp(packed[0], diagonal))
+        fourth.append(pp(packed[1], y_middle))
+        return packed[0]
+
+    packed = send_far(0, held[1])
+    held = own_pairs(2, "served", [mid], held, (packed,), (ready_2,))
+    held = own_pairs(
+        6, "asked", [[third], [third_diagonal]], held, (fourth[0], fourth_diagonal[0])
+    )
     packed = send_far(1, held[1])
     gone = amplitudes("client", 3, per_orb, client, client_left, [far], cap, after=(packed,))
     ready_3 = pp(gone, outward)
-    held = own_pairs(6, "asked", [[third]], held, (gone,))
-    held = own_pairs(7, "asked", [fourth, fourth_diagonal], held)
+    held = own_pairs(7, "asked", [fourth, fourth_diagonal], held, (gone,))
     t_all, e_all = own_pairs(3, "served", [far], held, ready=(ready_3,))
 
     away = swap_core(density_rows(t_all, (1 - core) * half, per_orb, half))

time: 172 us -> 173 us (level)
    pallas_call x9 -> x6, Pallas kernels: 9.49 us -> 6.9 us  [pack(): pl.pallas_call(lambda *refs: pack_kernel(kinds, len(tbls), *refs), out_sh...]
    unnamed x38 -> x46, local copies, waits for them, and re-layouts: 11 us -> 11 us
  transfers between devices with their start and end apart: 29 -> 29, of which waited for: 10 -> 9; matrix products, arithmetic and copies ran while one was open for 2% -> 3% of each run, Pallas kernels for 16% -> 15%
where the time goes in v10:
time: 173 us; the launch traced here: 172 us
  waiting for transfers between devices  89.7 us (52%)
  Pallas kernels  31.7 us (18%)
  starting transfers between devices  30.9 us (18%)
  local copies, waits for them, and re-layouts  14.7 us (8%)
  other arithmetic  4.14 us (2%)
    ppermute x24, waiting for transfers between devices, pp(): return lax.ppermute(x, 'orb', perm)  89.7 us
    ppermute x24, starting transfers between devices, pp(): return lax.ppermute(x, 'orb', perm)  29.8 us
    pallas_call x10, Pallas kernels, amplitudes(): pl.pallas_call(lambda *refs: amplitudes_kernel(mode, call, per_orb, [len(...  15.2 us
    unnamed x46, local copies, waits for them, and re-layouts  11 us
    pallas_call x6, Pallas kernels, pack(): pl.pallas_call(lambda *refs: pack_kernel(kinds, len(tbls), *refs), out_sh...  6.9 us
    pallas_call x2, Pallas kernels, turn(): pl.pallas_call(turn_kernel, out_shape=[jax.ShapeDtypeStruct((count, cols,...  4.26 us
    pallas_call x2, Pallas kernels, density_rows(): pl.pallas_call(density_kernel, out_shape=jax.ShapeDtypeStruct((occ, half,...  3.88 us
  transfers between devices with their start and end apart: 29, of which 9 were waited for; matrix products, arithmetic and copies ran while one was open for 3% of the time, Pallas kernels for 15%

profile of v10, /device:TPU:0, one launch (start us, length us, event | category | flops | bytes accessed | tf_op | source)
XLA Modules:
  0.0 172.3 jit_solution(12882065227324522302)
XLA Ops:
  4.7 2.6 %collective-permute-start = (f32[24,384]{1,0:T(8,128)S(1)}, f32[24,384]{1,0:T(8,128)S(1)}, u32[]{:S(2)}, u32[]{:S(2)}) collective-permute-start(f32[24,384]{1,0:T(8,128)S(1)} %get-tuple-element.55.refs_1_), channel_id=1, source_target_pairs={{0,2},{2,0},{4,6},{6,4},{8,10},{10,8},{12,14},{14,12},{1,3},{3,1},... | collective-permute-start | bytes 110600 | tf_op jit(solution)/shard_map/ppermute | solution.py:417
  7.3 1.6 collective-permute-start.1
  8.9 3.0 %collective-permute-start.3 = (f32[24,384]{1,0:T(8,128)S(1)}, f32[24,384]{1,0:T(8,128)S(1)}, u32[]{:S(2)}, u32[]{:S(2)}) collective-permute-start(f32[24,384]{1,0:T(8,128)S(1)} %get-tuple-element.55.refs_1_), channel_id=1, source_target_pairs={{0,8},{2,10},{4,12},{6,14},{8,0},{10,2},{12,4},{14,6},{1,9},{3,11}... | collective-permute-start | bytes 110600 | tf_op jit(solution)/shard_map/ppermute | solution.py:417
  11.8 1.4 collective-permute-start.4
  13.3 3.5 %collective-permute-start.5 = (f32[24,384]{1,0:T(8,128)S(1)}, f32[24,384]{1,0:T(8,128)S(1)}, u32[]{:S(2)}, u32[]{:S(2)}) collective-permute-start(f32[24,384]{1,0:T(8,128)S(1)} %get-tuple-element.55.refs_1_), channel_id=1, source_target_pairs={{0,12},{2,14},{4,8},{6,10},{8,4},{10,6},{12,0},{14,2},{1,13},{3,15... | collective-permute-start | bytes 110600 | tf_op jit(solution)/shard_map/ppermute | solution.py:417
  17.0 2.4 %constant_dynamic-slice_fusion.1.refs_2_.refs_5_ = bf16[16,256,128]{2,1,0:T(8,128)(2,1)} fusion(bf16[16,256,256]{2,1,0:T(8,128)(2,1)} %refs_0_.3, s32[]{:T(128)S(6)} %select_n.4), kind=kLoop, calls=%fused_computation.4 | loop fusion | bytes 2097156 | tf_op jit(solution)/shard_map/dynamic_slice | solution.py:434
  19.4 4.0 %collective-permute-done.6.refs_8_ = f32[24,384]{1,0:T(8,128)S(1)} collective-permute-done((f32[24,384]{1,0:T(8,128)S(1)}, f32[24,384]{1,0:T(8,128)S(1)}, u32[]{:S(2)}, u32[]{:S(2)}) %collective-permute-start.6) | collective-permute-done | bytes 36896 | tf_op jit(solution)/shard_map/ppermute | solution.py:417
  23.4 0.7 collective-permute-start.12
  24.2 1.3 tables.1
  25.7 1.5 pack.6.refs_7_
  27.8 3.2 %collective-permute-start.10 = (bf16[16,256,128]{2,1,0:T(8,128)(2,1)S(1)}, bf16[16,256,128]{2,1,0:T(8,128)(2,1)S(1)}, u32[]{:S(2)}, u32[]{:S(2)}) collective-permute-start(bf16[16,256,128]{2,1,0:T(8,128)(2,1)S(1)} %constant_dynamic-slice_fusion.refs_3_.refs_6_), channel_id=1, source_target_pairs={{0,4},{2,6},{4,0},{6,2},{8,12},{10,14},{12,8},{14,10},{1,5},{3,7},... | collective-permute-start | bytes 3145736 | tf_op jit(solution)/shard_map/ppermute | solution.py:417
  31.7 1.3 turn.2
  33.7 2.8 %amplitudes.10 = (bf16[64,256,128]{2,1,0:T(8,128)(2,1)S(1)}, f32[64,128]{1,0:T(8,128)S(1)}) custom-call(s32[8,128]{1,0:T(8,128)S(1)} %get-tuple-element.63.refs_0_, f32[64,128]{1,0:T(8,128)S(1)} %get-tuple-element.64.refs_1_, f32[16,256,128]{2,1,0:T(8,128)S(1)} %broadcast_in_dim.4.refs_2_, bf16[16,256,256]{2,1,0:T(8,128)(2,1)S(1)} %get-tuple-element.65.refs_3_, ...), custom_call_target="tpu_custom_call" | custom-call | flops 1 | bytes 1 | tf_op jit(solution)/shard_map/amplitudes/pallas_call | solution.py:364
  36.5 13.4 %collective-permute-done.8.refs_2_.refs_0_.refs_5_ = bf16[16,256,128]{2,1,0:T(8,128)(2,1)} collective-permute-done((bf16[16,256,128]{2,1,0:T(8,128)(2,1)}, bf16[16,256,128]{2,1,0:T(8,128)(2,1)}, u32[]{:S(2)}, u32[]{:S(2)}) %collective-permute-start.8) | collective-permute-done | bytes 1048608 | tf_op jit(solution)/shard_map/ppermute | solution.py:417
  49.8 1.3 pack.7.refs_6_
  51.7 9.6 %collective-permute-done.13.refs_7_.refs_5_ = bf16[1,8,256,128]{3,2,1,0:T(8,128)(2,1)S(1)} collective-permute-done((bf16[1,8,256,128]{3,2,1,0:T(8,128)(2,1)S(1)}, bf16[1,8,256,128]{3,2,1,0:T(8,128)(2,1)S(1)}, u32[]{:S(2)}, u32[]{:S(2)}) %collective-permute-start.13) | collective-permute-done | bytes 524320 | tf_op jit(solution)/shard_map/ppermute | solution.py:417
  61.2 1.3 amplitudes.11
  62.5 6.3 %collective-permute-done.10.refs_1_.refs_2_.refs_6_ = bf16[16,256,128]{2,1,0:T(8,128)(2,1)S(1)} collective-permute-done((bf16[16,256,128]{2,1,0:T(8,128)(2,1)S(1)}, bf16[16,256,128]{2,1,0:T(8,128)(2,1)S(1)}, u32[]{:S(2)}, u32[]{:S(2)}) %collective-permute-start.10) | collective-permute-done | bytes 1048608 | tf_op jit(solution)/shard_map/ppermute | solution.py:417
  69.5 1.3 collective-permute-start.19
  70.8 0.7 collective-permute-start.9
  72.8 0.7 collective-permute-start.18
  73.5 0.7 collective-permute-start.14
  74.3 2.9 %turn.3 = (bf16[16,128,256]{2,1,0:T(8,128)(2,1)S(1)}, bf16[16,128,256]{2,1,0:T(8,128)(2,1)S(1)}, bf16[16,128,256]{2,1,0:T(8,128)(2,1)S(1)}, bf16[16,128,256]{2,1,0:T(8,128)(2,1)S(1)}) custom-call(bf16[16,256,128]{2,1,0:T(8,128)(2,1)} %collective-permute-done.8.refs_2_.refs_0_.refs_5_, ...), custom_call_target="tpu_custom_call" | custom-call | flops 1 | bytes 1 | tf_op jit(solution)/shard_map/turn/pallas_call | solution.py:256
  78.4 19.5 %collective-permute-done.19.refs_8_.refs_6_ = bf16[2,8,256,128]{3,2,1,0:T(8,128)(2,1)S(1)} collective-permute-done((bf16[2,8,256,128]{3,2,1,0:T(8,128)(2,1)S(1)}, bf16[2,8,256,128]{3,2,1,0:T(8,128)(2,1)S(1)}, u32[]{:S(2)}, u32[]{:S(2)}) %collective-permute-start.19) | collective-permute-done | bytes 1048608 | tf_op jit(solution)/shard_map/ppermute | solution.py:417
  98.0 1.3 collective-permute-start.23
  99.2 2.0 %amplitudes.13 = (bf16[64,256,128]{2,1,0:T(8,128)(2,1)S(1)}, f32[64,128]{1,0:T(8,128)S(1)}) custom-call(s32[8,128]{1,0:T(8,128)S(1)} %get-tuple-element.63.refs_0_, f32[64,128]{1,0:T(8,128)S(1)} %get-tuple-element.64.refs_1_, f32[16,256,128]{2,1,0:T(8,128)S(1)} %broadcast_in_dim.4.refs_2_, ...), custom_call_target="tpu_custom_call", output_to_operand_aliasing={{0}: (9, {}), {1}: (10, {})} | custom-call | flops 1 | bytes 1 | tf_op jit(solution)/shard_map/amplitudes/pallas_call | solution.py:364
  101.2 7.9 %collective-permute-done.20.refs_6_ = bf16[1,8,256,128]{3,2,1,0:T(8,128)(2,1)S(1)} collective-permute-done((bf16[1,8,256,128]{3,2,1,0:T(8,128)(2,1)S(1)}, bf16[1,8,256,128]{3,2,1,0:T(8,128)(2,1)S(1)}, u32[]{:S(2)}, u32[]{:S(2)}) %collective-permute-start.20) | collective-permute-done | bytes 524320 | tf_op jit(solution)/shard_map/ppermute | solution.py:417
  109.1 1.3 amplitudes.14
  111.8 1.3 collective-permute-start.22
  113.1 0.9 amplitudes.15
  114.1 14.4 %collective-permute-done.22.refs_8_.refs_7_ = bf16[1,8,256,128]{3,2,1,0:T(8,128)(2,1)S(1)} collective-permute-done((bf16[1,8,256,128]{3,2,1,0:T(8,128)(2,1)S(1)}, bf16[1,8,256,128]{3,2,1,0:T(8,128)(2,1)S(1)}, u32[]{:S(2)}, u32[]{:S(2)}) %collective-permute-start.22) | collective-permute-done | bytes 524320 | tf_op jit(solution)/shard_map/ppermute | solution.py:417
  128.5 1.4 amplitudes.16
  129.9 2.1 %pack.11 = (bf16[1,8,256,128]{3,2,1,0:T(8,128)(2,1)}, bf16[1,8,256,128]{3,2,1,0:T(8,128)(2,1)}) custom-call(s32[8,128]{1,0:T(8,128)S(1)} %get-tuple-element.68.refs_0_, s32[8,128]{1,0:T(8,128)S(1)} %get-tuple-element.69.refs_1_, bf16[16,256,128]{2,1,0:T(8,128)(2,1)S(1)} %collective-permute-done.14.refs_2_.refs_3_.refs_8_.refs_6_, ...), custom_call_target="tpu_custom_call" | custom-call | flops 1 | bytes 1 | tf_op jit(solution)/shard_map/pack/pallas_call | solution.py:234
  132.0 1.4 collective-permute-start.25
  133.5 1.4 collective-permute-start.26
  134.9 1.4 amplitudes.17.refs_9_
  136.4 1.5 collective-permute-start.24
  137.8 13.7 %collective-permute-done.26.refs_8_ = bf16[1,8,256,128]{3,2,1,0:T(8,128)(2,1)} collective-permute-done((bf16[1,8,256,128]{3,2,1,0:T(8,128)(2,1)}, bf16[1,8,256,128]{3,2,1,0:T(8,128)(2,1)}, u32[]{:S(2)}, u32[]{:S(2)}) %collective-permute-start.26) | collective-permute-done | bytes 524320 | tf_op jit(solution)/shard_map/ppermute | solution.py:417
  151.6 2.2 %copy-done.1 = bf16[64,256,128]{2,1,0:T(8,128)(2,1)S(1)} copy-done((bf16[64,256,128]{2,1,0:T(8,128)(2,1)S(1)}, bf16[64,256,128]{2,1,0:T(8,128)(2,1)}, u32[]{:S(2)}) %copy-start.1) | copy-done | bytes 4194328
  153.8 1.6 copy-done.5
  155.4 1.6 copy-done.7
  157.0 2.1 %amplitudes.18 = (bf16[64,256,128]{2,1,0:T(8,128)(2,1)S(1)}, f32[64,128]{1,0:T(8,128)S(1)}) custom-call(s32[8,128]{1,0:T(8,128)S(1)} %get-tuple-element.63.refs_0_, f32[64,128]{1,0:T(8,128)S(1)} %get-tuple-element.64.refs_1_, f32[16,256,128]{2,1,0:T(8,128)S(1)} %broadcast_in_dim.4.refs_2_, ...), custom_call_target="tpu_custom_call", output_to_operand_aliasing={{0}: (10, {}), {1}: (11, {})} | custom-call | flops 1 | bytes 1 | tf_op jit(solution)/shard_map/amplitudes/pallas_call | solution.py:364
  159.1 0.9 collective-permute-done.24.refs_7_
  160.1 1.4 amplitudes.19
  161.4 1.9 %density_rows.3 = f32[16,128,256]{2,1,0:T(8,128)S(1)} custom-call(s32[1]{0:T(128)} %bitcast.6.start, bf16[64,256,128]{2,1,0:T(8,128)(2,1)S(1)} %get-tuple-element.103.t), custom_call_target="tpu_custom_call" | custom-call | flops 1 | bytes 1 | tf_op jit(solution)/shard_map/density_rows/pallas_call | solution.py:391
  164.3 2.2 %copy-done.3 = bf16[64,256,128]{2,1,0:T(8,128)(2,1)S(1)} copy-done((bf16[64,256,128]{2,1,0:T(8,128)(2,1)S(1)}, bf16[64,256,128]{2,1,0:T(8,128)(2,1)}, u32[]{:S(2)}) %copy-start.3) | copy-done | bytes 4194328
  166.5 1.9 %density_rows.2 = f32[16,128,256]{2,1,0:T(8,128)S(1)} custom-call(s32[1]{0:T(128)} %bitcast.5.start, bf16[64,256,128]{2,1,0:T(8,128)(2,1)S(1)} %copy-done.3), custom_call_target="tpu_custom_call" | custom-call | flops 1 | bytes 1 | tf_op jit(solution)/shard_map/density_rows/pallas_call | solution.py:391
  168.9 3.3 %add.12 = f32[16,128,256]{2,1,0:T(8,128)} add(f32[16,128,256]{2,1,0:T(8,128)S(1)} %density_rows.2, f32[16,128,256]{2,1,0:T(8,128)} %collective-permute-done.28) | non-fusion elementwise | flops 524288 | bytes 6291456 | tf_op jit(solution)/shard_map/add | solution.py:496
  (88 shorter events, 13.1 us)
Async XLA Ops:
  0.6 24.9 %collective-permute-start.7 = (bf16[16,256,256]{2,1,0:T(8,128)(2,1)}, bf16[16,256,256]{2,1,0:T(8,128)(2,1)S(1)}, u32[]{:S(2)}, u32[]{:S(2)}) collective-permute-start(bf16[16,256,256]{2,1,0:T(8,128)(2,1)} %refs_0_.3), channel_id=1, source_target_pairs={{0,1},{1,0},{2,3},{3,2},{4,5},{5,4},{6,7},{7,6},{8,9},{9,8},{10,11... | collective-permute-start | bytes 6291464 | tf_op jit(solution)/shard_map/ppermute | solution.py:420
  1.1 0.7 copy-start.17
  4.7 7.2 %collective-permute-start = (f32[24,384]{1,0:T(8,128)S(1)}, f32[24,384]{1,0:T(8,128)S(1)}, u32[]{:S(2)}, u32[]{:S(2)}) collective-permute-start(f32[24,384]{1,0:T(8,128)S(1)} %get-tuple-element.55.refs_1_), channel_id=1, source_target_pairs={{0,2},{2,0},{4,6},{6,4},{8,10},{10,8},{12,14},{14,12},{1,3},{3,1},... | collective-permute-start | bytes 110600 | tf_op jit(solution)/shard_map/ppermute | solution.py:417
  7.3 6.0 %collective-permute-start.1 = (f32[24,384]{1,0:T(8,128)S(1)}, f32[24,384]{1,0:T(8,128)S(1)}, u32[]{:S(2)}, u32[]{:S(2)}) collective-permute-start(f32[24,384]{1,0:T(8,128)S(1)} %get-tuple-element.55.refs_1_), channel_id=1, source_target_pairs={{0,4},{2,6},{4,0},{6,2},{8,12},{10,14},{12,8},{14,10},{1,5},{3,7},... | collective-permute-start | bytes 110600 | tf_op jit(solution)/shard_map/ppermute | solution.py:417
  8.8 7.9 %collective-permute-start.2 = (f32[24,384]{1,0:T(8,128)S(1)}, f32[24,384]{1,0:T(8,128)S(1)}, u32[]{:S(2)}, u32[]{:S(2)}) collective-permute-start(f32[24,384]{1,0:T(8,128)S(1)} %get-tuple-element.55.refs_1_), channel_id=1, source_target_pairs={{0,6},{2,4},{4,2},{6,0},{8,14},{10,12},{12,10},{14,8},{1,7},{3,5},... | collective-permute-start | bytes 110600 | tf_op jit(solution)/shard_map/ppermute | solution.py:417
  8.9 10.5 %collective-permute-start.3 = (f32[24,384]{1,0:T(8,128)S(1)}, f32[24,384]{1,0:T(8,128)S(1)}, u32[]{:S(2)}, u32[]{:S(2)}) collective-permute-start(f32[24,384]{1,0:T(8,128)S(1)} %get-tuple-element.55.refs_1_), channel_id=1, source_target_pairs={{0,8},{2,10},{4,12},{6,14},{8,0},{10,2},{12,4},{14,6},{1,9},{3,11}... | collective-permute-start | bytes 110600 | tf_op jit(solution)/shard_map/ppermute | solution.py:417
  11.8 7.6 %collective-permute-start.4 = (f32[24,384]{1,0:T(8,128)S(1)}, f32[24,384]{1,0:T(8,128)S(1)}, u32[]{:S(2)}, u32[]{:S(2)}) collective-permute-start(f32[24,384]{1,0:T(8,128)S(1)} %get-tuple-element.55.refs_1_), channel_id=1, source_target_pairs={{0,10},{2,8},{4,14},{6,12},{8,2},{10,0},{12,6},{14,4},{1,11},{3,9}... | collective-permute-start | bytes 110600 | tf_op jit(solution)/shard_map/ppermute | solution.py:417
  13.3 6.1 %collective-permute-start.5 = (f32[24,384]{1,0:T(8,128)S(1)}, f32[24,384]{1,0:T(8,128)S(1)}, u32[]{:S(2)}, u32[]{:S(2)}) collective-permute-start(f32[24,384]{1,0:T(8,128)S(1)} %get-tuple-element.55.refs_1_), channel_id=1, source_target_pairs={{0,12},{2,14},{4,8},{6,10},{8,4},{10,6},{12,0},{14,2},{1,13},{3,15... | collective-permute-start | bytes 110600 | tf_op jit(solution)/shard_map/ppermute | solution.py:417
  16.7 6.7 %collective-permute-start.6 = (f32[24,384]{1,0:T(8,128)S(1)}, f32[24,384]{1,0:T(8,128)S(1)}, u32[]{:S(2)}, u32[]{:S(2)}) collective-permute-start(f32[24,384]{1,0:T(8,128)S(1)} %get-tuple-element.55.refs_1_), channel_id=1, source_target_pairs={{0,14},{2,12},{4,10},{6,8},{8,6},{10,4},{12,2},{14,0},{1,15},{3,13... | collective-permute-start | bytes 110600 | tf_op jit(solution)/shard_map/ppermute | solution.py:417
  23.4 26.4 %collective-permute-start.8 = (bf16[16,256,128]{2,1,0:T(8,128)(2,1)}, bf16[16,256,128]{2,1,0:T(8,128)(2,1)}, u32[]{:S(2)}, u32[]{:S(2)}) collective-permute-start(bf16[16,256,128]{2,1,0:T(8,128)(2,1)} %constant_dynamic-slice_fusion.1.refs_2_.refs_5_), channel_id=1, source_target_pairs={{0,4},{2,6},{4,0},{6,2},{8,12},{10,14},{12,8},{14,10},{1,5},{3,7},... | collective-permute-start | bytes 3145736 | tf_op jit(solution)/shard_map/ppermute | solution.py:417
  23.4 26.4 %collective-permute-start.12 = (bf16[16,256,128]{2,1,0:T(8,128)(2,1)}, bf16[16,256,128]{2,1,0:T(8,128)(2,1)S(1)}, u32[]{:S(2)}, u32[]{:S(2)}) collective-permute-start(bf16[16,256,128]{2,1,0:T(8,128)(2,1)} %constant_dynamic-slice_fusion.1.refs_2_.refs_5_), channel_id=1, source_target_pairs={{4,8},{6,10},{8,4},{10,6},{5,9},{7,11},{9,5},{11,7},{20,24},{22,26... | collective-permute-start | bytes 3145736 | tf_op jit(solution)/shard_map/ppermute | solution.py:417
  25.7 6.0 %copy-start.12 = (bf16[16,256,256]{2,1,0:T(8,128)(2,1)S(1)}, bf16[16,256,256]{2,1,0:T(8,128)(2,1)}, u32[]{:S(2)}) copy-start(bf16[16,256,256]{2,1,0:T(8,128)(2,1)} %refs_0_.3) | copy-start | bytes 6291460
  27.2 5.9 %copy-start.18 = (f32[16,256]{1,0:T(8,128)S(1)}, f32[16,256]{1,0:T(8,128)}, u32[]{:S(2)}) copy-start(f32[16,256]{1,0:T(8,128)} %refs_0_.2) | copy-start | bytes 49156
  27.2 34.0 %collective-permute-start.11 = (bf16[2,8,256,128]{3,2,1,0:T(8,128)(2,1)S(1)}, bf16[2,8,256,128]{3,2,1,0:T(8,128)(2,1)S(1)}, u32[]{:S(2)}, u32[]{:S(2)}) collective-permute-start(bf16[2,8,256,128]{3,2,1,0:T(8,128)(2,1)S(1)} %pack.6.refs_7_), channel_id=1, source_target_pairs={{0,2},{2,0},{4,6},{6,4},{8,10},{10,8},{12,14},{14,12},{1,3},{3,1},... | collective-permute-start | bytes 3145736 | tf_op jit(solution)/shard_map/ppermute | solution.py:417
  27.8 41.0 %collective-permute-start.10 = (bf16[16,256,128]{2,1,0:T(8,128)(2,1)S(1)}, bf16[16,256,128]{2,1,0:T(8,128)(2,1)S(1)}, u32[]{:S(2)}, u32[]{:S(2)}) collective-permute-start(bf16[16,256,128]{2,1,0:T(8,128)(2,1)S(1)} %constant_dynamic-slice_fusion.refs_3_.refs_6_), channel_id=1, source_target_pairs={{0,4},{2,6},{4,0},{6,2},{8,12},{10,14},{12,8},{14,10},{1,5},{3,7},... | collective-permute-start | bytes 3145736 | tf_op jit(solution)/shard_map/ppermute | solution.py:417
  31.0 37.8 %collective-permute-start.17 = (bf16[16,256,128]{2,1,0:T(8,128)(2,1)S(1)}, bf16[16,256,128]{2,1,0:T(8,128)(2,1)S(1)}, u32[]{:S(2)}, u32[]{:S(2)}) collective-permute-start(bf16[16,256,128]{2,1,0:T(8,128)(2,1)S(1)} %constant_dynamic-slice_fusion.refs_3_.refs_6_), channel_id=1, source_target_pairs={{4,8},{6,10},{8,4},{10,6},{5,9},{7,11},{9,5},{11,7},{20,24},{22,26... | collective-permute-start | bytes 3145736 | tf_op jit(solution)/shard_map/ppermute | solution.py:417
  33.1 95.5 %copy-start.4 = (bf16[16,256,256]{2,1,0:T(8,128)(2,1)}, bf16[16,256,256]{2,1,0:T(8,128)(2,1)S(1)}, u32[]{:S(2)}) copy-start(bf16[16,256,256]{2,1,0:T(8,128)(2,1)S(1)} %get-tuple-element.65.refs_3_) | copy-start | bytes 6291460
  33.1 95.4 %copy-start.6 = (bf16[16,256,256]{2,1,0:T(8,128)(2,1)}, bf16[16,256,256]{2,1,0:T(8,128)(2,1)S(1)}, u32[]{:S(2)}) copy-start(bf16[16,256,256]{2,1,0:T(8,128)(2,1)S(1)} %get-tuple-element.66.refs_4_) | copy-start | bytes 6291460
  51.1 10.1 %collective-permute-start.13 = (bf16[1,8,256,128]{3,2,1,0:T(8,128)(2,1)S(1)}, bf16[1,8,256,128]{3,2,1,0:T(8,128)(2,1)S(1)}, u32[]{:S(2)}, u32[]{:S(2)}) collective-permute-start(bf16[1,8,256,128]{3,2,1,0:T(8,128)(2,1)S(1)} %pack.7.refs_6_), channel_id=1, source_target_pairs={{0,2},{2,0},{4,6},{6,4},{8,10},{10,8},{12,14},{14,12},{1,3},{3,1},... | collective-permute-start | bytes 1572872 | tf_op jit(solution)/shard_map/ppermute | solution.py:417
  51.7 21.1 %collective-permute-start.15 = (bf16[16,256,128]{2,1,0:T(8,128)(2,1)}, bf16[16,256,128]{2,1,0:T(8,128)(2,1)S(1)}, u32[]{:S(2)}, u32[]{:S(2)}) collective-permute-start(bf16[16,256,128]{2,1,0:T(8,128)(2,1)} %collective-permute-done.8.refs_2_.refs_0_.refs_5_), channel_id=1, source_target_pairs={{0,1},{1,0},{2,3},{3,2},{4,5},{5,4},{6,7},{7,6},{8,9},{9,8},{10,11... | collective-permute-start | bytes 3145736 | tf_op jit(solution)/shard_map/ppermute | solution.py:420
  68.8 4.7 %collective-permute-start.16 = (bf16[16,256,128]{2,1,0:T(8,128)(2,1)S(1)}, bf16[16,256,128]{2,1,0:T(8,128)(2,1)S(1)}, u32[]{:S(2)}, u32[]{:S(2)}) collective-permute-start(bf16[16,256,128]{2,1,0:T(8,128)(2,1)S(1)} %collective-permute-done.10.refs_1_.refs_2_.refs_6_), channel_id=1, source_target_pairs={{0,1},{1,0},{2,3},{3,2},{4,5},{5,4},{6,7},{7,6},{8,9},{9,8},{10,11... | collective-permute-start | bytes 3145736 | tf_op jit(solution)/shard_map/ppermute | solution.py:420
  69.5 28.5 %collective-permute-start.19 = (bf16[2,8,256,128]{3,2,1,0:T(8,128)(2,1)S(1)}, bf16[2,8,256,128]{3,2,1,0:T(8,128)(2,1)S(1)}, u32[]{:S(2)}, u32[]{:S(2)}) collective-permute-start(bf16[2,8,256,128]{3,2,1,0:T(8,128)(2,1)S(1)} %get-tuple-element.86.refs_3_), channel_id=1, source_target_pairs={{4,2},{6,0},{8,14},{10,12},{5,3},{7,1},{9,15},{11,13},{20,18},{22,... | collective-permute-start | bytes 3145736 | tf_op jit(solution)/shard_map/ppermute | solution.py:417
  70.8 39.6 %collective-permute-start.9 = (bf16[16,256,128]{2,1,0:T(8,128)(2,1)}, bf16[16,256,128]{2,1,0:T(8,128)(2,1)S(1)}, u32[]{:S(2)}, u32[]{:S(2)}) collective-permute-start(bf16[16,256,128]{2,1,0:T(8,128)(2,1)} %collective-permute-done.8.refs_2_.refs_0_.refs_5_), channel_id=1, source_target_pairs={{4,8},{6,10},{8,4},{10,6},{5,9},{7,11},{9,5},{11,7},{20,24},{22,26... | collective-permute-start | bytes 3145736 | tf_op jit(solution)/shard_map/ppermute | solution.py:417
  72.2 36.8 %collective-permute-start.20 = (bf16[1,8,256,128]{3,2,1,0:T(8,128)(2,1)S(1)}, bf16[1,8,256,128]{3,2,1,0:T(8,128)(2,1)S(1)}, u32[]{:S(2)}, u32[]{:S(2)}) collective-permute-start(bf16[1,8,256,128]{3,2,1,0:T(8,128)(2,1)S(1)} %pack.9.refs_9_), channel_id=1, source_target_pairs={{0,2},{2,0},{4,6},{6,4},{8,10},{10,8},{12,14},{14,12},{1,3},{3,1},... | collective-permute-start | bytes 1572872 | tf_op jit(solution)/shard_map/ppermute | solution.py:417
  72.8 41.2 %collective-permute-start.18 = (bf16[2,8,256,128]{3,2,1,0:T(8,128)(2,1)S(1)}, bf16[2,8,256,128]{3,2,1,0:T(8,128)(2,1)S(1)}, u32[]{:S(2)}, u32[]{:S(2)}) collective-permute-start(bf16[2,8,256,128]{3,2,1,0:T(8,128)(2,1)S(1)} %get-tuple-element.85), channel_id=1, source_target_pairs={{4,6},{6,4},{8,10},{10,8},{5,7},{7,5},{9,11},{11,9},{20,22},{22,20... | collective-permute-start | bytes 3145736 | tf_op jit(solution)/shard_map/ppermute | solution.py:417
  73.5 56.4 %collective-permute-start.14 = (bf16[16,256,128]{2,1,0:T(8,128)(2,1)S(1)}, bf16[16,256,128]{2,1,0:T(8,128)(2,1)S(1)}, u32[]{:S(2)}, u32[]{:S(2)}) collective-permute-start(bf16[16,256,128]{2,1,0:T(8,128)(2,1)S(1)} %collective-permute-done.10.refs_1_.refs_2_.refs_6_), channel_id=1, source_target_pairs={{4,8},{6,10},{8,4},{10,6},{5,9},{7,11},{9,5},{11,7},{20,24},{22,26... | collective-permute-start | bytes 3145736 | tf_op jit(solution)/shard_map/ppermute | solution.py:417
  98.0 15.2 %collective-permute-start.23 = (bf16[8,256,128]{2,1,0:T(8,128)(2,1)S(1)}, bf16[8,256,128]{2,1,0:T(8,128)(2,1)S(1)}, u32[]{:S(2)}, u32[]{:S(2)}) collective-permute-start(bf16[8,256,128]{2,1,0:T(8,128)(2,1)S(1)} %amplitudes.12.refs_7_), channel_id=1, source_target_pairs={{4,0},{6,2},{8,12},{10,14},{5,1},{7,3},{9,13},{11,15},{20,16},{22,... | collective-permute-start | bytes 1572872 | tf_op jit(solution)/shard_map/ppermute | solution.py:417
  110.4 24.5 %copy-start.8 = (bf16[16,256,128]{2,1,0:T(8,128)(2,1)}, bf16[16,256,128]{2,1,0:T(8,128)(2,1)S(1)}, u32[]{:S(2)}) copy-start(bf16[16,256,128]{2,1,0:T(8,128)(2,1)S(1)} %collective-permute-done.9.refs_2_.refs_3_.refs_7_.refs_5_) | copy-start | bytes 3145732
  111.1 3.0 %collective-permute-start.21 = (bf16[1,8,256,128]{3,2,1,0:T(8,128)(2,1)S(1)}, bf16[1,8,256,128]{3,2,1,0:T(8,128)(2,1)S(1)}, u32[]{:S(2)}, u32[]{:S(2)}) collective-permute-start(bf16[1,8,256,128]{3,2,1,0:T(8,128)(2,1)S(1)} %get-tuple-element.91), channel_id=1, source_target_pairs={{4,6},{6,4},{8,10},{10,8},{5,7},{7,5},{9,11},{11,9},{20,22},{22,20... | collective-permute-start | bytes 1572872 | tf_op jit(solution)/shard_map/ppermute | solution.py:417
  111.8 16.7 %collective-permute-start.22 = (bf16[1,8,256,128]{3,2,1,0:T(8,128)(2,1)S(1)}, bf16[1,8,256,128]{3,2,1,0:T(8,128)(2,1)S(1)}, u32[]{:S(2)}, u32[]{:S(2)}) collective-permute-start(bf16[1,8,256,128]{3,2,1,0:T(8,128)(2,1)S(1)} %get-tuple-element.92.refs_8_), channel_id=1, source_target_pairs={{4,2},{6,0},{8,14},{10,12},{5,3},{7,1},{9,15},{11,13},{20,18},{22,... | collective-permute-start | bytes 1572872 | tf_op jit(solution)/shard_map/ppermute | solution.py:417
  114.1 15.8 %copy-start.13 = (bf16[1,8,256,128]{3,2,1,0:T(8,128)(2,1)}, bf16[1,8,256,128]{3,2,1,0:T(8,128)(2,1)S(1)}, u32[]{:S(2)}) copy-start(bf16[1,8,256,128]{3,2,1,0:T(8,128)(2,1)S(1)} %collective-permute-done.21.refs_7_.refs_5_) | copy-start | bytes 1572868
  128.5 1.4 copy-start.15
  129.9 6.5 %copy-start = (bf16[64,256,128]{2,1,0:T(8,128)(2,1)}, bf16[64,256,128]{2,1,0:T(8,128)(2,1)S(1)}, u32[]{:S(2)}) copy-start(bf16[64,256,128]{2,1,0:T(8,128)(2,1)S(1)} %get-tuple-element.99.refs_10_) | copy-start | bytes 12582916
  129.9 6.4 %copy-start.10 = (bf16[16,256,128]{2,1,0:T(8,128)(2,1)}, bf16[16,256,128]{2,1,0:T(8,128)(2,1)S(1)}, u32[]{:S(2)}) copy-start(bf16[16,256,128]{2,1,0:T(8,128)(2,1)S(1)} %collective-permute-done.14.refs_2_.refs_3_.refs_8_.refs_6_) | copy-start | bytes 3145732
  132.0 5.8 %collective-permute-start.25 = (bf16[1,8,256,128]{3,2,1,0:T(8,128)(2,1)}, bf16[1,8,256,128]{3,2,1,0:T(8,128)(2,1)}, u32[]{:S(2)}, u32[]{:S(2)}) collective-permute-start(bf16[1,8,256,128]{3,2,1,0:T(8,128)(2,1)} %get-tuple-element.98), channel_id=1, source_target_pairs={{4,6},{6,4},{8,10},{10,8},{5,7},{7,5},{9,11},{11,9},{20,22},{22,20... | collective-permute-start | bytes 1572872 | tf_op jit(solution)/shard_map/ppermute | solution.py:417
  133.5 18.1 %copy-start.14 = (bf16[1,8,256,128]{3,2,1,0:T(8,128)(2,1)S(1)}, bf16[1,8,256,128]{3,2,1,0:T(8,128)(2,1)}, u32[]{:S(2)}) copy-start(bf16[1,8,256,128]{3,2,1,0:T(8,128)(2,1)} %copy-done.13) | copy-start | bytes 1572868
  133.5 18.1 %copy-start.16 = (bf16[1,8,256,128]{3,2,1,0:T(8,128)(2,1)S(1)}, bf16[1,8,256,128]{3,2,1,0:T(8,128)(2,1)}, u32[]{:S(2)}) copy-start(bf16[1,8,256,128]{3,2,1,0:T(8,128)(2,1)} %copy-done.15) | copy-start | bytes 1572868
  133.5 18.1 %collective-permute-start.26 = (bf16[1,8,256,128]{3,2,1,0:T(8,128)(2,1)}, bf16[1,8,256,128]{3,2,1,0:T(8,128)(2,1)}, u32[]{:S(2)}, u32[]{:S(2)}) collective-permute-start(bf16[1,8,256,128]{3,2,1,0:T(8,128)(2,1)} %get-tuple-element.97.refs_9_), channel_id=1, source_target_pairs={{4,2},{6,0},{8,14},{10,12},{5,3},{7,1},{9,15},{11,13},{20,18},{22,... | collective-permute-start | bytes 1572872 | tf_op jit(solution)/shard_map/ppermute | solution.py:417
  136.4 23.7 %collective-permute-start.24 = (bf16[8,256,128]{2,1,0:T(8,128)(2,1)}, bf16[8,256,128]{2,1,0:T(8,128)(2,1)}, u32[]{:S(2)}, u32[]{:S(2)}) collective-permute-start(bf16[8,256,128]{2,1,0:T(8,128)(2,1)} %amplitudes.17.refs_9_), channel_id=1, source_target_pairs={{4,0},{6,2},{8,12},{10,14},{5,1},{7,3},{9,13},{11,15},{20,16},{22,... | collective-permute-start | bytes 1572872 | tf_op jit(solution)/shard_map/ppermute | solution.py:417
  151.6 2.2 %copy-start.1 = (bf16[64,256,128]{2,1,0:T(8,128)(2,1)S(1)}, bf16[64,256,128]{2,1,0:T(8,128)(2,1)}, u32[]{:S(2)}) copy-start(bf16[64,256,128]{2,1,0:T(8,128)(2,1)} %copy-done) | copy-start | bytes 12582916
  153.8 1.6 copy-start.5
  155.4 1.6 copy-start.7
  157.0 3.1 %copy-start.9 = (bf16[16,256,128]{2,1,0:T(8,128)(2,1)S(1)}, bf16[16,256,128]{2,1,0:T(8,128)(2,1)}, u32[]{:S(2)}) copy-start(bf16[16,256,128]{2,1,0:T(8,128)(2,1)} %copy-done.8) | copy-start | bytes 3145732
  157.0 3.1 %copy-start.11 = (bf16[16,256,128]{2,1,0:T(8,128)(2,1)S(1)}, bf16[16,256,128]{2,1,0:T(8,128)(2,1)}, u32[]{:S(2)}) copy-start(bf16[16,256,128]{2,1,0:T(8,128)(2,1)} %copy-done.10) | copy-start | bytes 3145732
  161.4 2.0 %copy-start.2 = (bf16[64,256,128]{2,1,0:T(8,128)(2,1)}, bf16[64,256,128]{2,1,0:T(8,128)(2,1)S(1)}, u32[]{:S(2)}) copy-start(bf16[64,256,128]{2,1,0:T(8,128)(2,1)S(1)} %get-tuple-element.103.t) | copy-start | bytes 12582916
  163.4 5.5 %collective-permute-start.28 = (f32[16,128,256]{2,1,0:T(8,128)S(1)}, f32[16,128,256]{2,1,0:T(8,128)}, u32[]{:S(2)}, u32[]{:S(2)}) collective-permute-start(f32[16,128,256]{2,1,0:T(8,128)S(1)} %density_rows.3), channel_id=1, source_target_pairs={{0,1},{1,0},{2,3},{3,2},{4,5},{5,4},{6,7},{7,6},{8,9},{9,8},{10,11... | collective-permute-start | bytes 6291464 | tf_op jit(solution)/shard_map/ppermute | solution.py:420
  163.7 4.7 %collective-permute-start.27 = (f32[64]{0:T(128)S(1)}, f32[64]{0:T(128)S(1)}, u32[]{:S(2)}, u32[]{:S(2)}) collective-permute-start(f32[64]{0:T(128)S(1)} %multiply_reduce_fusion), channel_id=1, source_target_pairs={{0,1},{1,0},{2,3},{3,2},{4,5},{5,4},{6,7},{7,6},{8,9},{9,8},{10,11... | collective-permute-start | bytes 776 | tf_op jit(solution)/shard_map/ppermute | solution.py:420
  164.3 2.2 %copy-start.3 = (bf16[64,256,128]{2,1,0:T(8,128)(2,1)S(1)}, bf16[64,256,128]{2,1,0:T(8,128)(2,1)}, u32[]{:S(2)}) copy-start(bf16[64,256,128]{2,1,0:T(8,128)(2,1)} %copy-done.2) | copy-start | bytes 12582916
  (4 other events, 2.6 us)

commit v11 on v10

--- a/solution.py
+++ b/solution.py
@@ -373,7 +373,8 @@
     )(*operands, *held)
 
 
-def density_kernel(start, t, d):
+def density_kernel(start, t, *refs):
+    d = refs[-1]
     count, half = d.shape[:2]
     per_orb = t.shape[0] // count
     first = pl.multiple_of(start[0], half)
@@ -381,10 +382,11 @@
         own = range(o * per_orb, (o + 1) * per_orb)
         left = jnp.concatenate([t[k, pl.ds(first, half), :] for k in own], axis=1)
         right = jnp.concatenate([t[k] for k in own], axis=1)
-        d[o] = lax.dot_general(left, right, (((1,), (1,)), ((), ())), preferred_element_type=f32)
-
-
-def density_rows(t_all, start, per_orb, half):
+        rows = lax.dot_general(left, right, (((1,), (1,)), ((), ())), preferred_element_type=f32)
+        d[o] = rows if len(refs) == 1 else rows + refs[0][o]
+
+
+def density_rows(t_all, start, per_orb, half, *away):
     npair, nvd, width = t_all.shape
     occ = npair // per_orb
     step = 4 if occ % 4 == 0 else 1
@@ -394,13 +396,14 @@
         grid_spec=pltpu.PrefetchScalarGridSpec(
             num_scalar_prefetch=1,
             grid=(occ // step,),
-            in_specs=[pl.BlockSpec((step * per_orb, nvd, width), lambda i, s: (i, 0, 0))],
+            in_specs=[pl.BlockSpec((step * per_orb, nvd, width), lambda i, s: (i, 0, 0))]
+            + [pl.BlockSpec((step, half, nvd), lambda i, s: (i, 0, 0))] * len(away),
             out_specs=pl.BlockSpec((step, half, nvd), lambda i, s: (i, 0, 0)),
         ),
         compiler_params=pltpu.CompilerParams(vmem_limit_bytes=LIMIT),
         cost_estimate=TINY,
         name="density_rows",
-    )(start.reshape(1), t_all)
+    )(start.reshape(1), t_all, *away)
 
 
 def line_plan(blocks, vir_energy, occ_energy, domain_size, partner_owner, partner_slot):
@@ -472,28 +475,26 @@
     ready_2 = pp(gone, outward)
     held = own_pairs(1, "slots", [near], held, (gone, third_diagonal))
     held = own_pairs(5, "asked", [beside_near], held)
-    fourth_diagonal, fourth = [], []
-
-    def send_far(q, token):
-        jobs = [(1, 3, far[q : q + 1], True), (0, 3, far[q : q + 1], True)]
-        packed = pack(lists_of, jobs, cap, after=(token,))
-        fourth_diagonal.append(pp(packed[0], diagonal))
-        fourth.append(pp(packed[1], y_middle))
-        return packed[0]
-
-    packed = send_far(0, held[1])
-    held = own_pairs(2, "served", [mid], held, (packed,), (ready_2,))
-    held = own_pairs(
-        6, "asked", [[third], [third_diagonal]], held, (fourth[0], fourth_diagonal[0])
-    )
-    packed = send_far(1, held[1])
+    jobs = [(1, 3, far[:1], True), (0, 3, far[:1], True)]
+    packed = pack(lists_of, jobs, cap, after=(held[1],))
+    fourth_diagonal, fourth = [pp(packed[0], diagonal)], [pp(packed[1], y_middle)]
+    held = own_pairs(2, "served", [mid], held, (packed[0],), (ready_2,))
+    (packed,) = pack(lists_of, [(1, 3, far[1:], True)], cap, after=(held[1],))
+    fourth_diagonal.append(pp(packed, diagonal))
     gone = amplitudes("client", 3, per_orb, client, client_left, [far], cap, after=(packed,))
     ready_3 = pp(gone, outward)
-    held = own_pairs(7, "asked", [fourth, fourth_diagonal], held, (gone,))
-    t_all, e_all = own_pairs(3, "served", [far], held, ready=(ready_3,))
+    (packed,) = pack(
+        lists_of, [(0, 3, far[1:], True)], cap, after=(gone,)
+    )
+    fourth.append(pp(packed, y_middle))
+    held = own_pairs(
+        6, "asked", [[third], [third_diagonal]], held, (packed, fourth[0], *fourth_diagonal)
+    )
+    held = own_pairs(3, "served", [far], held, ready=(ready_3,))
+    t_all, e_all = own_pairs(7, "asked", [fourth, fourth_diagonal], held)
 
     away = swap_core(density_rows(t_all, (1 - core) * half, per_orb, half))
-    density = density_rows(t_all, core * half, per_orb, half) + away
+    density = density_rows(t_all, core * half, per_orb, half, away)
 
     energy = jnp.sum(hit * jnp.sum(e_all, axis=1)[None, :], axis=1)
     energy = (energy + swap_core(energy)) / nvd

time: 173 us -> 177 us (1.023)
  Pallas kernels: 31.7 us -> 37.1 us
  other arithmetic: 4.14 us -> 0.81 us
  local copies, waits for them, and re-layouts: 14.7 us -> 16.9 us
    ppermute x24, waiting for transfers between devices: 89.7 us -> 84.8 us  [pp(): return lax.ppermute(x, 'orb', perm)]
    add x1 -> x0, other arithmetic: 3.33 us -> none  [line_plan(): density = density_rows(t_all, core * half, per_orb, half) + away]
    ppermute x5, waiting for transfers between devices: 0.01 us -> 3.33 us  [swap_core(): return lax.ppermute(x, 'aux', [(0, 1), (1, 0)])]
    pallas_call x2, Pallas kernels: 3.88 us -> 6.6 us  [density_rows(): pl.pallas_call(density_kernel, out_shape=jax.ShapeDtypeStruct((occ, half,...]
    pallas_call x6 -> x7, Pallas kernels: 6.9 us -> 9.23 us  [pack(): pl.pallas_call(lambda *refs: pack_kernel(kinds, len(tbls), *refs), out_sh...]
    unnamed x46, local copies, waits for them, and re-layouts: 11 us -> 13.2 us
  transfers between devices with their start and end apart: 29 -> 29, of which waited for: 9 -> 10; matrix products, arithmetic and copies ran while one was open for 3% -> 3% of each run, Pallas kernels for 15% -> 16%
where the time goes in v11:
time: 177 us; the launch traced here: 176 us
  waiting for transfers between devices  88.1 us (50%)
  Pallas kernels  37.1 us (21%)
  starting transfers between devices  31.5 us (18%)
  local copies, waits for them, and re-layouts  16.9 us (10%)
    ppermute x24, waiting for transfers between devices, pp(): return lax.ppermute(x, 'orb', perm)  84.8 us
    ppermute x24, starting transfers between devices, pp(): return lax.ppermute(x, 'orb', perm)  30.4 us
    pallas_call x10, Pallas kernels, amplitudes(): pl.pallas_call(lambda *refs: amplitudes_kernel(mode, call, per_orb, [len(...  15.6 us
    unnamed x46, local copies, waits for them, and re-layouts  13.2 us
    pallas_call x7, Pallas kernels, pack(): pl.pallas_call(lambda *refs: pack_kernel(kinds, len(tbls), *refs), out_sh...  9.23 us
    pallas_call x2, Pallas kernels, density_rows(): pl.pallas_call(density_kernel, out_shape=jax.ShapeDtypeStruct((occ, half,...  6.6 us
    pallas_call x2, Pallas kernels, turn(): pl.pallas_call(turn_kernel, out_shape=[jax.ShapeDtypeStruct((count, cols,...  4.25 us
  transfers between devices with their start and end apart: 29, of which 10 were waited for; matrix products, arithmetic and copies ran while one was open for 3% of the time, Pallas kernels for 16%

profile of v11, /device:TPU:0, one launch (start us, length us, event | category | flops | bytes accessed | tf_op | source)
XLA Modules:
  0.0 175.5 jit_solution(9299498493414960539)
XLA Ops:
  4.7 2.6 %collective-permute-start = (f32[24,384]{1,0:T(8,128)S(1)}, f32[24,384]{1,0:T(8,128)S(1)}, u32[]{:S(2)}, u32[]{:S(2)}) collective-permute-start(f32[24,384]{1,0:T(8,128)S(1)} %get-tuple-element.53.refs_1_), channel_id=1, source_target_pairs={{0,2},{2,0},{4,6},{6,4},{8,10},{10,8},{12,14},{14,12},{1,3},{3,1},... | collective-permute-start | bytes 110600 | tf_op jit(solution)/shard_map/ppermute | solution.py:420
  7.3 1.6 collective-permute-start.1
  8.9 3.0 %collective-permute-start.3 = (f32[24,384]{1,0:T(8,128)S(1)}, f32[24,384]{1,0:T(8,128)S(1)}, u32[]{:S(2)}, u32[]{:S(2)}) collective-permute-start(f32[24,384]{1,0:T(8,128)S(1)} %get-tuple-element.53.refs_1_), channel_id=1, source_target_pairs={{0,8},{2,10},{4,12},{6,14},{8,0},{10,2},{12,4},{14,6},{1,9},{3,11}... | collective-permute-start | bytes 110600 | tf_op jit(solution)/shard_map/ppermute | solution.py:420
  11.8 1.4 collective-permute-start.4
  13.3 3.5 %collective-permute-start.5 = (f32[24,384]{1,0:T(8,128)S(1)}, f32[24,384]{1,0:T(8,128)S(1)}, u32[]{:S(2)}, u32[]{:S(2)}) collective-permute-start(f32[24,384]{1,0:T(8,128)S(1)} %get-tuple-element.53.refs_1_), channel_id=1, source_target_pairs={{0,12},{2,14},{4,8},{6,10},{8,4},{10,6},{12,0},{14,2},{1,13},{3,15... | collective-permute-start | bytes 110600 | tf_op jit(solution)/shard_map/ppermute | solution.py:420
  17.0 2.3 %constant_dynamic-slice_fusion.1.refs_2_.refs_5_ = bf16[16,256,128]{2,1,0:T(8,128)(2,1)} fusion(bf16[16,256,256]{2,1,0:T(8,128)(2,1)} %refs_0_.3, s32[]{:T(128)S(6)} %select_n.4), kind=kLoop, calls=%fused_computation.4 | loop fusion | bytes 2097156 | tf_op jit(solution)/shard_map/dynamic_slice | solution.py:437
  19.4 4.0 %collective-permute-done.6.refs_8_ = f32[24,384]{1,0:T(8,128)S(1)} collective-permute-done((f32[24,384]{1,0:T(8,128)S(1)}, f32[24,384]{1,0:T(8,128)S(1)}, u32[]{:S(2)}, u32[]{:S(2)}) %collective-permute-start.6) | collective-permute-done | bytes 36896 | tf_op jit(solution)/shard_map/ppermute | solution.py:420
  24.2 1.3 tables.1
  25.7 1.5 pack.7.refs_7_
  27.8 3.2 %collective-permute-start.12 = (bf16[16,256,128]{2,1,0:T(8,128)(2,1)S(1)}, bf16[16,256,128]{2,1,0:T(8,128)(2,1)S(1)}, u32[]{:S(2)}, u32[]{:S(2)}) collective-permute-start(bf16[16,256,128]{2,1,0:T(8,128)(2,1)S(1)} %constant_dynamic-slice_fusion.refs_3_.refs_6_), channel_id=1, source_target_pairs={{0,4},{2,6},{4,0},{6,2},{8,12},{10,14},{12,8},{14,10},{1,5},{3,7},... | collective-permute-start | bytes 3145736 | tf_op jit(solution)/shard_map/ppermute | solution.py:420
  31.7 1.3 turn.2
  33.7 2.8 %amplitudes.10 = (bf16[64,256,128]{2,1,0:T(8,128)(2,1)S(1)}, f32[64,128]{1,0:T(8,128)S(1)}) custom-call(s32[8,128]{1,0:T(8,128)S(1)} %get-tuple-element.61.refs_0_, f32[64,128]{1,0:T(8,128)S(1)} %get-tuple-element.62.refs_1_, f32[16,256,128]{2,1,0:T(8,128)S(1)} %broadcast_in_dim.4.refs_2_, bf16[16,256,256]{2,1,0:T(8,128)(2,1)S(1)} %get-tuple-element.63.refs_3_, ...), custom_call_target="tpu_custom_call" | custom-call | flops 1 | bytes 1 | tf_op jit(solution)/shard_map/amplitudes/pallas_call | solution.py:364
  36.5 13.4 %collective-permute-done.8.refs_2_.refs_0_.refs_5_ = bf16[16,256,128]{2,1,0:T(8,128)(2,1)} collective-permute-done((bf16[16,256,128]{2,1,0:T(8,128)(2,1)}, bf16[16,256,128]{2,1,0:T(8,128)(2,1)}, u32[]{:S(2)}, u32[]{:S(2)}) %collective-permute-start.8) | collective-permute-done | bytes 1048608 | tf_op jit(solution)/shard_map/ppermute | solution.py:420
  49.8 1.3 pack.8.refs_6_
  51.7 9.6 %collective-permute-done.11.refs_7_.refs_5_ = bf16[1,8,256,128]{3,2,1,0:T(8,128)(2,1)S(1)} collective-permute-done((bf16[1,8,256,128]{3,2,1,0:T(8,128)(2,1)S(1)}, bf16[1,8,256,128]{3,2,1,0:T(8,128)(2,1)S(1)}, u32[]{:S(2)}, u32[]{:S(2)}) %collective-permute-start.11) | collective-permute-done | bytes 524320 | tf_op jit(solution)/shard_map/ppermute | solution.py:420
  61.2 1.3 amplitudes.11
  62.5 6.3 %collective-permute-done.12.refs_2_.refs_1_.refs_6_ = bf16[16,256,128]{2,1,0:T(8,128)(2,1)S(1)} collective-permute-done((bf16[16,256,128]{2,1,0:T(8,128)(2,1)S(1)}, bf16[16,256,128]{2,1,0:T(8,128)(2,1)S(1)}, u32[]{:S(2)}, u32[]{:S(2)}) %collective-permute-start.12) | collective-permute-done | bytes 1048608 | tf_op jit(solution)/shard_map/ppermute | solution.py:420
  69.5 1.3 collective-permute-start.18
  74.3 2.9 %turn.3 = (bf16[16,128,256]{2,1,0:T(8,128)(2,1)S(1)}, bf16[16,128,256]{2,1,0:T(8,128)(2,1)S(1)}, bf16[16,128,256]{2,1,0:T(8,128)(2,1)S(1)}, bf16[16,128,256]{2,1,0:T(8,128)(2,1)S(1)}) custom-call(bf16[16,256,128]{2,1,0:T(8,128)(2,1)} %collective-permute-done.8.refs_2_.refs_0_.refs_5_, ...), custom_call_target="tpu_custom_call" | custom-call | flops 1 | bytes 1 | tf_op jit(solution)/shard_map/turn/pallas_call | solution.py:256
  78.4 19.5 %collective-permute-done.18.refs_8_.refs_6_ = bf16[2,8,256,128]{3,2,1,0:T(8,128)(2,1)S(1)} collective-permute-done((bf16[2,8,256,128]{3,2,1,0:T(8,128)(2,1)S(1)}, bf16[2,8,256,128]{3,2,1,0:T(8,128)(2,1)S(1)}, u32[]{:S(2)}, u32[]{:S(2)}) %collective-permute-start.18) | collective-permute-done | bytes 1048608 | tf_op jit(solution)/shard_map/ppermute | solution.py:420
  98.0 1.3 collective-permute-start.21
  99.2 2.0 %amplitudes.13 = (bf16[64,256,128]{2,1,0:T(8,128)(2,1)S(1)}, f32[64,128]{1,0:T(8,128)S(1)}) custom-call(s32[8,128]{1,0:T(8,128)S(1)} %get-tuple-element.61.refs_0_, f32[64,128]{1,0:T(8,128)S(1)} %get-tuple-element.62.refs_1_, f32[16,256,128]{2,1,0:T(8,128)S(1)} %broadcast_in_dim.4.refs_2_, ...), custom_call_target="tpu_custom_call", output_to_operand_aliasing={{0}: (9, {}), {1}: (10, {})} | custom-call | flops 1 | bytes 1 | tf_op jit(solution)/shard_map/amplitudes/pallas_call | solution.py:364
  101.2 7.9 %collective-permute-done.15.refs_6_ = bf16[1,8,256,128]{3,2,1,0:T(8,128)(2,1)S(1)} collective-permute-done((bf16[1,8,256,128]{3,2,1,0:T(8,128)(2,1)S(1)}, bf16[1,8,256,128]{3,2,1,0:T(8,128)(2,1)S(1)}, u32[]{:S(2)}, u32[]{:S(2)}) %collective-permute-start.15) | collective-permute-done | bytes 524320 | tf_op jit(solution)/shard_map/ppermute | solution.py:420
  109.1 1.3 amplitudes.14
  110.4 1.7 pack.11
  112.1 1.4 collective-permute-start.19
  113.5 1.3 collective-permute-start.23
  114.8 0.9 amplitudes.15
  115.8 2.0 %pack.12.refs_9_ = bf16[1,8,256,128]{3,2,1,0:T(8,128)(2,1)} custom-call(s32[8,128]{1,0:T(8,128)S(1)} %get-tuple-element.65.refs_0_, s32[8,128]{1,0:T(8,128)S(1)} %get-tuple-element.66.refs_1_, bf16[16,256,128]{2,1,0:T(8,128)(2,1)S(1)} %collective-permute-done.20.refs_2_.refs_8_.refs_6_, f32[64,128]{1,0:T(8,128)S(1)} %get-tuple-element.91.refs_3_.refs_12_), custom_call_target="tpu_custom_call" | custom-call | flops 1 | bytes 1 | tf_op jit(solution)/shard_map/pack/pallas_call | solution.py:234
  117.8 1.3 collective-permute-start.24
  119.1 1.4 amplitudes.16.refs_3_
  120.5 1.4 collective-permute-start.25
  121.9 1.5 pack.13.refs_7_
  123.4 1.0 copy-done.15
  124.4 1.5 collective-permute-start.22
  125.9 12.1 %collective-permute-done.23.refs_9_.refs_7_ = bf16[1,8,256,128]{3,2,1,0:T(8,128)(2,1)} collective-permute-done((bf16[1,8,256,128]{3,2,1,0:T(8,128)(2,1)}, bf16[1,8,256,128]{3,2,1,0:T(8,128)(2,1)}, u32[]{:S(2)}, u32[]{:S(2)}) %collective-permute-start.23) | collective-permute-done | bytes 524320 | tf_op jit(solution)/shard_map/ppermute | solution.py:420
  138.0 11.2 %collective-permute-done.24.refs_10_.refs_8_ = bf16[1,8,256,128]{3,2,1,0:T(8,128)(2,1)} collective-permute-done((bf16[1,8,256,128]{3,2,1,0:T(8,128)(2,1)}, bf16[1,8,256,128]{3,2,1,0:T(8,128)(2,1)}, u32[]{:S(2)}, u32[]{:S(2)}) %collective-permute-start.24) | collective-permute-done | bytes 524320 | tf_op jit(solution)/shard_map/ppermute | solution.py:420
  149.3 2.2 %copy-done.1 = bf16[64,256,128]{2,1,0:T(8,128)(2,1)S(1)} copy-done((bf16[64,256,128]{2,1,0:T(8,128)(2,1)S(1)}, bf16[64,256,128]{2,1,0:T(8,128)(2,1)}, u32[]{:S(2)}) %copy-start.1) | copy-done | bytes 4194328
  151.5 1.6 copy-done.5
  153.0 1.6 copy-done.7
  154.6 1.2 copy-done.16
  155.9 1.4 amplitudes.17
  158.1 1.5 amplitudes.18
  159.7 2.3 %amplitudes.19 = (bf16[64,256,128]{2,1,0:T(8,128)(2,1)S(1)}, f32[64,128]{1,0:T(8,128)S(1)}) custom-call(s32[8,128]{1,0:T(8,128)S(1)} %get-tuple-element.61.refs_0_, f32[64,128]{1,0:T(8,128)S(1)} %get-tuple-element.62.refs_1_, f32[16,256,128]{2,1,0:T(8,128)S(1)} %broadcast_in_dim.4.refs_2_, ...), custom_call_target="tpu_custom_call", output_to_operand_aliasing={{0}: (9, {}), {1}: (10, {})} | custom-call | flops 1 | bytes 1 | tf_op jit(solution)/shard_map/amplitudes/pallas_call | solution.py:364
  162.0 1.9 %density_rows.2 = f32[16,128,256]{2,1,0:T(8,128)S(1)} custom-call(s32[1]{0:T(128)} %bitcast.6.start, bf16[64,256,128]{2,1,0:T(8,128)(2,1)S(1)} %get-tuple-element.99.t), custom_call_target="tpu_custom_call" | custom-call | flops 1 | bytes 1 | tf_op jit(solution)/shard_map/density_rows/pallas_call | solution.py:393
  164.8 3.3 %collective-permute-done.27 = f32[64]{0:T(128)S(1)} collective-permute-done((f32[64]{0:T(128)S(1)}, f32[64]{0:T(128)S(1)}, u32[]{:S(2)}, u32[]{:S(2)}) %collective-permute-start.27) | collective-permute-done | bytes 288 | tf_op jit(solution)/shard_map/ppermute | solution.py:423
  168.7 2.2 %copy-done.3 = bf16[64,256,128]{2,1,0:T(8,128)(2,1)S(1)} copy-done((bf16[64,256,128]{2,1,0:T(8,128)(2,1)S(1)}, bf16[64,256,128]{2,1,0:T(8,128)(2,1)}, u32[]{:S(2)}) %copy-start.3) | copy-done | bytes 4194328
  170.9 4.7 %density_rows.3 = f32[16,128,256]{2,1,0:T(8,128)} custom-call(s32[1]{0:T(128)} %bitcast.5.start, bf16[64,256,128]{2,1,0:T(8,128)(2,1)S(1)} %copy-done.3, f32[16,128,256]{2,1,0:T(8,128)} %collective-permute-done.28.refs_0_), custom_call_target="tpu_custom_call" | custom-call | flops 1 | bytes 1 | tf_op jit(solution)/shard_map/density_rows/pallas_call | solution.py:393
  (88 shorter events, 15.5 us)
Async XLA Ops:
  0.6 24.9 %collective-permute-start.7 = (bf16[16,256,256]{2,1,0:T(8,128)(2,1)}, bf16[16,256,256]{2,1,0:T(8,128)(2,1)S(1)}, u32[]{:S(2)}, u32[]{:S(2)}) collective-permute-start(bf16[16,256,256]{2,1,0:T(8,128)(2,1)} %refs_0_.3), channel_id=1, source_target_pairs={{0,1},{1,0},{2,3},{3,2},{4,5},{5,4},{6,7},{7,6},{8,9},{9,8},{10,11... | collective-permute-start | bytes 6291464 | tf_op jit(solution)/shard_map/ppermute | solution.py:423
  1.1 0.7 copy-start.17
  4.7 7.2 %collective-permute-start = (f32[24,384]{1,0:T(8,128)S(1)}, f32[24,384]{1,0:T(8,128)S(1)}, u32[]{:S(2)}, u32[]{:S(2)}) collective-permute-start(f32[24,384]{1,0:T(8,128)S(1)} %get-tuple-element.53.refs_1_), channel_id=1, source_target_pairs={{0,2},{2,0},{4,6},{6,4},{8,10},{10,8},{12,14},{14,12},{1,3},{3,1},... | collective-permute-start | bytes 110600 | tf_op jit(solution)/shard_map/ppermute | solution.py:420
  7.3 6.0 %collective-permute-start.1 = (f32[24,384]{1,0:T(8,128)S(1)}, f32[24,384]{1,0:T(8,128)S(1)}, u32[]{:S(2)}, u32[]{:S(2)}) collective-permute-start(f32[24,384]{1,0:T(8,128)S(1)} %get-tuple-element.53.refs_1_), channel_id=1, source_target_pairs={{0,4},{2,6},{4,0},{6,2},{8,12},{10,14},{12,8},{14,10},{1,5},{3,7},... | collective-permute-start | bytes 110600 | tf_op jit(solution)/shard_map/ppermute | solution.py:420
  8.8 7.9 %collective-permute-start.2 = (f32[24,384]{1,0:T(8,128)S(1)}, f32[24,384]{1,0:T(8,128)S(1)}, u32[]{:S(2)}, u32[]{:S(2)}) collective-permute-start(f32[24,384]{1,0:T(8,128)S(1)} %get-tuple-element.53.refs_1_), channel_id=1, source_target_pairs={{0,6},{2,4},{4,2},{6,0},{8,14},{10,12},{12,10},{14,8},{1,7},{3,5},... | collective-permute-start | bytes 110600 | tf_op jit(solution)/shard_map/ppermute | solution.py:420
  8.9 10.5 %collective-permute-start.3 = (f32[24,384]{1,0:T(8,128)S(1)}, f32[24,384]{1,0:T(8,128)S(1)}, u32[]{:S(2)}, u32[]{:S(2)}) collective-permute-start(f32[24,384]{1,0:T(8,128)S(1)} %get-tuple-element.53.refs_1_), channel_id=1, source_target_pairs={{0,8},{2,10},{4,12},{6,14},{8,0},{10,2},{12,4},{14,6},{1,9},{3,11}... | collective-permute-start | bytes 110600 | tf_op jit(solution)/shard_map/ppermute | solution.py:420
  11.8 7.5 %collective-permute-start.4 = (f32[24,384]{1,0:T(8,128)S(1)}, f32[24,384]{1,0:T(8,128)S(1)}, u32[]{:S(2)}, u32[]{:S(2)}) collective-permute-start(f32[24,384]{1,0:T(8,128)S(1)} %get-tuple-element.53.refs_1_), channel_id=1, source_target_pairs={{0,10},{2,8},{4,14},{6,12},{8,2},{10,0},{12,6},{14,4},{1,11},{3,9}... | collective-permute-start | bytes 110600 | tf_op jit(solution)/shard_map/ppermute | solution.py:420
  13.3 6.1 %collective-permute-start.5 = (f32[24,384]{1,0:T(8,128)S(1)}, f32[24,384]{1,0:T(8,128)S(1)}, u32[]{:S(2)}, u32[]{:S(2)}) collective-permute-start(f32[24,384]{1,0:T(8,128)S(1)} %get-tuple-element.53.refs_1_), channel_id=1, source_target_pairs={{0,12},{2,14},{4,8},{6,10},{8,4},{10,6},{12,0},{14,2},{1,13},{3,15... | collective-permute-start | bytes 110600 | tf_op jit(solution)/shard_map/ppermute | solution.py:420
  16.7 6.7 %collective-permute-start.6 = (f32[24,384]{1,0:T(8,128)S(1)}, f32[24,384]{1,0:T(8,128)S(1)}, u32[]{:S(2)}, u32[]{:S(2)}) collective-permute-start(f32[24,384]{1,0:T(8,128)S(1)} %get-tuple-element.53.refs_1_), channel_id=1, source_target_pairs={{0,14},{2,12},{4,10},{6,8},{8,6},{10,4},{12,2},{14,0},{1,15},{3,13... | collective-permute-start | bytes 110600 | tf_op jit(solution)/shard_map/ppermute | solution.py:420
  23.4 26.4 %collective-permute-start.8 = (bf16[16,256,128]{2,1,0:T(8,128)(2,1)}, bf16[16,256,128]{2,1,0:T(8,128)(2,1)}, u32[]{:S(2)}, u32[]{:S(2)}) collective-permute-start(bf16[16,256,128]{2,1,0:T(8,128)(2,1)} %constant_dynamic-slice_fusion.1.refs_2_.refs_5_), channel_id=1, source_target_pairs={{0,4},{2,6},{4,0},{6,2},{8,12},{10,14},{12,8},{14,10},{1,5},{3,7},... | collective-permute-start | bytes 3145736 | tf_op jit(solution)/shard_map/ppermute | solution.py:420
  23.4 26.4 %collective-permute-start.10 = (bf16[16,256,128]{2,1,0:T(8,128)(2,1)}, bf16[16,256,128]{2,1,0:T(8,128)(2,1)S(1)}, u32[]{:S(2)}, u32[]{:S(2)}) collective-permute-start(bf16[16,256,128]{2,1,0:T(8,128)(2,1)} %constant_dynamic-slice_fusion.1.refs_2_.refs_5_), channel_id=1, source_target_pairs={{4,8},{6,10},{8,4},{10,6},{5,9},{7,11},{9,5},{11,7},{20,24},{22,26... | collective-permute-start | bytes 3145736 | tf_op jit(solution)/shard_map/ppermute | solution.py:420
  25.7 6.0 %copy-start.12 = (bf16[16,256,256]{2,1,0:T(8,128)(2,1)S(1)}, bf16[16,256,256]{2,1,0:T(8,128)(2,1)}, u32[]{:S(2)}) copy-start(bf16[16,256,256]{2,1,0:T(8,128)(2,1)} %refs_0_.3) | copy-start | bytes 6291460
  27.2 5.9 %copy-start.18 = (f32[16,256]{1,0:T(8,128)S(1)}, f32[16,256]{1,0:T(8,128)}, u32[]{:S(2)}) copy-start(f32[16,256]{1,0:T(8,128)} %refs_0_.2) | copy-start | bytes 49156
  27.2 34.0 %collective-permute-start.13 = (bf16[2,8,256,128]{3,2,1,0:T(8,128)(2,1)S(1)}, bf16[2,8,256,128]{3,2,1,0:T(8,128)(2,1)S(1)}, u32[]{:S(2)}, u32[]{:S(2)}) collective-permute-start(bf16[2,8,256,128]{3,2,1,0:T(8,128)(2,1)S(1)} %pack.7.refs_7_), channel_id=1, source_target_pairs={{0,2},{2,0},{4,6},{6,4},{8,10},{10,8},{12,14},{14,12},{1,3},{3,1},... | collective-permute-start | bytes 3145736 | tf_op jit(solution)/shard_map/ppermute | solution.py:420
  27.8 41.0 %collective-permute-start.12 = (bf16[16,256,128]{2,1,0:T(8,128)(2,1)S(1)}, bf16[16,256,128]{2,1,0:T(8,128)(2,1)S(1)}, u32[]{:S(2)}, u32[]{:S(2)}) collective-permute-start(bf16[16,256,128]{2,1,0:T(8,128)(2,1)S(1)} %constant_dynamic-slice_fusion.refs_3_.refs_6_), channel_id=1, source_target_pairs={{0,4},{2,6},{4,0},{6,2},{8,12},{10,14},{12,8},{14,10},{1,5},{3,7},... | collective-permute-start | bytes 3145736 | tf_op jit(solution)/shard_map/ppermute | solution.py:420
  31.0 37.8 %collective-permute-start.14 = (bf16[16,256,128]{2,1,0:T(8,128)(2,1)S(1)}, bf16[16,256,128]{2,1,0:T(8,128)(2,1)S(1)}, u32[]{:S(2)}, u32[]{:S(2)}) collective-permute-start(bf16[16,256,128]{2,1,0:T(8,128)(2,1)S(1)} %constant_dynamic-slice_fusion.refs_3_.refs_6_), channel_id=1, source_target_pairs={{4,8},{6,10},{8,4},{10,6},{5,9},{7,11},{9,5},{11,7},{20,24},{22,26... | collective-permute-start | bytes 3145736 | tf_op jit(solution)/shard_map/ppermute | solution.py:420
  33.1 81.8 %copy-start.4 = (bf16[16,256,256]{2,1,0:T(8,128)(2,1)}, bf16[16,256,256]{2,1,0:T(8,128)(2,1)S(1)}, u32[]{:S(2)}) copy-start(bf16[16,256,256]{2,1,0:T(8,128)(2,1)S(1)} %get-tuple-element.63.refs_3_) | copy-start | bytes 6291460
  33.1 81.8 %copy-start.6 = (bf16[16,256,256]{2,1,0:T(8,128)(2,1)}, bf16[16,256,256]{2,1,0:T(8,128)(2,1)S(1)}, u32[]{:S(2)}) copy-start(bf16[16,256,256]{2,1,0:T(8,128)(2,1)S(1)} %get-tuple-element.64.refs_4_) | copy-start | bytes 6291460
  51.1 10.1 %collective-permute-start.11 = (bf16[1,8,256,128]{3,2,1,0:T(8,128)(2,1)S(1)}, bf16[1,8,256,128]{3,2,1,0:T(8,128)(2,1)S(1)}, u32[]{:S(2)}, u32[]{:S(2)}) collective-permute-start(bf16[1,8,256,128]{3,2,1,0:T(8,128)(2,1)S(1)} %pack.8.refs_6_), channel_id=1, source_target_pairs={{0,2},{2,0},{4,6},{6,4},{8,10},{10,8},{12,14},{14,12},{1,3},{3,1},... | collective-permute-start | bytes 1572872 | tf_op jit(solution)/shard_map/ppermute | solution.py:420
  51.7 20.6 %collective-permute-start.16 = (bf16[16,256,128]{2,1,0:T(8,128)(2,1)}, bf16[16,256,128]{2,1,0:T(8,128)(2,1)S(1)}, u32[]{:S(2)}, u32[]{:S(2)}) collective-permute-start(bf16[16,256,128]{2,1,0:T(8,128)(2,1)} %collective-permute-done.8.refs_2_.refs_0_.refs_5_), channel_id=1, source_target_pairs={{0,1},{1,0},{2,3},{3,2},{4,5},{5,4},{6,7},{7,6},{8,9},{9,8},{10,11... | collective-permute-start | bytes 3145736 | tf_op jit(solution)/shard_map/ppermute | solution.py:423
  68.8 4.9 %collective-permute-start.17 = (bf16[16,256,128]{2,1,0:T(8,128)(2,1)S(1)}, bf16[16,256,128]{2,1,0:T(8,128)(2,1)S(1)}, u32[]{:S(2)}, u32[]{:S(2)}) collective-permute-start(bf16[16,256,128]{2,1,0:T(8,128)(2,1)S(1)} %collective-permute-done.12.refs_2_.refs_1_.refs_6_), channel_id=1, source_target_pairs={{0,1},{1,0},{2,3},{3,2},{4,5},{5,4},{6,7},{7,6},{8,9},{9,8},{10,11... | collective-permute-start | bytes 3145736 | tf_op jit(solution)/shard_map/ppermute | solution.py:423
  69.5 28.5 %collective-permute-start.18 = (bf16[2,8,256,128]{3,2,1,0:T(8,128)(2,1)S(1)}, bf16[2,8,256,128]{3,2,1,0:T(8,128)(2,1)S(1)}, u32[]{:S(2)}, u32[]{:S(2)}) collective-permute-start(bf16[2,8,256,128]{3,2,1,0:T(8,128)(2,1)S(1)} %get-tuple-element.77.refs_3_), channel_id=1, source_target_pairs={{4,2},{6,0},{8,14},{10,12},{5,3},{7,1},{9,15},{11,13},{20,18},{22,... | collective-permute-start | bytes 3145736 | tf_op jit(solution)/shard_map/ppermute | solution.py:420
  70.8 39.6 %collective-permute-start.9 = (bf16[16,256,128]{2,1,0:T(8,128)(2,1)}, bf16[16,256,128]{2,1,0:T(8,128)(2,1)S(1)}, u32[]{:S(2)}, u32[]{:S(2)}) collective-permute-start(bf16[16,256,128]{2,1,0:T(8,128)(2,1)} %collective-permute-done.8.refs_2_.refs_0_.refs_5_), channel_id=1, source_target_pairs={{4,8},{6,10},{8,4},{10,6},{5,9},{7,11},{9,5},{11,7},{20,24},{22,26... | collective-permute-start | bytes 3145736 | tf_op jit(solution)/shard_map/ppermute | solution.py:420
  71.5 44.3 %collective-permute-start.20 = (bf16[16,256,128]{2,1,0:T(8,128)(2,1)S(1)}, bf16[16,256,128]{2,1,0:T(8,128)(2,1)S(1)}, u32[]{:S(2)}, u32[]{:S(2)}) collective-permute-start(bf16[16,256,128]{2,1,0:T(8,128)(2,1)S(1)} %collective-permute-done.12.refs_2_.refs_1_.refs_6_), channel_id=1, source_target_pairs={{4,8},{6,10},{8,4},{10,6},{5,9},{7,11},{9,5},{11,7},{20,24},{22,26... | collective-permute-start | bytes 3145736 | tf_op jit(solution)/shard_map/ppermute | solution.py:420
  72.3 51.1 %collective-permute-start.26 = (bf16[2,8,256,128]{3,2,1,0:T(8,128)(2,1)S(1)}, bf16[2,8,256,128]{3,2,1,0:T(8,128)(2,1)S(1)}, u32[]{:S(2)}, u32[]{:S(2)}) collective-permute-start(bf16[2,8,256,128]{3,2,1,0:T(8,128)(2,1)S(1)} %get-tuple-element.92), channel_id=1, source_target_pairs={{4,6},{6,4},{8,10},{10,8},{5,7},{7,5},{9,11},{11,9},{20,22},{22,20... | collective-permute-start | bytes 3145736 | tf_op jit(solution)/shard_map/ppermute | solution.py:420
  73.7 35.4 %collective-permute-start.15 = (bf16[1,8,256,128]{3,2,1,0:T(8,128)(2,1)S(1)}, bf16[1,8,256,128]{3,2,1,0:T(8,128)(2,1)S(1)}, u32[]{:S(2)}, u32[]{:S(2)}) collective-permute-start(bf16[1,8,256,128]{3,2,1,0:T(8,128)(2,1)S(1)} %pack.10.refs_9_), channel_id=1, source_target_pairs={{0,2},{2,0},{4,6},{6,4},{8,10},{10,8},{12,14},{14,12},{1,3},{3,1},... | collective-permute-start | bytes 1572872 | tf_op jit(solution)/shard_map/ppermute | solution.py:420
  98.0 3.3 %copy-start.13 = (bf16[2,8,256,128]{3,2,1,0:T(8,128)(2,1)}, bf16[2,8,256,128]{3,2,1,0:T(8,128)(2,1)S(1)}, u32[]{:S(2)}) copy-start(bf16[2,8,256,128]{3,2,1,0:T(8,128)(2,1)S(1)} %collective-permute-done.18.refs_8_.refs_6_) | copy-start | bytes 3145732
  98.0 16.9 %collective-permute-start.21 = (bf16[8,256,128]{2,1,0:T(8,128)(2,1)S(1)}, bf16[8,256,128]{2,1,0:T(8,128)(2,1)S(1)}, u32[]{:S(2)}, u32[]{:S(2)}) collective-permute-start(bf16[8,256,128]{2,1,0:T(8,128)(2,1)S(1)} %amplitudes.12.refs_7_), channel_id=1, source_target_pairs={{4,0},{6,2},{8,12},{10,14},{5,1},{7,3},{9,13},{11,15},{20,16},{22,... | collective-permute-start | bytes 1572872 | tf_op jit(solution)/shard_map/ppermute | solution.py:420
  110.4 8.7 %copy-start.8 = (bf16[16,256,128]{2,1,0:T(8,128)(2,1)}, bf16[16,256,128]{2,1,0:T(8,128)(2,1)S(1)}, u32[]{:S(2)}) copy-start(bf16[16,256,128]{2,1,0:T(8,128)(2,1)S(1)} %collective-permute-done.9.refs_2_.refs_3_.refs_7_.refs_5_) | copy-start | bytes 3145732
  112.1 13.8 %collective-permute-start.19 = (bf16[1,8,256,128]{3,2,1,0:T(8,128)(2,1)}, bf16[1,8,256,128]{3,2,1,0:T(8,128)(2,1)}, u32[]{:S(2)}, u32[]{:S(2)}) collective-permute-start(bf16[1,8,256,128]{3,2,1,0:T(8,128)(2,1)} %get-tuple-element.88), channel_id=1, source_target_pairs={{4,6},{6,4},{8,10},{10,8},{5,7},{7,5},{9,11},{11,9},{20,22},{22,20... | collective-permute-start | bytes 1572872 | tf_op jit(solution)/shard_map/ppermute | solution.py:420
  113.5 24.5 %collective-permute-start.23 = (bf16[1,8,256,128]{3,2,1,0:T(8,128)(2,1)}, bf16[1,8,256,128]{3,2,1,0:T(8,128)(2,1)}, u32[]{:S(2)}, u32[]{:S(2)}) collective-permute-start(bf16[1,8,256,128]{3,2,1,0:T(8,128)(2,1)} %get-tuple-element.89.refs_8_), channel_id=1, source_target_pairs={{4,2},{6,0},{8,14},{10,12},{5,3},{7,1},{9,15},{11,13},{20,18},{22,... | collective-permute-start | bytes 1572872 | tf_op jit(solution)/shard_map/ppermute | solution.py:420
  115.8 4.7 %copy-start = (bf16[64,256,128]{2,1,0:T(8,128)(2,1)}, bf16[64,256,128]{2,1,0:T(8,128)(2,1)S(1)}, u32[]{:S(2)}) copy-start(bf16[64,256,128]{2,1,0:T(8,128)(2,1)S(1)} %get-tuple-element.93.refs_11_) | copy-start | bytes 12582916
  115.8 6.1 %copy-start.10 = (bf16[16,256,128]{2,1,0:T(8,128)(2,1)}, bf16[16,256,128]{2,1,0:T(8,128)(2,1)S(1)}, u32[]{:S(2)}) copy-start(bf16[16,256,128]{2,1,0:T(8,128)(2,1)S(1)} %collective-permute-done.20.refs_2_.refs_8_.refs_6_) | copy-start | bytes 3145732
  117.8 31.5 %collective-permute-start.24 = (bf16[1,8,256,128]{3,2,1,0:T(8,128)(2,1)}, bf16[1,8,256,128]{3,2,1,0:T(8,128)(2,1)}, u32[]{:S(2)}, u32[]{:S(2)}) collective-permute-start(bf16[1,8,256,128]{3,2,1,0:T(8,128)(2,1)} %pack.12.refs_9_), channel_id=1, source_target_pairs={{4,2},{6,0},{8,14},{10,12},{5,3},{7,1},{9,15},{11,13},{20,18},{22,... | collective-permute-start | bytes 1572872 | tf_op jit(solution)/shard_map/ppermute | solution.py:420
  120.5 28.8 %copy-start.14 = (bf16[2,8,256,128]{3,2,1,0:T(8,128)(2,1)S(1)}, bf16[2,8,256,128]{3,2,1,0:T(8,128)(2,1)}, u32[]{:S(2)}) copy-start(bf16[2,8,256,128]{3,2,1,0:T(8,128)(2,1)} %copy-done.13) | copy-start | bytes 3145732
  120.5 37.6 %collective-permute-start.25 = (bf16[8,256,128]{2,1,0:T(8,128)(2,1)}, bf16[8,256,128]{2,1,0:T(8,128)(2,1)}, u32[]{:S(2)}, u32[]{:S(2)}) collective-permute-start(bf16[8,256,128]{2,1,0:T(8,128)(2,1)} %amplitudes.16.refs_3_), channel_id=1, source_target_pairs={{4,0},{6,2},{8,12},{10,14},{5,1},{7,3},{9,13},{11,15},{20,16},{22,... | collective-permute-start | bytes 1572872 | tf_op jit(solution)/shard_map/ppermute | solution.py:420
  123.4 1.0 copy-start.15
  124.4 35.3 %collective-permute-start.22 = (bf16[1,8,256,128]{3,2,1,0:T(8,128)(2,1)}, bf16[1,8,256,128]{3,2,1,0:T(8,128)(2,1)}, u32[]{:S(2)}, u32[]{:S(2)}) collective-permute-start(bf16[1,8,256,128]{3,2,1,0:T(8,128)(2,1)} %pack.13.refs_7_), channel_id=1, source_target_pairs={{4,6},{6,4},{8,10},{10,8},{5,7},{7,5},{9,11},{11,9},{20,22},{22,20... | collective-permute-start | bytes 1572872 | tf_op jit(solution)/shard_map/ppermute | solution.py:420
  149.3 2.2 %copy-start.1 = (bf16[64,256,128]{2,1,0:T(8,128)(2,1)S(1)}, bf16[64,256,128]{2,1,0:T(8,128)(2,1)}, u32[]{:S(2)}) copy-start(bf16[64,256,128]{2,1,0:T(8,128)(2,1)} %copy-done) | copy-start | bytes 12582916
  151.5 1.6 copy-start.5
  153.0 1.6 copy-start.7
  154.6 1.2 copy-start.16
  155.9 2.2 %copy-start.9 = (bf16[16,256,128]{2,1,0:T(8,128)(2,1)S(1)}, bf16[16,256,128]{2,1,0:T(8,128)(2,1)}, u32[]{:S(2)}) copy-start(bf16[16,256,128]{2,1,0:T(8,128)(2,1)} %copy-done.8) | copy-start | bytes 3145732
  155.9 2.2 %copy-start.11 = (bf16[16,256,128]{2,1,0:T(8,128)(2,1)S(1)}, bf16[16,256,128]{2,1,0:T(8,128)(2,1)}, u32[]{:S(2)}) copy-start(bf16[16,256,128]{2,1,0:T(8,128)(2,1)} %copy-done.10) | copy-start | bytes 3145732
  162.0 2.0 %copy-start.2 = (bf16[64,256,128]{2,1,0:T(8,128)(2,1)}, bf16[64,256,128]{2,1,0:T(8,128)(2,1)S(1)}, u32[]{:S(2)}) copy-start(bf16[64,256,128]{2,1,0:T(8,128)(2,1)S(1)} %get-tuple-element.99.t) | copy-start | bytes 12582916
  164.0 4.7 %collective-permute-start.28 = (f32[16,128,256]{2,1,0:T(8,128)S(1)}, f32[16,128,256]{2,1,0:T(8,128)}, u32[]{:S(2)}, u32[]{:S(2)}) collective-permute-start(f32[16,128,256]{2,1,0:T(8,128)S(1)} %density_rows.2), channel_id=1, source_target_pairs={{0,1},{1,0},{2,3},{3,2},{4,5},{5,4},{6,7},{7,6},{8,9},{9,8},{10,11... | collective-permute-start | bytes 6291464 | tf_op jit(solution)/shard_map/ppermute | solution.py:423
  164.3 3.9 %collective-permute-start.27 = (f32[64]{0:T(128)S(1)}, f32[64]{0:T(128)S(1)}, u32[]{:S(2)}, u32[]{:S(2)}) collective-permute-start(f32[64]{0:T(128)S(1)} %multiply_reduce_fusion), channel_id=1, source_target_pairs={{0,1},{1,0},{2,3},{3,2},{4,5},{5,4},{6,7},{7,6},{8,9},{9,8},{10,11... | collective-permute-start | bytes 776 | tf_op jit(solution)/shard_map/ppermute | solution.py:423
  168.7 2.2 %copy-start.3 = (bf16[64,256,128]{2,1,0:T(8,128)(2,1)S(1)}, bf16[64,256,128]{2,1,0:T(8,128)(2,1)}, u32[]{:S(2)}) copy-start(bf16[64,256,128]{2,1,0:T(8,128)(2,1)} %copy-done.2) | copy-start | bytes 12582916
  (4 other events, 2.6 us)

commit v12 on v11

--- a/solution.py
+++ b/solution.py
@@ -93,6 +93,7 @@
 
 TINY = pl.CostEstimate(flops=1, bytes_accessed=1, transcendentals=0)
 PARAMS = pltpu.CompilerParams(vmem_limit_bytes=LIMIT)
+LIGHT = pltpu.CompilerParams(vmem_limit_bytes=LIMIT // 4)
 
 
 def lists_kernel(cap, vir, occ, size, owner, slot, small, hit):
@@ -202,7 +203,7 @@
         out_shape=(table, rows, table, rows, table, table),
         in_specs=[SMEM] + [VMEM] * 8,
         out_specs=[VMEM] * 6,
-        compiler_params=PARAMS,
+        compiler_params=LIGHT,
         cost_estimate=TINY,
         name="tables",
     )(meta, *smalls)
@@ -236,7 +237,7 @@
         out_shape=[jax.ShapeDtypeStruct((k[2], cap) + block, bf16) for k in kinds],
         in_specs=[SMEM] * len(tbls) + [VMEM] * len(operands) + [HBM] * len(after),
         out_specs=[VMEM] * len(jobs),
-        compiler_params=PARAMS,
+        compiler_params=LIGHT,
         cost_estimate=TINY,
         name="pack",
     )(*tbls, *operands, *after)
@@ -367,14 +368,13 @@
         in_specs=[SMEM] + [VMEM] * len(blocks) + [HBM] * len(after) + [VMEM] * len(held),
         out_specs=out_specs,
         input_output_aliases=aliases,
-        compiler_params=PARAMS,
+        compiler_params=LIGHT,
         cost_estimate=TINY,
         name="amplitudes",
     )(*operands, *held)
 
 
-def density_kernel(start, t, *refs):
-    d = refs[-1]
+def density_kernel(start, t, d):
     count, half = d.shape[:2]
     per_orb = t.shape[0] // count
     first = pl.multiple_of(start[0], half)
@@ -382,11 +382,10 @@
         own = range(o * per_orb, (o + 1) * per_orb)
         left = jnp.concatenate([t[k, pl.ds(first, half), :] for k in own], axis=1)
         right = jnp.concatenate([t[k] for k in own], axis=1)
-        rows = lax.dot_general(left, right, (((1,), (1,)), ((), ())), preferred_element_type=f32)
-        d[o] = rows if len(refs) == 1 else rows + refs[0][o]
-
-
-def density_rows(t_all, start, per_orb, half, *away):
+        d[o] = lax.dot_general(left, right, (((1,), (1,)), ((), ())), preferred_element_type=f32)
+
+
+def density_rows(t_all, start, per_orb, half):
     npair, nvd, width = t_all.shape
     occ = npair // per_orb
     step = 4 if occ % 4 == 0 else 1
@@ -396,14 +395,13 @@
         grid_spec=pltpu.PrefetchScalarGridSpec(
             num_scalar_prefetch=1,
             grid=(occ // step,),
-            in_specs=[pl.BlockSpec((step * per_orb, nvd, width), lambda i, s: (i, 0, 0))]
-            + [pl.BlockSpec((step, half, nvd), lambda i, s: (i, 0, 0))] * len(away),
+            in_specs=[pl.BlockSpec((step * per_orb, nvd, width), lambda i, s: (i, 0, 0))],
             out_specs=pl.BlockSpec((step, half, nvd), lambda i, s: (i, 0, 0)),
         ),
         compiler_params=pltpu.CompilerParams(vmem_limit_bytes=LIMIT),
         cost_estimate=TINY,
         name="density_rows",
-    )(start.reshape(1), t_all, *away)
+    )(start.reshape(1), t_all)
 
 
 def line_plan(blocks, vir_energy, occ_energy, domain_size, partner_owner, partner_slot):
@@ -474,11 +472,11 @@
     gone = amplitudes("client", 2, per_orb, client, client_left, [mid], cap, after=(packed,))
     ready_2 = pp(gone, outward)
     held = own_pairs(1, "slots", [near], held, (gone, third_diagonal))
-    held = own_pairs(5, "asked", [beside_near], held)
     jobs = [(1, 3, far[:1], True), (0, 3, far[:1], True)]
     packed = pack(lists_of, jobs, cap, after=(held[1],))
     fourth_diagonal, fourth = [pp(packed[0], diagonal)], [pp(packed[1], y_middle)]
     held = own_pairs(2, "served", [mid], held, (packed[0],), (ready_2,))
+    held = own_pairs(5, "asked", [beside_near], held)
     (packed,) = pack(lists_of, [(1, 3, far[1:], True)], cap, after=(held[1],))
     fourth_diagonal.append(pp(packed, diagonal))
     gone = amplitudes("client", 3, per_orb, client, client_left, [far], cap, after=(packed,))
@@ -494,7 +492,7 @@
     t_all, e_all = own_pairs(7, "asked", [fourth, fourth_diagonal], held)
 
     away = swap_core(density_rows(t_all, (1 - core) * half, per_orb, half))
-    density = density_rows(t_all, core * half, per_orb, half, away)
+    density = density_rows(t_all, core * half, per_orb, half) + away
 
     energy = jnp.sum(hit * jnp.sum(e_all, axis=1)[None, :], axis=1)
     energy = (energy + swap_core(energy)) / nvd

time: 177 us -> 168 us (0.949)
  waiting for transfers between devices: 88.1 us -> 73.9 us
  local copies, waits for them, and re-layouts: 16.9 us -> 21.2 us
  other arithmetic: 0.81 us -> 4.14 us
  Pallas kernels: 37.1 us -> 34.2 us
    ppermute x24, waiting for transfers between devices: 84.8 us -> 73.9 us  [pp(): return lax.ppermute(x, 'orb', perm)]
    unnamed x46 -> x48, local copies, waits for them, and re-layouts: 13.2 us -> 17.5 us
    add x0 -> x1, other arithmetic: none -> 3.33 us  [line_plan(): density = density_rows(t_all, core * half, per_orb, half) + away]
    ppermute x5, waiting for transfers between devices: 3.33 us -> 0.01 us  [swap_core(): return lax.ppermute(x, 'aux', [(0, 1), (1, 0)])]
    pallas_call x2, Pallas kernels: 6.6 us -> 3.84 us  [density_rows(): pl.pallas_call(density_kernel, out_shape=jax.ShapeDtypeStruct((occ, half,...]
  transfers between devices with their start and end apart: 29 -> 29, of which waited for: 10 -> 9; matrix products, arithmetic and copies ran while one was open for 3% -> 3% of each run, Pallas kernels for 16% -> 18%
where the time goes in v12:
time: 168 us; the launch traced here: 167 us
  waiting for transfers between devices  73.9 us (44%)
  Pallas kernels  34.2 us (20%)
  starting transfers between devices  32.6 us (19%)
  local copies, waits for them, and re-layouts  21.2 us (13%)
  other arithmetic  4.14 us (2%)
    ppermute x24, waiting for transfers between devices, pp(): return lax.ppermute(x, 'orb', perm)  73.9 us
    ppermute x24, starting transfers between devices, pp(): return lax.ppermute(x, 'orb', perm)  31.5 us
    unnamed x48, local copies, waits for them, and re-layouts  17.5 us
    pallas_call x10, Pallas kernels, amplitudes(): pl.pallas_call(lambda *refs: amplitudes_kernel(mode, call, per_orb, [len(...  15.5 us
    pallas_call x7, Pallas kernels, pack(): pl.pallas_call(lambda *refs: pack_kernel(kinds, len(tbls), *refs), out_sh...  9.2 us
    pallas_call x2, Pallas kernels, turn(): pl.pallas_call(turn_kernel, out_shape=[jax.ShapeDtypeStruct((count, cols,...  4.26 us
    pallas_call x2, Pallas kernels, density_rows(): pl.pallas_call(density_kernel, out_shape=jax.ShapeDtypeStruct((occ, half,...  3.84 us
  transfers between devices with their start and end apart: 29, of which 9 were waited for; matrix products, arithmetic and copies ran while one was open for 3% of the time, Pallas kernels for 18%

profile of v12, /device:TPU:0, one launch (start us, length us, event | category | flops | bytes accessed | tf_op | source)
XLA Modules:
  0.0 167.1 jit_solution(12661758317595519769)
XLA Ops:
  4.7 2.6 %collective-permute-start = (f32[24,384]{1,0:T(8,128)S(1)}, f32[24,384]{1,0:T(8,128)S(1)}, u32[]{:S(2)}, u32[]{:S(2)}) collective-permute-start(f32[24,384]{1,0:T(8,128)S(1)} %get-tuple-element.53.refs_1_), channel_id=1, source_target_pairs={{0,2},{2,0},{4,6},{6,4},{8,10},{10,8},{12,14},{14,12},{1,3},{3,1},... | collective-permute-start | bytes 110600 | tf_op jit(solution)/shard_map/ppermute | solution.py:418
  7.3 1.6 collective-permute-start.1
  8.9 3.0 %collective-permute-start.3 = (f32[24,384]{1,0:T(8,128)S(1)}, f32[24,384]{1,0:T(8,128)S(1)}, u32[]{:S(2)}, u32[]{:S(2)}) collective-permute-start(f32[24,384]{1,0:T(8,128)S(1)} %get-tuple-element.53.refs_1_), channel_id=1, source_target_pairs={{0,8},{2,10},{4,12},{6,14},{8,0},{10,2},{12,4},{14,6},{1,9},{3,11}... | collective-permute-start | bytes 110600 | tf_op jit(solution)/shard_map/ppermute | solution.py:418
  11.8 1.4 collective-permute-start.4
  13.3 3.5 %collective-permute-start.5 = (f32[24,384]{1,0:T(8,128)S(1)}, f32[24,384]{1,0:T(8,128)S(1)}, u32[]{:S(2)}, u32[]{:S(2)}) collective-permute-start(f32[24,384]{1,0:T(8,128)S(1)} %get-tuple-element.53.refs_1_), channel_id=1, source_target_pairs={{0,12},{2,14},{4,8},{6,10},{8,4},{10,6},{12,0},{14,2},{1,13},{3,15... | collective-permute-start | bytes 110600 | tf_op jit(solution)/shard_map/ppermute | solution.py:418
  17.0 2.4 %constant_dynamic-slice_fusion.1.refs_2_.refs_5_ = bf16[16,256,128]{2,1,0:T(8,128)(2,1)} fusion(bf16[16,256,256]{2,1,0:T(8,128)(2,1)} %refs_0_.3, s32[]{:T(128)S(6)} %select_n.4), kind=kLoop, calls=%fused_computation.4 | loop fusion | bytes 2097156 | tf_op jit(solution)/shard_map/dynamic_slice | solution.py:435
  19.4 4.0 %collective-permute-done.6.refs_8_ = f32[24,384]{1,0:T(8,128)S(1)} collective-permute-done((f32[24,384]{1,0:T(8,128)S(1)}, f32[24,384]{1,0:T(8,128)S(1)}, u32[]{:S(2)}, u32[]{:S(2)}) %collective-permute-start.6) | collective-permute-done | bytes 36896 | tf_op jit(solution)/shard_map/ppermute | solution.py:418
  24.2 1.3 tables.1
  25.7 1.5 pack.7.refs_7_
  27.8 3.2 %collective-permute-start.10 = (bf16[16,256,128]{2,1,0:T(8,128)(2,1)S(1)}, bf16[16,256,128]{2,1,0:T(8,128)(2,1)S(1)}, u32[]{:S(2)}, u32[]{:S(2)}) collective-permute-start(bf16[16,256,128]{2,1,0:T(8,128)(2,1)S(1)} %constant_dynamic-slice_fusion.refs_3_.refs_6_), channel_id=1, source_target_pairs={{0,4},{2,6},{4,0},{6,2},{8,12},{10,14},{12,8},{14,10},{1,5},{3,7},... | collective-permute-start | bytes 3145736 | tf_op jit(solution)/shard_map/ppermute | solution.py:418
  31.7 1.3 turn.2
  33.7 2.7 %amplitudes.10 = (bf16[64,256,128]{2,1,0:T(8,128)(2,1)S(1)}, f32[64,128]{1,0:T(8,128)S(1)}) custom-call(s32[8,128]{1,0:T(8,128)S(1)} %get-tuple-element.61.refs_0_, f32[64,128]{1,0:T(8,128)S(1)} %get-tuple-element.62.refs_1_, f32[16,256,128]{2,1,0:T(8,128)S(1)} %broadcast_in_dim.4.refs_2_, bf16[16,256,256]{2,1,0:T(8,128)(2,1)S(1)} %get-tuple-element.63.refs_3_, ...), custom_call_target="tpu_custom_call" | custom-call | flops 1 | bytes 1 | tf_op jit(solution)/shard_map/amplitudes/pallas_call | solution.py:365
  36.4 13.4 %collective-permute-done.8.refs_2_.refs_0_.refs_5_ = bf16[16,256,128]{2,1,0:T(8,128)(2,1)} collective-permute-done((bf16[16,256,128]{2,1,0:T(8,128)(2,1)}, bf16[16,256,128]{2,1,0:T(8,128)(2,1)}, u32[]{:S(2)}, u32[]{:S(2)}) %collective-permute-start.8) | collective-permute-done | bytes 1048608 | tf_op jit(solution)/shard_map/ppermute | solution.py:418
  49.8 1.3 pack.8.refs_6_
  51.7 9.6 %collective-permute-done.13.refs_7_.refs_5_ = bf16[1,8,256,128]{3,2,1,0:T(8,128)(2,1)S(1)} collective-permute-done((bf16[1,8,256,128]{3,2,1,0:T(8,128)(2,1)S(1)}, bf16[1,8,256,128]{3,2,1,0:T(8,128)(2,1)S(1)}, u32[]{:S(2)}, u32[]{:S(2)}) %collective-permute-start.13) | collective-permute-done | bytes 524320 | tf_op jit(solution)/shard_map/ppermute | solution.py:418
  61.2 1.3 amplitudes.11
  62.5 6.3 %collective-permute-done.10.refs_1_.refs_2_.refs_6_ = bf16[16,256,128]{2,1,0:T(8,128)(2,1)S(1)} collective-permute-done((bf16[16,256,128]{2,1,0:T(8,128)(2,1)S(1)}, bf16[16,256,128]{2,1,0:T(8,128)(2,1)S(1)}, u32[]{:S(2)}, u32[]{:S(2)}) %collective-permute-start.10) | collective-permute-done | bytes 1048608 | tf_op jit(solution)/shard_map/ppermute | solution.py:418
  69.5 1.3 collective-permute-start.17
  73.7 2.9 %turn.3 = (bf16[16,128,256]{2,1,0:T(8,128)(2,1)S(1)}, bf16[16,128,256]{2,1,0:T(8,128)(2,1)S(1)}, bf16[16,128,256]{2,1,0:T(8,128)(2,1)S(1)}, bf16[16,128,256]{2,1,0:T(8,128)(2,1)S(1)}) custom-call(bf16[16,256,128]{2,1,0:T(8,128)(2,1)} %collective-permute-done.8.refs_2_.refs_0_.refs_5_, ...), custom_call_target="tpu_custom_call" | custom-call | flops 1 | bytes 1 | tf_op jit(solution)/shard_map/turn/pallas_call | solution.py:257
  77.9 1.3 collective-permute-start.21
  79.2 19.2 %collective-permute-done.17.refs_8_.refs_6_ = bf16[2,8,256,128]{3,2,1,0:T(8,128)(2,1)S(1)} collective-permute-done((bf16[2,8,256,128]{3,2,1,0:T(8,128)(2,1)S(1)}, bf16[2,8,256,128]{3,2,1,0:T(8,128)(2,1)S(1)}, u32[]{:S(2)}, u32[]{:S(2)}) %collective-permute-start.17) | collective-permute-done | bytes 1048608 | tf_op jit(solution)/shard_map/ppermute | solution.py:418
  98.4 1.6 collective-permute-start.20
  100.1 1.9 %amplitudes.13 = (bf16[64,256,128]{2,1,0:T(8,128)(2,1)S(1)}, f32[64,128]{1,0:T(8,128)S(1)}) custom-call(s32[8,128]{1,0:T(8,128)S(1)} %get-tuple-element.61.refs_0_, f32[64,128]{1,0:T(8,128)S(1)} %get-tuple-element.62.refs_1_, f32[16,256,128]{2,1,0:T(8,128)S(1)} %broadcast_in_dim.4.refs_2_, ...), custom_call_target="tpu_custom_call", output_to_operand_aliasing={{0}: (9, {}), {1}: (10, {})} | custom-call | flops 1 | bytes 1 | tf_op jit(solution)/shard_map/amplitudes/pallas_call | solution.py:365
  102.0 1.6 pack.11
  103.7 1.4 collective-permute-start.18
  105.1 3.0 %collective-permute-done.21.refs_7_ = bf16[8,256,128]{2,1,0:T(8,128)(2,1)S(1)} collective-permute-done((bf16[8,256,128]{2,1,0:T(8,128)(2,1)S(1)}, bf16[8,256,128]{2,1,0:T(8,128)(2,1)S(1)}, u32[]{:S(2)}, u32[]{:S(2)}) %collective-permute-start.21) | collective-permute-done | bytes 524320 | tf_op jit(solution)/shard_map/ppermute | solution.py:418
  108.1 1.3 collective-permute-start.23
  111.2 1.3 amplitudes.15
  112.6 2.0 %pack.12.refs_9_ = bf16[1,8,256,128]{3,2,1,0:T(8,128)(2,1)} custom-call(s32[8,128]{1,0:T(8,128)S(1)} %get-tuple-element.65.refs_0_, s32[8,128]{1,0:T(8,128)S(1)} %get-tuple-element.66.refs_1_, bf16[16,256,128]{2,1,0:T(8,128)(2,1)S(1)} %collective-permute-done.19.refs_2_.refs_8_.refs_6_, f32[64,128]{1,0:T(8,128)S(1)} %get-tuple-element.91.refs_3_.refs_12_), custom_call_target="tpu_custom_call" | custom-call | flops 1 | bytes 1 | tf_op jit(solution)/shard_map/pack/pallas_call | solution.py:235
  114.5 1.3 collective-permute-start.24
  115.8 1.4 amplitudes.16.refs_3_
  117.2 1.4 collective-permute-start.25
  118.7 1.5 pack.13.refs_7_
  121.1 1.5 collective-permute-start.22
  123.5 16.7 %collective-permute-done.24.refs_10_.refs_8_ = bf16[1,8,256,128]{3,2,1,0:T(8,128)(2,1)} collective-permute-done((bf16[1,8,256,128]{3,2,1,0:T(8,128)(2,1)}, bf16[1,8,256,128]{3,2,1,0:T(8,128)(2,1)}, u32[]{:S(2)}, u32[]{:S(2)}) %collective-permute-start.24) | collective-permute-done | bytes 524320 | tf_op jit(solution)/shard_map/ppermute | solution.py:418
  140.2 2.2 %copy-done.1 = bf16[64,256,128]{2,1,0:T(8,128)(2,1)S(1)} copy-done((bf16[64,256,128]{2,1,0:T(8,128)(2,1)S(1)}, bf16[64,256,128]{2,1,0:T(8,128)(2,1)}, u32[]{:S(2)}) %copy-start.1) | copy-done | bytes 4194328
  142.4 1.6 copy-done.6
  144.0 1.6 copy-done.8
  145.6 1.2 copy-done.17
  146.8 1.4 amplitudes.17
  148.3 1.5 amplitudes.18
  149.9 2.3 %amplitudes.19 = (bf16[64,256,128]{2,1,0:T(8,128)(2,1)S(1)}, f32[64,128]{1,0:T(8,128)S(1)}) custom-call(s32[8,128]{1,0:T(8,128)S(1)} %get-tuple-element.61.refs_0_, f32[64,128]{1,0:T(8,128)S(1)} %get-tuple-element.62.refs_1_, f32[16,256,128]{2,1,0:T(8,128)S(1)} %broadcast_in_dim.4.refs_2_, ...), custom_call_target="tpu_custom_call", output_to_operand_aliasing={{0}: (9, {}), {1}: (10, {})} | custom-call | flops 1 | bytes 1 | tf_op jit(solution)/shard_map/amplitudes/pallas_call | solution.py:365
  152.2 2.0 %copy-done.2 = bf16[64,256,128]{2,1,0:T(8,128)(2,1)} copy-done((bf16[64,256,128]{2,1,0:T(8,128)(2,1)}, bf16[64,256,128]{2,1,0:T(8,128)(2,1)S(1)}, u32[]{:S(2)}) %copy-start.2) | copy-done | bytes 4194328
  154.2 2.2 %copy-done.3 = bf16[64,256,128]{2,1,0:T(8,128)(2,1)S(1)} copy-done((bf16[64,256,128]{2,1,0:T(8,128)(2,1)S(1)}, bf16[64,256,128]{2,1,0:T(8,128)(2,1)}, u32[]{:S(2)}) %copy-start.3) | copy-done | bytes 4194328
  156.4 1.9 %density_rows.3 = f32[16,128,256]{2,1,0:T(8,128)S(1)} custom-call(s32[1]{0:T(128)} %bitcast.6.start, bf16[64,256,128]{2,1,0:T(8,128)(2,1)S(1)} %copy-done.3), custom_call_target="tpu_custom_call" | custom-call | flops 1 | bytes 1 | tf_op jit(solution)/shard_map/density_rows/pallas_call | solution.py:392
  159.2 2.2 %copy-done.4 = bf16[64,256,128]{2,1,0:T(8,128)(2,1)S(1)} copy-done((bf16[64,256,128]{2,1,0:T(8,128)(2,1)S(1)}, bf16[64,256,128]{2,1,0:T(8,128)(2,1)}, u32[]{:S(2)}) %copy-start.4) | copy-done | bytes 4194328
  161.4 1.9 %density_rows.2 = f32[16,128,256]{2,1,0:T(8,128)S(1)} custom-call(s32[1]{0:T(128)} %bitcast.5.start, bf16[64,256,128]{2,1,0:T(8,128)(2,1)S(1)} %copy-done.4), custom_call_target="tpu_custom_call" | custom-call | flops 1 | bytes 1 | tf_op jit(solution)/shard_map/density_rows/pallas_call | solution.py:392
  163.8 3.3 %add.12 = f32[16,128,256]{2,1,0:T(8,128)} add(f32[16,128,256]{2,1,0:T(8,128)S(1)} %density_rows.2, f32[16,128,256]{2,1,0:T(8,128)} %collective-permute-done.28) | non-fusion elementwise | flops 524288 | bytes 6291456 | tf_op jit(solution)/shard_map/add | solution.py:495
  (91 shorter events, 17.8 us)
Async XLA Ops:
  0.6 24.9 %collective-permute-start.7 = (bf16[16,256,256]{2,1,0:T(8,128)(2,1)}, bf16[16,256,256]{2,1,0:T(8,128)(2,1)S(1)}, u32[]{:S(2)}, u32[]{:S(2)}) collective-permute-start(bf16[16,256,256]{2,1,0:T(8,128)(2,1)} %refs_0_.3), channel_id=1, source_target_pairs={{0,1},{1,0},{2,3},{3,2},{4,5},{5,4},{6,7},{7,6},{8,9},{9,8},{10,11... | collective-permute-start | bytes 6291464 | tf_op jit(solution)/shard_map/ppermute | solution.py:421
  4.7 7.2 %collective-permute-start = (f32[24,384]{1,0:T(8,128)S(1)}, f32[24,384]{1,0:T(8,128)S(1)}, u32[]{:S(2)}, u32[]{:S(2)}) collective-permute-start(f32[24,384]{1,0:T(8,128)S(1)} %get-tuple-element.53.refs_1_), channel_id=1, source_target_pairs={{0,2},{2,0},{4,6},{6,4},{8,10},{10,8},{12,14},{14,12},{1,3},{3,1},... | collective-permute-start | bytes 110600 | tf_op jit(solution)/shard_map/ppermute | solution.py:418
  7.3 6.0 %collective-permute-start.1 = (f32[24,384]{1,0:T(8,128)S(1)}, f32[24,384]{1,0:T(8,128)S(1)}, u32[]{:S(2)}, u32[]{:S(2)}) collective-permute-start(f32[24,384]{1,0:T(8,128)S(1)} %get-tuple-element.53.refs_1_), channel_id=1, source_target_pairs={{0,4},{2,6},{4,0},{6,2},{8,12},{10,14},{12,8},{14,10},{1,5},{3,7},... | collective-permute-start | bytes 110600 | tf_op jit(solution)/shard_map/ppermute | solution.py:418
  8.8 7.9 %collective-permute-start.2 = (f32[24,384]{1,0:T(8,128)S(1)}, f32[24,384]{1,0:T(8,128)S(1)}, u32[]{:S(2)}, u32[]{:S(2)}) collective-permute-start(f32[24,384]{1,0:T(8,128)S(1)} %get-tuple-element.53.refs_1_), channel_id=1, source_target_pairs={{0,6},{2,4},{4,2},{6,0},{8,14},{10,12},{12,10},{14,8},{1,7},{3,5},... | collective-permute-start | bytes 110600 | tf_op jit(solution)/shard_map/ppermute | solution.py:418
  8.9 10.5 %collective-permute-start.3 = (f32[24,384]{1,0:T(8,128)S(1)}, f32[24,384]{1,0:T(8,128)S(1)}, u32[]{:S(2)}, u32[]{:S(2)}) collective-permute-start(f32[24,384]{1,0:T(8,128)S(1)} %get-tuple-element.53.refs_1_), channel_id=1, source_target_pairs={{0,8},{2,10},{4,12},{6,14},{8,0},{10,2},{12,4},{14,6},{1,9},{3,11}... | collective-permute-start | bytes 110600 | tf_op jit(solution)/shard_map/ppermute | solution.py:418
  11.8 7.6 %collective-permute-start.4 = (f32[24,384]{1,0:T(8,128)S(1)}, f32[24,384]{1,0:T(8,128)S(1)}, u32[]{:S(2)}, u32[]{:S(2)}) collective-permute-start(f32[24,384]{1,0:T(8,128)S(1)} %get-tuple-element.53.refs_1_), channel_id=1, source_target_pairs={{0,10},{2,8},{4,14},{6,12},{8,2},{10,0},{12,6},{14,4},{1,11},{3,9}... | collective-permute-start | bytes 110600 | tf_op jit(solution)/shard_map/ppermute | solution.py:418
  13.3 6.1 %collective-permute-start.5 = (f32[24,384]{1,0:T(8,128)S(1)}, f32[24,384]{1,0:T(8,128)S(1)}, u32[]{:S(2)}, u32[]{:S(2)}) collective-permute-start(f32[24,384]{1,0:T(8,128)S(1)} %get-tuple-element.53.refs_1_), channel_id=1, source_target_pairs={{0,12},{2,14},{4,8},{6,10},{8,4},{10,6},{12,0},{14,2},{1,13},{3,15... | collective-permute-start | bytes 110600 | tf_op jit(solution)/shard_map/ppermute | solution.py:418
  16.7 6.7 %collective-permute-start.6 = (f32[24,384]{1,0:T(8,128)S(1)}, f32[24,384]{1,0:T(8,128)S(1)}, u32[]{:S(2)}, u32[]{:S(2)}) collective-permute-start(f32[24,384]{1,0:T(8,128)S(1)} %get-tuple-element.53.refs_1_), channel_id=1, source_target_pairs={{0,14},{2,12},{4,10},{6,8},{8,6},{10,4},{12,2},{14,0},{1,15},{3,13... | collective-permute-start | bytes 110600 | tf_op jit(solution)/shard_map/ppermute | solution.py:418
  23.4 26.4 %collective-permute-start.8 = (bf16[16,256,128]{2,1,0:T(8,128)(2,1)}, bf16[16,256,128]{2,1,0:T(8,128)(2,1)}, u32[]{:S(2)}, u32[]{:S(2)}) collective-permute-start(bf16[16,256,128]{2,1,0:T(8,128)(2,1)} %constant_dynamic-slice_fusion.1.refs_2_.refs_5_), channel_id=1, source_target_pairs={{0,4},{2,6},{4,0},{6,2},{8,12},{10,14},{12,8},{14,10},{1,5},{3,7},... | collective-permute-start | bytes 3145736 | tf_op jit(solution)/shard_map/ppermute | solution.py:418
  23.4 26.4 %collective-permute-start.12 = (bf16[16,256,128]{2,1,0:T(8,128)(2,1)}, bf16[16,256,128]{2,1,0:T(8,128)(2,1)S(1)}, u32[]{:S(2)}, u32[]{:S(2)}) collective-permute-start(bf16[16,256,128]{2,1,0:T(8,128)(2,1)} %constant_dynamic-slice_fusion.1.refs_2_.refs_5_), channel_id=1, source_target_pairs={{4,8},{6,10},{8,4},{10,6},{5,9},{7,11},{9,5},{11,7},{20,24},{22,26... | collective-permute-start | bytes 3145736 | tf_op jit(solution)/shard_map/ppermute | solution.py:418
  25.7 6.0 %copy-start.13 = (bf16[16,256,256]{2,1,0:T(8,128)(2,1)S(1)}, bf16[16,256,256]{2,1,0:T(8,128)(2,1)}, u32[]{:S(2)}) copy-start(bf16[16,256,256]{2,1,0:T(8,128)(2,1)} %refs_0_.3) | copy-start | bytes 6291460
  27.2 5.9 %copy-start.19 = (f32[16,256]{1,0:T(8,128)S(1)}, f32[16,256]{1,0:T(8,128)}, u32[]{:S(2)}) copy-start(f32[16,256]{1,0:T(8,128)} %refs_0_.2) | copy-start | bytes 49156
  27.2 34.0 %collective-permute-start.11 = (bf16[2,8,256,128]{3,2,1,0:T(8,128)(2,1)S(1)}, bf16[2,8,256,128]{3,2,1,0:T(8,128)(2,1)S(1)}, u32[]{:S(2)}, u32[]{:S(2)}) collective-permute-start(bf16[2,8,256,128]{3,2,1,0:T(8,128)(2,1)S(1)} %pack.7.refs_7_), channel_id=1, source_target_pairs={{0,2},{2,0},{4,6},{6,4},{8,10},{10,8},{12,14},{14,12},{1,3},{3,1},... | collective-permute-start | bytes 3145736 | tf_op jit(solution)/shard_map/ppermute | solution.py:418
  27.8 41.0 %collective-permute-start.10 = (bf16[16,256,128]{2,1,0:T(8,128)(2,1)S(1)}, bf16[16,256,128]{2,1,0:T(8,128)(2,1)S(1)}, u32[]{:S(2)}, u32[]{:S(2)}) collective-permute-start(bf16[16,256,128]{2,1,0:T(8,128)(2,1)S(1)} %constant_dynamic-slice_fusion.refs_3_.refs_6_), channel_id=1, source_target_pairs={{0,4},{2,6},{4,0},{6,2},{8,12},{10,14},{12,8},{14,10},{1,5},{3,7},... | collective-permute-start | bytes 3145736 | tf_op jit(solution)/shard_map/ppermute | solution.py:418
  31.0 37.8 %collective-permute-start.16 = (bf16[16,256,128]{2,1,0:T(8,128)(2,1)S(1)}, bf16[16,256,128]{2,1,0:T(8,128)(2,1)S(1)}, u32[]{:S(2)}, u32[]{:S(2)}) collective-permute-start(bf16[16,256,128]{2,1,0:T(8,128)(2,1)S(1)} %constant_dynamic-slice_fusion.refs_3_.refs_6_), channel_id=1, source_target_pairs={{4,8},{6,10},{8,4},{10,6},{5,9},{7,11},{9,5},{11,7},{20,24},{22,26... | collective-permute-start | bytes 3145736 | tf_op jit(solution)/shard_map/ppermute | solution.py:418
  33.1 78.2 %copy-start.5 = (bf16[16,256,256]{2,1,0:T(8,128)(2,1)}, bf16[16,256,256]{2,1,0:T(8,128)(2,1)S(1)}, u32[]{:S(2)}) copy-start(bf16[16,256,256]{2,1,0:T(8,128)(2,1)S(1)} %get-tuple-element.63.refs_3_) | copy-start | bytes 6291460
  33.1 78.2 %copy-start.7 = (bf16[16,256,256]{2,1,0:T(8,128)(2,1)}, bf16[16,256,256]{2,1,0:T(8,128)(2,1)S(1)}, u32[]{:S(2)}) copy-start(bf16[16,256,256]{2,1,0:T(8,128)(2,1)S(1)} %get-tuple-element.64.refs_4_) | copy-start | bytes 6291460
  51.1 10.1 %collective-permute-start.13 = (bf16[1,8,256,128]{3,2,1,0:T(8,128)(2,1)S(1)}, bf16[1,8,256,128]{3,2,1,0:T(8,128)(2,1)S(1)}, u32[]{:S(2)}, u32[]{:S(2)}) collective-permute-start(bf16[1,8,256,128]{3,2,1,0:T(8,128)(2,1)S(1)} %pack.8.refs_6_), channel_id=1, source_target_pairs={{0,2},{2,0},{4,6},{6,4},{8,10},{10,8},{12,14},{14,12},{1,3},{3,1},... | collective-permute-start | bytes 1572872 | tf_op jit(solution)/shard_map/ppermute | solution.py:418
  51.7 20.6 %collective-permute-start.14 = (bf16[16,256,128]{2,1,0:T(8,128)(2,1)}, bf16[16,256,128]{2,1,0:T(8,128)(2,1)S(1)}, u32[]{:S(2)}, u32[]{:S(2)}) collective-permute-start(bf16[16,256,128]{2,1,0:T(8,128)(2,1)} %collective-permute-done.8.refs_2_.refs_0_.refs_5_), channel_id=1, source_target_pairs={{0,1},{1,0},{2,3},{3,2},{4,5},{5,4},{6,7},{7,6},{8,9},{9,8},{10,11... | collective-permute-start | bytes 3145736 | tf_op jit(solution)/shard_map/ppermute | solution.py:421
  68.8 4.9 %collective-permute-start.15 = (bf16[16,256,128]{2,1,0:T(8,128)(2,1)S(1)}, bf16[16,256,128]{2,1,0:T(8,128)(2,1)S(1)}, u32[]{:S(2)}, u32[]{:S(2)}) collective-permute-start(bf16[16,256,128]{2,1,0:T(8,128)(2,1)S(1)} %collective-permute-done.10.refs_1_.refs_2_.refs_6_), channel_id=1, source_target_pairs={{0,1},{1,0},{2,3},{3,2},{4,5},{5,4},{6,7},{7,6},{8,9},{9,8},{10,11... | collective-permute-start | bytes 3145736 | tf_op jit(solution)/shard_map/ppermute | solution.py:421
  69.5 28.9 %collective-permute-start.17 = (bf16[2,8,256,128]{3,2,1,0:T(8,128)(2,1)S(1)}, bf16[2,8,256,128]{3,2,1,0:T(8,128)(2,1)S(1)}, u32[]{:S(2)}, u32[]{:S(2)}) collective-permute-start(bf16[2,8,256,128]{3,2,1,0:T(8,128)(2,1)S(1)} %get-tuple-element.83.refs_3_), channel_id=1, source_target_pairs={{4,2},{6,0},{8,14},{10,12},{5,3},{7,1},{9,15},{11,13},{20,18},{22,... | collective-permute-start | bytes 3145736 | tf_op jit(solution)/shard_map/ppermute | solution.py:418
  70.8 31.2 %collective-permute-start.9 = (bf16[16,256,128]{2,1,0:T(8,128)(2,1)}, bf16[16,256,128]{2,1,0:T(8,128)(2,1)S(1)}, u32[]{:S(2)}, u32[]{:S(2)}) collective-permute-start(bf16[16,256,128]{2,1,0:T(8,128)(2,1)} %collective-permute-done.8.refs_2_.refs_0_.refs_5_), channel_id=1, source_target_pairs={{4,8},{6,10},{8,4},{10,6},{5,9},{7,11},{9,5},{11,7},{20,24},{22,26... | collective-permute-start | bytes 3145736 | tf_op jit(solution)/shard_map/ppermute | solution.py:418
  71.5 41.0 %collective-permute-start.19 = (bf16[16,256,128]{2,1,0:T(8,128)(2,1)S(1)}, bf16[16,256,128]{2,1,0:T(8,128)(2,1)S(1)}, u32[]{:S(2)}, u32[]{:S(2)}) collective-permute-start(bf16[16,256,128]{2,1,0:T(8,128)(2,1)S(1)} %collective-permute-done.10.refs_1_.refs_2_.refs_6_), channel_id=1, source_target_pairs={{4,8},{6,10},{8,4},{10,6},{5,9},{7,11},{9,5},{11,7},{20,24},{22,26... | collective-permute-start | bytes 3145736 | tf_op jit(solution)/shard_map/ppermute | solution.py:418
  72.3 47.9 %collective-permute-start.26 = (bf16[2,8,256,128]{3,2,1,0:T(8,128)(2,1)S(1)}, bf16[2,8,256,128]{3,2,1,0:T(8,128)(2,1)S(1)}, u32[]{:S(2)}, u32[]{:S(2)}) collective-permute-start(bf16[2,8,256,128]{3,2,1,0:T(8,128)(2,1)S(1)} %get-tuple-element.92), channel_id=1, source_target_pairs={{4,6},{6,4},{8,10},{10,8},{5,7},{7,5},{9,11},{11,9},{20,22},{22,20... | collective-permute-start | bytes 3145736 | tf_op jit(solution)/shard_map/ppermute | solution.py:418
  77.9 30.2 %collective-permute-start.21 = (bf16[8,256,128]{2,1,0:T(8,128)(2,1)S(1)}, bf16[8,256,128]{2,1,0:T(8,128)(2,1)S(1)}, u32[]{:S(2)}, u32[]{:S(2)}) collective-permute-start(bf16[8,256,128]{2,1,0:T(8,128)(2,1)S(1)} %amplitudes.12.refs_7_), channel_id=1, source_target_pairs={{4,0},{6,2},{8,12},{10,14},{5,1},{7,3},{9,13},{11,15},{20,16},{22,... | collective-permute-start | bytes 1572872 | tf_op jit(solution)/shard_map/ppermute | solution.py:418
  98.4 3.6 %copy-start.14 = (bf16[2,8,256,128]{3,2,1,0:T(8,128)(2,1)}, bf16[2,8,256,128]{3,2,1,0:T(8,128)(2,1)S(1)}, u32[]{:S(2)}) copy-start(bf16[2,8,256,128]{3,2,1,0:T(8,128)(2,1)S(1)} %collective-permute-done.17.refs_8_.refs_6_) | copy-start | bytes 3145732
  98.4 12.8 %collective-permute-start.20 = (bf16[1,8,256,128]{3,2,1,0:T(8,128)(2,1)S(1)}, bf16[1,8,256,128]{3,2,1,0:T(8,128)(2,1)S(1)}, u32[]{:S(2)}, u32[]{:S(2)}) collective-permute-start(bf16[1,8,256,128]{3,2,1,0:T(8,128)(2,1)S(1)} %pack.10.refs_9_), channel_id=1, source_target_pairs={{0,2},{2,0},{4,6},{6,4},{8,10},{10,8},{12,14},{14,12},{1,3},{3,1},... | collective-permute-start | bytes 1572872 | tf_op jit(solution)/shard_map/ppermute | solution.py:418
  102.0 13.8 %copy-start.9 = (bf16[16,256,128]{2,1,0:T(8,128)(2,1)}, bf16[16,256,128]{2,1,0:T(8,128)(2,1)S(1)}, u32[]{:S(2)}) copy-start(bf16[16,256,128]{2,1,0:T(8,128)(2,1)S(1)} %collective-permute-done.9.refs_2_.refs_3_.refs_7_.refs_5_) | copy-start | bytes 3145732
  103.7 18.9 %collective-permute-start.18 = (bf16[1,8,256,128]{3,2,1,0:T(8,128)(2,1)}, bf16[1,8,256,128]{3,2,1,0:T(8,128)(2,1)}, u32[]{:S(2)}, u32[]{:S(2)}) collective-permute-start(bf16[1,8,256,128]{3,2,1,0:T(8,128)(2,1)} %get-tuple-element.86), channel_id=1, source_target_pairs={{4,6},{6,4},{8,10},{10,8},{5,7},{7,5},{9,11},{11,9},{20,22},{22,20... | collective-permute-start | bytes 1572872 | tf_op jit(solution)/shard_map/ppermute | solution.py:418
  108.1 15.3 %collective-permute-start.23 = (bf16[1,8,256,128]{3,2,1,0:T(8,128)(2,1)}, bf16[1,8,256,128]{3,2,1,0:T(8,128)(2,1)}, u32[]{:S(2)}, u32[]{:S(2)}) collective-permute-start(bf16[1,8,256,128]{3,2,1,0:T(8,128)(2,1)} %get-tuple-element.87.refs_8_), channel_id=1, source_target_pairs={{4,2},{6,0},{8,14},{10,12},{5,3},{7,1},{9,15},{11,13},{20,18},{22,... | collective-permute-start | bytes 1572872 | tf_op jit(solution)/shard_map/ppermute | solution.py:418
  112.5 4.7 %copy-start = (bf16[64,256,128]{2,1,0:T(8,128)(2,1)}, bf16[64,256,128]{2,1,0:T(8,128)(2,1)S(1)}, u32[]{:S(2)}) copy-start(bf16[64,256,128]{2,1,0:T(8,128)(2,1)S(1)} %get-tuple-element.93.refs_11_) | copy-start | bytes 12582916
  112.6 6.1 %copy-start.11 = (bf16[16,256,128]{2,1,0:T(8,128)(2,1)}, bf16[16,256,128]{2,1,0:T(8,128)(2,1)S(1)}, u32[]{:S(2)}) copy-start(bf16[16,256,128]{2,1,0:T(8,128)(2,1)S(1)} %collective-permute-done.19.refs_2_.refs_8_.refs_6_) | copy-start | bytes 3145732
  114.5 25.6 %collective-permute-start.24 = (bf16[1,8,256,128]{3,2,1,0:T(8,128)(2,1)}, bf16[1,8,256,128]{3,2,1,0:T(8,128)(2,1)}, u32[]{:S(2)}, u32[]{:S(2)}) collective-permute-start(bf16[1,8,256,128]{3,2,1,0:T(8,128)(2,1)} %pack.12.refs_9_), channel_id=1, source_target_pairs={{4,2},{6,0},{8,14},{10,12},{5,3},{7,1},{9,15},{11,13},{20,18},{22,... | collective-permute-start | bytes 1572872 | tf_op jit(solution)/shard_map/ppermute | solution.py:418
  117.2 22.9 %copy-start.15 = (bf16[2,8,256,128]{3,2,1,0:T(8,128)(2,1)S(1)}, bf16[2,8,256,128]{3,2,1,0:T(8,128)(2,1)}, u32[]{:S(2)}) copy-start(bf16[2,8,256,128]{3,2,1,0:T(8,128)(2,1)} %copy-done.14) | copy-start | bytes 3145732
  117.2 30.9 %collective-permute-start.25 = (bf16[8,256,128]{2,1,0:T(8,128)(2,1)}, bf16[8,256,128]{2,1,0:T(8,128)(2,1)}, u32[]{:S(2)}, u32[]{:S(2)}) collective-permute-start(bf16[8,256,128]{2,1,0:T(8,128)(2,1)} %amplitudes.16.refs_3_), channel_id=1, source_target_pairs={{4,0},{6,2},{8,12},{10,14},{5,1},{7,3},{9,13},{11,15},{20,16},{22,... | collective-permute-start | bytes 1572872 | tf_op jit(solution)/shard_map/ppermute | solution.py:418
  120.1 1.0 copy-start.16
  121.1 28.7 %collective-permute-start.22 = (bf16[1,8,256,128]{3,2,1,0:T(8,128)(2,1)}, bf16[1,8,256,128]{3,2,1,0:T(8,128)(2,1)}, u32[]{:S(2)}, u32[]{:S(2)}) collective-permute-start(bf16[1,8,256,128]{3,2,1,0:T(8,128)(2,1)} %pack.13.refs_7_), channel_id=1, source_target_pairs={{4,6},{6,4},{8,10},{10,8},{5,7},{7,5},{9,11},{11,9},{20,22},{22,20... | collective-permute-start | bytes 1572872 | tf_op jit(solution)/shard_map/ppermute | solution.py:418
  140.2 2.2 %copy-start.1 = (bf16[64,256,128]{2,1,0:T(8,128)(2,1)S(1)}, bf16[64,256,128]{2,1,0:T(8,128)(2,1)}, u32[]{:S(2)}) copy-start(bf16[64,256,128]{2,1,0:T(8,128)(2,1)} %copy-done) | copy-start | bytes 12582916
  142.4 1.6 copy-start.6
  144.0 1.6 copy-start.8
  145.6 1.2 copy-start.17
  146.8 1.4 copy-start.10
  146.8 1.5 copy-start.12
  152.2 2.0 %copy-start.2 = (bf16[64,256,128]{2,1,0:T(8,128)(2,1)}, bf16[64,256,128]{2,1,0:T(8,128)(2,1)S(1)}, u32[]{:S(2)}) copy-start(bf16[64,256,128]{2,1,0:T(8,128)(2,1)S(1)} %get-tuple-element.99.t) | copy-start | bytes 12582916
  154.2 2.2 %copy-start.3 = (bf16[64,256,128]{2,1,0:T(8,128)(2,1)S(1)}, bf16[64,256,128]{2,1,0:T(8,128)(2,1)}, u32[]{:S(2)}) copy-start(bf16[64,256,128]{2,1,0:T(8,128)(2,1)} %copy-done.2) | copy-start | bytes 12582916
  158.3 5.5 %collective-permute-start.28 = (f32[16,128,256]{2,1,0:T(8,128)S(1)}, f32[16,128,256]{2,1,0:T(8,128)}, u32[]{:S(2)}, u32[]{:S(2)}) collective-permute-start(f32[16,128,256]{2,1,0:T(8,128)S(1)} %density_rows.3), channel_id=1, source_target_pairs={{0,1},{1,0},{2,3},{3,2},{4,5},{5,4},{6,7},{7,6},{8,9},{9,8},{10,11... | collective-permute-start | bytes 6291464 | tf_op jit(solution)/shard_map/ppermute | solution.py:421
  158.6 4.7 %collective-permute-start.27 = (f32[64]{0:T(128)S(1)}, f32[64]{0:T(128)S(1)}, u32[]{:S(2)}, u32[]{:S(2)}) collective-permute-start(f32[64]{0:T(128)S(1)} %multiply_reduce_fusion), channel_id=1, source_target_pairs={{0,1},{1,0},{2,3},{3,2},{4,5},{5,4},{6,7},{7,6},{8,9},{9,8},{10,11... | collective-permute-start | bytes 776 | tf_op jit(solution)/shard_map/ppermute | solution.py:421
  159.2 2.2 %copy-start.4 = (bf16[64,256,128]{2,1,0:T(8,128)(2,1)S(1)}, bf16[64,256,128]{2,1,0:T(8,128)(2,1)}, u32[]{:S(2)}) copy-start(bf16[64,256,128]{2,1,0:T(8,128)(2,1)} %copy-done.2) | copy-start | bytes 12582916
  (5 other events, 3.3 us)

commit v13 on v12

--- a/solution.py
+++ b/solution.py
@@ -374,33 +374,31 @@
     )(*operands, *held)
 
 
-def density_kernel(start, t, d):
-    count, half = d.shape[:2]
+def density_kernel(start, t, mine, away):
+    count, half = mine.shape[:2]
     per_orb = t.shape[0] // count
     first = pl.multiple_of(start[0], half)
     for o in range(count):
         own = range(o * per_orb, (o + 1) * per_orb)
-        left = jnp.concatenate([t[k, pl.ds(first, half), :] for k in own], axis=1)
         right = jnp.concatenate([t[k] for k in own], axis=1)
-        d[o] = lax.dot_general(left, right, (((1,), (1,)), ((), ())), preferred_element_type=f32)
-
-
-def density_rows(t_all, start, per_orb, half):
-    npair, nvd, width = t_all.shape
-    occ = npair // per_orb
-    step = 4 if occ % 4 == 0 else 1
+        for out, row in ((away, pl.multiple_of(half - first, half)), (mine, first)):
+            left = jnp.concatenate([t[k, pl.ds(row, half), :] for k in own], axis=1)
+            out[o] = lax.dot_general(
+                left, right, (((1,), (1,)), ((), ())), preferred_element_type=f32
+            )
+
+
+def densities(t_all, start, per_orb, half):
+    npair, nvd, _ = t_all.shape
+    shape = jax.ShapeDtypeStruct((npair // per_orb, half, nvd), f32)
     return pl.pallas_call(
         density_kernel,
-        out_shape=jax.ShapeDtypeStruct((occ, half, nvd), f32),
-        grid_spec=pltpu.PrefetchScalarGridSpec(
-            num_scalar_prefetch=1,
-            grid=(occ // step,),
-            in_specs=[pl.BlockSpec((step * per_orb, nvd, width), lambda i, s: (i, 0, 0))],
-            out_specs=pl.BlockSpec((step, half, nvd), lambda i, s: (i, 0, 0)),
-        ),
-        compiler_params=pltpu.CompilerParams(vmem_limit_bytes=LIMIT),
+        out_shape=(shape, shape),
+        in_specs=[SMEM, VMEM],
+        out_specs=(VMEM, VMEM),
+        compiler_params=LIGHT,
         cost_estimate=TINY,
-        name="density_rows",
+        name="densities",
     )(start.reshape(1), t_all)
 
 
@@ -486,13 +484,13 @@
     )
     fourth.append(pp(packed, y_middle))
     held = own_pairs(
-        6, "asked", [[third], [third_diagonal]], held, (packed, fourth[0], *fourth_diagonal)
-    )
-    held = own_pairs(3, "served", [far], held, ready=(ready_3,))
+        6, "asked", [[third], [third_diagonal]], held, (packed, fourth[0], fourth_diagonal[0])
+    )
+    held = own_pairs(3, "served", [far], held, (fourth_diagonal[1],), (ready_3,))
     t_all, e_all = own_pairs(7, "asked", [fourth, fourth_diagonal], held)
 
-    away = swap_core(density_rows(t_all, (1 - core) * half, per_orb, half))
-    density = density_rows(t_all, core * half, per_orb, half) + away
+    mine, away = densities(t_all, col0, per_orb, half)
+    density = mine + swap_core(away)
 
     energy = jnp.sum(hit * jnp.sum(e_all, axis=1)[None, :], axis=1)
     energy = (energy + swap_core(energy)) / nvd

time: 168 us -> 162 us (0.964)
  waiting for transfers between devices: 73.9 us -> 92.5 us
  local copies, waits for them, and re-layouts: 21.2 us -> 7.14 us
  Pallas kernels: 34.2 us -> 26 us
  starting transfers between devices: 32.6 us -> 30.3 us
    ppermute x24, waiting for transfers between devices: 73.9 us -> 89.2 us  [pp(): return lax.ppermute(x, 'orb', perm)]
    unnamed x48 -> x14, local copies, waits for them, and re-layouts: 17.5 us -> 3.35 us
    pallas_call x7, Pallas kernels: 9.2 us -> 4.83 us  [pack(): pl.pallas_call(lambda *refs: pack_kernel(kinds, len(tbls), *refs), out_sh...]
    pallas_call x10, Pallas kernels: 15.5 us -> 11.2 us  [amplitudes(): pl.pallas_call(lambda *refs: amplitudes_kernel(mode, call, per_orb, [len(...]
    ppermute x5, waiting for transfers between devices: 0.01 us -> 3.3 us  [swap_core(): return lax.ppermute(x, 'aux', [(0, 1), (1, 0)])]
    ppermute x24, starting transfers between devices: 31.5 us -> 29.2 us  [pp(): return lax.ppermute(x, 'orb', perm)]
    pallas_call x2 -> x1, Pallas kernels: 3.84 us -> 4.07 us  [densities(): pl.pallas_call(density_kernel, out_shape=(shape, shape), in_specs=[SMEM,...]
  transfers between devices with their start and end apart: 29 -> 29, of which waited for: 9 -> 12; matrix products, arithmetic and copies ran while one was open for 3% -> 3% of each run, Pallas kernels for 18% -> 13%
where the time goes in v13:
time: 162 us; the launch traced here: 161 us
  waiting for transfers between devices  92.5 us (57%)
  starting transfers between devices  30.3 us (19%)
  Pallas kernels  26 us (16%)
  local copies, waits for them, and re-layouts  7.14 us (4%)
  other arithmetic  3.99 us (2%)
    ppermute x24, waiting for transfers between devices, pp(): return lax.ppermute(x, 'orb', perm)  89.2 us
    ppermute x24, starting transfers between devices, pp(): return lax.ppermute(x, 'orb', perm)  29.2 us
    pallas_call x10, Pallas kernels, amplitudes(): pl.pallas_call(lambda *refs: amplitudes_kernel(mode, call, per_orb, [len(...  11.2 us
    pallas_call x7, Pallas kernels, pack(): pl.pallas_call(lambda *refs: pack_kernel(kinds, len(tbls), *refs), out_sh...  4.83 us
    pallas_call x2, Pallas kernels, turn(): pl.pallas_call(turn_kernel, out_shape=[jax.ShapeDtypeStruct((count, cols,...  4.47 us
    pallas_call x1, Pallas kernels, densities(): pl.pallas_call(density_kernel, out_shape=(shape, shape), in_specs=[SMEM,...  4.07 us
    unnamed x14, local copies, waits for them, and re-layouts  3.35 us
    ppermute x5, waiting for transfers between devices, swap_core(): return lax.ppermute(x, 'aux', [(0, 1), (1, 0)])  3.3 us
  transfers between devices with their start and end apart: 29, of which 12 were waited for; matrix products, arithmetic and copies ran while one was open for 3% of the time, Pallas kernels for 13%

profile of v13, /device:TPU:0, one launch (start us, length us, event | category | flops | bytes accessed | tf_op | source)
XLA Modules:
  0.0 160.9 jit_solution(11940250172291876827)
XLA Ops:
  1.2 0.7 copy-done.1
  4.7 2.6 %collective-permute-start = (f32[24,384]{1,0:T(8,128)S(1)}, f32[24,384]{1,0:T(8,128)S(1)}, u32[]{:S(2)}, u32[]{:S(2)}) collective-permute-start(f32[24,384]{1,0:T(8,128)S(1)} %get-tuple-element.55.refs_1_), channel_id=1, source_target_pairs={{0,2},{2,0},{4,6},{6,4},{8,10},{10,8},{12,14},{14,12},{1,3},{3,1},... | collective-permute-start | bytes 110600 | tf_op jit(solution)/shard_map/ppermute | solution.py:416
  7.3 1.6 collective-permute-start.1
  8.9 3.0 %collective-permute-start.3 = (f32[24,384]{1,0:T(8,128)S(1)}, f32[24,384]{1,0:T(8,128)S(1)}, u32[]{:S(2)}, u32[]{:S(2)}) collective-permute-start(f32[24,384]{1,0:T(8,128)S(1)} %get-tuple-element.55.refs_1_), channel_id=1, source_target_pairs={{0,8},{2,10},{4,12},{6,14},{8,0},{10,2},{12,4},{14,6},{1,9},{3,11}... | collective-permute-start | bytes 110600 | tf_op jit(solution)/shard_map/ppermute | solution.py:416
  11.8 1.4 collective-permute-start.4
  13.3 3.5 %collective-permute-start.5 = (f32[24,384]{1,0:T(8,128)S(1)}, f32[24,384]{1,0:T(8,128)S(1)}, u32[]{:S(2)}, u32[]{:S(2)}) collective-permute-start(f32[24,384]{1,0:T(8,128)S(1)} %get-tuple-element.55.refs_1_), channel_id=1, source_target_pairs={{0,12},{2,14},{4,8},{6,10},{8,4},{10,6},{12,0},{14,2},{1,13},{3,15... | collective-permute-start | bytes 110600 | tf_op jit(solution)/shard_map/ppermute | solution.py:416
  17.0 1.3 constant_dynamic-slice_fusion.1.refs_2_.refs_5_
  18.4 0.8 collective-permute-done.5.refs_7_
  19.2 4.6 %collective-permute-done.6.refs_8_ = f32[24,384]{1,0:T(8,128)S(1)} collective-permute-done((f32[24,384]{1,0:T(8,128)S(1)}, f32[24,384]{1,0:T(8,128)S(1)}, u32[]{:S(2)}, u32[]{:S(2)}) %collective-permute-start.6) | collective-permute-done | bytes 36896 | tf_op jit(solution)/shard_map/ppermute | solution.py:416
  23.8 0.7 collective-permute-start.12
  24.6 1.3 tables.1
  25.9 1.3 constant_dynamic-slice_fusion.refs_3_.refs_6_
  27.2 0.7 pack.7.refs_7_
  28.2 3.2 %collective-permute-start.10 = (bf16[16,256,128]{2,1,0:T(8,128)(2,1)S(1)}, bf16[16,256,128]{2,1,0:T(8,128)(2,1)S(1)}, u32[]{:S(2)}, u32[]{:S(2)}) collective-permute-start(bf16[16,256,128]{2,1,0:T(8,128)(2,1)S(1)} %constant_dynamic-slice_fusion.refs_3_.refs_6_), channel_id=1, source_target_pairs={{0,4},{2,6},{4,0},{6,2},{8,12},{10,14},{12,8},{14,10},{1,5},{3,7},... | collective-permute-start | bytes 3145736 | tf_op jit(solution)/shard_map/ppermute | solution.py:416
  31.4 0.7 collective-permute-start.16
  32.2 3.1 %turn.2 = (bf16[16,256,256]{2,1,0:T(8,128)(2,1)S(1)}, bf16[16,256,256]{2,1,0:T(8,128)(2,1)S(1)}) custom-call(bf16[16,256,256]{2,1,0:T(8,128)(2,1)S(1)} %copy-done, bf16[16,256,256]{2,1,0:T(8,128)(2,1)} %collective-permute-done.7.refs_1_), custom_call_target="tpu_custom_call" | custom-call | flops 1 | bytes 1 | tf_op jit(solution)/shard_map/turn/pallas_call | solution.py:257
  35.9 1.3 amplitudes.10
  37.2 12.6 %collective-permute-done.8.refs_2_.refs_0_.refs_5_ = bf16[16,256,128]{2,1,0:T(8,128)(2,1)S(1)} collective-permute-done((bf16[16,256,128]{2,1,0:T(8,128)(2,1)S(1)}, bf16[16,256,128]{2,1,0:T(8,128)(2,1)S(1)}, u32[]{:S(2)}, u32[]{:S(2)}) %collective-permute-start.8) | collective-permute-done | bytes 1048608 | tf_op jit(solution)/shard_map/ppermute | solution.py:416
  49.9 0.7 pack.8.refs_6_
  50.9 10.7 %collective-permute-done.13.refs_7_.refs_5_ = bf16[1,8,256,128]{3,2,1,0:T(8,128)(2,1)S(1)} collective-permute-done((bf16[1,8,256,128]{3,2,1,0:T(8,128)(2,1)S(1)}, bf16[1,8,256,128]{3,2,1,0:T(8,128)(2,1)S(1)}, u32[]{:S(2)}, u32[]{:S(2)}) %collective-permute-start.13) | collective-permute-done | bytes 524320 | tf_op jit(solution)/shard_map/ppermute | solution.py:416
  61.6 1.3 amplitudes.11
  62.9 5.7 %collective-permute-done.10.refs_1_.refs_2_.refs_6_ = bf16[16,256,128]{2,1,0:T(8,128)(2,1)S(1)} collective-permute-done((bf16[16,256,128]{2,1,0:T(8,128)(2,1)S(1)}, bf16[16,256,128]{2,1,0:T(8,128)(2,1)S(1)}, u32[]{:S(2)}, u32[]{:S(2)}) %collective-permute-start.10) | collective-permute-done | bytes 1048608 | tf_op jit(solution)/shard_map/ppermute | solution.py:416
  69.3 1.3 collective-permute-start.17
  70.6 0.7 collective-permute-start.9
  71.3 0.7 collective-permute-start.19
  72.1 0.7 collective-permute-start.26
  72.8 0.7 pack.10.refs_9_
  73.5 1.3 turn.3
  76.1 1.3 collective-permute-start.21
  77.4 20.8 %collective-permute-done.17.refs_8_.refs_6_ = bf16[2,8,256,128]{3,2,1,0:T(8,128)(2,1)S(1)} collective-permute-done((bf16[2,8,256,128]{3,2,1,0:T(8,128)(2,1)S(1)}, bf16[2,8,256,128]{3,2,1,0:T(8,128)(2,1)S(1)}, u32[]{:S(2)}, u32[]{:S(2)}) %collective-permute-start.17) | collective-permute-done | bytes 1048608 | tf_op jit(solution)/shard_map/ppermute | solution.py:416
  98.2 1.6 %collective-permute-start.20 = (bf16[1,8,256,128]{3,2,1,0:T(8,128)(2,1)S(1)}, bf16[1,8,256,128]{3,2,1,0:T(8,128)(2,1)S(1)}, u32[]{:S(2)}, u32[]{:S(2)}) collective-permute-start(bf16[1,8,256,128]{3,2,1,0:T(8,128)(2,1)S(1)} %pack.10.refs_9_), channel_id=1, source_target_pairs={{0,2},{2,0},{4,6},{6,4},{8,10},{10,8},{12,14},{14,12},{1,3},{3,1},... | collective-permute-start | bytes 1572872 | tf_op jit(solution)/shard_map/ppermute | solution.py:416
  99.8 1.3 amplitudes.13
  102.6 5.5 %collective-permute-done.21.refs_7_ = bf16[8,256,128]{2,1,0:T(8,128)(2,1)S(1)} collective-permute-done((bf16[8,256,128]{2,1,0:T(8,128)(2,1)S(1)}, bf16[8,256,128]{2,1,0:T(8,128)(2,1)S(1)}, u32[]{:S(2)}, u32[]{:S(2)}) %collective-permute-start.21) | collective-permute-done | bytes 524320 | tf_op jit(solution)/shard_map/ppermute | solution.py:416
  108.0 1.3 collective-permute-start.23
  109.3 0.9 amplitudes.14
  110.2 0.8 collective-permute-done.20.refs_6_
  111.0 1.3 amplitudes.15
  113.0 1.3 collective-permute-start.24
  114.9 1.3 collective-permute-start.25
  117.6 5.5 %collective-permute-done.23.refs_9_.refs_7_ = bf16[1,8,256,128]{3,2,1,0:T(8,128)(2,1)S(1)} collective-permute-done((bf16[1,8,256,128]{3,2,1,0:T(8,128)(2,1)S(1)}, bf16[1,8,256,128]{3,2,1,0:T(8,128)(2,1)S(1)}, u32[]{:S(2)}, u32[]{:S(2)}) %collective-permute-start.23) | collective-permute-done | bytes 524320 | tf_op jit(solution)/shard_map/ppermute | solution.py:416
  123.1 1.3 amplitudes.17
  124.5 14.2 %collective-permute-done.24.refs_8_ = bf16[1,8,256,128]{3,2,1,0:T(8,128)(2,1)S(1)} collective-permute-done((bf16[1,8,256,128]{3,2,1,0:T(8,128)(2,1)S(1)}, bf16[1,8,256,128]{3,2,1,0:T(8,128)(2,1)S(1)}, u32[]{:S(2)}, u32[]{:S(2)}) %collective-permute-start.24) | collective-permute-done | bytes 524320 | tf_op jit(solution)/shard_map/ppermute | solution.py:416
  138.7 7.9 %collective-permute-done.25.refs_7_ = bf16[8,256,128]{2,1,0:T(8,128)(2,1)S(1)} collective-permute-done((bf16[8,256,128]{2,1,0:T(8,128)(2,1)S(1)}, bf16[8,256,128]{2,1,0:T(8,128)(2,1)S(1)}, u32[]{:S(2)}, u32[]{:S(2)}) %collective-permute-start.25) | collective-permute-done | bytes 524320 | tf_op jit(solution)/shard_map/ppermute | solution.py:416
  146.6 1.1 amplitudes.18
  147.7 1.4 amplitudes.19
  149.1 4.1 %densities.1 = (f32[16,128,256]{2,1,0:T(8,128)S(1)}, f32[16,128,256]{2,1,0:T(8,128)}) custom-call(s32[1]{0:T(128)} %bitcast.5.start, bf16[64,256,128]{2,1,0:T(8,128)(2,1)S(1)} %get-tuple-element.101.t), custom_call_target="tpu_custom_call" | custom-call | flops 1 | bytes 1 | tf_op jit(solution)/shard_map/densities/pallas_call | solution.py:394
  154.0 3.3 %collective-permute-done.27 = f32[64]{0:T(128)S(1)} collective-permute-done((f32[64]{0:T(128)S(1)}, f32[64]{0:T(128)S(1)}, u32[]{:S(2)}, u32[]{:S(2)}) %collective-permute-start.27) | collective-permute-done | bytes 288 | tf_op jit(solution)/shard_map/ppermute | solution.py:419
  157.8 3.2 %add.12 = f32[16,128,256]{2,1,0:T(8,128)} add(f32[16,128,256]{2,1,0:T(8,128)S(1)} %get-tuple-element.102, f32[16,128,256]{2,1,0:T(8,128)} %collective-permute-done.28) | non-fusion elementwise | flops 524288 | bytes 6291456 | tf_op jit(solution)/shard_map/add | solution.py:493
  (56 shorter events, 12.0 us)
Async XLA Ops:
  0.6 25.2 %collective-permute-start.7 = (bf16[16,256,256]{2,1,0:T(8,128)(2,1)}, bf16[16,256,256]{2,1,0:T(8,128)(2,1)}, u32[]{:S(2)}, u32[]{:S(2)}) collective-permute-start(bf16[16,256,256]{2,1,0:T(8,128)(2,1)} %refs_0_.3), channel_id=1, source_target_pairs={{0,1},{1,0},{2,3},{3,2},{4,5},{5,4},{6,7},{7,6},{8,9},{9,8},{10,11... | collective-permute-start | bytes 6291464 | tf_op jit(solution)/shard_map/ppermute | solution.py:419
  1.1 0.7 copy-start.1
  1.9 0.7 copy-start.3
  2.5 0.7 copy-start.4
  3.2 0.7 copy-start.5
  3.8 0.7 copy-start.6
  4.7 7.2 %collective-permute-start = (f32[24,384]{1,0:T(8,128)S(1)}, f32[24,384]{1,0:T(8,128)S(1)}, u32[]{:S(2)}, u32[]{:S(2)}) collective-permute-start(f32[24,384]{1,0:T(8,128)S(1)} %get-tuple-element.55.refs_1_), channel_id=1, source_target_pairs={{0,2},{2,0},{4,6},{6,4},{8,10},{10,8},{12,14},{14,12},{1,3},{3,1},... | collective-permute-start | bytes 110600 | tf_op jit(solution)/shard_map/ppermute | solution.py:416
  7.3 6.0 %collective-permute-start.1 = (f32[24,384]{1,0:T(8,128)S(1)}, f32[24,384]{1,0:T(8,128)S(1)}, u32[]{:S(2)}, u32[]{:S(2)}) collective-permute-start(f32[24,384]{1,0:T(8,128)S(1)} %get-tuple-element.55.refs_1_), channel_id=1, source_target_pairs={{0,4},{2,6},{4,0},{6,2},{8,12},{10,14},{12,8},{14,10},{1,5},{3,7},... | collective-permute-start | bytes 110600 | tf_op jit(solution)/shard_map/ppermute | solution.py:416
  8.8 7.9 %collective-permute-start.2 = (f32[24,384]{1,0:T(8,128)S(1)}, f32[24,384]{1,0:T(8,128)S(1)}, u32[]{:S(2)}, u32[]{:S(2)}) collective-permute-start(f32[24,384]{1,0:T(8,128)S(1)} %get-tuple-element.55.refs_1_), channel_id=1, source_target_pairs={{0,6},{2,4},{4,2},{6,0},{8,14},{10,12},{12,10},{14,8},{1,7},{3,5},... | collective-permute-start | bytes 110600 | tf_op jit(solution)/shard_map/ppermute | solution.py:416
  8.9 9.5 %collective-permute-start.3 = (f32[24,384]{1,0:T(8,128)S(1)}, f32[24,384]{1,0:T(8,128)S(1)}, u32[]{:S(2)}, u32[]{:S(2)}) collective-permute-start(f32[24,384]{1,0:T(8,128)S(1)} %get-tuple-element.55.refs_1_), channel_id=1, source_target_pairs={{0,8},{2,10},{4,12},{6,14},{8,0},{10,2},{12,4},{14,6},{1,9},{3,11}... | collective-permute-start | bytes 110600 | tf_op jit(solution)/shard_map/ppermute | solution.py:416
  11.8 6.5 %collective-permute-start.4 = (f32[24,384]{1,0:T(8,128)S(1)}, f32[24,384]{1,0:T(8,128)S(1)}, u32[]{:S(2)}, u32[]{:S(2)}) collective-permute-start(f32[24,384]{1,0:T(8,128)S(1)} %get-tuple-element.55.refs_1_), channel_id=1, source_target_pairs={{0,10},{2,8},{4,14},{6,12},{8,2},{10,0},{12,6},{14,4},{1,11},{3,9}... | collective-permute-start | bytes 110600 | tf_op jit(solution)/shard_map/ppermute | solution.py:416
  13.3 5.9 %collective-permute-start.5 = (f32[24,384]{1,0:T(8,128)S(1)}, f32[24,384]{1,0:T(8,128)S(1)}, u32[]{:S(2)}, u32[]{:S(2)}) collective-permute-start(f32[24,384]{1,0:T(8,128)S(1)} %get-tuple-element.55.refs_1_), channel_id=1, source_target_pairs={{0,12},{2,14},{4,8},{6,10},{8,4},{10,6},{12,0},{14,2},{1,13},{3,15... | collective-permute-start | bytes 110600 | tf_op jit(solution)/shard_map/ppermute | solution.py:416
  16.7 7.1 %collective-permute-start.6 = (f32[24,384]{1,0:T(8,128)S(1)}, f32[24,384]{1,0:T(8,128)S(1)}, u32[]{:S(2)}, u32[]{:S(2)}) collective-permute-start(f32[24,384]{1,0:T(8,128)S(1)} %get-tuple-element.55.refs_1_), channel_id=1, source_target_pairs={{0,14},{2,12},{4,10},{6,8},{8,6},{10,4},{12,2},{14,0},{1,15},{3,13... | collective-permute-start | bytes 110600 | tf_op jit(solution)/shard_map/ppermute | solution.py:416
  23.8 26.1 %collective-permute-start.8 = (bf16[16,256,128]{2,1,0:T(8,128)(2,1)S(1)}, bf16[16,256,128]{2,1,0:T(8,128)(2,1)S(1)}, u32[]{:S(2)}, u32[]{:S(2)}) collective-permute-start(bf16[16,256,128]{2,1,0:T(8,128)(2,1)S(1)} %constant_dynamic-slice_fusion.1.refs_2_.refs_5_), channel_id=1, source_target_pairs={{0,4},{2,6},{4,0},{6,2},{8,12},{10,14},{12,8},{14,10},{1,5},{3,7},... | collective-permute-start | bytes 3145736 | tf_op jit(solution)/shard_map/ppermute | solution.py:416
  23.8 26.1 %collective-permute-start.12 = (bf16[16,256,128]{2,1,0:T(8,128)(2,1)S(1)}, bf16[16,256,128]{2,1,0:T(8,128)(2,1)S(1)}, u32[]{:S(2)}, u32[]{:S(2)}) collective-permute-start(bf16[16,256,128]{2,1,0:T(8,128)(2,1)S(1)} %constant_dynamic-slice_fusion.1.refs_2_.refs_5_), channel_id=1, source_target_pairs={{4,8},{6,10},{8,4},{10,6},{5,9},{7,11},{9,5},{11,7},{20,24},{22,26... | collective-permute-start | bytes 3145736 | tf_op jit(solution)/shard_map/ppermute | solution.py:416
  27.2 5.0 %copy-start = (bf16[16,256,256]{2,1,0:T(8,128)(2,1)S(1)}, bf16[16,256,256]{2,1,0:T(8,128)(2,1)}, u32[]{:S(2)}) copy-start(bf16[16,256,256]{2,1,0:T(8,128)(2,1)} %refs_0_.3) | copy-start | bytes 6291460
  28.0 7.4 %copy-start.2 = (f32[16,256]{1,0:T(8,128)S(1)}, f32[16,256]{1,0:T(8,128)}, u32[]{:S(2)}) copy-start(f32[16,256]{1,0:T(8,128)} %refs_0_.2) | copy-start | bytes 49156
  28.0 33.6 %collective-permute-start.11 = (bf16[2,8,256,128]{3,2,1,0:T(8,128)(2,1)S(1)}, bf16[2,8,256,128]{3,2,1,0:T(8,128)(2,1)S(1)}, u32[]{:S(2)}, u32[]{:S(2)}) collective-permute-start(bf16[2,8,256,128]{3,2,1,0:T(8,128)(2,1)S(1)} %pack.7.refs_7_), channel_id=1, source_target_pairs={{0,2},{2,0},{4,6},{6,4},{8,10},{10,8},{12,14},{14,12},{1,3},{3,1},... | collective-permute-start | bytes 3145736 | tf_op jit(solution)/shard_map/ppermute | solution.py:416
  28.2 40.4 %collective-permute-start.10 = (bf16[16,256,128]{2,1,0:T(8,128)(2,1)S(1)}, bf16[16,256,128]{2,1,0:T(8,128)(2,1)S(1)}, u32[]{:S(2)}, u32[]{:S(2)}) collective-permute-start(bf16[16,256,128]{2,1,0:T(8,128)(2,1)S(1)} %constant_dynamic-slice_fusion.refs_3_.refs_6_), channel_id=1, source_target_pairs={{0,4},{2,6},{4,0},{6,2},{8,12},{10,14},{12,8},{14,10},{1,5},{3,7},... | collective-permute-start | bytes 3145736 | tf_op jit(solution)/shard_map/ppermute | solution.py:416
  31.4 37.2 %collective-permute-start.16 = (bf16[16,256,128]{2,1,0:T(8,128)(2,1)S(1)}, bf16[16,256,128]{2,1,0:T(8,128)(2,1)S(1)}, u32[]{:S(2)}, u32[]{:S(2)}) collective-permute-start(bf16[16,256,128]{2,1,0:T(8,128)(2,1)S(1)} %constant_dynamic-slice_fusion.refs_3_.refs_6_), channel_id=1, source_target_pairs={{4,8},{6,10},{8,4},{10,6},{5,9},{7,11},{9,5},{11,7},{20,24},{22,26... | collective-permute-start | bytes 3145736 | tf_op jit(solution)/shard_map/ppermute | solution.py:416
  50.6 11.0 %collective-permute-start.13 = (bf16[1,8,256,128]{3,2,1,0:T(8,128)(2,1)S(1)}, bf16[1,8,256,128]{3,2,1,0:T(8,128)(2,1)S(1)}, u32[]{:S(2)}, u32[]{:S(2)}) collective-permute-start(bf16[1,8,256,128]{3,2,1,0:T(8,128)(2,1)S(1)} %pack.8.refs_6_), channel_id=1, source_target_pairs={{0,2},{2,0},{4,6},{6,4},{8,10},{10,8},{12,14},{14,12},{1,3},{3,1},... | collective-permute-start | bytes 1572872 | tf_op jit(solution)/shard_map/ppermute | solution.py:416
  50.9 21.2 %collective-permute-start.14 = (bf16[16,256,128]{2,1,0:T(8,128)(2,1)S(1)}, bf16[16,256,128]{2,1,0:T(8,128)(2,1)S(1)}, u32[]{:S(2)}, u32[]{:S(2)}) collective-permute-start(bf16[16,256,128]{2,1,0:T(8,128)(2,1)S(1)} %collective-permute-done.8.refs_2_.refs_0_.refs_5_), channel_id=1, source_target_pairs={{0,1},{1,0},{2,3},{3,2},{4,5},{5,4},{6,7},{7,6},{8,9},{9,8},{10,11... | collective-permute-start | bytes 3145736 | tf_op jit(solution)/shard_map/ppermute | solution.py:419
  68.6 4.9 %collective-permute-start.15 = (bf16[16,256,128]{2,1,0:T(8,128)(2,1)S(1)}, bf16[16,256,128]{2,1,0:T(8,128)(2,1)S(1)}, u32[]{:S(2)}, u32[]{:S(2)}) collective-permute-start(bf16[16,256,128]{2,1,0:T(8,128)(2,1)S(1)} %collective-permute-done.10.refs_1_.refs_2_.refs_6_), channel_id=1, source_target_pairs={{0,1},{1,0},{2,3},{3,2},{4,5},{5,4},{6,7},{7,6},{8,9},{9,8},{10,11... | collective-permute-start | bytes 3145736 | tf_op jit(solution)/shard_map/ppermute | solution.py:419
  69.3 28.9 %collective-permute-start.17 = (bf16[2,8,256,128]{3,2,1,0:T(8,128)(2,1)S(1)}, bf16[2,8,256,128]{3,2,1,0:T(8,128)(2,1)S(1)}, u32[]{:S(2)}, u32[]{:S(2)}) collective-permute-start(bf16[2,8,256,128]{3,2,1,0:T(8,128)(2,1)S(1)} %get-tuple-element.85.refs_3_), channel_id=1, source_target_pairs={{4,2},{6,0},{8,14},{10,12},{5,3},{7,1},{9,15},{11,13},{20,18},{22,... | collective-permute-start | bytes 3145736 | tf_op jit(solution)/shard_map/ppermute | solution.py:416
  70.6 30.6 %collective-permute-start.9 = (bf16[16,256,128]{2,1,0:T(8,128)(2,1)S(1)}, bf16[16,256,128]{2,1,0:T(8,128)(2,1)S(1)}, u32[]{:S(2)}, u32[]{:S(2)}) collective-permute-start(bf16[16,256,128]{2,1,0:T(8,128)(2,1)S(1)} %collective-permute-done.8.refs_2_.refs_0_.refs_5_), channel_id=1, source_target_pairs={{4,8},{6,10},{8,4},{10,6},{5,9},{7,11},{9,5},{11,7},{20,24},{22,26... | collective-permute-start | bytes 3145736 | tf_op jit(solution)/shard_map/ppermute | solution.py:416
  71.3 41.0 %collective-permute-start.19 = (bf16[16,256,128]{2,1,0:T(8,128)(2,1)S(1)}, bf16[16,256,128]{2,1,0:T(8,128)(2,1)S(1)}, u32[]{:S(2)}, u32[]{:S(2)}) collective-permute-start(bf16[16,256,128]{2,1,0:T(8,128)(2,1)S(1)} %collective-permute-done.10.refs_1_.refs_2_.refs_6_), channel_id=1, source_target_pairs={{4,8},{6,10},{8,4},{10,6},{5,9},{7,11},{9,5},{11,7},{20,24},{22,26... | collective-permute-start | bytes 3145736 | tf_op jit(solution)/shard_map/ppermute | solution.py:416
  72.1 44.8 %collective-permute-start.26 = (bf16[2,8,256,128]{3,2,1,0:T(8,128)(2,1)S(1)}, bf16[2,8,256,128]{3,2,1,0:T(8,128)(2,1)S(1)}, u32[]{:S(2)}, u32[]{:S(2)}) collective-permute-start(bf16[2,8,256,128]{3,2,1,0:T(8,128)(2,1)S(1)} %get-tuple-element.94), channel_id=1, source_target_pairs={{4,6},{6,4},{8,10},{10,8},{5,7},{7,5},{9,11},{11,9},{20,22},{22,20... | collective-permute-start | bytes 3145736 | tf_op jit(solution)/shard_map/ppermute | solution.py:416
  76.1 31.9 %collective-permute-start.21 = (bf16[8,256,128]{2,1,0:T(8,128)(2,1)S(1)}, bf16[8,256,128]{2,1,0:T(8,128)(2,1)S(1)}, u32[]{:S(2)}, u32[]{:S(2)}) collective-permute-start(bf16[8,256,128]{2,1,0:T(8,128)(2,1)S(1)} %amplitudes.12.refs_7_), channel_id=1, source_target_pairs={{4,0},{6,2},{8,12},{10,14},{5,1},{7,3},{9,13},{11,15},{20,16},{22,... | collective-permute-start | bytes 1572872 | tf_op jit(solution)/shard_map/ppermute | solution.py:416
  98.2 12.8 %collective-permute-start.20 = (bf16[1,8,256,128]{3,2,1,0:T(8,128)(2,1)S(1)}, bf16[1,8,256,128]{3,2,1,0:T(8,128)(2,1)S(1)}, u32[]{:S(2)}, u32[]{:S(2)}) collective-permute-start(bf16[1,8,256,128]{3,2,1,0:T(8,128)(2,1)S(1)} %pack.10.refs_9_), channel_id=1, source_target_pairs={{0,2},{2,0},{4,6},{6,4},{8,10},{10,8},{12,14},{14,12},{1,3},{3,1},... | collective-permute-start | bytes 1572872 | tf_op jit(solution)/shard_map/ppermute | solution.py:416
  101.9 15.8 %collective-permute-start.18 = (bf16[1,8,256,128]{3,2,1,0:T(8,128)(2,1)S(1)}, bf16[1,8,256,128]{3,2,1,0:T(8,128)(2,1)S(1)}, u32[]{:S(2)}, u32[]{:S(2)}) collective-permute-start(bf16[1,8,256,128]{3,2,1,0:T(8,128)(2,1)S(1)} %get-tuple-element.88), channel_id=1, source_target_pairs={{4,6},{6,4},{8,10},{10,8},{5,7},{7,5},{9,11},{11,9},{20,22},{22,20... | collective-permute-start | bytes 1572872 | tf_op jit(solution)/shard_map/ppermute | solution.py:416
  108.0 15.1 %collective-permute-start.23 = (bf16[1,8,256,128]{3,2,1,0:T(8,128)(2,1)S(1)}, bf16[1,8,256,128]{3,2,1,0:T(8,128)(2,1)S(1)}, u32[]{:S(2)}, u32[]{:S(2)}) collective-permute-start(bf16[1,8,256,128]{3,2,1,0:T(8,128)(2,1)S(1)} %get-tuple-element.89.refs_8_), channel_id=1, source_target_pairs={{4,2},{6,0},{8,14},{10,12},{5,3},{7,1},{9,15},{11,13},{20,18},{22,... | collective-permute-start | bytes 1572872 | tf_op jit(solution)/shard_map/ppermute | solution.py:416
  113.0 25.7 %collective-permute-start.24 = (bf16[1,8,256,128]{3,2,1,0:T(8,128)(2,1)S(1)}, bf16[1,8,256,128]{3,2,1,0:T(8,128)(2,1)S(1)}, u32[]{:S(2)}, u32[]{:S(2)}) collective-permute-start(bf16[1,8,256,128]{3,2,1,0:T(8,128)(2,1)S(1)} %pack.12.refs_9_), channel_id=1, source_target_pairs={{4,2},{6,0},{8,14},{10,12},{5,3},{7,1},{9,15},{11,13},{20,18},{22,... | collective-permute-start | bytes 1572872 | tf_op jit(solution)/shard_map/ppermute | solution.py:416
  114.9 31.7 %collective-permute-start.25 = (bf16[8,256,128]{2,1,0:T(8,128)(2,1)S(1)}, bf16[8,256,128]{2,1,0:T(8,128)(2,1)S(1)}, u32[]{:S(2)}, u32[]{:S(2)}) collective-permute-start(bf16[8,256,128]{2,1,0:T(8,128)(2,1)S(1)} %amplitudes.16.refs_3_), channel_id=1, source_target_pairs={{4,0},{6,2},{8,12},{10,14},{5,1},{7,3},{9,13},{11,15},{20,16},{22,... | collective-permute-start | bytes 1572872 | tf_op jit(solution)/shard_map/ppermute | solution.py:416
  116.9 30.8 %collective-permute-start.22 = (bf16[1,8,256,128]{3,2,1,0:T(8,128)(2,1)S(1)}, bf16[1,8,256,128]{3,2,1,0:T(8,128)(2,1)S(1)}, u32[]{:S(2)}, u32[]{:S(2)}) collective-permute-start(bf16[1,8,256,128]{3,2,1,0:T(8,128)(2,1)S(1)} %pack.13.refs_7_), channel_id=1, source_target_pairs={{4,6},{6,4},{8,10},{10,8},{5,7},{7,5},{9,11},{11,9},{20,22},{22,20... | collective-permute-start | bytes 1572872 | tf_op jit(solution)/shard_map/ppermute | solution.py:416
  153.1 4.6 %collective-permute-start.28 = (f32[16,128,256]{2,1,0:T(8,128)}, f32[16,128,256]{2,1,0:T(8,128)}, u32[]{:S(2)}, u32[]{:S(2)}) collective-permute-start(f32[16,128,256]{2,1,0:T(8,128)} %get-tuple-element.103), channel_id=1, source_target_pairs={{0,1},{1,0},{2,3},{3,2},{4,5},{5,4},{6,7},{7,6},{8,9},{9,8},{10,11... | collective-permute-start | bytes 6291464 | tf_op jit(solution)/shard_map/ppermute | solution.py:419
  153.4 3.9 %collective-permute-start.27 = (f32[64]{0:T(128)S(1)}, f32[64]{0:T(128)S(1)}, u32[]{:S(2)}, u32[]{:S(2)}) collective-permute-start(f32[64]{0:T(128)S(1)} %multiply_reduce_fusion), channel_id=1, source_target_pairs={{0,1},{1,0},{2,3},{3,2},{4,5},{5,4},{6,7},{7,6},{8,9},{9,8},{10,11... | collective-permute-start | bytes 776 | tf_op jit(solution)/shard_map/ppermute | solution.py:419

commit v14 on v13

--- a/solution.py
+++ b/solution.py
@@ -374,18 +374,15 @@
     )(*operands, *held)
 
 
-def density_kernel(start, t, mine, away):
-    count, half = mine.shape[:2]
+def density_kernel(start, t, d):
+    count, half = d.shape[:2]
     per_orb = t.shape[0] // count
     first = pl.multiple_of(start[0], half)
     for o in range(count):
         own = range(o * per_orb, (o + 1) * per_orb)
         right = jnp.concatenate([t[k] for k in own], axis=1)
-        for out, row in ((away, pl.multiple_of(half - first, half)), (mine, first)):
-            left = jnp.concatenate([t[k, pl.ds(row, half), :] for k in own], axis=1)
-            out[o] = lax.dot_general(
-                left, right, (((1,), (1,)), ((), ())), preferred_element_type=f32
-            )
+        left = jnp.concatenate([t[k, pl.ds(first, half), :] for k in own], axis=1)
+        d[o] = lax.dot_general(left, right, (((1,), (1,)), ((), ())), preferred_element_type=f32)
 
 
 def densities(t_all, start, per_orb, half):
@@ -393,9 +390,9 @@
     shape = jax.ShapeDtypeStruct((npair // per_orb, half, nvd), f32)
     return pl.pallas_call(
         density_kernel,
-        out_shape=(shape, shape),
+        out_shape=shape,
         in_specs=[SMEM, VMEM],
-        out_specs=(VMEM, VMEM),
+        out_specs=VMEM,
         compiler_params=LIGHT,
         cost_estimate=TINY,
         name="densities",
@@ -451,7 +448,7 @@
     (packed,) = pack(lists_of, [(0, 0, own, False)], cap)
     beside = pp(packed, flip(1))
     left = turn([blocks, other])
-    held = own_pairs(0, "slots", [own], after=(packed,))
+    held = own_pairs(0, "slots", [own], after=(packed, mid[0]))
     first, held = lax.optimization_barrier((near[0], held))
     far = [pp(first, cross)]
     across = [swap_core(first)]
@@ -489,8 +486,8 @@
     held = own_pairs(3, "served", [far], held, (fourth_diagonal[1],), (ready_3,))
     t_all, e_all = own_pairs(7, "asked", [fourth, fourth_diagonal], held)
 
-    mine, away = densities(t_all, col0, per_orb, half)
-    density = mine + swap_core(away)
+    away = swap_core(densities(t_all, half - col0, per_orb, half))
+    density = densities(t_all, col0, per_orb, half) + away
 
     energy = jnp.sum(hit * jnp.sum(e_all, axis=1)[None, :], axis=1)
     energy = (energy + swap_core(energy)) / nvd

time: 162 us -> 165 us (1.019)
  waiting for transfers between devices: 92.5 us -> 78 us
  local copies, waits for them, and re-layouts: 7.14 us -> 17.4 us
  Pallas kernels: 26 us -> 33.4 us
    ppermute x24, waiting for transfers between devices: 89.2 us -> 78 us  [pp(): return lax.ppermute(x, 'orb', perm)]
    unnamed x14 -> x46, local copies, waits for them, and re-layouts: 3.35 us -> 13.6 us
    pallas_call x10, Pallas kernels: 11.2 us -> 15.6 us  [amplitudes(): pl.pallas_call(lambda *refs: amplitudes_kernel(mode, call, per_orb, [len(...]
    pallas_call x7, Pallas kernels: 4.83 us -> 9.14 us  [pack(): pl.pallas_call(lambda *refs: pack_kernel(kinds, len(tbls), *refs), out_sh...]
    ppermute x5, waiting for transfers between devices: 3.3 us -> 0.01 us  [swap_core(): return lax.ppermute(x, 'aux', [(0, 1), (1, 0)])]
    pallas_call x1 -> x2, Pallas kernels: 4.07 us -> 2.95 us  [densities(): pl.pallas_call(density_kernel, out_shape=shape, in_specs=[SMEM, VMEM], ou...]
  transfers between devices with their start and end apart: 29 -> 29, of which waited for: 12 -> 10; matrix products, arithmetic and copies ran while one was open for 3% -> 3% of each run, Pallas kernels for 13% -> 18%
where the time goes in v14:
time: 165 us; the launch traced here: 164 us
  waiting for transfers between devices  78 us (47%)
  Pallas kernels  33.4 us (20%)
  starting transfers between devices  30.3 us (18%)
  local copies, waits for them, and re-layouts  17.4 us (11%)
  other arithmetic  4.14 us (3%)
    ppermute x24, waiting for transfers between devices, pp(): return lax.ppermute(x, 'orb', perm)  78 us
    ppermute x24, starting transfers between devices, pp(): return lax.ppermute(x, 'orb', perm)  29.2 us
    pallas_call x10, Pallas kernels, amplitudes(): pl.pallas_call(lambda *refs: amplitudes_kernel(mode, call, per_orb, [len(...  15.6 us
    unnamed x46, local copies, waits for them, and re-layouts  13.6 us
    pallas_call x7, Pallas kernels, pack(): pl.pallas_call(lambda *refs: pack_kernel(kinds, len(tbls), *refs), out_sh...  9.14 us
    pallas_call x2, Pallas kernels, turn(): pl.pallas_call(turn_kernel, out_shape=[jax.ShapeDtypeStruct((count, cols,...  4.26 us
    add x1, other arithmetic, line_plan(): density = densities(t_all, col0, per_orb, half) + away  3.33 us
  transfers between devices with their start and end apart: 29, of which 10 were waited for; matrix products, arithmetic and copies ran while one was open for 3% of the time, Pallas kernels for 18%

profile of v14, /device:TPU:0, one launch (start us, length us, event | category | flops | bytes accessed | tf_op | source)
XLA Modules:
  0.0 164.2 jit_solution(13640029115651116078)
XLA Ops:
  4.7 2.6 %collective-permute-start = (f32[24,384]{1,0:T(8,128)S(1)}, f32[24,384]{1,0:T(8,128)S(1)}, u32[]{:S(2)}, u32[]{:S(2)}) collective-permute-start(f32[24,384]{1,0:T(8,128)S(1)} %get-tuple-element.53.refs_1_), channel_id=1, source_target_pairs={{0,2},{2,0},{4,6},{6,4},{8,10},{10,8},{12,14},{14,12},{1,3},{3,1},... | collective-permute-start | bytes 110600 | tf_op jit(solution)/shard_map/ppermute | solution.py:413
  7.3 1.6 collective-permute-start.1
  8.9 3.0 %collective-permute-start.3 = (f32[24,384]{1,0:T(8,128)S(1)}, f32[24,384]{1,0:T(8,128)S(1)}, u32[]{:S(2)}, u32[]{:S(2)}) collective-permute-start(f32[24,384]{1,0:T(8,128)S(1)} %get-tuple-element.53.refs_1_), channel_id=1, source_target_pairs={{0,8},{2,10},{4,12},{6,14},{8,0},{10,2},{12,4},{14,6},{1,9},{3,11}... | collective-permute-start | bytes 110600 | tf_op jit(solution)/shard_map/ppermute | solution.py:413
  11.8 1.4 collective-permute-start.4
  13.3 3.5 %collective-permute-start.5 = (f32[24,384]{1,0:T(8,128)S(1)}, f32[24,384]{1,0:T(8,128)S(1)}, u32[]{:S(2)}, u32[]{:S(2)}) collective-permute-start(f32[24,384]{1,0:T(8,128)S(1)} %get-tuple-element.53.refs_1_), channel_id=1, source_target_pairs={{0,12},{2,14},{4,8},{6,10},{8,4},{10,6},{12,0},{14,2},{1,13},{3,15... | collective-permute-start | bytes 110600 | tf_op jit(solution)/shard_map/ppermute | solution.py:413
  17.0 2.3 %constant_dynamic-slice_fusion.1.refs_2_.refs_5_ = bf16[16,256,128]{2,1,0:T(8,128)(2,1)} fusion(bf16[16,256,256]{2,1,0:T(8,128)(2,1)} %refs_0_.3, s32[]{:T(128)S(6)} %select_n.4), kind=kLoop, calls=%fused_computation.4 | loop fusion | bytes 2097156 | tf_op jit(solution)/shard_map/dynamic_slice | solution.py:430
  19.4 4.0 %collective-permute-done.6.refs_8_ = f32[24,384]{1,0:T(8,128)S(1)} collective-permute-done((f32[24,384]{1,0:T(8,128)S(1)}, f32[24,384]{1,0:T(8,128)S(1)}, u32[]{:S(2)}, u32[]{:S(2)}) %collective-permute-start.6) | collective-permute-done | bytes 36896 | tf_op jit(solution)/shard_map/ppermute | solution.py:413
  24.5 1.3 tables.1
  26.0 1.5 pack.7.refs_7_
  28.0 1.9 %collective-permute-start.11 = (bf16[16,256,128]{2,1,0:T(8,128)(2,1)S(1)}, bf16[16,256,128]{2,1,0:T(8,128)(2,1)S(1)}, u32[]{:S(2)}, u32[]{:S(2)}) collective-permute-start(bf16[16,256,128]{2,1,0:T(8,128)(2,1)S(1)} %constant_dynamic-slice_fusion.refs_3_.refs_6_), channel_id=1, source_target_pairs={{0,4},{2,6},{4,0},{6,2},{8,12},{10,14},{12,8},{14,10},{1,5},{3,7},... | collective-permute-start | bytes 3145736 | tf_op jit(solution)/shard_map/ppermute | solution.py:413
  30.6 1.3 turn.2
  32.6 2.8 %amplitudes.10 = (bf16[64,256,128]{2,1,0:T(8,128)(2,1)S(1)}, f32[64,128]{1,0:T(8,128)S(1)}) custom-call(s32[8,128]{1,0:T(8,128)S(1)} %get-tuple-element.61.refs_0_, f32[64,128]{1,0:T(8,128)S(1)} %get-tuple-element.62.refs_1_, f32[16,256,128]{2,1,0:T(8,128)S(1)} %broadcast_in_dim.4.refs_2_, bf16[16,256,256]{2,1,0:T(8,128)(2,1)S(1)} %get-tuple-element.63.refs_3_, ...), custom_call_target="tpu_custom_call" | custom-call | flops 1 | bytes 1 | tf_op jit(solution)/shard_map/amplitudes/pallas_call | solution.py:365
  35.3 15.3 %collective-permute-done.8.refs_2_.refs_0_.refs_5_ = bf16[16,256,128]{2,1,0:T(8,128)(2,1)} collective-permute-done((bf16[16,256,128]{2,1,0:T(8,128)(2,1)}, bf16[16,256,128]{2,1,0:T(8,128)(2,1)}, u32[]{:S(2)}, u32[]{:S(2)}) %collective-permute-start.8) | collective-permute-done | bytes 1048608 | tf_op jit(solution)/shard_map/ppermute | solution.py:413
  50.6 1.3 pack.8.refs_6_
  52.5 9.2 %collective-permute-done.13.refs_7_.refs_5_ = bf16[1,8,256,128]{3,2,1,0:T(8,128)(2,1)S(1)} collective-permute-done((bf16[1,8,256,128]{3,2,1,0:T(8,128)(2,1)S(1)}, bf16[1,8,256,128]{3,2,1,0:T(8,128)(2,1)S(1)}, u32[]{:S(2)}, u32[]{:S(2)}) %collective-permute-start.13) | collective-permute-done | bytes 524320 | tf_op jit(solution)/shard_map/ppermute | solution.py:413
  61.6 1.3 amplitudes.11
  62.9 6.6 %collective-permute-done.11.refs_1_.refs_2_.refs_6_ = bf16[16,256,128]{2,1,0:T(8,128)(2,1)S(1)} collective-permute-done((bf16[16,256,128]{2,1,0:T(8,128)(2,1)S(1)}, bf16[16,256,128]{2,1,0:T(8,128)(2,1)S(1)}, u32[]{:S(2)}, u32[]{:S(2)}) %collective-permute-start.11) | collective-permute-done | bytes 1048608 | tf_op jit(solution)/shard_map/ppermute | solution.py:413
  70.3 1.3 collective-permute-start.17
  74.5 2.9 %turn.3 = (bf16[16,128,256]{2,1,0:T(8,128)(2,1)S(1)}, bf16[16,128,256]{2,1,0:T(8,128)(2,1)S(1)}, bf16[16,128,256]{2,1,0:T(8,128)(2,1)S(1)}, bf16[16,128,256]{2,1,0:T(8,128)(2,1)S(1)}) custom-call(bf16[16,256,128]{2,1,0:T(8,128)(2,1)} %collective-permute-done.8.refs_2_.refs_0_.refs_5_, ...), custom_call_target="tpu_custom_call" | custom-call | flops 1 | bytes 1 | tf_op jit(solution)/shard_map/turn/pallas_call | solution.py:257
  78.7 1.3 collective-permute-start.21
  80.0 19.0 %collective-permute-done.17.refs_8_.refs_6_ = bf16[2,8,256,128]{3,2,1,0:T(8,128)(2,1)S(1)} collective-permute-done((bf16[2,8,256,128]{3,2,1,0:T(8,128)(2,1)S(1)}, bf16[2,8,256,128]{3,2,1,0:T(8,128)(2,1)S(1)}, u32[]{:S(2)}, u32[]{:S(2)}) %collective-permute-start.17) | collective-permute-done | bytes 1048608 | tf_op jit(solution)/shard_map/ppermute | solution.py:413
  99.5 2.0 %amplitudes.13 = (bf16[64,256,128]{2,1,0:T(8,128)(2,1)S(1)}, f32[64,128]{1,0:T(8,128)S(1)}) custom-call(s32[8,128]{1,0:T(8,128)S(1)} %get-tuple-element.61.refs_0_, f32[64,128]{1,0:T(8,128)S(1)} %get-tuple-element.62.refs_1_, f32[16,256,128]{2,1,0:T(8,128)S(1)} %broadcast_in_dim.4.refs_2_, ...), custom_call_target="tpu_custom_call", output_to_operand_aliasing={{0}: (9, {}), {1}: (10, {})} | custom-call | flops 1 | bytes 1 | tf_op jit(solution)/shard_map/amplitudes/pallas_call | solution.py:365
  101.5 1.7 %pack.11 = (bf16[1,8,256,128]{3,2,1,0:T(8,128)(2,1)}, bf16[1,8,256,128]{3,2,1,0:T(8,128)(2,1)}) custom-call(s32[8,128]{1,0:T(8,128)S(1)} %get-tuple-element.65.refs_0_, s32[8,128]{1,0:T(8,128)S(1)} %get-tuple-element.66.refs_1_, bf16[16,256,128]{2,1,0:T(8,128)(2,1)S(1)} %collective-permute-done.10.refs_2_.refs_3_.refs_7_.refs_5_, ...), custom_call_target="tpu_custom_call" | custom-call | flops 1 | bytes 1 | tf_op jit(solution)/shard_map/pack/pallas_call | solution.py:235
  103.2 1.4 collective-permute-start.18
  104.6 4.3 %collective-permute-done.21.refs_7_ = bf16[8,256,128]{2,1,0:T(8,128)(2,1)S(1)} collective-permute-done((bf16[8,256,128]{2,1,0:T(8,128)(2,1)S(1)}, bf16[8,256,128]{2,1,0:T(8,128)(2,1)S(1)}, u32[]{:S(2)}, u32[]{:S(2)}) %collective-permute-start.21) | collective-permute-done | bytes 524320 | tf_op jit(solution)/shard_map/ppermute | solution.py:413
  108.9 1.3 collective-permute-start.23
  111.1 1.1 collective-permute-done.20.refs_6_
  112.2 1.3 amplitudes.15
  113.5 1.9 %pack.12.refs_9_ = bf16[1,8,256,128]{3,2,1,0:T(8,128)(2,1)} custom-call(s32[8,128]{1,0:T(8,128)S(1)} %get-tuple-element.65.refs_0_, s32[8,128]{1,0:T(8,128)S(1)} %get-tuple-element.66.refs_1_, bf16[16,256,128]{2,1,0:T(8,128)(2,1)S(1)} %collective-permute-done.19.refs_2_.refs_8_.refs_6_, f32[64,128]{1,0:T(8,128)S(1)} %get-tuple-element.91.refs_3_.refs_11_), custom_call_target="tpu_custom_call" | custom-call | flops 1 | bytes 1 | tf_op jit(solution)/shard_map/pack/pallas_call | solution.py:235
  115.5 1.3 collective-permute-start.24
  116.7 1.4 amplitudes.16.refs_3_
  118.2 1.4 collective-permute-start.25
  119.6 1.5 pack.13.refs_7_
  122.1 1.5 collective-permute-start.22
  123.6 2.0 %collective-permute-done.23.refs_9_.refs_7_ = bf16[1,8,256,128]{3,2,1,0:T(8,128)(2,1)} collective-permute-done((bf16[1,8,256,128]{3,2,1,0:T(8,128)(2,1)}, bf16[1,8,256,128]{3,2,1,0:T(8,128)(2,1)}, u32[]{:S(2)}, u32[]{:S(2)}) %collective-permute-start.23) | collective-permute-done | bytes 524320 | tf_op jit(solution)/shard_map/ppermute | solution.py:413
  125.6 2.2 %copy-done.1 = bf16[64,256,128]{2,1,0:T(8,128)(2,1)S(1)} copy-done((bf16[64,256,128]{2,1,0:T(8,128)(2,1)S(1)}, bf16[64,256,128]{2,1,0:T(8,128)(2,1)}, u32[]{:S(2)}) %copy-start.1) | copy-done | bytes 4194328
  127.8 1.6 copy-done.5
  129.4 1.6 copy-done.7
  130.9 1.2 copy-done.16
  132.2 1.4 amplitudes.17
  133.6 7.4 %collective-permute-done.24.refs_8_ = bf16[1,8,256,128]{3,2,1,0:T(8,128)(2,1)} collective-permute-done((bf16[1,8,256,128]{3,2,1,0:T(8,128)(2,1)}, bf16[1,8,256,128]{3,2,1,0:T(8,128)(2,1)}, u32[]{:S(2)}, u32[]{:S(2)}) %collective-permute-start.24) | collective-permute-done | bytes 524320 | tf_op jit(solution)/shard_map/ppermute | solution.py:413
  140.9 9.1 %collective-permute-done.25.refs_7_ = bf16[8,256,128]{2,1,0:T(8,128)(2,1)} collective-permute-done((bf16[8,256,128]{2,1,0:T(8,128)(2,1)}, bf16[8,256,128]{2,1,0:T(8,128)(2,1)}, u32[]{:S(2)}, u32[]{:S(2)}) %collective-permute-start.25) | collective-permute-done | bytes 524320 | tf_op jit(solution)/shard_map/ppermute | solution.py:413
  150.0 1.5 amplitudes.18
  151.6 2.3 %amplitudes.19 = (bf16[64,256,128]{2,1,0:T(8,128)(2,1)S(1)}, f32[64,128]{1,0:T(8,128)S(1)}) custom-call(s32[8,128]{1,0:T(8,128)S(1)} %get-tuple-element.61.refs_0_, f32[64,128]{1,0:T(8,128)S(1)} %get-tuple-element.62.refs_1_, f32[16,256,128]{2,1,0:T(8,128)S(1)} %broadcast_in_dim.4.refs_2_, ...), custom_call_target="tpu_custom_call", output_to_operand_aliasing={{0}: (9, {}), {1}: (10, {})} | custom-call | flops 1 | bytes 1 | tf_op jit(solution)/shard_map/amplitudes/pallas_call | solution.py:365
  153.9 1.5 densities.3
  156.7 2.2 %copy-done.3 = bf16[64,256,128]{2,1,0:T(8,128)(2,1)S(1)} copy-done((bf16[64,256,128]{2,1,0:T(8,128)(2,1)S(1)}, bf16[64,256,128]{2,1,0:T(8,128)(2,1)}, u32[]{:S(2)}) %copy-start.3) | copy-done | bytes 4194328
  158.9 1.5 densities.2
  160.9 3.3 %add.12 = f32[16,128,256]{2,1,0:T(8,128)} add(f32[16,128,256]{2,1,0:T(8,128)S(1)} %densities.2, f32[16,128,256]{2,1,0:T(8,128)} %collective-permute-done.28) | non-fusion elementwise | flops 524288 | bytes 6291456 | tf_op jit(solution)/shard_map/add | solution.py:490
  (89 shorter events, 17.1 us)
Async XLA Ops:
  0.6 25.1 %collective-permute-start.7 = (bf16[16,256,256]{2,1,0:T(8,128)(2,1)}, bf16[16,256,256]{2,1,0:T(8,128)(2,1)S(1)}, u32[]{:S(2)}, u32[]{:S(2)}) collective-permute-start(bf16[16,256,256]{2,1,0:T(8,128)(2,1)} %refs_0_.3), channel_id=1, source_target_pairs={{0,1},{1,0},{2,3},{3,2},{4,5},{5,4},{6,7},{7,6},{8,9},{9,8},{10,11... | collective-permute-start | bytes 6291464 | tf_op jit(solution)/shard_map/ppermute | solution.py:416
  1.1 0.7 copy-start.17
  4.7 7.2 %collective-permute-start = (f32[24,384]{1,0:T(8,128)S(1)}, f32[24,384]{1,0:T(8,128)S(1)}, u32[]{:S(2)}, u32[]{:S(2)}) collective-permute-start(f32[24,384]{1,0:T(8,128)S(1)} %get-tuple-element.53.refs_1_), channel_id=1, source_target_pairs={{0,2},{2,0},{4,6},{6,4},{8,10},{10,8},{12,14},{14,12},{1,3},{3,1},... | collective-permute-start | bytes 110600 | tf_op jit(solution)/shard_map/ppermute | solution.py:413
  7.3 6.0 %collective-permute-start.1 = (f32[24,384]{1,0:T(8,128)S(1)}, f32[24,384]{1,0:T(8,128)S(1)}, u32[]{:S(2)}, u32[]{:S(2)}) collective-permute-start(f32[24,384]{1,0:T(8,128)S(1)} %get-tuple-element.53.refs_1_), channel_id=1, source_target_pairs={{0,4},{2,6},{4,0},{6,2},{8,12},{10,14},{12,8},{14,10},{1,5},{3,7},... | collective-permute-start | bytes 110600 | tf_op jit(solution)/shard_map/ppermute | solution.py:413
  8.8 7.9 %collective-permute-start.2 = (f32[24,384]{1,0:T(8,128)S(1)}, f32[24,384]{1,0:T(8,128)S(1)}, u32[]{:S(2)}, u32[]{:S(2)}) collective-permute-start(f32[24,384]{1,0:T(8,128)S(1)} %get-tuple-element.53.refs_1_), channel_id=1, source_target_pairs={{0,6},{2,4},{4,2},{6,0},{8,14},{10,12},{12,10},{14,8},{1,7},{3,5},... | collective-permute-start | bytes 110600 | tf_op jit(solution)/shard_map/ppermute | solution.py:413
  8.9 10.5 %collective-permute-start.3 = (f32[24,384]{1,0:T(8,128)S(1)}, f32[24,384]{1,0:T(8,128)S(1)}, u32[]{:S(2)}, u32[]{:S(2)}) collective-permute-start(f32[24,384]{1,0:T(8,128)S(1)} %get-tuple-element.53.refs_1_), channel_id=1, source_target_pairs={{0,8},{2,10},{4,12},{6,14},{8,0},{10,2},{12,4},{14,6},{1,9},{3,11}... | collective-permute-start | bytes 110600 | tf_op jit(solution)/shard_map/ppermute | solution.py:413
  11.8 7.5 %collective-permute-start.4 = (f32[24,384]{1,0:T(8,128)S(1)}, f32[24,384]{1,0:T(8,128)S(1)}, u32[]{:S(2)}, u32[]{:S(2)}) collective-permute-start(f32[24,384]{1,0:T(8,128)S(1)} %get-tuple-element.53.refs_1_), channel_id=1, source_target_pairs={{0,10},{2,8},{4,14},{6,12},{8,2},{10,0},{12,6},{14,4},{1,11},{3,9}... | collective-permute-start | bytes 110600 | tf_op jit(solution)/shard_map/ppermute | solution.py:413
  13.3 6.1 %collective-permute-start.5 = (f32[24,384]{1,0:T(8,128)S(1)}, f32[24,384]{1,0:T(8,128)S(1)}, u32[]{:S(2)}, u32[]{:S(2)}) collective-permute-start(f32[24,384]{1,0:T(8,128)S(1)} %get-tuple-element.53.refs_1_), channel_id=1, source_target_pairs={{0,12},{2,14},{4,8},{6,10},{8,4},{10,6},{12,0},{14,2},{1,13},{3,15... | collective-permute-start | bytes 110600 | tf_op jit(solution)/shard_map/ppermute | solution.py:413
  16.7 6.7 %collective-permute-start.6 = (f32[24,384]{1,0:T(8,128)S(1)}, f32[24,384]{1,0:T(8,128)S(1)}, u32[]{:S(2)}, u32[]{:S(2)}) collective-permute-start(f32[24,384]{1,0:T(8,128)S(1)} %get-tuple-element.53.refs_1_), channel_id=1, source_target_pairs={{0,14},{2,12},{4,10},{6,8},{8,6},{10,4},{12,2},{14,0},{1,15},{3,13... | collective-permute-start | bytes 110600 | tf_op jit(solution)/shard_map/ppermute | solution.py:413
  23.4 8.6 %collective-permute-start.9 = (bf16[16,256,128]{2,1,0:T(8,128)(2,1)}, bf16[16,256,128]{2,1,0:T(8,128)(2,1)S(1)}, u32[]{:S(2)}, u32[]{:S(2)}) collective-permute-start(bf16[16,256,128]{2,1,0:T(8,128)(2,1)} %constant_dynamic-slice_fusion.1.refs_2_.refs_5_), channel_id=1, source_target_pairs={{4,8},{6,10},{8,4},{10,6},{5,9},{7,11},{9,5},{11,7},{20,24},{22,26... | collective-permute-start | bytes 3145736 | tf_op jit(solution)/shard_map/ppermute | solution.py:413
  24.1 26.5 %collective-permute-start.8 = (bf16[16,256,128]{2,1,0:T(8,128)(2,1)}, bf16[16,256,128]{2,1,0:T(8,128)(2,1)}, u32[]{:S(2)}, u32[]{:S(2)}) collective-permute-start(bf16[16,256,128]{2,1,0:T(8,128)(2,1)} %constant_dynamic-slice_fusion.1.refs_2_.refs_5_), channel_id=1, source_target_pairs={{0,4},{2,6},{4,0},{6,2},{8,12},{10,14},{12,8},{14,10},{1,5},{3,7},... | collective-permute-start | bytes 3145736 | tf_op jit(solution)/shard_map/ppermute | solution.py:413
  26.0 4.6 %copy-start.12 = (bf16[16,256,256]{2,1,0:T(8,128)(2,1)S(1)}, bf16[16,256,256]{2,1,0:T(8,128)(2,1)}, u32[]{:S(2)}) copy-start(bf16[16,256,256]{2,1,0:T(8,128)(2,1)} %refs_0_.3) | copy-start | bytes 6291460
  27.4 4.5 %copy-start.18 = (f32[16,256]{1,0:T(8,128)S(1)}, f32[16,256]{1,0:T(8,128)}, u32[]{:S(2)}) copy-start(f32[16,256]{1,0:T(8,128)} %refs_0_.2) | copy-start | bytes 49156
  27.5 34.2 %collective-permute-start.12 = (bf16[2,8,256,128]{3,2,1,0:T(8,128)(2,1)S(1)}, bf16[2,8,256,128]{3,2,1,0:T(8,128)(2,1)S(1)}, u32[]{:S(2)}, u32[]{:S(2)}) collective-permute-start(bf16[2,8,256,128]{3,2,1,0:T(8,128)(2,1)S(1)} %pack.7.refs_7_), channel_id=1, source_target_pairs={{0,2},{2,0},{4,6},{6,4},{8,10},{10,8},{12,14},{14,12},{1,3},{3,1},... | collective-permute-start | bytes 3145736 | tf_op jit(solution)/shard_map/ppermute | solution.py:413
  28.0 41.6 %collective-permute-start.11 = (bf16[16,256,128]{2,1,0:T(8,128)(2,1)S(1)}, bf16[16,256,128]{2,1,0:T(8,128)(2,1)S(1)}, u32[]{:S(2)}, u32[]{:S(2)}) collective-permute-start(bf16[16,256,128]{2,1,0:T(8,128)(2,1)S(1)} %constant_dynamic-slice_fusion.refs_3_.refs_6_), channel_id=1, source_target_pairs={{0,4},{2,6},{4,0},{6,2},{8,12},{10,14},{12,8},{14,10},{1,5},{3,7},... | collective-permute-start | bytes 3145736 | tf_op jit(solution)/shard_map/ppermute | solution.py:413
  29.8 39.7 %collective-permute-start.16 = (bf16[16,256,128]{2,1,0:T(8,128)(2,1)S(1)}, bf16[16,256,128]{2,1,0:T(8,128)(2,1)S(1)}, u32[]{:S(2)}, u32[]{:S(2)}) collective-permute-start(bf16[16,256,128]{2,1,0:T(8,128)(2,1)S(1)} %constant_dynamic-slice_fusion.refs_3_.refs_6_), channel_id=1, source_target_pairs={{4,8},{6,10},{8,4},{10,6},{5,9},{7,11},{9,5},{11,7},{20,24},{22,26... | collective-permute-start | bytes 3145736 | tf_op jit(solution)/shard_map/ppermute | solution.py:413
  31.9 80.3 %copy-start.4 = (bf16[16,256,256]{2,1,0:T(8,128)(2,1)}, bf16[16,256,256]{2,1,0:T(8,128)(2,1)S(1)}, u32[]{:S(2)}) copy-start(bf16[16,256,256]{2,1,0:T(8,128)(2,1)S(1)} %get-tuple-element.63.refs_3_) | copy-start | bytes 6291460
  31.9 80.3 %copy-start.6 = (bf16[16,256,256]{2,1,0:T(8,128)(2,1)}, bf16[16,256,256]{2,1,0:T(8,128)(2,1)S(1)}, u32[]{:S(2)}) copy-start(bf16[16,256,256]{2,1,0:T(8,128)(2,1)S(1)} %get-tuple-element.64.refs_4_) | copy-start | bytes 6291460
  51.9 9.7 %collective-permute-start.13 = (bf16[1,8,256,128]{3,2,1,0:T(8,128)(2,1)S(1)}, bf16[1,8,256,128]{3,2,1,0:T(8,128)(2,1)S(1)}, u32[]{:S(2)}, u32[]{:S(2)}) collective-permute-start(bf16[1,8,256,128]{3,2,1,0:T(8,128)(2,1)S(1)} %pack.8.refs_6_), channel_id=1, source_target_pairs={{0,2},{2,0},{4,6},{6,4},{8,10},{10,8},{12,14},{14,12},{1,3},{3,1},... | collective-permute-start | bytes 1572872 | tf_op jit(solution)/shard_map/ppermute | solution.py:413
  52.5 20.6 %collective-permute-start.14 = (bf16[16,256,128]{2,1,0:T(8,128)(2,1)}, bf16[16,256,128]{2,1,0:T(8,128)(2,1)S(1)}, u32[]{:S(2)}, u32[]{:S(2)}) collective-permute-start(bf16[16,256,128]{2,1,0:T(8,128)(2,1)} %collective-permute-done.8.refs_2_.refs_0_.refs_5_), channel_id=1, source_target_pairs={{0,1},{1,0},{2,3},{3,2},{4,5},{5,4},{6,7},{7,6},{8,9},{9,8},{10,11... | collective-permute-start | bytes 3145736 | tf_op jit(solution)/shard_map/ppermute | solution.py:416
  69.6 4.9 %collective-permute-start.15 = (bf16[16,256,128]{2,1,0:T(8,128)(2,1)S(1)}, bf16[16,256,128]{2,1,0:T(8,128)(2,1)S(1)}, u32[]{:S(2)}, u32[]{:S(2)}) collective-permute-start(bf16[16,256,128]{2,1,0:T(8,128)(2,1)S(1)} %collective-permute-done.11.refs_1_.refs_2_.refs_6_), channel_id=1, source_target_pairs={{0,1},{1,0},{2,3},{3,2},{4,5},{5,4},{6,7},{7,6},{8,9},{9,8},{10,11... | collective-permute-start | bytes 3145736 | tf_op jit(solution)/shard_map/ppermute | solution.py:416
  70.3 28.7 %collective-permute-start.17 = (bf16[2,8,256,128]{3,2,1,0:T(8,128)(2,1)S(1)}, bf16[2,8,256,128]{3,2,1,0:T(8,128)(2,1)S(1)}, u32[]{:S(2)}, u32[]{:S(2)}) collective-permute-start(bf16[2,8,256,128]{3,2,1,0:T(8,128)(2,1)S(1)} %get-tuple-element.83.refs_3_), channel_id=1, source_target_pairs={{4,2},{6,0},{8,14},{10,12},{5,3},{7,1},{9,15},{11,13},{20,18},{22,... | collective-permute-start | bytes 3145736 | tf_op jit(solution)/shard_map/ppermute | solution.py:413
  71.6 29.9 %collective-permute-start.10 = (bf16[16,256,128]{2,1,0:T(8,128)(2,1)}, bf16[16,256,128]{2,1,0:T(8,128)(2,1)S(1)}, u32[]{:S(2)}, u32[]{:S(2)}) collective-permute-start(bf16[16,256,128]{2,1,0:T(8,128)(2,1)} %collective-permute-done.8.refs_2_.refs_0_.refs_5_), channel_id=1, source_target_pairs={{4,8},{6,10},{8,4},{10,6},{5,9},{7,11},{9,5},{11,7},{20,24},{22,26... | collective-permute-start | bytes 3145736 | tf_op jit(solution)/shard_map/ppermute | solution.py:413
  72.3 41.2 %collective-permute-start.19 = (bf16[16,256,128]{2,1,0:T(8,128)(2,1)S(1)}, bf16[16,256,128]{2,1,0:T(8,128)(2,1)S(1)}, u32[]{:S(2)}, u32[]{:S(2)}) collective-permute-start(bf16[16,256,128]{2,1,0:T(8,128)(2,1)S(1)} %collective-permute-done.11.refs_1_.refs_2_.refs_6_), channel_id=1, source_target_pairs={{4,8},{6,10},{8,4},{10,6},{5,9},{7,11},{9,5},{11,7},{20,24},{22,26... | collective-permute-start | bytes 3145736 | tf_op jit(solution)/shard_map/ppermute | solution.py:413
  73.1 48.0 %collective-permute-start.26 = (bf16[2,8,256,128]{3,2,1,0:T(8,128)(2,1)S(1)}, bf16[2,8,256,128]{3,2,1,0:T(8,128)(2,1)S(1)}, u32[]{:S(2)}, u32[]{:S(2)}) collective-permute-start(bf16[2,8,256,128]{3,2,1,0:T(8,128)(2,1)S(1)} %get-tuple-element.92), channel_id=1, source_target_pairs={{4,6},{6,4},{8,10},{10,8},{5,7},{7,5},{9,11},{11,9},{20,22},{22,20... | collective-permute-start | bytes 3145736 | tf_op jit(solution)/shard_map/ppermute | solution.py:413
  78.7 30.2 %collective-permute-start.21 = (bf16[8,256,128]{2,1,0:T(8,128)(2,1)S(1)}, bf16[8,256,128]{2,1,0:T(8,128)(2,1)S(1)}, u32[]{:S(2)}, u32[]{:S(2)}) collective-permute-start(bf16[8,256,128]{2,1,0:T(8,128)(2,1)S(1)} %amplitudes.12.refs_7_), channel_id=1, source_target_pairs={{4,0},{6,2},{8,12},{10,14},{5,1},{7,3},{9,13},{11,15},{20,16},{22,... | collective-permute-start | bytes 1572872 | tf_op jit(solution)/shard_map/ppermute | solution.py:413
  99.0 2.5 %copy-start.13 = (bf16[2,8,256,128]{3,2,1,0:T(8,128)(2,1)}, bf16[2,8,256,128]{3,2,1,0:T(8,128)(2,1)S(1)}, u32[]{:S(2)}) copy-start(bf16[2,8,256,128]{3,2,1,0:T(8,128)(2,1)S(1)} %collective-permute-done.17.refs_8_.refs_6_) | copy-start | bytes 3145732
  99.0 13.2 %collective-permute-start.20 = (bf16[1,8,256,128]{3,2,1,0:T(8,128)(2,1)S(1)}, bf16[1,8,256,128]{3,2,1,0:T(8,128)(2,1)S(1)}, u32[]{:S(2)}, u32[]{:S(2)}) collective-permute-start(bf16[1,8,256,128]{3,2,1,0:T(8,128)(2,1)S(1)} %pack.10.refs_9_), channel_id=1, source_target_pairs={{0,2},{2,0},{4,6},{6,4},{8,10},{10,8},{12,14},{14,12},{1,3},{3,1},... | collective-permute-start | bytes 1572872 | tf_op jit(solution)/shard_map/ppermute | solution.py:413
  101.5 15.2 %copy-start.8 = (bf16[16,256,128]{2,1,0:T(8,128)(2,1)}, bf16[16,256,128]{2,1,0:T(8,128)(2,1)S(1)}, u32[]{:S(2)}) copy-start(bf16[16,256,128]{2,1,0:T(8,128)(2,1)S(1)} %collective-permute-done.10.refs_2_.refs_3_.refs_7_.refs_5_) | copy-start | bytes 3145732
  103.2 20.4 %collective-permute-start.18 = (bf16[1,8,256,128]{3,2,1,0:T(8,128)(2,1)}, bf16[1,8,256,128]{3,2,1,0:T(8,128)(2,1)}, u32[]{:S(2)}, u32[]{:S(2)}) collective-permute-start(bf16[1,8,256,128]{3,2,1,0:T(8,128)(2,1)} %get-tuple-element.86), channel_id=1, source_target_pairs={{4,6},{6,4},{8,10},{10,8},{5,7},{7,5},{9,11},{11,9},{20,22},{22,20... | collective-permute-start | bytes 1572872 | tf_op jit(solution)/shard_map/ppermute | solution.py:413
  108.9 16.7 %collective-permute-start.23 = (bf16[1,8,256,128]{3,2,1,0:T(8,128)(2,1)}, bf16[1,8,256,128]{3,2,1,0:T(8,128)(2,1)}, u32[]{:S(2)}, u32[]{:S(2)}) collective-permute-start(bf16[1,8,256,128]{3,2,1,0:T(8,128)(2,1)} %get-tuple-element.87.refs_8_), channel_id=1, source_target_pairs={{4,2},{6,0},{8,14},{10,12},{5,3},{7,1},{9,15},{11,13},{20,18},{22,... | collective-permute-start | bytes 1572872 | tf_op jit(solution)/shard_map/ppermute | solution.py:413
  113.5 4.7 %copy-start = (bf16[64,256,128]{2,1,0:T(8,128)(2,1)}, bf16[64,256,128]{2,1,0:T(8,128)(2,1)S(1)}, u32[]{:S(2)}) copy-start(bf16[64,256,128]{2,1,0:T(8,128)(2,1)S(1)} %get-tuple-element.93.refs_10_) | copy-start | bytes 12582916
  113.5 6.1 %copy-start.10 = (bf16[16,256,128]{2,1,0:T(8,128)(2,1)}, bf16[16,256,128]{2,1,0:T(8,128)(2,1)S(1)}, u32[]{:S(2)}) copy-start(bf16[16,256,128]{2,1,0:T(8,128)(2,1)S(1)} %collective-permute-done.19.refs_2_.refs_8_.refs_6_) | copy-start | bytes 3145732
  115.5 25.5 %collective-permute-start.24 = (bf16[1,8,256,128]{3,2,1,0:T(8,128)(2,1)}, bf16[1,8,256,128]{3,2,1,0:T(8,128)(2,1)}, u32[]{:S(2)}, u32[]{:S(2)}) collective-permute-start(bf16[1,8,256,128]{3,2,1,0:T(8,128)(2,1)} %pack.12.refs_9_), channel_id=1, source_target_pairs={{4,2},{6,0},{8,14},{10,12},{5,3},{7,1},{9,15},{11,13},{20,18},{22,... | collective-permute-start | bytes 1572872 | tf_op jit(solution)/shard_map/ppermute | solution.py:413
  118.2 7.4 %copy-start.14 = (bf16[2,8,256,128]{3,2,1,0:T(8,128)(2,1)S(1)}, bf16[2,8,256,128]{3,2,1,0:T(8,128)(2,1)}, u32[]{:S(2)}) copy-start(bf16[2,8,256,128]{3,2,1,0:T(8,128)(2,1)} %copy-done.13) | copy-start | bytes 3145732
  118.2 31.8 %collective-permute-start.25 = (bf16[8,256,128]{2,1,0:T(8,128)(2,1)}, bf16[8,256,128]{2,1,0:T(8,128)(2,1)}, u32[]{:S(2)}, u32[]{:S(2)}) collective-permute-start(bf16[8,256,128]{2,1,0:T(8,128)(2,1)} %amplitudes.16.refs_3_), channel_id=1, source_target_pairs={{4,0},{6,2},{8,12},{10,14},{5,1},{7,3},{9,13},{11,15},{20,16},{22,... | collective-permute-start | bytes 1572872 | tf_op jit(solution)/shard_map/ppermute | solution.py:413
  121.1 1.0 copy-start.15
  122.1 29.5 %collective-permute-start.22 = (bf16[1,8,256,128]{3,2,1,0:T(8,128)(2,1)}, bf16[1,8,256,128]{3,2,1,0:T(8,128)(2,1)}, u32[]{:S(2)}, u32[]{:S(2)}) collective-permute-start(bf16[1,8,256,128]{3,2,1,0:T(8,128)(2,1)} %pack.13.refs_7_), channel_id=1, source_target_pairs={{4,6},{6,4},{8,10},{10,8},{5,7},{7,5},{9,11},{11,9},{20,22},{22,20... | collective-permute-start | bytes 1572872 | tf_op jit(solution)/shard_map/ppermute | solution.py:413
  125.6 2.2 %copy-start.1 = (bf16[64,256,128]{2,1,0:T(8,128)(2,1)S(1)}, bf16[64,256,128]{2,1,0:T(8,128)(2,1)}, u32[]{:S(2)}) copy-start(bf16[64,256,128]{2,1,0:T(8,128)(2,1)} %copy-done) | copy-start | bytes 12582916
  127.8 1.6 copy-start.5
  129.4 1.6 copy-start.7
  130.9 1.2 copy-start.16
  132.2 17.8 %copy-start.9 = (bf16[16,256,128]{2,1,0:T(8,128)(2,1)S(1)}, bf16[16,256,128]{2,1,0:T(8,128)(2,1)}, u32[]{:S(2)}) copy-start(bf16[16,256,128]{2,1,0:T(8,128)(2,1)} %copy-done.8) | copy-start | bytes 3145732
  132.2 17.8 %copy-start.11 = (bf16[16,256,128]{2,1,0:T(8,128)(2,1)S(1)}, bf16[16,256,128]{2,1,0:T(8,128)(2,1)}, u32[]{:S(2)}) copy-start(bf16[16,256,128]{2,1,0:T(8,128)(2,1)} %copy-done.10) | copy-start | bytes 3145732
  153.9 2.0 %copy-start.2 = (bf16[64,256,128]{2,1,0:T(8,128)(2,1)}, bf16[64,256,128]{2,1,0:T(8,128)(2,1)S(1)}, u32[]{:S(2)}) copy-start(bf16[64,256,128]{2,1,0:T(8,128)(2,1)S(1)} %get-tuple-element.99.t) | copy-start | bytes 12582916
  155.9 5.0 %collective-permute-start.28 = (f32[16,128,256]{2,1,0:T(8,128)S(1)}, f32[16,128,256]{2,1,0:T(8,128)}, u32[]{:S(2)}, u32[]{:S(2)}) collective-permute-start(f32[16,128,256]{2,1,0:T(8,128)S(1)} %densities.3), channel_id=1, source_target_pairs={{0,1},{1,0},{2,3},{3,2},{4,5},{5,4},{6,7},{7,6},{8,9},{9,8},{10,11... | collective-permute-start | bytes 6291464 | tf_op jit(solution)/shard_map/ppermute | solution.py:416
  156.1 4.2 %collective-permute-start.27 = (f32[64]{0:T(128)S(1)}, f32[64]{0:T(128)S(1)}, u32[]{:S(2)}, u32[]{:S(2)}) collective-permute-start(f32[64]{0:T(128)S(1)} %multiply_reduce_fusion), channel_id=1, source_target_pairs={{0,1},{1,0},{2,3},{3,2},{4,5},{5,4},{6,7},{7,6},{8,9},{9,8},{10,11... | collective-permute-start | bytes 776 | tf_op jit(solution)/shard_map/ppermute | solution.py:416
  156.7 2.2 %copy-start.3 = (bf16[64,256,128]{2,1,0:T(8,128)(2,1)S(1)}, bf16[64,256,128]{2,1,0:T(8,128)(2,1)}, u32[]{:S(2)}) copy-start(bf16[64,256,128]{2,1,0:T(8,128)(2,1)} %copy-done.2) | copy-start | bytes 12582916
  (4 other events, 2.6 us)

commit v15 on v13

--- a/solution.py
+++ b/solution.py
@@ -451,7 +451,7 @@
     (packed,) = pack(lists_of, [(0, 0, own, False)], cap)
     beside = pp(packed, flip(1))
     left = turn([blocks, other])
-    held = own_pairs(0, "slots", [own], after=(packed,))
+    held = own_pairs(0, "slots", [own], after=(packed, mid[0]))
     first, held = lax.optimization_barrier((near[0], held))
     far = [pp(first, cross)]
     across = [swap_core(first)]

time: 162 us -> 163 us (level)
  waiting for transfers between devices: 92.5 us -> 95.9 us
  starting transfers between devices: 30.3 us -> 28.6 us
    ppermute x24, waiting for transfers between devices: 89.2 us -> 92.6 us  [pp(): return lax.ppermute(x, 'orb', perm)]
where the time goes in v15:
time: 163 us
  waiting for transfers between devices  95.9 us (59%)
  starting transfers between devices  28.6 us (18%)
  Pallas kernels  26 us (16%)
  local copies, waits for them, and re-layouts  7.14 us (4%)
  other arithmetic  3.99 us (2%)
    ppermute x24, waiting for transfers between devices, pp(): return lax.ppermute(x, 'orb', perm)  92.6 us
    ppermute x24, starting transfers between devices, pp(): return lax.ppermute(x, 'orb', perm)  27.5 us
    pallas_call x10, Pallas kernels, amplitudes(): pl.pallas_call(lambda *refs: amplitudes_kernel(mode, call, per_orb, [len(...  11.2 us
    pallas_call x7, Pallas kernels, pack(): pl.pallas_call(lambda *refs: pack_kernel(kinds, len(tbls), *refs), out_sh...  4.83 us
    pallas_call x2, Pallas kernels, turn(): pl.pallas_call(turn_kernel, out_shape=[jax.ShapeDtypeStruct((count, cols,...  4.47 us
    pallas_call x1, Pallas kernels, densities(): pl.pallas_call(density_kernel, out_shape=(shape, shape), in_specs=[SMEM,...  4.07 us
    unnamed x14, local copies, waits for them, and re-layouts  3.35 us
    ppermute x5, waiting for transfers between devices, swap_core(): return lax.ppermute(x, 'aux', [(0, 1), (1, 0)])  3.3 us
  transfers between devices with their start and end apart: 29, of which 12 were waited for; matrix products, arithmetic and copies ran while one was open for 3% of the time, Pallas kernels for 13%

profile of v15, /device:TPU:0, one launch (start us, length us, event | category | flops | bytes accessed | tf_op | source)
XLA Modules:
  0.0 162.7 jit_solution(4126798543595309496)
XLA Ops:
  1.2 0.7 copy-done.1
  4.7 2.6 %collective-permute-start = (f32[24,384]{1,0:T(8,128)S(1)}, f32[24,384]{1,0:T(8,128)S(1)}, u32[]{:S(2)}, u32[]{:S(2)}) collective-permute-start(f32[24,384]{1,0:T(8,128)S(1)} %get-tuple-element.55.refs_1_), channel_id=1, source_target_pairs={{0,2},{2,0},{4,6},{6,4},{8,10},{10,8},{12,14},{14,12},{1,3},{3,1},... | collective-permute-start | bytes 110600 | tf_op jit(solution)/shard_map/ppermute | solution.py:416
  7.3 1.6 collective-permute-start.1
  8.9 3.0 %collective-permute-start.3 = (f32[24,384]{1,0:T(8,128)S(1)}, f32[24,384]{1,0:T(8,128)S(1)}, u32[]{:S(2)}, u32[]{:S(2)}) collective-permute-start(f32[24,384]{1,0:T(8,128)S(1)} %get-tuple-element.55.refs_1_), channel_id=1, source_target_pairs={{0,8},{2,10},{4,12},{6,14},{8,0},{10,2},{12,4},{14,6},{1,9},{3,11}... | collective-permute-start | bytes 110600 | tf_op jit(solution)/shard_map/ppermute | solution.py:416
  11.8 1.4 collective-permute-start.4
  13.3 3.5 %collective-permute-start.5 = (f32[24,384]{1,0:T(8,128)S(1)}, f32[24,384]{1,0:T(8,128)S(1)}, u32[]{:S(2)}, u32[]{:S(2)}) collective-permute-start(f32[24,384]{1,0:T(8,128)S(1)} %get-tuple-element.55.refs_1_), channel_id=1, source_target_pairs={{0,12},{2,14},{4,8},{6,10},{8,4},{10,6},{12,0},{14,2},{1,13},{3,15... | collective-permute-start | bytes 110600 | tf_op jit(solution)/shard_map/ppermute | solution.py:416
  17.0 1.3 constant_dynamic-slice_fusion.1.refs_2_.refs_5_
  18.4 0.8 collective-permute-done.5.refs_7_
  19.2 4.2 %collective-permute-done.6.refs_8_ = f32[24,384]{1,0:T(8,128)S(1)} collective-permute-done((f32[24,384]{1,0:T(8,128)S(1)}, f32[24,384]{1,0:T(8,128)S(1)}, u32[]{:S(2)}, u32[]{:S(2)}) %collective-permute-start.6) | collective-permute-done | bytes 36896 | tf_op jit(solution)/shard_map/ppermute | solution.py:416
  23.4 0.7 collective-permute-start.9
  24.5 1.3 tables.1
  25.8 1.3 constant_dynamic-slice_fusion.refs_3_.refs_6_
  27.1 0.7 pack.7.refs_7_
  28.4 1.9 %collective-permute-start.11 = (bf16[16,256,128]{2,1,0:T(8,128)(2,1)S(1)}, bf16[16,256,128]{2,1,0:T(8,128)(2,1)S(1)}, u32[]{:S(2)}, u32[]{:S(2)}) collective-permute-start(bf16[16,256,128]{2,1,0:T(8,128)(2,1)S(1)} %constant_dynamic-slice_fusion.refs_3_.refs_6_), channel_id=1, source_target_pairs={{0,4},{2,6},{4,0},{6,2},{8,12},{10,14},{12,8},{14,10},{1,5},{3,7},... | collective-permute-start | bytes 3145736 | tf_op jit(solution)/shard_map/ppermute | solution.py:416
  30.2 0.7 collective-permute-start.16
  31.0 3.1 %turn.2 = (bf16[16,256,256]{2,1,0:T(8,128)(2,1)S(1)}, bf16[16,256,256]{2,1,0:T(8,128)(2,1)S(1)}) custom-call(bf16[16,256,256]{2,1,0:T(8,128)(2,1)S(1)} %copy-done, bf16[16,256,256]{2,1,0:T(8,128)(2,1)} %collective-permute-done.7.refs_1_), custom_call_target="tpu_custom_call" | custom-call | flops 1 | bytes 1 | tf_op jit(solution)/shard_map/turn/pallas_call | solution.py:257
  34.7 1.3 amplitudes.10
  36.0 14.2 %collective-permute-done.8.refs_2_.refs_0_.refs_5_ = bf16[16,256,128]{2,1,0:T(8,128)(2,1)S(1)} collective-permute-done((bf16[16,256,128]{2,1,0:T(8,128)(2,1)S(1)}, bf16[16,256,128]{2,1,0:T(8,128)(2,1)S(1)}, u32[]{:S(2)}, u32[]{:S(2)}) %collective-permute-start.8) | collective-permute-done | bytes 1048608 | tf_op jit(solution)/shard_map/ppermute | solution.py:416
  50.3 0.7 pack.8.refs_6_
  51.6 10.4 %collective-permute-done.13.refs_7_.refs_5_ = bf16[1,8,256,128]{3,2,1,0:T(8,128)(2,1)S(1)} collective-permute-done((bf16[1,8,256,128]{3,2,1,0:T(8,128)(2,1)S(1)}, bf16[1,8,256,128]{3,2,1,0:T(8,128)(2,1)S(1)}, u32[]{:S(2)}, u32[]{:S(2)}) %collective-permute-start.13) | collective-permute-done | bytes 524320 | tf_op jit(solution)/shard_map/ppermute | solution.py:416
  62.0 1.3 amplitudes.11
  63.3 6.1 %collective-permute-done.11.refs_1_.refs_2_.refs_6_ = bf16[16,256,128]{2,1,0:T(8,128)(2,1)S(1)} collective-permute-done((bf16[16,256,128]{2,1,0:T(8,128)(2,1)S(1)}, bf16[16,256,128]{2,1,0:T(8,128)(2,1)S(1)}, u32[]{:S(2)}, u32[]{:S(2)}) %collective-permute-start.11) | collective-permute-done | bytes 1048608 | tf_op jit(solution)/shard_map/ppermute | solution.py:416
  70.1 1.3 collective-permute-start.17
  71.4 0.7 collective-permute-start.10
  72.1 0.7 collective-permute-start.19
  72.8 0.7 collective-permute-start.26
  73.6 0.7 pack.10.refs_9_
  74.3 1.3 turn.3
  76.9 1.3 collective-permute-start.21
  78.2 20.6 %collective-permute-done.17.refs_8_.refs_6_ = bf16[2,8,256,128]{3,2,1,0:T(8,128)(2,1)S(1)} collective-permute-done((bf16[2,8,256,128]{3,2,1,0:T(8,128)(2,1)S(1)}, bf16[2,8,256,128]{3,2,1,0:T(8,128)(2,1)S(1)}, u32[]{:S(2)}, u32[]{:S(2)}) %collective-permute-start.17) | collective-permute-done | bytes 1048608 | tf_op jit(solution)/shard_map/ppermute | solution.py:416
  99.3 1.3 amplitudes.13
  101.3 0.7 collective-permute-start.18
  102.0 6.7 %collective-permute-done.21.refs_7_ = bf16[8,256,128]{2,1,0:T(8,128)(2,1)S(1)} collective-permute-done((bf16[8,256,128]{2,1,0:T(8,128)(2,1)S(1)}, bf16[8,256,128]{2,1,0:T(8,128)(2,1)S(1)}, u32[]{:S(2)}, u32[]{:S(2)}) %collective-permute-start.21) | collective-permute-done | bytes 524320 | tf_op jit(solution)/shard_map/ppermute | solution.py:416
  108.7 1.3 collective-permute-start.23
  110.0 0.9 amplitudes.14
  110.9 1.1 collective-permute-done.20.refs_6_
  112.0 1.3 amplitudes.15
  114.0 1.3 collective-permute-start.24
  115.9 1.3 collective-permute-start.25
  118.6 6.4 %collective-permute-done.23.refs_9_.refs_7_ = bf16[1,8,256,128]{3,2,1,0:T(8,128)(2,1)S(1)} collective-permute-done((bf16[1,8,256,128]{3,2,1,0:T(8,128)(2,1)S(1)}, bf16[1,8,256,128]{3,2,1,0:T(8,128)(2,1)S(1)}, u32[]{:S(2)}, u32[]{:S(2)}) %collective-permute-start.23) | collective-permute-done | bytes 524320 | tf_op jit(solution)/shard_map/ppermute | solution.py:416
  125.0 1.4 amplitudes.17
  126.4 13.0 %collective-permute-done.24.refs_8_ = bf16[1,8,256,128]{3,2,1,0:T(8,128)(2,1)S(1)} collective-permute-done((bf16[1,8,256,128]{3,2,1,0:T(8,128)(2,1)S(1)}, bf16[1,8,256,128]{3,2,1,0:T(8,128)(2,1)S(1)}, u32[]{:S(2)}, u32[]{:S(2)}) %collective-permute-start.24) | collective-permute-done | bytes 524320 | tf_op jit(solution)/shard_map/ppermute | solution.py:416
  139.4 9.0 %collective-permute-done.25.refs_7_ = bf16[8,256,128]{2,1,0:T(8,128)(2,1)S(1)} collective-permute-done((bf16[8,256,128]{2,1,0:T(8,128)(2,1)S(1)}, bf16[8,256,128]{2,1,0:T(8,128)(2,1)S(1)}, u32[]{:S(2)}, u32[]{:S(2)}) %collective-permute-start.25) | collective-permute-done | bytes 524320 | tf_op jit(solution)/shard_map/ppermute | solution.py:416
  148.4 1.1 amplitudes.18
  149.5 1.4 amplitudes.19
  150.9 4.1 %densities.1 = (f32[16,128,256]{2,1,0:T(8,128)S(1)}, f32[16,128,256]{2,1,0:T(8,128)}) custom-call(s32[1]{0:T(128)} %bitcast.5.start, bf16[64,256,128]{2,1,0:T(8,128)(2,1)S(1)} %get-tuple-element.101.t), custom_call_target="tpu_custom_call" | custom-call | flops 1 | bytes 1 | tf_op jit(solution)/shard_map/densities/pallas_call | solution.py:394
  155.7 3.3 %collective-permute-done.27 = f32[64]{0:T(128)S(1)} collective-permute-done((f32[64]{0:T(128)S(1)}, f32[64]{0:T(128)S(1)}, u32[]{:S(2)}, u32[]{:S(2)}) %collective-permute-start.27) | collective-permute-done | bytes 288 | tf_op jit(solution)/shard_map/ppermute | solution.py:419
  159.5 3.2 %add.12 = f32[16,128,256]{2,1,0:T(8,128)} add(f32[16,128,256]{2,1,0:T(8,128)S(1)} %get-tuple-element.102, f32[16,128,256]{2,1,0:T(8,128)} %collective-permute-done.28) | non-fusion elementwise | flops 524288 | bytes 6291456 | tf_op jit(solution)/shard_map/add | solution.py:493
  (56 shorter events, 12.7 us)
Async XLA Ops:
  0.6 25.1 %collective-permute-start.7 = (bf16[16,256,256]{2,1,0:T(8,128)(2,1)}, bf16[16,256,256]{2,1,0:T(8,128)(2,1)}, u32[]{:S(2)}, u32[]{:S(2)}) collective-permute-start(bf16[16,256,256]{2,1,0:T(8,128)(2,1)} %refs_0_.3), channel_id=1, source_target_pairs={{0,1},{1,0},{2,3},{3,2},{4,5},{5,4},{6,7},{7,6},{8,9},{9,8},{10,11... | collective-permute-start | bytes 6291464 | tf_op jit(solution)/shard_map/ppermute | solution.py:419
  1.1 0.7 copy-start.1
  1.9 0.7 copy-start.3
  2.5 0.7 copy-start.4
  3.2 0.7 copy-start.5
  3.8 0.7 copy-start.6
  4.7 7.2 %collective-permute-start = (f32[24,384]{1,0:T(8,128)S(1)}, f32[24,384]{1,0:T(8,128)S(1)}, u32[]{:S(2)}, u32[]{:S(2)}) collective-permute-start(f32[24,384]{1,0:T(8,128)S(1)} %get-tuple-element.55.refs_1_), channel_id=1, source_target_pairs={{0,2},{2,0},{4,6},{6,4},{8,10},{10,8},{12,14},{14,12},{1,3},{3,1},... | collective-permute-start | bytes 110600 | tf_op jit(solution)/shard_map/ppermute | solution.py:416
  7.3 6.0 %collective-permute-start.1 = (f32[24,384]{1,0:T(8,128)S(1)}, f32[24,384]{1,0:T(8,128)S(1)}, u32[]{:S(2)}, u32[]{:S(2)}) collective-permute-start(f32[24,384]{1,0:T(8,128)S(1)} %get-tuple-element.55.refs_1_), channel_id=1, source_target_pairs={{0,4},{2,6},{4,0},{6,2},{8,12},{10,14},{12,8},{14,10},{1,5},{3,7},... | collective-permute-start | bytes 110600 | tf_op jit(solution)/shard_map/ppermute | solution.py:416
  8.8 7.9 %collective-permute-start.2 = (f32[24,384]{1,0:T(8,128)S(1)}, f32[24,384]{1,0:T(8,128)S(1)}, u32[]{:S(2)}, u32[]{:S(2)}) collective-permute-start(f32[24,384]{1,0:T(8,128)S(1)} %get-tuple-element.55.refs_1_), channel_id=1, source_target_pairs={{0,6},{2,4},{4,2},{6,0},{8,14},{10,12},{12,10},{14,8},{1,7},{3,5},... | collective-permute-start | bytes 110600 | tf_op jit(solution)/shard_map/ppermute | solution.py:416
  8.9 9.5 %collective-permute-start.3 = (f32[24,384]{1,0:T(8,128)S(1)}, f32[24,384]{1,0:T(8,128)S(1)}, u32[]{:S(2)}, u32[]{:S(2)}) collective-permute-start(f32[24,384]{1,0:T(8,128)S(1)} %get-tuple-element.55.refs_1_), channel_id=1, source_target_pairs={{0,8},{2,10},{4,12},{6,14},{8,0},{10,2},{12,4},{14,6},{1,9},{3,11}... | collective-permute-start | bytes 110600 | tf_op jit(solution)/shard_map/ppermute | solution.py:416
  11.8 6.5 %collective-permute-start.4 = (f32[24,384]{1,0:T(8,128)S(1)}, f32[24,384]{1,0:T(8,128)S(1)}, u32[]{:S(2)}, u32[]{:S(2)}) collective-permute-start(f32[24,384]{1,0:T(8,128)S(1)} %get-tuple-element.55.refs_1_), channel_id=1, source_target_pairs={{0,10},{2,8},{4,14},{6,12},{8,2},{10,0},{12,6},{14,4},{1,11},{3,9}... | collective-permute-start | bytes 110600 | tf_op jit(solution)/shard_map/ppermute | solution.py:416
  13.3 5.9 %collective-permute-start.5 = (f32[24,384]{1,0:T(8,128)S(1)}, f32[24,384]{1,0:T(8,128)S(1)}, u32[]{:S(2)}, u32[]{:S(2)}) collective-permute-start(f32[24,384]{1,0:T(8,128)S(1)} %get-tuple-element.55.refs_1_), channel_id=1, source_target_pairs={{0,12},{2,14},{4,8},{6,10},{8,4},{10,6},{12,0},{14,2},{1,13},{3,15... | collective-permute-start | bytes 110600 | tf_op jit(solution)/shard_map/ppermute | solution.py:416
  16.7 6.7 %collective-permute-start.6 = (f32[24,384]{1,0:T(8,128)S(1)}, f32[24,384]{1,0:T(8,128)S(1)}, u32[]{:S(2)}, u32[]{:S(2)}) collective-permute-start(f32[24,384]{1,0:T(8,128)S(1)} %get-tuple-element.55.refs_1_), channel_id=1, source_target_pairs={{0,14},{2,12},{4,10},{6,8},{8,6},{10,4},{12,2},{14,0},{1,15},{3,13... | collective-permute-start | bytes 110600 | tf_op jit(solution)/shard_map/ppermute | solution.py:416
  23.4 10.7 %collective-permute-start.9 = (bf16[16,256,128]{2,1,0:T(8,128)(2,1)S(1)}, bf16[16,256,128]{2,1,0:T(8,128)(2,1)S(1)}, u32[]{:S(2)}, u32[]{:S(2)}) collective-permute-start(bf16[16,256,128]{2,1,0:T(8,128)(2,1)S(1)} %constant_dynamic-slice_fusion.1.refs_2_.refs_5_), channel_id=1, source_target_pairs={{4,8},{6,10},{8,4},{10,6},{5,9},{7,11},{9,5},{11,7},{20,24},{22,26... | collective-permute-start | bytes 3145736 | tf_op jit(solution)/shard_map/ppermute | solution.py:416
  24.1 26.2 %collective-permute-start.8 = (bf16[16,256,128]{2,1,0:T(8,128)(2,1)S(1)}, bf16[16,256,128]{2,1,0:T(8,128)(2,1)S(1)}, u32[]{:S(2)}, u32[]{:S(2)}) collective-permute-start(bf16[16,256,128]{2,1,0:T(8,128)(2,1)S(1)} %constant_dynamic-slice_fusion.1.refs_2_.refs_5_), channel_id=1, source_target_pairs={{0,4},{2,6},{4,0},{6,2},{8,12},{10,14},{12,8},{14,10},{1,5},{3,7},... | collective-permute-start | bytes 3145736 | tf_op jit(solution)/shard_map/ppermute | solution.py:416
  27.1 3.9 %copy-start = (bf16[16,256,256]{2,1,0:T(8,128)(2,1)S(1)}, bf16[16,256,256]{2,1,0:T(8,128)(2,1)}, u32[]{:S(2)}) copy-start(bf16[16,256,256]{2,1,0:T(8,128)(2,1)} %refs_0_.3) | copy-start | bytes 6291460
  27.8 6.3 %copy-start.2 = (f32[16,256]{1,0:T(8,128)S(1)}, f32[16,256]{1,0:T(8,128)}, u32[]{:S(2)}) copy-start(f32[16,256]{1,0:T(8,128)} %refs_0_.2) | copy-start | bytes 49156
  27.8 34.2 %collective-permute-start.12 = (bf16[2,8,256,128]{3,2,1,0:T(8,128)(2,1)S(1)}, bf16[2,8,256,128]{3,2,1,0:T(8,128)(2,1)S(1)}, u32[]{:S(2)}, u32[]{:S(2)}) collective-permute-start(bf16[2,8,256,128]{3,2,1,0:T(8,128)(2,1)S(1)} %pack.7.refs_7_), channel_id=1, source_target_pairs={{0,2},{2,0},{4,6},{6,4},{8,10},{10,8},{12,14},{14,12},{1,3},{3,1},... | collective-permute-start | bytes 3145736 | tf_op jit(solution)/shard_map/ppermute | solution.py:416
  28.4 41.0 %collective-permute-start.11 = (bf16[16,256,128]{2,1,0:T(8,128)(2,1)S(1)}, bf16[16,256,128]{2,1,0:T(8,128)(2,1)S(1)}, u32[]{:S(2)}, u32[]{:S(2)}) collective-permute-start(bf16[16,256,128]{2,1,0:T(8,128)(2,1)S(1)} %constant_dynamic-slice_fusion.refs_3_.refs_6_), channel_id=1, source_target_pairs={{0,4},{2,6},{4,0},{6,2},{8,12},{10,14},{12,8},{14,10},{1,5},{3,7},... | collective-permute-start | bytes 3145736 | tf_op jit(solution)/shard_map/ppermute | solution.py:416
  30.2 39.2 %collective-permute-start.16 = (bf16[16,256,128]{2,1,0:T(8,128)(2,1)S(1)}, bf16[16,256,128]{2,1,0:T(8,128)(2,1)S(1)}, u32[]{:S(2)}, u32[]{:S(2)}) collective-permute-start(bf16[16,256,128]{2,1,0:T(8,128)(2,1)S(1)} %constant_dynamic-slice_fusion.refs_3_.refs_6_), channel_id=1, source_target_pairs={{4,8},{6,10},{8,4},{10,6},{5,9},{7,11},{9,5},{11,7},{20,24},{22,26... | collective-permute-start | bytes 3145736 | tf_op jit(solution)/shard_map/ppermute | solution.py:416
  51.0 11.0 %collective-permute-start.13 = (bf16[1,8,256,128]{3,2,1,0:T(8,128)(2,1)S(1)}, bf16[1,8,256,128]{3,2,1,0:T(8,128)(2,1)S(1)}, u32[]{:S(2)}, u32[]{:S(2)}) collective-permute-start(bf16[1,8,256,128]{3,2,1,0:T(8,128)(2,1)S(1)} %pack.8.refs_6_), channel_id=1, source_target_pairs={{0,2},{2,0},{4,6},{6,4},{8,10},{10,8},{12,14},{14,12},{1,3},{3,1},... | collective-permute-start | bytes 1572872 | tf_op jit(solution)/shard_map/ppermute | solution.py:416
  51.6 21.3 %collective-permute-start.14 = (bf16[16,256,128]{2,1,0:T(8,128)(2,1)S(1)}, bf16[16,256,128]{2,1,0:T(8,128)(2,1)S(1)}, u32[]{:S(2)}, u32[]{:S(2)}) collective-permute-start(bf16[16,256,128]{2,1,0:T(8,128)(2,1)S(1)} %collective-permute-done.8.refs_2_.refs_0_.refs_5_), channel_id=1, source_target_pairs={{0,1},{1,0},{2,3},{3,2},{4,5},{5,4},{6,7},{7,6},{8,9},{9,8},{10,11... | collective-permute-start | bytes 3145736 | tf_op jit(solution)/shard_map/ppermute | solution.py:419
  69.4 4.9 %collective-permute-start.15 = (bf16[16,256,128]{2,1,0:T(8,128)(2,1)S(1)}, bf16[16,256,128]{2,1,0:T(8,128)(2,1)S(1)}, u32[]{:S(2)}, u32[]{:S(2)}) collective-permute-start(bf16[16,256,128]{2,1,0:T(8,128)(2,1)S(1)} %collective-permute-done.11.refs_1_.refs_2_.refs_6_), channel_id=1, source_target_pairs={{0,1},{1,0},{2,3},{3,2},{4,5},{5,4},{6,7},{7,6},{8,9},{9,8},{10,11... | collective-permute-start | bytes 3145736 | tf_op jit(solution)/shard_map/ppermute | solution.py:419
  70.1 28.7 %collective-permute-start.17 = (bf16[2,8,256,128]{3,2,1,0:T(8,128)(2,1)S(1)}, bf16[2,8,256,128]{3,2,1,0:T(8,128)(2,1)S(1)}, u32[]{:S(2)}, u32[]{:S(2)}) collective-permute-start(bf16[2,8,256,128]{3,2,1,0:T(8,128)(2,1)S(1)} %get-tuple-element.85.refs_3_), channel_id=1, source_target_pairs={{4,2},{6,0},{8,14},{10,12},{5,3},{7,1},{9,15},{11,13},{20,18},{22,... | collective-permute-start | bytes 3145736 | tf_op jit(solution)/shard_map/ppermute | solution.py:416
  71.4 29.3 %collective-permute-start.10 = (bf16[16,256,128]{2,1,0:T(8,128)(2,1)S(1)}, bf16[16,256,128]{2,1,0:T(8,128)(2,1)S(1)}, u32[]{:S(2)}, u32[]{:S(2)}) collective-permute-start(bf16[16,256,128]{2,1,0:T(8,128)(2,1)S(1)} %collective-permute-done.8.refs_2_.refs_0_.refs_5_), channel_id=1, source_target_pairs={{4,8},{6,10},{8,4},{10,6},{5,9},{7,11},{9,5},{11,7},{20,24},{22,26... | collective-permute-start | bytes 3145736 | tf_op jit(solution)/shard_map/ppermute | solution.py:416
  72.1 41.2 %collective-permute-start.19 = (bf16[16,256,128]{2,1,0:T(8,128)(2,1)S(1)}, bf16[16,256,128]{2,1,0:T(8,128)(2,1)S(1)}, u32[]{:S(2)}, u32[]{:S(2)}) collective-permute-start(bf16[16,256,128]{2,1,0:T(8,128)(2,1)S(1)} %collective-permute-done.11.refs_1_.refs_2_.refs_6_), channel_id=1, source_target_pairs={{4,8},{6,10},{8,4},{10,6},{5,9},{7,11},{9,5},{11,7},{20,24},{22,26... | collective-permute-start | bytes 3145736 | tf_op jit(solution)/shard_map/ppermute | solution.py:416
  72.8 45.0 %collective-permute-start.26 = (bf16[2,8,256,128]{3,2,1,0:T(8,128)(2,1)S(1)}, bf16[2,8,256,128]{3,2,1,0:T(8,128)(2,1)S(1)}, u32[]{:S(2)}, u32[]{:S(2)}) collective-permute-start(bf16[2,8,256,128]{3,2,1,0:T(8,128)(2,1)S(1)} %get-tuple-element.94), channel_id=1, source_target_pairs={{4,6},{6,4},{8,10},{10,8},{5,7},{7,5},{9,11},{11,9},{20,22},{22,20... | collective-permute-start | bytes 3145736 | tf_op jit(solution)/shard_map/ppermute | solution.py:416
  76.9 31.8 %collective-permute-start.21 = (bf16[8,256,128]{2,1,0:T(8,128)(2,1)S(1)}, bf16[8,256,128]{2,1,0:T(8,128)(2,1)S(1)}, u32[]{:S(2)}, u32[]{:S(2)}) collective-permute-start(bf16[8,256,128]{2,1,0:T(8,128)(2,1)S(1)} %amplitudes.12.refs_7_), channel_id=1, source_target_pairs={{4,0},{6,2},{8,12},{10,14},{5,1},{7,3},{9,13},{11,15},{20,16},{22,... | collective-permute-start | bytes 1572872 | tf_op jit(solution)/shard_map/ppermute | solution.py:416
  98.8 13.2 %collective-permute-start.20 = (bf16[1,8,256,128]{3,2,1,0:T(8,128)(2,1)S(1)}, bf16[1,8,256,128]{3,2,1,0:T(8,128)(2,1)S(1)}, u32[]{:S(2)}, u32[]{:S(2)}) collective-permute-start(bf16[1,8,256,128]{3,2,1,0:T(8,128)(2,1)S(1)} %pack.10.refs_9_), channel_id=1, source_target_pairs={{0,2},{2,0},{4,6},{6,4},{8,10},{10,8},{12,14},{14,12},{1,3},{3,1},... | collective-permute-start | bytes 1572872 | tf_op jit(solution)/shard_map/ppermute | solution.py:416
  101.3 17.3 %collective-permute-start.18 = (bf16[1,8,256,128]{3,2,1,0:T(8,128)(2,1)S(1)}, bf16[1,8,256,128]{3,2,1,0:T(8,128)(2,1)S(1)}, u32[]{:S(2)}, u32[]{:S(2)}) collective-permute-start(bf16[1,8,256,128]{3,2,1,0:T(8,128)(2,1)S(1)} %get-tuple-element.88), channel_id=1, source_target_pairs={{4,6},{6,4},{8,10},{10,8},{5,7},{7,5},{9,11},{11,9},{20,22},{22,20... | collective-permute-start | bytes 1572872 | tf_op jit(solution)/shard_map/ppermute | solution.py:416
  108.7 16.3 %collective-permute-start.23 = (bf16[1,8,256,128]{3,2,1,0:T(8,128)(2,1)S(1)}, bf16[1,8,256,128]{3,2,1,0:T(8,128)(2,1)S(1)}, u32[]{:S(2)}, u32[]{:S(2)}) collective-permute-start(bf16[1,8,256,128]{3,2,1,0:T(8,128)(2,1)S(1)} %get-tuple-element.89.refs_8_), channel_id=1, source_target_pairs={{4,2},{6,0},{8,14},{10,12},{5,3},{7,1},{9,15},{11,13},{20,18},{22,... | collective-permute-start | bytes 1572872 | tf_op jit(solution)/shard_map/ppermute | solution.py:416
  114.0 25.4 %collective-permute-start.24 = (bf16[1,8,256,128]{3,2,1,0:T(8,128)(2,1)S(1)}, bf16[1,8,256,128]{3,2,1,0:T(8,128)(2,1)S(1)}, u32[]{:S(2)}, u32[]{:S(2)}) collective-permute-start(bf16[1,8,256,128]{3,2,1,0:T(8,128)(2,1)S(1)} %pack.12.refs_9_), channel_id=1, source_target_pairs={{4,2},{6,0},{8,14},{10,12},{5,3},{7,1},{9,15},{11,13},{20,18},{22,... | collective-permute-start | bytes 1572872 | tf_op jit(solution)/shard_map/ppermute | solution.py:416
  115.9 32.5 %collective-permute-start.25 = (bf16[8,256,128]{2,1,0:T(8,128)(2,1)S(1)}, bf16[8,256,128]{2,1,0:T(8,128)(2,1)S(1)}, u32[]{:S(2)}, u32[]{:S(2)}) collective-permute-start(bf16[8,256,128]{2,1,0:T(8,128)(2,1)S(1)} %amplitudes.16.refs_3_), channel_id=1, source_target_pairs={{4,0},{6,2},{8,12},{10,14},{5,1},{7,3},{9,13},{11,15},{20,16},{22,... | collective-permute-start | bytes 1572872 | tf_op jit(solution)/shard_map/ppermute | solution.py:416
  117.9 31.6 %collective-permute-start.22 = (bf16[1,8,256,128]{3,2,1,0:T(8,128)(2,1)S(1)}, bf16[1,8,256,128]{3,2,1,0:T(8,128)(2,1)S(1)}, u32[]{:S(2)}, u32[]{:S(2)}) collective-permute-start(bf16[1,8,256,128]{3,2,1,0:T(8,128)(2,1)S(1)} %pack.13.refs_7_), channel_id=1, source_target_pairs={{4,6},{6,4},{8,10},{10,8},{5,7},{7,5},{9,11},{11,9},{20,22},{22,20... | collective-permute-start | bytes 1572872 | tf_op jit(solution)/shard_map/ppermute | solution.py:416
  154.9 4.6 %collective-permute-start.28 = (f32[16,128,256]{2,1,0:T(8,128)}, f32[16,128,256]{2,1,0:T(8,128)}, u32[]{:S(2)}, u32[]{:S(2)}) collective-permute-start(f32[16,128,256]{2,1,0:T(8,128)} %get-tuple-element.103), channel_id=1, source_target_pairs={{0,1},{1,0},{2,3},{3,2},{4,5},{5,4},{6,7},{7,6},{8,9},{9,8},{10,11... | collective-permute-start | bytes 6291464 | tf_op jit(solution)/shard_map/ppermute | solution.py:419
  155.2 3.9 %collective-permute-start.27 = (f32[64]{0:T(128)S(1)}, f32[64]{0:T(128)S(1)}, u32[]{:S(2)}, u32[]{:S(2)}) collective-permute-start(f32[64]{0:T(128)S(1)} %multiply_reduce_fusion), channel_id=1, source_target_pairs={{0,1},{1,0},{2,3},{3,2},{4,5},{5,4},{6,7},{7,6},{8,9},{9,8},{10,11... | collective-permute-start | bytes 776 | tf_op jit(solution)/shard_map/ppermute | solution.py:419

commit v16 on v13

--- a/solution.py
+++ b/solution.py
@@ -385,7 +385,7 @@
             left = jnp.concatenate([t[k, pl.ds(row, half), :] for k in own], axis=1)
             out[o] = lax.dot_general(
                 left, right, (((1,), (1,)), ((), ())), preferred_element_type=f32
-            )
+            ).astype(out.dtype)
 
 
 def densities(t_all, start, per_orb, half):
@@ -393,7 +393,7 @@
     shape = jax.ShapeDtypeStruct((npair // per_orb, half, nvd), f32)
     return pl.pallas_call(
         density_kernel,
-        out_shape=(shape, shape),
+        out_shape=(shape, jax.ShapeDtypeStruct(shape.shape, bf16)),
         in_specs=[SMEM, VMEM],
         out_specs=(VMEM, VMEM),
         compiler_params=LIGHT,
@@ -490,7 +490,7 @@
     t_all, e_all = own_pairs(7, "asked", [fourth, fourth_diagonal], held)
 
     mine, away = densities(t_all, col0, per_orb, half)
-    density = mine + swap_core(away)
+    density = mine + swap_core(away).astype(f32)
 
     energy = jnp.sum(hit * jnp.sum(e_all, axis=1)[None, :], axis=1)
     energy = (energy + swap_core(energy)) / nvd

time: 162 us -> 158 us (0.975)
  no operation moved by 1% of the time
where the time goes in v16:
time: 158 us
  waiting for transfers between devices  91 us (58%)
  starting transfers between devices  30.3 us (19%)
  Pallas kernels  24.7 us (16%)
  local copies, waits for them, and re-layouts  7.14 us (5%)
  other arithmetic  3.63 us (2%)
    ppermute x24, waiting for transfers between devices, pp(): return lax.ppermute(x, 'orb', perm)  89.2 us
    ppermute x24, starting transfers between devices, pp(): return lax.ppermute(x, 'orb', perm)  29.2 us
    pallas_call x10, Pallas kernels, amplitudes(): pl.pallas_call(lambda *refs: amplitudes_kernel(mode, call, per_orb, [len(...  11.2 us
    pallas_call x7, Pallas kernels, pack(): pl.pallas_call(lambda *refs: pack_kernel(kinds, len(tbls), *refs), out_sh...  4.83 us
    pallas_call x2, Pallas kernels, turn(): pl.pallas_call(turn_kernel, out_shape=[jax.ShapeDtypeStruct((count, cols,...  4.47 us
    unnamed x14, local copies, waits for them, and re-layouts  3.35 us
  transfers between devices with their start and end apart: 29, of which 12 were waited for; matrix products, arithmetic and copies ran while one was open for 3% of the time, Pallas kernels for 13%

profile of v16, /device:TPU:0, one launch (start us, length us, event | category | flops | bytes accessed | tf_op | source)
XLA Modules:
  0.0 157.9 jit_solution(12529930255478143291)
XLA Ops:
  1.2 0.7 copy-done.1
  4.7 2.6 %collective-permute-start = (f32[24,384]{1,0:T(8,128)S(1)}, f32[24,384]{1,0:T(8,128)S(1)}, u32[]{:S(2)}, u32[]{:S(2)}) collective-permute-start(f32[24,384]{1,0:T(8,128)S(1)} %get-tuple-element.55.refs_1_), channel_id=1, source_target_pairs={{0,2},{2,0},{4,6},{6,4},{8,10},{10,8},{12,14},{14,12},{1,3},{3,1},... | collective-permute-start | bytes 110600 | tf_op jit(solution)/shard_map/ppermute | solution.py:416
  7.3 1.6 collective-permute-start.1
  8.9 3.0 %collective-permute-start.3 = (f32[24,384]{1,0:T(8,128)S(1)}, f32[24,384]{1,0:T(8,128)S(1)}, u32[]{:S(2)}, u32[]{:S(2)}) collective-permute-start(f32[24,384]{1,0:T(8,128)S(1)} %get-tuple-element.55.refs_1_), channel_id=1, source_target_pairs={{0,8},{2,10},{4,12},{6,14},{8,0},{10,2},{12,4},{14,6},{1,9},{3,11}... | collective-permute-start | bytes 110600 | tf_op jit(solution)/shard_map/ppermute | solution.py:416
  11.8 1.4 collective-permute-start.4
  13.3 3.5 %collective-permute-start.5 = (f32[24,384]{1,0:T(8,128)S(1)}, f32[24,384]{1,0:T(8,128)S(1)}, u32[]{:S(2)}, u32[]{:S(2)}) collective-permute-start(f32[24,384]{1,0:T(8,128)S(1)} %get-tuple-element.55.refs_1_), channel_id=1, source_target_pairs={{0,12},{2,14},{4,8},{6,10},{8,4},{10,6},{12,0},{14,2},{1,13},{3,15... | collective-permute-start | bytes 110600 | tf_op jit(solution)/shard_map/ppermute | solution.py:416
  17.0 1.3 constant_dynamic-slice_fusion.1.refs_2_.refs_5_
  18.4 0.8 collective-permute-done.5.refs_7_
  19.2 4.6 %collective-permute-done.6.refs_8_ = f32[24,384]{1,0:T(8,128)S(1)} collective-permute-done((f32[24,384]{1,0:T(8,128)S(1)}, f32[24,384]{1,0:T(8,128)S(1)}, u32[]{:S(2)}, u32[]{:S(2)}) %collective-permute-start.6) | collective-permute-done | bytes 36896 | tf_op jit(solution)/shard_map/ppermute | solution.py:416
  23.8 0.7 collective-permute-start.12
  24.6 1.3 tables.1
  25.9 1.3 constant_dynamic-slice_fusion.refs_3_.refs_6_
  27.2 0.7 pack.7.refs_7_
  28.2 3.2 %collective-permute-start.10 = (bf16[16,256,128]{2,1,0:T(8,128)(2,1)S(1)}, bf16[16,256,128]{2,1,0:T(8,128)(2,1)S(1)}, u32[]{:S(2)}, u32[]{:S(2)}) collective-permute-start(bf16[16,256,128]{2,1,0:T(8,128)(2,1)S(1)} %constant_dynamic-slice_fusion.refs_3_.refs_6_), channel_id=1, source_target_pairs={{0,4},{2,6},{4,0},{6,2},{8,12},{10,14},{12,8},{14,10},{1,5},{3,7},... | collective-permute-start | bytes 3145736 | tf_op jit(solution)/shard_map/ppermute | solution.py:416
  31.4 0.7 collective-permute-start.16
  32.2 3.1 %turn.2 = (bf16[16,256,256]{2,1,0:T(8,128)(2,1)S(1)}, bf16[16,256,256]{2,1,0:T(8,128)(2,1)S(1)}) custom-call(bf16[16,256,256]{2,1,0:T(8,128)(2,1)S(1)} %copy-done, bf16[16,256,256]{2,1,0:T(8,128)(2,1)} %collective-permute-done.7.refs_1_), custom_call_target="tpu_custom_call" | custom-call | flops 1 | bytes 1 | tf_op jit(solution)/shard_map/turn/pallas_call | solution.py:257
  35.9 1.3 amplitudes.10
  37.2 12.6 %collective-permute-done.8.refs_2_.refs_0_.refs_5_ = bf16[16,256,128]{2,1,0:T(8,128)(2,1)S(1)} collective-permute-done((bf16[16,256,128]{2,1,0:T(8,128)(2,1)S(1)}, bf16[16,256,128]{2,1,0:T(8,128)(2,1)S(1)}, u32[]{:S(2)}, u32[]{:S(2)}) %collective-permute-start.8) | collective-permute-done | bytes 1048608 | tf_op jit(solution)/shard_map/ppermute | solution.py:416
  49.9 0.7 pack.8.refs_6_
  50.9 10.7 %collective-permute-done.13.refs_7_.refs_5_ = bf16[1,8,256,128]{3,2,1,0:T(8,128)(2,1)S(1)} collective-permute-done((bf16[1,8,256,128]{3,2,1,0:T(8,128)(2,1)S(1)}, bf16[1,8,256,128]{3,2,1,0:T(8,128)(2,1)S(1)}, u32[]{:S(2)}, u32[]{:S(2)}) %collective-permute-start.13) | collective-permute-done | bytes 524320 | tf_op jit(solution)/shard_map/ppermute | solution.py:416
  61.6 1.3 amplitudes.11
  62.9 5.7 %collective-permute-done.10.refs_1_.refs_2_.refs_6_ = bf16[16,256,128]{2,1,0:T(8,128)(2,1)S(1)} collective-permute-done((bf16[16,256,128]{2,1,0:T(8,128)(2,1)S(1)}, bf16[16,256,128]{2,1,0:T(8,128)(2,1)S(1)}, u32[]{:S(2)}, u32[]{:S(2)}) %collective-permute-start.10) | collective-permute-done | bytes 1048608 | tf_op jit(solution)/shard_map/ppermute | solution.py:416
  69.3 1.3 collective-permute-start.17
  70.6 0.7 collective-permute-start.9
  71.3 0.7 collective-permute-start.19
  72.1 0.7 collective-permute-start.26
  72.8 0.7 pack.10.refs_9_
  73.5 1.3 turn.3
  76.1 1.3 collective-permute-start.21
  77.4 20.8 %collective-permute-done.17.refs_8_.refs_6_ = bf16[2,8,256,128]{3,2,1,0:T(8,128)(2,1)S(1)} collective-permute-done((bf16[2,8,256,128]{3,2,1,0:T(8,128)(2,1)S(1)}, bf16[2,8,256,128]{3,2,1,0:T(8,128)(2,1)S(1)}, u32[]{:S(2)}, u32[]{:S(2)}) %collective-permute-start.17) | collective-permute-done | bytes 1048608 | tf_op jit(solution)/shard_map/ppermute | solution.py:416
  98.2 1.6 %collective-permute-start.20 = (bf16[1,8,256,128]{3,2,1,0:T(8,128)(2,1)S(1)}, bf16[1,8,256,128]{3,2,1,0:T(8,128)(2,1)S(1)}, u32[]{:S(2)}, u32[]{:S(2)}) collective-permute-start(bf16[1,8,256,128]{3,2,1,0:T(8,128)(2,1)S(1)} %pack.10.refs_9_), channel_id=1, source_target_pairs={{0,2},{2,0},{4,6},{6,4},{8,10},{10,8},{12,14},{14,12},{1,3},{3,1},... | collective-permute-start | bytes 1572872 | tf_op jit(solution)/shard_map/ppermute | solution.py:416
  99.8 1.3 amplitudes.13
  102.6 5.5 %collective-permute-done.21.refs_7_ = bf16[8,256,128]{2,1,0:T(8,128)(2,1)S(1)} collective-permute-done((bf16[8,256,128]{2,1,0:T(8,128)(2,1)S(1)}, bf16[8,256,128]{2,1,0:T(8,128)(2,1)S(1)}, u32[]{:S(2)}, u32[]{:S(2)}) %collective-permute-start.21) | collective-permute-done | bytes 524320 | tf_op jit(solution)/shard_map/ppermute | solution.py:416
  108.0 1.3 collective-permute-start.23
  109.3 0.9 amplitudes.14
  110.2 0.8 collective-permute-done.20.refs_6_
  111.0 1.3 amplitudes.15
  113.0 1.3 collective-permute-start.24
  114.9 1.3 collective-permute-start.25
  117.6 5.5 %collective-permute-done.23.refs_9_.refs_7_ = bf16[1,8,256,128]{3,2,1,0:T(8,128)(2,1)S(1)} collective-permute-done((bf16[1,8,256,128]{3,2,1,0:T(8,128)(2,1)S(1)}, bf16[1,8,256,128]{3,2,1,0:T(8,128)(2,1)S(1)}, u32[]{:S(2)}, u32[]{:S(2)}) %collective-permute-start.23) | collective-permute-done | bytes 524320 | tf_op jit(solution)/shard_map/ppermute | solution.py:416
  123.1 1.3 amplitudes.17
  124.5 14.2 %collective-permute-done.24.refs_8_ = bf16[1,8,256,128]{3,2,1,0:T(8,128)(2,1)S(1)} collective-permute-done((bf16[1,8,256,128]{3,2,1,0:T(8,128)(2,1)S(1)}, bf16[1,8,256,128]{3,2,1,0:T(8,128)(2,1)S(1)}, u32[]{:S(2)}, u32[]{:S(2)}) %collective-permute-start.24) | collective-permute-done | bytes 524320 | tf_op jit(solution)/shard_map/ppermute | solution.py:416
  138.7 7.9 %collective-permute-done.25.refs_7_ = bf16[8,256,128]{2,1,0:T(8,128)(2,1)S(1)} collective-permute-done((bf16[8,256,128]{2,1,0:T(8,128)(2,1)S(1)}, bf16[8,256,128]{2,1,0:T(8,128)(2,1)S(1)}, u32[]{:S(2)}, u32[]{:S(2)}) %collective-permute-start.25) | collective-permute-done | bytes 524320 | tf_op jit(solution)/shard_map/ppermute | solution.py:416
  146.6 1.1 amplitudes.18
  147.7 1.4 amplitudes.19
  149.1 2.7 %densities.1 = (f32[16,128,256]{2,1,0:T(8,128)S(1)}, bf16[16,128,256]{2,1,0:T(8,128)(2,1)S(1)}) custom-call(s32[1]{0:T(128)} %bitcast.5.start, bf16[64,256,128]{2,1,0:T(8,128)(2,1)S(1)} %get-tuple-element.101.t), custom_call_target="tpu_custom_call" | custom-call | flops 1 | bytes 1 | tf_op jit(solution)/shard_map/densities/pallas_call | solution.py:394
  152.7 1.8 %collective-permute-done.27 = f32[64]{0:T(128)S(1)} collective-permute-done((f32[64]{0:T(128)S(1)}, f32[64]{0:T(128)S(1)}, u32[]{:S(2)}, u32[]{:S(2)}) %collective-permute-start.27) | collective-permute-done | bytes 288 | tf_op jit(solution)/shard_map/ppermute | solution.py:419
  155.0 2.8 %convert_add_fusion = f32[16,128,256]{2,1,0:T(8,128)} fusion(f32[16,128,256]{2,1,0:T(8,128)S(1)} %get-tuple-element.102, bf16[16,128,256]{2,1,0:T(8,128)(2,1)} %collective-permute-done.28), kind=kLoop, calls=%fused_computation | loop fusion | flops 1048576 | bytes 5242880 | tf_op jit(solution)/shard_map/add | solution.py:493
  (56 shorter events, 12.1 us)
Async XLA Ops:
  0.6 25.2 %collective-permute-start.7 = (bf16[16,256,256]{2,1,0:T(8,128)(2,1)}, bf16[16,256,256]{2,1,0:T(8,128)(2,1)}, u32[]{:S(2)}, u32[]{:S(2)}) collective-permute-start(bf16[16,256,256]{2,1,0:T(8,128)(2,1)} %refs_0_.3), channel_id=1, source_target_pairs={{0,1},{1,0},{2,3},{3,2},{4,5},{5,4},{6,7},{7,6},{8,9},{9,8},{10,11... | collective-permute-start | bytes 6291464 | tf_op jit(solution)/shard_map/ppermute | solution.py:419
  1.1 0.7 copy-start.1
  1.9 0.7 copy-start.3
  2.5 0.7 copy-start.4
  3.2 0.7 copy-start.5
  3.8 0.7 copy-start.6
  4.7 7.2 %collective-permute-start = (f32[24,384]{1,0:T(8,128)S(1)}, f32[24,384]{1,0:T(8,128)S(1)}, u32[]{:S(2)}, u32[]{:S(2)}) collective-permute-start(f32[24,384]{1,0:T(8,128)S(1)} %get-tuple-element.55.refs_1_), channel_id=1, source_target_pairs={{0,2},{2,0},{4,6},{6,4},{8,10},{10,8},{12,14},{14,12},{1,3},{3,1},... | collective-permute-start | bytes 110600 | tf_op jit(solution)/shard_map/ppermute | solution.py:416
  7.3 6.0 %collective-permute-start.1 = (f32[24,384]{1,0:T(8,128)S(1)}, f32[24,384]{1,0:T(8,128)S(1)}, u32[]{:S(2)}, u32[]{:S(2)}) collective-permute-start(f32[24,384]{1,0:T(8,128)S(1)} %get-tuple-element.55.refs_1_), channel_id=1, source_target_pairs={{0,4},{2,6},{4,0},{6,2},{8,12},{10,14},{12,8},{14,10},{1,5},{3,7},... | collective-permute-start | bytes 110600 | tf_op jit(solution)/shard_map/ppermute | solution.py:416
  8.8 7.9 %collective-permute-start.2 = (f32[24,384]{1,0:T(8,128)S(1)}, f32[24,384]{1,0:T(8,128)S(1)}, u32[]{:S(2)}, u32[]{:S(2)}) collective-permute-start(f32[24,384]{1,0:T(8,128)S(1)} %get-tuple-element.55.refs_1_), channel_id=1, source_target_pairs={{0,6},{2,4},{4,2},{6,0},{8,14},{10,12},{12,10},{14,8},{1,7},{3,5},... | collective-permute-start | bytes 110600 | tf_op jit(solution)/shard_map/ppermute | solution.py:416
  8.9 9.5 %collective-permute-start.3 = (f32[24,384]{1,0:T(8,128)S(1)}, f32[24,384]{1,0:T(8,128)S(1)}, u32[]{:S(2)}, u32[]{:S(2)}) collective-permute-start(f32[24,384]{1,0:T(8,128)S(1)} %get-tuple-element.55.refs_1_), channel_id=1, source_target_pairs={{0,8},{2,10},{4,12},{6,14},{8,0},{10,2},{12,4},{14,6},{1,9},{3,11}... | collective-permute-start | bytes 110600 | tf_op jit(solution)/shard_map/ppermute | solution.py:416
  11.8 6.5 %collective-permute-start.4 = (f32[24,384]{1,0:T(8,128)S(1)}, f32[24,384]{1,0:T(8,128)S(1)}, u32[]{:S(2)}, u32[]{:S(2)}) collective-permute-start(f32[24,384]{1,0:T(8,128)S(1)} %get-tuple-element.55.refs_1_), channel_id=1, source_target_pairs={{0,10},{2,8},{4,14},{6,12},{8,2},{10,0},{12,6},{14,4},{1,11},{3,9}... | collective-permute-start | bytes 110600 | tf_op jit(solution)/shard_map/ppermute | solution.py:416
  13.3 5.9 %collective-permute-start.5 = (f32[24,384]{1,0:T(8,128)S(1)}, f32[24,384]{1,0:T(8,128)S(1)}, u32[]{:S(2)}, u32[]{:S(2)}) collective-permute-start(f32[24,384]{1,0:T(8,128)S(1)} %get-tuple-element.55.refs_1_), channel_id=1, source_target_pairs={{0,12},{2,14},{4,8},{6,10},{8,4},{10,6},{12,0},{14,2},{1,13},{3,15... | collective-permute-start | bytes 110600 | tf_op jit(solution)/shard_map/ppermute | solution.py:416
  16.7 7.1 %collective-permute-start.6 = (f32[24,384]{1,0:T(8,128)S(1)}, f32[24,384]{1,0:T(8,128)S(1)}, u32[]{:S(2)}, u32[]{:S(2)}) collective-permute-start(f32[24,384]{1,0:T(8,128)S(1)} %get-tuple-element.55.refs_1_), channel_id=1, source_target_pairs={{0,14},{2,12},{4,10},{6,8},{8,6},{10,4},{12,2},{14,0},{1,15},{3,13... | collective-permute-start | bytes 110600 | tf_op jit(solution)/shard_map/ppermute | solution.py:416
  23.8 26.1 %collective-permute-start.8 = (bf16[16,256,128]{2,1,0:T(8,128)(2,1)S(1)}, bf16[16,256,128]{2,1,0:T(8,128)(2,1)S(1)}, u32[]{:S(2)}, u32[]{:S(2)}) collective-permute-start(bf16[16,256,128]{2,1,0:T(8,128)(2,1)S(1)} %constant_dynamic-slice_fusion.1.refs_2_.refs_5_), channel_id=1, source_target_pairs={{0,4},{2,6},{4,0},{6,2},{8,12},{10,14},{12,8},{14,10},{1,5},{3,7},... | collective-permute-start | bytes 3145736 | tf_op jit(solution)/shard_map/ppermute | solution.py:416
  23.8 26.1 %collective-permute-start.12 = (bf16[16,256,128]{2,1,0:T(8,128)(2,1)S(1)}, bf16[16,256,128]{2,1,0:T(8,128)(2,1)S(1)}, u32[]{:S(2)}, u32[]{:S(2)}) collective-permute-start(bf16[16,256,128]{2,1,0:T(8,128)(2,1)S(1)} %constant_dynamic-slice_fusion.1.refs_2_.refs_5_), channel_id=1, source_target_pairs={{4,8},{6,10},{8,4},{10,6},{5,9},{7,11},{9,5},{11,7},{20,24},{22,26... | collective-permute-start | bytes 3145736 | tf_op jit(solution)/shard_map/ppermute | solution.py:416
  27.2 5.0 %copy-start = (bf16[16,256,256]{2,1,0:T(8,128)(2,1)S(1)}, bf16[16,256,256]{2,1,0:T(8,128)(2,1)}, u32[]{:S(2)}) copy-start(bf16[16,256,256]{2,1,0:T(8,128)(2,1)} %refs_0_.3) | copy-start | bytes 6291460
  28.0 7.4 %copy-start.2 = (f32[16,256]{1,0:T(8,128)S(1)}, f32[16,256]{1,0:T(8,128)}, u32[]{:S(2)}) copy-start(f32[16,256]{1,0:T(8,128)} %refs_0_.2) | copy-start | bytes 49156
  28.0 33.6 %collective-permute-start.11 = (bf16[2,8,256,128]{3,2,1,0:T(8,128)(2,1)S(1)}, bf16[2,8,256,128]{3,2,1,0:T(8,128)(2,1)S(1)}, u32[]{:S(2)}, u32[]{:S(2)}) collective-permute-start(bf16[2,8,256,128]{3,2,1,0:T(8,128)(2,1)S(1)} %pack.7.refs_7_), channel_id=1, source_target_pairs={{0,2},{2,0},{4,6},{6,4},{8,10},{10,8},{12,14},{14,12},{1,3},{3,1},... | collective-permute-start | bytes 3145736 | tf_op jit(solution)/shard_map/ppermute | solution.py:416
  28.2 40.4 %collective-permute-start.10 = (bf16[16,256,128]{2,1,0:T(8,128)(2,1)S(1)}, bf16[16,256,128]{2,1,0:T(8,128)(2,1)S(1)}, u32[]{:S(2)}, u32[]{:S(2)}) collective-permute-start(bf16[16,256,128]{2,1,0:T(8,128)(2,1)S(1)} %constant_dynamic-slice_fusion.refs_3_.refs_6_), channel_id=1, source_target_pairs={{0,4},{2,6},{4,0},{6,2},{8,12},{10,14},{12,8},{14,10},{1,5},{3,7},... | collective-permute-start | bytes 3145736 | tf_op jit(solution)/shard_map/ppermute | solution.py:416
  31.4 37.2 %collective-permute-start.16 = (bf16[16,256,128]{2,1,0:T(8,128)(2,1)S(1)}, bf16[16,256,128]{2,1,0:T(8,128)(2,1)S(1)}, u32[]{:S(2)}, u32[]{:S(2)}) collective-permute-start(bf16[16,256,128]{2,1,0:T(8,128)(2,1)S(1)} %constant_dynamic-slice_fusion.refs_3_.refs_6_), channel_id=1, source_target_pairs={{4,8},{6,10},{8,4},{10,6},{5,9},{7,11},{9,5},{11,7},{20,24},{22,26... | collective-permute-start | bytes 3145736 | tf_op jit(solution)/shard_map/ppermute | solution.py:416
  50.6 11.0 %collective-permute-start.13 = (bf16[1,8,256,128]{3,2,1,0:T(8,128)(2,1)S(1)}, bf16[1,8,256,128]{3,2,1,0:T(8,128)(2,1)S(1)}, u32[]{:S(2)}, u32[]{:S(2)}) collective-permute-start(bf16[1,8,256,128]{3,2,1,0:T(8,128)(2,1)S(1)} %pack.8.refs_6_), channel_id=1, source_target_pairs={{0,2},{2,0},{4,6},{6,4},{8,10},{10,8},{12,14},{14,12},{1,3},{3,1},... | collective-permute-start | bytes 1572872 | tf_op jit(solution)/shard_map/ppermute | solution.py:416
  50.9 21.2 %collective-permute-start.14 = (bf16[16,256,128]{2,1,0:T(8,128)(2,1)S(1)}, bf16[16,256,128]{2,1,0:T(8,128)(2,1)S(1)}, u32[]{:S(2)}, u32[]{:S(2)}) collective-permute-start(bf16[16,256,128]{2,1,0:T(8,128)(2,1)S(1)} %collective-permute-done.8.refs_2_.refs_0_.refs_5_), channel_id=1, source_target_pairs={{0,1},{1,0},{2,3},{3,2},{4,5},{5,4},{6,7},{7,6},{8,9},{9,8},{10,11... | collective-permute-start | bytes 3145736 | tf_op jit(solution)/shard_map/ppermute | solution.py:419
  68.6 4.9 %collective-permute-start.15 = (bf16[16,256,128]{2,1,0:T(8,128)(2,1)S(1)}, bf16[16,256,128]{2,1,0:T(8,128)(2,1)S(1)}, u32[]{:S(2)}, u32[]{:S(2)}) collective-permute-start(bf16[16,256,128]{2,1,0:T(8,128)(2,1)S(1)} %collective-permute-done.10.refs_1_.refs_2_.refs_6_), channel_id=1, source_target_pairs={{0,1},{1,0},{2,3},{3,2},{4,5},{5,4},{6,7},{7,6},{8,9},{9,8},{10,11... | collective-permute-start | bytes 3145736 | tf_op jit(solution)/shard_map/ppermute | solution.py:419
  69.3 28.9 %collective-permute-start.17 = (bf16[2,8,256,128]{3,2,1,0:T(8,128)(2,1)S(1)}, bf16[2,8,256,128]{3,2,1,0:T(8,128)(2,1)S(1)}, u32[]{:S(2)}, u32[]{:S(2)}) collective-permute-start(bf16[2,8,256,128]{3,2,1,0:T(8,128)(2,1)S(1)} %get-tuple-element.85.refs_3_), channel_id=1, source_target_pairs={{4,2},{6,0},{8,14},{10,12},{5,3},{7,1},{9,15},{11,13},{20,18},{22,... | collective-permute-start | bytes 3145736 | tf_op jit(solution)/shard_map/ppermute | solution.py:416
  70.6 30.6 %collective-permute-start.9 = (bf16[16,256,128]{2,1,0:T(8,128)(2,1)S(1)}, bf16[16,256,128]{2,1,0:T(8,128)(2,1)S(1)}, u32[]{:S(2)}, u32[]{:S(2)}) collective-permute-start(bf16[16,256,128]{2,1,0:T(8,128)(2,1)S(1)} %collective-permute-done.8.refs_2_.refs_0_.refs_5_), channel_id=1, source_target_pairs={{4,8},{6,10},{8,4},{10,6},{5,9},{7,11},{9,5},{11,7},{20,24},{22,26... | collective-permute-start | bytes 3145736 | tf_op jit(solution)/shard_map/ppermute | solution.py:416
  71.3 41.0 %collective-permute-start.19 = (bf16[16,256,128]{2,1,0:T(8,128)(2,1)S(1)}, bf16[16,256,128]{2,1,0:T(8,128)(2,1)S(1)}, u32[]{:S(2)}, u32[]{:S(2)}) collective-permute-start(bf16[16,256,128]{2,1,0:T(8,128)(2,1)S(1)} %collective-permute-done.10.refs_1_.refs_2_.refs_6_), channel_id=1, source_target_pairs={{4,8},{6,10},{8,4},{10,6},{5,9},{7,11},{9,5},{11,7},{20,24},{22,26... | collective-permute-start | bytes 3145736 | tf_op jit(solution)/shard_map/ppermute | solution.py:416
  72.1 44.8 %collective-permute-start.26 = (bf16[2,8,256,128]{3,2,1,0:T(8,128)(2,1)S(1)}, bf16[2,8,256,128]{3,2,1,0:T(8,128)(2,1)S(1)}, u32[]{:S(2)}, u32[]{:S(2)}) collective-permute-start(bf16[2,8,256,128]{3,2,1,0:T(8,128)(2,1)S(1)} %get-tuple-element.94), channel_id=1, source_target_pairs={{4,6},{6,4},{8,10},{10,8},{5,7},{7,5},{9,11},{11,9},{20,22},{22,20... | collective-permute-start | bytes 3145736 | tf_op jit(solution)/shard_map/ppermute | solution.py:416
  76.1 31.9 %collective-permute-start.21 = (bf16[8,256,128]{2,1,0:T(8,128)(2,1)S(1)}, bf16[8,256,128]{2,1,0:T(8,128)(2,1)S(1)}, u32[]{:S(2)}, u32[]{:S(2)}) collective-permute-start(bf16[8,256,128]{2,1,0:T(8,128)(2,1)S(1)} %amplitudes.12.refs_7_), channel_id=1, source_target_pairs={{4,0},{6,2},{8,12},{10,14},{5,1},{7,3},{9,13},{11,15},{20,16},{22,... | collective-permute-start | bytes 1572872 | tf_op jit(solution)/shard_map/ppermute | solution.py:416
  98.2 12.8 %collective-permute-start.20 = (bf16[1,8,256,128]{3,2,1,0:T(8,128)(2,1)S(1)}, bf16[1,8,256,128]{3,2,1,0:T(8,128)(2,1)S(1)}, u32[]{:S(2)}, u32[]{:S(2)}) collective-permute-start(bf16[1,8,256,128]{3,2,1,0:T(8,128)(2,1)S(1)} %pack.10.refs_9_), channel_id=1, source_target_pairs={{0,2},{2,0},{4,6},{6,4},{8,10},{10,8},{12,14},{14,12},{1,3},{3,1},... | collective-permute-start | bytes 1572872 | tf_op jit(solution)/shard_map/ppermute | solution.py:416
  101.9 15.8 %collective-permute-start.18 = (bf16[1,8,256,128]{3,2,1,0:T(8,128)(2,1)S(1)}, bf16[1,8,256,128]{3,2,1,0:T(8,128)(2,1)S(1)}, u32[]{:S(2)}, u32[]{:S(2)}) collective-permute-start(bf16[1,8,256,128]{3,2,1,0:T(8,128)(2,1)S(1)} %get-tuple-element.88), channel_id=1, source_target_pairs={{4,6},{6,4},{8,10},{10,8},{5,7},{7,5},{9,11},{11,9},{20,22},{22,20... | collective-permute-start | bytes 1572872 | tf_op jit(solution)/shard_map/ppermute | solution.py:416
  108.0 15.1 %collective-permute-start.23 = (bf16[1,8,256,128]{3,2,1,0:T(8,128)(2,1)S(1)}, bf16[1,8,256,128]{3,2,1,0:T(8,128)(2,1)S(1)}, u32[]{:S(2)}, u32[]{:S(2)}) collective-permute-start(bf16[1,8,256,128]{3,2,1,0:T(8,128)(2,1)S(1)} %get-tuple-element.89.refs_8_), channel_id=1, source_target_pairs={{4,2},{6,0},{8,14},{10,12},{5,3},{7,1},{9,15},{11,13},{20,18},{22,... | collective-permute-start | bytes 1572872 | tf_op jit(solution)/shard_map/ppermute | solution.py:416
  113.0 25.7 %collective-permute-start.24 = (bf16[1,8,256,128]{3,2,1,0:T(8,128)(2,1)S(1)}, bf16[1,8,256,128]{3,2,1,0:T(8,128)(2,1)S(1)}, u32[]{:S(2)}, u32[]{:S(2)}) collective-permute-start(bf16[1,8,256,128]{3,2,1,0:T(8,128)(2,1)S(1)} %pack.12.refs_9_), channel_id=1, source_target_pairs={{4,2},{6,0},{8,14},{10,12},{5,3},{7,1},{9,15},{11,13},{20,18},{22,... | collective-permute-start | bytes 1572872 | tf_op jit(solution)/shard_map/ppermute | solution.py:416
  114.9 31.7 %collective-permute-start.25 = (bf16[8,256,128]{2,1,0:T(8,128)(2,1)S(1)}, bf16[8,256,128]{2,1,0:T(8,128)(2,1)S(1)}, u32[]{:S(2)}, u32[]{:S(2)}) collective-permute-start(bf16[8,256,128]{2,1,0:T(8,128)(2,1)S(1)} %amplitudes.16.refs_3_), channel_id=1, source_target_pairs={{4,0},{6,2},{8,12},{10,14},{5,1},{7,3},{9,13},{11,15},{20,16},{22,... | collective-permute-start | bytes 1572872 | tf_op jit(solution)/shard_map/ppermute | solution.py:416
  116.9 30.8 %collective-permute-start.22 = (bf16[1,8,256,128]{3,2,1,0:T(8,128)(2,1)S(1)}, bf16[1,8,256,128]{3,2,1,0:T(8,128)(2,1)S(1)}, u32[]{:S(2)}, u32[]{:S(2)}) collective-permute-start(bf16[1,8,256,128]{3,2,1,0:T(8,128)(2,1)S(1)} %pack.13.refs_7_), channel_id=1, source_target_pairs={{4,6},{6,4},{8,10},{10,8},{5,7},{7,5},{9,11},{11,9},{20,22},{22,20... | collective-permute-start | bytes 1572872 | tf_op jit(solution)/shard_map/ppermute | solution.py:416
  151.8 3.2 %collective-permute-start.28 = (bf16[16,128,256]{2,1,0:T(8,128)(2,1)S(1)}, bf16[16,128,256]{2,1,0:T(8,128)(2,1)}, u32[]{:S(2)}, u32[]{:S(2)}) collective-permute-start(bf16[16,128,256]{2,1,0:T(8,128)(2,1)S(1)} %get-tuple-element.103), channel_id=1, source_target_pairs={{0,1},{1,0},{2,3},{3,2},{4,5},{5,4},{6,7},{7,6},{8,9},{9,8},{10,11... | collective-permute-start | bytes 3145736 | tf_op jit(solution)/shard_map/ppermute | solution.py:419
  152.1 2.4 %collective-permute-start.27 = (f32[64]{0:T(128)S(1)}, f32[64]{0:T(128)S(1)}, u32[]{:S(2)}, u32[]{:S(2)}) collective-permute-start(f32[64]{0:T(128)S(1)} %multiply_reduce_fusion), channel_id=1, source_target_pairs={{0,1},{1,0},{2,3},{3,2},{4,5},{5,4},{6,7},{7,6},{8,9},{9,8},{10,11... | collective-permute-start | bytes 776 | tf_op jit(solution)/shard_map/ppermute | solution.py:419

commit v17 on v16

--- a/solution.py
+++ b/solution.py
@@ -489,12 +489,12 @@
     held = own_pairs(3, "served", [far], held, (fourth_diagonal[1],), (ready_3,))
     t_all, e_all = own_pairs(7, "asked", [fourth, fourth_diagonal], held)
 
+    energy = jnp.sum(hit * jnp.sum(e_all, axis=1)[None, :], axis=1)
+    t_all, energy = lax.optimization_barrier((t_all, energy))
+    crossed = swap_core(energy)
     mine, away = densities(t_all, col0, per_orb, half)
     density = mine + swap_core(away).astype(f32)
-
-    energy = jnp.sum(hit * jnp.sum(e_all, axis=1)[None, :], axis=1)
-    energy = (energy + swap_core(energy)) / nvd
-    return (energy, density)
+    return ((energy + crossed) / nvd, density)
 
 
 def solution(mesh):

time: 158 us -> 162 us (1.025)
  local copies, waits for them, and re-layouts: 7.14 us -> 11.3 us
    unnamed x14 -> x18, local copies, waits for them, and re-layouts: 3.35 us -> 7.5 us
where the time goes in v17:
time: 162 us; the launch traced here: 161 us
  waiting for transfers between devices  91.4 us (56%)
  starting transfers between devices  30.2 us (19%)
  Pallas kernels  24.7 us (15%)
  local copies, waits for them, and re-layouts  11.3 us (7%)
  other arithmetic  2.41 us (1%)
    ppermute x24, waiting for transfers between devices, pp(): return lax.ppermute(x, 'orb', perm)  89.2 us
    ppermute x24, starting transfers between devices, pp(): return lax.ppermute(x, 'orb', perm)  29.2 us
    pallas_call x10, Pallas kernels, amplitudes(): pl.pallas_call(lambda *refs: amplitudes_kernel(mode, call, per_orb, [len(...  11.2 us
    unnamed x18, local copies, waits for them, and re-layouts  7.5 us
    pallas_call x7, Pallas kernels, pack(): pl.pallas_call(lambda *refs: pack_kernel(kinds, len(tbls), *refs), out_sh...  4.83 us
    pallas_call x2, Pallas kernels, turn(): pl.pallas_call(turn_kernel, out_shape=[jax.ShapeDtypeStruct((count, cols,...  4.47 us
  transfers between devices with their start and end apart: 29, of which 12 were waited for; matrix products, arithmetic and copies ran while one was open for 3% of the time, Pallas kernels for 13%

profile of v17, /device:TPU:0, one launch (start us, length us, event | category | flops | bytes accessed | tf_op | source)
XLA Modules:
  0.0 161.1 jit_solution(8753731239928991286)
XLA Ops:
  1.2 0.7 copy-done.3
  4.7 2.6 %collective-permute-start = (f32[24,384]{1,0:T(8,128)S(1)}, f32[24,384]{1,0:T(8,128)S(1)}, u32[]{:S(2)}, u32[]{:S(2)}) collective-permute-start(f32[24,384]{1,0:T(8,128)S(1)} %get-tuple-element.56.refs_1_), channel_id=1, source_target_pairs={{0,2},{2,0},{4,6},{6,4},{8,10},{10,8},{12,14},{14,12},{1,3},{3,1},... | collective-permute-start | bytes 110600 | tf_op jit(solution)/shard_map/ppermute | solution.py:416
  7.3 1.6 collective-permute-start.1
  8.9 3.0 %collective-permute-start.3 = (f32[24,384]{1,0:T(8,128)S(1)}, f32[24,384]{1,0:T(8,128)S(1)}, u32[]{:S(2)}, u32[]{:S(2)}) collective-permute-start(f32[24,384]{1,0:T(8,128)S(1)} %get-tuple-element.56.refs_1_), channel_id=1, source_target_pairs={{0,8},{2,10},{4,12},{6,14},{8,0},{10,2},{12,4},{14,6},{1,9},{3,11}... | collective-permute-start | bytes 110600 | tf_op jit(solution)/shard_map/ppermute | solution.py:416
  11.8 1.4 collective-permute-start.4
  13.3 3.5 %collective-permute-start.5 = (f32[24,384]{1,0:T(8,128)S(1)}, f32[24,384]{1,0:T(8,128)S(1)}, u32[]{:S(2)}, u32[]{:S(2)}) collective-permute-start(f32[24,384]{1,0:T(8,128)S(1)} %get-tuple-element.56.refs_1_), channel_id=1, source_target_pairs={{0,12},{2,14},{4,8},{6,10},{8,4},{10,6},{12,0},{14,2},{1,13},{3,15... | collective-permute-start | bytes 110600 | tf_op jit(solution)/shard_map/ppermute | solution.py:416
  17.0 1.3 constant_dynamic-slice_fusion.1.refs_2_.refs_5_
  18.4 0.8 collective-permute-done.5.refs_7_
  19.2 4.6 %collective-permute-done.6.refs_8_ = f32[24,384]{1,0:T(8,128)S(1)} collective-permute-done((f32[24,384]{1,0:T(8,128)S(1)}, f32[24,384]{1,0:T(8,128)S(1)}, u32[]{:S(2)}, u32[]{:S(2)}) %collective-permute-start.6) | collective-permute-done | bytes 36896 | tf_op jit(solution)/shard_map/ppermute | solution.py:416
  23.8 0.7 collective-permute-start.12
  24.6 1.3 tables.1
  25.9 1.3 constant_dynamic-slice_fusion.refs_3_.refs_6_
  27.2 0.7 pack.7.refs_7_
  28.2 3.2 %collective-permute-start.10 = (bf16[16,256,128]{2,1,0:T(8,128)(2,1)S(1)}, bf16[16,256,128]{2,1,0:T(8,128)(2,1)S(1)}, u32[]{:S(2)}, u32[]{:S(2)}) collective-permute-start(bf16[16,256,128]{2,1,0:T(8,128)(2,1)S(1)} %constant_dynamic-slice_fusion.refs_3_.refs_6_), channel_id=1, source_target_pairs={{0,4},{2,6},{4,0},{6,2},{8,12},{10,14},{12,8},{14,10},{1,5},{3,7},... | collective-permute-start | bytes 3145736 | tf_op jit(solution)/shard_map/ppermute | solution.py:416
  31.4 0.7 collective-permute-start.16
  32.2 3.1 %turn.2 = (bf16[16,256,256]{2,1,0:T(8,128)(2,1)S(1)}, bf16[16,256,256]{2,1,0:T(8,128)(2,1)S(1)}) custom-call(bf16[16,256,256]{2,1,0:T(8,128)(2,1)S(1)} %copy-done.2, bf16[16,256,256]{2,1,0:T(8,128)(2,1)} %collective-permute-done.7.refs_1_), custom_call_target="tpu_custom_call" | custom-call | flops 1 | bytes 1 | tf_op jit(solution)/shard_map/turn/pallas_call | solution.py:257
  35.9 1.3 amplitudes.10
  37.2 12.6 %collective-permute-done.8.refs_2_.refs_0_.refs_5_ = bf16[16,256,128]{2,1,0:T(8,128)(2,1)S(1)} collective-permute-done((bf16[16,256,128]{2,1,0:T(8,128)(2,1)S(1)}, bf16[16,256,128]{2,1,0:T(8,128)(2,1)S(1)}, u32[]{:S(2)}, u32[]{:S(2)}) %collective-permute-start.8) | collective-permute-done | bytes 1048608 | tf_op jit(solution)/shard_map/ppermute | solution.py:416
  50.9 10.7 %collective-permute-done.13.refs_7_.refs_5_ = bf16[1,8,256,128]{3,2,1,0:T(8,128)(2,1)S(1)} collective-permute-done((bf16[1,8,256,128]{3,2,1,0:T(8,128)(2,1)S(1)}, bf16[1,8,256,128]{3,2,1,0:T(8,128)(2,1)S(1)}, u32[]{:S(2)}, u32[]{:S(2)}) %collective-permute-start.13) | collective-permute-done | bytes 524320 | tf_op jit(solution)/shard_map/ppermute | solution.py:416
  61.6 1.3 amplitudes.11
  62.9 5.7 %collective-permute-done.10.refs_1_.refs_2_.refs_6_ = bf16[16,256,128]{2,1,0:T(8,128)(2,1)S(1)} collective-permute-done((bf16[16,256,128]{2,1,0:T(8,128)(2,1)S(1)}, bf16[16,256,128]{2,1,0:T(8,128)(2,1)S(1)}, u32[]{:S(2)}, u32[]{:S(2)}) %collective-permute-start.10) | collective-permute-done | bytes 1048608 | tf_op jit(solution)/shard_map/ppermute | solution.py:416
  69.3 1.3 collective-permute-start.17
  70.6 0.7 collective-permute-start.9
  71.3 0.7 collective-permute-start.19
  72.1 0.7 collective-permute-start.26
  73.5 1.3 turn.3
  76.1 1.3 collective-permute-start.21
  77.4 20.8 %collective-permute-done.17.refs_8_.refs_6_ = bf16[2,8,256,128]{3,2,1,0:T(8,128)(2,1)S(1)} collective-permute-done((bf16[2,8,256,128]{3,2,1,0:T(8,128)(2,1)S(1)}, bf16[2,8,256,128]{3,2,1,0:T(8,128)(2,1)S(1)}, u32[]{:S(2)}, u32[]{:S(2)}) %collective-permute-start.17) | collective-permute-done | bytes 1048608 | tf_op jit(solution)/shard_map/ppermute | solution.py:416
  98.2 1.6 %collective-permute-start.20 = (bf16[1,8,256,128]{3,2,1,0:T(8,128)(2,1)S(1)}, bf16[1,8,256,128]{3,2,1,0:T(8,128)(2,1)S(1)}, u32[]{:S(2)}, u32[]{:S(2)}) collective-permute-start(bf16[1,8,256,128]{3,2,1,0:T(8,128)(2,1)S(1)} %pack.10.refs_9_), channel_id=1, source_target_pairs={{0,2},{2,0},{4,6},{6,4},{8,10},{10,8},{12,14},{14,12},{1,3},{3,1},... | collective-permute-start | bytes 1572872 | tf_op jit(solution)/shard_map/ppermute | solution.py:416
  99.8 1.3 amplitudes.13
  102.6 5.5 %collective-permute-done.21.refs_7_ = bf16[8,256,128]{2,1,0:T(8,128)(2,1)S(1)} collective-permute-done((bf16[8,256,128]{2,1,0:T(8,128)(2,1)S(1)}, bf16[8,256,128]{2,1,0:T(8,128)(2,1)S(1)}, u32[]{:S(2)}, u32[]{:S(2)}) %collective-permute-start.21) | collective-permute-done | bytes 524320 | tf_op jit(solution)/shard_map/ppermute | solution.py:416
  108.0 1.3 collective-permute-start.23
  109.3 0.9 amplitudes.14
  110.2 0.8 collective-permute-done.20.refs_6_
  111.0 1.3 amplitudes.15
  113.0 1.3 collective-permute-start.24
  114.9 1.3 collective-permute-start.25
  117.6 5.5 %collective-permute-done.23.refs_9_.refs_7_ = bf16[1,8,256,128]{3,2,1,0:T(8,128)(2,1)S(1)} collective-permute-done((bf16[1,8,256,128]{3,2,1,0:T(8,128)(2,1)S(1)}, bf16[1,8,256,128]{3,2,1,0:T(8,128)(2,1)S(1)}, u32[]{:S(2)}, u32[]{:S(2)}) %collective-permute-start.23) | collective-permute-done | bytes 524320 | tf_op jit(solution)/shard_map/ppermute | solution.py:416
  123.1 1.3 amplitudes.17
  124.5 14.2 %collective-permute-done.24.refs_8_ = bf16[1,8,256,128]{3,2,1,0:T(8,128)(2,1)S(1)} collective-permute-done((bf16[1,8,256,128]{3,2,1,0:T(8,128)(2,1)S(1)}, bf16[1,8,256,128]{3,2,1,0:T(8,128)(2,1)S(1)}, u32[]{:S(2)}, u32[]{:S(2)}) %collective-permute-start.24) | collective-permute-done | bytes 524320 | tf_op jit(solution)/shard_map/ppermute | solution.py:416
  138.7 7.9 %collective-permute-done.25.refs_7_ = bf16[8,256,128]{2,1,0:T(8,128)(2,1)S(1)} collective-permute-done((bf16[8,256,128]{2,1,0:T(8,128)(2,1)S(1)}, bf16[8,256,128]{2,1,0:T(8,128)(2,1)S(1)}, u32[]{:S(2)}, u32[]{:S(2)}) %collective-permute-start.25) | collective-permute-done | bytes 524320 | tf_op jit(solution)/shard_map/ppermute | solution.py:416
  146.6 1.1 amplitudes.18
  147.7 1.4 amplitudes.19
  149.1 2.0 %copy-done = bf16[64,256,128]{2,1,0:T(8,128)(2,1)} copy-done((bf16[64,256,128]{2,1,0:T(8,128)(2,1)}, bf16[64,256,128]{2,1,0:T(8,128)(2,1)S(1)}, u32[]{:S(2)}) %copy-start) | copy-done | bytes 4194328
  151.3 2.2 %copy-done.1 = bf16[64,256,128]{2,1,0:T(8,128)(2,1)S(1)} copy-done((bf16[64,256,128]{2,1,0:T(8,128)(2,1)S(1)}, bf16[64,256,128]{2,1,0:T(8,128)(2,1)}, u32[]{:S(2)}) %copy-start.1) | copy-done | bytes 4194328
  153.5 2.7 %densities.1 = (f32[16,128,256]{2,1,0:T(8,128)S(1)}, bf16[16,128,256]{2,1,0:T(8,128)(2,1)S(1)}) custom-call(s32[1]{0:T(128)} %bitcast.1.start, bf16[64,256,128]{2,1,0:T(8,128)(2,1)S(1)} %copy-done.1), custom_call_target="tpu_custom_call" | custom-call | flops 1 | bytes 1 | tf_op jit(solution)/shard_map/densities/pallas_call | solution.py:394
  156.8 2.1 %collective-permute-done.27 = f32[64]{0:T(128)S(1)} collective-permute-done((f32[64]{0:T(128)S(1)}, f32[64]{0:T(128)S(1)}, u32[]{:S(2)}, u32[]{:S(2)}) %collective-permute-start.27) | collective-permute-done | bytes 288 | tf_op jit(solution)/shard_map/ppermute | solution.py:419
  159.5 1.6 convert_add_fusion
  (60 shorter events, 13.5 us)
Async XLA Ops:
  0.6 25.2 %collective-permute-start.7 = (bf16[16,256,256]{2,1,0:T(8,128)(2,1)}, bf16[16,256,256]{2,1,0:T(8,128)(2,1)}, u32[]{:S(2)}, u32[]{:S(2)}) collective-permute-start(bf16[16,256,256]{2,1,0:T(8,128)(2,1)} %refs_0_.3), channel_id=1, source_target_pairs={{0,1},{1,0},{2,3},{3,2},{4,5},{5,4},{6,7},{7,6},{8,9},{9,8},{10,11... | collective-permute-start | bytes 6291464 | tf_op jit(solution)/shard_map/ppermute | solution.py:419
  1.1 0.7 copy-start.3
  1.9 0.7 copy-start.5
  2.5 0.7 copy-start.6
  3.2 0.7 copy-start.7
  3.8 0.7 copy-start.8
  4.7 7.2 %collective-permute-start = (f32[24,384]{1,0:T(8,128)S(1)}, f32[24,384]{1,0:T(8,128)S(1)}, u32[]{:S(2)}, u32[]{:S(2)}) collective-permute-start(f32[24,384]{1,0:T(8,128)S(1)} %get-tuple-element.56.refs_1_), channel_id=1, source_target_pairs={{0,2},{2,0},{4,6},{6,4},{8,10},{10,8},{12,14},{14,12},{1,3},{3,1},... | collective-permute-start | bytes 110600 | tf_op jit(solution)/shard_map/ppermute | solution.py:416
  7.3 6.0 %collective-permute-start.1 = (f32[24,384]{1,0:T(8,128)S(1)}, f32[24,384]{1,0:T(8,128)S(1)}, u32[]{:S(2)}, u32[]{:S(2)}) collective-permute-start(f32[24,384]{1,0:T(8,128)S(1)} %get-tuple-element.56.refs_1_), channel_id=1, source_target_pairs={{0,4},{2,6},{4,0},{6,2},{8,12},{10,14},{12,8},{14,10},{1,5},{3,7},... | collective-permute-start | bytes 110600 | tf_op jit(solution)/shard_map/ppermute | solution.py:416
  8.8 7.9 %collective-permute-start.2 = (f32[24,384]{1,0:T(8,128)S(1)}, f32[24,384]{1,0:T(8,128)S(1)}, u32[]{:S(2)}, u32[]{:S(2)}) collective-permute-start(f32[24,384]{1,0:T(8,128)S(1)} %get-tuple-element.56.refs_1_), channel_id=1, source_target_pairs={{0,6},{2,4},{4,2},{6,0},{8,14},{10,12},{12,10},{14,8},{1,7},{3,5},... | collective-permute-start | bytes 110600 | tf_op jit(solution)/shard_map/ppermute | solution.py:416
  8.9 9.5 %collective-permute-start.3 = (f32[24,384]{1,0:T(8,128)S(1)}, f32[24,384]{1,0:T(8,128)S(1)}, u32[]{:S(2)}, u32[]{:S(2)}) collective-permute-start(f32[24,384]{1,0:T(8,128)S(1)} %get-tuple-element.56.refs_1_), channel_id=1, source_target_pairs={{0,8},{2,10},{4,12},{6,14},{8,0},{10,2},{12,4},{14,6},{1,9},{3,11}... | collective-permute-start | bytes 110600 | tf_op jit(solution)/shard_map/ppermute | solution.py:416
  11.8 6.5 %collective-permute-start.4 = (f32[24,384]{1,0:T(8,128)S(1)}, f32[24,384]{1,0:T(8,128)S(1)}, u32[]{:S(2)}, u32[]{:S(2)}) collective-permute-start(f32[24,384]{1,0:T(8,128)S(1)} %get-tuple-element.56.refs_1_), channel_id=1, source_target_pairs={{0,10},{2,8},{4,14},{6,12},{8,2},{10,0},{12,6},{14,4},{1,11},{3,9}... | collective-permute-start | bytes 110600 | tf_op jit(solution)/shard_map/ppermute | solution.py:416
  13.3 5.9 %collective-permute-start.5 = (f32[24,384]{1,0:T(8,128)S(1)}, f32[24,384]{1,0:T(8,128)S(1)}, u32[]{:S(2)}, u32[]{:S(2)}) collective-permute-start(f32[24,384]{1,0:T(8,128)S(1)} %get-tuple-element.56.refs_1_), channel_id=1, source_target_pairs={{0,12},{2,14},{4,8},{6,10},{8,4},{10,6},{12,0},{14,2},{1,13},{3,15... | collective-permute-start | bytes 110600 | tf_op jit(solution)/shard_map/ppermute | solution.py:416
  16.7 7.1 %collective-permute-start.6 = (f32[24,384]{1,0:T(8,128)S(1)}, f32[24,384]{1,0:T(8,128)S(1)}, u32[]{:S(2)}, u32[]{:S(2)}) collective-permute-start(f32[24,384]{1,0:T(8,128)S(1)} %get-tuple-element.56.refs_1_), channel_id=1, source_target_pairs={{0,14},{2,12},{4,10},{6,8},{8,6},{10,4},{12,2},{14,0},{1,15},{3,13... | collective-permute-start | bytes 110600 | tf_op jit(solution)/shard_map/ppermute | solution.py:416
  23.8 26.1 %collective-permute-start.8 = (bf16[16,256,128]{2,1,0:T(8,128)(2,1)S(1)}, bf16[16,256,128]{2,1,0:T(8,128)(2,1)S(1)}, u32[]{:S(2)}, u32[]{:S(2)}) collective-permute-start(bf16[16,256,128]{2,1,0:T(8,128)(2,1)S(1)} %constant_dynamic-slice_fusion.1.refs_2_.refs_5_), channel_id=1, source_target_pairs={{0,4},{2,6},{4,0},{6,2},{8,12},{10,14},{12,8},{14,10},{1,5},{3,7},... | collective-permute-start | bytes 3145736 | tf_op jit(solution)/shard_map/ppermute | solution.py:416
  23.8 26.1 %collective-permute-start.12 = (bf16[16,256,128]{2,1,0:T(8,128)(2,1)S(1)}, bf16[16,256,128]{2,1,0:T(8,128)(2,1)S(1)}, u32[]{:S(2)}, u32[]{:S(2)}) collective-permute-start(bf16[16,256,128]{2,1,0:T(8,128)(2,1)S(1)} %constant_dynamic-slice_fusion.1.refs_2_.refs_5_), channel_id=1, source_target_pairs={{4,8},{6,10},{8,4},{10,6},{5,9},{7,11},{9,5},{11,7},{20,24},{22,26... | collective-permute-start | bytes 3145736 | tf_op jit(solution)/shard_map/ppermute | solution.py:416
  27.2 5.0 %copy-start.2 = (bf16[16,256,256]{2,1,0:T(8,128)(2,1)S(1)}, bf16[16,256,256]{2,1,0:T(8,128)(2,1)}, u32[]{:S(2)}) copy-start(bf16[16,256,256]{2,1,0:T(8,128)(2,1)} %refs_0_.3) | copy-start | bytes 6291460
  28.0 7.4 %copy-start.4 = (f32[16,256]{1,0:T(8,128)S(1)}, f32[16,256]{1,0:T(8,128)}, u32[]{:S(2)}) copy-start(f32[16,256]{1,0:T(8,128)} %refs_0_.2) | copy-start | bytes 49156
  28.0 33.6 %collective-permute-start.11 = (bf16[2,8,256,128]{3,2,1,0:T(8,128)(2,1)S(1)}, bf16[2,8,256,128]{3,2,1,0:T(8,128)(2,1)S(1)}, u32[]{:S(2)}, u32[]{:S(2)}) collective-permute-start(bf16[2,8,256,128]{3,2,1,0:T(8,128)(2,1)S(1)} %pack.7.refs_7_), channel_id=1, source_target_pairs={{0,2},{2,0},{4,6},{6,4},{8,10},{10,8},{12,14},{14,12},{1,3},{3,1},... | collective-permute-start | bytes 3145736 | tf_op jit(solution)/shard_map/ppermute | solution.py:416
  28.2 40.4 %collective-permute-start.10 = (bf16[16,256,128]{2,1,0:T(8,128)(2,1)S(1)}, bf16[16,256,128]{2,1,0:T(8,128)(2,1)S(1)}, u32[]{:S(2)}, u32[]{:S(2)}) collective-permute-start(bf16[16,256,128]{2,1,0:T(8,128)(2,1)S(1)} %constant_dynamic-slice_fusion.refs_3_.refs_6_), channel_id=1, source_target_pairs={{0,4},{2,6},{4,0},{6,2},{8,12},{10,14},{12,8},{14,10},{1,5},{3,7},... | collective-permute-start | bytes 3145736 | tf_op jit(solution)/shard_map/ppermute | solution.py:416
  31.4 37.2 %collective-permute-start.16 = (bf16[16,256,128]{2,1,0:T(8,128)(2,1)S(1)}, bf16[16,256,128]{2,1,0:T(8,128)(2,1)S(1)}, u32[]{:S(2)}, u32[]{:S(2)}) collective-permute-start(bf16[16,256,128]{2,1,0:T(8,128)(2,1)S(1)} %constant_dynamic-slice_fusion.refs_3_.refs_6_), channel_id=1, source_target_pairs={{4,8},{6,10},{8,4},{10,6},{5,9},{7,11},{9,5},{11,7},{20,24},{22,26... | collective-permute-start | bytes 3145736 | tf_op jit(solution)/shard_map/ppermute | solution.py:416
  50.6 11.0 %collective-permute-start.13 = (bf16[1,8,256,128]{3,2,1,0:T(8,128)(2,1)S(1)}, bf16[1,8,256,128]{3,2,1,0:T(8,128)(2,1)S(1)}, u32[]{:S(2)}, u32[]{:S(2)}) collective-permute-start(bf16[1,8,256,128]{3,2,1,0:T(8,128)(2,1)S(1)} %pack.8.refs_6_), channel_id=1, source_target_pairs={{0,2},{2,0},{4,6},{6,4},{8,10},{10,8},{12,14},{14,12},{1,3},{3,1},... | collective-permute-start | bytes 1572872 | tf_op jit(solution)/shard_map/ppermute | solution.py:416
  50.9 21.2 %collective-permute-start.14 = (bf16[16,256,128]{2,1,0:T(8,128)(2,1)S(1)}, bf16[16,256,128]{2,1,0:T(8,128)(2,1)S(1)}, u32[]{:S(2)}, u32[]{:S(2)}) collective-permute-start(bf16[16,256,128]{2,1,0:T(8,128)(2,1)S(1)} %collective-permute-done.8.refs_2_.refs_0_.refs_5_), channel_id=1, source_target_pairs={{0,1},{1,0},{2,3},{3,2},{4,5},{5,4},{6,7},{7,6},{8,9},{9,8},{10,11... | collective-permute-start | bytes 3145736 | tf_op jit(solution)/shard_map/ppermute | solution.py:419
  68.6 4.9 %collective-permute-start.15 = (bf16[16,256,128]{2,1,0:T(8,128)(2,1)S(1)}, bf16[16,256,128]{2,1,0:T(8,128)(2,1)S(1)}, u32[]{:S(2)}, u32[]{:S(2)}) collective-permute-start(bf16[16,256,128]{2,1,0:T(8,128)(2,1)S(1)} %collective-permute-done.10.refs_1_.refs_2_.refs_6_), channel_id=1, source_target_pairs={{0,1},{1,0},{2,3},{3,2},{4,5},{5,4},{6,7},{7,6},{8,9},{9,8},{10,11... | collective-permute-start | bytes 3145736 | tf_op jit(solution)/shard_map/ppermute | solution.py:419
  69.3 28.9 %collective-permute-start.17 = (bf16[2,8,256,128]{3,2,1,0:T(8,128)(2,1)S(1)}, bf16[2,8,256,128]{3,2,1,0:T(8,128)(2,1)S(1)}, u32[]{:S(2)}, u32[]{:S(2)}) collective-permute-start(bf16[2,8,256,128]{3,2,1,0:T(8,128)(2,1)S(1)} %get-tuple-element.86.refs_3_), channel_id=1, source_target_pairs={{4,2},{6,0},{8,14},{10,12},{5,3},{7,1},{9,15},{11,13},{20,18},{22,... | collective-permute-start | bytes 3145736 | tf_op jit(solution)/shard_map/ppermute | solution.py:416
  70.6 30.6 %collective-permute-start.9 = (bf16[16,256,128]{2,1,0:T(8,128)(2,1)S(1)}, bf16[16,256,128]{2,1,0:T(8,128)(2,1)S(1)}, u32[]{:S(2)}, u32[]{:S(2)}) collective-permute-start(bf16[16,256,128]{2,1,0:T(8,128)(2,1)S(1)} %collective-permute-done.8.refs_2_.refs_0_.refs_5_), channel_id=1, source_target_pairs={{4,8},{6,10},{8,4},{10,6},{5,9},{7,11},{9,5},{11,7},{20,24},{22,26... | collective-permute-start | bytes 3145736 | tf_op jit(solution)/shard_map/ppermute | solution.py:416
  71.3 41.0 %collective-permute-start.19 = (bf16[16,256,128]{2,1,0:T(8,128)(2,1)S(1)}, bf16[16,256,128]{2,1,0:T(8,128)(2,1)S(1)}, u32[]{:S(2)}, u32[]{:S(2)}) collective-permute-start(bf16[16,256,128]{2,1,0:T(8,128)(2,1)S(1)} %collective-permute-done.10.refs_1_.refs_2_.refs_6_), channel_id=1, source_target_pairs={{4,8},{6,10},{8,4},{10,6},{5,9},{7,11},{9,5},{11,7},{20,24},{22,26... | collective-permute-start | bytes 3145736 | tf_op jit(solution)/shard_map/ppermute | solution.py:416
  72.1 44.8 %collective-permute-start.26 = (bf16[2,8,256,128]{3,2,1,0:T(8,128)(2,1)S(1)}, bf16[2,8,256,128]{3,2,1,0:T(8,128)(2,1)S(1)}, u32[]{:S(2)}, u32[]{:S(2)}) collective-permute-start(bf16[2,8,256,128]{3,2,1,0:T(8,128)(2,1)S(1)} %get-tuple-element.95), channel_id=1, source_target_pairs={{4,6},{6,4},{8,10},{10,8},{5,7},{7,5},{9,11},{11,9},{20,22},{22,20... | collective-permute-start | bytes 3145736 | tf_op jit(solution)/shard_map/ppermute | solution.py:416
  76.1 31.9 %collective-permute-start.21 = (bf16[8,256,128]{2,1,0:T(8,128)(2,1)S(1)}, bf16[8,256,128]{2,1,0:T(8,128)(2,1)S(1)}, u32[]{:S(2)}, u32[]{:S(2)}) collective-permute-start(bf16[8,256,128]{2,1,0:T(8,128)(2,1)S(1)} %amplitudes.12.refs_7_), channel_id=1, source_target_pairs={{4,0},{6,2},{8,12},{10,14},{5,1},{7,3},{9,13},{11,15},{20,16},{22,... | collective-permute-start | bytes 1572872 | tf_op jit(solution)/shard_map/ppermute | solution.py:416
  98.2 12.8 %collective-permute-start.20 = (bf16[1,8,256,128]{3,2,1,0:T(8,128)(2,1)S(1)}, bf16[1,8,256,128]{3,2,1,0:T(8,128)(2,1)S(1)}, u32[]{:S(2)}, u32[]{:S(2)}) collective-permute-start(bf16[1,8,256,128]{3,2,1,0:T(8,128)(2,1)S(1)} %pack.10.refs_9_), channel_id=1, source_target_pairs={{0,2},{2,0},{4,6},{6,4},{8,10},{10,8},{12,14},{14,12},{1,3},{3,1},... | collective-permute-start | bytes 1572872 | tf_op jit(solution)/shard_map/ppermute | solution.py:416
  101.9 15.8 %collective-permute-start.18 = (bf16[1,8,256,128]{3,2,1,0:T(8,128)(2,1)S(1)}, bf16[1,8,256,128]{3,2,1,0:T(8,128)(2,1)S(1)}, u32[]{:S(2)}, u32[]{:S(2)}) collective-permute-start(bf16[1,8,256,128]{3,2,1,0:T(8,128)(2,1)S(1)} %get-tuple-element.89), channel_id=1, source_target_pairs={{4,6},{6,4},{8,10},{10,8},{5,7},{7,5},{9,11},{11,9},{20,22},{22,20... | collective-permute-start | bytes 1572872 | tf_op jit(solution)/shard_map/ppermute | solution.py:416
  108.0 15.1 %collective-permute-start.23 = (bf16[1,8,256,128]{3,2,1,0:T(8,128)(2,1)S(1)}, bf16[1,8,256,128]{3,2,1,0:T(8,128)(2,1)S(1)}, u32[]{:S(2)}, u32[]{:S(2)}) collective-permute-start(bf16[1,8,256,128]{3,2,1,0:T(8,128)(2,1)S(1)} %get-tuple-element.90.refs_8_), channel_id=1, source_target_pairs={{4,2},{6,0},{8,14},{10,12},{5,3},{7,1},{9,15},{11,13},{20,18},{22,... | collective-permute-start | bytes 1572872 | tf_op jit(solution)/shard_map/ppermute | solution.py:416
  113.0 25.7 %collective-permute-start.24 = (bf16[1,8,256,128]{3,2,1,0:T(8,128)(2,1)S(1)}, bf16[1,8,256,128]{3,2,1,0:T(8,128)(2,1)S(1)}, u32[]{:S(2)}, u32[]{:S(2)}) collective-permute-start(bf16[1,8,256,128]{3,2,1,0:T(8,128)(2,1)S(1)} %pack.12.refs_9_), channel_id=1, source_target_pairs={{4,2},{6,0},{8,14},{10,12},{5,3},{7,1},{9,15},{11,13},{20,18},{22,... | collective-permute-start | bytes 1572872 | tf_op jit(solution)/shard_map/ppermute | solution.py:416
  114.9 31.7 %collective-permute-start.25 = (bf16[8,256,128]{2,1,0:T(8,128)(2,1)S(1)}, bf16[8,256,128]{2,1,0:T(8,128)(2,1)S(1)}, u32[]{:S(2)}, u32[]{:S(2)}) collective-permute-start(bf16[8,256,128]{2,1,0:T(8,128)(2,1)S(1)} %amplitudes.16.refs_3_), channel_id=1, source_target_pairs={{4,0},{6,2},{8,12},{10,14},{5,1},{7,3},{9,13},{11,15},{20,16},{22,... | collective-permute-start | bytes 1572872 | tf_op jit(solution)/shard_map/ppermute | solution.py:416
  116.9 30.8 %collective-permute-start.22 = (bf16[1,8,256,128]{3,2,1,0:T(8,128)(2,1)S(1)}, bf16[1,8,256,128]{3,2,1,0:T(8,128)(2,1)S(1)}, u32[]{:S(2)}, u32[]{:S(2)}) collective-permute-start(bf16[1,8,256,128]{3,2,1,0:T(8,128)(2,1)S(1)} %pack.13.refs_7_), channel_id=1, source_target_pairs={{4,6},{6,4},{8,10},{10,8},{5,7},{7,5},{9,11},{11,9},{20,22},{22,20... | collective-permute-start | bytes 1572872 | tf_op jit(solution)/shard_map/ppermute | solution.py:416
  149.1 2.0 %copy-start = (bf16[64,256,128]{2,1,0:T(8,128)(2,1)}, bf16[64,256,128]{2,1,0:T(8,128)(2,1)S(1)}, u32[]{:S(2)}) copy-start(bf16[64,256,128]{2,1,0:T(8,128)(2,1)S(1)} %get-tuple-element.105.t) | copy-start | bytes 12582916
  151.3 2.2 %copy-start.1 = (bf16[64,256,128]{2,1,0:T(8,128)(2,1)S(1)}, bf16[64,256,128]{2,1,0:T(8,128)(2,1)}, u32[]{:S(2)}) copy-start(bf16[64,256,128]{2,1,0:T(8,128)(2,1)} %copy-done) | copy-start | bytes 12582916
  156.2 3.2 %collective-permute-start.28 = (bf16[16,128,256]{2,1,0:T(8,128)(2,1)S(1)}, bf16[16,128,256]{2,1,0:T(8,128)(2,1)S(1)}, u32[]{:S(2)}, u32[]{:S(2)}) collective-permute-start(bf16[16,128,256]{2,1,0:T(8,128)(2,1)S(1)} %get-tuple-element.107), channel_id=1, source_target_pairs={{0,1},{1,0},{2,3},{3,2},{4,5},{5,4},{6,7},{7,6},{8,9},{9,8},{10,11... | collective-permute-start | bytes 3145736 | tf_op jit(solution)/shard_map/ppermute | solution.py:419
  156.3 2.6 %collective-permute-start.27 = (f32[64]{0:T(128)S(1)}, f32[64]{0:T(128)S(1)}, u32[]{:S(2)}, u32[]{:S(2)}) collective-permute-start(f32[64]{0:T(128)S(1)} %multiply_reduce_fusion), channel_id=1, source_target_pairs={{0,1},{1,0},{2,3},{3,2},{4,5},{5,4},{6,7},{7,6},{8,9},{9,8},{10,11... | collective-permute-start | bytes 776 | tf_op jit(solution)/shard_map/ppermute | solution.py:419

commit v18 on v16

--- a/solution.py
+++ b/solution.py
@@ -96,8 +96,10 @@
 LIGHT = pltpu.CompilerParams(vmem_limit_bytes=LIMIT // 4)
 
 
-def lists_kernel(cap, vir, occ, size, owner, slot, small, hit):
+def lists_kernel(cap, vir, vectors, small, hit):
     n, (count, nvd) = hit.shape[0], vir.shape
+    occ, size = vectors[0:1, :count], vectors[1:2, :count]
+    owner, slot = vectors[2:3, :n], vectors[3:4, :n]
 
     def column(row, m):
         eye = lax.broadcasted_iota(i32, (m, m), 0) == lax.broadcasted_iota(i32, (m, m), 1)
@@ -105,7 +107,7 @@
 
     down = lax.broadcasted_iota(i32, (n, n), 0).astype(f32)
     along = lax.broadcasted_iota(i32, (n, n), 1).astype(f32)
-    owner_row = owner[...].astype(f32)
+    owner_row = owner
     owner_col = column(owner_row, n)
     before = (owner_col == owner_row) & (along < down)
     target = owner_col * cap + jnp.sum(jnp.where(before, 1.0, 0.0), axis=1, keepdims=True)
@@ -114,10 +116,10 @@
     small[...] = jnp.zeros_like(small)
     small[:count, :nvd] = vir[...]
     lane = lax.broadcasted_iota(i32, (count, 128), 1)
-    occ_col, size_col = column(occ[...], count), column(size[...].astype(f32), count)
+    occ_col, size_col = column(occ, count), column(size, count)
     small[:count, nvd:] = jnp.where(lane == 0, occ_col, jnp.where(lane == 1, size_col, 0.0))
     small[count : count + 1, :n] = jnp.sum(jnp.where(found, down, 0.0), axis=0, keepdims=True)
-    slot_col = column(slot[...].astype(f32), n)
+    slot_col = column(slot, n)
     small[count : count + 1, 128 : 128 + n] = jnp.sum(
         jnp.where(found, slot_col, 0.0), axis=0, keepdims=True
     )
@@ -126,18 +128,24 @@
 def lists(vir, occ, size, owner, slot, cap):
     count, nvd = vir.shape
     n = slot.shape[0]
+    vectors = jnp.stack(
+        [
+            jnp.pad(x.reshape(-1).astype(f32), (0, 128 - x.size))
+            for x in (occ, size, owner, slot)
+        ]
+    )
     return pl.pallas_call(
         lambda *refs: lists_kernel(cap, *refs),
         out_shape=(
             jax.ShapeDtypeStruct((count + 8, nvd + 128), f32),
             jax.ShapeDtypeStruct((n, n), f32),
         ),
-        in_specs=[VMEM] * 5,
+        in_specs=[VMEM] * 2,
         out_specs=(VMEM, VMEM),
         compiler_params=PARAMS,
         cost_estimate=TINY,
         name="lists",
-    )(vir, occ.reshape(1, -1), size.reshape(1, -1), owner.reshape(1, -1), slot.reshape(1, -1))
+    )(vir, vectors)
 
 
 ORDER, SLOT, SIZE_I, SIZE_J, HEAD = range(5)

time: 158 us -> 159 us (level)
  other arithmetic: 3.63 us -> 5.62 us
  local copies, waits for them, and re-layouts: 7.14 us -> 5.2 us
    unnamed x14 -> x6, local copies, waits for them, and re-layouts: 3.35 us -> 0.72 us
    convert_element_type x0 -> x3, other arithmetic: none -> 1.97 us  [lists(): x.reshape(-1).astype(f32)]
  transfers between devices with their start and end apart: 29 -> 29, of which waited for: 12 -> 12; matrix products, arithmetic and copies ran while one was open for 3% -> 5% of each run, Pallas kernels for 13% -> 13%
where the time goes in v18:
time: 159 us; the launch traced here: 158 us
  waiting for transfers between devices  91 us (57%)
  starting transfers between devices  30.3 us (19%)
  Pallas kernels  24.7 us (16%)
  other arithmetic  5.62 us (4%)
  local copies, waits for them, and re-layouts  5.2 us (3%)
    ppermute x24, waiting for transfers between devices, pp(): return lax.ppermute(x, 'orb', perm)  89.2 us
    ppermute x24, starting transfers between devices, pp(): return lax.ppermute(x, 'orb', perm)  29.2 us
    pallas_call x10, Pallas kernels, amplitudes(): pl.pallas_call(lambda *refs: amplitudes_kernel(mode, call, per_orb, [len(...  11.2 us
    pallas_call x7, Pallas kernels, pack(): pl.pallas_call(lambda *refs: pack_kernel(kinds, len(tbls), *refs), out_sh...  4.83 us
    pallas_call x2, Pallas kernels, turn(): pl.pallas_call(turn_kernel, out_shape=[jax.ShapeDtypeStruct((count, cols,...  4.47 us
  transfers between devices with their start and end apart: 29, of which 12 were waited for; matrix products, arithmetic and copies ran while one was open for 5% of the time, Pallas kernels for 13%

profile of v18, /device:TPU:0, one launch (start us, length us, event | category | flops | bytes accessed | tf_op | source)
XLA Modules:
  0.0 157.9 jit_solution(16690640676838557052)
XLA Ops:
  3.8 0.7 copy-done.1
  4.7 2.6 %collective-permute-start = (f32[24,384]{1,0:T(8,128)S(1)}, f32[24,384]{1,0:T(8,128)S(1)}, u32[]{:S(2)}, u32[]{:S(2)}) collective-permute-start(f32[24,384]{1,0:T(8,128)S(1)} %get-tuple-element.55.refs_1_), channel_id=1, source_target_pairs={{0,2},{2,0},{4,6},{6,4},{8,10},{10,8},{12,14},{14,12},{1,3},{3,1},... | collective-permute-start | bytes 110600 | tf_op jit(solution)/shard_map/ppermute | solution.py:424
  7.3 1.6 collective-permute-start.1
  8.9 3.0 %collective-permute-start.3 = (f32[24,384]{1,0:T(8,128)S(1)}, f32[24,384]{1,0:T(8,128)S(1)}, u32[]{:S(2)}, u32[]{:S(2)}) collective-permute-start(f32[24,384]{1,0:T(8,128)S(1)} %get-tuple-element.55.refs_1_), channel_id=1, source_target_pairs={{0,8},{2,10},{4,12},{6,14},{8,0},{10,2},{12,4},{14,6},{1,9},{3,11}... | collective-permute-start | bytes 110600 | tf_op jit(solution)/shard_map/ppermute | solution.py:424
  11.9 1.4 collective-permute-start.4
  13.3 3.5 %collective-permute-start.5 = (f32[24,384]{1,0:T(8,128)S(1)}, f32[24,384]{1,0:T(8,128)S(1)}, u32[]{:S(2)}, u32[]{:S(2)}) collective-permute-start(f32[24,384]{1,0:T(8,128)S(1)} %get-tuple-element.55.refs_1_), channel_id=1, source_target_pairs={{0,12},{2,14},{4,8},{6,10},{8,4},{10,6},{12,0},{14,2},{1,13},{3,15... | collective-permute-start | bytes 110600 | tf_op jit(solution)/shard_map/ppermute | solution.py:424
  17.1 1.3 constant_dynamic-slice_fusion.1.refs_2_.refs_5_
  18.4 0.8 collective-permute-done.5.refs_7_
  19.2 4.6 %collective-permute-done.6.refs_8_ = f32[24,384]{1,0:T(8,128)S(1)} collective-permute-done((f32[24,384]{1,0:T(8,128)S(1)}, f32[24,384]{1,0:T(8,128)S(1)}, u32[]{:S(2)}, u32[]{:S(2)}) %collective-permute-start.6) | collective-permute-done | bytes 36896 | tf_op jit(solution)/shard_map/ppermute | solution.py:424
  23.8 0.7 collective-permute-start.12
  24.6 1.3 tables.1
  25.9 1.3 constant_dynamic-slice_fusion.refs_3_.refs_6_
  27.3 0.7 pack.7.refs_7_
  28.3 3.2 %collective-permute-start.10 = (bf16[16,256,128]{2,1,0:T(8,128)(2,1)S(1)}, bf16[16,256,128]{2,1,0:T(8,128)(2,1)S(1)}, u32[]{:S(2)}, u32[]{:S(2)}) collective-permute-start(bf16[16,256,128]{2,1,0:T(8,128)(2,1)S(1)} %constant_dynamic-slice_fusion.refs_3_.refs_6_), channel_id=1, source_target_pairs={{0,4},{2,6},{4,0},{6,2},{8,12},{10,14},{12,8},{14,10},{1,5},{3,7},... | collective-permute-start | bytes 3145736 | tf_op jit(solution)/shard_map/ppermute | solution.py:424
  31.5 0.7 collective-permute-start.16
  32.2 3.1 %turn.2 = (bf16[16,256,256]{2,1,0:T(8,128)(2,1)S(1)}, bf16[16,256,256]{2,1,0:T(8,128)(2,1)S(1)}) custom-call(bf16[16,256,256]{2,1,0:T(8,128)(2,1)S(1)} %copy-done, bf16[16,256,256]{2,1,0:T(8,128)(2,1)} %collective-permute-done.7.refs_1_), custom_call_target="tpu_custom_call" | custom-call | flops 1 | bytes 1 | tf_op jit(solution)/shard_map/turn/pallas_call | solution.py:265
  36.0 1.3 amplitudes.10
  37.3 12.6 %collective-permute-done.8.refs_2_.refs_0_.refs_5_ = bf16[16,256,128]{2,1,0:T(8,128)(2,1)S(1)} collective-permute-done((bf16[16,256,128]{2,1,0:T(8,128)(2,1)S(1)}, bf16[16,256,128]{2,1,0:T(8,128)(2,1)S(1)}, u32[]{:S(2)}, u32[]{:S(2)}) %collective-permute-start.8) | collective-permute-done | bytes 1048608 | tf_op jit(solution)/shard_map/ppermute | solution.py:424
  49.9 0.7 pack.8.refs_6_
  50.9 10.8 %collective-permute-done.13.refs_7_.refs_5_ = bf16[1,8,256,128]{3,2,1,0:T(8,128)(2,1)S(1)} collective-permute-done((bf16[1,8,256,128]{3,2,1,0:T(8,128)(2,1)S(1)}, bf16[1,8,256,128]{3,2,1,0:T(8,128)(2,1)S(1)}, u32[]{:S(2)}, u32[]{:S(2)}) %collective-permute-start.13) | collective-permute-done | bytes 524320 | tf_op jit(solution)/shard_map/ppermute | solution.py:424
  61.7 1.3 amplitudes.11
  63.0 5.7 %collective-permute-done.10.refs_1_.refs_2_.refs_6_ = bf16[16,256,128]{2,1,0:T(8,128)(2,1)S(1)} collective-permute-done((bf16[16,256,128]{2,1,0:T(8,128)(2,1)S(1)}, bf16[16,256,128]{2,1,0:T(8,128)(2,1)S(1)}, u32[]{:S(2)}, u32[]{:S(2)}) %collective-permute-start.10) | collective-permute-done | bytes 1048608 | tf_op jit(solution)/shard_map/ppermute | solution.py:424
  69.3 1.3 collective-permute-start.17
  70.6 0.7 collective-permute-start.9
  71.3 0.7 collective-permute-start.19
  72.1 0.7 collective-permute-start.26
  72.8 0.7 pack.10.refs_9_
  73.6 1.3 turn.3
  76.1 1.3 collective-permute-start.21
  77.4 20.8 %collective-permute-done.17.refs_8_.refs_6_ = bf16[2,8,256,128]{3,2,1,0:T(8,128)(2,1)S(1)} collective-permute-done((bf16[2,8,256,128]{3,2,1,0:T(8,128)(2,1)S(1)}, bf16[2,8,256,128]{3,2,1,0:T(8,128)(2,1)S(1)}, u32[]{:S(2)}, u32[]{:S(2)}) %collective-permute-start.17) | collective-permute-done | bytes 1048608 | tf_op jit(solution)/shard_map/ppermute | solution.py:424
  98.2 1.6 %collective-permute-start.20 = (bf16[1,8,256,128]{3,2,1,0:T(8,128)(2,1)S(1)}, bf16[1,8,256,128]{3,2,1,0:T(8,128)(2,1)S(1)}, u32[]{:S(2)}, u32[]{:S(2)}) collective-permute-start(bf16[1,8,256,128]{3,2,1,0:T(8,128)(2,1)S(1)} %pack.10.refs_9_), channel_id=1, source_target_pairs={{0,2},{2,0},{4,6},{6,4},{8,10},{10,8},{12,14},{14,12},{1,3},{3,1},... | collective-permute-start | bytes 1572872 | tf_op jit(solution)/shard_map/ppermute | solution.py:424
  99.9 1.3 amplitudes.13
  102.6 5.5 %collective-permute-done.21.refs_7_ = bf16[8,256,128]{2,1,0:T(8,128)(2,1)S(1)} collective-permute-done((bf16[8,256,128]{2,1,0:T(8,128)(2,1)S(1)}, bf16[8,256,128]{2,1,0:T(8,128)(2,1)S(1)}, u32[]{:S(2)}, u32[]{:S(2)}) %collective-permute-start.21) | collective-permute-done | bytes 524320 | tf_op jit(solution)/shard_map/ppermute | solution.py:424
  108.0 1.3 collective-permute-start.23
  109.3 0.9 amplitudes.14
  110.2 0.8 collective-permute-done.20.refs_6_
  111.0 1.3 amplitudes.15
  113.0 1.3 collective-permute-start.24
  114.9 1.3 collective-permute-start.25
  117.6 5.5 %collective-permute-done.23.refs_9_.refs_7_ = bf16[1,8,256,128]{3,2,1,0:T(8,128)(2,1)S(1)} collective-permute-done((bf16[1,8,256,128]{3,2,1,0:T(8,128)(2,1)S(1)}, bf16[1,8,256,128]{3,2,1,0:T(8,128)(2,1)S(1)}, u32[]{:S(2)}, u32[]{:S(2)}) %collective-permute-start.23) | collective-permute-done | bytes 524320 | tf_op jit(solution)/shard_map/ppermute | solution.py:424
  123.2 1.4 amplitudes.17
  124.5 14.2 %collective-permute-done.24.refs_8_ = bf16[1,8,256,128]{3,2,1,0:T(8,128)(2,1)S(1)} collective-permute-done((bf16[1,8,256,128]{3,2,1,0:T(8,128)(2,1)S(1)}, bf16[1,8,256,128]{3,2,1,0:T(8,128)(2,1)S(1)}, u32[]{:S(2)}, u32[]{:S(2)}) %collective-permute-start.24) | collective-permute-done | bytes 524320 | tf_op jit(solution)/shard_map/ppermute | solution.py:424
  138.7 7.9 %collective-permute-done.25.refs_7_ = bf16[8,256,128]{2,1,0:T(8,128)(2,1)S(1)} collective-permute-done((bf16[8,256,128]{2,1,0:T(8,128)(2,1)S(1)}, bf16[8,256,128]{2,1,0:T(8,128)(2,1)S(1)}, u32[]{:S(2)}, u32[]{:S(2)}) %collective-permute-start.25) | collective-permute-done | bytes 524320 | tf_op jit(solution)/shard_map/ppermute | solution.py:424
  146.6 1.1 amplitudes.18
  147.7 1.4 amplitudes.19
  149.1 2.7 %densities.1 = (f32[16,128,256]{2,1,0:T(8,128)S(1)}, bf16[16,128,256]{2,1,0:T(8,128)(2,1)S(1)}) custom-call(s32[1]{0:T(128)} %bitcast.6.start, bf16[64,256,128]{2,1,0:T(8,128)(2,1)S(1)} %get-tuple-element.101.t), custom_call_target="tpu_custom_call" | custom-call | flops 1 | bytes 1 | tf_op jit(solution)/shard_map/densities/pallas_call | solution.py:402
  152.7 1.8 %collective-permute-done.27 = f32[64]{0:T(128)S(1)} collective-permute-done((f32[64]{0:T(128)S(1)}, f32[64]{0:T(128)S(1)}, u32[]{:S(2)}, u32[]{:S(2)}) %collective-permute-start.27) | collective-permute-done | bytes 288 | tf_op jit(solution)/shard_map/ppermute | solution.py:427
  155.1 2.8 %convert_add_fusion = f32[16,128,256]{2,1,0:T(8,128)} fusion(f32[16,128,256]{2,1,0:T(8,128)S(1)} %get-tuple-element.102, bf16[16,128,256]{2,1,0:T(8,128)(2,1)} %collective-permute-done.28), kind=kLoop, calls=%fused_computation | loop fusion | flops 1048576 | bytes 5242880 | tf_op jit(solution)/shard_map/add | solution.py:501
  (54 shorter events, 12.1 us)
Async XLA Ops:
  0.6 25.3 %collective-permute-start.7 = (bf16[16,256,256]{2,1,0:T(8,128)(2,1)}, bf16[16,256,256]{2,1,0:T(8,128)(2,1)}, u32[]{:S(2)}, u32[]{:S(2)}) collective-permute-start(bf16[16,256,256]{2,1,0:T(8,128)(2,1)} %refs_0_.3), channel_id=1, source_target_pairs={{0,1},{1,0},{2,3},{3,2},{4,5},{5,4},{6,7},{7,6},{8,9},{9,8},{10,11... | collective-permute-start | bytes 6291464 | tf_op jit(solution)/shard_map/ppermute | solution.py:427
  3.8 0.7 copy-start.1
  4.7 7.2 %collective-permute-start = (f32[24,384]{1,0:T(8,128)S(1)}, f32[24,384]{1,0:T(8,128)S(1)}, u32[]{:S(2)}, u32[]{:S(2)}) collective-permute-start(f32[24,384]{1,0:T(8,128)S(1)} %get-tuple-element.55.refs_1_), channel_id=1, source_target_pairs={{0,2},{2,0},{4,6},{6,4},{8,10},{10,8},{12,14},{14,12},{1,3},{3,1},... | collective-permute-start | bytes 110600 | tf_op jit(solution)/shard_map/ppermute | solution.py:424
  7.3 6.0 %collective-permute-start.1 = (f32[24,384]{1,0:T(8,128)S(1)}, f32[24,384]{1,0:T(8,128)S(1)}, u32[]{:S(2)}, u32[]{:S(2)}) collective-permute-start(f32[24,384]{1,0:T(8,128)S(1)} %get-tuple-element.55.refs_1_), channel_id=1, source_target_pairs={{0,4},{2,6},{4,0},{6,2},{8,12},{10,14},{12,8},{14,10},{1,5},{3,7},... | collective-permute-start | bytes 110600 | tf_op jit(solution)/shard_map/ppermute | solution.py:424
  8.9 7.9 %collective-permute-start.2 = (f32[24,384]{1,0:T(8,128)S(1)}, f32[24,384]{1,0:T(8,128)S(1)}, u32[]{:S(2)}, u32[]{:S(2)}) collective-permute-start(f32[24,384]{1,0:T(8,128)S(1)} %get-tuple-element.55.refs_1_), channel_id=1, source_target_pairs={{0,6},{2,4},{4,2},{6,0},{8,14},{10,12},{12,10},{14,8},{1,7},{3,5},... | collective-permute-start | bytes 110600 | tf_op jit(solution)/shard_map/ppermute | solution.py:424
  8.9 9.5 %collective-permute-start.3 = (f32[24,384]{1,0:T(8,128)S(1)}, f32[24,384]{1,0:T(8,128)S(1)}, u32[]{:S(2)}, u32[]{:S(2)}) collective-permute-start(f32[24,384]{1,0:T(8,128)S(1)} %get-tuple-element.55.refs_1_), channel_id=1, source_target_pairs={{0,8},{2,10},{4,12},{6,14},{8,0},{10,2},{12,4},{14,6},{1,9},{3,11}... | collective-permute-start | bytes 110600 | tf_op jit(solution)/shard_map/ppermute | solution.py:424
  11.9 6.5 %collective-permute-start.4 = (f32[24,384]{1,0:T(8,128)S(1)}, f32[24,384]{1,0:T(8,128)S(1)}, u32[]{:S(2)}, u32[]{:S(2)}) collective-permute-start(f32[24,384]{1,0:T(8,128)S(1)} %get-tuple-element.55.refs_1_), channel_id=1, source_target_pairs={{0,10},{2,8},{4,14},{6,12},{8,2},{10,0},{12,6},{14,4},{1,11},{3,9}... | collective-permute-start | bytes 110600 | tf_op jit(solution)/shard_map/ppermute | solution.py:424
  13.3 5.9 %collective-permute-start.5 = (f32[24,384]{1,0:T(8,128)S(1)}, f32[24,384]{1,0:T(8,128)S(1)}, u32[]{:S(2)}, u32[]{:S(2)}) collective-permute-start(f32[24,384]{1,0:T(8,128)S(1)} %get-tuple-element.55.refs_1_), channel_id=1, source_target_pairs={{0,12},{2,14},{4,8},{6,10},{8,4},{10,6},{12,0},{14,2},{1,13},{3,15... | collective-permute-start | bytes 110600 | tf_op jit(solution)/shard_map/ppermute | solution.py:424
  16.8 7.0 %collective-permute-start.6 = (f32[24,384]{1,0:T(8,128)S(1)}, f32[24,384]{1,0:T(8,128)S(1)}, u32[]{:S(2)}, u32[]{:S(2)}) collective-permute-start(f32[24,384]{1,0:T(8,128)S(1)} %get-tuple-element.55.refs_1_), channel_id=1, source_target_pairs={{0,14},{2,12},{4,10},{6,8},{8,6},{10,4},{12,2},{14,0},{1,15},{3,13... | collective-permute-start | bytes 110600 | tf_op jit(solution)/shard_map/ppermute | solution.py:424
  23.8 26.1 %collective-permute-start.8 = (bf16[16,256,128]{2,1,0:T(8,128)(2,1)S(1)}, bf16[16,256,128]{2,1,0:T(8,128)(2,1)S(1)}, u32[]{:S(2)}, u32[]{:S(2)}) collective-permute-start(bf16[16,256,128]{2,1,0:T(8,128)(2,1)S(1)} %constant_dynamic-slice_fusion.1.refs_2_.refs_5_), channel_id=1, source_target_pairs={{0,4},{2,6},{4,0},{6,2},{8,12},{10,14},{12,8},{14,10},{1,5},{3,7},... | collective-permute-start | bytes 3145736 | tf_op jit(solution)/shard_map/ppermute | solution.py:424
  23.8 26.1 %collective-permute-start.12 = (bf16[16,256,128]{2,1,0:T(8,128)(2,1)S(1)}, bf16[16,256,128]{2,1,0:T(8,128)(2,1)S(1)}, u32[]{:S(2)}, u32[]{:S(2)}) collective-permute-start(bf16[16,256,128]{2,1,0:T(8,128)(2,1)S(1)} %constant_dynamic-slice_fusion.1.refs_2_.refs_5_), channel_id=1, source_target_pairs={{4,8},{6,10},{8,4},{10,6},{5,9},{7,11},{9,5},{11,7},{20,24},{22,26... | collective-permute-start | bytes 3145736 | tf_op jit(solution)/shard_map/ppermute | solution.py:424
  27.2 5.0 %copy-start = (bf16[16,256,256]{2,1,0:T(8,128)(2,1)S(1)}, bf16[16,256,256]{2,1,0:T(8,128)(2,1)}, u32[]{:S(2)}) copy-start(bf16[16,256,256]{2,1,0:T(8,128)(2,1)} %refs_0_.3) | copy-start | bytes 6291460
  28.0 7.4 %copy-start.2 = (f32[16,256]{1,0:T(8,128)S(1)}, f32[16,256]{1,0:T(8,128)}, u32[]{:S(2)}) copy-start(f32[16,256]{1,0:T(8,128)} %refs_0_.2) | copy-start | bytes 49156
  28.0 33.6 %collective-permute-start.11 = (bf16[2,8,256,128]{3,2,1,0:T(8,128)(2,1)S(1)}, bf16[2,8,256,128]{3,2,1,0:T(8,128)(2,1)S(1)}, u32[]{:S(2)}, u32[]{:S(2)}) collective-permute-start(bf16[2,8,256,128]{3,2,1,0:T(8,128)(2,1)S(1)} %pack.7.refs_7_), channel_id=1, source_target_pairs={{0,2},{2,0},{4,6},{6,4},{8,10},{10,8},{12,14},{14,12},{1,3},{3,1},... | collective-permute-start | bytes 3145736 | tf_op jit(solution)/shard_map/ppermute | solution.py:424
  28.3 40.4 %collective-permute-start.10 = (bf16[16,256,128]{2,1,0:T(8,128)(2,1)S(1)}, bf16[16,256,128]{2,1,0:T(8,128)(2,1)S(1)}, u32[]{:S(2)}, u32[]{:S(2)}) collective-permute-start(bf16[16,256,128]{2,1,0:T(8,128)(2,1)S(1)} %constant_dynamic-slice_fusion.refs_3_.refs_6_), channel_id=1, source_target_pairs={{0,4},{2,6},{4,0},{6,2},{8,12},{10,14},{12,8},{14,10},{1,5},{3,7},... | collective-permute-start | bytes 3145736 | tf_op jit(solution)/shard_map/ppermute | solution.py:424
  31.5 37.1 %collective-permute-start.16 = (bf16[16,256,128]{2,1,0:T(8,128)(2,1)S(1)}, bf16[16,256,128]{2,1,0:T(8,128)(2,1)S(1)}, u32[]{:S(2)}, u32[]{:S(2)}) collective-permute-start(bf16[16,256,128]{2,1,0:T(8,128)(2,1)S(1)} %constant_dynamic-slice_fusion.refs_3_.refs_6_), channel_id=1, source_target_pairs={{4,8},{6,10},{8,4},{10,6},{5,9},{7,11},{9,5},{11,7},{20,24},{22,26... | collective-permute-start | bytes 3145736 | tf_op jit(solution)/shard_map/ppermute | solution.py:424
  50.6 11.0 %collective-permute-start.13 = (bf16[1,8,256,128]{3,2,1,0:T(8,128)(2,1)S(1)}, bf16[1,8,256,128]{3,2,1,0:T(8,128)(2,1)S(1)}, u32[]{:S(2)}, u32[]{:S(2)}) collective-permute-start(bf16[1,8,256,128]{3,2,1,0:T(8,128)(2,1)S(1)} %pack.8.refs_6_), channel_id=1, source_target_pairs={{0,2},{2,0},{4,6},{6,4},{8,10},{10,8},{12,14},{14,12},{1,3},{3,1},... | collective-permute-start | bytes 1572872 | tf_op jit(solution)/shard_map/ppermute | solution.py:424
  50.9 21.2 %collective-permute-start.14 = (bf16[16,256,128]{2,1,0:T(8,128)(2,1)S(1)}, bf16[16,256,128]{2,1,0:T(8,128)(2,1)S(1)}, u32[]{:S(2)}, u32[]{:S(2)}) collective-permute-start(bf16[16,256,128]{2,1,0:T(8,128)(2,1)S(1)} %collective-permute-done.8.refs_2_.refs_0_.refs_5_), channel_id=1, source_target_pairs={{0,1},{1,0},{2,3},{3,2},{4,5},{5,4},{6,7},{7,6},{8,9},{9,8},{10,11... | collective-permute-start | bytes 3145736 | tf_op jit(solution)/shard_map/ppermute | solution.py:427
  68.6 4.9 %collective-permute-start.15 = (bf16[16,256,128]{2,1,0:T(8,128)(2,1)S(1)}, bf16[16,256,128]{2,1,0:T(8,128)(2,1)S(1)}, u32[]{:S(2)}, u32[]{:S(2)}) collective-permute-start(bf16[16,256,128]{2,1,0:T(8,128)(2,1)S(1)} %collective-permute-done.10.refs_1_.refs_2_.refs_6_), channel_id=1, source_target_pairs={{0,1},{1,0},{2,3},{3,2},{4,5},{5,4},{6,7},{7,6},{8,9},{9,8},{10,11... | collective-permute-start | bytes 3145736 | tf_op jit(solution)/shard_map/ppermute | solution.py:427
  69.3 28.9 %collective-permute-start.17 = (bf16[2,8,256,128]{3,2,1,0:T(8,128)(2,1)S(1)}, bf16[2,8,256,128]{3,2,1,0:T(8,128)(2,1)S(1)}, u32[]{:S(2)}, u32[]{:S(2)}) collective-permute-start(bf16[2,8,256,128]{3,2,1,0:T(8,128)(2,1)S(1)} %get-tuple-element.85.refs_3_), channel_id=1, source_target_pairs={{4,2},{6,0},{8,14},{10,12},{5,3},{7,1},{9,15},{11,13},{20,18},{22,... | collective-permute-start | bytes 3145736 | tf_op jit(solution)/shard_map/ppermute | solution.py:424
  70.6 30.6 %collective-permute-start.9 = (bf16[16,256,128]{2,1,0:T(8,128)(2,1)S(1)}, bf16[16,256,128]{2,1,0:T(8,128)(2,1)S(1)}, u32[]{:S(2)}, u32[]{:S(2)}) collective-permute-start(bf16[16,256,128]{2,1,0:T(8,128)(2,1)S(1)} %collective-permute-done.8.refs_2_.refs_0_.refs_5_), channel_id=1, source_target_pairs={{4,8},{6,10},{8,4},{10,6},{5,9},{7,11},{9,5},{11,7},{20,24},{22,26... | collective-permute-start | bytes 3145736 | tf_op jit(solution)/shard_map/ppermute | solution.py:424
  71.3 41.0 %collective-permute-start.19 = (bf16[16,256,128]{2,1,0:T(8,128)(2,1)S(1)}, bf16[16,256,128]{2,1,0:T(8,128)(2,1)S(1)}, u32[]{:S(2)}, u32[]{:S(2)}) collective-permute-start(bf16[16,256,128]{2,1,0:T(8,128)(2,1)S(1)} %collective-permute-done.10.refs_1_.refs_2_.refs_6_), channel_id=1, source_target_pairs={{4,8},{6,10},{8,4},{10,6},{5,9},{7,11},{9,5},{11,7},{20,24},{22,26... | collective-permute-start | bytes 3145736 | tf_op jit(solution)/shard_map/ppermute | solution.py:424
  72.1 44.8 %collective-permute-start.26 = (bf16[2,8,256,128]{3,2,1,0:T(8,128)(2,1)S(1)}, bf16[2,8,256,128]{3,2,1,0:T(8,128)(2,1)S(1)}, u32[]{:S(2)}, u32[]{:S(2)}) collective-permute-start(bf16[2,8,256,128]{3,2,1,0:T(8,128)(2,1)S(1)} %get-tuple-element.94), channel_id=1, source_target_pairs={{4,6},{6,4},{8,10},{10,8},{5,7},{7,5},{9,11},{11,9},{20,22},{22,20... | collective-permute-start | bytes 3145736 | tf_op jit(solution)/shard_map/ppermute | solution.py:424
  76.1 31.9 %collective-permute-start.21 = (bf16[8,256,128]{2,1,0:T(8,128)(2,1)S(1)}, bf16[8,256,128]{2,1,0:T(8,128)(2,1)S(1)}, u32[]{:S(2)}, u32[]{:S(2)}) collective-permute-start(bf16[8,256,128]{2,1,0:T(8,128)(2,1)S(1)} %amplitudes.12.refs_7_), channel_id=1, source_target_pairs={{4,0},{6,2},{8,12},{10,14},{5,1},{7,3},{9,13},{11,15},{20,16},{22,... | collective-permute-start | bytes 1572872 | tf_op jit(solution)/shard_map/ppermute | solution.py:424
  98.2 12.8 %collective-permute-start.20 = (bf16[1,8,256,128]{3,2,1,0:T(8,128)(2,1)S(1)}, bf16[1,8,256,128]{3,2,1,0:T(8,128)(2,1)S(1)}, u32[]{:S(2)}, u32[]{:S(2)}) collective-permute-start(bf16[1,8,256,128]{3,2,1,0:T(8,128)(2,1)S(1)} %pack.10.refs_9_), channel_id=1, source_target_pairs={{0,2},{2,0},{4,6},{6,4},{8,10},{10,8},{12,14},{14,12},{1,3},{3,1},... | collective-permute-start | bytes 1572872 | tf_op jit(solution)/shard_map/ppermute | solution.py:424
  101.9 15.8 %collective-permute-start.18 = (bf16[1,8,256,128]{3,2,1,0:T(8,128)(2,1)S(1)}, bf16[1,8,256,128]{3,2,1,0:T(8,128)(2,1)S(1)}, u32[]{:S(2)}, u32[]{:S(2)}) collective-permute-start(bf16[1,8,256,128]{3,2,1,0:T(8,128)(2,1)S(1)} %get-tuple-element.88), channel_id=1, source_target_pairs={{4,6},{6,4},{8,10},{10,8},{5,7},{7,5},{9,11},{11,9},{20,22},{22,20... | collective-permute-start | bytes 1572872 | tf_op jit(solution)/shard_map/ppermute | solution.py:424
  108.0 15.1 %collective-permute-start.23 = (bf16[1,8,256,128]{3,2,1,0:T(8,128)(2,1)S(1)}, bf16[1,8,256,128]{3,2,1,0:T(8,128)(2,1)S(1)}, u32[]{:S(2)}, u32[]{:S(2)}) collective-permute-start(bf16[1,8,256,128]{3,2,1,0:T(8,128)(2,1)S(1)} %get-tuple-element.89.refs_8_), channel_id=1, source_target_pairs={{4,2},{6,0},{8,14},{10,12},{5,3},{7,1},{9,15},{11,13},{20,18},{22,... | collective-permute-start | bytes 1572872 | tf_op jit(solution)/shard_map/ppermute | solution.py:424
  113.0 25.7 %collective-permute-start.24 = (bf16[1,8,256,128]{3,2,1,0:T(8,128)(2,1)S(1)}, bf16[1,8,256,128]{3,2,1,0:T(8,128)(2,1)S(1)}, u32[]{:S(2)}, u32[]{:S(2)}) collective-permute-start(bf16[1,8,256,128]{3,2,1,0:T(8,128)(2,1)S(1)} %pack.12.refs_9_), channel_id=1, source_target_pairs={{4,2},{6,0},{8,14},{10,12},{5,3},{7,1},{9,15},{11,13},{20,18},{22,... | collective-permute-start | bytes 1572872 | tf_op jit(solution)/shard_map/ppermute | solution.py:424
  114.9 31.7 %collective-permute-start.25 = (bf16[8,256,128]{2,1,0:T(8,128)(2,1)S(1)}, bf16[8,256,128]{2,1,0:T(8,128)(2,1)S(1)}, u32[]{:S(2)}, u32[]{:S(2)}) collective-permute-start(bf16[8,256,128]{2,1,0:T(8,128)(2,1)S(1)} %amplitudes.16.refs_3_), channel_id=1, source_target_pairs={{4,0},{6,2},{8,12},{10,14},{5,1},{7,3},{9,13},{11,15},{20,16},{22,... | collective-permute-start | bytes 1572872 | tf_op jit(solution)/shard_map/ppermute | solution.py:424
  116.9 30.8 %collective-permute-start.22 = (bf16[1,8,256,128]{3,2,1,0:T(8,128)(2,1)S(1)}, bf16[1,8,256,128]{3,2,1,0:T(8,128)(2,1)S(1)}, u32[]{:S(2)}, u32[]{:S(2)}) collective-permute-start(bf16[1,8,256,128]{3,2,1,0:T(8,128)(2,1)S(1)} %pack.13.refs_7_), channel_id=1, source_target_pairs={{4,6},{6,4},{8,10},{10,8},{5,7},{7,5},{9,11},{11,9},{20,22},{22,20... | collective-permute-start | bytes 1572872 | tf_op jit(solution)/shard_map/ppermute | solution.py:424
  151.9 3.2 %collective-permute-start.28 = (bf16[16,128,256]{2,1,0:T(8,128)(2,1)S(1)}, bf16[16,128,256]{2,1,0:T(8,128)(2,1)}, u32[]{:S(2)}, u32[]{:S(2)}) collective-permute-start(bf16[16,128,256]{2,1,0:T(8,128)(2,1)S(1)} %get-tuple-element.103), channel_id=1, source_target_pairs={{0,1},{1,0},{2,3},{3,2},{4,5},{5,4},{6,7},{7,6},{8,9},{9,8},{10,11... | collective-permute-start | bytes 3145736 | tf_op jit(solution)/shard_map/ppermute | solution.py:427
  152.2 2.4 %collective-permute-start.27 = (f32[64]{0:T(128)S(1)}, f32[64]{0:T(128)S(1)}, u32[]{:S(2)}, u32[]{:S(2)}) collective-permute-start(f32[64]{0:T(128)S(1)} %multiply_reduce_fusion), channel_id=1, source_target_pairs={{0,1},{1,0},{2,3},{3,2},{4,5},{5,4},{6,7},{7,6},{8,9},{9,8},{10,11... | collective-permute-start | bytes 776 | tf_op jit(solution)/shard_map/ppermute | solution.py:427
